TPU v7x, 32 devices: a whole 2x2x4 slice. The times are simulated.
32 devices in a mesh: groups: 2 (over x), seq: 4 (over y, core), head: 4 (over z).
Axes of the slice: x: 2, y: 2, z: 4, core: 2. Of those that a mesh axis runs over, the one named last changes fastest.
Arguments:
- latent_cache: bfloat16 [32768, 576], P(('groups', 'seq')), parts along dimension 0, may hold values from -6 to 6
- lengths: int32 [8, 16], P('groups'), parts along dimension 0, may hold values from 1 to 512, 4096 in all within a row
- decode_rows: int32 [128], P('groups'), parts along dimension 0, may hold values from 0 to 63, as said below
- q_nope: bfloat16 [4, 128, 128, 128], P(None, ('groups', 'seq'), 'head'), parts along dimension 1, may hold values from -6 to 6
- q_rope: bfloat16 [4, 128, 128, 64], P(None, ('groups', 'seq'), 'head'), parts along dimension 1, may hold values from -90 to 90
- new_latent: bfloat16 [4, 128, 576], P(None, ('groups', 'seq')), parts along dimension 1, may hold values from -13 to 13
- key_up: bfloat16 [128, 128, 512], P('head'), may hold values from -0.5 to 0.5
- value_up: bfloat16 [128, 512, 128], P('head'), may hold values from -0.25 to 0.25
- out_proj: bfloat16 [16384, 7168], P('head', 'seq'), may hold values from -0.046875 to 0.046875
Outputs:
- mixed: bfloat16 [4, 128, 7168], P(None, 'groups', 'seq'), parts along dimension 1
There are 2 independent parts, one for each index of `groups`. A program takes and returns all parts, laid end to end along the dimension named above; an argument that names none is the same for every part. Nothing has to cross between parts.
Inputs may be any that keep to these rules, and one draw needn't show every extreme that they name: `decode_rows`: a permutation of the rows; the rows of decode owner o are o * 16 to o * 16 + 15, and every prefill device hands exactly 4 of its requests to every owner. Each prefill device's lengths sum to 4096.
All inputs are finite; a program needn't handle non-finite values.
Results may differ from a plain program's by a relative error of at most 0.0077.
Values may be sent and summed in bfloat16 or wider, within the bound.
No kernel may reach another device: no remote copies, remote signals or barrier semaphores. Data moves between devices by JAX's collectives and lax.ppermute only.
A program may use at most 128 MiB of HBM per device.

v0:
```python
import jax
import jax.numpy as jnp
from jax import lax
from jax.sharding import PartitionSpec as P

LATENT = 512
MOST = 512


def attend(queries, cache_rows, fresh_tokens, live_length, latent_width, scale):
    step_count = queries.shape[0]
    slot_count = cache_rows.shape[1]
    cache_scores = (
        jnp.einsum("tnhc,njc->tnhj", queries, cache_rows, preferred_element_type=jnp.float32)
        * scale
    )
    new_scores = (
        jnp.einsum("tnhc,unc->tnhu", queries, fresh_tokens, preferred_element_type=jnp.float32)
        * scale
    )
    live_mask = jnp.arange(slot_count, dtype=jnp.int32)[None, :] < live_length[:, None]
    cache_scores = jnp.where(live_mask[None, :, None, :], cache_scores, -jnp.inf)
    causal = jnp.arange(step_count)[None, :] <= jnp.arange(step_count)[:, None]
    new_scores = jnp.where(causal[:, None, None, :], new_scores, -jnp.inf)
    weights = jax.nn.softmax(jnp.concatenate([cache_scores, new_scores], axis=3), axis=3).astype(
        jnp.bfloat16
    )
    latent_out = jnp.einsum(
        "tnhj,njc->tnhc",
        weights[..., :slot_count],
        cache_rows[..., :latent_width],
        preferred_element_type=jnp.float32,
    )
    latent_out = latent_out + jnp.einsum(
        "tnhu,unc->tnhc",
        weights[..., slot_count:],
        fresh_tokens[..., :latent_width],
        preferred_element_type=jnp.float32,
    )
    return latent_out.astype(jnp.bfloat16)


def local(
    latent_cache, lengths, decode_rows, q_nope, q_rope, new_latent, key_up, value_up, out_proj
):
    seq_count = lax.axis_size("seq")
    owner_index = lax.axis_index("seq")
    requests = lengths.shape[1]
    per_pair = requests // seq_count
    token_width = latent_cache.shape[1]
    step_count = q_nope.shape[0]
    heads_local = q_nope.shape[2]
    scale = (q_nope.shape[3] + q_rope.shape[3]) ** (-0.5)
    owner_of = decode_rows.reshape(seq_count, requests) // requests
    local_row = decode_rows.reshape(seq_count, requests) % requests
    request_order = jnp.arange(requests, dtype=jnp.int32)
    earlier = (owner_of[:, :, None] == owner_of[:, None, :]) & (
        request_order[None, None, :] < request_order[None, :, None]
    )
    earlier_count = jnp.sum(earlier.astype(jnp.int32), axis=2)
    offsets = jnp.cumsum(lengths, axis=1) - lengths
    slot_order = jnp.arange(per_pair, dtype=jnp.int32)
    chosen = (
        (owner_of == owner_index)[:, None, :]
        & (earlier_count[:, None, :] == slot_order[None, :, None])
    ).astype(jnp.int32)
    slot_row = jnp.sum(chosen * local_row[:, None, :], axis=2).reshape(requests)
    owners = jnp.arange(seq_count, dtype=jnp.int32)
    my_owner = lax.dynamic_index_in_dim(owner_of, owner_index, 0, keepdims=False)
    my_count = lax.dynamic_index_in_dim(earlier_count, owner_index, 0, keepdims=False)
    my_offset = lax.dynamic_index_in_dim(offsets, owner_index, 0, keepdims=False)
    my_length = lax.dynamic_index_in_dim(lengths, owner_index, 0, keepdims=False)
    picked = (
        (my_owner[None, None, :] == owners[:, None, None])
        & (my_count[None, None, :] == slot_order[None, :, None])
    ).astype(jnp.int32)
    send_offset = jnp.sum(picked * my_offset[None, None, :], axis=2)
    send_length = jnp.sum(picked * my_length[None, None, :], axis=2).reshape(requests)
    positions = jnp.minimum(
        send_offset[:, :, None] + jnp.arange(MOST, dtype=jnp.int32)[None, None, :],
        latent_cache.shape[0] - 1,
    )
    outgoing = jnp.take(latent_cache, positions.reshape(-1), axis=0).reshape(
        seq_count, per_pair, MOST, token_width
    )
    q_abs = jnp.einsum("tbhn,hnc->tbhc", q_nope, key_up, preferred_element_type=jnp.float32).astype(
        jnp.bfloat16
    )
    queries = jnp.concatenate([q_abs, q_rope], axis=3)
    slot_queries = jnp.take(queries, slot_row, axis=1)
    slot_fresh = jnp.take(new_latent, slot_row, axis=1)
    sent_queries = slot_queries.reshape(step_count, seq_count, per_pair, heads_local, token_width)
    sent_fresh = slot_fresh.reshape(step_count, seq_count, per_pair, token_width)
    recv_queries, recv_fresh = (
        lax.all_to_all(sent_queries, "seq", split_axis=1, concat_axis=1, tiled=True),
        lax.all_to_all(sent_fresh, "seq", split_axis=1, concat_axis=1, tiled=True),
    )
    finished = attend(
        recv_queries.reshape(step_count, requests, heads_local, token_width),
        outgoing.reshape(requests, MOST, token_width),
        recv_fresh.reshape(step_count, requests, token_width),
        send_length,
        LATENT,
        scale,
    )
    returned = lax.all_to_all(
        finished.reshape(step_count, seq_count, per_pair, heads_local, LATENT),
        "seq",
        split_axis=1,
        concat_axis=1,
        tiled=True,
    )
    latent_out = returned.reshape(step_count, requests, heads_local, LATENT)
    head_out = jnp.einsum(
        "tshc,hcv->tshv", latent_out, value_up, preferred_element_type=jnp.float32
    ).astype(jnp.bfloat16)
    row_slot = jnp.sum(
        (slot_row[None, :] == request_order[:, None]).astype(jnp.int32) * request_order[None, :],
        axis=1,
    )
    head_rows = jnp.take(head_out, row_slot, axis=1).reshape(
        step_count, requests, heads_local * head_out.shape[3]
    )
    partial_value = jnp.einsum(
        "tbk,kd->tbd",
        lax.all_gather(head_rows, "seq", axis=1, tiled=True),
        out_proj,
        preferred_element_type=jnp.float32,
    )
    return lax.psum(partial_value, "head").astype(jnp.bfloat16)


def solution(mesh):
    return jax.shard_map(
        local,
        mesh=mesh,
        in_specs=(
            P(("groups", "seq"), None),
            P("groups", None),
            P("groups"),
            P(None, ("groups", "seq"), "head", None),
            P(None, ("groups", "seq"), "head", None),
            P(None, ("groups", "seq"), None),
            P("head", None, None),
            P("head", None, None),
            P("head", "seq"),
        ),
        out_specs=P(None, "groups", "seq"),
        check_vma=False,
    )
```

profile of v0, /device:TPU:0, one launch (start us, length us, event | category | flops | bytes accessed | tf_op | source)
XLA Modules:
  0.0 257.4 jit_solution(455208318366504239)
XLA Ops:
  6.5 0.8 reshape.326
  7.3 0.2 convert_reduce_fusion
  7.6 0.2 select_reduce_fusion.1
  7.7 0.1 reshape.327
  7.8 0.8 gather_fusion.2
  8.7 0.7 broadcast_select_fusion.2
  9.4 4.2 %all-to-all-start.1 = ((bf16[4,4,4,576]{3,0,2,1:T(4,128)(2,1)}), bf16[4,4,4,576]{3,0,2,1:T(4,128)(2,1)S(1)}, u32[]{:S(2)}, u32[]{:S(2)}) async-start(bf16[4,4,4,576]{3,0,2,1:T(4,128)(2,1)} %broadcast_select_fusion.2), calls=%async_computation.1 | async-start | bytes 163840 | tf_op jit(solution)/shard_map/all_to_all | solution.py:96
  13.7 0.9 reduce_window_sum.11
  14.6 0.7 sub.18
  15.3 0.7 fusion.33
  15.9 0.2 fusion.28
  16.4 1.2 copy.67
  17.6 2.9 %fusion.40 = f32[32,512,64]{1,2,0:S(1)} fusion(bf16[32,128,64]{1,2,0:T(8,128)(2,1)S(1)} %bitcast.93, bf16[32,128,512]{2,1,0:T(8,128)(2,1)} %param.15), kind=kOutput, calls=%fused_computation.85 | convolution fusion | flops 268435456 | bytes 8912896
  20.5 0.3 convert_bitcast_fusion
  20.9 0.7 copy-done.4
  21.6 0.2 copy.68
  21.8 0.4 pad_maximum_fusion
  22.2 1.5 copy.69
  23.7 2.4 gather_fusion.1
  26.1 3.6 %broadcast_select_fusion.1 = bf16[4,4,4,32,576]{4,3,0,2,1:T(8,128)(2,1)} fusion(bf16[4,4,4,32,576]{4,3,0,2,1:T(8,128)(2,1)} %bitcast.90, pred[4,4]{1,0:T(4,128)(4,1)S(1)} %compare_and_fusion), kind=kLoop, calls=%fused_computation.20 | loop fusion | flops 1179648 | bytes 4718608 | tf_op jit(solution)/shard_map/jit(_take)/select_n | solution.py:90
  29.7 0.1 add.126
  29.7 7.6 %copy.66 = bf16[4096,576]{1,0:T(8,128)(2,1)} copy(bf16[4096,576]{0,1:T(8,128)(2,1)} %param.9) | data formatting | bytes 9437184 | tf_op args[0]
  37.4 0.1 lt.116
  37.5 3.8 %all-to-all-start = ((bf16[4,4,4,32,576]{4,3,0,2,1:T(8,128)(2,1)}), bf16[4,4,4,32,576]{4,3,0,2,1:T(8,128)(2,1)S(1)}, u32[]{:S(2)}, u32[]{:S(2)}) async-start(bf16[4,4,4,32,576]{4,3,0,2,1:T(8,128)(2,1)} %broadcast_select_fusion.1), calls=%async_computation | async-start | bytes 5242880 | tf_op jit(solution)/shard_map/all_to_all | solution.py:95
  41.3 38.1 %gather_fusion = bf16[8192,576]{1,0:T(8,128)(2,1)} fusion(bf16[4096,576]{1,0:T(8,128)(2,1)} %copy.66, s32[8192]{0:T(1024)S(1)} %broadcast_clamp_fusion), kind=kCustom, calls=%fused_computation | custom fusion | bytes 18907136 | tf_op jit(solution)/shard_map/jit(_take)/gather | solution.py:83
  79.4 0.1 fusion.26
  79.6 10.4 %broadcast_select_fusion = bf16[16,512,576]{2,1,0:T(8,128)(2,1)} fusion(bf16[16,512,576]{2,1,0:T(8,128)(2,1)} %bitcast.86, pred[16,512]{1,0:T(8,128)(4,1)S(1)} %fusion.26), kind=kLoop, calls=%fused_computation.8 | loop fusion | flops 4718592 | bytes 18882560 | tf_op jit(solution)/shard_map/jit(_take)/select_n | solution.py:83
  90.0 2.1 fusion.39
  92.1 0.1 fusion.37
  92.2 1.5 copy.73
  93.7 8.2 %fusion.38 = (f32[4,16,32]{2,0,1:T(4,128)S(1)}, f32[4,16,32,512]{3,2,0,1:T(8,128)S(1)}) fusion(bf16[4,16,32,576]{3,2,0,1:T(8,128)(2,1)} %bitcast.89, bf16[16,512,576]{2,1,0:T(8,128)(2,1)} %broadcast_select_fusion, pred[16,512]{1,0:T(8,128)(4,1)S(1)} %iota_compare_fusion), kind=kOutput, calls=%fused_computation.83 | convolution fusion | flops 1211103232 | bytes 16007168 | tf_op jit(solution)/shard_map/tnhc,njc->tnhj/dot_general | solution.py:14
  101.9 2.4 fusion.8
  104.4 1.1 divide_convert_fusion
  105.5 4.2 %fusion.4 = f32[16,512,4,32]{1,3,2,0:T(8,128)S(1)} fusion(bf16[16,512,576]{2,1,0:T(8,128)(2,1)} %broadcast_select_fusion, bf16[4,16,32,516]{3,2,0,1:T(8,128)(2,1)S(1)} %divide_convert_fusion), kind=kOutput, calls=%fused_computation.10 | convolution fusion | flops 1073741824 | bytes 14680064 | tf_op jit(solution)/shard_map/tnhj,njc->tnhc/dot_general | solution.py:28
  109.7 2.0 add_convert_fusion
  111.8 3.6 %all-to-all-start.2 = ((bf16[4,4,4,32,512]{4,3,0,2,1:T(8,128)(2,1)}), bf16[4,4,4,32,512]{4,3,0,2,1:T(8,128)(2,1)S(1)}, u32[]{:S(2)}, u32[]{:S(2)}) async-start(bf16[4,4,4,32,512]{4,3,0,2,1:T(8,128)(2,1)} %bitcast.92), calls=%async_computation.2 | async-start | bytes 4194304 | tf_op jit(solution)/shard_map/all_to_all | solution.py:106
  115.4 0.3 all-gather.2.cloned.1.call-start
  115.6 0.1 eq.99
  115.7 0.1 select_reduce_fusion
  115.9 25.2 %all-to-all-done.2 = bf16[4,4,4,32,512]{4,3,0,2,1:T(8,128)(2,1)S(1)} async-done(((bf16[4,4,4,32,512]{4,3,0,2,1:T(8,128)(2,1)}), bf16[4,4,4,32,512]{4,3,0,2,1:T(8,128)(2,1)S(1)}, u32[]{:S(2)}, u32[]{:S(2)}) %all-to-all-start.2) | async-done | bytes 2097184 | tf_op jit(solution)/shard_map/all_to_all | solution.py:106
  141.0 4.7 %fusion.18 = bf16[4,16,32,128]{3,1,0,2:T(8,128)(2,1)S(1)} fusion(bf16[32,512,128]{2,1,0:T(8,128)(2,1)} %param.16, bf16[4,16,32,512]{3,2,0,1:T(8,128)(2,1)S(1)} %bitcast.91), kind=kOutput, calls=%fused_computation.25 | convolution fusion | flops 268697600 | bytes 6815744 | tf_op jit(solution)/shard_map/tshc,hcv->tshv/dot_general | solution.py:114
  145.7 0.3 copy.77
  146.1 0.6 gather_fusion.3
  146.7 0.1 reshape.372
  146.9 1.4 copy_select_fusion
  148.3 23.6 %all-gather.2.cloned.1.call-done = bf16[4,64,4096]{2,1,0:T(8,128)(2,1)} async-done(((bf16[4,16,4096]{2,1,0:T(8,128)(2,1)}), bf16[4,64,4096]{2,1,0:T(8,128)(2,1)}) %all-gather.2.cloned.1.call-update) | async-done | bytes 2097168 | tf_op jit(solution)/shard_map/all_gather | solution.py:126
  171.9 8.4 %fusion = f32[4,64,1792]{2,1,0:T(8,128)S(1)} fusion(bf16[4,64,4096]{2,1,0:T(8,128)(2,1)} %all-gather.2.cloned.1.call-done, bf16[4096,1792]{1,0:T(8,128)(2,1)} %param.17), kind=kOutput, calls=%fused_computation.4 | convolution fusion | flops 3758096384 | bytes 18612224 | tf_op jit(solution)/shard_map/tbk,kd->tbd/dot_general | solution.py:124
  180.3 70.3 %all-reduce.1 = bf16[4,64,1792]{2,1,0:T(8,128)(2,1)} all-reduce(f32[4,64,1792]{2,1,0:T(8,128)S(1)} %fusion), channel_id=1, replica_groups=mesh['groups'=2,'seq'=4,'head'=4] {'head'}, use_global_device_ids=true, to_apply=%region_9.10 | all-reduce | flops 458752 | bytes 2752512 | tf_op jit(solution)/shard_map/psum | solution.py:130
  (32 shorter events, 0.4 us)
Async XLA Ops:
  6.5 1.3 copy-start
  9.4 28.0 %all-to-all-start.1 = ((bf16[4,4,4,576]{3,0,2,1:T(4,128)(2,1)}), bf16[4,4,4,576]{3,0,2,1:T(4,128)(2,1)S(1)}, u32[]{:S(2)}, u32[]{:S(2)}) async-start(bf16[4,4,4,576]{3,0,2,1:T(4,128)(2,1)} %broadcast_select_fusion.2), calls=%async_computation.1 | async-start | bytes 163840 | tf_op jit(solution)/shard_map/all_to_all | solution.py:96
  20.5 1.0 copy-start.4
  37.5 52.5 %all-to-all-start = ((bf16[4,4,4,32,576]{4,3,0,2,1:T(8,128)(2,1)}), bf16[4,4,4,32,576]{4,3,0,2,1:T(8,128)(2,1)S(1)}, u32[]{:S(2)}, u32[]{:S(2)}) async-start(bf16[4,4,4,32,576]{4,3,0,2,1:T(8,128)(2,1)} %broadcast_select_fusion.1), calls=%async_computation | async-start | bytes 5242880 | tf_op jit(solution)/shard_map/all_to_all | solution.py:95
  90.0 2.2 copy-start.2
  101.9 2.5 copy-start.3
  111.8 29.3 %all-to-all-start.2 = ((bf16[4,4,4,32,512]{4,3,0,2,1:T(8,128)(2,1)}), bf16[4,4,4,32,512]{4,3,0,2,1:T(8,128)(2,1)S(1)}, u32[]{:S(2)}, u32[]{:S(2)}) async-start(bf16[4,4,4,32,512]{4,3,0,2,1:T(8,128)(2,1)} %bitcast.92), calls=%async_computation.2 | async-start | bytes 4194304 | tf_op jit(solution)/shard_map/all_to_all | solution.py:106
  115.4 56.5 %all-gather.2.cloned.1.call-start = ((), (), s32[]{:S(2)}) async-start(), calls=%async_computation.3 | async-start | bytes 2621440 | tf_op jit(solution)/shard_map/all_gather | solution.py:126
  171.9 78.7 %copy-start.1 = (bf16[4,16,576]{2,1,0:T(8,128)(2,1)S(1)}, bf16[4,16,576]{2,1,0:T(8,128)(2,1)}, u32[]{:S(2)}) copy-start(bf16[4,16,576]{2,1,0:T(8,128)(2,1)} %param.14) | copy-start | bytes 221188
Sparse Core Ops, SparseCore 0:
  148.4 23.4 all-gather.1
where the time goes:
time: 258 us; the launch traced here: 257 us
  blocking collectives  70.3 us (27%)
  local copies, waits for them, and re-layouts  57 us (22%)
  waiting for transfers between devices  48.8 us (19%)
  matrix products  32.6 us (13%)
  other arithmetic  23.2 us (9%)
  between operations  13.7 us (5%)
  starting transfers between devices  11.9 us (5%)
    psum x1, blocking collectives, local(): return lax.psum(partial_value, 'head').astype(jnp.bfloat16)  70.3 us
    gather x1, local copies, waits for them, and re-layouts, local(): jnp.take(latent_cache, positions.reshape(-1), axis=0)  38.1 us
    all_to_all x1, waiting for transfers between devices, local(): lax.all_to_all(finished.reshape(step_count, seq_count, per_pair, heads_lo...  25.2 us
    all_gather x1, waiting for transfers between devices, local(): lax.all_gather(head_rows, 'seq', axis=1, tiled=True)  23.6 us
    select_n x2, other arithmetic, local(): jnp.take(latent_cache, positions.reshape(-1), axis=0)  10.5 us
    unnamed x13, local copies, waits for them, and re-layouts  9.82 us
    dot_general x1, matrix products, local(): jnp.einsum('tbk,kd->tbd', lax.all_gather(head_rows, 'seq', axis=1, tiled=...  8.43 us
    dot_general x1, matrix products, attend(): jnp.einsum('tnhc,njc->tnhj', queries, cache_rows, preferred_element_type=...  8.19 us
  transfers between devices with their start and end apart: 4, of which 2 were waited for; matrix products, arithmetic and copies ran while one was open for 28% of the time, Pallas kernels for 0%

commit v1 on v0

v1 whole, which is shorter than its diff:
```python
import functools

import jax
import jax.numpy as jnp
from jax import lax
from jax.experimental import pallas as pl
from jax.experimental.pallas import tpu as pltpu
from jax.sharding import PartitionSpec as P

LATENT = 512
BLOCK = 256
LANES = 128
LOG2E = 1.4426950408889634
NEG = -1e30
VMEM_LIMIT = 56 * 1024 * 1024


def own_slots(decode_ref, slot_ref, me, sources, requests, per_pair):
    def one_source(s, carry):
        count = jnp.int32(0)
        for r in range(requests):
            row = decode_ref[s * requests + r]
            slot_ref[s * (per_pair + 1) + jnp.minimum(count, per_pair)] = row - me * requests
            count = count + jnp.where(row // requests == me, 1, 0).astype(jnp.int32)
        return carry

    lax.fori_loop(0, sources, one_source, jnp.int32(0))


def pack_kernel(sizes, me_ref, decode_ref, nope_ref, rope_ref, fresh_ref, out_ref, slots, nope_wide, rope_wide):
    sources, per_pair, steps, heads, requests, fresh_rows = sizes
    me = me_ref[0]
    pair_rows = per_pair * steps
    rope_base = heads * pair_rows
    half = heads * steps // 2
    fresh_base = rope_base + per_pair * half
    own_slots(decode_ref, slots, me, sources, requests, per_pair)

    def one_dest(s, carry):
        for j in range(per_pair):
            row = slots[s * (per_pair + 1) + j]
            for t in range(steps):
                nope_wide[pl.ds(j * steps + t, heads, stride=pair_rows), :] = nope_ref[t, row].astype(jnp.float32)
                rope_wide[pl.ds(t, heads, stride=steps), :] = jnp.concatenate(
                    [rope_ref[t, row].astype(jnp.float32)] * 2, axis=1
                )
            low = lax.broadcasted_iota(jnp.int32, (half, LANES), 1) < LANES // 2
            packed = jnp.where(low, rope_wide[0:half, :], rope_wide[half : 2 * half, :])
            out_ref[s, rope_base + j * half : rope_base + (j + 1) * half, :] = packed.astype(jnp.bfloat16)
        out_ref[s, 0:rope_base, :] = nope_wide[...].astype(jnp.bfloat16)
        return carry

    lax.fori_loop(0, sources, one_dest, jnp.int32(0))
    shape = (sources * fresh_rows, steps * requests)
    row_id = lax.broadcasted_iota(jnp.int32, shape, 0)
    col_id = lax.broadcasted_iota(jnp.int32, shape, 1)
    wanted = jnp.full(shape, -1, jnp.int32)
    for s in range(sources):
        for j in range(per_pair):
            first = s * fresh_rows + j * steps
            here = (row_id >= first) & (row_id < first + steps)
            wanted = jnp.where(here, (row_id - first) * requests + slots[s * (per_pair + 1) + j], wanted)
    pick = jnp.where(col_id == wanted, 1.0, 0.0).astype(jnp.bfloat16)
    width = fresh_ref.shape[2]
    source_rows = jnp.concatenate([fresh_ref[t] for t in range(steps)], axis=0)
    picked = jnp.dot(pick, source_rows, preferred_element_type=jnp.float32).astype(jnp.bfloat16)
    for s in range(sources):
        for c in range(-(-width // LANES)):
            piece = picked[s * fresh_rows : (s + 1) * fresh_rows, c * LANES : min((c + 1) * LANES, width)]
            if piece.shape[1] < LANES:
                piece = jnp.concatenate([piece] * (LANES // piece.shape[1]), axis=1)
            first = fresh_base + c * fresh_rows
            out_ref[s, first : first + fresh_rows, :] = piece


def attend_kernel(
    sizes, scale, me_ref, decode_ref, length_ref, recv_ref, cache_hbm, key_hbm, value_hbm, out_ref,
    slot_offset, slot_length, owner_count, pair_slot, pair_block, first_pair,
    cache, key_up, value_up, queries, fresh, part_out, part_max, part_sum, latent, sems,
):
    sources, per_pair, steps, heads, requests, fresh_rows = sizes
    width = cache.shape[0]
    pair_rows = per_pair * steps
    rope_base = heads * pair_rows
    rows = heads * steps
    half = rows // 2
    fresh_base = rope_base + per_pair * half
    group = 16 // steps
    copies = [
        pltpu.make_async_copy(key_hbm, key_up, sems.at[0]),
        pltpu.make_async_copy(cache_hbm, cache, sems.at[1]),
        pltpu.make_async_copy(value_hbm, value_up, sems.at[2]),
    ]
    for copy in copies:
        copy.start()

    me = me_ref[0]
    for o in range(sources):
        owner_count[o] = jnp.int32(0)
    total = jnp.int32(0)
    for r in range(requests):
        owner = decode_ref[me * requests + r] // requests
        at = owner_count[owner]
        owner_count[owner] = at + 1
        slot = owner * per_pair + at
        slot_offset[slot] = total
        slot_length[slot] = length_ref[me, r]
        total = total + length_ref[me, r]
    count = jnp.int32(0)
    spans = 512 // BLOCK + 1
    for slot in range(requests):
        first_block = slot_offset[slot] // BLOCK
        last_block = (slot_offset[slot] + slot_length[slot] - 1) // BLOCK
        first_pair[slot] = count
        for k in range(spans):
            pair_slot[count] = jnp.int32(slot)
            pair_block[count] = first_block + k
            count = count + jnp.where(first_block + k <= last_block, 1, 0).astype(jnp.int32)
    first_pair[requests] = count

    for o in range(sources):
        for c in range(-(-width // LANES)):
            lanes = min(LANES, width - c * LANES)
            first = fresh_base + c * fresh_rows
            fresh[o * fresh_rows : (o + 1) * fresh_rows, c * LANES : c * LANES + lanes] = recv_ref[
                o, first : first + fresh_rows, 0:lanes
            ]
        for j in range(per_pair):
            slot = o * per_pair + j
            first = rope_base + j * half
            piece = recv_ref[o, first : first + half, :]
            queries[slot * rows : slot * rows + half, LATENT:width] = piece[:, 0 : width - LATENT]
            queries[slot * rows + half : (slot + 1) * rows, LATENT:width] = piece[:, LANES - (width - LATENT) :]

    copies[0].wait()

    def absorb(i, carry):
        results = []
        for u in range(group):
            head = i * group + u
            if pair_rows % 16 == 0:
                first = pl.multiple_of(head * pair_rows, 16)
                left = jnp.concatenate([recv_ref[o, pl.ds(first, pair_rows), :] for o in range(sources)], axis=0)
            else:
                first = pl.multiple_of(i * group * pair_rows, 16)
                left = jnp.concatenate(
                    [
                        recv_ref[o, pl.ds(first, group * pair_rows), :].astype(jnp.float32)[
                            u * pair_rows : (u + 1) * pair_rows
                        ]
                        for o in range(sources)
                    ],
                    axis=0,
                ).astype(jnp.bfloat16)
            results.append(jnp.dot(left, key_up[head], preferred_element_type=jnp.float32))
        for slot in range(requests):
            tile = jnp.concatenate([res[slot * steps : (slot + 1) * steps] for res in results], axis=0)
            queries[pl.ds(pl.multiple_of(slot * rows + i * 16, 16), 16), 0:LATENT] = tile.astype(jnp.bfloat16)
        return carry

    lax.fori_loop(0, heads // group, absorb, jnp.int32(0))
    copies[1].wait()

    unroll = 2
    factor = scale * LOG2E

    def some_pairs(i, carry):
        for u in range(unroll):
            p = jnp.minimum(i * unroll + u, count - 1)
            slot = pair_slot[p]
            start = pair_block[p] * BLOCK
            low = slot_offset[slot] - start
            high = low + slot_length[slot]
            q = queries[pl.ds(pl.multiple_of(slot * rows, 16), rows), :]
            keys = cache[:, pl.ds(pl.multiple_of(start, BLOCK), BLOCK)]
            scores = jnp.dot(q, keys, preferred_element_type=jnp.float32) * factor
            token = lax.broadcasted_iota(jnp.int32, scores.shape, 1)
            scores = jnp.where((token >= low) & (token < high), scores, NEG)
            top = jnp.max(scores, axis=1, keepdims=True)
            weights = jnp.exp2(scores - top)
            part_max[p] = jnp.broadcast_to(top, (rows, LANES))
            part_sum[p] = jnp.broadcast_to(jnp.sum(weights, axis=1, keepdims=True), (rows, LANES))
            part_out[p] = lax.dot_general(
                weights.astype(jnp.bfloat16),
                keys[0:LATENT],
                (((1,), (1,)), ((), ())),
                preferred_element_type=jnp.float32,
            )
        return carry

    lax.fori_loop(0, (count + unroll - 1) // unroll, some_pairs, jnp.int32(0))

    def merge(slot, carry):
        q = queries[pl.ds(pl.multiple_of(slot * rows, 16), rows), :]
        scores = (
            lax.dot_general(q, fresh[...], (((1,), (1,)), ((), ())), preferred_element_type=jnp.float32) * factor
        )
        row_id = lax.broadcasted_iota(jnp.int32, scores.shape, 0)
        col_id = lax.broadcasted_iota(jnp.int32, scores.shape, 1)
        base = (slot // per_pair) * fresh_rows + (slot % per_pair) * steps
        scores = jnp.where((col_id >= base) & (col_id <= base + (row_id & (steps - 1))), scores, NEG)
        top = jnp.max(scores, axis=1, keepdims=True)
        first = first_pair[slot]
        last = first_pair[slot + 1] - 1
        tops = []
        for k in range(spans):
            own = part_max[jnp.minimum(first + k, last)][:, 0:1]
            own = jnp.where(first + k <= last, own, 2 * NEG)
            tops.append(own)
        highest = functools.reduce(jnp.maximum, tops, top)
        weights = jnp.exp2(scores - highest)
        norm = jnp.sum(weights, axis=1, keepdims=True)
        out = jnp.dot(weights.astype(jnp.bfloat16), fresh[:, 0:LATENT], preferred_element_type=jnp.float32)
        for k in range(spans):
            at = jnp.minimum(first + k, last)
            share = jnp.exp2(tops[k] - highest)
            norm = norm + share * part_sum[at][:, 0:1]
            out = out + share * part_out[at]
        latent[pl.ds(pl.multiple_of(slot * rows, 16), rows), :] = (out / norm).astype(jnp.bfloat16)
        return carry

    lax.fori_loop(0, requests, merge, jnp.int32(0))
    copies[2].wait()

    def project(i, carry):
        tiles = [
            latent[pl.ds(pl.multiple_of(slot * rows + i * 16, 16), 16), :].astype(jnp.float32)
            for slot in range(requests)
        ]
        for u in range(group):
            head = i * group + u
            left = jnp.concatenate([tile[u * steps : (u + 1) * steps] for tile in tiles], axis=0)
            res = jnp.dot(left.astype(jnp.bfloat16), value_up[head], preferred_element_type=jnp.float32)
            vdim = res.shape[1]
            out_ref[:, pl.ds(pl.multiple_of(head * vdim, vdim), vdim)] = res.astype(jnp.bfloat16)
        return carry

    lax.fori_loop(0, heads // group, project, jnp.int32(0))


def order_kernel(sizes, relative, me_ref, decode_ref, x_ref, out_ref, owner_count, place):
    sources, per_pair, steps, requests = sizes
    me = me_ref[0]
    rows = sources * requests

    def one_source(q, carry):
        s = me ^ q if relative else q
        for o in range(sources):
            owner_count[o] = jnp.int32(0)
        for r in range(requests):
            row = decode_ref[s * requests + r]
            owner = row // requests
            at = owner_count[owner]
            owner_count[owner] = at + 1
            place[row] = (q * requests + owner * per_pair + at) * steps
        return carry

    lax.fori_loop(0, sources, one_source, jnp.int32(0))
    narrow = (rows, LANES)
    row_id = lax.broadcasted_iota(jnp.int32, narrow, 0)

    def put(b, wanted):
        return jnp.where(row_id == b, place[b], wanted)

    wanted = lax.fori_loop(0, rows, put, jnp.zeros(narrow, jnp.int32), unroll=8)[:, 0:1]
    col_id = lax.broadcasted_iota(jnp.int32, (rows, rows * steps), 1)
    for t in range(steps):
        pick = jnp.where(col_id == wanted + t, 1.0, 0.0).astype(jnp.bfloat16)
        out_ref[t] = jnp.dot(pick, x_ref[...], preferred_element_type=jnp.float32).astype(jnp.bfloat16)


def smem():
    return pl.BlockSpec(memory_space=pltpu.SMEM)


def vmem():
    return pl.BlockSpec(memory_space=pltpu.VMEM)


def hbm():
    return pl.BlockSpec(memory_space=pl.ANY)


def local(latent_cache, lengths, decode_rows, q_nope, q_rope, new_latent, key_up, value_up, out_proj):
    sources = lax.axis_size("seq")
    groups_of_heads = lax.axis_size("head")
    me = lax.axis_index("seq")
    requests = lengths.shape[1]
    per_pair = requests // sources
    tokens, width = latent_cache.shape
    steps, _, heads, nope = q_nope.shape
    rope = q_rope.shape[3]
    scale = (nope + rope) ** (-0.5)
    fresh_rows = -(-per_pair * steps // 16) * 16
    pair_rows = per_pair * steps
    rows = heads * steps
    packed_rows = heads * pair_rows + per_pair * rows // 2 + -(-width // LANES) * fresh_rows
    sizes = (sources, per_pair, steps, heads, requests, fresh_rows)
    params = pltpu.CompilerParams(vmem_limit_bytes=VMEM_LIMIT)
    me_array = me.astype(jnp.int32).reshape(1)

    packed = pl.pallas_call(
        functools.partial(pack_kernel, sizes),
        out_shape=jax.ShapeDtypeStruct((sources, packed_rows, LANES), jnp.bfloat16),
        in_specs=[smem(), smem(), vmem(), vmem(), vmem()],
        out_specs=vmem(),
        scratch_shapes=[
            pltpu.SMEM((sources * (per_pair + 1),), jnp.int32),
            pltpu.VMEM((heads * pair_rows, LANES), jnp.float32),
            pltpu.VMEM((rows, LANES), jnp.float32),
        ],
        compiler_params=params,
        name="pack_queries",
    )(me_array, decode_rows, q_nope, q_rope, new_latent)
    received = lax.all_to_all(packed, "seq", split_axis=0, concat_axis=0, tiled=True)

    pairs = tokens // BLOCK + requests + 2
    head_rows = pl.pallas_call(
        functools.partial(attend_kernel, sizes, scale),
        out_shape=jax.ShapeDtypeStruct((requests * steps, heads * value_up.shape[2]), jnp.bfloat16),
        in_specs=[smem(), smem(), smem(), vmem(), hbm(), hbm(), hbm()],
        out_specs=vmem(),
        scratch_shapes=[
            pltpu.SMEM((requests,), jnp.int32),
            pltpu.SMEM((requests,), jnp.int32),
            pltpu.SMEM((sources,), jnp.int32),
            pltpu.SMEM((pairs,), jnp.int32),
            pltpu.SMEM((pairs,), jnp.int32),
            pltpu.SMEM((requests + 1,), jnp.int32),
            pltpu.VMEM((width, tokens), jnp.bfloat16),
            pltpu.VMEM(key_up.shape, jnp.bfloat16),
            pltpu.VMEM(value_up.shape, jnp.bfloat16),
            pltpu.VMEM((requests * rows, width), jnp.bfloat16),
            pltpu.VMEM((sources * fresh_rows, width), jnp.bfloat16),
            pltpu.VMEM((pairs, rows, LATENT), jnp.float32),
            pltpu.VMEM((pairs, rows, LANES), jnp.float32),
            pltpu.VMEM((pairs, rows, LANES), jnp.float32),
            pltpu.VMEM((requests * rows, LATENT), jnp.bfloat16),
            pltpu.SemaphoreType.DMA((3,)),
        ],
        compiler_params=params,
        name="attend",
    )(me_array, decode_rows, lengths, received, latent_cache.T, key_up, value_up)

    relative = sources == 4
    if relative:
        across = lax.ppermute(head_rows, "seq", [(i, i ^ 2) for i in range(4)])
        beside = lax.ppermute(head_rows, "seq", [(i, i ^ 1) for i in range(4)])
        beyond = lax.ppermute(across, "seq", [(i, i ^ 1) for i in range(4)])
        every_row = jnp.concatenate([head_rows, beside, across, beyond], axis=0)
    else:
        every_row = lax.all_gather(head_rows, "seq", axis=0, tiled=True)
    partial_value = jnp.dot(every_row, out_proj, preferred_element_type=jnp.float32).astype(jnp.bfloat16)
    shares = lax.all_to_all(partial_value, "head", split_axis=0, concat_axis=0, tiled=True)
    shares = shares.reshape(groups_of_heads, -1, shares.shape[1])
    summed = jnp.sum(shares.astype(jnp.float32), axis=0).astype(jnp.bfloat16)
    mixed = lax.all_gather(summed, "head", axis=0, tiled=True)
    return pl.pallas_call(
        functools.partial(order_kernel, (sources, per_pair, steps, requests), relative),
        out_shape=jax.ShapeDtypeStruct((steps, sources * requests, out_proj.shape[1]), jnp.bfloat16),
        in_specs=[smem(), smem(), vmem()],
        out_specs=vmem(),
        scratch_shapes=[pltpu.SMEM((sources,), jnp.int32), pltpu.SMEM((sources * requests,), jnp.int32)],
        compiler_params=params,
        name="order_rows",
    )(me_array, decode_rows, mixed)


def solution(mesh):
    return jax.shard_map(
        local,
        mesh=mesh,
        in_specs=(
            P(("groups", "seq"), None),
            P("groups", None),
            P("groups"),
            P(None, ("groups", "seq"), "head", None),
            P(None, ("groups", "seq"), "head", None),
            P(None, ("groups", "seq"), None),
            P("head", None, None),
            P("head", None, None),
            P("head", "seq"),
        ),
        out_specs=P(None, "groups", "seq"),
        check_vma=False,
    )
```

time: 258 us -> 125 us (0.48)
  local copies, waits for them, and re-layouts: 57 us -> 0 us
  Pallas kernels: 0 us -> 34.1 us
  waiting for transfers between devices: 48.8 us -> 14.9 us
  matrix products: 32.6 us -> 9.32 us
  other arithmetic: 23.2 us -> 0.16 us
  between operations: 13.7 us -> 0.04 us
  starting transfers between devices: 11.9 us -> 0.14 us
  blocking collectives: 70.3 us -> 65.8 us
    psum x1 -> x0, blocking collectives: 70.3 us -> none  [local(): return lax.psum(partial_value, 'head').astype(jnp.bfloat16)]
    all_to_all x0 -> x2, blocking collectives: none -> 46.1 us  [the longest x1 28.7 us: local(): lax.all_to_all(partial_value, 'head', split_axis=0, concat_axis=0, tiled=...]
    gather x6 -> x0, local copies, waits for them, and re-layouts: 42 us -> none  [the longest x1 38.1 us: local(): jnp.take(latent_cache, positions.reshape(-1), axis=0)]
    pallas_call x0 -> x3, Pallas kernels: none -> 34.1 us  [the longest x1 26.9 us: local(): pl.pallas_call(functools.partial(attend_kernel, sizes, scale), out_shape=...]
    all_to_all x3 -> x0, waiting for transfers between devices: 25.2 us -> none  [the longest x1 25.2 us: local(): lax.all_to_all(finished.reshape(step_count, seq_count, per_pair, heads_lo...]
    all_gather x1 -> x0, waiting for transfers between devices: 23.6 us -> none  [local(): lax.all_gather(head_rows, 'seq', axis=1, tiled=True)]
    dot_general x6 -> x1, matrix products: 29.7 us -> 9.32 us  [local(): jnp.dot(every_row, out_proj, preferred_element_type=jnp.float32)]
    all_gather x0 -> x1, blocking collectives: none -> 19.6 us  [local(): mixed = lax.all_gather(summed, 'head', axis=0, tiled=True)]
  transfers between devices with their start and end apart: 4 -> 3, of which waited for: 2 -> 2; matrix products, arithmetic and copies ran while one was open for 28% -> 0% of each run, Pallas kernels for 0% -> 0%
where the time goes in v1:
time: 125 us; the launch traced here: 124 us
  blocking collectives  65.8 us (53%)
  Pallas kernels  34.1 us (27%)
  waiting for transfers between devices  14.9 us (12%)
  matrix products  9.32 us (7%)
    all_to_all x1, blocking collectives, local(): lax.all_to_all(partial_value, 'head', split_axis=0, concat_axis=0, tiled=...  28.7 us
    pallas_call x1, Pallas kernels, local(): pl.pallas_call(functools.partial(attend_kernel, sizes, scale), out_shape=...  26.9 us
    all_gather x1, blocking collectives, local(): mixed = lax.all_gather(summed, 'head', axis=0, tiled=True)  19.6 us
    all_to_all x1, blocking collectives, local(): lax.all_to_all(packed, 'seq', split_axis=0, concat_axis=0, tiled=True)  17.4 us
    ppermute x1, waiting for transfers between devices, local(): across = lax.ppermute(head_rows, 'seq', [(i, i ^ 2) for i in range(4)])  13 us
    dot_general x1, matrix products, local(): jnp.dot(every_row, out_proj, preferred_element_type=jnp.float32)  9.32 us
    pallas_call x1, Pallas kernels, local(): pl.pallas_call(functools.partial(pack_kernel, sizes), out_shape=jax.Shape...  3.69 us
    pallas_call x1, Pallas kernels, local(): pl.pallas_call(functools.partial(order_kernel, (sources, per_pair, steps,...  3.5 us
  transfers between devices with their start and end apart: 3, of which 2 were waited for; matrix products, arithmetic and copies ran while one was open for 0% of the time, Pallas kernels for 0%

profile of v1, /device:TPU:0, one launch (start us, length us, event | category | flops | bytes accessed | tf_op | source)
XLA Modules:
  0.0 124.5 jit_solution(15898756539126375623)
XLA Ops:
  0.0 3.7 %pack_queries.1 = bf16[4,848,128]{2,1,0:T(8,128)(2,1)} custom-call(s32[1]{0:T(128)} %bitcast.me_ref, s32[64]{0:T(128)} %decode_ref.5, bf16[4,16,32,128]{3,2,1,0:T(8,128)(2,1)} %nope_ref.1, bf16[4,16,32,64]{3,2,1,0:T(8,128)(2,1)} %rope_ref.1, bf16[4,16,576]{2,1,0:T(8,128)(2,1)} %fresh_ref.1), custom_call_target="tpu_custom_call" | custom-call | tf_op jit(solution)/shard_map/pack_queries/pallas_call | solution.py:302
  3.7 17.4 %all_to_all.14.recv_ref = bf16[4,848,128]{2,1,0:T(8,128)(2,1)} all-to-all(bf16[4,848,128]{2,1,0:T(8,128)(2,1)} %pack_queries.1), channel_id=1, replica_groups=mesh['groups'=2,'seq'=4,'head'=4] {'seq'}, dimensions={0} | all-to-all | bytes 1736704 | tf_op jit(solution)/shard_map/all_to_all | solution.py:315
  21.1 26.9 %attend.1 = bf16[64,4096]{1,0:T(8,128)(2,1)} custom-call(s32[1]{0:T(128)} %bitcast.me_ref, s32[64]{0:T(128)} %decode_ref.5, s32[4,16]{1,0:T(4,128)} %length_ref.1, bf16[4,848,128]{2,1,0:T(8,128)(2,1)} %all_to_all.14.recv_ref, bf16[576,4096]{1,0:T(8,128)(2,1)} %bitcast.4, bf16[32,128,512]{2,1,0:T(8,128)(2,1)} %key_hbm.1, bf16[32,512,128]{2,1,0:T(8,128)(2,1)} %value_hbm.1), custom_call_target="tpu_custom_call" | custom-call | tf_op jit(solution)/shard_map/attend/pallas_call | solution.py:318
  48.1 0.1 collective-permute-start.1
  48.1 0.1 collective-permute-start
  48.2 13.0 %collective-permute-done.1 = bf16[64,4096]{1,0:T(8,128)(2,1)S(1)} collective-permute-done((bf16[64,4096]{1,0:T(8,128)(2,1)}, bf16[64,4096]{1,0:T(8,128)(2,1)S(1)}, u32[]{:S(2)}, u32[]{:S(2)}) %collective-permute-start.1) | collective-permute-done | bytes 524320 | tf_op jit(solution)/shard_map/ppermute | solution.py:347
  61.3 0.0 collective-permute-start.2
  61.3 0.0 collective-permute-done
  61.3 1.9 %collective-permute-done.2 = bf16[64,4096]{1,0:T(8,128)(2,1)S(1)} collective-permute-done((bf16[64,4096]{1,0:T(8,128)(2,1)S(1)}, bf16[64,4096]{1,0:T(8,128)(2,1)S(1)}, u32[]{:S(2)}, u32[]{:S(2)}) %collective-permute-start.2) | collective-permute-done | bytes 524320 | tf_op jit(solution)/shard_map/ppermute | solution.py:349
  63.2 9.3 %convolution_convert_fusion = bf16[256,1792]{1,0:T(8,128)(2,1)S(1)} fusion(bf16[4096,1792]{1,0:T(8,128)(2,1)} %param.17, bf16[64,4096]{1,0:T(8,128)(2,1)S(1)} %collective-permute-done.2, bf16[64,4096]{1,0:T(8,128)(2,1)S(1)} %collective-permute-done.1, bf16[64,4096]{1,0:T(8,128)(2,1)S(1)} %collective-permute-done, bf16[64,4096]{1,0:T(8,128)(2,1)} %attend.1), kind=kOutput, calls=%fused_computation | convolution fusion | flops 3766943744 | bytes 17694720 | tf_op jit(solution)/shard_map/dot_general | solution.py:353
  72.5 28.7 %all_to_all.15 = bf16[4,64,1792]{2,1,0:T(8,128)(2,1)S(1)} all-to-all(bf16[4,64,1792]{2,1,0:T(8,128)(2,1)S(1)} %bitcast.5), channel_id=1, replica_groups=mesh['groups'=2,'seq'=4,'head'=4] {'head'}, dimensions={0} | all-to-all | bytes 1835008 | tf_op jit(solution)/shard_map/all_to_all | solution.py:354
  101.2 0.2 reduce_sum.12
  101.4 19.6 %all_gather.3.x_ref = bf16[256,1792]{1,0:T(8,128)(2,1)} all-gather(bf16[64,1792]{1,0:T(8,128)(2,1)S(1)} %reduce_sum.12), channel_id=1, replica_groups=mesh['groups'=2,'seq'=4,'head'=4] {'head'}, dimensions={0}, use_global_device_ids=true | all-gather | bytes 1146880 | tf_op jit(solution)/shard_map/all_gather | solution.py:357
  121.0 3.5 %order_rows.1 = bf16[4,64,1792]{2,1,0:T(8,128)(2,1)} custom-call(s32[1]{0:T(128)} %bitcast.me_ref, s32[64]{0:T(128)} %decode_ref.5, bf16[256,1792]{1,0:T(8,128)(2,1)} %all_gather.3.x_ref), custom_call_target="tpu_custom_call" | custom-call | tf_op jit(solution)/shard_map/order_rows/pallas_call | solution.py:358
Async XLA Ops:
  48.1 13.2 %collective-permute-start.1 = (bf16[64,4096]{1,0:T(8,128)(2,1)}, bf16[64,4096]{1,0:T(8,128)(2,1)S(1)}, u32[]{:S(2)}, u32[]{:S(2)}) collective-permute-start(bf16[64,4096]{1,0:T(8,128)(2,1)} %attend.1), channel_id=1, source_target_pairs={{0,8},{4,12},{8,0},{12,4},{1,9},{5,13},{9,1},{13,5},{2,10},{6,14},... | collective-permute-start | bytes 1572872 | tf_op jit(solution)/shard_map/ppermute | solution.py:347
  48.1 13.1 %collective-permute-start = (bf16[64,4096]{1,0:T(8,128)(2,1)}, bf16[64,4096]{1,0:T(8,128)(2,1)S(1)}, u32[]{:S(2)}, u32[]{:S(2)}) collective-permute-start(bf16[64,4096]{1,0:T(8,128)(2,1)} %attend.1), channel_id=1, source_target_pairs={{0,4},{4,0},{8,12},{12,8},{1,5},{5,1},{9,13},{13,9},{2,6},{6,2},{1... | collective-permute-start | bytes 1572872 | tf_op jit(solution)/shard_map/ppermute | solution.py:348
  61.3 1.9 %collective-permute-start.2 = (bf16[64,4096]{1,0:T(8,128)(2,1)S(1)}, bf16[64,4096]{1,0:T(8,128)(2,1)S(1)}, u32[]{:S(2)}, u32[]{:S(2)}) collective-permute-start(bf16[64,4096]{1,0:T(8,128)(2,1)S(1)} %collective-permute-done.1), channel_id=1, source_target_pairs={{0,4},{4,0},{8,12},{12,8},{1,5},{5,1},{9,13},{13,9},{2,6},{6,2},{1... | collective-permute-start | bytes 1572872 | tf_op jit(solution)/shard_map/ppermute | solution.py:349

commit v2 on v1

v2 whole, which is shorter than its diff:
```python
import functools

import jax
import jax.numpy as jnp
from jax import lax
from jax.experimental import pallas as pl
from jax.experimental.pallas import tpu as pltpu
from jax.sharding import PartitionSpec as P

LATENT = 512
BLOCK = 256
LANES = 128
LOG2E = 1.4426950408889634
NEG = -1e30


def own_slots(decode_ref, slot_ref, me, sources, requests, per_pair):
    shift = requests.bit_length() - 1

    def one_source(s, carry):
        count = jnp.int32(0)
        for r in range(requests):
            row = decode_ref[s * requests + r]
            slot_ref[s * (per_pair + 1) + jnp.minimum(count, per_pair)] = row & (requests - 1)
            count = count + jnp.where((row >> shift) == me, 1, 0).astype(jnp.int32)
        return carry

    lax.fori_loop(0, sources, one_source, jnp.int32(0))


def pack_kernel(sizes, relative, me_ref, decode_ref, nope_ref, rope_ref, fresh_ref, *rest):
    sources, per_pair, steps, heads, requests, fresh_rows = sizes
    out_refs, (slots, nope_wide, rope_wide) = rest[:-3], rest[-3:]
    me = me_ref[0]
    pair_rows = per_pair * steps
    rope_base = heads * pair_rows
    half = heads * steps // 2
    fresh_base = rope_base + per_pair * half
    own_slots(decode_ref, slots, me, sources, requests, per_pair)

    def one_dest(s, out_ref, e):
        for j in range(per_pair):
            row = slots[s * (per_pair + 1) + j]
            for t in range(steps):
                nope_wide[pl.ds(j * steps + t, heads, stride=pair_rows), :] = nope_ref[t, row].astype(jnp.float32)
                rope_wide[pl.ds(t, heads, stride=steps), :] = jnp.concatenate(
                    [rope_ref[t, row].astype(jnp.float32)] * 2, axis=1
                )
            low = lax.broadcasted_iota(jnp.int32, (half, LANES), 1) < LANES // 2
            packed = jnp.where(low, rope_wide[0:half, :], rope_wide[half : 2 * half, :])
            out_ref[e, rope_base + j * half : rope_base + (j + 1) * half, :] = packed.astype(jnp.bfloat16)
        out_ref[e, 0:rope_base, :] = nope_wide[...].astype(jnp.bfloat16)

    if relative:
        dests = [me ^ k for k in range(sources)]
        for k in range(sources):
            one_dest(dests[k], out_refs[k], 0)
    else:
        dests = list(range(sources))

        def step(s, carry):
            one_dest(s, out_refs[0], s)
            return carry

        lax.fori_loop(0, sources, step, jnp.int32(0))
    shape = (sources * fresh_rows, steps * requests)
    row_id = lax.broadcasted_iota(jnp.int32, shape, 0)
    col_id = lax.broadcasted_iota(jnp.int32, shape, 1)
    wanted = jnp.full(shape, -1, jnp.int32)
    for k in range(sources):
        for j in range(per_pair):
            first = k * fresh_rows + j * steps
            here = (row_id >= first) & (row_id < first + steps)
            wanted = jnp.where(here, (row_id - first) * requests + slots[dests[k] * (per_pair + 1) + j], wanted)
    pick = jnp.where(col_id == wanted, 1.0, 0.0).astype(jnp.bfloat16)
    width = fresh_ref.shape[2]
    source_rows = jnp.concatenate([fresh_ref[t] for t in range(steps)], axis=0)
    picked = jnp.dot(pick, source_rows, preferred_element_type=jnp.float32).astype(jnp.bfloat16)
    for k in range(sources):
        for c in range(-(-width // LANES)):
            piece = picked[k * fresh_rows : (k + 1) * fresh_rows, c * LANES : min((c + 1) * LANES, width)]
            if piece.shape[1] < LANES:
                piece = jnp.concatenate([piece] * (LANES // piece.shape[1]), axis=1)
            first = fresh_base + c * fresh_rows
            if relative:
                out_refs[k][0, first : first + fresh_rows, :] = piece
            else:
                out_refs[0][k, first : first + fresh_rows, :] = piece


def attend_kernel(sizes, scale, relative, base, recv_count, me_ref, decode_ref, length_ref, *rest):
    sources, per_pair, steps, heads, requests, fresh_rows = sizes
    recv_refs = rest[:recv_count]
    (
        cache, key_up, value_up, out_ref,
        slot_offset, slot_length, owner_count, pair_slot, pair_start, first_pair,
        queries, fresh, part_out, part_max, part_sum, latent,
    ) = rest[recv_count:]
    owners = [(ref, e) for ref in recv_refs for e in range(ref.shape[0])]
    here = len(owners)
    slots = here * per_pair
    width, tokens = cache.shape
    pair_rows = per_pair * steps
    rope_base = heads * pair_rows
    rows = heads * steps
    half = rows // 2
    fresh_base = rope_base + per_pair * half
    group = 16 // steps
    shift = requests.bit_length() - 1

    me = me_ref[0]
    for o in range(sources):
        owner_count[o] = jnp.int32(0)
    total = jnp.int32(0)
    for r in range(requests):
        owner = decode_ref[me * requests + r] >> shift
        at = owner_count[owner]
        owner_count[owner] = at + 1
        e = (owner ^ me) - base if relative else owner
        slot = jnp.where((e >= 0) & (e < here), e * per_pair + at, slots)
        length = length_ref[me, r]
        slot_offset[slot] = total
        slot_length[slot] = length
        total = total + length
    count = jnp.int32(0)
    spans = 512 // BLOCK + 1
    for slot in range(slots):
        start = slot_offset[slot] & ~(LANES - 1)
        end = slot_offset[slot] + slot_length[slot]
        first_pair[slot] = count
        for k in range(spans):
            pair_slot[count] = jnp.int32(slot)
            pair_start[count] = start + k * BLOCK
            count = count + jnp.where(start + k * BLOCK < end, 1, 0).astype(jnp.int32)
    first_pair[slots] = count

    for e in range(here):
        ref, at = owners[e]
        for c in range(-(-width // LANES)):
            lanes = min(LANES, width - c * LANES)
            first = fresh_base + c * fresh_rows
            fresh[e * fresh_rows : (e + 1) * fresh_rows, c * LANES : c * LANES + lanes] = ref[
                at, first : first + fresh_rows, 0:lanes
            ]
        for j in range(per_pair):
            slot = e * per_pair + j
            first = rope_base + j * half
            piece = ref[at, first : first + half, :]
            queries[slot * rows : slot * rows + half, LATENT:width] = piece[:, 0 : width - LATENT]
            queries[slot * rows + half : (slot + 1) * rows, LATENT:width] = piece[:, LANES - (width - LATENT) :]

    def absorb(i, carry):
        results = []
        for u in range(group):
            head = i * group + u
            if pair_rows % 16 == 0:
                first = pl.multiple_of(head * pair_rows, 16)
                left = jnp.concatenate([ref[at, pl.ds(first, pair_rows), :] for ref, at in owners], axis=0)
            else:
                first = pl.multiple_of(i * group * pair_rows, 16)
                left = jnp.concatenate(
                    [
                        ref[at, pl.ds(first, group * pair_rows), :].astype(jnp.float32)[
                            u * pair_rows : (u + 1) * pair_rows
                        ]
                        for ref, at in owners
                    ],
                    axis=0,
                ).astype(jnp.bfloat16)
            results.append(jnp.dot(left, key_up[head], preferred_element_type=jnp.float32))
        for slot in range(slots):
            tile = jnp.concatenate([res[slot * steps : (slot + 1) * steps] for res in results], axis=0)
            queries[pl.ds(pl.multiple_of(slot * rows + i * 16, 16), 16), 0:LATENT] = tile.astype(jnp.bfloat16)
        return carry

    lax.fori_loop(0, heads // group, absorb, jnp.int32(0))

    unroll = 2
    factor = scale * LOG2E

    def some_pairs(i, carry):
        for u in range(unroll):
            p = jnp.minimum(i * unroll + u, count - 1)
            slot = pair_slot[p]
            start = pair_start[p]
            read = jnp.minimum(start, tokens - BLOCK)
            low = jnp.maximum(slot_offset[slot], start) - read
            high = jnp.minimum(slot_offset[slot] + slot_length[slot], start + BLOCK) - read
            q = queries[pl.ds(pl.multiple_of(slot * rows, 16), rows), :]
            keys = cache[:, pl.ds(pl.multiple_of(read, LANES), BLOCK)]
            scores = jnp.dot(q, keys, preferred_element_type=jnp.float32) * factor
            token = lax.broadcasted_iota(jnp.int32, scores.shape, 1)
            scores = jnp.where((token >= low) & (token < high), scores, NEG)
            top = jnp.max(scores, axis=1, keepdims=True)
            weights = jnp.exp2(scores - top)
            part_max[p] = jnp.broadcast_to(top, (rows, LANES))
            part_sum[p] = jnp.broadcast_to(jnp.sum(weights, axis=1, keepdims=True), (rows, LANES))
            part_out[p] = lax.dot_general(
                weights.astype(jnp.bfloat16),
                keys[0:LATENT],
                (((1,), (1,)), ((), ())),
                preferred_element_type=jnp.float32,
            )
        return carry

    lax.fori_loop(0, (count + unroll - 1) // unroll, some_pairs, jnp.int32(0))

    def merge(slot, carry):
        q = queries[pl.ds(pl.multiple_of(slot * rows, 16), rows), :]
        scores = (
            lax.dot_general(q, fresh[...], (((1,), (1,)), ((), ())), preferred_element_type=jnp.float32) * factor
        )
        row_id = lax.broadcasted_iota(jnp.int32, scores.shape, 0)
        col_id = lax.broadcasted_iota(jnp.int32, scores.shape, 1)
        first_col = (slot // per_pair) * fresh_rows + (slot % per_pair) * steps
        scores = jnp.where(
            (col_id >= first_col) & (col_id <= first_col + (row_id & (steps - 1))), scores, NEG
        )
        top = jnp.max(scores, axis=1, keepdims=True)
        first = first_pair[slot]
        last = first_pair[slot + 1] - 1
        tops = []
        for k in range(spans):
            own = part_max[jnp.minimum(first + k, last)][:, 0:1]
            own = jnp.where(first + k <= last, own, 2 * NEG)
            tops.append(own)
        highest = functools.reduce(jnp.maximum, tops, top)
        weights = jnp.exp2(scores - highest)
        norm = jnp.sum(weights, axis=1, keepdims=True)
        out = jnp.dot(weights.astype(jnp.bfloat16), fresh[:, 0:LATENT], preferred_element_type=jnp.float32)
        for k in range(spans):
            at = jnp.minimum(first + k, last)
            share = jnp.exp2(tops[k] - highest)
            norm = norm + share * part_sum[at][:, 0:1]
            out = out + share * part_out[at]
        latent[pl.ds(pl.multiple_of(slot * rows, 16), rows), :] = (out / norm).astype(jnp.bfloat16)
        return carry

    lax.fori_loop(0, slots, merge, jnp.int32(0))

    def project(i, carry):
        tiles = [
            latent[pl.ds(pl.multiple_of(slot * rows + i * 16, 16), 16), :].astype(jnp.float32)
            for slot in range(slots)
        ]
        count_rows = slots * steps
        vdim = value_up.shape[2]
        for u in range(0, group, 2):
            head = i * group + u
            left = jnp.concatenate(
                [tile[v * steps : (v + 1) * steps] for v in (u, u + 1) for tile in tiles], axis=0
            ).astype(jnp.bfloat16)
            right = jnp.concatenate([value_up[head], value_up[head + 1]], axis=1)
            res = jnp.dot(left, right, preferred_element_type=jnp.float32)
            both = jnp.concatenate([res[:count_rows, :vdim], res[count_rows:, vdim:]], axis=1)
            out_ref[:, pl.ds(pl.multiple_of(head * vdim, vdim), 2 * vdim)] = both.astype(jnp.bfloat16)
        return carry

    lax.fori_loop(0, heads // group, project, jnp.int32(0))


def place_kernel(sizes, relative, me_ref, decode_ref, out_ref, owner_count, place):
    sources, per_pair, steps, requests = sizes
    me = me_ref[0]
    rows = sources * requests
    shift = requests.bit_length() - 1

    def one_source(s, carry):
        for o in range(sources):
            owner_count[o] = jnp.int32(0)
        for r in range(requests):
            row = decode_ref[s * requests + r]
            owner = row >> shift
            at = owner_count[owner]
            owner_count[owner] = at + 1
            if relative:
                e = owner ^ s
                at_row = (e >> 1) * (2 * sources * per_pair) + (me ^ s) * (2 * per_pair) + (e & 1) * per_pair + at
            else:
                at_row = s * requests + owner * per_pair + at
            place[row] = at_row * steps
        return carry

    lax.fori_loop(0, sources, one_source, jnp.int32(0))
    narrow = (rows, LANES)
    row_id = lax.broadcasted_iota(jnp.int32, narrow, 0)

    def put(b, wanted):
        return jnp.where(row_id == b, place[b], wanted)

    wanted = lax.fori_loop(0, rows, put, jnp.zeros(narrow, jnp.int32), unroll=8)[:, 0:1]
    col_id = lax.broadcasted_iota(jnp.int32, (rows, rows * steps), 1)
    for t in range(steps):
        out_ref[t] = jnp.where(col_id == wanted + t, 1.0, 0.0).astype(jnp.bfloat16)


def order_kernel(pieces, z_ref, pick_ref, *rest):
    out_ref, x = rest[2 * pieces], rest[2 * pieces + 1]
    if pieces == 0:
        x_ref, out_ref = rest
        for t in range(pick_ref.shape[0]):
            out_ref[t] = jnp.dot(pick_ref[t], x_ref[...], preferred_element_type=jnp.float32).astype(jnp.bfloat16)
        return
    inner = (z_ref[0] == 1) | (z_ref[0] == 2)
    rows = x.shape[0] // pieces

    @pl.when(inner)
    def _():
        for i in range(pieces):
            x[i * rows : (i + 1) * rows, :] = rest[2 * i][...]

    @pl.when(jnp.logical_not(inner))
    def _():
        for i in range(pieces):
            x[i * rows : (i + 1) * rows, :] = rest[2 * i + 1][...]

    for t in range(pick_ref.shape[0]):
        out_ref[t] = jnp.dot(pick_ref[t], x[...], preferred_element_type=jnp.float32).astype(jnp.bfloat16)


def project_kernel(pieces, *rest):
    parts, weight, outs, x = rest[:4], rest[4], rest[5 : 5 + pieces], rest[5 + pieces]
    rows = parts[0].shape[0]
    for q in range(4):
        x[q * rows : (q + 1) * rows, :] = parts[q][...]
    out_rows = outs[0].shape[0]

    def tile(n, carry):
        cols = pl.ds(pl.multiple_of(n * BLOCK, BLOCK), BLOCK)
        res = jnp.dot(x[...], weight[:, cols], preferred_element_type=jnp.float32).astype(jnp.bfloat16)
        for i in range(pieces):
            outs[i][:, cols] = res[i * out_rows : (i + 1) * out_rows]
        return carry

    lax.fori_loop(0, weight.shape[1] // BLOCK, tile, jnp.int32(0))


def smem():
    return pl.BlockSpec(memory_space=pltpu.SMEM)


def vmem():
    return pl.BlockSpec(memory_space=pltpu.VMEM)


def limit(mib):
    return pltpu.CompilerParams(vmem_limit_bytes=mib * 1024 * 1024)


def cost(microseconds):
    return pl.CostEstimate(
        flops=int(microseconds * 1.0e9), bytes_accessed=int(microseconds * 3.0e6), transcendentals=0
    )


def flip(x, axis, distance):
    size = lax.axis_size(axis)
    return lax.ppermute(x, axis, [(i, i ^ distance) for i in range(size)])


def line_sum(piece):
    inward = lax.ppermute(piece, "head", [(0, 1), (3, 2)])
    pair = (piece.astype(jnp.float32) + inward.astype(jnp.float32)).astype(jnp.bfloat16)
    crossed = lax.ppermute(pair, "head", [(1, 2), (2, 1)])
    whole = (pair.astype(jnp.float32) + crossed.astype(jnp.float32)).astype(jnp.bfloat16)
    outward = lax.ppermute(whole, "head", [(1, 0), (2, 3)])
    return whole, outward


def local(latent_cache, lengths, decode_rows, q_nope, q_rope, new_latent, key_up, value_up, out_proj):
    sources = lax.axis_size("seq")
    head_devices = lax.axis_size("head")
    relative = sources == 4 and head_devices == 4
    requests = lengths.shape[1]
    per_pair = requests // sources
    tokens, width = latent_cache.shape
    steps, _, heads, nope = q_nope.shape
    scale = (nope + q_rope.shape[3]) ** (-0.5)
    fresh_rows = -(-per_pair * steps // 16) * 16
    pair_rows = per_pair * steps
    rows = heads * steps
    columns = out_proj.shape[1]
    packed_rows = heads * pair_rows + per_pair * rows // 2 + -(-width // LANES) * fresh_rows
    sizes = (sources, per_pair, steps, heads, requests, fresh_rows)
    me = lax.axis_index("seq").astype(jnp.int32).reshape(1)
    z = lax.axis_index("head").astype(jnp.int32).reshape(1)
    cache = latent_cache.T

    outs, each = (sources, 1) if relative else (1, sources)
    packed = pl.pallas_call(
        functools.partial(pack_kernel, sizes, relative),
        out_shape=[jax.ShapeDtypeStruct((each, packed_rows, LANES), jnp.bfloat16)] * outs,
        in_specs=[smem(), smem(), vmem(), vmem(), vmem()],
        out_specs=[vmem()] * outs,
        scratch_shapes=[
            pltpu.SMEM((sources * (per_pair + 1),), jnp.int32),
            pltpu.VMEM((heads * pair_rows, LANES), jnp.float32),
            pltpu.VMEM((rows, LANES), jnp.float32),
        ],
        compiler_params=limit(12),
        cost_estimate=cost(3),
        name="pack_queries",
    )(me, decode_rows, q_nope, q_rope, new_latent)

    def attend(received, base):
        here = sum(part.shape[0] for part in received)
        slots = here * per_pair
        pairs = slots * (512 // BLOCK + 1) + 1
        return pl.pallas_call(
            functools.partial(attend_kernel, sizes, scale, relative, base, len(received)),
            out_shape=jax.ShapeDtypeStruct((slots * steps, heads * value_up.shape[2]), jnp.bfloat16),
            in_specs=[smem(), smem(), smem()] + [vmem()] * (len(received) + 3),
            out_specs=vmem(),
            scratch_shapes=[
                pltpu.SMEM((slots + 1,), jnp.int32),
                pltpu.SMEM((slots + 1,), jnp.int32),
                pltpu.SMEM((sources,), jnp.int32),
                pltpu.SMEM((pairs,), jnp.int32),
                pltpu.SMEM((pairs,), jnp.int32),
                pltpu.SMEM((slots + 1,), jnp.int32),
                pltpu.VMEM((slots * rows, width), jnp.bfloat16),
                pltpu.VMEM((here * fresh_rows, width), jnp.bfloat16),
                pltpu.VMEM((pairs, rows, LATENT), jnp.float32),
                pltpu.VMEM((pairs, rows, LANES), jnp.float32),
                pltpu.VMEM((pairs, rows, LANES), jnp.float32),
                pltpu.VMEM((slots * rows, LATENT), jnp.bfloat16),
            ],
            compiler_params=limit(32),
            cost_estimate=cost(14),
            name="attend",
        )(me, decode_rows, lengths, *received, cache, key_up, value_up)

    pick = pl.pallas_call(
        functools.partial(place_kernel, (sources, per_pair, steps, requests), relative),
        out_shape=jax.ShapeDtypeStruct((steps, sources * requests, steps * sources * requests), jnp.bfloat16),
        in_specs=[smem(), smem()],
        out_specs=vmem(),
        scratch_shapes=[pltpu.SMEM((sources,), jnp.int32), pltpu.SMEM((sources * requests,), jnp.int32)],
        compiler_params=limit(12),
        cost_estimate=cost(2),
        name="place_rows",
    )(me, decode_rows)

    def order(pieces, arrays, scratch):
        return pl.pallas_call(
            functools.partial(order_kernel, pieces),
            out_shape=jax.ShapeDtypeStruct((steps, sources * requests, columns), jnp.bfloat16),
            in_specs=[smem()] + [vmem()] * (1 + len(arrays)),
            out_specs=vmem(),
            scratch_shapes=scratch,
            compiler_params=limit(16),
            cost_estimate=cost(2),
            name="order_rows",
        )(z, pick, *arrays)

    if not relative:
        received = lax.all_to_all(packed[0], "seq", split_axis=0, concat_axis=0, tiled=True)
        every_row = lax.all_gather(attend([received], 0), "seq", axis=0, tiled=True)
        partial_value = jnp.dot(every_row, out_proj, preferred_element_type=jnp.float32).astype(jnp.bfloat16)
        shares = lax.all_to_all(partial_value, "head", split_axis=0, concat_axis=0, tiled=True)
        shares = shares.reshape(head_devices, -1, columns)
        summed = jnp.sum(shares.astype(jnp.float32), axis=0).astype(jnp.bfloat16)
        return order(0, [lax.all_gather(summed, "head", axis=0, tiled=True)], [])

    pieces = 2

    def project(parts):
        part_rows = parts[0].shape[0]
        return pl.pallas_call(
            functools.partial(project_kernel, pieces),
            out_shape=[jax.ShapeDtypeStruct((4 * part_rows // pieces, columns), jnp.bfloat16)] * pieces,
            in_specs=[vmem()] * 5,
            out_specs=[vmem()] * pieces,
            scratch_shapes=[pltpu.VMEM((4 * part_rows, out_proj.shape[0]), jnp.bfloat16)],
            compiler_params=limit(24),
            cost_estimate=cost(6),
            name="project_out",
        )(*parts, out_proj)

    received = [packed[0]] + [flip(packed[k], "seq", k) for k in range(1, 4)]
    near = attend(received[:2], 0)
    near_parts = [near] + [flip(near, "seq", k) for k in range(1, 4)]
    far = attend(received[2:], 2)
    far_across = flip(far, "seq", 2)
    far_parts = [far, flip(far, "seq", 1), far_across, flip(far_across, "seq", 1)]
    sums = [line_sum(piece) for piece in project(near_parts)]
    sums += [line_sum(piece) for piece in project(far_parts)]
    arrays = [array for pair in sums for array in pair]
    return order(len(sums), arrays, [pltpu.VMEM((steps * sources * requests, columns), jnp.bfloat16)])


def solution(mesh):
    return jax.shard_map(
        local,
        mesh=mesh,
        in_specs=(
            P(("groups", "seq"), None),
            P("groups", None),
            P("groups"),
            P(None, ("groups", "seq"), "head", None),
            P(None, ("groups", "seq"), "head", None),
            P(None, ("groups", "seq"), None),
            P("head", None, None),
            P("head", None, None),
            P("head", "seq"),
        ),
        out_specs=P(None, "groups", "seq"),
        check_vma=False,
    )
```

time: 125 us -> 99.7 us (0.80)
  blocking collectives: 65.8 us -> 0 us
  starting transfers between devices: 0.14 us -> 28.9 us
  waiting for transfers between devices: 14.9 us -> 27 us
  matrix products: 9.32 us -> 0 us
  local copies, waits for them, and re-layouts: 0 us -> 5.84 us
  Pallas kernels: 34.1 us -> 36.9 us
    all_to_all x2 -> x0, blocking collectives: 46.1 us -> none  [the longest x1 28.7 us: local(): lax.all_to_all(partial_value, 'head', split_axis=0, concat_axis=0, tiled=...]
    ppermute x3 -> x21, starting transfers between devices: 0.14 us -> 28.9 us  [the longest x4 13.6 us: line_sum(): inward = lax.ppermute(piece, 'head', [(0, 1), (3, 2)])]
    all_gather x1 -> x0, blocking collectives: 19.6 us -> none  [local(): mixed = lax.all_gather(summed, 'head', axis=0, tiled=True)]
    ppermute x3 -> x21, waiting for transfers between devices: 14.9 us -> 27 us  [the longest x4 15.1 us: line_sum(): outward = lax.ppermute(whole, 'head', [(1, 0), (2, 3)])]
    dot_general x1 -> x0, matrix products: 9.32 us -> none  [local(): jnp.dot(every_row, out_proj, preferred_element_type=jnp.float32)]
    unnamed x0 -> x26, local copies, waits for them, and re-layouts: none -> 5.84 us
    pallas_call x3 -> x7, Pallas kernels: 34.1 us -> 36.9 us  [the longest x2 25.9 us: attend(): pl.pallas_call(functools.partial(attend_kernel, sizes, scale, relative, b...]
  transfers between devices with their start and end apart: 3 -> 21, of which waited for: 2 -> 7; matrix products, arithmetic and copies ran while one was open for 0% -> 0% of each run, Pallas kernels for 0% -> 34%
where the time goes in v2:
time: 99.7 us; the launch traced here: 99.5 us
  Pallas kernels  36.9 us (37%)
  starting transfers between devices  28.9 us (29%)
  waiting for transfers between devices  27 us (27%)
  local copies, waits for them, and re-layouts  5.84 us (6%)
    pallas_call x2, Pallas kernels, attend(): pl.pallas_call(functools.partial(attend_kernel, sizes, scale, relative, b...  25.9 us
    ppermute x4, waiting for transfers between devices, line_sum(): outward = lax.ppermute(whole, 'head', [(1, 0), (2, 3)])  15.1 us
    ppermute x4, starting transfers between devices, line_sum(): inward = lax.ppermute(piece, 'head', [(0, 1), (3, 2)])  13.6 us
    ppermute x4, waiting for transfers between devices, line_sum(): inward = lax.ppermute(piece, 'head', [(0, 1), (3, 2)])  11.8 us
    ppermute x9, starting transfers between devices, flip(): return lax.ppermute(x, axis, [(i, i ^ distance) for i in range(size)])  7.42 us
    pallas_call x2, Pallas kernels, project(): pl.pallas_call(functools.partial(project_kernel, pieces), out_shape=[jax....  6.72 us
    unnamed x26, local copies, waits for them, and re-layouts  5.84 us
    ppermute x4, starting transfers between devices, line_sum(): outward = lax.ppermute(whole, 'head', [(1, 0), (2, 3)])  5.17 us
  transfers between devices with their start and end apart: 21, of which 7 were waited for; matrix products, arithmetic and copies ran while one was open for 0% of the time, Pallas kernels for 34%

profile of v2, /device:TPU:0, one launch (start us, length us, event | category | flops | bytes accessed | tf_op | source)
XLA Modules:
  0.0 99.5 jit_solution(2291650380152805734)
XLA Ops:
  0.0 1.0 %copy-done.3 = bf16[4,16,32,128]{3,2,1,0:T(8,128)(2,1)S(1)} copy-done((bf16[4,16,32,128]{3,2,1,0:T(8,128)(2,1)S(1)}, bf16[4,16,32,128]{3,2,1,0:T(8,128)(2,1)}, u32[]{:S(2)}) %copy-start.3) | copy-done | bytes 524312
  1.0 1.0 %copy-done.4 = bf16[4,16,32,64]{3,2,1,0:T(8,128)(2,1)S(1)} copy-done((bf16[4,16,32,64]{3,2,1,0:T(8,128)(2,1)S(1)}, bf16[4,16,32,64]{3,2,1,0:T(8,128)(2,1)}, u32[]{:S(2)}) %copy-start.4) | copy-done | bytes 262168
  2.1 0.9 copy-done.5
  3.0 0.7 copy-done.7
  3.6 1.5 %pack_queries.1 = (bf16[1,848,128]{2,1,0:T(8,128)(2,1)S(1)}, bf16[1,848,128]{2,1,0:T(8,128)(2,1)S(1)}, bf16[1,848,128]{2,1,0:T(8,128)(2,1)S(1)}, bf16[1,848,128]{2,1,0:T(8,128)(2,1)S(1)}) custom-call(s32[1]{0:T(128)} %bitcast.1.me_ref, s32[64]{0:T(128)S(1)} %copy-done.7, bf16[4,16,32,128]{3,2,1,0:T(8,128)(2,1)S(1)} %copy-done.3, ...), custom_call_target="tpu_custom_call" | custom-call | flops 3000000000 | bytes 9000000 | tf_op jit(solution)/shard_map/pack_queries/pallas_call | solution.py:390
  5.1 0.5 collective-permute-start
  5.7 2.6 %collective-permute-start.10 = (bf16[1,848,128]{2,1,0:T(8,128)(2,1)S(1)}, bf16[1,848,128]{2,1,0:T(8,128)(2,1)S(1)}, u32[]{:S(2)}, u32[]{:S(2)}) collective-permute-start(bf16[1,848,128]{2,1,0:T(8,128)(2,1)S(1)} %get-tuple-element.17), channel_id=1, source_target_pairs={{0,8},{4,12},{8,0},{12,4},{1,9},{5,13},{9,1},{13,5},{2,10},{6,14},... | collective-permute-start | bytes 651272 | tf_op jit(solution)/shard_map/ppermute | solution.py:358
  8.3 0.1 collective-permute-start.11
  8.4 2.2 %copy-done.2 = bf16[32,512,128]{2,1,0:T(8,128)(2,1)S(1)} copy-done((bf16[32,512,128]{2,1,0:T(8,128)(2,1)S(1)}, bf16[32,512,128]{2,1,0:T(8,128)(2,1)}, u32[]{:S(2)}) %copy-start.2) | copy-done | bytes 4194328
  10.6 12.4 %attend.2.rest_0_ = bf16[32,4096]{1,0:T(8,128)(2,1)S(1)} custom-call(s32[1]{0:T(128)} %bitcast.1.me_ref, s32[64]{0:T(128)S(1)} %copy-done.8, s32[4,16]{1,0:T(4,128)S(1)} %copy-done.6, bf16[1,848,128]{2,1,0:T(8,128)(2,1)S(1)} %get-tuple-element.13.rest_0_, bf16[1,848,128]{2,1,0:T(8,128)(2,1)S(1)} %collective-permute-done.rest_1_, ...), custom_call_target="tpu_custom_call" | custom-call | flops 14000000000 | bytes 42000000 | tf_op jit(solution)/shard_map/attend/pallas_call | solution.py:409
  22.9 1.7 %collective-permute-start.3 = (bf16[32,4096]{1,0:T(8,128)(2,1)S(1)}, bf16[32,4096]{1,0:T(8,128)(2,1)S(1)}, u32[]{:S(2)}, u32[]{:S(2)}) collective-permute-start(bf16[32,4096]{1,0:T(8,128)(2,1)S(1)} %attend.2.rest_0_), channel_id=1, source_target_pairs={{0,12},{4,8},{8,4},{12,0},{1,13},{5,9},{9,5},{13,1},{2,14},{6,10},... | collective-permute-start | bytes 786440 | tf_op jit(solution)/shard_map/ppermute | solution.py:358
  24.7 0.9 collective-permute-start.2
  25.5 0.0 collective-permute-start.1
  25.6 13.5 %attend.3.rest_0_ = bf16[32,4096]{1,0:T(8,128)(2,1)S(1)} custom-call(s32[1]{0:T(128)} %bitcast.1.me_ref, s32[64]{0:T(128)S(1)} %copy-done.8, s32[4,16]{1,0:T(4,128)S(1)} %copy-done.6, bf16[1,848,128]{2,1,0:T(8,128)(2,1)S(1)} %collective-permute-done.10.rest_0_, bf16[1,848,128]{2,1,0:T(8,128)(2,1)S(1)} %collective-permute-done.11.rest_1_, ...), custom_call_target="tpu_custom_call" | custom-call | flops 14000000000 | bytes 42000000 | tf_op jit(solution)/shard_map/attend/pallas_call | solution.py:409
  39.1 1.2 %collective-permute-start.13 = (bf16[32,4096]{1,0:T(8,128)(2,1)S(1)}, bf16[32,4096]{1,0:T(8,128)(2,1)S(1)}, u32[]{:S(2)}, u32[]{:S(2)}) collective-permute-start(bf16[32,4096]{1,0:T(8,128)(2,1)S(1)} %attend.3.rest_0_), channel_id=1, source_target_pairs={{0,8},{4,12},{8,0},{12,4},{1,9},{5,13},{9,1},{13,5},{2,10},{6,14},... | collective-permute-start | bytes 786440 | tf_op jit(solution)/shard_map/ppermute | solution.py:358
  40.4 3.4 %project_out.2 = (bf16[64,1792]{1,0:T(8,128)(2,1)S(1)}, bf16[64,1792]{1,0:T(8,128)(2,1)S(1)}) custom-call(bf16[32,4096]{1,0:T(8,128)(2,1)S(1)} %attend.2.rest_0_, bf16[32,4096]{1,0:T(8,128)(2,1)S(1)} %collective-permute-done.1.rest_1_, bf16[32,4096]{1,0:T(8,128)(2,1)S(1)} %collective-permute-done.2.rest_2_, ...), custom_call_target="tpu_custom_call" | custom-call | flops 6000000000 | bytes 18000000 | tf_op jit(solution)/shard_map/project_out/pallas_call | solution.py:469
  43.8 3.5 %collective-permute-start.4 = (bf16[64,1792]{1,0:T(8,128)(2,1)S(1)}, bf16[64,1792]{1,0:T(8,128)(2,1)S(1)}, u32[]{:S(2)}, u32[]{:S(2)}) collective-permute-start(bf16[64,1792]{1,0:T(8,128)(2,1)S(1)} %get-tuple-element.15), channel_id=1, source_target_pairs={{0,1},{3,2},{4,5},{7,6},{8,9},{11,10},{12,13},{15,14},{16,17},{19,... | collective-permute-start | bytes 688136 | tf_op jit(solution)/shard_map/ppermute | solution.py:362
  47.3 0.1 collective-permute-start.12
  47.4 1.6 %collective-permute-start.7 = (bf16[64,1792]{1,0:T(8,128)(2,1)S(1)}, bf16[64,1792]{1,0:T(8,128)(2,1)S(1)}, u32[]{:S(2)}, u32[]{:S(2)}) collective-permute-start(bf16[64,1792]{1,0:T(8,128)(2,1)S(1)} %get-tuple-element.16), channel_id=1, source_target_pairs={{0,1},{3,2},{4,5},{7,6},{8,9},{11,10},{12,13},{15,14},{16,17},{19,... | collective-permute-start | bytes 688136 | tf_op jit(solution)/shard_map/ppermute | solution.py:362
  49.0 0.3 collective-permute-start.14
  49.2 4.0 %collective-permute-done.4 = bf16[64,1792]{1,0:T(8,128)(2,1)S(1)} collective-permute-done((bf16[64,1792]{1,0:T(8,128)(2,1)S(1)}, bf16[64,1792]{1,0:T(8,128)(2,1)S(1)}, u32[]{:S(2)}, u32[]{:S(2)}) %collective-permute-start.4) | collective-permute-done | bytes 229408 | tf_op jit(solution)/shard_map/ppermute | solution.py:362
  53.2 0.1 add_convert_fusion.7
  53.3 0.7 collective-permute-start.5
  53.9 3.6 %collective-permute-done.7 = bf16[64,1792]{1,0:T(8,128)(2,1)S(1)} collective-permute-done((bf16[64,1792]{1,0:T(8,128)(2,1)S(1)}, bf16[64,1792]{1,0:T(8,128)(2,1)S(1)}, u32[]{:S(2)}, u32[]{:S(2)}) %collective-permute-start.7) | collective-permute-done | bytes 229408 | tf_op jit(solution)/shard_map/ppermute | solution.py:362
  57.5 0.1 add_convert_fusion.5
  57.6 0.7 collective-permute-start.8
  58.3 3.4 %project_out.3 = (bf16[64,1792]{1,0:T(8,128)(2,1)S(1)}, bf16[64,1792]{1,0:T(8,128)(2,1)S(1)}) custom-call(bf16[32,4096]{1,0:T(8,128)(2,1)S(1)} %attend.3.rest_0_, bf16[32,4096]{1,0:T(8,128)(2,1)S(1)} %collective-permute-done.12.rest_1_, bf16[32,4096]{1,0:T(8,128)(2,1)S(1)} %collective-permute-done.13.rest_2_, ...), custom_call_target="tpu_custom_call" | custom-call | flops 6000000000 | bytes 18000000 | tf_op jit(solution)/shard_map/project_out/pallas_call | solution.py:469
  61.6 7.2 %collective-permute-start.15 = (bf16[64,1792]{1,0:T(8,128)(2,1)S(1)}, bf16[64,1792]{1,0:T(8,128)(2,1)S(1)}, u32[]{:S(2)}, u32[]{:S(2)}) collective-permute-start(bf16[64,1792]{1,0:T(8,128)(2,1)S(1)} %get-tuple-element.19), channel_id=1, source_target_pairs={{0,1},{3,2},{4,5},{7,6},{8,9},{11,10},{12,13},{15,14},{16,17},{19,... | collective-permute-start | bytes 688136 | tf_op jit(solution)/shard_map/ppermute | solution.py:362
  68.9 1.3 %collective-permute-start.18 = (bf16[64,1792]{1,0:T(8,128)(2,1)S(1)}, bf16[64,1792]{1,0:T(8,128)(2,1)S(1)}, u32[]{:S(2)}, u32[]{:S(2)}) collective-permute-start(bf16[64,1792]{1,0:T(8,128)(2,1)S(1)} %get-tuple-element.20), channel_id=1, source_target_pairs={{0,1},{3,2},{4,5},{7,6},{8,9},{11,10},{12,13},{15,14},{16,17},{19,... | collective-permute-start | bytes 688136 | tf_op jit(solution)/shard_map/ppermute | solution.py:362
  70.2 0.1 add_convert_fusion.6.rest_0_
  70.2 1.3 %collective-permute-start.6 = (bf16[64,1792]{1,0:T(8,128)(2,1)S(1)}, bf16[64,1792]{1,0:T(8,128)(2,1)S(1)}, u32[]{:S(2)}, u32[]{:S(2)}) collective-permute-start(bf16[64,1792]{1,0:T(8,128)(2,1)S(1)} %add_convert_fusion.6.rest_0_), channel_id=1, source_target_pairs={{1,0},{2,3},{5,4},{6,7},{9,8},{10,11},{13,12},{14,15},{17,16},{18,... | collective-permute-start | bytes 688136 | tf_op jit(solution)/shard_map/ppermute | solution.py:366
  71.6 0.1 add_convert_fusion.4.rest_2_
  71.6 1.3 %collective-permute-start.9 = (bf16[64,1792]{1,0:T(8,128)(2,1)S(1)}, bf16[64,1792]{1,0:T(8,128)(2,1)S(1)}, u32[]{:S(2)}, u32[]{:S(2)}) collective-permute-start(bf16[64,1792]{1,0:T(8,128)(2,1)S(1)} %add_convert_fusion.4.rest_2_), channel_id=1, source_target_pairs={{1,0},{2,3},{5,4},{6,7},{9,8},{10,11},{13,12},{14,15},{17,16},{18,... | collective-permute-start | bytes 688136 | tf_op jit(solution)/shard_map/ppermute | solution.py:366
  72.9 2.0 %collective-permute-done.15 = bf16[64,1792]{1,0:T(8,128)(2,1)S(1)} collective-permute-done((bf16[64,1792]{1,0:T(8,128)(2,1)S(1)}, bf16[64,1792]{1,0:T(8,128)(2,1)S(1)}, u32[]{:S(2)}, u32[]{:S(2)}) %collective-permute-start.15) | collective-permute-done | bytes 229408 | tf_op jit(solution)/shard_map/ppermute | solution.py:362
  74.9 0.1 add_convert_fusion.3
  74.9 0.7 collective-permute-start.16
  75.6 2.4 %collective-permute-done.18 = bf16[64,1792]{1,0:T(8,128)(2,1)S(1)} collective-permute-done((bf16[64,1792]{1,0:T(8,128)(2,1)S(1)}, bf16[64,1792]{1,0:T(8,128)(2,1)S(1)}, u32[]{:S(2)}, u32[]{:S(2)}) %collective-permute-start.18) | collective-permute-done | bytes 229408 | tf_op jit(solution)/shard_map/ppermute | solution.py:362
  78.0 0.1 add_convert_fusion.1
  78.0 0.7 collective-permute-start.19
  78.7 0.1 add_convert_fusion.2.rest_4_
  78.8 1.3 %collective-permute-start.17 = (bf16[64,1792]{1,0:T(8,128)(2,1)S(1)}, bf16[64,1792]{1,0:T(8,128)(2,1)S(1)}, u32[]{:S(2)}, u32[]{:S(2)}) collective-permute-start(bf16[64,1792]{1,0:T(8,128)(2,1)S(1)} %add_convert_fusion.2.rest_4_), channel_id=1, source_target_pairs={{1,0},{2,3},{5,4},{6,7},{9,8},{10,11},{13,12},{14,15},{17,16},{18,... | collective-permute-start | bytes 688136 | tf_op jit(solution)/shard_map/ppermute | solution.py:366
  80.1 0.1 add_convert_fusion.rest_6_
  80.2 1.3 %collective-permute-start.20 = (bf16[64,1792]{1,0:T(8,128)(2,1)S(1)}, bf16[64,1792]{1,0:T(8,128)(2,1)S(1)}, u32[]{:S(2)}, u32[]{:S(2)}) collective-permute-start(bf16[64,1792]{1,0:T(8,128)(2,1)S(1)} %add_convert_fusion.rest_6_), channel_id=1, source_target_pairs={{1,0},{2,3},{5,4},{6,7},{9,8},{10,11},{13,12},{14,15},{17,16},{18,... | collective-permute-start | bytes 688136 | tf_op jit(solution)/shard_map/ppermute | solution.py:366
  81.5 1.1 %place_rows.1.pick_ref = bf16[4,64,256]{2,1,0:T(8,128)(2,1)S(1)} custom-call(s32[1]{0:T(128)} %bitcast.1.me_ref, s32[64]{0:T(128)S(1)} %copy-done.8), custom_call_target="tpu_custom_call" | custom-call | flops 2000000000 | bytes 6000000 | tf_op jit(solution)/shard_map/place_rows/pallas_call | solution.py:433
  82.6 1.1 %collective-permute-done.9.rest_3_ = bf16[64,1792]{1,0:T(8,128)(2,1)S(1)} collective-permute-done((bf16[64,1792]{1,0:T(8,128)(2,1)S(1)}, bf16[64,1792]{1,0:T(8,128)(2,1)S(1)}, u32[]{:S(2)}, u32[]{:S(2)}) %collective-permute-start.9) | collective-permute-done | bytes 229408 | tf_op jit(solution)/shard_map/ppermute | solution.py:366
  83.7 11.5 %collective-permute-done.17.rest_5_ = bf16[64,1792]{1,0:T(8,128)(2,1)S(1)} collective-permute-done((bf16[64,1792]{1,0:T(8,128)(2,1)S(1)}, bf16[64,1792]{1,0:T(8,128)(2,1)S(1)}, u32[]{:S(2)}, u32[]{:S(2)}) %collective-permute-start.17) | collective-permute-done | bytes 229408 | tf_op jit(solution)/shard_map/ppermute | solution.py:366
  95.2 2.6 %collective-permute-done.20.rest_7_ = bf16[64,1792]{1,0:T(8,128)(2,1)S(1)} collective-permute-done((bf16[64,1792]{1,0:T(8,128)(2,1)S(1)}, bf16[64,1792]{1,0:T(8,128)(2,1)S(1)}, u32[]{:S(2)}, u32[]{:S(2)}) %collective-permute-start.20) | collective-permute-done | bytes 229408 | tf_op jit(solution)/shard_map/ppermute | solution.py:366
  97.7 1.7 %order_rows.1 = bf16[4,64,1792]{2,1,0:T(8,128)(2,1)} custom-call(s32[1]{0:T(128)} %bitcast.z_ref, bf16[4,64,256]{2,1,0:T(8,128)(2,1)S(1)} %place_rows.1.pick_ref, bf16[64,1792]{1,0:T(8,128)(2,1)S(1)} %add_convert_fusion.6.rest_0_, bf16[64,1792]{1,0:T(8,128)(2,1)S(1)} %collective-permute-done.6.rest_1_, bf16[64,1792]{1,0:T(8,128)(2,1)S(1)} %add_convert_fusion.4.rest_2_, ...), custom_call_target="tpu_custom_call" | custom-call | flops 2000000000 | bytes 6000000 | tf_op jit(solution)/shard_map/order_rows/pallas_call | solution.py:445
  (36 shorter events, 0.1 us)
Async XLA Ops:
  0.0 1.0 %copy-start.3 = (bf16[4,16,32,128]{3,2,1,0:T(8,128)(2,1)S(1)}, bf16[4,16,32,128]{3,2,1,0:T(8,128)(2,1)}, u32[]{:S(2)}) copy-start(bf16[4,16,32,128]{3,2,1,0:T(8,128)(2,1)} %nope_ref.1) | copy-start | bytes 1572868
  1.0 1.0 %copy-start.4 = (bf16[4,16,32,64]{3,2,1,0:T(8,128)(2,1)S(1)}, bf16[4,16,32,64]{3,2,1,0:T(8,128)(2,1)}, u32[]{:S(2)}) copy-start(bf16[4,16,32,64]{3,2,1,0:T(8,128)(2,1)} %rope_ref.1) | copy-start | bytes 786436
  2.1 0.9 copy-start.5
  3.0 0.7 copy-start.7
  3.6 4.7 %copy-start = (bf16[4096,576]{0,1:T(8,128)(2,1)S(1)}, bf16[4096,576]{0,1:T(8,128)(2,1)}, u32[]{:S(2)}) copy-start(bf16[4096,576]{0,1:T(8,128)(2,1)} %param.9) | copy-start | bytes 14155780
  3.6 4.7 %copy-start.1 = (bf16[32,128,512]{2,1,0:T(8,128)(2,1)S(1)}, bf16[32,128,512]{2,1,0:T(8,128)(2,1)}, u32[]{:S(2)}) copy-start(bf16[32,128,512]{2,1,0:T(8,128)(2,1)} %rest_3_.3) | copy-start | bytes 12582916
  3.6 4.7 %copy-start.6 = (s32[4,16]{1,0:T(4,128)S(1)}, s32[4,16]{1,0:T(4,128)}, u32[]{:S(2)}) copy-start(s32[4,16]{1,0:T(4,128)} %length_ref.3) | copy-start | bytes 772
  3.6 4.7 %copy-start.8 = (s32[64]{0:T(128)S(1)}, s32[64]{0:T(128)}, u32[]{:S(2)}) copy-start(s32[64]{0:T(128)} %decode_ref.7) | copy-start | bytes 772
  5.1 3.2 %collective-permute-start = (bf16[1,848,128]{2,1,0:T(8,128)(2,1)S(1)}, bf16[1,848,128]{2,1,0:T(8,128)(2,1)S(1)}, u32[]{:S(2)}, u32[]{:S(2)}) collective-permute-start(bf16[1,848,128]{2,1,0:T(8,128)(2,1)S(1)} %get-tuple-element.14), channel_id=1, source_target_pairs={{0,4},{4,0},{8,12},{12,8},{1,5},{5,1},{9,13},{13,9},{2,6},{6,2},{1... | collective-permute-start | bytes 651272 | tf_op jit(solution)/shard_map/ppermute | solution.py:358
  5.7 19.9 %collective-permute-start.10 = (bf16[1,848,128]{2,1,0:T(8,128)(2,1)S(1)}, bf16[1,848,128]{2,1,0:T(8,128)(2,1)S(1)}, u32[]{:S(2)}, u32[]{:S(2)}) collective-permute-start(bf16[1,848,128]{2,1,0:T(8,128)(2,1)S(1)} %get-tuple-element.17), channel_id=1, source_target_pairs={{0,8},{4,12},{8,0},{12,4},{1,9},{5,13},{9,1},{13,5},{2,10},{6,14},... | collective-permute-start | bytes 651272 | tf_op jit(solution)/shard_map/ppermute | solution.py:358
  8.3 17.3 %collective-permute-start.11 = (bf16[1,848,128]{2,1,0:T(8,128)(2,1)S(1)}, bf16[1,848,128]{2,1,0:T(8,128)(2,1)S(1)}, u32[]{:S(2)}, u32[]{:S(2)}) collective-permute-start(bf16[1,848,128]{2,1,0:T(8,128)(2,1)S(1)} %get-tuple-element.18), channel_id=1, source_target_pairs={{0,12},{4,8},{8,4},{12,0},{1,13},{5,9},{9,5},{13,1},{2,14},{6,10},... | collective-permute-start | bytes 651272 | tf_op jit(solution)/shard_map/ppermute | solution.py:358
  8.4 2.2 %copy-start.2 = (bf16[32,512,128]{2,1,0:T(8,128)(2,1)S(1)}, bf16[32,512,128]{2,1,0:T(8,128)(2,1)}, u32[]{:S(2)}) copy-start(bf16[32,512,128]{2,1,0:T(8,128)(2,1)} %rest_4_.6) | copy-start | bytes 12582916
  10.5 29.8 %slice-start = ((s8[14680064]{0:T(1024)(128)(4,1)}), s8[4194304]{0:T(1024)(128)(4,1)S(1)}, s32[]{:S(2)}) async-start(s8[14680064]{0:T(1024)(128)(4,1)} %bitcast.3), calls=%async_computation | async-start | bytes 8388608
  10.5 29.8 %slice-start.1 = ((s8[14680064]{0:T(1024)(128)(4,1)}), s8[4194304]{0:T(1024)(128)(4,1)S(1)}, s32[]{:S(2)}) async-start(s8[14680064]{0:T(1024)(128)(4,1)} %bitcast.3), calls=%async_computation.1 | async-start | bytes 8388608
  10.6 29.8 %slice-start.2 = ((s8[14680064]{0:T(1024)(128)(4,1)}), s8[4194304]{0:T(1024)(128)(4,1)S(1)}, s32[]{:S(2)}) async-start(s8[14680064]{0:T(1024)(128)(4,1)} %bitcast.3), calls=%async_computation.2 | async-start | bytes 8388608
  22.9 17.5 %slice-start.3 = ((s8[14680064]{0:T(1024)(128)(4,1)}), s8[2097152]{0:T(1024)(128)(4,1)S(1)}, s32[]{:S(2)}) async-start(s8[14680064]{0:T(1024)(128)(4,1)} %bitcast.3), calls=%async_computation.3 | async-start | bytes 4194304
  22.9 17.4 %collective-permute-start.3 = (bf16[32,4096]{1,0:T(8,128)(2,1)S(1)}, bf16[32,4096]{1,0:T(8,128)(2,1)S(1)}, u32[]{:S(2)}, u32[]{:S(2)}) collective-permute-start(bf16[32,4096]{1,0:T(8,128)(2,1)S(1)} %attend.2.rest_0_), channel_id=1, source_target_pairs={{0,12},{4,8},{8,4},{12,0},{1,13},{5,9},{9,5},{13,1},{2,14},{6,10},... | collective-permute-start | bytes 786440 | tf_op jit(solution)/shard_map/ppermute | solution.py:358
  24.7 15.7 %collective-permute-start.2 = (bf16[32,4096]{1,0:T(8,128)(2,1)S(1)}, bf16[32,4096]{1,0:T(8,128)(2,1)S(1)}, u32[]{:S(2)}, u32[]{:S(2)}) collective-permute-start(bf16[32,4096]{1,0:T(8,128)(2,1)S(1)} %attend.2.rest_0_), channel_id=1, source_target_pairs={{0,8},{4,12},{8,0},{12,4},{1,9},{5,13},{9,1},{13,5},{2,10},{6,14},... | collective-permute-start | bytes 786440 | tf_op jit(solution)/shard_map/ppermute | solution.py:358
  25.5 14.8 %collective-permute-start.1 = (bf16[32,4096]{1,0:T(8,128)(2,1)S(1)}, bf16[32,4096]{1,0:T(8,128)(2,1)S(1)}, u32[]{:S(2)}, u32[]{:S(2)}) collective-permute-start(bf16[32,4096]{1,0:T(8,128)(2,1)S(1)} %attend.2.rest_0_), channel_id=1, source_target_pairs={{0,4},{4,0},{8,12},{12,8},{1,5},{5,1},{9,13},{13,9},{2,6},{6,2},{1... | collective-permute-start | bytes 786440 | tf_op jit(solution)/shard_map/ppermute | solution.py:358
  39.1 9.8 %collective-permute-start.13 = (bf16[32,4096]{1,0:T(8,128)(2,1)S(1)}, bf16[32,4096]{1,0:T(8,128)(2,1)S(1)}, u32[]{:S(2)}, u32[]{:S(2)}) collective-permute-start(bf16[32,4096]{1,0:T(8,128)(2,1)S(1)} %attend.3.rest_0_), channel_id=1, source_target_pairs={{0,8},{4,12},{8,0},{12,4},{1,9},{5,13},{9,1},{13,5},{2,10},{6,14},... | collective-permute-start | bytes 786440 | tf_op jit(solution)/shard_map/ppermute | solution.py:358
  43.8 9.4 %collective-permute-start.4 = (bf16[64,1792]{1,0:T(8,128)(2,1)S(1)}, bf16[64,1792]{1,0:T(8,128)(2,1)S(1)}, u32[]{:S(2)}, u32[]{:S(2)}) collective-permute-start(bf16[64,1792]{1,0:T(8,128)(2,1)S(1)} %get-tuple-element.15), channel_id=1, source_target_pairs={{0,1},{3,2},{4,5},{7,6},{8,9},{11,10},{12,13},{15,14},{16,17},{19,... | collective-permute-start | bytes 688136 | tf_op jit(solution)/shard_map/ppermute | solution.py:362
  47.3 11.0 %collective-permute-start.12 = (bf16[32,4096]{1,0:T(8,128)(2,1)S(1)}, bf16[32,4096]{1,0:T(8,128)(2,1)S(1)}, u32[]{:S(2)}, u32[]{:S(2)}) collective-permute-start(bf16[32,4096]{1,0:T(8,128)(2,1)S(1)} %attend.3.rest_0_), channel_id=1, source_target_pairs={{0,4},{4,0},{8,12},{12,8},{1,5},{5,1},{9,13},{13,9},{2,6},{6,2},{1... | collective-permute-start | bytes 786440 | tf_op jit(solution)/shard_map/ppermute | solution.py:358
  47.4 10.1 %collective-permute-start.7 = (bf16[64,1792]{1,0:T(8,128)(2,1)S(1)}, bf16[64,1792]{1,0:T(8,128)(2,1)S(1)}, u32[]{:S(2)}, u32[]{:S(2)}) collective-permute-start(bf16[64,1792]{1,0:T(8,128)(2,1)S(1)} %get-tuple-element.16), channel_id=1, source_target_pairs={{0,1},{3,2},{4,5},{7,6},{8,9},{11,10},{12,13},{15,14},{16,17},{19,... | collective-permute-start | bytes 688136 | tf_op jit(solution)/shard_map/ppermute | solution.py:362
  49.0 9.3 %collective-permute-start.14 = (bf16[32,4096]{1,0:T(8,128)(2,1)S(1)}, bf16[32,4096]{1,0:T(8,128)(2,1)S(1)}, u32[]{:S(2)}, u32[]{:S(2)}) collective-permute-start(bf16[32,4096]{1,0:T(8,128)(2,1)S(1)} %collective-permute-done.13.rest_2_), channel_id=1, source_target_pairs={{0,4},{4,0},{8,12},{12,8},{1,5},{5,1},{9,13},{13,9},{2,6},{6,2},{1... | collective-permute-start | bytes 786440 | tf_op jit(solution)/shard_map/ppermute | solution.py:358
  53.3 16.9 %collective-permute-start.5 = (bf16[64,1792]{1,0:T(8,128)(2,1)S(1)}, bf16[64,1792]{1,0:T(8,128)(2,1)S(1)}, u32[]{:S(2)}, u32[]{:S(2)}) collective-permute-start(bf16[64,1792]{1,0:T(8,128)(2,1)S(1)} %add_convert_fusion.7), channel_id=1, source_target_pairs={{1,2},{2,1},{5,6},{6,5},{9,10},{10,9},{13,14},{14,13},{17,18},{18,... | collective-permute-start | bytes 688136 | tf_op jit(solution)/shard_map/ppermute | solution.py:364
  57.6 14.0 %collective-permute-start.8 = (bf16[64,1792]{1,0:T(8,128)(2,1)S(1)}, bf16[64,1792]{1,0:T(8,128)(2,1)S(1)}, u32[]{:S(2)}, u32[]{:S(2)}) collective-permute-start(bf16[64,1792]{1,0:T(8,128)(2,1)S(1)} %add_convert_fusion.5), channel_id=1, source_target_pairs={{1,2},{2,1},{5,6},{6,5},{9,10},{10,9},{13,14},{14,13},{17,18},{18,... | collective-permute-start | bytes 688136 | tf_op jit(solution)/shard_map/ppermute | solution.py:364
  61.6 13.3 %collective-permute-start.15 = (bf16[64,1792]{1,0:T(8,128)(2,1)S(1)}, bf16[64,1792]{1,0:T(8,128)(2,1)S(1)}, u32[]{:S(2)}, u32[]{:S(2)}) collective-permute-start(bf16[64,1792]{1,0:T(8,128)(2,1)S(1)} %get-tuple-element.19), channel_id=1, source_target_pairs={{0,1},{3,2},{4,5},{7,6},{8,9},{11,10},{12,13},{15,14},{16,17},{19,... | collective-permute-start | bytes 688136 | tf_op jit(solution)/shard_map/ppermute | solution.py:362
  68.9 9.1 %collective-permute-start.18 = (bf16[64,1792]{1,0:T(8,128)(2,1)S(1)}, bf16[64,1792]{1,0:T(8,128)(2,1)S(1)}, u32[]{:S(2)}, u32[]{:S(2)}) collective-permute-start(bf16[64,1792]{1,0:T(8,128)(2,1)S(1)} %get-tuple-element.20), channel_id=1, source_target_pairs={{0,1},{3,2},{4,5},{7,6},{8,9},{11,10},{12,13},{15,14},{16,17},{19,... | collective-permute-start | bytes 688136 | tf_op jit(solution)/shard_map/ppermute | solution.py:362
  70.2 12.3 %collective-permute-start.6 = (bf16[64,1792]{1,0:T(8,128)(2,1)S(1)}, bf16[64,1792]{1,0:T(8,128)(2,1)S(1)}, u32[]{:S(2)}, u32[]{:S(2)}) collective-permute-start(bf16[64,1792]{1,0:T(8,128)(2,1)S(1)} %add_convert_fusion.6.rest_0_), channel_id=1, source_target_pairs={{1,0},{2,3},{5,4},{6,7},{9,8},{10,11},{13,12},{14,15},{17,16},{18,... | collective-permute-start | bytes 688136 | tf_op jit(solution)/shard_map/ppermute | solution.py:366
  71.6 12.0 %collective-permute-start.9 = (bf16[64,1792]{1,0:T(8,128)(2,1)S(1)}, bf16[64,1792]{1,0:T(8,128)(2,1)S(1)}, u32[]{:S(2)}, u32[]{:S(2)}) collective-permute-start(bf16[64,1792]{1,0:T(8,128)(2,1)S(1)} %add_convert_fusion.4.rest_2_), channel_id=1, source_target_pairs={{1,0},{2,3},{5,4},{6,7},{9,8},{10,11},{13,12},{14,15},{17,16},{18,... | collective-permute-start | bytes 688136 | tf_op jit(solution)/shard_map/ppermute | solution.py:366
  74.9 3.8 %collective-permute-start.16 = (bf16[64,1792]{1,0:T(8,128)(2,1)S(1)}, bf16[64,1792]{1,0:T(8,128)(2,1)S(1)}, u32[]{:S(2)}, u32[]{:S(2)}) collective-permute-start(bf16[64,1792]{1,0:T(8,128)(2,1)S(1)} %add_convert_fusion.3), channel_id=1, source_target_pairs={{1,2},{2,1},{5,6},{6,5},{9,10},{10,9},{13,14},{14,13},{17,18},{18,... | collective-permute-start | bytes 688136 | tf_op jit(solution)/shard_map/ppermute | solution.py:364
  78.0 2.1 %collective-permute-start.19 = (bf16[64,1792]{1,0:T(8,128)(2,1)S(1)}, bf16[64,1792]{1,0:T(8,128)(2,1)S(1)}, u32[]{:S(2)}, u32[]{:S(2)}) collective-permute-start(bf16[64,1792]{1,0:T(8,128)(2,1)S(1)} %add_convert_fusion.1), channel_id=1, source_target_pairs={{1,2},{2,1},{5,6},{6,5},{9,10},{10,9},{13,14},{14,13},{17,18},{18,... | collective-permute-start | bytes 688136 | tf_op jit(solution)/shard_map/ppermute | solution.py:364
  78.8 16.4 %collective-permute-start.17 = (bf16[64,1792]{1,0:T(8,128)(2,1)S(1)}, bf16[64,1792]{1,0:T(8,128)(2,1)S(1)}, u32[]{:S(2)}, u32[]{:S(2)}) collective-permute-start(bf16[64,1792]{1,0:T(8,128)(2,1)S(1)} %add_convert_fusion.2.rest_4_), channel_id=1, source_target_pairs={{1,0},{2,3},{5,4},{6,7},{9,8},{10,11},{13,12},{14,15},{17,16},{18,... | collective-permute-start | bytes 688136 | tf_op jit(solution)/shard_map/ppermute | solution.py:366
  80.2 17.5 %collective-permute-start.20 = (bf16[64,1792]{1,0:T(8,128)(2,1)S(1)}, bf16[64,1792]{1,0:T(8,128)(2,1)S(1)}, u32[]{:S(2)}, u32[]{:S(2)}) collective-permute-start(bf16[64,1792]{1,0:T(8,128)(2,1)S(1)} %add_convert_fusion.rest_6_), channel_id=1, source_target_pairs={{1,0},{2,3},{5,4},{6,7},{9,8},{10,11},{13,12},{14,15},{17,16},{18,... | collective-permute-start | bytes 688136 | tf_op jit(solution)/shard_map/ppermute | solution.py:366

commit v3 on v2

--- a/solution.py
+++ b/solution.py
@@ -28,13 +28,13 @@
     lax.fori_loop(0, sources, one_source, jnp.int32(0))
 
 
-def pack_kernel(sizes, relative, me_ref, decode_ref, nope_ref, rope_ref, fresh_ref, *rest):
+def pack_kernel(sizes, relative, me_ref, decode_ref, nope_ref, rope_ref, fresh_ref, after_ref, *rest):
     sources, per_pair, steps, heads, requests, fresh_rows = sizes
-    out_refs, (slots, nope_wide, rope_wide) = rest[:-3], rest[-3:]
+    out_refs, (slots, wide) = rest[:-2], rest[-2:]
     me = me_ref[0]
-    pair_rows = per_pair * steps
-    rope_base = heads * pair_rows
-    half = heads * steps // 2
+    rows = heads * steps
+    half = rows // 2
+    rope_base = per_pair * rows
     fresh_base = rope_base + per_pair * half
     own_slots(decode_ref, slots, me, sources, requests, per_pair)
 
@@ -42,14 +42,15 @@
         for j in range(per_pair):
             row = slots[s * (per_pair + 1) + j]
             for t in range(steps):
-                nope_wide[pl.ds(j * steps + t, heads, stride=pair_rows), :] = nope_ref[t, row].astype(jnp.float32)
-                rope_wide[pl.ds(t, heads, stride=steps), :] = jnp.concatenate(
+                wide[2 * j, pl.ds(t, heads, stride=steps), :] = nope_ref[t, row].astype(jnp.float32)
+                wide[2 * j + 1, pl.ds(t, heads, stride=steps), :] = jnp.concatenate(
                     [rope_ref[t, row].astype(jnp.float32)] * 2, axis=1
                 )
+        for j in range(per_pair):
+            out_ref[e, j * rows : (j + 1) * rows, :] = wide[2 * j].astype(jnp.bfloat16)
             low = lax.broadcasted_iota(jnp.int32, (half, LANES), 1) < LANES // 2
-            packed = jnp.where(low, rope_wide[0:half, :], rope_wide[half : 2 * half, :])
+            packed = jnp.where(low, wide[2 * j + 1, 0:half, :], wide[2 * j + 1, half : 2 * half, :])
             out_ref[e, rope_base + j * half : rope_base + (j + 1) * half, :] = packed.astype(jnp.bfloat16)
-        out_ref[e, 0:rope_base, :] = nope_wide[...].astype(jnp.bfloat16)
 
     if relative:
         dests = [me ^ k for k in range(sources)]
@@ -93,20 +94,48 @@
     recv_refs = rest[:recv_count]
     (
         cache, key_up, value_up, out_ref,
-        slot_offset, slot_length, owner_count, pair_slot, pair_start, first_pair,
-        queries, fresh, part_out, part_max, part_sum, latent,
+        slot_offset, slot_length, owner_count, pair_slot, pair_start,
+        queries, fresh, acc, run_max, run_sum, latent,
     ) = rest[recv_count:]
     owners = [(ref, e) for ref in recv_refs for e in range(ref.shape[0])]
     here = len(owners)
     slots = here * per_pair
     width, tokens = cache.shape
-    pair_rows = per_pair * steps
-    rope_base = heads * pair_rows
     rows = heads * steps
     half = rows // 2
+    rope_base = per_pair * rows
     fresh_base = rope_base + per_pair * half
     group = 16 // steps
     shift = requests.bit_length() - 1
+    factor = scale * LOG2E
+
+    for e in range(here):
+        ref, at = owners[e]
+        for c in range(-(-width // LANES)):
+            lanes = min(LANES, width - c * LANES)
+            first = fresh_base + c * fresh_rows
+            fresh[e * fresh_rows : (e + 1) * fresh_rows, c * LANES : c * LANES + lanes] = ref[
+                at, first : first + fresh_rows, 0:lanes
+            ]
+        for j in range(per_pair):
+            slot = e * per_pair + j
+            first = rope_base + j * half
+            piece = ref[at, first : first + half, :]
+            queries[slot * rows : slot * rows + half, LATENT:width] = piece[:, 0 : width - LATENT]
+            queries[slot * rows + half : (slot + 1) * rows, LATENT:width] = piece[:, LANES - (width - LATENT) :]
+
+    inner_head = lax.broadcasted_iota(jnp.int32, (slots * 16, LANES), 0) // steps % group
+    own_head = [jnp.where(inner_head == u, 1.0, 0.0).astype(jnp.bfloat16) for u in range(group)]
+    for i in range(heads // group):
+        tall = jnp.concatenate(
+            [ref[at, j * rows + i * 16 : j * rows + (i + 1) * 16, :] for ref, at in owners for j in range(per_pair)],
+            axis=0,
+        )
+        left = jnp.concatenate([tall * own_head[u] for u in range(group)], axis=1)
+        right = jnp.concatenate([key_up[i * group + u] for u in range(group)], axis=0)
+        res = jnp.dot(left, right, preferred_element_type=jnp.float32).astype(jnp.bfloat16)
+        for slot in range(slots):
+            queries[slot * rows + i * 16 : slot * rows + (i + 1) * 16, 0:LATENT] = res[slot * 16 : (slot + 1) * 16]
 
     me = me_ref[0]
     for o in range(sources):
@@ -123,69 +152,44 @@
         slot_length[slot] = length
         total = total + length
     count = jnp.int32(0)
-    spans = 512 // BLOCK + 1
     for slot in range(slots):
         start = slot_offset[slot] & ~(LANES - 1)
         end = slot_offset[slot] + slot_length[slot]
-        first_pair[slot] = count
-        for k in range(spans):
+        for k in range(512 // BLOCK + 1):
             pair_slot[count] = jnp.int32(slot)
             pair_start[count] = start + k * BLOCK
             count = count + jnp.where(start + k * BLOCK < end, 1, 0).astype(jnp.int32)
-    first_pair[slots] = count
-
-    for e in range(here):
-        ref, at = owners[e]
-        for c in range(-(-width // LANES)):
-            lanes = min(LANES, width - c * LANES)
-            first = fresh_base + c * fresh_rows
-            fresh[e * fresh_rows : (e + 1) * fresh_rows, c * LANES : c * LANES + lanes] = ref[
-                at, first : first + fresh_rows, 0:lanes
-            ]
-        for j in range(per_pair):
-            slot = e * per_pair + j
-            first = rope_base + j * half
-            piece = ref[at, first : first + half, :]
-            queries[slot * rows : slot * rows + half, LATENT:width] = piece[:, 0 : width - LATENT]
-            queries[slot * rows + half : (slot + 1) * rows, LATENT:width] = piece[:, LANES - (width - LATENT) :]
-
-    def absorb(i, carry):
-        results = []
-        for u in range(group):
-            head = i * group + u
-            if pair_rows % 16 == 0:
-                first = pl.multiple_of(head * pair_rows, 16)
-                left = jnp.concatenate([ref[at, pl.ds(first, pair_rows), :] for ref, at in owners], axis=0)
-            else:
-                first = pl.multiple_of(i * group * pair_rows, 16)
-                left = jnp.concatenate(
-                    [
-                        ref[at, pl.ds(first, group * pair_rows), :].astype(jnp.float32)[
-                            u * pair_rows : (u + 1) * pair_rows
-                        ]
-                        for ref, at in owners
-                    ],
-                    axis=0,
-                ).astype(jnp.bfloat16)
-            results.append(jnp.dot(left, key_up[head], preferred_element_type=jnp.float32))
-        for slot in range(slots):
-            tile = jnp.concatenate([res[slot * steps : (slot + 1) * steps] for res in results], axis=0)
-            queries[pl.ds(pl.multiple_of(slot * rows + i * 16, 16), 16), 0:LATENT] = tile.astype(jnp.bfloat16)
-        return carry
-
-    lax.fori_loop(0, heads // group, absorb, jnp.int32(0))
-
-    unroll = 2
-    factor = scale * LOG2E
+
+    fresh_scores = (
+        lax.dot_general(queries[...], fresh[...], (((1,), (1,)), ((), ())), preferred_element_type=jnp.float32) * factor
+    )
+    row_id = lax.broadcasted_iota(jnp.int32, (rows, here * fresh_rows), 0)
+    col_id = lax.broadcasted_iota(jnp.int32, (rows, here * fresh_rows), 1)
+    behind = row_id & (steps - 1)
+    fresh_weights = []
+    for slot in range(slots):
+        first = (slot // per_pair) * fresh_rows + (slot % per_pair) * steps
+        seen = (col_id >= first) & (col_id <= first + behind)
+        scores = jnp.where(seen, fresh_scores[slot * rows : (slot + 1) * rows], NEG)
+        top = jnp.max(scores, axis=1, keepdims=True)
+        weights = jnp.exp2(scores - top)
+        run_max[slot] = jnp.broadcast_to(top, (rows, LANES))
+        run_sum[slot] = jnp.broadcast_to(jnp.sum(weights, axis=1, keepdims=True), (rows, LANES))
+        fresh_weights.append(weights.astype(jnp.bfloat16))
+    for slot in range(slots):
+        acc[slot] = jnp.dot(fresh_weights[slot], fresh[:, 0:LATENT], preferred_element_type=jnp.float32)
+
+    unroll = 4
 
     def some_pairs(i, carry):
         for u in range(unroll):
-            p = jnp.minimum(i * unroll + u, count - 1)
-            slot = pair_slot[p]
-            start = pair_start[p]
+            p = i * unroll + u
+            slot = pair_slot[jnp.minimum(p, count - 1)]
+            start = pair_start[jnp.minimum(p, count - 1)]
             read = jnp.minimum(start, tokens - BLOCK)
             low = jnp.maximum(slot_offset[slot], start) - read
             high = jnp.minimum(slot_offset[slot] + slot_length[slot], start + BLOCK) - read
+            high = jnp.where(p < count, high, low)
             q = queries[pl.ds(pl.multiple_of(slot * rows, 16), rows), :]
             keys = cache[:, pl.ds(pl.multiple_of(read, LANES), BLOCK)]
             scores = jnp.dot(q, keys, preferred_element_type=jnp.float32) * factor
@@ -193,70 +197,49 @@
             scores = jnp.where((token >= low) & (token < high), scores, NEG)
             top = jnp.max(scores, axis=1, keepdims=True)
             weights = jnp.exp2(scores - top)
-            part_max[p] = jnp.broadcast_to(top, (rows, LANES))
-            part_sum[p] = jnp.broadcast_to(jnp.sum(weights, axis=1, keepdims=True), (rows, LANES))
-            part_out[p] = lax.dot_general(
+            part_sum = jnp.broadcast_to(jnp.sum(weights, axis=1, keepdims=True), (rows, LANES))
+            part = lax.dot_general(
                 weights.astype(jnp.bfloat16),
                 keys[0:LATENT],
                 (((1,), (1,)), ((), ())),
                 preferred_element_type=jnp.float32,
             )
+            part_max = jnp.broadcast_to(top, (rows, LANES))
+            old_max = run_max[slot]
+            new_max = jnp.maximum(old_max, part_max)
+            keep = jnp.exp2(old_max - new_max)
+            add = jnp.exp2(part_max - new_max)
+            run_max[slot] = new_max
+            run_sum[slot] = run_sum[slot] * keep + part_sum * add
+            for c in range(LATENT // LANES):
+                cols = slice(c * LANES, (c + 1) * LANES)
+                acc[slot, :, cols] = acc[slot, :, cols] * keep + part[:, cols] * add
         return carry
 
     lax.fori_loop(0, (count + unroll - 1) // unroll, some_pairs, jnp.int32(0))
 
-    def merge(slot, carry):
-        q = queries[pl.ds(pl.multiple_of(slot * rows, 16), rows), :]
-        scores = (
-            lax.dot_general(q, fresh[...], (((1,), (1,)), ((), ())), preferred_element_type=jnp.float32) * factor
+    for slot in range(slots):
+        inverse = 1.0 / run_sum[slot]
+        for c in range(LATENT // LANES):
+            cols = slice(c * LANES, (c + 1) * LANES)
+            latent[slot * rows : (slot + 1) * rows, cols] = (acc[slot, :, cols] * inverse).astype(jnp.bfloat16)
+    vdim = value_up.shape[2]
+    for i in range(heads // group):
+        left = jnp.concatenate(
+            [latent[slot * rows + i * 16 : slot * rows + (i + 1) * 16, :] for slot in range(slots)], axis=0
         )
-        row_id = lax.broadcasted_iota(jnp.int32, scores.shape, 0)
-        col_id = lax.broadcasted_iota(jnp.int32, scores.shape, 1)
-        first_col = (slot // per_pair) * fresh_rows + (slot % per_pair) * steps
-        scores = jnp.where(
-            (col_id >= first_col) & (col_id <= first_col + (row_id & (steps - 1))), scores, NEG
-        )
-        top = jnp.max(scores, axis=1, keepdims=True)
-        first = first_pair[slot]
-        last = first_pair[slot + 1] - 1
-        tops = []
-        for k in range(spans):
-            own = part_max[jnp.minimum(first + k, last)][:, 0:1]
-            own = jnp.where(first + k <= last, own, 2 * NEG)
-            tops.append(own)
-        highest = functools.reduce(jnp.maximum, tops, top)
-        weights = jnp.exp2(scores - highest)
-        norm = jnp.sum(weights, axis=1, keepdims=True)
-        out = jnp.dot(weights.astype(jnp.bfloat16), fresh[:, 0:LATENT], preferred_element_type=jnp.float32)
-        for k in range(spans):
-            at = jnp.minimum(first + k, last)
-            share = jnp.exp2(tops[k] - highest)
-            norm = norm + share * part_sum[at][:, 0:1]
-            out = out + share * part_out[at]
-        latent[pl.ds(pl.multiple_of(slot * rows, 16), rows), :] = (out / norm).astype(jnp.bfloat16)
-        return carry
-
-    lax.fori_loop(0, slots, merge, jnp.int32(0))
-
-    def project(i, carry):
-        tiles = [
-            latent[pl.ds(pl.multiple_of(slot * rows + i * 16, 16), 16), :].astype(jnp.float32)
-            for slot in range(slots)
-        ]
-        count_rows = slots * steps
-        vdim = value_up.shape[2]
-        for u in range(0, group, 2):
+        right = jnp.concatenate([value_up[i * group + u] for u in range(group)], axis=1)
+        res = jnp.dot(left, right, preferred_element_type=jnp.float32)
+        for u in range(group):
+            own = jnp.concatenate(
+                [
+                    res[slot * 16 + u * steps : slot * 16 + (u + 1) * steps, u * vdim : (u + 1) * vdim]
+                    for slot in range(slots)
+                ],
+                axis=0,
+            )
             head = i * group + u
-            left = jnp.concatenate(
-                [tile[v * steps : (v + 1) * steps] for v in (u, u + 1) for tile in tiles], axis=0
-            ).astype(jnp.bfloat16)
-            right = jnp.concatenate([value_up[head], value_up[head + 1]], axis=1)
-            res = jnp.dot(left, right, preferred_element_type=jnp.float32)
-            both = jnp.concatenate([res[:count_rows, :vdim], res[count_rows:, vdim:]], axis=1)
-            out_ref[:, pl.ds(pl.multiple_of(head * vdim, vdim), 2 * vdim)] = both.astype(jnp.bfloat16)
-        return carry
-
-    lax.fori_loop(0, heads // group, project, jnp.int32(0))
+            out_ref[:, head * vdim : (head + 1) * vdim] = own.astype(jnp.bfloat16)
 
 
 def place_kernel(sizes, relative, me_ref, decode_ref, out_ref, owner_count, place):
@@ -343,6 +326,10 @@
     return pl.BlockSpec(memory_space=pltpu.VMEM)
 
 
+def anywhere():
+    return pl.BlockSpec(memory_space=pl.ANY)
+
+
 def limit(mib):
     return pltpu.CompilerParams(vmem_limit_bytes=mib * 1024 * 1024)
 
@@ -358,13 +345,20 @@
     return lax.ppermute(x, axis, [(i, i ^ distance) for i in range(size)])
 
 
-def line_sum(piece):
-    inward = lax.ppermute(piece, "head", [(0, 1), (3, 2)])
-    pair = (piece.astype(jnp.float32) + inward.astype(jnp.float32)).astype(jnp.bfloat16)
-    crossed = lax.ppermute(pair, "head", [(1, 2), (2, 1)])
-    whole = (pair.astype(jnp.float32) + crossed.astype(jnp.float32)).astype(jnp.bfloat16)
-    outward = lax.ppermute(whole, "head", [(1, 0), (2, 3)])
-    return whole, outward
+def add(x, y):
+    return (x.astype(jnp.float32) + y.astype(jnp.float32)).astype(jnp.bfloat16)
+
+
+def inwards(piece):
+    return lax.ppermute(piece, "head", [(0, 1), (3, 2)])
+
+
+def across_middle(pair):
+    return lax.ppermute(pair, "head", [(1, 2), (2, 1)])
+
+
+def outwards(whole):
+    return lax.ppermute(whole, "head", [(1, 0), (2, 3)])
 
 
 def local(latent_cache, lengths, decode_rows, q_nope, q_rope, new_latent, key_up, value_up, out_proj):
@@ -377,30 +371,39 @@
     steps, _, heads, nope = q_nope.shape
     scale = (nope + q_rope.shape[3]) ** (-0.5)
     fresh_rows = -(-per_pair * steps // 16) * 16
-    pair_rows = per_pair * steps
     rows = heads * steps
     columns = out_proj.shape[1]
-    packed_rows = heads * pair_rows + per_pair * rows // 2 + -(-width // LANES) * fresh_rows
+    packed_rows = per_pair * rows + per_pair * rows // 2 + -(-width // LANES) * fresh_rows
     sizes = (sources, per_pair, steps, heads, requests, fresh_rows)
     me = lax.axis_index("seq").astype(jnp.int32).reshape(1)
     z = lax.axis_index("head").astype(jnp.int32).reshape(1)
     cache = latent_cache.T
 
+    pick = pl.pallas_call(
+        functools.partial(place_kernel, (sources, per_pair, steps, requests), relative),
+        out_shape=jax.ShapeDtypeStruct((steps, sources * requests, steps * sources * requests), jnp.bfloat16),
+        in_specs=[smem(), smem()],
+        out_specs=vmem(),
+        scratch_shapes=[pltpu.SMEM((sources,), jnp.int32), pltpu.SMEM((sources * requests,), jnp.int32)],
+        compiler_params=limit(12),
+        cost_estimate=cost(2),
+        name="place_rows",
+    )(me, decode_rows)
+
     outs, each = (sources, 1) if relative else (1, sources)
     packed = pl.pallas_call(
         functools.partial(pack_kernel, sizes, relative),
         out_shape=[jax.ShapeDtypeStruct((each, packed_rows, LANES), jnp.bfloat16)] * outs,
-        in_specs=[smem(), smem(), vmem(), vmem(), vmem()],
+        in_specs=[smem(), smem(), vmem(), vmem(), vmem(), anywhere()],
         out_specs=[vmem()] * outs,
         scratch_shapes=[
             pltpu.SMEM((sources * (per_pair + 1),), jnp.int32),
-            pltpu.VMEM((heads * pair_rows, LANES), jnp.float32),
-            pltpu.VMEM((rows, LANES), jnp.float32),
+            pltpu.VMEM((2 * per_pair, rows, LANES), jnp.float32),
         ],
-        compiler_params=limit(12),
-        cost_estimate=cost(3),
+        compiler_params=limit(8),
+        cost_estimate=cost(6),
         name="pack_queries",
-    )(me, decode_rows, q_nope, q_rope, new_latent)
+    )(me, decode_rows, q_nope, q_rope, new_latent, pick)
 
     def attend(received, base):
         here = sum(part.shape[0] for part in received)
@@ -417,29 +420,17 @@
                 pltpu.SMEM((sources,), jnp.int32),
                 pltpu.SMEM((pairs,), jnp.int32),
                 pltpu.SMEM((pairs,), jnp.int32),
-                pltpu.SMEM((slots + 1,), jnp.int32),
                 pltpu.VMEM((slots * rows, width), jnp.bfloat16),
                 pltpu.VMEM((here * fresh_rows, width), jnp.bfloat16),
-                pltpu.VMEM((pairs, rows, LATENT), jnp.float32),
-                pltpu.VMEM((pairs, rows, LANES), jnp.float32),
-                pltpu.VMEM((pairs, rows, LANES), jnp.float32),
+                pltpu.VMEM((slots, rows, LATENT), jnp.float32),
+                pltpu.VMEM((slots, rows, LANES), jnp.float32),
+                pltpu.VMEM((slots, rows, LANES), jnp.float32),
                 pltpu.VMEM((slots * rows, LATENT), jnp.bfloat16),
             ],
-            compiler_params=limit(32),
-            cost_estimate=cost(14),
+            compiler_params=limit(18),
+            cost_estimate=cost(8),
             name="attend",
         )(me, decode_rows, lengths, *received, cache, key_up, value_up)
-
-    pick = pl.pallas_call(
-        functools.partial(place_kernel, (sources, per_pair, steps, requests), relative),
-        out_shape=jax.ShapeDtypeStruct((steps, sources * requests, steps * sources * requests), jnp.bfloat16),
-        in_specs=[smem(), smem()],
-        out_specs=vmem(),
-        scratch_shapes=[pltpu.SMEM((sources,), jnp.int32), pltpu.SMEM((sources * requests,), jnp.int32)],
-        compiler_params=limit(12),
-        cost_estimate=cost(2),
-        name="place_rows",
-    )(me, decode_rows)
 
     def order(pieces, arrays, scratch):
         return pl.pallas_call(
@@ -478,14 +469,29 @@
         )(*parts, out_proj)
 
     received = [packed[0]] + [flip(packed[k], "seq", k) for k in range(1, 4)]
-    near = attend(received[:2], 0)
-    near_parts = [near] + [flip(near, "seq", k) for k in range(1, 4)]
-    far = attend(received[2:], 2)
-    far_across = flip(far, "seq", 2)
-    far_parts = [far, flip(far, "seq", 1), far_across, flip(far_across, "seq", 1)]
-    sums = [line_sum(piece) for piece in project(near_parts)]
-    sums += [line_sum(piece) for piece in project(far_parts)]
-    arrays = [array for pair in sums for array in pair]
+    near_rows = attend(received[:2], 0)
+    near_across = flip(near_rows, "seq", 2)
+    far_rows = attend(received[2:], 2)
+    near_across, far_rows = lax.optimization_barrier((near_across, far_rows))
+    near = [near_rows, flip(near_rows, "seq", 1), near_across, flip(near_across, "seq", 1)]
+    far_across = flip(far_rows, "seq", 2)
+    far = [far_rows, flip(far_rows, "seq", 1), far_across, flip(far_across, "seq", 1)]
+    first, second = project(near)
+    first_in, second_in = inwards(first), inwards(second)
+    first_pair = add(first, first_in)
+    first_cross = across_middle(first_pair)
+    third, fourth = project(far)
+    second_in, first_cross, third, fourth = lax.optimization_barrier((second_in, first_cross, third, fourth))
+    second_pair = add(second, second_in)
+    second_cross = across_middle(second_pair)
+    third_in, fourth_in = inwards(third), inwards(fourth)
+    first_whole = add(first_pair, first_cross)
+    second_whole = add(second_pair, second_cross)
+    third_pair, fourth_pair = add(third, third_in), add(fourth, fourth_in)
+    third_whole = add(third_pair, across_middle(third_pair))
+    fourth_whole = add(fourth_pair, across_middle(fourth_pair))
+    sums = [(whole, outwards(whole)) for whole in (first_whole, second_whole, third_whole, fourth_whole)]
+    arrays = [array for both in sums for array in both]
     return order(len(sums), arrays, [pltpu.VMEM((steps * sources * requests, columns), jnp.bfloat16)])
 
 

time: 99.7 us -> 83.5 us (0.84); the launches traced: 99.5 us -> 82.1 us
  Pallas kernels: 36.9 us -> 26.2 us
  waiting for transfers between devices: 27 us -> 20.4 us
  local copies, waits for them, and re-layouts: 5.84 us -> 0.82 us
  starting transfers between devices: 28.9 us -> 33.7 us
    pallas_call x2, Pallas kernels: 25.9 us -> 15.6 us  [attend(): pl.pallas_call(functools.partial(attend_kernel, sizes, scale, relative, b...]
    ppermute x12, waiting for transfers between devices: 27 us -> 19.9 us  [the longest x4 12.3 us: outwards(): return lax.ppermute(whole, 'head', [(1, 0), (2, 3)])]
    unnamed x26 -> x28, local copies, waits for them, and re-layouts: 5.84 us -> 0.82 us
    ppermute x12, starting transfers between devices: 21.4 us -> 25.1 us  [the longest x4 17.3 us: inwards(): return lax.ppermute(piece, 'head', [(0, 1), (3, 2)])]
    ppermute x9, starting transfers between devices: 7.42 us -> 8.55 us  [flip(): return lax.ppermute(x, axis, [(i, i ^ distance) for i in range(size)])]
  transfers between devices with their start and end apart: 21 -> 21, of which waited for: 7 -> 6; matrix products, arithmetic and copies ran while one was open for 0% -> 0% of each run, Pallas kernels for 34% -> 27%
where the time goes in v3:
time: 83.5 us; the launch traced here: 82.1 us
  starting transfers between devices  33.7 us (40%)
  Pallas kernels  26.2 us (31%)
  waiting for transfers between devices  20.4 us (24%)
    ppermute x4, starting transfers between devices, inwards(): return lax.ppermute(piece, 'head', [(0, 1), (3, 2)])  17.3 us
    pallas_call x2, Pallas kernels, attend(): pl.pallas_call(functools.partial(attend_kernel, sizes, scale, relative, b...  15.6 us
    ppermute x4, waiting for transfers between devices, outwards(): return lax.ppermute(whole, 'head', [(1, 0), (2, 3)])  12.3 us
    ppermute x9, starting transfers between devices, flip(): return lax.ppermute(x, axis, [(i, i ^ distance) for i in range(size)])  8.55 us
    ppermute x4, waiting for transfers between devices, inwards(): return lax.ppermute(piece, 'head', [(0, 1), (3, 2)])  7.52 us
    pallas_call x2, Pallas kernels, project(): pl.pallas_call(functools.partial(project_kernel, pieces), out_shape=[jax....  6.68 us
    ppermute x4, starting transfers between devices, outwards(): return lax.ppermute(whole, 'head', [(1, 0), (2, 3)])  5.17 us
    ppermute x4, starting transfers between devices, across_middle(): return lax.ppermute(pair, 'head', [(1, 2), (2, 1)])  2.7 us
  transfers between devices with their start and end apart: 21, of which 6 were waited for; matrix products, arithmetic and copies ran while one was open for 0% of the time, Pallas kernels for 27%

profile of v3, /device:TPU:0, one launch (start us, length us, event | category | flops | bytes accessed | tf_op | source)
XLA Modules:
  0.0 82.1 jit_solution(13648120283302672537)
XLA Ops:
  0.0 0.7 copy-done.6
  0.8 1.1 %place_rows.1.after_ref.pick_ref = bf16[4,64,256]{2,1,0:T(8,128)(2,1)S(1)} custom-call(s32[1]{0:T(128)} %bitcast.1.me_ref, s32[64]{0:T(128)S(1)} %copy-done.6), custom_call_target="tpu_custom_call" | custom-call | flops 2000000000 | bytes 6000000 | tf_op jit(solution)/shard_map/place_rows/pallas_call | solution.py:382
  1.9 0.0 slice-start.5
  1.9 0.0 copy-start
  1.9 0.0 copy-start.5
  1.9 0.0 copy-start.7
  1.9 1.1 %pack_queries.1 = (bf16[1,848,128]{2,1,0:T(8,128)(2,1)S(1)}, bf16[1,848,128]{2,1,0:T(8,128)(2,1)S(1)}, bf16[1,848,128]{2,1,0:T(8,128)(2,1)S(1)}, bf16[1,848,128]{2,1,0:T(8,128)(2,1)S(1)}) custom-call(s32[1]{0:T(128)} %bitcast.1.me_ref, s32[64]{0:T(128)S(1)} %copy-done.6, bf16[4,16,32,128]{3,2,1,0:T(8,128)(2,1)S(1)} %copy-done.2, ...), custom_call_target="tpu_custom_call" | custom-call | flops 6000000000 | bytes 18000000 | tf_op jit(solution)/shard_map/pack_queries/pallas_call | solution.py:394
  3.1 0.5 collective-permute-start
  3.6 2.6 %collective-permute-start.3 = (bf16[1,848,128]{2,1,0:T(8,128)(2,1)S(1)}, bf16[1,848,128]{2,1,0:T(8,128)(2,1)S(1)}, u32[]{:S(2)}, u32[]{:S(2)}) collective-permute-start(bf16[1,848,128]{2,1,0:T(8,128)(2,1)S(1)} %get-tuple-element.21), channel_id=1, source_target_pairs={{0,8},{4,12},{8,0},{12,4},{1,9},{5,13},{9,1},{13,5},{2,10},{6,14},... | collective-permute-start | bytes 651272 | tf_op jit(solution)/shard_map/ppermute | solution.py:345
  6.2 0.1 collective-permute-start.4
  6.3 0.0 slice-start
  6.4 7.2 %attend.2.rest_0_ = bf16[32,4096]{1,0:T(8,128)(2,1)S(1)} custom-call(s32[1]{0:T(128)} %bitcast.1.me_ref, s32[64]{0:T(128)S(1)} %copy-done.7, s32[4,16]{1,0:T(4,128)S(1)} %copy-done.5, bf16[1,848,128]{2,1,0:T(8,128)(2,1)S(1)} %get-tuple-element.19.rest_0_, bf16[1,848,128]{2,1,0:T(8,128)(2,1)S(1)} %collective-permute-done.rest_1_, ...), custom_call_target="tpu_custom_call" | custom-call | flops 8000000000 | bytes 24000000 | tf_op jit(solution)/shard_map/attend/pallas_call | solution.py:412
  13.5 0.0 slice-start.2
  13.6 3.7 %collective-permute-start.2 = (bf16[32,4096]{1,0:T(8,128)(2,1)S(1)}, bf16[32,4096]{1,0:T(8,128)(2,1)S(1)}, u32[]{:S(2)}, u32[]{:S(2)}) collective-permute-start(bf16[32,4096]{1,0:T(8,128)(2,1)S(1)} %attend.2.rest_0_), channel_id=1, source_target_pairs={{0,8},{4,12},{8,0},{12,4},{1,9},{5,13},{9,1},{13,5},{2,10},{6,14},... | collective-permute-start | bytes 786440 | tf_op jit(solution)/shard_map/ppermute | solution.py:345
  17.3 8.4 %attend.3.rest_0_ = bf16[32,4096]{1,0:T(8,128)(2,1)S(1)} custom-call(s32[1]{0:T(128)} %bitcast.1.me_ref, s32[64]{0:T(128)S(1)} %copy-done.7, s32[4,16]{1,0:T(4,128)S(1)} %copy-done.5, bf16[1,848,128]{2,1,0:T(8,128)(2,1)S(1)} %collective-permute-done.3.rest_0_, bf16[1,848,128]{2,1,0:T(8,128)(2,1)S(1)} %collective-permute-done.4.rest_1_, ...), custom_call_target="tpu_custom_call" | custom-call | flops 8000000000 | bytes 24000000 | tf_op jit(solution)/shard_map/attend/pallas_call | solution.py:412
  25.8 0.1 collective-permute-start.5
  25.8 1.0 %collective-permute-start.10 = (bf16[32,4096]{1,0:T(8,128)(2,1)S(1)}, bf16[32,4096]{1,0:T(8,128)(2,1)S(1)}, u32[]{:S(2)}, u32[]{:S(2)}) collective-permute-start(bf16[32,4096]{1,0:T(8,128)(2,1)S(1)} %attend.3.rest_0_), channel_id=1, source_target_pairs={{0,8},{4,12},{8,0},{12,4},{1,9},{5,13},{9,1},{13,5},{2,10},{6,14},... | collective-permute-start | bytes 786440 | tf_op jit(solution)/shard_map/ppermute | solution.py:345
  26.9 0.5 collective-permute-done.5.rest_3_
  27.4 3.3 %project_out.2 = (bf16[64,1792]{1,0:T(8,128)(2,1)S(1)}, bf16[64,1792]{1,0:T(8,128)(2,1)S(1)}) custom-call(bf16[32,4096]{1,0:T(8,128)(2,1)S(1)} %attend.2.rest_0_, bf16[32,4096]{1,0:T(8,128)(2,1)S(1)} %collective-permute-done.1.rest_1_, bf16[32,4096]{1,0:T(8,128)(2,1)S(1)} %collective-permute-done.2.rest_2_, ...), custom_call_target="tpu_custom_call" | custom-call | flops 6000000000 | bytes 18000000 | tf_op jit(solution)/shard_map/project_out/pallas_call | solution.py:460
  30.7 3.5 %collective-permute-start.6 = (bf16[64,1792]{1,0:T(8,128)(2,1)S(1)}, bf16[64,1792]{1,0:T(8,128)(2,1)S(1)}, u32[]{:S(2)}, u32[]{:S(2)}) collective-permute-start(bf16[64,1792]{1,0:T(8,128)(2,1)S(1)} %get-tuple-element.24), channel_id=1, source_target_pairs={{0,1},{3,2},{4,5},{7,6},{8,9},{11,10},{12,13},{15,14},{16,17},{19,... | collective-permute-start | bytes 688136 | tf_op jit(solution)/shard_map/ppermute | solution.py:353
  34.2 0.1 collective-permute-start.9
  34.3 1.4 %collective-permute-start.7 = (bf16[64,1792]{1,0:T(8,128)(2,1)S(1)}, bf16[64,1792]{1,0:T(8,128)(2,1)S(1)}, u32[]{:S(2)}, u32[]{:S(2)}) collective-permute-start(bf16[64,1792]{1,0:T(8,128)(2,1)S(1)} %get-tuple-element.25), channel_id=1, source_target_pairs={{0,1},{3,2},{4,5},{7,6},{8,9},{11,10},{12,13},{15,14},{16,17},{19,... | collective-permute-start | bytes 688136 | tf_op jit(solution)/shard_map/ppermute | solution.py:353
  35.8 0.4 collective-permute-start.11
  36.2 4.0 %collective-permute-done.6 = bf16[64,1792]{1,0:T(8,128)(2,1)S(1)} collective-permute-done((bf16[64,1792]{1,0:T(8,128)(2,1)S(1)}, bf16[64,1792]{1,0:T(8,128)(2,1)S(1)}, u32[]{:S(2)}, u32[]{:S(2)}) %collective-permute-start.6) | collective-permute-done | bytes 229408 | tf_op jit(solution)/shard_map/ppermute | solution.py:353
  40.2 0.1 add_convert_fusion.7
  40.2 0.7 collective-permute-start.8
  41.0 3.3 %project_out.3 = (bf16[64,1792]{1,0:T(8,128)(2,1)S(1)}, bf16[64,1792]{1,0:T(8,128)(2,1)S(1)}) custom-call(bf16[32,4096]{1,0:T(8,128)(2,1)S(1)} %attend.3.rest_0_, bf16[32,4096]{1,0:T(8,128)(2,1)S(1)} %collective-permute-done.9.rest_1_, bf16[32,4096]{1,0:T(8,128)(2,1)S(1)} %collective-permute-done.10.rest_2_, ...), custom_call_target="tpu_custom_call" | custom-call | flops 6000000000 | bytes 18000000 | tf_op jit(solution)/shard_map/project_out/pallas_call | solution.py:460
  44.3 0.1 add_convert_fusion.5
  44.4 0.7 collective-permute-start.13
  45.1 0.1 add_convert_fusion.6.rest_0_
  45.1 1.3 %collective-permute-start.12 = (bf16[64,1792]{1,0:T(8,128)(2,1)S(1)}, bf16[64,1792]{1,0:T(8,128)(2,1)S(1)}, u32[]{:S(2)}, u32[]{:S(2)}) collective-permute-start(bf16[64,1792]{1,0:T(8,128)(2,1)S(1)} %add_convert_fusion.6.rest_0_), channel_id=1, source_target_pairs={{1,0},{2,3},{5,4},{6,7},{9,8},{10,11},{13,12},{14,15},{17,16},{18,... | collective-permute-start | bytes 688136 | tf_op jit(solution)/shard_map/ppermute | solution.py:361
  46.4 11.1 %collective-permute-start.15 = (bf16[64,1792]{1,0:T(8,128)(2,1)S(1)}, bf16[64,1792]{1,0:T(8,128)(2,1)S(1)}, u32[]{:S(2)}, u32[]{:S(2)}) collective-permute-start(bf16[64,1792]{1,0:T(8,128)(2,1)S(1)} %get-tuple-element.31), channel_id=1, source_target_pairs={{0,1},{3,2},{4,5},{7,6},{8,9},{11,10},{12,13},{15,14},{16,17},{19,... | collective-permute-start | bytes 688136 | tf_op jit(solution)/shard_map/ppermute | solution.py:353
  57.5 1.3 %collective-permute-start.18 = (bf16[64,1792]{1,0:T(8,128)(2,1)S(1)}, bf16[64,1792]{1,0:T(8,128)(2,1)S(1)}, u32[]{:S(2)}, u32[]{:S(2)}) collective-permute-start(bf16[64,1792]{1,0:T(8,128)(2,1)S(1)} %get-tuple-element.32), channel_id=1, source_target_pairs={{0,1},{3,2},{4,5},{7,6},{8,9},{11,10},{12,13},{15,14},{16,17},{19,... | collective-permute-start | bytes 688136 | tf_op jit(solution)/shard_map/ppermute | solution.py:353
  58.8 0.1 add_convert_fusion.4.rest_2_
  58.9 1.3 %collective-permute-start.14 = (bf16[64,1792]{1,0:T(8,128)(2,1)S(1)}, bf16[64,1792]{1,0:T(8,128)(2,1)S(1)}, u32[]{:S(2)}, u32[]{:S(2)}) collective-permute-start(bf16[64,1792]{1,0:T(8,128)(2,1)S(1)} %add_convert_fusion.4.rest_2_), channel_id=1, source_target_pairs={{1,0},{2,3},{5,4},{6,7},{9,8},{10,11},{13,12},{14,15},{17,16},{18,... | collective-permute-start | bytes 688136 | tf_op jit(solution)/shard_map/ppermute | solution.py:361
  60.2 1.8 %collective-permute-done.15 = bf16[64,1792]{1,0:T(8,128)(2,1)S(1)} collective-permute-done((bf16[64,1792]{1,0:T(8,128)(2,1)S(1)}, bf16[64,1792]{1,0:T(8,128)(2,1)S(1)}, u32[]{:S(2)}, u32[]{:S(2)}) %collective-permute-start.15) | collective-permute-done | bytes 229408 | tf_op jit(solution)/shard_map/ppermute | solution.py:353
  62.0 0.1 add_convert_fusion.3
  62.1 0.7 collective-permute-start.16
  62.7 1.7 %collective-permute-done.18 = bf16[64,1792]{1,0:T(8,128)(2,1)S(1)} collective-permute-done((bf16[64,1792]{1,0:T(8,128)(2,1)S(1)}, bf16[64,1792]{1,0:T(8,128)(2,1)S(1)}, u32[]{:S(2)}, u32[]{:S(2)}) %collective-permute-start.18) | collective-permute-done | bytes 229408 | tf_op jit(solution)/shard_map/ppermute | solution.py:353
  64.5 0.1 add_convert_fusion.1
  64.5 0.7 collective-permute-start.19
  65.2 0.1 add_convert_fusion.2.rest_4_
  65.3 1.3 %collective-permute-start.17 = (bf16[64,1792]{1,0:T(8,128)(2,1)S(1)}, bf16[64,1792]{1,0:T(8,128)(2,1)S(1)}, u32[]{:S(2)}, u32[]{:S(2)}) collective-permute-start(bf16[64,1792]{1,0:T(8,128)(2,1)S(1)} %add_convert_fusion.2.rest_4_), channel_id=1, source_target_pairs={{1,0},{2,3},{5,4},{6,7},{9,8},{10,11},{13,12},{14,15},{17,16},{18,... | collective-permute-start | bytes 688136 | tf_op jit(solution)/shard_map/ppermute | solution.py:361
  66.6 0.1 add_convert_fusion.rest_6_
  66.7 1.3 %collective-permute-start.20 = (bf16[64,1792]{1,0:T(8,128)(2,1)S(1)}, bf16[64,1792]{1,0:T(8,128)(2,1)S(1)}, u32[]{:S(2)}, u32[]{:S(2)}) collective-permute-start(bf16[64,1792]{1,0:T(8,128)(2,1)S(1)} %add_convert_fusion.rest_6_), channel_id=1, source_target_pairs={{1,0},{2,3},{5,4},{6,7},{9,8},{10,11},{13,12},{14,15},{17,16},{18,... | collective-permute-start | bytes 688136 | tf_op jit(solution)/shard_map/ppermute | solution.py:361
  68.0 9.9 %collective-permute-done.17.rest_5_ = bf16[64,1792]{1,0:T(8,128)(2,1)S(1)} collective-permute-done((bf16[64,1792]{1,0:T(8,128)(2,1)S(1)}, bf16[64,1792]{1,0:T(8,128)(2,1)S(1)}, u32[]{:S(2)}, u32[]{:S(2)}) %collective-permute-start.17) | collective-permute-done | bytes 229408 | tf_op jit(solution)/shard_map/ppermute | solution.py:361
  77.9 2.5 %collective-permute-done.20.rest_7_ = bf16[64,1792]{1,0:T(8,128)(2,1)S(1)} collective-permute-done((bf16[64,1792]{1,0:T(8,128)(2,1)S(1)}, bf16[64,1792]{1,0:T(8,128)(2,1)S(1)}, u32[]{:S(2)}, u32[]{:S(2)}) %collective-permute-start.20) | collective-permute-done | bytes 229408 | tf_op jit(solution)/shard_map/ppermute | solution.py:361
  80.3 1.7 %order_rows.1 = bf16[4,64,1792]{2,1,0:T(8,128)(2,1)} custom-call(s32[1]{0:T(128)} %bitcast.z_ref, bf16[4,64,256]{2,1,0:T(8,128)(2,1)S(1)} %place_rows.1.after_ref.pick_ref, bf16[64,1792]{1,0:T(8,128)(2,1)S(1)} %add_convert_fusion.6.rest_0_, bf16[64,1792]{1,0:T(8,128)(2,1)S(1)} %collective-permute-done.12.rest_1_, ...), custom_call_target="tpu_custom_call" | custom-call | flops 2000000000 | bytes 6000000 | tf_op jit(solution)/shard_map/order_rows/pallas_call | solution.py:436
  (39 shorter events, 0.1 us)
Async XLA Ops:
  0.0 1.8 %copy-start.4 = (bf16[4,16,576]{2,1,0:T(8,128)(2,1)S(1)}, bf16[4,16,576]{2,1,0:T(8,128)(2,1)}, u32[]{:S(2)}) copy-start(bf16[4,16,576]{2,1,0:T(8,128)(2,1)} %fresh_ref.1) | copy-start | bytes 221188
  0.0 1.9 %copy-start.3 = (bf16[4,16,32,64]{3,2,1,0:T(8,128)(2,1)S(1)}, bf16[4,16,32,64]{3,2,1,0:T(8,128)(2,1)}, u32[]{:S(2)}) copy-start(bf16[4,16,32,64]{3,2,1,0:T(8,128)(2,1)} %rope_ref.1) | copy-start | bytes 786436
  0.0 1.9 %copy-start.2 = (bf16[4,16,32,128]{3,2,1,0:T(8,128)(2,1)S(1)}, bf16[4,16,32,128]{3,2,1,0:T(8,128)(2,1)}, u32[]{:S(2)}) copy-start(bf16[4,16,32,128]{3,2,1,0:T(8,128)(2,1)} %nope_ref.1) | copy-start | bytes 1572868
  0.0 0.7 copy-start.6
  0.8 5.5 %slice-start.4 = ((s8[4718592]{0:T(1024)(128)(4,1)}), s8[4194304]{0:T(1024)(128)(4,1)S(1)}, s32[]{:S(2)}) async-start(s8[4718592]{0:T(1024)(128)(4,1)} %bitcast.5), calls=%async_computation.4 | async-start | bytes 8388608
  1.9 4.4 %slice-start.5 = ((s8[4718592]{0:T(1024)(128)(4,1)}), s8[524288]{0:T(1024)(128)(4,1)S(1)}, s32[]{:S(2)}) async-start(s8[4718592]{0:T(1024)(128)(4,1)} %bitcast.5), calls=%async_computation.5 | async-start | bytes 1048576
  1.9 4.4 %copy-start = (bf16[32,128,512]{2,1,0:T(8,128)(2,1)S(1)}, bf16[32,128,512]{2,1,0:T(8,128)(2,1)}, u32[]{:S(2)}) copy-start(bf16[32,128,512]{2,1,0:T(8,128)(2,1)} %rest_3_.3) | copy-start | bytes 12582916
  1.9 4.4 %copy-start.1 = (bf16[32,512,128]{2,1,0:T(8,128)(2,1)S(1)}, bf16[32,512,128]{2,1,0:T(8,128)(2,1)}, u32[]{:S(2)}) copy-start(bf16[32,512,128]{2,1,0:T(8,128)(2,1)} %rest_4_.5) | copy-start | bytes 12582916
  1.9 4.4 %copy-start.5 = (s32[4,16]{1,0:T(4,128)S(1)}, s32[4,16]{1,0:T(4,128)}, u32[]{:S(2)}) copy-start(s32[4,16]{1,0:T(4,128)} %length_ref.3) | copy-start | bytes 772
  1.9 4.4 %copy-start.7 = (s32[64]{0:T(128)S(1)}, s32[64]{0:T(128)}, u32[]{:S(2)}) copy-start(s32[64]{0:T(128)} %decode_ref.7) | copy-start | bytes 772
  3.1 3.2 %collective-permute-start = (bf16[1,848,128]{2,1,0:T(8,128)(2,1)S(1)}, bf16[1,848,128]{2,1,0:T(8,128)(2,1)S(1)}, u32[]{:S(2)}, u32[]{:S(2)}) collective-permute-start(bf16[1,848,128]{2,1,0:T(8,128)(2,1)S(1)} %get-tuple-element.20), channel_id=1, source_target_pairs={{0,4},{4,0},{8,12},{12,8},{1,5},{5,1},{9,13},{13,9},{2,6},{6,2},{1... | collective-permute-start | bytes 651272 | tf_op jit(solution)/shard_map/ppermute | solution.py:345
  3.6 13.7 %collective-permute-start.3 = (bf16[1,848,128]{2,1,0:T(8,128)(2,1)S(1)}, bf16[1,848,128]{2,1,0:T(8,128)(2,1)S(1)}, u32[]{:S(2)}, u32[]{:S(2)}) collective-permute-start(bf16[1,848,128]{2,1,0:T(8,128)(2,1)S(1)} %get-tuple-element.21), channel_id=1, source_target_pairs={{0,8},{4,12},{8,0},{12,4},{1,9},{5,13},{9,1},{13,5},{2,10},{6,14},... | collective-permute-start | bytes 651272 | tf_op jit(solution)/shard_map/ppermute | solution.py:345
  6.2 11.1 %collective-permute-start.4 = (bf16[1,848,128]{2,1,0:T(8,128)(2,1)S(1)}, bf16[1,848,128]{2,1,0:T(8,128)(2,1)S(1)}, u32[]{:S(2)}, u32[]{:S(2)}) collective-permute-start(bf16[1,848,128]{2,1,0:T(8,128)(2,1)S(1)} %get-tuple-element.22), channel_id=1, source_target_pairs={{0,12},{4,8},{8,4},{12,0},{1,13},{5,9},{9,5},{13,1},{2,14},{6,10},... | collective-permute-start | bytes 651272 | tf_op jit(solution)/shard_map/ppermute | solution.py:345
  6.3 21.0 %slice-start = ((s8[14680064]{0:T(1024)(128)(4,1)}), s8[4194304]{0:T(1024)(128)(4,1)S(1)}, s32[]{:S(2)}) async-start(s8[14680064]{0:T(1024)(128)(4,1)} %bitcast.3), calls=%async_computation | async-start | bytes 8388608
  6.3 21.0 %slice-start.1 = ((s8[14680064]{0:T(1024)(128)(4,1)}), s8[4194304]{0:T(1024)(128)(4,1)S(1)}, s32[]{:S(2)}) async-start(s8[14680064]{0:T(1024)(128)(4,1)} %bitcast.3), calls=%async_computation.1 | async-start | bytes 8388608
  13.5 13.8 %slice-start.2 = ((s8[14680064]{0:T(1024)(128)(4,1)}), s8[4194304]{0:T(1024)(128)(4,1)S(1)}, s32[]{:S(2)}) async-start(s8[14680064]{0:T(1024)(128)(4,1)} %bitcast.3), calls=%async_computation.2 | async-start | bytes 8388608
  13.6 13.8 %slice-start.3 = ((s8[14680064]{0:T(1024)(128)(4,1)}), s8[2097152]{0:T(1024)(128)(4,1)S(1)}, s32[]{:S(2)}) async-start(s8[14680064]{0:T(1024)(128)(4,1)} %bitcast.3), calls=%async_computation.3 | async-start | bytes 4194304
  13.6 12.2 %collective-permute-start.2 = (bf16[32,4096]{1,0:T(8,128)(2,1)S(1)}, bf16[32,4096]{1,0:T(8,128)(2,1)S(1)}, u32[]{:S(2)}, u32[]{:S(2)}) collective-permute-start(bf16[32,4096]{1,0:T(8,128)(2,1)S(1)} %attend.2.rest_0_), channel_id=1, source_target_pairs={{0,8},{4,12},{8,0},{12,4},{1,9},{5,13},{9,1},{13,5},{2,10},{6,14},... | collective-permute-start | bytes 786440 | tf_op jit(solution)/shard_map/ppermute | solution.py:345
  17.3 9.6 %collective-permute-start.1 = (bf16[32,4096]{1,0:T(8,128)(2,1)S(1)}, bf16[32,4096]{1,0:T(8,128)(2,1)S(1)}, u32[]{:S(2)}, u32[]{:S(2)}) collective-permute-start(bf16[32,4096]{1,0:T(8,128)(2,1)S(1)} %attend.2.rest_0_), channel_id=1, source_target_pairs={{0,4},{4,0},{8,12},{12,8},{1,5},{5,1},{9,13},{13,9},{2,6},{6,2},{1... | collective-permute-start | bytes 786440 | tf_op jit(solution)/shard_map/ppermute | solution.py:345
  25.8 1.6 %collective-permute-start.5 = (bf16[32,4096]{1,0:T(8,128)(2,1)S(1)}, bf16[32,4096]{1,0:T(8,128)(2,1)S(1)}, u32[]{:S(2)}, u32[]{:S(2)}) collective-permute-start(bf16[32,4096]{1,0:T(8,128)(2,1)S(1)} %collective-permute-done.2.rest_2_), channel_id=1, source_target_pairs={{0,4},{4,0},{8,12},{12,8},{1,5},{5,1},{9,13},{13,9},{2,6},{6,2},{1... | collective-permute-start | bytes 786440 | tf_op jit(solution)/shard_map/ppermute | solution.py:345
  25.8 9.9 %collective-permute-start.10 = (bf16[32,4096]{1,0:T(8,128)(2,1)S(1)}, bf16[32,4096]{1,0:T(8,128)(2,1)S(1)}, u32[]{:S(2)}, u32[]{:S(2)}) collective-permute-start(bf16[32,4096]{1,0:T(8,128)(2,1)S(1)} %attend.3.rest_0_), channel_id=1, source_target_pairs={{0,8},{4,12},{8,0},{12,4},{1,9},{5,13},{9,1},{13,5},{2,10},{6,14},... | collective-permute-start | bytes 786440 | tf_op jit(solution)/shard_map/ppermute | solution.py:345
  30.7 9.4 %collective-permute-start.6 = (bf16[64,1792]{1,0:T(8,128)(2,1)S(1)}, bf16[64,1792]{1,0:T(8,128)(2,1)S(1)}, u32[]{:S(2)}, u32[]{:S(2)}) collective-permute-start(bf16[64,1792]{1,0:T(8,128)(2,1)S(1)} %get-tuple-element.24), channel_id=1, source_target_pairs={{0,1},{3,2},{4,5},{7,6},{8,9},{11,10},{12,13},{15,14},{16,17},{19,... | collective-permute-start | bytes 688136 | tf_op jit(solution)/shard_map/ppermute | solution.py:353
  34.2 6.7 %collective-permute-start.9 = (bf16[32,4096]{1,0:T(8,128)(2,1)S(1)}, bf16[32,4096]{1,0:T(8,128)(2,1)S(1)}, u32[]{:S(2)}, u32[]{:S(2)}) collective-permute-start(bf16[32,4096]{1,0:T(8,128)(2,1)S(1)} %attend.3.rest_0_), channel_id=1, source_target_pairs={{0,4},{4,0},{8,12},{12,8},{1,5},{5,1},{9,13},{13,9},{2,6},{6,2},{1... | collective-permute-start | bytes 786440 | tf_op jit(solution)/shard_map/ppermute | solution.py:345
  34.3 10.0 %collective-permute-start.7 = (bf16[64,1792]{1,0:T(8,128)(2,1)S(1)}, bf16[64,1792]{1,0:T(8,128)(2,1)S(1)}, u32[]{:S(2)}, u32[]{:S(2)}) collective-permute-start(bf16[64,1792]{1,0:T(8,128)(2,1)S(1)} %get-tuple-element.25), channel_id=1, source_target_pairs={{0,1},{3,2},{4,5},{7,6},{8,9},{11,10},{12,13},{15,14},{16,17},{19,... | collective-permute-start | bytes 688136 | tf_op jit(solution)/shard_map/ppermute | solution.py:353
  35.8 5.2 %collective-permute-start.11 = (bf16[32,4096]{1,0:T(8,128)(2,1)S(1)}, bf16[32,4096]{1,0:T(8,128)(2,1)S(1)}, u32[]{:S(2)}, u32[]{:S(2)}) collective-permute-start(bf16[32,4096]{1,0:T(8,128)(2,1)S(1)} %collective-permute-done.10.rest_2_), channel_id=1, source_target_pairs={{0,4},{4,0},{8,12},{12,8},{1,5},{5,1},{9,13},{13,9},{2,6},{6,2},{1... | collective-permute-start | bytes 786440 | tf_op jit(solution)/shard_map/ppermute | solution.py:345
  40.2 4.1 %collective-permute-start.8 = (bf16[64,1792]{1,0:T(8,128)(2,1)S(1)}, bf16[64,1792]{1,0:T(8,128)(2,1)S(1)}, u32[]{:S(2)}, u32[]{:S(2)}) collective-permute-start(bf16[64,1792]{1,0:T(8,128)(2,1)S(1)} %add_convert_fusion.7), channel_id=1, source_target_pairs={{1,2},{2,1},{5,6},{6,5},{9,10},{10,9},{13,14},{14,13},{17,18},{18,... | collective-permute-start | bytes 688136 | tf_op jit(solution)/shard_map/ppermute | solution.py:357
  44.4 14.4 %collective-permute-start.13 = (bf16[64,1792]{1,0:T(8,128)(2,1)S(1)}, bf16[64,1792]{1,0:T(8,128)(2,1)S(1)}, u32[]{:S(2)}, u32[]{:S(2)}) collective-permute-start(bf16[64,1792]{1,0:T(8,128)(2,1)S(1)} %add_convert_fusion.5), channel_id=1, source_target_pairs={{1,2},{2,1},{5,6},{6,5},{9,10},{10,9},{13,14},{14,13},{17,18},{18,... | collective-permute-start | bytes 688136 | tf_op jit(solution)/shard_map/ppermute | solution.py:357
  45.1 22.8 %collective-permute-start.12 = (bf16[64,1792]{1,0:T(8,128)(2,1)S(1)}, bf16[64,1792]{1,0:T(8,128)(2,1)S(1)}, u32[]{:S(2)}, u32[]{:S(2)}) collective-permute-start(bf16[64,1792]{1,0:T(8,128)(2,1)S(1)} %add_convert_fusion.6.rest_0_), channel_id=1, source_target_pairs={{1,0},{2,3},{5,4},{6,7},{9,8},{10,11},{13,12},{14,15},{17,16},{18,... | collective-permute-start | bytes 688136 | tf_op jit(solution)/shard_map/ppermute | solution.py:361
  46.4 15.6 %collective-permute-start.15 = (bf16[64,1792]{1,0:T(8,128)(2,1)S(1)}, bf16[64,1792]{1,0:T(8,128)(2,1)S(1)}, u32[]{:S(2)}, u32[]{:S(2)}) collective-permute-start(bf16[64,1792]{1,0:T(8,128)(2,1)S(1)} %get-tuple-element.31), channel_id=1, source_target_pairs={{0,1},{3,2},{4,5},{7,6},{8,9},{11,10},{12,13},{15,14},{16,17},{19,... | collective-permute-start | bytes 688136 | tf_op jit(solution)/shard_map/ppermute | solution.py:353
  57.5 7.0 %collective-permute-start.18 = (bf16[64,1792]{1,0:T(8,128)(2,1)S(1)}, bf16[64,1792]{1,0:T(8,128)(2,1)S(1)}, u32[]{:S(2)}, u32[]{:S(2)}) collective-permute-start(bf16[64,1792]{1,0:T(8,128)(2,1)S(1)} %get-tuple-element.32), channel_id=1, source_target_pairs={{0,1},{3,2},{4,5},{7,6},{8,9},{11,10},{12,13},{15,14},{16,17},{19,... | collective-permute-start | bytes 688136 | tf_op jit(solution)/shard_map/ppermute | solution.py:353
  58.9 9.1 %collective-permute-start.14 = (bf16[64,1792]{1,0:T(8,128)(2,1)S(1)}, bf16[64,1792]{1,0:T(8,128)(2,1)S(1)}, u32[]{:S(2)}, u32[]{:S(2)}) collective-permute-start(bf16[64,1792]{1,0:T(8,128)(2,1)S(1)} %add_convert_fusion.4.rest_2_), channel_id=1, source_target_pairs={{1,0},{2,3},{5,4},{6,7},{9,8},{10,11},{13,12},{14,15},{17,16},{18,... | collective-permute-start | bytes 688136 | tf_op jit(solution)/shard_map/ppermute | solution.py:361
  62.1 3.1 %collective-permute-start.16 = (bf16[64,1792]{1,0:T(8,128)(2,1)S(1)}, bf16[64,1792]{1,0:T(8,128)(2,1)S(1)}, u32[]{:S(2)}, u32[]{:S(2)}) collective-permute-start(bf16[64,1792]{1,0:T(8,128)(2,1)S(1)} %add_convert_fusion.3), channel_id=1, source_target_pairs={{1,2},{2,1},{5,6},{6,5},{9,10},{10,9},{13,14},{14,13},{17,18},{18,... | collective-permute-start | bytes 688136 | tf_op jit(solution)/shard_map/ppermute | solution.py:357
  64.5 2.1 %collective-permute-start.19 = (bf16[64,1792]{1,0:T(8,128)(2,1)S(1)}, bf16[64,1792]{1,0:T(8,128)(2,1)S(1)}, u32[]{:S(2)}, u32[]{:S(2)}) collective-permute-start(bf16[64,1792]{1,0:T(8,128)(2,1)S(1)} %add_convert_fusion.1), channel_id=1, source_target_pairs={{1,2},{2,1},{5,6},{6,5},{9,10},{10,9},{13,14},{14,13},{17,18},{18,... | collective-permute-start | bytes 688136 | tf_op jit(solution)/shard_map/ppermute | solution.py:357
  65.3 12.6 %collective-permute-start.17 = (bf16[64,1792]{1,0:T(8,128)(2,1)S(1)}, bf16[64,1792]{1,0:T(8,128)(2,1)S(1)}, u32[]{:S(2)}, u32[]{:S(2)}) collective-permute-start(bf16[64,1792]{1,0:T(8,128)(2,1)S(1)} %add_convert_fusion.2.rest_4_), channel_id=1, source_target_pairs={{1,0},{2,3},{5,4},{6,7},{9,8},{10,11},{13,12},{14,15},{17,16},{18,... | collective-permute-start | bytes 688136 | tf_op jit(solution)/shard_map/ppermute | solution.py:361
  66.7 13.7 %collective-permute-start.20 = (bf16[64,1792]{1,0:T(8,128)(2,1)S(1)}, bf16[64,1792]{1,0:T(8,128)(2,1)S(1)}, u32[]{:S(2)}, u32[]{:S(2)}) collective-permute-start(bf16[64,1792]{1,0:T(8,128)(2,1)S(1)} %add_convert_fusion.rest_6_), channel_id=1, source_target_pairs={{1,0},{2,3},{5,4},{6,7},{9,8},{10,11},{13,12},{14,15},{17,16},{18,... | collective-permute-start | bytes 688136 | tf_op jit(solution)/shard_map/ppermute | solution.py:361

commit v4 on v3

--- a/solution.py
+++ b/solution.py
@@ -277,42 +277,22 @@
         out_ref[t] = jnp.where(col_id == wanted + t, 1.0, 0.0).astype(jnp.bfloat16)
 
 
-def order_kernel(pieces, z_ref, pick_ref, *rest):
-    out_ref, x = rest[2 * pieces], rest[2 * pieces + 1]
-    if pieces == 0:
-        x_ref, out_ref = rest
-        for t in range(pick_ref.shape[0]):
-            out_ref[t] = jnp.dot(pick_ref[t], x_ref[...], preferred_element_type=jnp.float32).astype(jnp.bfloat16)
-        return
-    inner = (z_ref[0] == 1) | (z_ref[0] == 2)
-    rows = x.shape[0] // pieces
-
-    @pl.when(inner)
-    def _():
-        for i in range(pieces):
-            x[i * rows : (i + 1) * rows, :] = rest[2 * i][...]
-
-    @pl.when(jnp.logical_not(inner))
-    def _():
-        for i in range(pieces):
-            x[i * rows : (i + 1) * rows, :] = rest[2 * i + 1][...]
-
+def order_kernel(pieces, pick_ref, *rest):
+    out_ref = rest[pieces]
+    whole = jnp.concatenate([rest[i][...] for i in range(pieces)], axis=0)
     for t in range(pick_ref.shape[0]):
-        out_ref[t] = jnp.dot(pick_ref[t], x[...], preferred_element_type=jnp.float32).astype(jnp.bfloat16)
-
-
-def project_kernel(pieces, *rest):
-    parts, weight, outs, x = rest[:4], rest[4], rest[5 : 5 + pieces], rest[5 + pieces]
+        out_ref[t] = jnp.dot(pick_ref[t], whole, preferred_element_type=jnp.float32).astype(jnp.bfloat16)
+
+
+def project_kernel(*rest):
+    parts, weight, out, x = rest[:4], rest[4], rest[5], rest[6]
     rows = parts[0].shape[0]
     for q in range(4):
         x[q * rows : (q + 1) * rows, :] = parts[q][...]
-    out_rows = outs[0].shape[0]
 
     def tile(n, carry):
         cols = pl.ds(pl.multiple_of(n * BLOCK, BLOCK), BLOCK)
-        res = jnp.dot(x[...], weight[:, cols], preferred_element_type=jnp.float32).astype(jnp.bfloat16)
-        for i in range(pieces):
-            outs[i][:, cols] = res[i * out_rows : (i + 1) * out_rows]
+        out[:, cols] = jnp.dot(x[...], weight[:, cols], preferred_element_type=jnp.float32).astype(jnp.bfloat16)
         return carry
 
     lax.fori_loop(0, weight.shape[1] // BLOCK, tile, jnp.int32(0))
@@ -343,22 +323,6 @@
 def flip(x, axis, distance):
     size = lax.axis_size(axis)
     return lax.ppermute(x, axis, [(i, i ^ distance) for i in range(size)])
-
-
-def add(x, y):
-    return (x.astype(jnp.float32) + y.astype(jnp.float32)).astype(jnp.bfloat16)
-
-
-def inwards(piece):
-    return lax.ppermute(piece, "head", [(0, 1), (3, 2)])
-
-
-def across_middle(pair):
-    return lax.ppermute(pair, "head", [(1, 2), (2, 1)])
-
-
-def outwards(whole):
-    return lax.ppermute(whole, "head", [(1, 0), (2, 3)])
 
 
 def local(latent_cache, lengths, decode_rows, q_nope, q_rope, new_latent, key_up, value_up, out_proj):
@@ -376,7 +340,6 @@
     packed_rows = per_pair * rows + per_pair * rows // 2 + -(-width // LANES) * fresh_rows
     sizes = (sources, per_pair, steps, heads, requests, fresh_rows)
     me = lax.axis_index("seq").astype(jnp.int32).reshape(1)
-    z = lax.axis_index("head").astype(jnp.int32).reshape(1)
     cache = latent_cache.T
 
     pick = pl.pallas_call(
@@ -432,36 +395,30 @@
             name="attend",
         )(me, decode_rows, lengths, *received, cache, key_up, value_up)
 
-    def order(pieces, arrays, scratch):
+    def order(*pieces):
         return pl.pallas_call(
-            functools.partial(order_kernel, pieces),
+            functools.partial(order_kernel, len(pieces)),
             out_shape=jax.ShapeDtypeStruct((steps, sources * requests, columns), jnp.bfloat16),
-            in_specs=[smem()] + [vmem()] * (1 + len(arrays)),
+            in_specs=[vmem()] * (1 + len(pieces)),
             out_specs=vmem(),
-            scratch_shapes=scratch,
             compiler_params=limit(16),
             cost_estimate=cost(2),
             name="order_rows",
-        )(z, pick, *arrays)
+        )(pick, *pieces)
 
     if not relative:
         received = lax.all_to_all(packed[0], "seq", split_axis=0, concat_axis=0, tiled=True)
         every_row = lax.all_gather(attend([received], 0), "seq", axis=0, tiled=True)
         partial_value = jnp.dot(every_row, out_proj, preferred_element_type=jnp.float32).astype(jnp.bfloat16)
-        shares = lax.all_to_all(partial_value, "head", split_axis=0, concat_axis=0, tiled=True)
-        shares = shares.reshape(head_devices, -1, columns)
-        summed = jnp.sum(shares.astype(jnp.float32), axis=0).astype(jnp.bfloat16)
-        return order(0, [lax.all_gather(summed, "head", axis=0, tiled=True)], [])
-
-    pieces = 2
+        return order(lax.psum(partial_value, "head"))
 
     def project(parts):
         part_rows = parts[0].shape[0]
         return pl.pallas_call(
-            functools.partial(project_kernel, pieces),
-            out_shape=[jax.ShapeDtypeStruct((4 * part_rows // pieces, columns), jnp.bfloat16)] * pieces,
+            project_kernel,
+            out_shape=jax.ShapeDtypeStruct((4 * part_rows, columns), jnp.bfloat16),
             in_specs=[vmem()] * 5,
-            out_specs=[vmem()] * pieces,
+            out_specs=vmem(),
             scratch_shapes=[pltpu.VMEM((4 * part_rows, out_proj.shape[0]), jnp.bfloat16)],
             compiler_params=limit(24),
             cost_estimate=cost(6),
@@ -476,23 +433,10 @@
     near = [near_rows, flip(near_rows, "seq", 1), near_across, flip(near_across, "seq", 1)]
     far_across = flip(far_rows, "seq", 2)
     far = [far_rows, flip(far_rows, "seq", 1), far_across, flip(far_across, "seq", 1)]
-    first, second = project(near)
-    first_in, second_in = inwards(first), inwards(second)
-    first_pair = add(first, first_in)
-    first_cross = across_middle(first_pair)
-    third, fourth = project(far)
-    second_in, first_cross, third, fourth = lax.optimization_barrier((second_in, first_cross, third, fourth))
-    second_pair = add(second, second_in)
-    second_cross = across_middle(second_pair)
-    third_in, fourth_in = inwards(third), inwards(fourth)
-    first_whole = add(first_pair, first_cross)
-    second_whole = add(second_pair, second_cross)
-    third_pair, fourth_pair = add(third, third_in), add(fourth, fourth_in)
-    third_whole = add(third_pair, across_middle(third_pair))
-    fourth_whole = add(fourth_pair, across_middle(fourth_pair))
-    sums = [(whole, outwards(whole)) for whole in (first_whole, second_whole, third_whole, fourth_whole)]
-    arrays = [array for both in sums for array in both]
-    return order(len(sums), arrays, [pltpu.VMEM((steps * sources * requests, columns), jnp.bfloat16)])
+    near_sum = lax.psum(project(near), "head")
+    far_share = lax.psum_scatter(project(far), "head", scatter_dimension=0, tiled=True)
+    far_sum = lax.all_gather(far_share, "head", axis=0, tiled=True)
+    return order(near_sum, far_sum)
 
 
 def solution(mesh):

time: 83.5 us -> 118 us (1.41)
  starting transfers between devices: 33.7 us -> 7.28 us
  waiting for transfers between devices: 20.4 us -> 43.2 us
  blocking collectives: 0 us -> 17.6 us
  between operations: 0.47 us -> 13.6 us
  local copies, waits for them, and re-layouts: 0.82 us -> 7.01 us
  Pallas kernels: 26.2 us -> 28.8 us
    ppermute x12 -> x0, starting transfers between devices: 25.1 us -> none  [the longest x4 17.3 us: inwards(): return lax.ppermute(piece, 'head', [(0, 1), (3, 2)])]
    psum x0 -> x1, waiting for transfers between devices: none -> 22.3 us  [local(): near_sum = lax.psum(project(near), 'head')]
    ppermute x12 -> x0, waiting for transfers between devices: 19.9 us -> none  [the longest x4 12.3 us: outwards(): return lax.ppermute(whole, 'head', [(1, 0), (2, 3)])]
    all_gather x0 -> x1, blocking collectives: none -> 17.6 us  [local(): far_sum = lax.all_gather(far_share, 'head', axis=0, tiled=True)]
    reduce_scatter x0 -> x1, waiting for transfers between devices: none -> 11.3 us  [local(): lax.psum_scatter(project(far), 'head', scatter_dimension=0, tiled=True)]
    ppermute x9, waiting for transfers between devices: 0.51 us -> 9.69 us  [flip(): return lax.ppermute(x, axis, [(i, i ^ distance) for i in range(size)])]
    unnamed x28 -> x32, local copies, waits for them, and re-layouts: 0.82 us -> 7.01 us
    pallas_call x3, Pallas kernels: 8.42 us -> 9.9 us  [the longest x2 8.23 us: project(): pl.pallas_call(project_kernel, out_shape=jax.ShapeDtypeStruct((4 * part_r...]
  transfers between devices with their start and end apart: 21 -> 11, of which waited for: 6 -> 6; matrix products, arithmetic and copies ran while one was open for 0% -> 0% of each run, Pallas kernels for 27% -> 18%
where the time goes in v4:
time: 118 us
  waiting for transfers between devices  43.2 us (37%)
  Pallas kernels  28.8 us (24%)
  blocking collectives  17.6 us (15%)
  between operations  13.6 us (12%)
  starting transfers between devices  7.28 us (6%)
  local copies, waits for them, and re-layouts  7.01 us (6%)
    psum x1, waiting for transfers between devices, local(): near_sum = lax.psum(project(near), 'head')  22.3 us
    all_gather x1, blocking collectives, local(): far_sum = lax.all_gather(far_share, 'head', axis=0, tiled=True)  17.6 us
    pallas_call x2, Pallas kernels, attend(): pl.pallas_call(functools.partial(attend_kernel, sizes, scale, relative, b...  16.7 us
    reduce_scatter x1, waiting for transfers between devices, local(): lax.psum_scatter(project(far), 'head', scatter_dimension=0, tiled=True)  11.3 us
    ppermute x9, waiting for transfers between devices, flip(): return lax.ppermute(x, axis, [(i, i ^ distance) for i in range(size)])  9.69 us
    pallas_call x2, Pallas kernels, project(): pl.pallas_call(project_kernel, out_shape=jax.ShapeDtypeStruct((4 * part_r...  8.23 us
    ppermute x9, starting transfers between devices, flip(): return lax.ppermute(x, axis, [(i, i ^ distance) for i in range(size)])  7.23 us
    unnamed x32, local copies, waits for them, and re-layouts  7.01 us
  transfers between devices with their start and end apart: 11, of which 6 were waited for; matrix products, arithmetic and copies ran while one was open for 0% of the time, Pallas kernels for 18%

profile of v4, /device:TPU:0, one launch (start us, length us, event | category | flops | bytes accessed | tf_op | source)
XLA Modules:
  0.0 117.5 jit_solution(7209303712384637343)
XLA Ops:
  6.6 0.7 copy-done.8
  7.3 1.1 place_rows.1.after_ref.pick_ref
  8.4 0.0 copy-done.3
  8.4 0.0 copy-done.4
  8.4 0.0 copy-done.6
  8.4 0.0 slice-start.5
  8.4 0.0 copy-start.1
  8.4 0.0 copy-start.2
  8.5 0.0 copy-start.7
  8.5 0.0 copy-start.9
  8.5 1.1 pack_queries.1
  9.6 0.5 collective-permute-start
  10.1 2.6 %collective-permute-start.3 = (bf16[1,848,128]{2,1,0:T(8,128)(2,1)S(1)}, bf16[1,848,128]{2,1,0:T(8,128)(2,1)S(1)}, u32[]{:S(2)}, u32[]{:S(2)}) collective-permute-start(bf16[1,848,128]{2,1,0:T(8,128)(2,1)S(1)} %get-tuple-element.13), channel_id=1, source_target_pairs={{0,8},{4,12},{8,0},{12,4},{1,9},{5,13},{9,1},{13,5},{2,10},{6,14},... | collective-permute-start | bytes 651272 | tf_op jit(solution)/shard_map/ppermute | solution.py:325
  12.7 0.1 collective-permute-start.4
  12.8 0.0 collective-permute-done.rest_1_
  12.8 0.0 slice-done.5
  12.9 0.0 slice-start
  12.9 0.0 slice-start.1
  12.9 8.4 %attend.2.rest_0_ = bf16[32,4096]{1,0:T(8,128)(2,1)S(1)} custom-call(s32[1]{0:T(128)} %bitcast.me_ref, s32[64]{0:T(128)S(1)} %copy-done.9, s32[4,16]{1,0:T(4,128)S(1)} %copy-done.7, bf16[1,848,128]{2,1,0:T(8,128)(2,1)S(1)} %get-tuple-element.11.rest_0_, bf16[1,848,128]{2,1,0:T(8,128)(2,1)S(1)} %collective-permute-done.rest_1_, ...), custom_call_target="tpu_custom_call" | custom-call | flops 8000000000 | bytes 24000000 | tf_op jit(solution)/shard_map/attend/pallas_call | solution.py:375
  21.2 0.0 slice-start.2
  21.3 0.0 slice-start.3
  21.3 2.5 %collective-permute-start.2 = (bf16[32,4096]{1,0:T(8,128)(2,1)S(1)}, bf16[32,4096]{1,0:T(8,128)(2,1)S(1)}, u32[]{:S(2)}, u32[]{:S(2)}) collective-permute-start(bf16[32,4096]{1,0:T(8,128)(2,1)S(1)} %attend.2.rest_0_), channel_id=1, source_target_pairs={{0,8},{4,12},{8,0},{12,4},{1,9},{5,13},{9,1},{13,5},{2,10},{6,14},... | collective-permute-start | bytes 786440 | tf_op jit(solution)/shard_map/ppermute | solution.py:325
  23.8 0.0 collective-permute-done.3.rest_0_
  23.8 0.0 collective-permute-done.4.rest_1_
  23.8 8.3 %attend.3.rest_0_ = bf16[32,4096]{1,0:T(8,128)(2,1)S(1)} custom-call(s32[1]{0:T(128)} %bitcast.me_ref, s32[64]{0:T(128)S(1)} %copy-done.9, s32[4,16]{1,0:T(4,128)S(1)} %copy-done.7, bf16[1,848,128]{2,1,0:T(8,128)(2,1)S(1)} %collective-permute-done.3.rest_0_, bf16[1,848,128]{2,1,0:T(8,128)(2,1)S(1)} %collective-permute-done.4.rest_1_, ...), custom_call_target="tpu_custom_call" | custom-call | flops 8000000000 | bytes 24000000 | tf_op jit(solution)/shard_map/attend/pallas_call | solution.py:375
  32.1 0.0 collective-permute-done.2.rest_2_
  32.1 0.9 collective-permute-start.7
  33.0 0.1 collective-permute-start.6
  33.1 6.8 %collective-permute-done.7.rest_2_ = bf16[32,4096]{1,0:T(8,128)(2,1)S(1)} collective-permute-done((bf16[32,4096]{1,0:T(8,128)(2,1)S(1)}, bf16[32,4096]{1,0:T(8,128)(2,1)S(1)}, u32[]{:S(2)}, u32[]{:S(2)}) %collective-permute-start.7) | collective-permute-done | bytes 262176 | tf_op jit(solution)/shard_map/ppermute | solution.py:325
  39.9 0.0 collective-permute-start.8
  39.9 0.0 collective-permute-done.6.rest_1_
  39.9 1.5 %collective-permute-done.8.rest_3_ = bf16[32,4096]{1,0:T(8,128)(2,1)S(1)} collective-permute-done((bf16[32,4096]{1,0:T(8,128)(2,1)S(1)}, bf16[32,4096]{1,0:T(8,128)(2,1)S(1)}, u32[]{:S(2)}, u32[]{:S(2)}) %collective-permute-start.8) | collective-permute-done | bytes 262176 | tf_op jit(solution)/shard_map/ppermute | solution.py:325
  41.4 0.0 slice-done
  41.4 4.1 %project_out.3 = bf16[128,1792]{1,0:T(8,128)(2,1)} custom-call(bf16[32,4096]{1,0:T(8,128)(2,1)S(1)} %attend.3.rest_0_, bf16[32,4096]{1,0:T(8,128)(2,1)S(1)} %collective-permute-done.6.rest_1_, bf16[32,4096]{1,0:T(8,128)(2,1)S(1)} %collective-permute-done.7.rest_2_, bf16[32,4096]{1,0:T(8,128)(2,1)S(1)} %collective-permute-done.8.rest_3_, ...), custom_call_target="tpu_custom_call" | custom-call | flops 6000000000 | bytes 18000000 | tf_op jit(solution)/shard_map/project_out/pallas_call | solution.py:417
  45.5 0.0 reduce-scatter.2.cloned.1.call-update
  45.6 0.0 all-reduce.2.cloned.1.call-start
  45.6 0.2 collective-permute-start.1
  45.8 0.4 collective-permute-start.5
  46.2 1.0 collective-permute-done.1.rest_1_
  47.2 0.4 collective-permute-done.5.rest_3_
  47.6 5.2 %copy-done = bf16[4096,1792]{1,0:T(8,128)(2,1)S(1)} copy-done((bf16[4096,1792]{1,0:T(8,128)(2,1)S(1)}, bf16[4096,1792]{1,0:T(8,128)(2,1)}, u32[]{:S(2)}) %copy-start) | copy-done | bytes 14680088
  52.8 4.1 %project_out.2 = bf16[128,1792]{1,0:T(8,128)(2,1)} custom-call(bf16[32,4096]{1,0:T(8,128)(2,1)S(1)} %attend.2.rest_0_, bf16[32,4096]{1,0:T(8,128)(2,1)S(1)} %collective-permute-done.1.rest_1_, bf16[32,4096]{1,0:T(8,128)(2,1)S(1)} %collective-permute-done.2.rest_2_, bf16[32,4096]{1,0:T(8,128)(2,1)S(1)} %collective-permute-done.5.rest_3_, ...), custom_call_target="tpu_custom_call" | custom-call | flops 6000000000 | bytes 18000000 | tf_op jit(solution)/shard_map/project_out/pallas_call | solution.py:417
  56.9 0.0 all-reduce.2.cloned.1.call-update
  56.9 11.3 %reduce-scatter.2.cloned.1.call-done = bf16[32,1792]{1,0:T(8,128)(2,1)} async-done(((bf16[128,1792]{1,0:T(8,128)(2,1)}), bf16[32,1792]{1,0:T(8,128)(2,1)}) %reduce-scatter.2.cloned.1.call-update) | async-done | bytes 114704 | tf_op jit(solution)/shard_map/reduce_scatter | solution.py:437
  68.2 17.6 %all_gather.3.rest_1_ = bf16[128,1792]{1,0:T(8,128)(2,1)S(1)} all-gather(bf16[32,1792]{1,0:T(8,128)(2,1)} %reduce-scatter.2.cloned.1.call-done), channel_id=1, replica_groups=mesh['groups'=2,'seq'=4,'head'=4] {'head'}, dimensions={0}, use_global_device_ids=true | all-gather | bytes 573440 | tf_op jit(solution)/shard_map/all_gather | solution.py:438
  85.8 22.3 %all-reduce.2.cloned.1.call-done.rest_0_ = bf16[128,1792]{1,0:T(8,128)(2,1)} async-done(((bf16[128,1792]{1,0:T(8,128)(2,1)}), bf16[128,1792]{1,0:T(8,128)(2,1)}) %all-reduce.2.cloned.1.call-update) | async-done | bytes 458768 | tf_op jit(solution)/shard_map/psum | solution.py:436
  108.0 1.0 copy-done.5
  109.0 1.7 %order_rows.1 = bf16[4,64,1792]{2,1,0:T(8,128)(2,1)} custom-call(bf16[4,64,256]{2,1,0:T(8,128)(2,1)S(1)} %place_rows.1.after_ref.pick_ref, bf16[128,1792]{1,0:T(8,128)(2,1)S(1)} %copy-done.5, bf16[128,1792]{1,0:T(8,128)(2,1)S(1)} %all_gather.3.rest_1_), custom_call_target="tpu_custom_call" | custom-call | flops 2000000000 | bytes 6000000 | tf_op jit(solution)/shard_map/order_rows/pallas_call | solution.py:399
  (18 shorter events, 0.0 us)
Async XLA Ops:
  6.5 1.9 %copy-start.3 = (bf16[4,16,32,128]{3,2,1,0:T(8,128)(2,1)S(1)}, bf16[4,16,32,128]{3,2,1,0:T(8,128)(2,1)}, u32[]{:S(2)}) copy-start(bf16[4,16,32,128]{3,2,1,0:T(8,128)(2,1)} %nope_ref.1) | copy-start | bytes 1572868
  6.5 1.9 %copy-start.4 = (bf16[4,16,32,64]{3,2,1,0:T(8,128)(2,1)S(1)}, bf16[4,16,32,64]{3,2,1,0:T(8,128)(2,1)}, u32[]{:S(2)}) copy-start(bf16[4,16,32,64]{3,2,1,0:T(8,128)(2,1)} %rope_ref.1) | copy-start | bytes 786436
  6.5 1.9 %copy-start.6 = (bf16[4,16,576]{2,1,0:T(8,128)(2,1)S(1)}, bf16[4,16,576]{2,1,0:T(8,128)(2,1)}, u32[]{:S(2)}) copy-start(bf16[4,16,576]{2,1,0:T(8,128)(2,1)} %fresh_ref.1) | copy-start | bytes 221188
  6.5 61.6 %reduce-scatter.2.cloned.1.call-start = ((), (), s32[]{:S(2)}) async-start(), calls=%async_computation.2 | async-start | bytes 573440 | tf_op jit(solution)/shard_map/reduce_scatter | solution.py:437
  6.5 0.7 copy-start.8
  7.3 5.5 %slice-start.4 = ((s8[4718592]{0:T(1024)(128)(4,1)}), s8[4194304]{0:T(1024)(128)(4,1)S(1)}, s32[]{:S(2)}) async-start(s8[4718592]{0:T(1024)(128)(4,1)} %bitcast.4), calls=%async_computation.7 | async-start | bytes 8388608
  8.4 4.4 %slice-start.5 = ((s8[4718592]{0:T(1024)(128)(4,1)}), s8[524288]{0:T(1024)(128)(4,1)S(1)}, s32[]{:S(2)}) async-start(s8[4718592]{0:T(1024)(128)(4,1)} %bitcast.4), calls=%async_computation.8 | async-start | bytes 1048576
  8.4 4.4 %copy-start.1 = (bf16[32,128,512]{2,1,0:T(8,128)(2,1)S(1)}, bf16[32,128,512]{2,1,0:T(8,128)(2,1)}, u32[]{:S(2)}) copy-start(bf16[32,128,512]{2,1,0:T(8,128)(2,1)} %rest_3_.3) | copy-start | bytes 12582916
  8.4 4.4 %copy-start.2 = (bf16[32,512,128]{2,1,0:T(8,128)(2,1)S(1)}, bf16[32,512,128]{2,1,0:T(8,128)(2,1)}, u32[]{:S(2)}) copy-start(bf16[32,512,128]{2,1,0:T(8,128)(2,1)} %rest_4_.5) | copy-start | bytes 12582916
  8.5 4.4 %copy-start.7 = (s32[4,16]{1,0:T(4,128)S(1)}, s32[4,16]{1,0:T(4,128)}, u32[]{:S(2)}) copy-start(s32[4,16]{1,0:T(4,128)} %length_ref.3) | copy-start | bytes 772
  8.5 4.4 %copy-start.9 = (s32[64]{0:T(128)S(1)}, s32[64]{0:T(128)}, u32[]{:S(2)}) copy-start(s32[64]{0:T(128)} %decode_ref.7) | copy-start | bytes 772
  9.6 3.2 %collective-permute-start = (bf16[1,848,128]{2,1,0:T(8,128)(2,1)S(1)}, bf16[1,848,128]{2,1,0:T(8,128)(2,1)S(1)}, u32[]{:S(2)}, u32[]{:S(2)}) collective-permute-start(bf16[1,848,128]{2,1,0:T(8,128)(2,1)S(1)} %get-tuple-element.12), channel_id=1, source_target_pairs={{0,4},{4,0},{8,12},{12,8},{1,5},{5,1},{9,13},{13,9},{2,6},{6,2},{1... | collective-permute-start | bytes 651272 | tf_op jit(solution)/shard_map/ppermute | solution.py:325
  10.1 13.6 %collective-permute-start.3 = (bf16[1,848,128]{2,1,0:T(8,128)(2,1)S(1)}, bf16[1,848,128]{2,1,0:T(8,128)(2,1)S(1)}, u32[]{:S(2)}, u32[]{:S(2)}) collective-permute-start(bf16[1,848,128]{2,1,0:T(8,128)(2,1)S(1)} %get-tuple-element.13), channel_id=1, source_target_pairs={{0,8},{4,12},{8,0},{12,4},{1,9},{5,13},{9,1},{13,5},{2,10},{6,14},... | collective-permute-start | bytes 651272 | tf_op jit(solution)/shard_map/ppermute | solution.py:325
  12.7 11.0 %collective-permute-start.4 = (bf16[1,848,128]{2,1,0:T(8,128)(2,1)S(1)}, bf16[1,848,128]{2,1,0:T(8,128)(2,1)S(1)}, u32[]{:S(2)}, u32[]{:S(2)}) collective-permute-start(bf16[1,848,128]{2,1,0:T(8,128)(2,1)S(1)} %get-tuple-element.14), channel_id=1, source_target_pairs={{0,12},{4,8},{8,4},{12,0},{1,13},{5,9},{9,5},{13,1},{2,14},{6,10},... | collective-permute-start | bytes 651272 | tf_op jit(solution)/shard_map/ppermute | solution.py:325
  12.9 28.5 %slice-start = ((s8[14680064]{0:T(1024)(128)(4,1)}), s8[4194304]{0:T(1024)(128)(4,1)S(1)}, s32[]{:S(2)}) async-start(s8[14680064]{0:T(1024)(128)(4,1)} %bitcast.2), calls=%async_computation.3 | async-start | bytes 8388608
  12.9 28.5 %slice-start.1 = ((s8[14680064]{0:T(1024)(128)(4,1)}), s8[4194304]{0:T(1024)(128)(4,1)S(1)}, s32[]{:S(2)}) async-start(s8[14680064]{0:T(1024)(128)(4,1)} %bitcast.2), calls=%async_computation.4 | async-start | bytes 8388608
  21.2 20.2 %slice-start.2 = ((s8[14680064]{0:T(1024)(128)(4,1)}), s8[4194304]{0:T(1024)(128)(4,1)S(1)}, s32[]{:S(2)}) async-start(s8[14680064]{0:T(1024)(128)(4,1)} %bitcast.2), calls=%async_computation.5 | async-start | bytes 8388608
  21.3 20.2 %slice-start.3 = ((s8[14680064]{0:T(1024)(128)(4,1)}), s8[2097152]{0:T(1024)(128)(4,1)S(1)}, s32[]{:S(2)}) async-start(s8[14680064]{0:T(1024)(128)(4,1)} %bitcast.2), calls=%async_computation.6 | async-start | bytes 4194304
  21.3 10.9 %collective-permute-start.2 = (bf16[32,4096]{1,0:T(8,128)(2,1)S(1)}, bf16[32,4096]{1,0:T(8,128)(2,1)S(1)}, u32[]{:S(2)}, u32[]{:S(2)}) collective-permute-start(bf16[32,4096]{1,0:T(8,128)(2,1)S(1)} %attend.2.rest_0_), channel_id=1, source_target_pairs={{0,8},{4,12},{8,0},{12,4},{1,9},{5,13},{9,1},{13,5},{2,10},{6,14},... | collective-permute-start | bytes 786440 | tf_op jit(solution)/shard_map/ppermute | solution.py:325
  32.1 7.7 %collective-permute-start.7 = (bf16[32,4096]{1,0:T(8,128)(2,1)S(1)}, bf16[32,4096]{1,0:T(8,128)(2,1)S(1)}, u32[]{:S(2)}, u32[]{:S(2)}) collective-permute-start(bf16[32,4096]{1,0:T(8,128)(2,1)S(1)} %attend.3.rest_0_), channel_id=1, source_target_pairs={{0,8},{4,12},{8,0},{12,4},{1,9},{5,13},{9,1},{13,5},{2,10},{6,14},... | collective-permute-start | bytes 786440 | tf_op jit(solution)/shard_map/ppermute | solution.py:325
  33.0 6.8 %collective-permute-start.6 = (bf16[32,4096]{1,0:T(8,128)(2,1)S(1)}, bf16[32,4096]{1,0:T(8,128)(2,1)S(1)}, u32[]{:S(2)}, u32[]{:S(2)}) collective-permute-start(bf16[32,4096]{1,0:T(8,128)(2,1)S(1)} %attend.3.rest_0_), channel_id=1, source_target_pairs={{0,4},{4,0},{8,12},{12,8},{1,5},{5,1},{9,13},{13,9},{2,6},{6,2},{1... | collective-permute-start | bytes 786440 | tf_op jit(solution)/shard_map/ppermute | solution.py:325
  39.9 1.5 %collective-permute-start.8 = (bf16[32,4096]{1,0:T(8,128)(2,1)S(1)}, bf16[32,4096]{1,0:T(8,128)(2,1)S(1)}, u32[]{:S(2)}, u32[]{:S(2)}) collective-permute-start(bf16[32,4096]{1,0:T(8,128)(2,1)S(1)} %collective-permute-done.7.rest_2_), channel_id=1, source_target_pairs={{0,4},{4,0},{8,12},{12,8},{1,5},{5,1},{9,13},{13,9},{2,6},{6,2},{1... | collective-permute-start | bytes 786440 | tf_op jit(solution)/shard_map/ppermute | solution.py:325
  45.6 62.4 %all-reduce.2.cloned.1.call-start = ((), (), s32[]{:S(2)}) async-start(), calls=%async_computation.1 | async-start | bytes 917504 | tf_op jit(solution)/shard_map/psum | solution.py:436
  45.6 1.6 %collective-permute-start.1 = (bf16[32,4096]{1,0:T(8,128)(2,1)S(1)}, bf16[32,4096]{1,0:T(8,128)(2,1)S(1)}, u32[]{:S(2)}, u32[]{:S(2)}) collective-permute-start(bf16[32,4096]{1,0:T(8,128)(2,1)S(1)} %attend.2.rest_0_), channel_id=1, source_target_pairs={{0,4},{4,0},{8,12},{12,8},{1,5},{5,1},{9,13},{13,9},{2,6},{6,2},{1... | collective-permute-start | bytes 786440 | tf_op jit(solution)/shard_map/ppermute | solution.py:325
  45.8 1.8 %collective-permute-start.5 = (bf16[32,4096]{1,0:T(8,128)(2,1)S(1)}, bf16[32,4096]{1,0:T(8,128)(2,1)S(1)}, u32[]{:S(2)}, u32[]{:S(2)}) collective-permute-start(bf16[32,4096]{1,0:T(8,128)(2,1)S(1)} %collective-permute-done.2.rest_2_), channel_id=1, source_target_pairs={{0,4},{4,0},{8,12},{12,8},{1,5},{5,1},{9,13},{13,9},{2,6},{6,2},{1... | collective-permute-start | bytes 786440 | tf_op jit(solution)/shard_map/ppermute | solution.py:325
  47.6 5.2 %copy-start = (bf16[4096,1792]{1,0:T(8,128)(2,1)S(1)}, bf16[4096,1792]{1,0:T(8,128)(2,1)}, u32[]{:S(2)}) copy-start(bf16[4096,1792]{1,0:T(8,128)(2,1)} %rest_4_.7) | copy-start | bytes 44040196
  108.0 1.0 copy-start.5
Sparse Core Ops, SparseCore 0:
  45.7 22.4 reduce-scatter.1
  70.6 37.3 all-reduce.1

commit v5 on v4

--- a/solution.py
+++ b/solution.py
@@ -277,25 +277,39 @@
         out_ref[t] = jnp.where(col_id == wanted + t, 1.0, 0.0).astype(jnp.bfloat16)
 
 
-def order_kernel(pieces, pick_ref, *rest):
-    out_ref = rest[pieces]
-    whole = jnp.concatenate([rest[i][...] for i in range(pieces)], axis=0)
+def order_kernel(halves, z_ref, pick_ref, *rest):
+    pieces, out_ref, x = rest[:-2], rest[-2], rest[-1]
+    middle = (z_ref[0] == 1) | (z_ref[0] == 2)
+    rows = x.shape[0] // halves
+    each = len(pieces) // (2 * halves)
+    cols = x.shape[1] // each
+
+    def assemble(side):
+        for h in range(halves):
+            for c in range(each):
+                x[h * rows : (h + 1) * rows, c * cols : (c + 1) * cols] = pieces[2 * (h * each + c) + side][...]
+
+    pl.when(middle)(lambda: assemble(0))
+    pl.when(jnp.logical_not(middle))(lambda: assemble(1))
     for t in range(pick_ref.shape[0]):
-        out_ref[t] = jnp.dot(pick_ref[t], whole, preferred_element_type=jnp.float32).astype(jnp.bfloat16)
-
-
-def project_kernel(*rest):
+        out_ref[t] = jnp.dot(pick_ref[t], x[...], preferred_element_type=jnp.float32).astype(jnp.bfloat16)
+
+
+def order_whole_kernel(pick_ref, x_ref, out_ref):
+    for t in range(pick_ref.shape[0]):
+        out_ref[t] = jnp.dot(pick_ref[t], x_ref[...], preferred_element_type=jnp.float32).astype(jnp.bfloat16)
+
+
+def project_kernel(first_col, *rest):
     parts, weight, out, x = rest[:4], rest[4], rest[5], rest[6]
     rows = parts[0].shape[0]
     for q in range(4):
         x[q * rows : (q + 1) * rows, :] = parts[q][...]
-
-    def tile(n, carry):
-        cols = pl.ds(pl.multiple_of(n * BLOCK, BLOCK), BLOCK)
-        out[:, cols] = jnp.dot(x[...], weight[:, cols], preferred_element_type=jnp.float32).astype(jnp.bfloat16)
-        return carry
-
-    lax.fori_loop(0, weight.shape[1] // BLOCK, tile, jnp.int32(0))
+    cols = out.shape[1]
+    for c in range(0, cols, BLOCK):
+        n = min(BLOCK, cols - c)
+        tile = jnp.dot(x[...], weight[:, first_col + c : first_col + c + n], preferred_element_type=jnp.float32)
+        out[:, c : c + n] = tile.astype(jnp.bfloat16)
 
 
 def smem():
@@ -323,6 +337,22 @@
 def flip(x, axis, distance):
     size = lax.axis_size(axis)
     return lax.ppermute(x, axis, [(i, i ^ distance) for i in range(size)])
+
+
+def add(x, y):
+    return (x.astype(jnp.float32) + y.astype(jnp.float32)).astype(jnp.bfloat16)
+
+
+def inwards(piece):
+    return lax.ppermute(piece, "head", [(0, 1), (3, 2)])
+
+
+def across_middle(pair):
+    return lax.ppermute(pair, "head", [(1, 2), (2, 1)])
+
+
+def outwards(whole):
+    return lax.ppermute(whole, "head", [(1, 0), (2, 3)])
 
 
 def local(latent_cache, lengths, decode_rows, q_nope, q_rope, new_latent, key_up, value_up, out_proj):
@@ -340,6 +370,7 @@
     packed_rows = per_pair * rows + per_pair * rows // 2 + -(-width // LANES) * fresh_rows
     sizes = (sources, per_pair, steps, heads, requests, fresh_rows)
     me = lax.axis_index("seq").astype(jnp.int32).reshape(1)
+    z = lax.axis_index("head").astype(jnp.int32).reshape(1)
     cache = latent_cache.T
 
     pick = pl.pallas_call(
@@ -395,33 +426,41 @@
             name="attend",
         )(me, decode_rows, lengths, *received, cache, key_up, value_up)
 
-    def order(*pieces):
+    def order(kernel, in_specs, scratch, arrays):
         return pl.pallas_call(
-            functools.partial(order_kernel, len(pieces)),
+            kernel,
             out_shape=jax.ShapeDtypeStruct((steps, sources * requests, columns), jnp.bfloat16),
-            in_specs=[vmem()] * (1 + len(pieces)),
+            in_specs=in_specs,
             out_specs=vmem(),
+            scratch_shapes=scratch,
             compiler_params=limit(16),
             cost_estimate=cost(2),
             name="order_rows",
-        )(pick, *pieces)
+        )(*arrays)
 
     if not relative:
         received = lax.all_to_all(packed[0], "seq", split_axis=0, concat_axis=0, tiled=True)
         every_row = lax.all_gather(attend([received], 0), "seq", axis=0, tiled=True)
         partial_value = jnp.dot(every_row, out_proj, preferred_element_type=jnp.float32).astype(jnp.bfloat16)
-        return order(lax.psum(partial_value, "head"))
-
-    def project(parts):
+        shares = lax.all_to_all(partial_value, "head", split_axis=0, concat_axis=0, tiled=True)
+        shares = shares.reshape(head_devices, -1, columns)
+        summed = jnp.sum(shares.astype(jnp.float32), axis=0).astype(jnp.bfloat16)
+        whole = lax.all_gather(summed, "head", axis=0, tiled=True)
+        return order(order_whole_kernel, [vmem()] * 2, [], [pick, whole])
+
+    pieces = 2
+
+    def project(parts, piece):
         part_rows = parts[0].shape[0]
+        cols = columns // pieces
         return pl.pallas_call(
-            project_kernel,
-            out_shape=jax.ShapeDtypeStruct((4 * part_rows, columns), jnp.bfloat16),
+            functools.partial(project_kernel, piece * cols),
+            out_shape=jax.ShapeDtypeStruct((4 * part_rows, cols), jnp.bfloat16),
             in_specs=[vmem()] * 5,
             out_specs=vmem(),
             scratch_shapes=[pltpu.VMEM((4 * part_rows, out_proj.shape[0]), jnp.bfloat16)],
             compiler_params=limit(24),
-            cost_estimate=cost(6),
+            cost_estimate=cost(2),
             name="project_out",
         )(*parts, out_proj)
 
@@ -432,11 +471,34 @@
     near_across, far_rows = lax.optimization_barrier((near_across, far_rows))
     near = [near_rows, flip(near_rows, "seq", 1), near_across, flip(near_across, "seq", 1)]
     far_across = flip(far_rows, "seq", 2)
-    far = [far_rows, flip(far_rows, "seq", 1), far_across, flip(far_across, "seq", 1)]
-    near_sum = lax.psum(project(near), "head")
-    far_share = lax.psum_scatter(project(far), "head", scatter_dimension=0, tiled=True)
-    far_sum = lax.all_gather(far_share, "head", axis=0, tiled=True)
-    return order(near_sum, far_sum)
+    first, second = project(near, 0), project(near, 1)
+    relayed, _ = lax.optimization_barrier((far_across, second))
+    far = [far_rows, flip(far_rows, "seq", 1), far_across, flip(relayed, "seq", 1)]
+    first_in, second_in = inwards(first), inwards(second)
+    first_pair = add(first, first_in)
+    first_cross = across_middle(first_pair)
+    third, fourth = project(far, 0), project(far, 1)
+    third_in, fourth_in = inwards(third), inwards(fourth)
+    second_in, _ = lax.optimization_barrier((second_in, third))
+    second_pair = add(second, second_in)
+    second_cross = across_middle(second_pair)
+    first_cross, _ = lax.optimization_barrier((first_cross, fourth))
+    first_whole = add(first_pair, first_cross)
+    first_out = outwards(first_whole)
+    third_pair = add(third, third_in)
+    third_cross = across_middle(third_pair)
+    second_whole = add(second_pair, second_cross)
+    second_out = outwards(second_whole)
+    fourth_pair = add(fourth, fourth_in)
+    fourth_cross = across_middle(fourth_pair)
+    third_whole = add(third_pair, third_cross)
+    third_out = outwards(third_whole)
+    fourth_whole = add(fourth_pair, fourth_cross)
+    fourth_out = outwards(fourth_whole)
+    arrays = [first_whole, first_out, second_whole, second_out, third_whole, third_out, fourth_whole, fourth_out]
+    scratch = [pltpu.VMEM((steps * sources * requests, columns), jnp.bfloat16)]
+    kernel = functools.partial(order_kernel, 2)
+    return order(kernel, [smem()] + [vmem()] * (1 + len(arrays)), scratch, [z, pick] + arrays)
 
 
 def solution(mesh):

time: 118 us -> 81.8 us (0.69)
  starting transfers between devices: 7.28 us -> 33.6 us
  waiting for transfers between devices: 43.2 us -> 21.1 us
  blocking collectives: 17.6 us -> 0 us
  between operations: 13.6 us -> 0.47 us
  local copies, waits for them, and re-layouts: 7.01 us -> 0.82 us
  Pallas kernels: 28.8 us -> 24.7 us
    ppermute x0 -> x12, starting transfers between devices: none -> 25.5 us  [the longest x4 17.4 us: inwards(): return lax.ppermute(piece, 'head', [(0, 1), (3, 2)])]
    psum x1 -> x0, waiting for transfers between devices: 22.3 us -> none  [local(): near_sum = lax.psum(project(near), 'head')]
    ppermute x0 -> x12, waiting for transfers between devices: none -> 20 us  [the longest x4 18.3 us: outwards(): return lax.ppermute(whole, 'head', [(1, 0), (2, 3)])]
    all_gather x1 -> x0, blocking collectives: 17.6 us -> none  [local(): far_sum = lax.all_gather(far_share, 'head', axis=0, tiled=True)]
    reduce_scatter x1 -> x0, waiting for transfers between devices: 11.3 us -> none  [local(): lax.psum_scatter(project(far), 'head', scatter_dimension=0, tiled=True)]
    ppermute x9, waiting for transfers between devices: 9.69 us -> 1.07 us  [flip(): return lax.ppermute(x, axis, [(i, i ^ distance) for i in range(size)])]
    unnamed x32 -> x28, local copies, waits for them, and re-layouts: 7.01 us -> 0.82 us
    pallas_call x3 -> x5, Pallas kernels: 9.9 us -> 6.86 us  [the longest x4 5.11 us: project(): pl.pallas_call(functools.partial(project_kernel, piece * cols), out_shape...]
  transfers between devices with their start and end apart: 11 -> 21, of which waited for: 6 -> 6; matrix products, arithmetic and copies ran while one was open for 0% -> 1% of each run, Pallas kernels for 18% -> 26%
where the time goes in v5:
time: 81.8 us; the launch traced here: 81.1 us
  starting transfers between devices  33.6 us (41%)
  Pallas kernels  24.7 us (30%)
  waiting for transfers between devices  21.1 us (26%)
  local copies, waits for them, and re-layouts  0.82 us (1%)
    ppermute x4, waiting for transfers between devices, outwards(): return lax.ppermute(whole, 'head', [(1, 0), (2, 3)])  18.3 us
    ppermute x4, starting transfers between devices, inwards(): return lax.ppermute(piece, 'head', [(0, 1), (3, 2)])  17.4 us
    pallas_call x2, Pallas kernels, attend(): pl.pallas_call(functools.partial(attend_kernel, sizes, scale, relative, b...  15.6 us
    ppermute x9, starting transfers between devices, flip(): return lax.ppermute(x, axis, [(i, i ^ distance) for i in range(size)])  8.12 us
    ppermute x4, starting transfers between devices, outwards(): return lax.ppermute(whole, 'head', [(1, 0), (2, 3)])  5.17 us
    pallas_call x4, Pallas kernels, project(): pl.pallas_call(functools.partial(project_kernel, piece * cols), out_shape...  5.11 us
    ppermute x4, starting transfers between devices, across_middle(): return lax.ppermute(pair, 'head', [(1, 2), (2, 1)])  2.88 us
    pallas_call x1, Pallas kernels, order(): pl.pallas_call(kernel, out_shape=jax.ShapeDtypeStruct((steps, sources * r...  1.75 us
  transfers between devices with their start and end apart: 21, of which 6 were waited for; matrix products, arithmetic and copies ran while one was open for 1% of the time, Pallas kernels for 26%

profile of v5, /device:TPU:0, one launch (start us, length us, event | category | flops | bytes accessed | tf_op | source)
XLA Modules:
  0.0 81.1 jit_solution(11021153668069815070)
XLA Ops:
  0.0 0.7 copy-done.6
  0.8 1.1 %place_rows.1.after_ref.pick_ref = bf16[4,64,256]{2,1,0:T(8,128)(2,1)S(1)} custom-call(s32[1]{0:T(128)} %bitcast.1.me_ref, s32[64]{0:T(128)S(1)} %copy-done.6), custom_call_target="tpu_custom_call" | custom-call | flops 2000000000 | bytes 6000000 | tf_op jit(solution)/shard_map/place_rows/pallas_call | solution.py:376
  1.9 0.0 slice-start.5
  1.9 1.1 %pack_queries.1 = (bf16[1,848,128]{2,1,0:T(8,128)(2,1)S(1)}, bf16[1,848,128]{2,1,0:T(8,128)(2,1)S(1)}, bf16[1,848,128]{2,1,0:T(8,128)(2,1)S(1)}, bf16[1,848,128]{2,1,0:T(8,128)(2,1)S(1)}) custom-call(s32[1]{0:T(128)} %bitcast.1.me_ref, s32[64]{0:T(128)S(1)} %copy-done.6, bf16[4,16,32,128]{3,2,1,0:T(8,128)(2,1)S(1)} %copy-done.2, ...), custom_call_target="tpu_custom_call" | custom-call | flops 6000000000 | bytes 18000000 | tf_op jit(solution)/shard_map/pack_queries/pallas_call | solution.py:388
  3.1 0.5 collective-permute-start
  3.6 2.6 %collective-permute-start.3 = (bf16[1,848,128]{2,1,0:T(8,128)(2,1)S(1)}, bf16[1,848,128]{2,1,0:T(8,128)(2,1)S(1)}, u32[]{:S(2)}, u32[]{:S(2)}) collective-permute-start(bf16[1,848,128]{2,1,0:T(8,128)(2,1)S(1)} %get-tuple-element.16), channel_id=1, source_target_pairs={{0,8},{4,12},{8,0},{12,4},{1,9},{5,13},{9,1},{13,5},{2,10},{6,14},... | collective-permute-start | bytes 651272 | tf_op jit(solution)/shard_map/ppermute | solution.py:339
  6.2 0.1 collective-permute-start.4
  6.3 0.0 slice-start
  6.4 7.2 %attend.2.rest_0_ = bf16[32,4096]{1,0:T(8,128)(2,1)S(1)} custom-call(s32[1]{0:T(128)} %bitcast.1.me_ref, s32[64]{0:T(128)S(1)} %copy-done.7, s32[4,16]{1,0:T(4,128)S(1)} %copy-done.5, bf16[1,848,128]{2,1,0:T(8,128)(2,1)S(1)} %get-tuple-element.14.rest_0_, bf16[1,848,128]{2,1,0:T(8,128)(2,1)S(1)} %collective-permute-done.rest_1_, ...), custom_call_target="tpu_custom_call" | custom-call | flops 8000000000 | bytes 24000000 | tf_op jit(solution)/shard_map/attend/pallas_call | solution.py:406
  13.5 0.0 slice-start.2
  13.6 2.5 %collective-permute-start.2 = (bf16[32,4096]{1,0:T(8,128)(2,1)S(1)}, bf16[32,4096]{1,0:T(8,128)(2,1)S(1)}, u32[]{:S(2)}, u32[]{:S(2)}) collective-permute-start(bf16[32,4096]{1,0:T(8,128)(2,1)S(1)} %attend.2.rest_0_), channel_id=1, source_target_pairs={{0,8},{4,12},{8,0},{12,4},{1,9},{5,13},{9,1},{13,5},{2,10},{6,14},... | collective-permute-start | bytes 786440 | tf_op jit(solution)/shard_map/ppermute | solution.py:339
  16.0 0.8 %collective-permute-start.1 = (bf16[32,4096]{1,0:T(8,128)(2,1)S(1)}, bf16[32,4096]{1,0:T(8,128)(2,1)S(1)}, u32[]{:S(2)}, u32[]{:S(2)}) collective-permute-start(bf16[32,4096]{1,0:T(8,128)(2,1)S(1)} %attend.2.rest_0_), channel_id=1, source_target_pairs={{0,4},{4,0},{8,12},{12,8},{1,5},{5,1},{9,13},{13,9},{2,6},{6,2},{1... | collective-permute-start | bytes 786440 | tf_op jit(solution)/shard_map/ppermute | solution.py:339
  16.9 8.4 %attend.3.rest_0_ = bf16[32,4096]{1,0:T(8,128)(2,1)S(1)} custom-call(s32[1]{0:T(128)} %bitcast.1.me_ref, s32[64]{0:T(128)S(1)} %copy-done.7, s32[4,16]{1,0:T(4,128)S(1)} %copy-done.5, bf16[1,848,128]{2,1,0:T(8,128)(2,1)S(1)} %collective-permute-done.3.rest_0_, bf16[1,848,128]{2,1,0:T(8,128)(2,1)S(1)} %collective-permute-done.4.rest_1_, ...), custom_call_target="tpu_custom_call" | custom-call | flops 8000000000 | bytes 24000000 | tf_op jit(solution)/shard_map/attend/pallas_call | solution.py:406
  25.3 0.1 collective-permute-start.5
  25.4 1.5 %collective-permute-start.9 = (bf16[32,4096]{1,0:T(8,128)(2,1)S(1)}, bf16[32,4096]{1,0:T(8,128)(2,1)S(1)}, u32[]{:S(2)}, u32[]{:S(2)}) collective-permute-start(bf16[32,4096]{1,0:T(8,128)(2,1)S(1)} %attend.3.rest_0_), channel_id=1, source_target_pairs={{0,8},{4,12},{8,0},{12,4},{1,9},{5,13},{9,1},{13,5},{2,10},{6,14},... | collective-permute-start | bytes 786440 | tf_op jit(solution)/shard_map/ppermute | solution.py:339
  26.9 0.0 collective-permute-done.5.rest_3_
  26.9 1.3 %project_out.4 = bf16[128,896]{1,0:T(8,128)(2,1)S(1)} custom-call(bf16[32,4096]{1,0:T(8,128)(2,1)S(1)} %attend.2.rest_0_, bf16[32,4096]{1,0:T(8,128)(2,1)S(1)} %collective-permute-done.1.rest_1_, bf16[32,4096]{1,0:T(8,128)(2,1)S(1)} %collective-permute-done.2.rest_2_, bf16[32,4096]{1,0:T(8,128)(2,1)S(1)} %collective-permute-done.5.rest_3_, ...), custom_call_target="tpu_custom_call" | custom-call | flops 2000000000 | bytes 6000000 | tf_op jit(solution)/shard_map/project_out/pallas_call | solution.py:456
  28.2 3.5 %collective-permute-start.6 = (bf16[128,896]{1,0:T(8,128)(2,1)S(1)}, bf16[128,896]{1,0:T(8,128)(2,1)S(1)}, u32[]{:S(2)}, u32[]{:S(2)}) collective-permute-start(bf16[128,896]{1,0:T(8,128)(2,1)S(1)} %project_out.4), channel_id=1, source_target_pairs={{0,1},{3,2},{4,5},{7,6},{8,9},{11,10},{12,13},{15,14},{16,17},{19,... | collective-permute-start | bytes 688136 | tf_op jit(solution)/shard_map/ppermute | solution.py:347
  31.7 0.1 collective-permute-start.8
  31.8 1.3 %project_out.5 = bf16[128,896]{1,0:T(8,128)(2,1)S(1)} custom-call(bf16[32,4096]{1,0:T(8,128)(2,1)S(1)} %attend.2.rest_0_, bf16[32,4096]{1,0:T(8,128)(2,1)S(1)} %collective-permute-done.1.rest_1_, bf16[32,4096]{1,0:T(8,128)(2,1)S(1)} %collective-permute-done.2.rest_2_, bf16[32,4096]{1,0:T(8,128)(2,1)S(1)} %collective-permute-done.5.rest_3_, ...), custom_call_target="tpu_custom_call" | custom-call | flops 2000000000 | bytes 6000000 | tf_op jit(solution)/shard_map/project_out/pallas_call | solution.py:456
  33.1 1.0 %collective-permute-done.9.rest_2_ = bf16[32,4096]{1,0:T(8,128)(2,1)S(1)} collective-permute-done((bf16[32,4096]{1,0:T(8,128)(2,1)S(1)}, bf16[32,4096]{1,0:T(8,128)(2,1)S(1)}, u32[]{:S(2)}, u32[]{:S(2)}) %collective-permute-start.9) | collective-permute-done | bytes 262176 | tf_op jit(solution)/shard_map/ppermute | solution.py:339
  34.1 3.5 %collective-permute-start.12 = (bf16[128,896]{1,0:T(8,128)(2,1)S(1)}, bf16[128,896]{1,0:T(8,128)(2,1)S(1)}, u32[]{:S(2)}, u32[]{:S(2)}) collective-permute-start(bf16[128,896]{1,0:T(8,128)(2,1)S(1)} %project_out.5), channel_id=1, source_target_pairs={{0,1},{3,2},{4,5},{7,6},{8,9},{11,10},{12,13},{15,14},{16,17},{19,... | collective-permute-start | bytes 688136 | tf_op jit(solution)/shard_map/ppermute | solution.py:347
  37.6 0.1 add_convert_fusion.7
  37.7 0.9 %collective-permute-start.7 = (bf16[128,896]{1,0:T(8,128)(2,1)S(1)}, bf16[128,896]{1,0:T(8,128)(2,1)S(1)}, u32[]{:S(2)}, u32[]{:S(2)}) collective-permute-start(bf16[128,896]{1,0:T(8,128)(2,1)S(1)} %add_convert_fusion.7), channel_id=1, source_target_pairs={{1,2},{2,1},{5,6},{6,5},{9,10},{10,9},{13,14},{14,13},{17,18},{18,... | collective-permute-start | bytes 688136 | tf_op jit(solution)/shard_map/ppermute | solution.py:351
  38.6 1.3 %project_out.7 = bf16[128,896]{1,0:T(8,128)(2,1)S(1)} custom-call(bf16[32,4096]{1,0:T(8,128)(2,1)S(1)} %attend.3.rest_0_, bf16[32,4096]{1,0:T(8,128)(2,1)S(1)} %collective-permute-done.8.rest_1_, bf16[32,4096]{1,0:T(8,128)(2,1)S(1)} %collective-permute-done.9.rest_2_, bf16[32,4096]{1,0:T(8,128)(2,1)S(1)} %collective-permute-done.10.rest_3_, ...), custom_call_target="tpu_custom_call" | custom-call | flops 2000000000 | bytes 6000000 | tf_op jit(solution)/shard_map/project_out/pallas_call | solution.py:456
  39.8 6.5 %collective-permute-start.15 = (bf16[128,896]{1,0:T(8,128)(2,1)S(1)}, bf16[128,896]{1,0:T(8,128)(2,1)S(1)}, u32[]{:S(2)}, u32[]{:S(2)}) collective-permute-start(bf16[128,896]{1,0:T(8,128)(2,1)S(1)} %project_out.7), channel_id=1, source_target_pairs={{0,1},{3,2},{4,5},{7,6},{8,9},{11,10},{12,13},{15,14},{16,17},{19,... | collective-permute-start | bytes 688136 | tf_op jit(solution)/shard_map/ppermute | solution.py:347
  46.3 0.1 add_convert_fusion.5
  46.4 0.7 collective-permute-start.13
  47.1 1.3 %project_out.6 = bf16[128,896]{1,0:T(8,128)(2,1)S(1)} custom-call(bf16[32,4096]{1,0:T(8,128)(2,1)S(1)} %attend.3.rest_0_, bf16[32,4096]{1,0:T(8,128)(2,1)S(1)} %collective-permute-done.8.rest_1_, bf16[32,4096]{1,0:T(8,128)(2,1)S(1)} %collective-permute-done.9.rest_2_, bf16[32,4096]{1,0:T(8,128)(2,1)S(1)} %collective-permute-done.10.rest_3_, ...), custom_call_target="tpu_custom_call" | custom-call | flops 2000000000 | bytes 6000000 | tf_op jit(solution)/shard_map/project_out/pallas_call | solution.py:456
  48.3 4.0 %collective-permute-start.18 = (bf16[128,896]{1,0:T(8,128)(2,1)S(1)}, bf16[128,896]{1,0:T(8,128)(2,1)S(1)}, u32[]{:S(2)}, u32[]{:S(2)}) collective-permute-start(bf16[128,896]{1,0:T(8,128)(2,1)S(1)} %project_out.6), channel_id=1, source_target_pairs={{0,1},{3,2},{4,5},{7,6},{8,9},{11,10},{12,13},{15,14},{16,17},{19,... | collective-permute-start | bytes 688136 | tf_op jit(solution)/shard_map/ppermute | solution.py:347
  52.4 0.1 add_convert_fusion.6.rest_0_
  52.4 1.3 %collective-permute-start.11 = (bf16[128,896]{1,0:T(8,128)(2,1)S(1)}, bf16[128,896]{1,0:T(8,128)(2,1)S(1)}, u32[]{:S(2)}, u32[]{:S(2)}) collective-permute-start(bf16[128,896]{1,0:T(8,128)(2,1)S(1)} %add_convert_fusion.6.rest_0_), channel_id=1, source_target_pairs={{1,0},{2,3},{5,4},{6,7},{9,8},{10,11},{13,12},{14,15},{17,16},{18,... | collective-permute-start | bytes 688136 | tf_op jit(solution)/shard_map/ppermute | solution.py:355
  53.7 0.1 add_convert_fusion.4.rest_2_
  53.8 1.3 %collective-permute-start.14 = (bf16[128,896]{1,0:T(8,128)(2,1)S(1)}, bf16[128,896]{1,0:T(8,128)(2,1)S(1)}, u32[]{:S(2)}, u32[]{:S(2)}) collective-permute-start(bf16[128,896]{1,0:T(8,128)(2,1)S(1)} %add_convert_fusion.4.rest_2_), channel_id=1, source_target_pairs={{1,0},{2,3},{5,4},{6,7},{9,8},{10,11},{13,12},{14,15},{17,16},{18,... | collective-permute-start | bytes 688136 | tf_op jit(solution)/shard_map/ppermute | solution.py:355
  55.1 1.7 %collective-permute-done.18 = bf16[128,896]{1,0:T(8,128)(2,1)S(1)} collective-permute-done((bf16[128,896]{1,0:T(8,128)(2,1)S(1)}, bf16[128,896]{1,0:T(8,128)(2,1)S(1)}, u32[]{:S(2)}, u32[]{:S(2)}) %collective-permute-start.18) | collective-permute-done | bytes 229408 | tf_op jit(solution)/shard_map/ppermute | solution.py:347
  56.8 0.1 add_convert_fusion.1
  56.9 0.7 collective-permute-start.19
  57.5 0.1 add_convert_fusion.3
  57.6 0.7 collective-permute-start.16
  58.3 0.1 add_convert_fusion.rest_6_
  58.4 1.3 %collective-permute-start.20 = (bf16[128,896]{1,0:T(8,128)(2,1)S(1)}, bf16[128,896]{1,0:T(8,128)(2,1)S(1)}, u32[]{:S(2)}, u32[]{:S(2)}) collective-permute-start(bf16[128,896]{1,0:T(8,128)(2,1)S(1)} %add_convert_fusion.rest_6_), channel_id=1, source_target_pairs={{1,0},{2,3},{5,4},{6,7},{9,8},{10,11},{13,12},{14,15},{17,16},{18,... | collective-permute-start | bytes 688136 | tf_op jit(solution)/shard_map/ppermute | solution.py:355
  59.7 0.1 add_convert_fusion.2.rest_4_
  59.7 1.3 %collective-permute-start.17 = (bf16[128,896]{1,0:T(8,128)(2,1)S(1)}, bf16[128,896]{1,0:T(8,128)(2,1)S(1)}, u32[]{:S(2)}, u32[]{:S(2)}) collective-permute-start(bf16[128,896]{1,0:T(8,128)(2,1)S(1)} %add_convert_fusion.2.rest_4_), channel_id=1, source_target_pairs={{1,0},{2,3},{5,4},{6,7},{9,8},{10,11},{13,12},{14,15},{17,16},{18,... | collective-permute-start | bytes 688136 | tf_op jit(solution)/shard_map/ppermute | solution.py:355
  61.0 1.8 %collective-permute-done.11.rest_1_ = bf16[128,896]{1,0:T(8,128)(2,1)S(1)} collective-permute-done((bf16[128,896]{1,0:T(8,128)(2,1)S(1)}, bf16[128,896]{1,0:T(8,128)(2,1)S(1)}, u32[]{:S(2)}, u32[]{:S(2)}) %collective-permute-start.11) | collective-permute-done | bytes 229408 | tf_op jit(solution)/shard_map/ppermute | solution.py:355
  62.9 3.1 %collective-permute-done.14.rest_3_ = bf16[128,896]{1,0:T(8,128)(2,1)S(1)} collective-permute-done((bf16[128,896]{1,0:T(8,128)(2,1)S(1)}, bf16[128,896]{1,0:T(8,128)(2,1)S(1)}, u32[]{:S(2)}, u32[]{:S(2)}) %collective-permute-start.14) | collective-permute-done | bytes 229408 | tf_op jit(solution)/shard_map/ppermute | solution.py:355
  65.9 11.0 %collective-permute-done.20.rest_7_ = bf16[128,896]{1,0:T(8,128)(2,1)S(1)} collective-permute-done((bf16[128,896]{1,0:T(8,128)(2,1)S(1)}, bf16[128,896]{1,0:T(8,128)(2,1)S(1)}, u32[]{:S(2)}, u32[]{:S(2)}) %collective-permute-start.20) | collective-permute-done | bytes 229408 | tf_op jit(solution)/shard_map/ppermute | solution.py:355
  76.9 2.5 %collective-permute-done.17.rest_5_ = bf16[128,896]{1,0:T(8,128)(2,1)S(1)} collective-permute-done((bf16[128,896]{1,0:T(8,128)(2,1)S(1)}, bf16[128,896]{1,0:T(8,128)(2,1)S(1)}, u32[]{:S(2)}, u32[]{:S(2)}) %collective-permute-start.17) | collective-permute-done | bytes 229408 | tf_op jit(solution)/shard_map/ppermute | solution.py:355
  79.3 1.7 %order_rows.1 = bf16[4,64,1792]{2,1,0:T(8,128)(2,1)} custom-call(s32[1]{0:T(128)} %bitcast.z_ref, bf16[4,64,256]{2,1,0:T(8,128)(2,1)S(1)} %place_rows.1.after_ref.pick_ref, bf16[128,896]{1,0:T(8,128)(2,1)S(1)} %add_convert_fusion.6.rest_0_, bf16[128,896]{1,0:T(8,128)(2,1)S(1)} %collective-permute-done.11.rest_1_, ...), custom_call_target="tpu_custom_call" | custom-call | flops 2000000000 | bytes 6000000 | tf_op jit(solution)/shard_map/order_rows/pallas_call | solution.py:430
  (41 shorter events, 0.1 us)
Async XLA Ops:
  0.0 1.8 %copy-start.4 = (bf16[4,16,576]{2,1,0:T(8,128)(2,1)S(1)}, bf16[4,16,576]{2,1,0:T(8,128)(2,1)}, u32[]{:S(2)}) copy-start(bf16[4,16,576]{2,1,0:T(8,128)(2,1)} %fresh_ref.1) | copy-start | bytes 221188
  0.0 1.9 %copy-start.3 = (bf16[4,16,32,64]{3,2,1,0:T(8,128)(2,1)S(1)}, bf16[4,16,32,64]{3,2,1,0:T(8,128)(2,1)}, u32[]{:S(2)}) copy-start(bf16[4,16,32,64]{3,2,1,0:T(8,128)(2,1)} %rope_ref.1) | copy-start | bytes 786436
  0.0 1.9 %copy-start.2 = (bf16[4,16,32,128]{3,2,1,0:T(8,128)(2,1)S(1)}, bf16[4,16,32,128]{3,2,1,0:T(8,128)(2,1)}, u32[]{:S(2)}) copy-start(bf16[4,16,32,128]{3,2,1,0:T(8,128)(2,1)} %nope_ref.1) | copy-start | bytes 1572868
  0.0 0.7 copy-start.6
  0.8 5.5 %slice-start.4 = ((s8[4718592]{0:T(1024)(128)(4,1)}), s8[4194304]{0:T(1024)(128)(4,1)S(1)}, s32[]{:S(2)}) async-start(s8[4718592]{0:T(1024)(128)(4,1)} %bitcast.5), calls=%async_computation.4 | async-start | bytes 8388608
  1.9 4.4 %slice-start.5 = ((s8[4718592]{0:T(1024)(128)(4,1)}), s8[524288]{0:T(1024)(128)(4,1)S(1)}, s32[]{:S(2)}) async-start(s8[4718592]{0:T(1024)(128)(4,1)} %bitcast.5), calls=%async_computation.5 | async-start | bytes 1048576
  1.9 4.4 %copy-start = (bf16[32,128,512]{2,1,0:T(8,128)(2,1)S(1)}, bf16[32,128,512]{2,1,0:T(8,128)(2,1)}, u32[]{:S(2)}) copy-start(bf16[32,128,512]{2,1,0:T(8,128)(2,1)} %rest_3_.3) | copy-start | bytes 12582916
  1.9 4.4 %copy-start.1 = (bf16[32,512,128]{2,1,0:T(8,128)(2,1)S(1)}, bf16[32,512,128]{2,1,0:T(8,128)(2,1)}, u32[]{:S(2)}) copy-start(bf16[32,512,128]{2,1,0:T(8,128)(2,1)} %rest_4_.7) | copy-start | bytes 12582916
  1.9 4.4 %copy-start.5 = (s32[4,16]{1,0:T(4,128)S(1)}, s32[4,16]{1,0:T(4,128)}, u32[]{:S(2)}) copy-start(s32[4,16]{1,0:T(4,128)} %length_ref.3) | copy-start | bytes 772
  1.9 4.4 %copy-start.7 = (s32[64]{0:T(128)S(1)}, s32[64]{0:T(128)}, u32[]{:S(2)}) copy-start(s32[64]{0:T(128)} %decode_ref.7) | copy-start | bytes 772
  3.1 3.2 %collective-permute-start = (bf16[1,848,128]{2,1,0:T(8,128)(2,1)S(1)}, bf16[1,848,128]{2,1,0:T(8,128)(2,1)S(1)}, u32[]{:S(2)}, u32[]{:S(2)}) collective-permute-start(bf16[1,848,128]{2,1,0:T(8,128)(2,1)S(1)} %get-tuple-element.15), channel_id=1, source_target_pairs={{0,4},{4,0},{8,12},{12,8},{1,5},{5,1},{9,13},{13,9},{2,6},{6,2},{1... | collective-permute-start | bytes 651272 | tf_op jit(solution)/shard_map/ppermute | solution.py:339
  3.6 13.2 %collective-permute-start.3 = (bf16[1,848,128]{2,1,0:T(8,128)(2,1)S(1)}, bf16[1,848,128]{2,1,0:T(8,128)(2,1)S(1)}, u32[]{:S(2)}, u32[]{:S(2)}) collective-permute-start(bf16[1,848,128]{2,1,0:T(8,128)(2,1)S(1)} %get-tuple-element.16), channel_id=1, source_target_pairs={{0,8},{4,12},{8,0},{12,4},{1,9},{5,13},{9,1},{13,5},{2,10},{6,14},... | collective-permute-start | bytes 651272 | tf_op jit(solution)/shard_map/ppermute | solution.py:339
  6.2 10.7 %collective-permute-start.4 = (bf16[1,848,128]{2,1,0:T(8,128)(2,1)S(1)}, bf16[1,848,128]{2,1,0:T(8,128)(2,1)S(1)}, u32[]{:S(2)}, u32[]{:S(2)}) collective-permute-start(bf16[1,848,128]{2,1,0:T(8,128)(2,1)S(1)} %get-tuple-element.17), channel_id=1, source_target_pairs={{0,12},{4,8},{8,4},{12,0},{1,13},{5,9},{9,5},{13,1},{2,14},{6,10},... | collective-permute-start | bytes 651272 | tf_op jit(solution)/shard_map/ppermute | solution.py:339
  6.3 20.6 %slice-start = ((s8[14680064]{0:T(1024)(128)(4,1)}), s8[4194304]{0:T(1024)(128)(4,1)S(1)}, s32[]{:S(2)}) async-start(s8[14680064]{0:T(1024)(128)(4,1)} %bitcast.3), calls=%async_computation | async-start | bytes 8388608
  6.3 20.6 %slice-start.1 = ((s8[14680064]{0:T(1024)(128)(4,1)}), s8[4194304]{0:T(1024)(128)(4,1)S(1)}, s32[]{:S(2)}) async-start(s8[14680064]{0:T(1024)(128)(4,1)} %bitcast.3), calls=%async_computation.1 | async-start | bytes 8388608
  13.5 13.4 %slice-start.2 = ((s8[14680064]{0:T(1024)(128)(4,1)}), s8[4194304]{0:T(1024)(128)(4,1)S(1)}, s32[]{:S(2)}) async-start(s8[14680064]{0:T(1024)(128)(4,1)} %bitcast.3), calls=%async_computation.2 | async-start | bytes 8388608
  13.6 13.4 %slice-start.3 = ((s8[14680064]{0:T(1024)(128)(4,1)}), s8[2097152]{0:T(1024)(128)(4,1)S(1)}, s32[]{:S(2)}) async-start(s8[14680064]{0:T(1024)(128)(4,1)} %bitcast.3), calls=%async_computation.3 | async-start | bytes 4194304
  13.6 11.7 %collective-permute-start.2 = (bf16[32,4096]{1,0:T(8,128)(2,1)S(1)}, bf16[32,4096]{1,0:T(8,128)(2,1)S(1)}, u32[]{:S(2)}, u32[]{:S(2)}) collective-permute-start(bf16[32,4096]{1,0:T(8,128)(2,1)S(1)} %attend.2.rest_0_), channel_id=1, source_target_pairs={{0,8},{4,12},{8,0},{12,4},{1,9},{5,13},{9,1},{13,5},{2,10},{6,14},... | collective-permute-start | bytes 786440 | tf_op jit(solution)/shard_map/ppermute | solution.py:339
  16.0 10.8 %collective-permute-start.1 = (bf16[32,4096]{1,0:T(8,128)(2,1)S(1)}, bf16[32,4096]{1,0:T(8,128)(2,1)S(1)}, u32[]{:S(2)}, u32[]{:S(2)}) collective-permute-start(bf16[32,4096]{1,0:T(8,128)(2,1)S(1)} %attend.2.rest_0_), channel_id=1, source_target_pairs={{0,4},{4,0},{8,12},{12,8},{1,5},{5,1},{9,13},{13,9},{2,6},{6,2},{1... | collective-permute-start | bytes 786440 | tf_op jit(solution)/shard_map/ppermute | solution.py:339
  25.3 1.6 %collective-permute-start.5 = (bf16[32,4096]{1,0:T(8,128)(2,1)S(1)}, bf16[32,4096]{1,0:T(8,128)(2,1)S(1)}, u32[]{:S(2)}, u32[]{:S(2)}) collective-permute-start(bf16[32,4096]{1,0:T(8,128)(2,1)S(1)} %collective-permute-done.2.rest_2_), channel_id=1, source_target_pairs={{0,4},{4,0},{8,12},{12,8},{1,5},{5,1},{9,13},{13,9},{2,6},{6,2},{1... | collective-permute-start | bytes 786440 | tf_op jit(solution)/shard_map/ppermute | solution.py:339
  25.4 8.7 %collective-permute-start.9 = (bf16[32,4096]{1,0:T(8,128)(2,1)S(1)}, bf16[32,4096]{1,0:T(8,128)(2,1)S(1)}, u32[]{:S(2)}, u32[]{:S(2)}) collective-permute-start(bf16[32,4096]{1,0:T(8,128)(2,1)S(1)} %attend.3.rest_0_), channel_id=1, source_target_pairs={{0,8},{4,12},{8,0},{12,4},{1,9},{5,13},{9,1},{13,5},{2,10},{6,14},... | collective-permute-start | bytes 786440 | tf_op jit(solution)/shard_map/ppermute | solution.py:339
  28.2 9.4 %collective-permute-start.6 = (bf16[128,896]{1,0:T(8,128)(2,1)S(1)}, bf16[128,896]{1,0:T(8,128)(2,1)S(1)}, u32[]{:S(2)}, u32[]{:S(2)}) collective-permute-start(bf16[128,896]{1,0:T(8,128)(2,1)S(1)} %project_out.4), channel_id=1, source_target_pairs={{0,1},{3,2},{4,5},{7,6},{8,9},{11,10},{12,13},{15,14},{16,17},{19,... | collective-permute-start | bytes 688136 | tf_op jit(solution)/shard_map/ppermute | solution.py:347
  31.7 6.8 %collective-permute-start.8 = (bf16[32,4096]{1,0:T(8,128)(2,1)S(1)}, bf16[32,4096]{1,0:T(8,128)(2,1)S(1)}, u32[]{:S(2)}, u32[]{:S(2)}) collective-permute-start(bf16[32,4096]{1,0:T(8,128)(2,1)S(1)} %attend.3.rest_0_), channel_id=1, source_target_pairs={{0,4},{4,0},{8,12},{12,8},{1,5},{5,1},{9,13},{13,9},{2,6},{6,2},{1... | collective-permute-start | bytes 786440 | tf_op jit(solution)/shard_map/ppermute | solution.py:339
  34.1 4.4 %collective-permute-start.10 = (bf16[32,4096]{1,0:T(8,128)(2,1)S(1)}, bf16[32,4096]{1,0:T(8,128)(2,1)S(1)}, u32[]{:S(2)}, u32[]{:S(2)}) collective-permute-start(bf16[32,4096]{1,0:T(8,128)(2,1)S(1)} %collective-permute-done.9.rest_2_), channel_id=1, source_target_pairs={{0,4},{4,0},{8,12},{12,8},{1,5},{5,1},{9,13},{13,9},{2,6},{6,2},{1... | collective-permute-start | bytes 786440 | tf_op jit(solution)/shard_map/ppermute | solution.py:339
  34.1 12.2 %collective-permute-start.12 = (bf16[128,896]{1,0:T(8,128)(2,1)S(1)}, bf16[128,896]{1,0:T(8,128)(2,1)S(1)}, u32[]{:S(2)}, u32[]{:S(2)}) collective-permute-start(bf16[128,896]{1,0:T(8,128)(2,1)S(1)} %project_out.5), channel_id=1, source_target_pairs={{0,1},{3,2},{4,5},{7,6},{8,9},{11,10},{12,13},{15,14},{16,17},{19,... | collective-permute-start | bytes 688136 | tf_op jit(solution)/shard_map/ppermute | solution.py:347
  37.7 14.7 %collective-permute-start.7 = (bf16[128,896]{1,0:T(8,128)(2,1)S(1)}, bf16[128,896]{1,0:T(8,128)(2,1)S(1)}, u32[]{:S(2)}, u32[]{:S(2)}) collective-permute-start(bf16[128,896]{1,0:T(8,128)(2,1)S(1)} %add_convert_fusion.7), channel_id=1, source_target_pairs={{1,2},{2,1},{5,6},{6,5},{9,10},{10,9},{13,14},{14,13},{17,18},{18,... | collective-permute-start | bytes 688136 | tf_op jit(solution)/shard_map/ppermute | solution.py:351
  39.8 17.7 %collective-permute-start.15 = (bf16[128,896]{1,0:T(8,128)(2,1)S(1)}, bf16[128,896]{1,0:T(8,128)(2,1)S(1)}, u32[]{:S(2)}, u32[]{:S(2)}) collective-permute-start(bf16[128,896]{1,0:T(8,128)(2,1)S(1)} %project_out.7), channel_id=1, source_target_pairs={{0,1},{3,2},{4,5},{7,6},{8,9},{11,10},{12,13},{15,14},{16,17},{19,... | collective-permute-start | bytes 688136 | tf_op jit(solution)/shard_map/ppermute | solution.py:347
  46.4 7.3 %collective-permute-start.13 = (bf16[128,896]{1,0:T(8,128)(2,1)S(1)}, bf16[128,896]{1,0:T(8,128)(2,1)S(1)}, u32[]{:S(2)}, u32[]{:S(2)}) collective-permute-start(bf16[128,896]{1,0:T(8,128)(2,1)S(1)} %add_convert_fusion.5), channel_id=1, source_target_pairs={{1,2},{2,1},{5,6},{6,5},{9,10},{10,9},{13,14},{14,13},{17,18},{18,... | collective-permute-start | bytes 688136 | tf_op jit(solution)/shard_map/ppermute | solution.py:351
  48.3 8.5 %collective-permute-start.18 = (bf16[128,896]{1,0:T(8,128)(2,1)S(1)}, bf16[128,896]{1,0:T(8,128)(2,1)S(1)}, u32[]{:S(2)}, u32[]{:S(2)}) collective-permute-start(bf16[128,896]{1,0:T(8,128)(2,1)S(1)} %project_out.6), channel_id=1, source_target_pairs={{0,1},{3,2},{4,5},{7,6},{8,9},{11,10},{12,13},{15,14},{16,17},{19,... | collective-permute-start | bytes 688136 | tf_op jit(solution)/shard_map/ppermute | solution.py:347
  52.4 10.4 %collective-permute-start.11 = (bf16[128,896]{1,0:T(8,128)(2,1)S(1)}, bf16[128,896]{1,0:T(8,128)(2,1)S(1)}, u32[]{:S(2)}, u32[]{:S(2)}) collective-permute-start(bf16[128,896]{1,0:T(8,128)(2,1)S(1)} %add_convert_fusion.6.rest_0_), channel_id=1, source_target_pairs={{1,0},{2,3},{5,4},{6,7},{9,8},{10,11},{13,12},{14,15},{17,16},{18,... | collective-permute-start | bytes 688136 | tf_op jit(solution)/shard_map/ppermute | solution.py:355
  53.8 12.1 %collective-permute-start.14 = (bf16[128,896]{1,0:T(8,128)(2,1)S(1)}, bf16[128,896]{1,0:T(8,128)(2,1)S(1)}, u32[]{:S(2)}, u32[]{:S(2)}) collective-permute-start(bf16[128,896]{1,0:T(8,128)(2,1)S(1)} %add_convert_fusion.4.rest_2_), channel_id=1, source_target_pairs={{1,0},{2,3},{5,4},{6,7},{9,8},{10,11},{13,12},{14,15},{17,16},{18,... | collective-permute-start | bytes 688136 | tf_op jit(solution)/shard_map/ppermute | solution.py:355
  56.9 1.4 %collective-permute-start.19 = (bf16[128,896]{1,0:T(8,128)(2,1)S(1)}, bf16[128,896]{1,0:T(8,128)(2,1)S(1)}, u32[]{:S(2)}, u32[]{:S(2)}) collective-permute-start(bf16[128,896]{1,0:T(8,128)(2,1)S(1)} %add_convert_fusion.1), channel_id=1, source_target_pairs={{1,2},{2,1},{5,6},{6,5},{9,10},{10,9},{13,14},{14,13},{17,18},{18,... | collective-permute-start | bytes 688136 | tf_op jit(solution)/shard_map/ppermute | solution.py:351
  57.6 2.1 %collective-permute-start.16 = (bf16[128,896]{1,0:T(8,128)(2,1)S(1)}, bf16[128,896]{1,0:T(8,128)(2,1)S(1)}, u32[]{:S(2)}, u32[]{:S(2)}) collective-permute-start(bf16[128,896]{1,0:T(8,128)(2,1)S(1)} %add_convert_fusion.3), channel_id=1, source_target_pairs={{1,2},{2,1},{5,6},{6,5},{9,10},{10,9},{13,14},{14,13},{17,18},{18,... | collective-permute-start | bytes 688136 | tf_op jit(solution)/shard_map/ppermute | solution.py:351
  58.4 18.5 %collective-permute-start.20 = (bf16[128,896]{1,0:T(8,128)(2,1)S(1)}, bf16[128,896]{1,0:T(8,128)(2,1)S(1)}, u32[]{:S(2)}, u32[]{:S(2)}) collective-permute-start(bf16[128,896]{1,0:T(8,128)(2,1)S(1)} %add_convert_fusion.rest_6_), channel_id=1, source_target_pairs={{1,0},{2,3},{5,4},{6,7},{9,8},{10,11},{13,12},{14,15},{17,16},{18,... | collective-permute-start | bytes 688136 | tf_op jit(solution)/shard_map/ppermute | solution.py:355
  59.7 19.6 %collective-permute-start.17 = (bf16[128,896]{1,0:T(8,128)(2,1)S(1)}, bf16[128,896]{1,0:T(8,128)(2,1)S(1)}, u32[]{:S(2)}, u32[]{:S(2)}) collective-permute-start(bf16[128,896]{1,0:T(8,128)(2,1)S(1)} %add_convert_fusion.2.rest_4_), channel_id=1, source_target_pairs={{1,0},{2,3},{5,4},{6,7},{9,8},{10,11},{13,12},{14,15},{17,16},{18,... | collective-permute-start | bytes 688136 | tf_op jit(solution)/shard_map/ppermute | solution.py:355

commit v6 on v5

--- a/solution.py
+++ b/solution.py
@@ -277,20 +277,27 @@
         out_ref[t] = jnp.where(col_id == wanted + t, 1.0, 0.0).astype(jnp.bfloat16)
 
 
+def keeps_upper(z_ref):
+    return (z_ref[0] == 1) | (z_ref[0] == 2)
+
+
 def order_kernel(halves, z_ref, pick_ref, *rest):
     pieces, out_ref, x = rest[:-2], rest[-2], rest[-1]
-    middle = (z_ref[0] == 1) | (z_ref[0] == 2)
-    rows = x.shape[0] // halves
+    upper = keeps_upper(z_ref)
+    rows = x.shape[0] // (2 * halves)
     each = len(pieces) // (2 * halves)
     cols = x.shape[1] // each
 
-    def assemble(side):
+    def assemble(first, second):
         for h in range(halves):
             for c in range(each):
-                x[h * rows : (h + 1) * rows, c * cols : (c + 1) * cols] = pieces[2 * (h * each + c) + side][...]
-
-    pl.when(middle)(lambda: assemble(0))
-    pl.when(jnp.logical_not(middle))(lambda: assemble(1))
+                at = slice(c * cols, (c + 1) * cols)
+                i = 2 * (h * each + c)
+                x[2 * h * rows : (2 * h + 1) * rows, at] = pieces[i + first][...]
+                x[(2 * h + 1) * rows : (2 * h + 2) * rows, at] = pieces[i + second][...]
+
+    pl.when(upper)(lambda: assemble(1, 0))
+    pl.when(jnp.logical_not(upper))(lambda: assemble(0, 1))
     for t in range(pick_ref.shape[0]):
         out_ref[t] = jnp.dot(pick_ref[t], x[...], preferred_element_type=jnp.float32).astype(jnp.bfloat16)
 
@@ -300,16 +307,24 @@
         out_ref[t] = jnp.dot(pick_ref[t], x_ref[...], preferred_element_type=jnp.float32).astype(jnp.bfloat16)
 
 
-def project_kernel(first_col, *rest):
-    parts, weight, out, x = rest[:4], rest[4], rest[5], rest[6]
+def project_kernel(first_col, z_ref, *rest):
+    parts, weight, keep, send, x = rest[:4], rest[4], rest[5], rest[6], rest[7]
     rows = parts[0].shape[0]
-    for q in range(4):
-        x[q * rows : (q + 1) * rows, :] = parts[q][...]
-    cols = out.shape[1]
+    upper = keeps_upper(z_ref)
+
+    def assemble(order):
+        for place, q in enumerate(order):
+            x[place * rows : (place + 1) * rows, :] = parts[q][...]
+
+    pl.when(upper)(lambda: assemble((2, 3, 0, 1)))
+    pl.when(jnp.logical_not(upper))(lambda: assemble((0, 1, 2, 3)))
+    cols = keep.shape[1]
     for c in range(0, cols, BLOCK):
         n = min(BLOCK, cols - c)
         tile = jnp.dot(x[...], weight[:, first_col + c : first_col + c + n], preferred_element_type=jnp.float32)
-        out[:, c : c + n] = tile.astype(jnp.bfloat16)
+        tile = tile.astype(jnp.bfloat16)
+        keep[:, c : c + n] = tile[: 2 * rows]
+        send[:, c : c + n] = tile[2 * rows :]
 
 
 def smem():
@@ -341,18 +356,6 @@
 
 def add(x, y):
     return (x.astype(jnp.float32) + y.astype(jnp.float32)).astype(jnp.bfloat16)
-
-
-def inwards(piece):
-    return lax.ppermute(piece, "head", [(0, 1), (3, 2)])
-
-
-def across_middle(pair):
-    return lax.ppermute(pair, "head", [(1, 2), (2, 1)])
-
-
-def outwards(whole):
-    return lax.ppermute(whole, "head", [(1, 0), (2, 3)])
 
 
 def local(latent_cache, lengths, decode_rows, q_nope, q_rope, new_latent, key_up, value_up, out_proj):
@@ -455,14 +458,14 @@
         cols = columns // pieces
         return pl.pallas_call(
             functools.partial(project_kernel, piece * cols),
-            out_shape=jax.ShapeDtypeStruct((4 * part_rows, cols), jnp.bfloat16),
-            in_specs=[vmem()] * 5,
-            out_specs=vmem(),
+            out_shape=[jax.ShapeDtypeStruct((2 * part_rows, cols), jnp.bfloat16)] * 2,
+            in_specs=[smem()] + [vmem()] * 5,
+            out_specs=[vmem()] * 2,
             scratch_shapes=[pltpu.VMEM((4 * part_rows, out_proj.shape[0]), jnp.bfloat16)],
             compiler_params=limit(24),
             cost_estimate=cost(2),
             name="project_out",
-        )(*parts, out_proj)
+        )(z, *parts, out_proj)
 
     received = [packed[0]] + [flip(packed[k], "seq", k) for k in range(1, 4)]
     near_rows = attend(received[:2], 0)
@@ -472,30 +475,34 @@
     near = [near_rows, flip(near_rows, "seq", 1), near_across, flip(near_across, "seq", 1)]
     far_across = flip(far_rows, "seq", 2)
     first, second = project(near, 0), project(near, 1)
-    relayed, _ = lax.optimization_barrier((far_across, second))
+    relayed, _ = lax.optimization_barrier((far_across, second[0]))
     far = [far_rows, flip(far_rows, "seq", 1), far_across, flip(relayed, "seq", 1)]
-    first_in, second_in = inwards(first), inwards(second)
-    first_pair = add(first, first_in)
-    first_cross = across_middle(first_pair)
     third, fourth = project(far, 0), project(far, 1)
-    third_in, fourth_in = inwards(third), inwards(fourth)
-    second_in, _ = lax.optimization_barrier((second_in, third))
-    second_pair = add(second, second_in)
-    second_cross = across_middle(second_pair)
-    first_cross, _ = lax.optimization_barrier((first_cross, fourth))
-    first_whole = add(first_pair, first_cross)
-    first_out = outwards(first_whole)
-    third_pair = add(third, third_in)
-    third_cross = across_middle(third_pair)
-    second_whole = add(second_pair, second_cross)
-    second_out = outwards(second_whole)
-    fourth_pair = add(fourth, fourth_in)
-    fourth_cross = across_middle(fourth_pair)
-    third_whole = add(third_pair, third_cross)
-    third_out = outwards(third_whole)
-    fourth_whole = add(fourth_pair, fourth_cross)
-    fourth_out = outwards(fourth_whole)
-    arrays = [first_whole, first_out, second_whole, second_out, third_whole, third_out, fourth_whole, fourth_out]
+
+    def swap(piece):
+        return flip(piece[1], "head", 1)
+
+    first_in, second_in = swap(first), swap(second)
+    first_pair = add(first[0], first_in)
+    first_cross = flip(first_pair, "head", 3)
+    third_in, fourth_in = swap(third), swap(fourth)
+    second_in, _ = lax.optimization_barrier((second_in, third[0]))
+    second_pair = add(second[0], second_in)
+    second_cross = flip(second_pair, "head", 3)
+    first_cross, _ = lax.optimization_barrier((first_cross, fourth[0]))
+    first_sum = add(first_pair, first_cross)
+    first_other = flip(first_sum, "head", 1)
+    third_pair = add(third[0], third_in)
+    third_cross = flip(third_pair, "head", 3)
+    second_sum = add(second_pair, second_cross)
+    second_other = flip(second_sum, "head", 1)
+    fourth_pair = add(fourth[0], fourth_in)
+    fourth_cross = flip(fourth_pair, "head", 3)
+    third_sum = add(third_pair, third_cross)
+    third_other = flip(third_sum, "head", 1)
+    fourth_sum = add(fourth_pair, fourth_cross)
+    fourth_other = flip(fourth_sum, "head", 1)
+    arrays = [first_sum, first_other, second_sum, second_other, third_sum, third_other, fourth_sum, fourth_other]
     scratch = [pltpu.VMEM((steps * sources * requests, columns), jnp.bfloat16)]
     kernel = functools.partial(order_kernel, 2)
     return order(kernel, [smem()] + [vmem()] * (1 + len(arrays)), scratch, [z, pick] + arrays)

time: 81.8 us -> 77.9 us (0.952)
  starting transfers between devices: 33.6 us -> 25.3 us
  local copies, waits for them, and re-layouts: 0.82 us -> 5.99 us
    ppermute x12 -> x0, starting transfers between devices: 25.5 us -> none  [the longest x4 17.4 us: inwards(): return lax.ppermute(piece, 'head', [(0, 1), (3, 2)])]
    ppermute x12 -> x0, waiting for transfers between devices: 20 us -> none  [the longest x4 18.3 us: outwards(): return lax.ppermute(whole, 'head', [(1, 0), (2, 3)])]
    ppermute x9 -> x21, waiting for transfers between devices: 1.07 us -> 20.6 us  [flip(): return lax.ppermute(x, axis, [(i, i ^ distance) for i in range(size)])]
    ppermute x9 -> x21, starting transfers between devices: 8.12 us -> 25.3 us  [flip(): return lax.ppermute(x, axis, [(i, i ^ distance) for i in range(size)])]
    unnamed x28 -> x30, local copies, waits for them, and re-layouts: 0.82 us -> 5.99 us
  transfers between devices with their start and end apart: 21 -> 21, of which waited for: 6 -> 10; matrix products, arithmetic and copies ran while one was open for 1% -> 0% of each run, Pallas kernels for 26% -> 27%
where the time goes in v6:
time: 77.9 us; the launch traced here: 77.7 us
  starting transfers between devices  25.3 us (32%)
  Pallas kernels  25.2 us (32%)
  waiting for transfers between devices  20.6 us (26%)
  local copies, waits for them, and re-layouts  5.99 us (8%)
    ppermute x21, starting transfers between devices, flip(): return lax.ppermute(x, axis, [(i, i ^ distance) for i in range(size)])  25.3 us
    ppermute x21, waiting for transfers between devices, flip(): return lax.ppermute(x, axis, [(i, i ^ distance) for i in range(size)])  20.6 us
    pallas_call x2, Pallas kernels, attend(): pl.pallas_call(functools.partial(attend_kernel, sizes, scale, relative, b...  15.6 us
    unnamed x30, local copies, waits for them, and re-layouts  5.99 us
    pallas_call x4, Pallas kernels, project(): pl.pallas_call(functools.partial(project_kernel, piece * cols), out_shape...  5.68 us
    pallas_call x1, Pallas kernels, order(): pl.pallas_call(kernel, out_shape=jax.ShapeDtypeStruct((steps, sources * r...  1.74 us
  transfers between devices with their start and end apart: 21, of which 10 were waited for; matrix products, arithmetic and copies ran while one was open for 0% of the time, Pallas kernels for 27%

profile of v6, /device:TPU:0, one launch (start us, length us, event | category | flops | bytes accessed | tf_op | source)
XLA Modules:
  0.0 77.7 jit_solution(6620520205994767225)
XLA Ops:
  0.0 0.7 copy-done.7
  0.8 1.1 %place_rows.1.after_ref.pick_ref = bf16[4,64,256]{2,1,0:T(8,128)(2,1)S(1)} custom-call(s32[1]{0:T(128)} %bitcast.1.me_ref, s32[64]{0:T(128)S(1)} %copy-done.7), custom_call_target="tpu_custom_call" | custom-call | flops 2000000000 | bytes 6000000 | tf_op jit(solution)/shard_map/place_rows/pallas_call | solution.py:379
  1.9 0.0 slice-start.5
  1.9 0.0 copy-start.1
  1.9 0.0 copy-start.2
  1.9 0.0 copy-start.6
  1.9 0.0 copy-start.8
  1.9 1.1 %pack_queries.1 = (bf16[1,848,128]{2,1,0:T(8,128)(2,1)S(1)}, bf16[1,848,128]{2,1,0:T(8,128)(2,1)S(1)}, bf16[1,848,128]{2,1,0:T(8,128)(2,1)S(1)}, bf16[1,848,128]{2,1,0:T(8,128)(2,1)S(1)}) custom-call(s32[1]{0:T(128)} %bitcast.1.me_ref, s32[64]{0:T(128)S(1)} %copy-done.7, bf16[4,16,32,128]{3,2,1,0:T(8,128)(2,1)S(1)} %copy-done.3, ...), custom_call_target="tpu_custom_call" | custom-call | flops 6000000000 | bytes 18000000 | tf_op jit(solution)/shard_map/pack_queries/pallas_call | solution.py:391
  3.1 0.5 collective-permute-start
  3.6 2.6 %collective-permute-start.3 = (bf16[1,848,128]{2,1,0:T(8,128)(2,1)S(1)}, bf16[1,848,128]{2,1,0:T(8,128)(2,1)S(1)}, u32[]{:S(2)}, u32[]{:S(2)}) collective-permute-start(bf16[1,848,128]{2,1,0:T(8,128)(2,1)S(1)} %get-tuple-element.24), channel_id=1, source_target_pairs={{0,8},{4,12},{8,0},{12,4},{1,9},{5,13},{9,1},{13,5},{2,10},{6,14},... | collective-permute-start | bytes 651272 | tf_op jit(solution)/shard_map/ppermute | solution.py:354
  6.2 0.1 collective-permute-start.4
  6.3 8.4 %attend.2.rest_0_ = bf16[32,4096]{1,0:T(8,128)(2,1)S(1)} custom-call(s32[1]{0:T(128)} %bitcast.1.me_ref, s32[64]{0:T(128)S(1)} %copy-done.8, s32[4,16]{1,0:T(4,128)S(1)} %copy-done.6, bf16[1,848,128]{2,1,0:T(8,128)(2,1)S(1)} %get-tuple-element.22.rest_0_, bf16[1,848,128]{2,1,0:T(8,128)(2,1)S(1)} %collective-permute-done.rest_1_, ...), custom_call_target="tpu_custom_call" | custom-call | flops 8000000000 | bytes 24000000 | tf_op jit(solution)/shard_map/attend/pallas_call | solution.py:409
  14.8 0.2 collective-permute-start.1
  15.0 2.4 %collective-permute-start.2 = (bf16[32,4096]{1,0:T(8,128)(2,1)S(1)}, bf16[32,4096]{1,0:T(8,128)(2,1)S(1)}, u32[]{:S(2)}, u32[]{:S(2)}) collective-permute-start(bf16[32,4096]{1,0:T(8,128)(2,1)S(1)} %attend.2.rest_0_), channel_id=1, source_target_pairs={{0,8},{4,12},{8,0},{12,4},{1,9},{5,13},{9,1},{13,5},{2,10},{6,14},... | collective-permute-start | bytes 786440 | tf_op jit(solution)/shard_map/ppermute | solution.py:354
  17.4 7.2 %attend.3.rest_0_ = bf16[32,4096]{1,0:T(8,128)(2,1)S(1)} custom-call(s32[1]{0:T(128)} %bitcast.1.me_ref, s32[64]{0:T(128)S(1)} %copy-done.8, s32[4,16]{1,0:T(4,128)S(1)} %copy-done.6, bf16[1,848,128]{2,1,0:T(8,128)(2,1)S(1)} %collective-permute-done.3.rest_0_, bf16[1,848,128]{2,1,0:T(8,128)(2,1)S(1)} %collective-permute-done.4.rest_1_, ...), custom_call_target="tpu_custom_call" | custom-call | flops 8000000000 | bytes 24000000 | tf_op jit(solution)/shard_map/attend/pallas_call | solution.py:409
  24.5 1.5 %collective-permute-start.5 = (bf16[32,4096]{1,0:T(8,128)(2,1)S(1)}, bf16[32,4096]{1,0:T(8,128)(2,1)S(1)}, u32[]{:S(2)}, u32[]{:S(2)}) collective-permute-start(bf16[32,4096]{1,0:T(8,128)(2,1)S(1)} %collective-permute-done.2.rest_2_), channel_id=1, source_target_pairs={{0,4},{4,0},{8,12},{12,8},{1,5},{5,1},{9,13},{13,9},{2,6},{6,2},{1... | collective-permute-start | bytes 786440 | tf_op jit(solution)/shard_map/ppermute | solution.py:354
  26.0 0.1 collective-permute-start.8
  26.1 0.4 collective-permute-start.9
  26.5 0.7 collective-permute-done.5.rest_3_
  27.2 5.2 %copy-done = bf16[4096,1792]{1,0:T(8,128)(2,1)S(1)} copy-done((bf16[4096,1792]{1,0:T(8,128)(2,1)S(1)}, bf16[4096,1792]{1,0:T(8,128)(2,1)}, u32[]{:S(2)}) %copy-start) | copy-done | bytes 14680088
  32.4 1.4 %project_out.4 = (bf16[64,896]{1,0:T(8,128)(2,1)S(1)}, bf16[64,896]{1,0:T(8,128)(2,1)S(1)}) custom-call(s32[1]{0:T(128)} %bitcast.z_ref, bf16[32,4096]{1,0:T(8,128)(2,1)S(1)} %attend.2.rest_0_, bf16[32,4096]{1,0:T(8,128)(2,1)S(1)} %collective-permute-done.1.rest_1_, bf16[32,4096]{1,0:T(8,128)(2,1)S(1)} %collective-permute-done.2.rest_2_, ...), custom_call_target="tpu_custom_call" | custom-call | flops 2000000000 | bytes 6000000 | tf_op jit(solution)/shard_map/project_out/pallas_call | solution.py:459
  33.7 0.0 slice-start.2
  33.8 1.7 %collective-permute-start.6 = (bf16[64,896]{1,0:T(8,128)(2,1)S(1)}, bf16[64,896]{1,0:T(8,128)(2,1)S(1)}, u32[]{:S(2)}, u32[]{:S(2)}) collective-permute-start(bf16[64,896]{1,0:T(8,128)(2,1)S(1)} %get-tuple-element.28), channel_id=1, source_target_pairs={{0,1},{1,0},{2,3},{3,2},{4,5},{5,4},{6,7},{7,6},{8,9},{9,8},{10,11... | collective-permute-start | bytes 344072 | tf_op jit(solution)/shard_map/ppermute | solution.py:354
  35.4 1.4 %project_out.5 = (bf16[64,896]{1,0:T(8,128)(2,1)S(1)}, bf16[64,896]{1,0:T(8,128)(2,1)S(1)}) custom-call(s32[1]{0:T(128)} %bitcast.z_ref, bf16[32,4096]{1,0:T(8,128)(2,1)S(1)} %attend.2.rest_0_, bf16[32,4096]{1,0:T(8,128)(2,1)S(1)} %collective-permute-done.1.rest_1_, bf16[32,4096]{1,0:T(8,128)(2,1)S(1)} %collective-permute-done.2.rest_2_, ...), custom_call_target="tpu_custom_call" | custom-call | flops 2000000000 | bytes 6000000 | tf_op jit(solution)/shard_map/project_out/pallas_call | solution.py:459
  36.8 0.1 collective-permute-start.10
  37.0 0.4 collective-permute-start.12
  37.4 1.8 %collective-permute-done.6 = bf16[64,896]{1,0:T(8,128)(2,1)S(1)} collective-permute-done((bf16[64,896]{1,0:T(8,128)(2,1)S(1)}, bf16[64,896]{1,0:T(8,128)(2,1)S(1)}, u32[]{:S(2)}, u32[]{:S(2)}) %collective-permute-start.6) | collective-permute-done | bytes 114720 | tf_op jit(solution)/shard_map/ppermute | solution.py:354
  39.3 4.0 %collective-permute-start.7 = (bf16[64,896]{1,0:T(8,128)(2,1)S(1)}, bf16[64,896]{1,0:T(8,128)(2,1)S(1)}, u32[]{:S(2)}, u32[]{:S(2)}) collective-permute-start(bf16[64,896]{1,0:T(8,128)(2,1)S(1)} %add_convert_fusion.7), channel_id=1, source_target_pairs={{0,3},{1,2},{2,1},{3,0},{4,7},{5,6},{6,5},{7,4},{8,11},{9,10},{10,... | collective-permute-start | bytes 344072 | tf_op jit(solution)/shard_map/ppermute | solution.py:354
  43.3 1.6 %project_out.6 = (bf16[64,896]{1,0:T(8,128)(2,1)S(1)}, bf16[64,896]{1,0:T(8,128)(2,1)S(1)}) custom-call(s32[1]{0:T(128)} %bitcast.z_ref, bf16[32,4096]{1,0:T(8,128)(2,1)S(1)} %attend.3.rest_0_, bf16[32,4096]{1,0:T(8,128)(2,1)S(1)} %collective-permute-done.8.rest_1_, bf16[32,4096]{1,0:T(8,128)(2,1)S(1)} %collective-permute-done.9.rest_2_, ...), custom_call_target="tpu_custom_call" | custom-call | flops 2000000000 | bytes 6000000 | tf_op jit(solution)/shard_map/project_out/pallas_call | solution.py:459
  44.9 2.1 %collective-permute-done.7 = bf16[64,896]{1,0:T(8,128)(2,1)S(1)} collective-permute-done((bf16[64,896]{1,0:T(8,128)(2,1)S(1)}, bf16[64,896]{1,0:T(8,128)(2,1)S(1)}, u32[]{:S(2)}, u32[]{:S(2)}) %collective-permute-start.7) | collective-permute-done | bytes 114720 | tf_op jit(solution)/shard_map/ppermute | solution.py:354
  47.0 1.4 %project_out.7 = (bf16[64,896]{1,0:T(8,128)(2,1)S(1)}, bf16[64,896]{1,0:T(8,128)(2,1)S(1)}) custom-call(s32[1]{0:T(128)} %bitcast.z_ref, bf16[32,4096]{1,0:T(8,128)(2,1)S(1)} %attend.3.rest_0_, bf16[32,4096]{1,0:T(8,128)(2,1)S(1)} %collective-permute-done.8.rest_1_, bf16[32,4096]{1,0:T(8,128)(2,1)S(1)} %collective-permute-done.9.rest_2_, ...), custom_call_target="tpu_custom_call" | custom-call | flops 2000000000 | bytes 6000000 | tf_op jit(solution)/shard_map/project_out/pallas_call | solution.py:459
  48.5 2.9 %collective-permute-start.13 = (bf16[64,896]{1,0:T(8,128)(2,1)S(1)}, bf16[64,896]{1,0:T(8,128)(2,1)S(1)}, u32[]{:S(2)}, u32[]{:S(2)}) collective-permute-start(bf16[64,896]{1,0:T(8,128)(2,1)S(1)} %add_convert_fusion.5), channel_id=1, source_target_pairs={{0,3},{1,2},{2,1},{3,0},{4,7},{5,6},{6,5},{7,4},{8,11},{9,10},{10,... | collective-permute-start | bytes 344072 | tf_op jit(solution)/shard_map/ppermute | solution.py:354
  51.4 0.1 collective-permute-start.11
  51.5 2.0 %collective-permute-start.15 = (bf16[64,896]{1,0:T(8,128)(2,1)S(1)}, bf16[64,896]{1,0:T(8,128)(2,1)S(1)}, u32[]{:S(2)}, u32[]{:S(2)}) collective-permute-start(bf16[64,896]{1,0:T(8,128)(2,1)S(1)} %get-tuple-element.37), channel_id=1, source_target_pairs={{0,1},{1,0},{2,3},{3,2},{4,5},{5,4},{6,7},{7,6},{8,9},{9,8},{10,11... | collective-permute-start | bytes 344072 | tf_op jit(solution)/shard_map/ppermute | solution.py:354
  53.5 0.1 collective-permute-start.18
  53.6 2.8 %collective-permute-done.13 = bf16[64,896]{1,0:T(8,128)(2,1)S(1)} collective-permute-done((bf16[64,896]{1,0:T(8,128)(2,1)S(1)}, bf16[64,896]{1,0:T(8,128)(2,1)S(1)}, u32[]{:S(2)}, u32[]{:S(2)}) %collective-permute-start.13) | collective-permute-done | bytes 114720 | tf_op jit(solution)/shard_map/ppermute | solution.py:354
  56.4 0.2 collective-permute-start.14
  56.7 4.0 %collective-permute-done.15 = bf16[64,896]{1,0:T(8,128)(2,1)S(1)} collective-permute-done((bf16[64,896]{1,0:T(8,128)(2,1)S(1)}, bf16[64,896]{1,0:T(8,128)(2,1)S(1)}, u32[]{:S(2)}, u32[]{:S(2)}) %collective-permute-start.15) | collective-permute-done | bytes 114720 | tf_op jit(solution)/shard_map/ppermute | solution.py:354
  60.7 1.6 %collective-permute-start.16 = (bf16[64,896]{1,0:T(8,128)(2,1)S(1)}, bf16[64,896]{1,0:T(8,128)(2,1)S(1)}, u32[]{:S(2)}, u32[]{:S(2)}) collective-permute-start(bf16[64,896]{1,0:T(8,128)(2,1)S(1)} %add_convert_fusion.3), channel_id=1, source_target_pairs={{0,3},{1,2},{2,1},{3,0},{4,7},{5,6},{6,5},{7,4},{8,11},{9,10},{10,... | collective-permute-start | bytes 344072 | tf_op jit(solution)/shard_map/ppermute | solution.py:354
  62.3 0.7 collective-permute-done.18
  63.1 1.7 %collective-permute-start.19 = (bf16[64,896]{1,0:T(8,128)(2,1)S(1)}, bf16[64,896]{1,0:T(8,128)(2,1)S(1)}, u32[]{:S(2)}, u32[]{:S(2)}) collective-permute-start(bf16[64,896]{1,0:T(8,128)(2,1)S(1)} %add_convert_fusion.1), channel_id=1, source_target_pairs={{0,3},{1,2},{2,1},{3,0},{4,7},{5,6},{6,5},{7,4},{8,11},{9,10},{10,... | collective-permute-start | bytes 344072 | tf_op jit(solution)/shard_map/ppermute | solution.py:354
  64.8 3.9 %collective-permute-done.16 = bf16[64,896]{1,0:T(8,128)(2,1)S(1)} collective-permute-done((bf16[64,896]{1,0:T(8,128)(2,1)S(1)}, bf16[64,896]{1,0:T(8,128)(2,1)S(1)}, u32[]{:S(2)}, u32[]{:S(2)}) %collective-permute-start.16) | collective-permute-done | bytes 114720 | tf_op jit(solution)/shard_map/ppermute | solution.py:354
  68.8 1.5 %collective-permute-start.17 = (bf16[64,896]{1,0:T(8,128)(2,1)S(1)}, bf16[64,896]{1,0:T(8,128)(2,1)S(1)}, u32[]{:S(2)}, u32[]{:S(2)}) collective-permute-start(bf16[64,896]{1,0:T(8,128)(2,1)S(1)} %add_convert_fusion.2.rest_4_), channel_id=1, source_target_pairs={{0,1},{1,0},{2,3},{3,2},{4,5},{5,4},{6,7},{7,6},{8,9},{9,8},{10,11... | collective-permute-start | bytes 344072 | tf_op jit(solution)/shard_map/ppermute | solution.py:354
  70.2 0.8 %collective-permute-done.19 = bf16[64,896]{1,0:T(8,128)(2,1)S(1)} collective-permute-done((bf16[64,896]{1,0:T(8,128)(2,1)S(1)}, bf16[64,896]{1,0:T(8,128)(2,1)S(1)}, u32[]{:S(2)}, u32[]{:S(2)}) %collective-permute-start.19) | collective-permute-done | bytes 114720 | tf_op jit(solution)/shard_map/ppermute | solution.py:354
  71.0 1.2 %collective-permute-start.20 = (bf16[64,896]{1,0:T(8,128)(2,1)S(1)}, bf16[64,896]{1,0:T(8,128)(2,1)S(1)}, u32[]{:S(2)}, u32[]{:S(2)}) collective-permute-start(bf16[64,896]{1,0:T(8,128)(2,1)S(1)} %add_convert_fusion.rest_6_), channel_id=1, source_target_pairs={{0,1},{1,0},{2,3},{3,2},{4,5},{5,4},{6,7},{7,6},{8,9},{9,8},{10,11... | collective-permute-start | bytes 344072 | tf_op jit(solution)/shard_map/ppermute | solution.py:354
  72.3 1.3 %collective-permute-done.17.rest_5_ = bf16[64,896]{1,0:T(8,128)(2,1)S(1)} collective-permute-done((bf16[64,896]{1,0:T(8,128)(2,1)S(1)}, bf16[64,896]{1,0:T(8,128)(2,1)S(1)}, u32[]{:S(2)}, u32[]{:S(2)}) %collective-permute-start.17) | collective-permute-done | bytes 114720 | tf_op jit(solution)/shard_map/ppermute | solution.py:354
  73.6 2.3 %collective-permute-done.20.rest_7_ = bf16[64,896]{1,0:T(8,128)(2,1)S(1)} collective-permute-done((bf16[64,896]{1,0:T(8,128)(2,1)S(1)}, bf16[64,896]{1,0:T(8,128)(2,1)S(1)}, u32[]{:S(2)}, u32[]{:S(2)}) %collective-permute-start.20) | collective-permute-done | bytes 114720 | tf_op jit(solution)/shard_map/ppermute | solution.py:354
  75.9 1.7 %order_rows.1 = bf16[4,64,1792]{2,1,0:T(8,128)(2,1)} custom-call(s32[1]{0:T(128)} %bitcast.z_ref, bf16[4,64,256]{2,1,0:T(8,128)(2,1)S(1)} %place_rows.1.after_ref.pick_ref, bf16[64,896]{1,0:T(8,128)(2,1)S(1)} %add_convert_fusion.6.rest_0_, bf16[64,896]{1,0:T(8,128)(2,1)S(1)} %collective-permute-done.11.rest_1_, ...), custom_call_target="tpu_custom_call" | custom-call | flops 2000000000 | bytes 6000000 | tf_op jit(solution)/shard_map/order_rows/pallas_call | solution.py:433
  (43 shorter events, 0.3 us)
Async XLA Ops:
  0.0 1.8 %copy-start.3 = (bf16[4,16,32,128]{3,2,1,0:T(8,128)(2,1)S(1)}, bf16[4,16,32,128]{3,2,1,0:T(8,128)(2,1)}, u32[]{:S(2)}) copy-start(bf16[4,16,32,128]{3,2,1,0:T(8,128)(2,1)} %nope_ref.1) | copy-start | bytes 1572868
  0.0 1.9 %copy-start.4 = (bf16[4,16,32,64]{3,2,1,0:T(8,128)(2,1)S(1)}, bf16[4,16,32,64]{3,2,1,0:T(8,128)(2,1)}, u32[]{:S(2)}) copy-start(bf16[4,16,32,64]{3,2,1,0:T(8,128)(2,1)} %rope_ref.1) | copy-start | bytes 786436
  0.0 1.9 %copy-start.5 = (bf16[4,16,576]{2,1,0:T(8,128)(2,1)S(1)}, bf16[4,16,576]{2,1,0:T(8,128)(2,1)}, u32[]{:S(2)}) copy-start(bf16[4,16,576]{2,1,0:T(8,128)(2,1)} %fresh_ref.1) | copy-start | bytes 221188
  0.0 0.7 copy-start.7
  0.8 5.5 %slice-start.4 = ((s8[4718592]{0:T(1024)(128)(4,1)}), s8[4194304]{0:T(1024)(128)(4,1)S(1)}, s32[]{:S(2)}) async-start(s8[4718592]{0:T(1024)(128)(4,1)} %bitcast.5), calls=%async_computation.4 | async-start | bytes 8388608
  1.9 4.4 %slice-start.5 = ((s8[4718592]{0:T(1024)(128)(4,1)}), s8[524288]{0:T(1024)(128)(4,1)S(1)}, s32[]{:S(2)}) async-start(s8[4718592]{0:T(1024)(128)(4,1)} %bitcast.5), calls=%async_computation.5 | async-start | bytes 1048576
  1.9 4.4 %copy-start.1 = (bf16[32,128,512]{2,1,0:T(8,128)(2,1)S(1)}, bf16[32,128,512]{2,1,0:T(8,128)(2,1)}, u32[]{:S(2)}) copy-start(bf16[32,128,512]{2,1,0:T(8,128)(2,1)} %rest_3_.3) | copy-start | bytes 12582916
  1.9 4.4 %copy-start.2 = (bf16[32,512,128]{2,1,0:T(8,128)(2,1)S(1)}, bf16[32,512,128]{2,1,0:T(8,128)(2,1)}, u32[]{:S(2)}) copy-start(bf16[32,512,128]{2,1,0:T(8,128)(2,1)} %rest_4_.7) | copy-start | bytes 12582916
  1.9 4.4 %copy-start.6 = (s32[4,16]{1,0:T(4,128)S(1)}, s32[4,16]{1,0:T(4,128)}, u32[]{:S(2)}) copy-start(s32[4,16]{1,0:T(4,128)} %length_ref.3) | copy-start | bytes 772
  1.9 4.4 %copy-start.8 = (s32[64]{0:T(128)S(1)}, s32[64]{0:T(128)}, u32[]{:S(2)}) copy-start(s32[64]{0:T(128)} %decode_ref.7) | copy-start | bytes 772
  3.1 3.2 %collective-permute-start = (bf16[1,848,128]{2,1,0:T(8,128)(2,1)S(1)}, bf16[1,848,128]{2,1,0:T(8,128)(2,1)S(1)}, u32[]{:S(2)}, u32[]{:S(2)}) collective-permute-start(bf16[1,848,128]{2,1,0:T(8,128)(2,1)S(1)} %get-tuple-element.23), channel_id=1, source_target_pairs={{0,4},{4,0},{8,12},{12,8},{1,5},{5,1},{9,13},{13,9},{2,6},{6,2},{1... | collective-permute-start | bytes 651272 | tf_op jit(solution)/shard_map/ppermute | solution.py:354
  3.6 13.7 %collective-permute-start.3 = (bf16[1,848,128]{2,1,0:T(8,128)(2,1)S(1)}, bf16[1,848,128]{2,1,0:T(8,128)(2,1)S(1)}, u32[]{:S(2)}, u32[]{:S(2)}) collective-permute-start(bf16[1,848,128]{2,1,0:T(8,128)(2,1)S(1)} %get-tuple-element.24), channel_id=1, source_target_pairs={{0,8},{4,12},{8,0},{12,4},{1,9},{5,13},{9,1},{13,5},{2,10},{6,14},... | collective-permute-start | bytes 651272 | tf_op jit(solution)/shard_map/ppermute | solution.py:354
  6.2 11.1 %collective-permute-start.4 = (bf16[1,848,128]{2,1,0:T(8,128)(2,1)S(1)}, bf16[1,848,128]{2,1,0:T(8,128)(2,1)S(1)}, u32[]{:S(2)}, u32[]{:S(2)}) collective-permute-start(bf16[1,848,128]{2,1,0:T(8,128)(2,1)S(1)} %get-tuple-element.25), channel_id=1, source_target_pairs={{0,12},{4,8},{8,4},{12,0},{1,13},{5,9},{9,5},{13,1},{2,14},{6,10},... | collective-permute-start | bytes 651272 | tf_op jit(solution)/shard_map/ppermute | solution.py:354
  14.8 11.8 %collective-permute-start.1 = (bf16[32,4096]{1,0:T(8,128)(2,1)S(1)}, bf16[32,4096]{1,0:T(8,128)(2,1)S(1)}, u32[]{:S(2)}, u32[]{:S(2)}) collective-permute-start(bf16[32,4096]{1,0:T(8,128)(2,1)S(1)} %attend.2.rest_0_), channel_id=1, source_target_pairs={{0,4},{4,0},{8,12},{12,8},{1,5},{5,1},{9,13},{13,9},{2,6},{6,2},{1... | collective-permute-start | bytes 786440 | tf_op jit(solution)/shard_map/ppermute | solution.py:354
  15.0 9.5 %collective-permute-start.2 = (bf16[32,4096]{1,0:T(8,128)(2,1)S(1)}, bf16[32,4096]{1,0:T(8,128)(2,1)S(1)}, u32[]{:S(2)}, u32[]{:S(2)}) collective-permute-start(bf16[32,4096]{1,0:T(8,128)(2,1)S(1)} %attend.2.rest_0_), channel_id=1, source_target_pairs={{0,8},{4,12},{8,0},{12,4},{1,9},{5,13},{9,1},{13,5},{2,10},{6,14},... | collective-permute-start | bytes 786440 | tf_op jit(solution)/shard_map/ppermute | solution.py:354
  24.5 2.7 %collective-permute-start.5 = (bf16[32,4096]{1,0:T(8,128)(2,1)S(1)}, bf16[32,4096]{1,0:T(8,128)(2,1)S(1)}, u32[]{:S(2)}, u32[]{:S(2)}) collective-permute-start(bf16[32,4096]{1,0:T(8,128)(2,1)S(1)} %collective-permute-done.2.rest_2_), channel_id=1, source_target_pairs={{0,4},{4,0},{8,12},{12,8},{1,5},{5,1},{9,13},{13,9},{2,6},{6,2},{1... | collective-permute-start | bytes 786440 | tf_op jit(solution)/shard_map/ppermute | solution.py:354
  26.0 17.2 %collective-permute-start.8 = (bf16[32,4096]{1,0:T(8,128)(2,1)S(1)}, bf16[32,4096]{1,0:T(8,128)(2,1)S(1)}, u32[]{:S(2)}, u32[]{:S(2)}) collective-permute-start(bf16[32,4096]{1,0:T(8,128)(2,1)S(1)} %attend.3.rest_0_), channel_id=1, source_target_pairs={{0,4},{4,0},{8,12},{12,8},{1,5},{5,1},{9,13},{13,9},{2,6},{6,2},{1... | collective-permute-start | bytes 786440 | tf_op jit(solution)/shard_map/ppermute | solution.py:354
  26.1 10.7 %collective-permute-start.9 = (bf16[32,4096]{1,0:T(8,128)(2,1)S(1)}, bf16[32,4096]{1,0:T(8,128)(2,1)S(1)}, u32[]{:S(2)}, u32[]{:S(2)}) collective-permute-start(bf16[32,4096]{1,0:T(8,128)(2,1)S(1)} %attend.3.rest_0_), channel_id=1, source_target_pairs={{0,8},{4,12},{8,0},{12,4},{1,9},{5,13},{9,1},{13,5},{2,10},{6,14},... | collective-permute-start | bytes 786440 | tf_op jit(solution)/shard_map/ppermute | solution.py:354
  27.2 5.2 %copy-start = (bf16[4096,1792]{1,0:T(8,128)(2,1)S(1)}, bf16[4096,1792]{1,0:T(8,128)(2,1)}, u32[]{:S(2)}) copy-start(bf16[4096,1792]{1,0:T(8,128)(2,1)} %rest_4_.11) | copy-start | bytes 44040196
  32.4 10.9 %slice-start = ((s8[14680064]{0:T(1024)(128)(4,1)}), s8[4194304]{0:T(1024)(128)(4,1)S(1)}, s32[]{:S(2)}) async-start(s8[14680064]{0:T(1024)(128)(4,1)} %bitcast.3), calls=%async_computation | async-start | bytes 8388608
  32.4 10.9 %slice-start.1 = ((s8[14680064]{0:T(1024)(128)(4,1)}), s8[4194304]{0:T(1024)(128)(4,1)S(1)}, s32[]{:S(2)}) async-start(s8[14680064]{0:T(1024)(128)(4,1)} %bitcast.3), calls=%async_computation.1 | async-start | bytes 8388608
  33.7 9.5 %slice-start.2 = ((s8[14680064]{0:T(1024)(128)(4,1)}), s8[4194304]{0:T(1024)(128)(4,1)S(1)}, s32[]{:S(2)}) async-start(s8[14680064]{0:T(1024)(128)(4,1)} %bitcast.3), calls=%async_computation.2 | async-start | bytes 8388608
  33.8 9.5 %slice-start.3 = ((s8[14680064]{0:T(1024)(128)(4,1)}), s8[2097152]{0:T(1024)(128)(4,1)S(1)}, s32[]{:S(2)}) async-start(s8[14680064]{0:T(1024)(128)(4,1)} %bitcast.3), calls=%async_computation.3 | async-start | bytes 4194304
  33.8 5.5 %collective-permute-start.6 = (bf16[64,896]{1,0:T(8,128)(2,1)S(1)}, bf16[64,896]{1,0:T(8,128)(2,1)S(1)}, u32[]{:S(2)}, u32[]{:S(2)}) collective-permute-start(bf16[64,896]{1,0:T(8,128)(2,1)S(1)} %get-tuple-element.28), channel_id=1, source_target_pairs={{0,1},{1,0},{2,3},{3,2},{4,5},{5,4},{6,7},{7,6},{8,9},{9,8},{10,11... | collective-permute-start | bytes 344072 | tf_op jit(solution)/shard_map/ppermute | solution.py:354
  36.8 6.5 %collective-permute-start.10 = (bf16[32,4096]{1,0:T(8,128)(2,1)S(1)}, bf16[32,4096]{1,0:T(8,128)(2,1)S(1)}, u32[]{:S(2)}, u32[]{:S(2)}) collective-permute-start(bf16[32,4096]{1,0:T(8,128)(2,1)S(1)} %collective-permute-done.9.rest_2_), channel_id=1, source_target_pairs={{0,4},{4,0},{8,12},{12,8},{1,5},{5,1},{9,13},{13,9},{2,6},{6,2},{1... | collective-permute-start | bytes 786440 | tf_op jit(solution)/shard_map/ppermute | solution.py:354
  37.0 11.4 %collective-permute-start.12 = (bf16[64,896]{1,0:T(8,128)(2,1)S(1)}, bf16[64,896]{1,0:T(8,128)(2,1)S(1)}, u32[]{:S(2)}, u32[]{:S(2)}) collective-permute-start(bf16[64,896]{1,0:T(8,128)(2,1)S(1)} %get-tuple-element.34), channel_id=1, source_target_pairs={{0,1},{1,0},{2,3},{3,2},{4,5},{5,4},{6,7},{7,6},{8,9},{9,8},{10,11... | collective-permute-start | bytes 344072 | tf_op jit(solution)/shard_map/ppermute | solution.py:354
  39.3 7.7 %collective-permute-start.7 = (bf16[64,896]{1,0:T(8,128)(2,1)S(1)}, bf16[64,896]{1,0:T(8,128)(2,1)S(1)}, u32[]{:S(2)}, u32[]{:S(2)}) collective-permute-start(bf16[64,896]{1,0:T(8,128)(2,1)S(1)} %add_convert_fusion.7), channel_id=1, source_target_pairs={{0,3},{1,2},{2,1},{3,0},{4,7},{5,6},{6,5},{7,4},{8,11},{9,10},{10,... | collective-permute-start | bytes 344072 | tf_op jit(solution)/shard_map/ppermute | solution.py:354
  48.5 7.9 %collective-permute-start.13 = (bf16[64,896]{1,0:T(8,128)(2,1)S(1)}, bf16[64,896]{1,0:T(8,128)(2,1)S(1)}, u32[]{:S(2)}, u32[]{:S(2)}) collective-permute-start(bf16[64,896]{1,0:T(8,128)(2,1)S(1)} %add_convert_fusion.5), channel_id=1, source_target_pairs={{0,3},{1,2},{2,1},{3,0},{4,7},{5,6},{6,5},{7,4},{8,11},{9,10},{10,... | collective-permute-start | bytes 344072 | tf_op jit(solution)/shard_map/ppermute | solution.py:354
  51.4 20.8 %collective-permute-start.11 = (bf16[64,896]{1,0:T(8,128)(2,1)S(1)}, bf16[64,896]{1,0:T(8,128)(2,1)S(1)}, u32[]{:S(2)}, u32[]{:S(2)}) collective-permute-start(bf16[64,896]{1,0:T(8,128)(2,1)S(1)} %add_convert_fusion.6.rest_0_), channel_id=1, source_target_pairs={{0,1},{1,0},{2,3},{3,2},{4,5},{5,4},{6,7},{7,6},{8,9},{9,8},{10,11... | collective-permute-start | bytes 344072 | tf_op jit(solution)/shard_map/ppermute | solution.py:354
  51.5 9.2 %collective-permute-start.15 = (bf16[64,896]{1,0:T(8,128)(2,1)S(1)}, bf16[64,896]{1,0:T(8,128)(2,1)S(1)}, u32[]{:S(2)}, u32[]{:S(2)}) collective-permute-start(bf16[64,896]{1,0:T(8,128)(2,1)S(1)} %get-tuple-element.37), channel_id=1, source_target_pairs={{0,1},{1,0},{2,3},{3,2},{4,5},{5,4},{6,7},{7,6},{8,9},{9,8},{10,11... | collective-permute-start | bytes 344072 | tf_op jit(solution)/shard_map/ppermute | solution.py:354
  53.5 9.5 %collective-permute-start.18 = (bf16[64,896]{1,0:T(8,128)(2,1)S(1)}, bf16[64,896]{1,0:T(8,128)(2,1)S(1)}, u32[]{:S(2)}, u32[]{:S(2)}) collective-permute-start(bf16[64,896]{1,0:T(8,128)(2,1)S(1)} %get-tuple-element.38), channel_id=1, source_target_pairs={{0,1},{1,0},{2,3},{3,2},{4,5},{5,4},{6,7},{7,6},{8,9},{9,8},{10,11... | collective-permute-start | bytes 344072 | tf_op jit(solution)/shard_map/ppermute | solution.py:354
  56.4 15.9 %collective-permute-start.14 = (bf16[64,896]{1,0:T(8,128)(2,1)S(1)}, bf16[64,896]{1,0:T(8,128)(2,1)S(1)}, u32[]{:S(2)}, u32[]{:S(2)}) collective-permute-start(bf16[64,896]{1,0:T(8,128)(2,1)S(1)} %add_convert_fusion.4.rest_2_), channel_id=1, source_target_pairs={{0,1},{1,0},{2,3},{3,2},{4,5},{5,4},{6,7},{7,6},{8,9},{9,8},{10,11... | collective-permute-start | bytes 344072 | tf_op jit(solution)/shard_map/ppermute | solution.py:354
  60.7 8.0 %collective-permute-start.16 = (bf16[64,896]{1,0:T(8,128)(2,1)S(1)}, bf16[64,896]{1,0:T(8,128)(2,1)S(1)}, u32[]{:S(2)}, u32[]{:S(2)}) collective-permute-start(bf16[64,896]{1,0:T(8,128)(2,1)S(1)} %add_convert_fusion.3), channel_id=1, source_target_pairs={{0,3},{1,2},{2,1},{3,0},{4,7},{5,6},{6,5},{7,4},{8,11},{9,10},{10,... | collective-permute-start | bytes 344072 | tf_op jit(solution)/shard_map/ppermute | solution.py:354
  63.1 8.0 %collective-permute-start.19 = (bf16[64,896]{1,0:T(8,128)(2,1)S(1)}, bf16[64,896]{1,0:T(8,128)(2,1)S(1)}, u32[]{:S(2)}, u32[]{:S(2)}) collective-permute-start(bf16[64,896]{1,0:T(8,128)(2,1)S(1)} %add_convert_fusion.1), channel_id=1, source_target_pairs={{0,3},{1,2},{2,1},{3,0},{4,7},{5,6},{6,5},{7,4},{8,11},{9,10},{10,... | collective-permute-start | bytes 344072 | tf_op jit(solution)/shard_map/ppermute | solution.py:354
  68.8 4.9 %collective-permute-start.17 = (bf16[64,896]{1,0:T(8,128)(2,1)S(1)}, bf16[64,896]{1,0:T(8,128)(2,1)S(1)}, u32[]{:S(2)}, u32[]{:S(2)}) collective-permute-start(bf16[64,896]{1,0:T(8,128)(2,1)S(1)} %add_convert_fusion.2.rest_4_), channel_id=1, source_target_pairs={{0,1},{1,0},{2,3},{3,2},{4,5},{5,4},{6,7},{7,6},{8,9},{9,8},{10,11... | collective-permute-start | bytes 344072 | tf_op jit(solution)/shard_map/ppermute | solution.py:354
  71.0 4.9 %collective-permute-start.20 = (bf16[64,896]{1,0:T(8,128)(2,1)S(1)}, bf16[64,896]{1,0:T(8,128)(2,1)S(1)}, u32[]{:S(2)}, u32[]{:S(2)}) collective-permute-start(bf16[64,896]{1,0:T(8,128)(2,1)S(1)} %add_convert_fusion.rest_6_), channel_id=1, source_target_pairs={{0,1},{1,0},{2,3},{3,2},{4,5},{5,4},{6,7},{7,6},{8,9},{9,8},{10,11... | collective-permute-start | bytes 344072 | tf_op jit(solution)/shard_map/ppermute | solution.py:354

commit v7 on v6

--- a/solution.py
+++ b/solution.py
@@ -424,7 +424,7 @@
                 pltpu.VMEM((slots, rows, LANES), jnp.float32),
                 pltpu.VMEM((slots * rows, LATENT), jnp.bfloat16),
             ],
-            compiler_params=limit(18),
+            compiler_params=limit(14),
             cost_estimate=cost(8),
             name="attend",
         )(me, decode_rows, lengths, *received, cache, key_up, value_up)
@@ -462,7 +462,7 @@
             in_specs=[smem()] + [vmem()] * 5,
             out_specs=[vmem()] * 2,
             scratch_shapes=[pltpu.VMEM((4 * part_rows, out_proj.shape[0]), jnp.bfloat16)],
-            compiler_params=limit(24),
+            compiler_params=limit(10),
             cost_estimate=cost(2),
             name="project_out",
         )(z, *parts, out_proj)
@@ -475,9 +475,7 @@
     near = [near_rows, flip(near_rows, "seq", 1), near_across, flip(near_across, "seq", 1)]
     far_across = flip(far_rows, "seq", 2)
     first, second = project(near, 0), project(near, 1)
-    relayed, _ = lax.optimization_barrier((far_across, second[0]))
-    far = [far_rows, flip(far_rows, "seq", 1), far_across, flip(relayed, "seq", 1)]
-    third, fourth = project(far, 0), project(far, 1)
+    far = [far_rows, flip(far_rows, "seq", 1), far_across, flip(far_across, "seq", 1)]
 
     def swap(piece):
         return flip(piece[1], "head", 1)
@@ -485,10 +483,13 @@
     first_in, second_in = swap(first), swap(second)
     first_pair = add(first[0], first_in)
     first_cross = flip(first_pair, "head", 3)
-    third_in, fourth_in = swap(third), swap(fourth)
-    second_in, _ = lax.optimization_barrier((second_in, third[0]))
     second_pair = add(second[0], second_in)
     second_cross = flip(second_pair, "head", 3)
+
+    third = project(far, 0)
+    third_in = swap(third)
+    fourth = project(far, 1)
+    fourth_in = swap(fourth)
     first_cross, _ = lax.optimization_barrier((first_cross, fourth[0]))
     first_sum = add(first_pair, first_cross)
     first_other = flip(first_sum, "head", 1)

time: 77.9 us -> 76.2 us (0.978); the launches traced: 77.7 us -> 76.9 us
  waiting for transfers between devices: 20.6 us -> 15.7 us
  starting transfers between devices: 25.3 us -> 28.2 us
  Pallas kernels: 25.2 us -> 26.5 us
    ppermute x21, waiting for transfers between devices: 20.6 us -> 15.7 us  [flip(): return lax.ppermute(x, axis, [(i, i ^ distance) for i in range(size)])]
    ppermute x21, starting transfers between devices: 25.3 us -> 28.2 us  [flip(): return lax.ppermute(x, axis, [(i, i ^ distance) for i in range(size)])]
    pallas_call x2, Pallas kernels: 15.6 us -> 16.9 us  [attend(): pl.pallas_call(functools.partial(attend_kernel, sizes, scale, relative, b...]
  transfers between devices with their start and end apart: 21 -> 21, of which waited for: 10 -> 9; matrix products, arithmetic and copies ran while one was open for 0% -> 0% of each run, Pallas kernels for 27% -> 29%
where the time goes in v7:
time: 76.2 us; the launch traced here: 76.9 us
  starting transfers between devices  28.2 us (37%)
  Pallas kernels  26.5 us (35%)
  waiting for transfers between devices  15.7 us (21%)
  local copies, waits for them, and re-layouts  5.99 us (8%)
    ppermute x21, starting transfers between devices, flip(): return lax.ppermute(x, axis, [(i, i ^ distance) for i in range(size)])  28.2 us
    pallas_call x2, Pallas kernels, attend(): pl.pallas_call(functools.partial(attend_kernel, sizes, scale, relative, b...  16.9 us
    ppermute x21, waiting for transfers between devices, flip(): return lax.ppermute(x, axis, [(i, i ^ distance) for i in range(size)])  15.7 us
    unnamed x30, local copies, waits for them, and re-layouts  5.99 us
    pallas_call x4, Pallas kernels, project(): pl.pallas_call(functools.partial(project_kernel, piece * cols), out_shape...  5.68 us
    pallas_call x1, Pallas kernels, order(): pl.pallas_call(kernel, out_shape=jax.ShapeDtypeStruct((steps, sources * r...  1.75 us
  transfers between devices with their start and end apart: 21, of which 9 were waited for; matrix products, arithmetic and copies ran while one was open for 0% of the time, Pallas kernels for 29%

profile of v7, /device:TPU:0, one launch (start us, length us, event | category | flops | bytes accessed | tf_op | source)
XLA Modules:
  0.0 76.9 jit_solution(5140238923305136873)
XLA Ops:
  0.0 0.7 copy-done.7
  0.8 1.1 %place_rows.1.after_ref.pick_ref = bf16[4,64,256]{2,1,0:T(8,128)(2,1)S(1)} custom-call(s32[1]{0:T(128)} %bitcast.1.me_ref, s32[64]{0:T(128)S(1)} %copy-done.7), custom_call_target="tpu_custom_call" | custom-call | flops 2000000000 | bytes 6000000 | tf_op jit(solution)/shard_map/place_rows/pallas_call | solution.py:379
  1.9 0.0 slice-start.5
  1.9 0.0 copy-start.1
  1.9 0.0 copy-start.2
  1.9 0.0 copy-start.6
  1.9 0.0 copy-start.8
  1.9 1.1 %pack_queries.1 = (bf16[1,848,128]{2,1,0:T(8,128)(2,1)S(1)}, bf16[1,848,128]{2,1,0:T(8,128)(2,1)S(1)}, bf16[1,848,128]{2,1,0:T(8,128)(2,1)S(1)}, bf16[1,848,128]{2,1,0:T(8,128)(2,1)S(1)}) custom-call(s32[1]{0:T(128)} %bitcast.1.me_ref, s32[64]{0:T(128)S(1)} %copy-done.7, bf16[4,16,32,128]{3,2,1,0:T(8,128)(2,1)S(1)} %copy-done.3, ...), custom_call_target="tpu_custom_call" | custom-call | flops 6000000000 | bytes 18000000 | tf_op jit(solution)/shard_map/pack_queries/pallas_call | solution.py:391
  3.1 0.5 collective-permute-start
  3.6 2.6 %collective-permute-start.3 = (bf16[1,848,128]{2,1,0:T(8,128)(2,1)S(1)}, bf16[1,848,128]{2,1,0:T(8,128)(2,1)S(1)}, u32[]{:S(2)}, u32[]{:S(2)}) collective-permute-start(bf16[1,848,128]{2,1,0:T(8,128)(2,1)S(1)} %get-tuple-element.22), channel_id=1, source_target_pairs={{0,8},{4,12},{8,0},{12,4},{1,9},{5,13},{9,1},{13,5},{2,10},{6,14},... | collective-permute-start | bytes 651272 | tf_op jit(solution)/shard_map/ppermute | solution.py:354
  6.2 0.1 collective-permute-start.4
  6.3 0.0 collective-permute-done.rest_1_
  6.3 8.4 %attend.2.rest_0_ = bf16[32,4096]{1,0:T(8,128)(2,1)S(1)} custom-call(s32[1]{0:T(128)} %bitcast.1.me_ref, s32[64]{0:T(128)S(1)} %copy-done.8, s32[4,16]{1,0:T(4,128)S(1)} %copy-done.6, bf16[1,848,128]{2,1,0:T(8,128)(2,1)S(1)} %get-tuple-element.20.rest_0_, bf16[1,848,128]{2,1,0:T(8,128)(2,1)S(1)} %collective-permute-done.rest_1_, ...), custom_call_target="tpu_custom_call" | custom-call | flops 8000000000 | bytes 24000000 | tf_op jit(solution)/shard_map/attend/pallas_call | solution.py:409
  14.8 3.7 %collective-permute-start.2 = (bf16[32,4096]{1,0:T(8,128)(2,1)S(1)}, bf16[32,4096]{1,0:T(8,128)(2,1)S(1)}, u32[]{:S(2)}, u32[]{:S(2)}) collective-permute-start(bf16[32,4096]{1,0:T(8,128)(2,1)S(1)} %attend.2.rest_0_), channel_id=1, source_target_pairs={{0,8},{4,12},{8,0},{12,4},{1,9},{5,13},{9,1},{13,5},{2,10},{6,14},... | collective-permute-start | bytes 786440 | tf_op jit(solution)/shard_map/ppermute | solution.py:354
  18.5 0.0 collective-permute-done.3.rest_0_
  18.5 0.0 collective-permute-done.4.rest_1_
  18.5 8.4 %attend.3.rest_0_ = bf16[32,4096]{1,0:T(8,128)(2,1)S(1)} custom-call(s32[1]{0:T(128)} %bitcast.1.me_ref, s32[64]{0:T(128)S(1)} %copy-done.8, s32[4,16]{1,0:T(4,128)S(1)} %copy-done.6, bf16[1,848,128]{2,1,0:T(8,128)(2,1)S(1)} %collective-permute-done.3.rest_0_, bf16[1,848,128]{2,1,0:T(8,128)(2,1)S(1)} %collective-permute-done.4.rest_1_, ...), custom_call_target="tpu_custom_call" | custom-call | flops 8000000000 | bytes 24000000 | tf_op jit(solution)/shard_map/attend/pallas_call | solution.py:409
  27.0 0.0 collective-permute-done.2.rest_2_
  27.0 0.6 collective-permute-start.5
  27.5 0.2 collective-permute-start.8
  27.7 1.0 %collective-permute-done.5.rest_3_ = bf16[32,4096]{1,0:T(8,128)(2,1)S(1)} collective-permute-done((bf16[32,4096]{1,0:T(8,128)(2,1)S(1)}, bf16[32,4096]{1,0:T(8,128)(2,1)S(1)}, u32[]{:S(2)}, u32[]{:S(2)}) %collective-permute-start.5) | collective-permute-done | bytes 262176 | tf_op jit(solution)/shard_map/ppermute | solution.py:354
  28.7 5.2 %copy-done = bf16[4096,1792]{1,0:T(8,128)(2,1)S(1)} copy-done((bf16[4096,1792]{1,0:T(8,128)(2,1)S(1)}, bf16[4096,1792]{1,0:T(8,128)(2,1)}, u32[]{:S(2)}) %copy-start) | copy-done | bytes 14680088
  33.9 1.4 %project_out.6 = (bf16[64,896]{1,0:T(8,128)(2,1)S(1)}, bf16[64,896]{1,0:T(8,128)(2,1)S(1)}) custom-call(s32[1]{0:T(128)} %bitcast.z_ref, bf16[32,4096]{1,0:T(8,128)(2,1)S(1)} %attend.2.rest_0_, bf16[32,4096]{1,0:T(8,128)(2,1)S(1)} %collective-permute-done.1.rest_1_, bf16[32,4096]{1,0:T(8,128)(2,1)S(1)} %collective-permute-done.2.rest_2_, ...), custom_call_target="tpu_custom_call" | custom-call | flops 2000000000 | bytes 6000000 | tf_op jit(solution)/shard_map/project_out/pallas_call | solution.py:459
  35.3 0.0 slice-start.2
  35.3 1.7 %collective-permute-start.12 = (bf16[64,896]{1,0:T(8,128)(2,1)S(1)}, bf16[64,896]{1,0:T(8,128)(2,1)S(1)}, u32[]{:S(2)}, u32[]{:S(2)}) collective-permute-start(bf16[64,896]{1,0:T(8,128)(2,1)S(1)} %get-tuple-element.31), channel_id=1, source_target_pairs={{0,1},{1,0},{2,3},{3,2},{4,5},{5,4},{6,7},{7,6},{8,9},{9,8},{10,11... | collective-permute-start | bytes 344072 | tf_op jit(solution)/shard_map/ppermute | solution.py:354
  36.9 1.4 %project_out.4 = (bf16[64,896]{1,0:T(8,128)(2,1)S(1)}, bf16[64,896]{1,0:T(8,128)(2,1)S(1)}) custom-call(s32[1]{0:T(128)} %bitcast.z_ref, bf16[32,4096]{1,0:T(8,128)(2,1)S(1)} %attend.2.rest_0_, bf16[32,4096]{1,0:T(8,128)(2,1)S(1)} %collective-permute-done.1.rest_1_, bf16[32,4096]{1,0:T(8,128)(2,1)S(1)} %collective-permute-done.2.rest_2_, ...), custom_call_target="tpu_custom_call" | custom-call | flops 2000000000 | bytes 6000000 | tf_op jit(solution)/shard_map/project_out/pallas_call | solution.py:459
  38.3 0.5 collective-permute-start.6
  38.8 1.9 %collective-permute-done.12 = bf16[64,896]{1,0:T(8,128)(2,1)S(1)} collective-permute-done((bf16[64,896]{1,0:T(8,128)(2,1)S(1)}, bf16[64,896]{1,0:T(8,128)(2,1)S(1)}, u32[]{:S(2)}, u32[]{:S(2)}) %collective-permute-start.12) | collective-permute-done | bytes 114720 | tf_op jit(solution)/shard_map/ppermute | solution.py:354
  40.8 4.2 %collective-permute-start.13 = (bf16[64,896]{1,0:T(8,128)(2,1)S(1)}, bf16[64,896]{1,0:T(8,128)(2,1)S(1)}, u32[]{:S(2)}, u32[]{:S(2)}) collective-permute-start(bf16[64,896]{1,0:T(8,128)(2,1)S(1)} %add_convert_fusion.5), channel_id=1, source_target_pairs={{0,3},{1,2},{2,1},{3,0},{4,7},{5,6},{6,5},{7,4},{8,11},{9,10},{10,... | collective-permute-start | bytes 344072 | tf_op jit(solution)/shard_map/ppermute | solution.py:354
  45.1 1.9 %collective-permute-start.7 = (bf16[64,896]{1,0:T(8,128)(2,1)S(1)}, bf16[64,896]{1,0:T(8,128)(2,1)S(1)}, u32[]{:S(2)}, u32[]{:S(2)}) collective-permute-start(bf16[64,896]{1,0:T(8,128)(2,1)S(1)} %add_convert_fusion.7), channel_id=1, source_target_pairs={{0,3},{1,2},{2,1},{3,0},{4,7},{5,6},{6,5},{7,4},{8,11},{9,10},{10,... | collective-permute-start | bytes 344072 | tf_op jit(solution)/shard_map/ppermute | solution.py:354
  46.9 1.3 %collective-permute-done.13 = bf16[64,896]{1,0:T(8,128)(2,1)S(1)} collective-permute-done((bf16[64,896]{1,0:T(8,128)(2,1)S(1)}, bf16[64,896]{1,0:T(8,128)(2,1)S(1)}, u32[]{:S(2)}, u32[]{:S(2)}) %collective-permute-start.13) | collective-permute-done | bytes 114720 | tf_op jit(solution)/shard_map/ppermute | solution.py:354
  48.2 4.9 %collective-permute-start.14 = (bf16[64,896]{1,0:T(8,128)(2,1)S(1)}, bf16[64,896]{1,0:T(8,128)(2,1)S(1)}, u32[]{:S(2)}, u32[]{:S(2)}) collective-permute-start(bf16[64,896]{1,0:T(8,128)(2,1)S(1)} %add_convert_fusion.4.rest_2_), channel_id=1, source_target_pairs={{0,1},{1,0},{2,3},{3,2},{4,5},{5,4},{6,7},{7,6},{8,9},{9,8},{10,11... | collective-permute-start | bytes 344072 | tf_op jit(solution)/shard_map/ppermute | solution.py:354
  53.2 1.6 %project_out.5 = (bf16[64,896]{1,0:T(8,128)(2,1)S(1)}, bf16[64,896]{1,0:T(8,128)(2,1)S(1)}) custom-call(s32[1]{0:T(128)} %bitcast.z_ref, bf16[32,4096]{1,0:T(8,128)(2,1)S(1)} %attend.3.rest_0_, bf16[32,4096]{1,0:T(8,128)(2,1)S(1)} %collective-permute-done.8.rest_1_, bf16[32,4096]{1,0:T(8,128)(2,1)S(1)} %collective-permute-done.9.rest_2_, ...), custom_call_target="tpu_custom_call" | custom-call | flops 2000000000 | bytes 6000000 | tf_op jit(solution)/shard_map/project_out/pallas_call | solution.py:459
  54.7 0.1 collective-permute-start.18
  54.8 1.4 %project_out.7 = (bf16[64,896]{1,0:T(8,128)(2,1)S(1)}, bf16[64,896]{1,0:T(8,128)(2,1)S(1)}) custom-call(s32[1]{0:T(128)} %bitcast.z_ref, bf16[32,4096]{1,0:T(8,128)(2,1)S(1)} %attend.3.rest_0_, bf16[32,4096]{1,0:T(8,128)(2,1)S(1)} %collective-permute-done.8.rest_1_, bf16[32,4096]{1,0:T(8,128)(2,1)S(1)} %collective-permute-done.9.rest_2_, ...), custom_call_target="tpu_custom_call" | custom-call | flops 2000000000 | bytes 6000000 | tf_op jit(solution)/shard_map/project_out/pallas_call | solution.py:459
  56.2 2.1 %collective-permute-start.15 = (bf16[64,896]{1,0:T(8,128)(2,1)S(1)}, bf16[64,896]{1,0:T(8,128)(2,1)S(1)}, u32[]{:S(2)}, u32[]{:S(2)}) collective-permute-start(bf16[64,896]{1,0:T(8,128)(2,1)S(1)} %get-tuple-element.33), channel_id=1, source_target_pairs={{0,1},{1,0},{2,3},{3,2},{4,5},{5,4},{6,7},{7,6},{8,9},{9,8},{10,11... | collective-permute-start | bytes 344072 | tf_op jit(solution)/shard_map/ppermute | solution.py:354
  58.3 0.1 collective-permute-start.11
  58.4 1.2 %collective-permute-done.18 = bf16[64,896]{1,0:T(8,128)(2,1)S(1)} collective-permute-done((bf16[64,896]{1,0:T(8,128)(2,1)S(1)}, bf16[64,896]{1,0:T(8,128)(2,1)S(1)}, u32[]{:S(2)}, u32[]{:S(2)}) %collective-permute-start.18) | collective-permute-done | bytes 114720 | tf_op jit(solution)/shard_map/ppermute | solution.py:354
  59.6 2.7 %collective-permute-start.19 = (bf16[64,896]{1,0:T(8,128)(2,1)S(1)}, bf16[64,896]{1,0:T(8,128)(2,1)S(1)}, u32[]{:S(2)}, u32[]{:S(2)}) collective-permute-start(bf16[64,896]{1,0:T(8,128)(2,1)S(1)} %add_convert_fusion.1), channel_id=1, source_target_pairs={{0,3},{1,2},{2,1},{3,0},{4,7},{5,6},{6,5},{7,4},{8,11},{9,10},{10,... | collective-permute-start | bytes 344072 | tf_op jit(solution)/shard_map/ppermute | solution.py:354
  62.3 0.8 collective-permute-done.15
  63.1 1.6 %collective-permute-start.16 = (bf16[64,896]{1,0:T(8,128)(2,1)S(1)}, bf16[64,896]{1,0:T(8,128)(2,1)S(1)}, u32[]{:S(2)}, u32[]{:S(2)}) collective-permute-start(bf16[64,896]{1,0:T(8,128)(2,1)S(1)} %add_convert_fusion.3), channel_id=1, source_target_pairs={{0,3},{1,2},{2,1},{3,0},{4,7},{5,6},{6,5},{7,4},{8,11},{9,10},{10,... | collective-permute-start | bytes 344072 | tf_op jit(solution)/shard_map/ppermute | solution.py:354
  64.7 3.9 %collective-permute-done.19 = bf16[64,896]{1,0:T(8,128)(2,1)S(1)} collective-permute-done((bf16[64,896]{1,0:T(8,128)(2,1)S(1)}, bf16[64,896]{1,0:T(8,128)(2,1)S(1)}, u32[]{:S(2)}, u32[]{:S(2)}) %collective-permute-start.19) | collective-permute-done | bytes 114720 | tf_op jit(solution)/shard_map/ppermute | solution.py:354
  68.7 0.1 collective-permute-start.20
  68.8 1.5 %collective-permute-done.16 = bf16[64,896]{1,0:T(8,128)(2,1)S(1)} collective-permute-done((bf16[64,896]{1,0:T(8,128)(2,1)S(1)}, bf16[64,896]{1,0:T(8,128)(2,1)S(1)}, u32[]{:S(2)}, u32[]{:S(2)}) %collective-permute-start.16) | collective-permute-done | bytes 114720 | tf_op jit(solution)/shard_map/ppermute | solution.py:354
  70.3 0.8 %collective-permute-start.17 = (bf16[64,896]{1,0:T(8,128)(2,1)S(1)}, bf16[64,896]{1,0:T(8,128)(2,1)S(1)}, u32[]{:S(2)}, u32[]{:S(2)}) collective-permute-start(bf16[64,896]{1,0:T(8,128)(2,1)S(1)} %add_convert_fusion.2.rest_4_), channel_id=1, source_target_pairs={{0,1},{1,0},{2,3},{3,2},{4,5},{5,4},{6,7},{7,6},{8,9},{9,8},{10,11... | collective-permute-start | bytes 344072 | tf_op jit(solution)/shard_map/ppermute | solution.py:354
  71.1 2.4 %collective-permute-done.20.rest_7_ = bf16[64,896]{1,0:T(8,128)(2,1)S(1)} collective-permute-done((bf16[64,896]{1,0:T(8,128)(2,1)S(1)}, bf16[64,896]{1,0:T(8,128)(2,1)S(1)}, u32[]{:S(2)}, u32[]{:S(2)}) %collective-permute-start.20) | collective-permute-done | bytes 114720 | tf_op jit(solution)/shard_map/ppermute | solution.py:354
  73.6 1.6 %collective-permute-done.17.rest_5_ = bf16[64,896]{1,0:T(8,128)(2,1)S(1)} collective-permute-done((bf16[64,896]{1,0:T(8,128)(2,1)S(1)}, bf16[64,896]{1,0:T(8,128)(2,1)S(1)}, u32[]{:S(2)}, u32[]{:S(2)}) %collective-permute-start.17) | collective-permute-done | bytes 114720 | tf_op jit(solution)/shard_map/ppermute | solution.py:354
  75.2 1.7 %order_rows.1 = bf16[4,64,1792]{2,1,0:T(8,128)(2,1)} custom-call(s32[1]{0:T(128)} %bitcast.z_ref, bf16[4,64,256]{2,1,0:T(8,128)(2,1)S(1)} %place_rows.1.after_ref.pick_ref, bf16[64,896]{1,0:T(8,128)(2,1)S(1)} %add_convert_fusion.6.rest_0_, bf16[64,896]{1,0:T(8,128)(2,1)S(1)} %collective-permute-done.11.rest_1_, ...), custom_call_target="tpu_custom_call" | custom-call | flops 2000000000 | bytes 6000000 | tf_op jit(solution)/shard_map/order_rows/pallas_call | solution.py:433
  (43 shorter events, 0.3 us)
Async XLA Ops:
  0.0 1.8 %copy-start.3 = (bf16[4,16,32,128]{3,2,1,0:T(8,128)(2,1)S(1)}, bf16[4,16,32,128]{3,2,1,0:T(8,128)(2,1)}, u32[]{:S(2)}) copy-start(bf16[4,16,32,128]{3,2,1,0:T(8,128)(2,1)} %nope_ref.1) | copy-start | bytes 1572868
  0.0 1.9 %copy-start.4 = (bf16[4,16,32,64]{3,2,1,0:T(8,128)(2,1)S(1)}, bf16[4,16,32,64]{3,2,1,0:T(8,128)(2,1)}, u32[]{:S(2)}) copy-start(bf16[4,16,32,64]{3,2,1,0:T(8,128)(2,1)} %rope_ref.1) | copy-start | bytes 786436
  0.0 1.9 %copy-start.5 = (bf16[4,16,576]{2,1,0:T(8,128)(2,1)S(1)}, bf16[4,16,576]{2,1,0:T(8,128)(2,1)}, u32[]{:S(2)}) copy-start(bf16[4,16,576]{2,1,0:T(8,128)(2,1)} %fresh_ref.1) | copy-start | bytes 221188
  0.0 0.7 copy-start.7
  0.8 5.5 %slice-start.4 = ((s8[4718592]{0:T(1024)(128)(4,1)}), s8[4194304]{0:T(1024)(128)(4,1)S(1)}, s32[]{:S(2)}) async-start(s8[4718592]{0:T(1024)(128)(4,1)} %bitcast.5), calls=%async_computation.4 | async-start | bytes 8388608
  1.9 4.4 %slice-start.5 = ((s8[4718592]{0:T(1024)(128)(4,1)}), s8[524288]{0:T(1024)(128)(4,1)S(1)}, s32[]{:S(2)}) async-start(s8[4718592]{0:T(1024)(128)(4,1)} %bitcast.5), calls=%async_computation.5 | async-start | bytes 1048576
  1.9 4.4 %copy-start.1 = (bf16[32,128,512]{2,1,0:T(8,128)(2,1)S(1)}, bf16[32,128,512]{2,1,0:T(8,128)(2,1)}, u32[]{:S(2)}) copy-start(bf16[32,128,512]{2,1,0:T(8,128)(2,1)} %rest_3_.3) | copy-start | bytes 12582916
  1.9 4.4 %copy-start.2 = (bf16[32,512,128]{2,1,0:T(8,128)(2,1)S(1)}, bf16[32,512,128]{2,1,0:T(8,128)(2,1)}, u32[]{:S(2)}) copy-start(bf16[32,512,128]{2,1,0:T(8,128)(2,1)} %rest_4_.7) | copy-start | bytes 12582916
  1.9 4.4 %copy-start.6 = (s32[4,16]{1,0:T(4,128)S(1)}, s32[4,16]{1,0:T(4,128)}, u32[]{:S(2)}) copy-start(s32[4,16]{1,0:T(4,128)} %length_ref.3) | copy-start | bytes 772
  1.9 4.4 %copy-start.8 = (s32[64]{0:T(128)S(1)}, s32[64]{0:T(128)}, u32[]{:S(2)}) copy-start(s32[64]{0:T(128)} %decode_ref.7) | copy-start | bytes 772
  3.1 3.2 %collective-permute-start = (bf16[1,848,128]{2,1,0:T(8,128)(2,1)S(1)}, bf16[1,848,128]{2,1,0:T(8,128)(2,1)S(1)}, u32[]{:S(2)}, u32[]{:S(2)}) collective-permute-start(bf16[1,848,128]{2,1,0:T(8,128)(2,1)S(1)} %get-tuple-element.21), channel_id=1, source_target_pairs={{0,4},{4,0},{8,12},{12,8},{1,5},{5,1},{9,13},{13,9},{2,6},{6,2},{1... | collective-permute-start | bytes 651272 | tf_op jit(solution)/shard_map/ppermute | solution.py:354
  3.6 14.9 %collective-permute-start.3 = (bf16[1,848,128]{2,1,0:T(8,128)(2,1)S(1)}, bf16[1,848,128]{2,1,0:T(8,128)(2,1)S(1)}, u32[]{:S(2)}, u32[]{:S(2)}) collective-permute-start(bf16[1,848,128]{2,1,0:T(8,128)(2,1)S(1)} %get-tuple-element.22), channel_id=1, source_target_pairs={{0,8},{4,12},{8,0},{12,4},{1,9},{5,13},{9,1},{13,5},{2,10},{6,14},... | collective-permute-start | bytes 651272 | tf_op jit(solution)/shard_map/ppermute | solution.py:354
  6.2 12.3 %collective-permute-start.4 = (bf16[1,848,128]{2,1,0:T(8,128)(2,1)S(1)}, bf16[1,848,128]{2,1,0:T(8,128)(2,1)S(1)}, u32[]{:S(2)}, u32[]{:S(2)}) collective-permute-start(bf16[1,848,128]{2,1,0:T(8,128)(2,1)S(1)} %get-tuple-element.23), channel_id=1, source_target_pairs={{0,12},{4,8},{8,4},{12,0},{1,13},{5,9},{9,5},{13,1},{2,14},{6,10},... | collective-permute-start | bytes 651272 | tf_op jit(solution)/shard_map/ppermute | solution.py:354
  14.8 12.2 %collective-permute-start.2 = (bf16[32,4096]{1,0:T(8,128)(2,1)S(1)}, bf16[32,4096]{1,0:T(8,128)(2,1)S(1)}, u32[]{:S(2)}, u32[]{:S(2)}) collective-permute-start(bf16[32,4096]{1,0:T(8,128)(2,1)S(1)} %attend.2.rest_0_), channel_id=1, source_target_pairs={{0,8},{4,12},{8,0},{12,4},{1,9},{5,13},{9,1},{13,5},{2,10},{6,14},... | collective-permute-start | bytes 786440 | tf_op jit(solution)/shard_map/ppermute | solution.py:354
  18.5 9.2 %collective-permute-start.1 = (bf16[32,4096]{1,0:T(8,128)(2,1)S(1)}, bf16[32,4096]{1,0:T(8,128)(2,1)S(1)}, u32[]{:S(2)}, u32[]{:S(2)}) collective-permute-start(bf16[32,4096]{1,0:T(8,128)(2,1)S(1)} %attend.2.rest_0_), channel_id=1, source_target_pairs={{0,4},{4,0},{8,12},{12,8},{1,5},{5,1},{9,13},{13,9},{2,6},{6,2},{1... | collective-permute-start | bytes 786440 | tf_op jit(solution)/shard_map/ppermute | solution.py:354
  27.0 1.7 %collective-permute-start.5 = (bf16[32,4096]{1,0:T(8,128)(2,1)S(1)}, bf16[32,4096]{1,0:T(8,128)(2,1)S(1)}, u32[]{:S(2)}, u32[]{:S(2)}) collective-permute-start(bf16[32,4096]{1,0:T(8,128)(2,1)S(1)} %collective-permute-done.2.rest_2_), channel_id=1, source_target_pairs={{0,4},{4,0},{8,12},{12,8},{1,5},{5,1},{9,13},{13,9},{2,6},{6,2},{1... | collective-permute-start | bytes 786440 | tf_op jit(solution)/shard_map/ppermute | solution.py:354
  27.5 11.3 %collective-permute-start.9 = (bf16[32,4096]{1,0:T(8,128)(2,1)S(1)}, bf16[32,4096]{1,0:T(8,128)(2,1)S(1)}, u32[]{:S(2)}, u32[]{:S(2)}) collective-permute-start(bf16[32,4096]{1,0:T(8,128)(2,1)S(1)} %attend.3.rest_0_), channel_id=1, source_target_pairs={{0,8},{4,12},{8,0},{12,4},{1,9},{5,13},{9,1},{13,5},{2,10},{6,14},... | collective-permute-start | bytes 786440 | tf_op jit(solution)/shard_map/ppermute | solution.py:354
  27.5 25.6 %collective-permute-start.8 = (bf16[32,4096]{1,0:T(8,128)(2,1)S(1)}, bf16[32,4096]{1,0:T(8,128)(2,1)S(1)}, u32[]{:S(2)}, u32[]{:S(2)}) collective-permute-start(bf16[32,4096]{1,0:T(8,128)(2,1)S(1)} %attend.3.rest_0_), channel_id=1, source_target_pairs={{0,4},{4,0},{8,12},{12,8},{1,5},{5,1},{9,13},{13,9},{2,6},{6,2},{1... | collective-permute-start | bytes 786440 | tf_op jit(solution)/shard_map/ppermute | solution.py:354
  28.7 5.2 %copy-start = (bf16[4096,1792]{1,0:T(8,128)(2,1)S(1)}, bf16[4096,1792]{1,0:T(8,128)(2,1)}, u32[]{:S(2)}) copy-start(bf16[4096,1792]{1,0:T(8,128)(2,1)} %rest_4_.11) | copy-start | bytes 44040196
  33.9 19.2 %slice-start = ((s8[14680064]{0:T(1024)(128)(4,1)}), s8[4194304]{0:T(1024)(128)(4,1)S(1)}, s32[]{:S(2)}) async-start(s8[14680064]{0:T(1024)(128)(4,1)} %bitcast.3), calls=%async_computation | async-start | bytes 8388608
  33.9 19.2 %slice-start.1 = ((s8[14680064]{0:T(1024)(128)(4,1)}), s8[4194304]{0:T(1024)(128)(4,1)S(1)}, s32[]{:S(2)}) async-start(s8[14680064]{0:T(1024)(128)(4,1)} %bitcast.3), calls=%async_computation.1 | async-start | bytes 8388608
  35.3 17.9 %slice-start.2 = ((s8[14680064]{0:T(1024)(128)(4,1)}), s8[4194304]{0:T(1024)(128)(4,1)S(1)}, s32[]{:S(2)}) async-start(s8[14680064]{0:T(1024)(128)(4,1)} %bitcast.3), calls=%async_computation.2 | async-start | bytes 8388608
  35.3 17.9 %slice-start.3 = ((s8[14680064]{0:T(1024)(128)(4,1)}), s8[2097152]{0:T(1024)(128)(4,1)S(1)}, s32[]{:S(2)}) async-start(s8[14680064]{0:T(1024)(128)(4,1)} %bitcast.3), calls=%async_computation.3 | async-start | bytes 4194304
  35.3 5.5 %collective-permute-start.12 = (bf16[64,896]{1,0:T(8,128)(2,1)S(1)}, bf16[64,896]{1,0:T(8,128)(2,1)S(1)}, u32[]{:S(2)}, u32[]{:S(2)}) collective-permute-start(bf16[64,896]{1,0:T(8,128)(2,1)S(1)} %get-tuple-element.31), channel_id=1, source_target_pairs={{0,1},{1,0},{2,3},{3,2},{4,5},{5,4},{6,7},{7,6},{8,9},{9,8},{10,11... | collective-permute-start | bytes 344072 | tf_op jit(solution)/shard_map/ppermute | solution.py:354
  38.3 6.7 %collective-permute-start.6 = (bf16[64,896]{1,0:T(8,128)(2,1)S(1)}, bf16[64,896]{1,0:T(8,128)(2,1)S(1)}, u32[]{:S(2)}, u32[]{:S(2)}) collective-permute-start(bf16[64,896]{1,0:T(8,128)(2,1)S(1)} %get-tuple-element.26), channel_id=1, source_target_pairs={{0,1},{1,0},{2,3},{3,2},{4,5},{5,4},{6,7},{7,6},{8,9},{9,8},{10,11... | collective-permute-start | bytes 344072 | tf_op jit(solution)/shard_map/ppermute | solution.py:354
  38.8 14.3 %collective-permute-start.10 = (bf16[32,4096]{1,0:T(8,128)(2,1)S(1)}, bf16[32,4096]{1,0:T(8,128)(2,1)S(1)}, u32[]{:S(2)}, u32[]{:S(2)}) collective-permute-start(bf16[32,4096]{1,0:T(8,128)(2,1)S(1)} %collective-permute-done.9.rest_2_), channel_id=1, source_target_pairs={{0,4},{4,0},{8,12},{12,8},{1,5},{5,1},{9,13},{13,9},{2,6},{6,2},{1... | collective-permute-start | bytes 786440 | tf_op jit(solution)/shard_map/ppermute | solution.py:354
  40.8 7.4 %collective-permute-start.13 = (bf16[64,896]{1,0:T(8,128)(2,1)S(1)}, bf16[64,896]{1,0:T(8,128)(2,1)S(1)}, u32[]{:S(2)}, u32[]{:S(2)}) collective-permute-start(bf16[64,896]{1,0:T(8,128)(2,1)S(1)} %add_convert_fusion.5), channel_id=1, source_target_pairs={{0,3},{1,2},{2,1},{3,0},{4,7},{5,6},{6,5},{7,4},{8,11},{9,10},{10,... | collective-permute-start | bytes 344072 | tf_op jit(solution)/shard_map/ppermute | solution.py:354
  45.1 13.2 %collective-permute-start.7 = (bf16[64,896]{1,0:T(8,128)(2,1)S(1)}, bf16[64,896]{1,0:T(8,128)(2,1)S(1)}, u32[]{:S(2)}, u32[]{:S(2)}) collective-permute-start(bf16[64,896]{1,0:T(8,128)(2,1)S(1)} %add_convert_fusion.7), channel_id=1, source_target_pairs={{0,3},{1,2},{2,1},{3,0},{4,7},{5,6},{6,5},{7,4},{8,11},{9,10},{10,... | collective-permute-start | bytes 344072 | tf_op jit(solution)/shard_map/ppermute | solution.py:354
  48.2 22.9 %collective-permute-start.14 = (bf16[64,896]{1,0:T(8,128)(2,1)S(1)}, bf16[64,896]{1,0:T(8,128)(2,1)S(1)}, u32[]{:S(2)}, u32[]{:S(2)}) collective-permute-start(bf16[64,896]{1,0:T(8,128)(2,1)S(1)} %add_convert_fusion.4.rest_2_), channel_id=1, source_target_pairs={{0,1},{1,0},{2,3},{3,2},{4,5},{5,4},{6,7},{7,6},{8,9},{9,8},{10,11... | collective-permute-start | bytes 344072 | tf_op jit(solution)/shard_map/ppermute | solution.py:354
  54.7 4.9 %collective-permute-start.18 = (bf16[64,896]{1,0:T(8,128)(2,1)S(1)}, bf16[64,896]{1,0:T(8,128)(2,1)S(1)}, u32[]{:S(2)}, u32[]{:S(2)}) collective-permute-start(bf16[64,896]{1,0:T(8,128)(2,1)S(1)} %get-tuple-element.34), channel_id=1, source_target_pairs={{0,1},{1,0},{2,3},{3,2},{4,5},{5,4},{6,7},{7,6},{8,9},{9,8},{10,11... | collective-permute-start | bytes 344072 | tf_op jit(solution)/shard_map/ppermute | solution.py:354
  56.2 6.9 %collective-permute-start.15 = (bf16[64,896]{1,0:T(8,128)(2,1)S(1)}, bf16[64,896]{1,0:T(8,128)(2,1)S(1)}, u32[]{:S(2)}, u32[]{:S(2)}) collective-permute-start(bf16[64,896]{1,0:T(8,128)(2,1)S(1)} %get-tuple-element.33), channel_id=1, source_target_pairs={{0,1},{1,0},{2,3},{3,2},{4,5},{5,4},{6,7},{7,6},{8,9},{9,8},{10,11... | collective-permute-start | bytes 344072 | tf_op jit(solution)/shard_map/ppermute | solution.py:354
  58.3 12.8 %collective-permute-start.11 = (bf16[64,896]{1,0:T(8,128)(2,1)S(1)}, bf16[64,896]{1,0:T(8,128)(2,1)S(1)}, u32[]{:S(2)}, u32[]{:S(2)}) collective-permute-start(bf16[64,896]{1,0:T(8,128)(2,1)S(1)} %add_convert_fusion.6.rest_0_), channel_id=1, source_target_pairs={{0,1},{1,0},{2,3},{3,2},{4,5},{5,4},{6,7},{7,6},{8,9},{9,8},{10,11... | collective-permute-start | bytes 344072 | tf_op jit(solution)/shard_map/ppermute | solution.py:354
  59.6 9.0 %collective-permute-start.19 = (bf16[64,896]{1,0:T(8,128)(2,1)S(1)}, bf16[64,896]{1,0:T(8,128)(2,1)S(1)}, u32[]{:S(2)}, u32[]{:S(2)}) collective-permute-start(bf16[64,896]{1,0:T(8,128)(2,1)S(1)} %add_convert_fusion.1), channel_id=1, source_target_pairs={{0,3},{1,2},{2,1},{3,0},{4,7},{5,6},{6,5},{7,4},{8,11},{9,10},{10,... | collective-permute-start | bytes 344072 | tf_op jit(solution)/shard_map/ppermute | solution.py:354
  63.1 7.2 %collective-permute-start.16 = (bf16[64,896]{1,0:T(8,128)(2,1)S(1)}, bf16[64,896]{1,0:T(8,128)(2,1)S(1)}, u32[]{:S(2)}, u32[]{:S(2)}) collective-permute-start(bf16[64,896]{1,0:T(8,128)(2,1)S(1)} %add_convert_fusion.3), channel_id=1, source_target_pairs={{0,3},{1,2},{2,1},{3,0},{4,7},{5,6},{6,5},{7,4},{8,11},{9,10},{10,... | collective-permute-start | bytes 344072 | tf_op jit(solution)/shard_map/ppermute | solution.py:354
  68.7 4.9 %collective-permute-start.20 = (bf16[64,896]{1,0:T(8,128)(2,1)S(1)}, bf16[64,896]{1,0:T(8,128)(2,1)S(1)}, u32[]{:S(2)}, u32[]{:S(2)}) collective-permute-start(bf16[64,896]{1,0:T(8,128)(2,1)S(1)} %add_convert_fusion.rest_6_), channel_id=1, source_target_pairs={{0,1},{1,0},{2,3},{3,2},{4,5},{5,4},{6,7},{7,6},{8,9},{9,8},{10,11... | collective-permute-start | bytes 344072 | tf_op jit(solution)/shard_map/ppermute | solution.py:354
  70.3 4.9 %collective-permute-start.17 = (bf16[64,896]{1,0:T(8,128)(2,1)S(1)}, bf16[64,896]{1,0:T(8,128)(2,1)S(1)}, u32[]{:S(2)}, u32[]{:S(2)}) collective-permute-start(bf16[64,896]{1,0:T(8,128)(2,1)S(1)} %add_convert_fusion.2.rest_4_), channel_id=1, source_target_pairs={{0,1},{1,0},{2,3},{3,2},{4,5},{5,4},{6,7},{7,6},{8,9},{9,8},{10,11... | collective-permute-start | bytes 344072 | tf_op jit(solution)/shard_map/ppermute | solution.py:354

commit v8 on v7

--- a/solution.py
+++ b/solution.py
@@ -12,6 +12,7 @@
 LANES = 128
 LOG2E = 1.4426950408889634
 NEG = -1e30
+PLACES = 1024
 
 
 def own_slots(decode_ref, slot_ref, me, sources, requests, per_pair):
@@ -28,10 +29,10 @@
     lax.fori_loop(0, sources, one_source, jnp.int32(0))
 
 
-def pack_kernel(sizes, relative, me_ref, decode_ref, nope_ref, rope_ref, fresh_ref, after_ref, *rest):
+def pack_kernel(sizes, relative, ids_ref, decode_ref, nope_ref, rope_ref, fresh_ref, after_ref, *rest):
     sources, per_pair, steps, heads, requests, fresh_rows = sizes
     out_refs, (slots, wide) = rest[:-2], rest[-2:]
-    me = me_ref[0]
+    me = ids_ref[0] & (PLACES - 1)
     rows = heads * steps
     half = rows // 2
     rope_base = per_pair * rows
@@ -89,7 +90,7 @@
                 out_refs[0][k, first : first + fresh_rows, :] = piece
 
 
-def attend_kernel(sizes, scale, relative, base, recv_count, me_ref, decode_ref, length_ref, *rest):
+def attend_kernel(sizes, scale, relative, base, recv_count, ids_ref, decode_ref, length_ref, *rest):
     sources, per_pair, steps, heads, requests, fresh_rows = sizes
     recv_refs = rest[:recv_count]
     (
@@ -137,7 +138,7 @@
         for slot in range(slots):
             queries[slot * rows + i * 16 : slot * rows + (i + 1) * 16, 0:LATENT] = res[slot * 16 : (slot + 1) * 16]
 
-    me = me_ref[0]
+    me = ids_ref[0] & (PLACES - 1)
     for o in range(sources):
         owner_count[o] = jnp.int32(0)
     total = jnp.int32(0)
@@ -242,9 +243,9 @@
             out_ref[:, head * vdim : (head + 1) * vdim] = own.astype(jnp.bfloat16)
 
 
-def place_kernel(sizes, relative, me_ref, decode_ref, out_ref, owner_count, place):
+def place_kernel(sizes, relative, ids_ref, decode_ref, out_ref, owner_count, place):
     sources, per_pair, steps, requests = sizes
-    me = me_ref[0]
+    me = ids_ref[0] & (PLACES - 1)
     rows = sources * requests
     shift = requests.bit_length() - 1
 
@@ -277,13 +278,14 @@
         out_ref[t] = jnp.where(col_id == wanted + t, 1.0, 0.0).astype(jnp.bfloat16)
 
 
-def keeps_upper(z_ref):
-    return (z_ref[0] == 1) | (z_ref[0] == 2)
-
-
-def order_kernel(halves, z_ref, pick_ref, *rest):
+def keeps_upper(ids_ref):
+    z = ids_ref[0] // PLACES
+    return (z == 1) | (z == 2)
+
+
+def order_kernel(halves, ids_ref, pick_ref, *rest):
     pieces, out_ref, x = rest[:-2], rest[-2], rest[-1]
-    upper = keeps_upper(z_ref)
+    upper = keeps_upper(ids_ref)
     rows = x.shape[0] // (2 * halves)
     each = len(pieces) // (2 * halves)
     cols = x.shape[1] // each
@@ -307,10 +309,10 @@
         out_ref[t] = jnp.dot(pick_ref[t], x_ref[...], preferred_element_type=jnp.float32).astype(jnp.bfloat16)
 
 
-def project_kernel(first_col, z_ref, *rest):
+def project_kernel(first_col, ids_ref, *rest):
     parts, weight, keep, send, x = rest[:4], rest[4], rest[5], rest[6], rest[7]
     rows = parts[0].shape[0]
-    upper = keeps_upper(z_ref)
+    upper = keeps_upper(ids_ref)
 
     def assemble(order):
         for place, q in enumerate(order):
@@ -372,8 +374,7 @@
     columns = out_proj.shape[1]
     packed_rows = per_pair * rows + per_pair * rows // 2 + -(-width // LANES) * fresh_rows
     sizes = (sources, per_pair, steps, heads, requests, fresh_rows)
-    me = lax.axis_index("seq").astype(jnp.int32).reshape(1)
-    z = lax.axis_index("head").astype(jnp.int32).reshape(1)
+    ids = (lax.axis_index("seq") + PLACES * lax.axis_index("head")).astype(jnp.int32).reshape(1)
     cache = latent_cache.T
 
     pick = pl.pallas_call(
@@ -385,7 +386,7 @@
         compiler_params=limit(12),
         cost_estimate=cost(2),
         name="place_rows",
-    )(me, decode_rows)
+    )(ids, decode_rows)
 
     outs, each = (sources, 1) if relative else (1, sources)
     packed = pl.pallas_call(
@@ -400,7 +401,7 @@
         compiler_params=limit(8),
         cost_estimate=cost(6),
         name="pack_queries",
-    )(me, decode_rows, q_nope, q_rope, new_latent, pick)
+    )(ids, decode_rows, q_nope, q_rope, new_latent, pick)
 
     def attend(received, base):
         here = sum(part.shape[0] for part in received)
@@ -427,7 +428,7 @@
             compiler_params=limit(14),
             cost_estimate=cost(8),
             name="attend",
-        )(me, decode_rows, lengths, *received, cache, key_up, value_up)
+        )(ids, decode_rows, lengths, *received, cache, key_up, value_up)
 
     def order(kernel, in_specs, scratch, arrays):
         return pl.pallas_call(
@@ -465,7 +466,7 @@
             compiler_params=limit(10),
             cost_estimate=cost(2),
             name="project_out",
-        )(z, *parts, out_proj)
+        )(ids, *parts, out_proj)
 
     received = [packed[0]] + [flip(packed[k], "seq", k) for k in range(1, 4)]
     near_rows = attend(received[:2], 0)
@@ -474,31 +475,35 @@
     near_across, far_rows = lax.optimization_barrier((near_across, far_rows))
     near = [near_rows, flip(near_rows, "seq", 1), near_across, flip(near_across, "seq", 1)]
     far_across = flip(far_rows, "seq", 2)
-    first, second = project(near, 0), project(near, 1)
-    far = [far_rows, flip(far_rows, "seq", 1), far_across, flip(far_across, "seq", 1)]
+    def after(value, *others):
+        return lax.optimization_barrier((value,) + others)[0]
 
     def swap(piece):
         return flip(piece[1], "head", 1)
 
-    first_in, second_in = swap(first), swap(second)
+    first = project(near, 0)
+    first_in = swap(first)
+    second = project(near, 1)
+    second_in = swap(second)
+    far = [far_rows, flip(far_rows, "seq", 1), far_across, flip(far_across, "seq", 1)]
     first_pair = add(first[0], first_in)
     first_cross = flip(first_pair, "head", 3)
     second_pair = add(second[0], second_in)
     second_cross = flip(second_pair, "head", 3)
-
     third = project(far, 0)
     third_in = swap(third)
     fourth = project(far, 1)
     fourth_in = swap(fourth)
-    first_cross, _ = lax.optimization_barrier((first_cross, fourth[0]))
+    first_cross = after(first_cross, fourth[0])
+    second_cross = after(second_cross, fourth[0])
+    third_pair = add(third[0], third_in)
+    third_cross = flip(third_pair, "head", 3)
+    fourth_pair = add(fourth[0], fourth_in)
+    fourth_cross = flip(fourth_pair, "head", 3)
     first_sum = add(first_pair, first_cross)
     first_other = flip(first_sum, "head", 1)
-    third_pair = add(third[0], third_in)
-    third_cross = flip(third_pair, "head", 3)
     second_sum = add(second_pair, second_cross)
     second_other = flip(second_sum, "head", 1)
-    fourth_pair = add(fourth[0], fourth_in)
-    fourth_cross = flip(fourth_pair, "head", 3)
     third_sum = add(third_pair, third_cross)
     third_other = flip(third_sum, "head", 1)
     fourth_sum = add(fourth_pair, fourth_cross)
@@ -506,7 +511,7 @@
     arrays = [first_sum, first_other, second_sum, second_other, third_sum, third_other, fourth_sum, fourth_other]
     scratch = [pltpu.VMEM((steps * sources * requests, columns), jnp.bfloat16)]
     kernel = functools.partial(order_kernel, 2)
-    return order(kernel, [smem()] + [vmem()] * (1 + len(arrays)), scratch, [z, pick] + arrays)
+    return order(kernel, [smem()] + [vmem()] * (1 + len(arrays)), scratch, [ids, pick] + arrays)
 
 
 def solution(mesh):

time: 76.2 us -> 68.5 us (0.90)
  local copies, waits for them, and re-layouts: 5.99 us -> 0.82 us
  starting transfers between devices: 28.2 us -> 26.8 us
  waiting for transfers between devices: 15.7 us -> 14.3 us
    unnamed x30 -> x28, local copies, waits for them, and re-layouts: 5.99 us -> 0.82 us
    ppermute x21, waiting for transfers between devices: 15.7 us -> 14.3 us  [flip(): return lax.ppermute(x, axis, [(i, i ^ distance) for i in range(size)])]
    ppermute x21, starting transfers between devices: 28.2 us -> 26.8 us  [flip(): return lax.ppermute(x, axis, [(i, i ^ distance) for i in range(size)])]
  transfers between devices with their start and end apart: 21 -> 21, of which waited for: 9 -> 6; matrix products, arithmetic and copies ran while one was open for 0% -> 0% of each run, Pallas kernels for 29% -> 33%
where the time goes in v8:
time: 68.5 us; the launch traced here: 69 us
  starting transfers between devices  26.8 us (39%)
  Pallas kernels  26.5 us (39%)
  waiting for transfers between devices  14.3 us (21%)
  local copies, waits for them, and re-layouts  0.82 us (1%)
    ppermute x21, starting transfers between devices, flip(): return lax.ppermute(x, axis, [(i, i ^ distance) for i in range(size)])  26.8 us
    pallas_call x2, Pallas kernels, attend(): pl.pallas_call(functools.partial(attend_kernel, sizes, scale, relative, b...  16.8 us
    ppermute x21, waiting for transfers between devices, flip(): return lax.ppermute(x, axis, [(i, i ^ distance) for i in range(size)])  14.3 us
    pallas_call x4, Pallas kernels, project(): pl.pallas_call(functools.partial(project_kernel, piece * cols), out_shape...  5.7 us
    pallas_call x1, Pallas kernels, order(): pl.pallas_call(kernel, out_shape=jax.ShapeDtypeStruct((steps, sources * r...  1.75 us
  transfers between devices with their start and end apart: 21, of which 6 were waited for; matrix products, arithmetic and copies ran while one was open for 0% of the time, Pallas kernels for 33%

profile of v8, /device:TPU:0, one launch (start us, length us, event | category | flops | bytes accessed | tf_op | source)
XLA Modules:
  0.0 69.0 jit_solution(6643798097294754985)
XLA Ops:
  0.0 0.7 %copy-done.6 = s32[64]{0:T(128)S(1)} copy-done((s32[64]{0:T(128)S(1)}, s32[64]{0:T(128)}, u32[]{:S(2)}) %copy-start.6) | copy-done | bytes 280
  0.8 1.1 %place_rows.1.after_ref.pick_ref = bf16[4,64,256]{2,1,0:T(8,128)(2,1)S(1)} custom-call(s32[1]{0:T(128)} %bitcast.ids_ref, s32[64]{0:T(128)S(1)} %copy-done.6), custom_call_target="tpu_custom_call" | custom-call | flops 2000000000 | bytes 6000000 | tf_op jit(solution)/shard_map/place_rows/pallas_call | solution.py:380
  1.9 0.0 slice-start.5
  1.9 0.0 copy-start
  1.9 0.0 copy-start.1
  1.9 0.0 copy-start.5
  1.9 0.0 copy-start.7
  1.9 1.1 %pack_queries.1 = (bf16[1,848,128]{2,1,0:T(8,128)(2,1)S(1)}, bf16[1,848,128]{2,1,0:T(8,128)(2,1)S(1)}, bf16[1,848,128]{2,1,0:T(8,128)(2,1)S(1)}, bf16[1,848,128]{2,1,0:T(8,128)(2,1)S(1)}) custom-call(s32[1]{0:T(128)} %bitcast.ids_ref, s32[64]{0:T(128)S(1)} %copy-done.6, bf16[4,16,32,128]{3,2,1,0:T(8,128)(2,1)S(1)} %copy-done.2, ...), custom_call_target="tpu_custom_call" | custom-call | flops 6000000000 | bytes 18000000 | tf_op jit(solution)/shard_map/pack_queries/pallas_call | solution.py:392
  3.1 0.5 collective-permute-start
  3.6 2.6 %collective-permute-start.3 = (bf16[1,848,128]{2,1,0:T(8,128)(2,1)S(1)}, bf16[1,848,128]{2,1,0:T(8,128)(2,1)S(1)}, u32[]{:S(2)}, u32[]{:S(2)}) collective-permute-start(bf16[1,848,128]{2,1,0:T(8,128)(2,1)S(1)} %get-tuple-element.23), channel_id=1, source_target_pairs={{0,8},{4,12},{8,0},{12,4},{1,9},{5,13},{9,1},{13,5},{2,10},{6,14},... | collective-permute-start | bytes 651272 | tf_op jit(solution)/shard_map/ppermute | solution.py:356
  6.2 0.1 collective-permute-start.4
  6.3 0.0 slice-start
  6.3 0.0 slice-start.1
  6.4 7.2 %attend.2.rest_0_ = bf16[32,4096]{1,0:T(8,128)(2,1)S(1)} custom-call(s32[1]{0:T(128)} %bitcast.ids_ref, s32[64]{0:T(128)S(1)} %copy-done.7, s32[4,16]{1,0:T(4,128)S(1)} %copy-done.5, bf16[1,848,128]{2,1,0:T(8,128)(2,1)S(1)} %get-tuple-element.21.rest_0_, bf16[1,848,128]{2,1,0:T(8,128)(2,1)S(1)} %collective-permute-done.rest_1_, ...), custom_call_target="tpu_custom_call" | custom-call | flops 8000000000 | bytes 24000000 | tf_op jit(solution)/shard_map/attend/pallas_call | solution.py:410
  13.5 0.0 slice-start.2
  13.5 0.0 slice-start.3
  13.5 3.7 %collective-permute-start.2 = (bf16[32,4096]{1,0:T(8,128)(2,1)S(1)}, bf16[32,4096]{1,0:T(8,128)(2,1)S(1)}, u32[]{:S(2)}, u32[]{:S(2)}) collective-permute-start(bf16[32,4096]{1,0:T(8,128)(2,1)S(1)} %attend.2.rest_0_), channel_id=1, source_target_pairs={{0,8},{4,12},{8,0},{12,4},{1,9},{5,13},{9,1},{13,5},{2,10},{6,14},... | collective-permute-start | bytes 786440 | tf_op jit(solution)/shard_map/ppermute | solution.py:356
  17.3 0.0 collective-permute-start.1
  17.3 0.0 collective-permute-done.3.rest_0_
  17.3 0.0 collective-permute-done.4.rest_1_
  17.3 9.7 %attend.3.rest_0_ = bf16[32,4096]{1,0:T(8,128)(2,1)S(1)} custom-call(s32[1]{0:T(128)} %bitcast.ids_ref, s32[64]{0:T(128)S(1)} %copy-done.7, s32[4,16]{1,0:T(4,128)S(1)} %copy-done.5, bf16[1,848,128]{2,1,0:T(8,128)(2,1)S(1)} %collective-permute-done.3.rest_0_, bf16[1,848,128]{2,1,0:T(8,128)(2,1)S(1)} %collective-permute-done.4.rest_1_, ...), custom_call_target="tpu_custom_call" | custom-call | flops 8000000000 | bytes 24000000 | tf_op jit(solution)/shard_map/attend/pallas_call | solution.py:410
  27.0 0.1 collective-permute-start.5
  27.1 0.1 collective-permute-start.9
  27.2 0.4 collective-permute-start.8
  27.6 1.0 %collective-permute-done.5.rest_3_ = bf16[32,4096]{1,0:T(8,128)(2,1)S(1)} collective-permute-done((bf16[32,4096]{1,0:T(8,128)(2,1)S(1)}, bf16[32,4096]{1,0:T(8,128)(2,1)S(1)}, u32[]{:S(2)}, u32[]{:S(2)}) %collective-permute-start.5) | collective-permute-done | bytes 262176 | tf_op jit(solution)/shard_map/ppermute | solution.py:356
  28.6 1.4 %project_out.6 = (bf16[64,896]{1,0:T(8,128)(2,1)S(1)}, bf16[64,896]{1,0:T(8,128)(2,1)S(1)}) custom-call(s32[1]{0:T(128)} %bitcast.ids_ref, bf16[32,4096]{1,0:T(8,128)(2,1)S(1)} %attend.2.rest_0_, bf16[32,4096]{1,0:T(8,128)(2,1)S(1)} %collective-permute-done.1.rest_1_, bf16[32,4096]{1,0:T(8,128)(2,1)S(1)} %collective-permute-done.2.rest_2_, ...), custom_call_target="tpu_custom_call" | custom-call | flops 2000000000 | bytes 6000000 | tf_op jit(solution)/shard_map/project_out/pallas_call | solution.py:460
  30.0 1.6 %collective-permute-start.12 = (bf16[64,896]{1,0:T(8,128)(2,1)S(1)}, bf16[64,896]{1,0:T(8,128)(2,1)S(1)}, u32[]{:S(2)}, u32[]{:S(2)}) collective-permute-start(bf16[64,896]{1,0:T(8,128)(2,1)S(1)} %get-tuple-element.32), channel_id=1, source_target_pairs={{0,1},{1,0},{2,3},{3,2},{4,5},{5,4},{6,7},{7,6},{8,9},{9,8},{10,11... | collective-permute-start | bytes 344072 | tf_op jit(solution)/shard_map/ppermute | solution.py:356
  31.7 1.4 %project_out.4 = (bf16[64,896]{1,0:T(8,128)(2,1)S(1)}, bf16[64,896]{1,0:T(8,128)(2,1)S(1)}) custom-call(s32[1]{0:T(128)} %bitcast.ids_ref, bf16[32,4096]{1,0:T(8,128)(2,1)S(1)} %attend.2.rest_0_, bf16[32,4096]{1,0:T(8,128)(2,1)S(1)} %collective-permute-done.1.rest_1_, bf16[32,4096]{1,0:T(8,128)(2,1)S(1)} %collective-permute-done.2.rest_2_, ...), custom_call_target="tpu_custom_call" | custom-call | flops 2000000000 | bytes 6000000 | tf_op jit(solution)/shard_map/project_out/pallas_call | solution.py:460
  33.1 0.5 collective-permute-start.6
  33.6 2.2 %collective-permute-done.9.rest_2_ = bf16[32,4096]{1,0:T(8,128)(2,1)S(1)} collective-permute-done((bf16[32,4096]{1,0:T(8,128)(2,1)S(1)}, bf16[32,4096]{1,0:T(8,128)(2,1)S(1)}, u32[]{:S(2)}, u32[]{:S(2)}) %collective-permute-start.9) | collective-permute-done | bytes 262176 | tf_op jit(solution)/shard_map/ppermute | solution.py:356
  35.9 4.0 %collective-permute-start.13 = (bf16[64,896]{1,0:T(8,128)(2,1)S(1)}, bf16[64,896]{1,0:T(8,128)(2,1)S(1)}, u32[]{:S(2)}, u32[]{:S(2)}) collective-permute-start(bf16[64,896]{1,0:T(8,128)(2,1)S(1)} %add_convert_fusion.5), channel_id=1, source_target_pairs={{0,3},{1,2},{2,1},{3,0},{4,7},{5,6},{6,5},{7,4},{8,11},{9,10},{10,... | collective-permute-start | bytes 344072 | tf_op jit(solution)/shard_map/ppermute | solution.py:356
  39.8 0.0 collective-permute-done.6
  39.8 1.6 %collective-permute-start.7 = (bf16[64,896]{1,0:T(8,128)(2,1)S(1)}, bf16[64,896]{1,0:T(8,128)(2,1)S(1)}, u32[]{:S(2)}, u32[]{:S(2)}) collective-permute-start(bf16[64,896]{1,0:T(8,128)(2,1)S(1)} %add_convert_fusion.7), channel_id=1, source_target_pairs={{0,3},{1,2},{2,1},{3,0},{4,7},{5,6},{6,5},{7,4},{8,11},{9,10},{10,... | collective-permute-start | bytes 344072 | tf_op jit(solution)/shard_map/ppermute | solution.py:356
  41.5 1.6 %project_out.5 = (bf16[64,896]{1,0:T(8,128)(2,1)S(1)}, bf16[64,896]{1,0:T(8,128)(2,1)S(1)}) custom-call(s32[1]{0:T(128)} %bitcast.ids_ref, bf16[32,4096]{1,0:T(8,128)(2,1)S(1)} %attend.3.rest_0_, bf16[32,4096]{1,0:T(8,128)(2,1)S(1)} %collective-permute-done.8.rest_1_, bf16[32,4096]{1,0:T(8,128)(2,1)S(1)} %collective-permute-done.9.rest_2_, ...), custom_call_target="tpu_custom_call" | custom-call | flops 2000000000 | bytes 6000000 | tf_op jit(solution)/shard_map/project_out/pallas_call | solution.py:460
  43.0 0.1 collective-permute-start.18
  43.1 1.4 %project_out.7 = (bf16[64,896]{1,0:T(8,128)(2,1)S(1)}, bf16[64,896]{1,0:T(8,128)(2,1)S(1)}) custom-call(s32[1]{0:T(128)} %bitcast.ids_ref, bf16[32,4096]{1,0:T(8,128)(2,1)S(1)} %attend.3.rest_0_, bf16[32,4096]{1,0:T(8,128)(2,1)S(1)} %collective-permute-done.8.rest_1_, bf16[32,4096]{1,0:T(8,128)(2,1)S(1)} %collective-permute-done.9.rest_2_, ...), custom_call_target="tpu_custom_call" | custom-call | flops 2000000000 | bytes 6000000 | tf_op jit(solution)/shard_map/project_out/pallas_call | solution.py:460
  44.5 2.1 %collective-permute-start.15 = (bf16[64,896]{1,0:T(8,128)(2,1)S(1)}, bf16[64,896]{1,0:T(8,128)(2,1)S(1)}, u32[]{:S(2)}, u32[]{:S(2)}) collective-permute-start(bf16[64,896]{1,0:T(8,128)(2,1)S(1)} %get-tuple-element.35), channel_id=1, source_target_pairs={{0,1},{1,0},{2,3},{3,2},{4,5},{5,4},{6,7},{7,6},{8,9},{9,8},{10,11... | collective-permute-start | bytes 344072 | tf_op jit(solution)/shard_map/ppermute | solution.py:356
  46.6 2.2 %collective-permute-start.14 = (bf16[64,896]{1,0:T(8,128)(2,1)S(1)}, bf16[64,896]{1,0:T(8,128)(2,1)S(1)}, u32[]{:S(2)}, u32[]{:S(2)}) collective-permute-start(bf16[64,896]{1,0:T(8,128)(2,1)S(1)} %add_convert_fusion.4.rest_2_), channel_id=1, source_target_pairs={{0,1},{1,0},{2,3},{3,2},{4,5},{5,4},{6,7},{7,6},{8,9},{9,8},{10,11... | collective-permute-start | bytes 344072 | tf_op jit(solution)/shard_map/ppermute | solution.py:356
  48.8 1.7 %collective-permute-start.11 = (bf16[64,896]{1,0:T(8,128)(2,1)S(1)}, bf16[64,896]{1,0:T(8,128)(2,1)S(1)}, u32[]{:S(2)}, u32[]{:S(2)}) collective-permute-start(bf16[64,896]{1,0:T(8,128)(2,1)S(1)} %add_convert_fusion.6.rest_0_), channel_id=1, source_target_pairs={{0,1},{1,0},{2,3},{3,2},{4,5},{5,4},{6,7},{7,6},{8,9},{9,8},{10,11... | collective-permute-start | bytes 344072 | tf_op jit(solution)/shard_map/ppermute | solution.py:356
  50.6 2.5 %collective-permute-start.19 = (bf16[64,896]{1,0:T(8,128)(2,1)S(1)}, bf16[64,896]{1,0:T(8,128)(2,1)S(1)}, u32[]{:S(2)}, u32[]{:S(2)}) collective-permute-start(bf16[64,896]{1,0:T(8,128)(2,1)S(1)} %add_convert_fusion.1), channel_id=1, source_target_pairs={{0,3},{1,2},{2,1},{3,0},{4,7},{5,6},{6,5},{7,4},{8,11},{9,10},{10,... | collective-permute-start | bytes 344072 | tf_op jit(solution)/shard_map/ppermute | solution.py:356
  53.1 1.4 %collective-permute-start.16 = (bf16[64,896]{1,0:T(8,128)(2,1)S(1)}, bf16[64,896]{1,0:T(8,128)(2,1)S(1)}, u32[]{:S(2)}, u32[]{:S(2)}) collective-permute-start(bf16[64,896]{1,0:T(8,128)(2,1)S(1)} %add_convert_fusion.3), channel_id=1, source_target_pairs={{0,3},{1,2},{2,1},{3,0},{4,7},{5,6},{6,5},{7,4},{8,11},{9,10},{10,... | collective-permute-start | bytes 344072 | tf_op jit(solution)/shard_map/ppermute | solution.py:356
  54.6 5.3 %collective-permute-done.19 = bf16[64,896]{1,0:T(8,128)(2,1)S(1)} collective-permute-done((bf16[64,896]{1,0:T(8,128)(2,1)S(1)}, bf16[64,896]{1,0:T(8,128)(2,1)S(1)}, u32[]{:S(2)}, u32[]{:S(2)}) %collective-permute-start.19) | collective-permute-done | bytes 114720 | tf_op jit(solution)/shard_map/ppermute | solution.py:356
  59.9 0.1 collective-permute-start.20
  60.0 1.6 %collective-permute-done.16 = bf16[64,896]{1,0:T(8,128)(2,1)S(1)} collective-permute-done((bf16[64,896]{1,0:T(8,128)(2,1)S(1)}, bf16[64,896]{1,0:T(8,128)(2,1)S(1)}, u32[]{:S(2)}, u32[]{:S(2)}) %collective-permute-start.16) | collective-permute-done | bytes 114720 | tf_op jit(solution)/shard_map/ppermute | solution.py:356
  61.7 1.6 %collective-permute-start.17 = (bf16[64,896]{1,0:T(8,128)(2,1)S(1)}, bf16[64,896]{1,0:T(8,128)(2,1)S(1)}, u32[]{:S(2)}, u32[]{:S(2)}) collective-permute-start(bf16[64,896]{1,0:T(8,128)(2,1)S(1)} %add_convert_fusion.2.rest_4_), channel_id=1, source_target_pairs={{0,1},{1,0},{2,3},{3,2},{4,5},{5,4},{6,7},{7,6},{8,9},{9,8},{10,11... | collective-permute-start | bytes 344072 | tf_op jit(solution)/shard_map/ppermute | solution.py:356
  63.3 2.7 %collective-permute-done.20.rest_7_ = bf16[64,896]{1,0:T(8,128)(2,1)S(1)} collective-permute-done((bf16[64,896]{1,0:T(8,128)(2,1)S(1)}, bf16[64,896]{1,0:T(8,128)(2,1)S(1)}, u32[]{:S(2)}, u32[]{:S(2)}) %collective-permute-start.20) | collective-permute-done | bytes 114720 | tf_op jit(solution)/shard_map/ppermute | solution.py:356
  66.0 1.3 %collective-permute-done.17.rest_5_ = bf16[64,896]{1,0:T(8,128)(2,1)S(1)} collective-permute-done((bf16[64,896]{1,0:T(8,128)(2,1)S(1)}, bf16[64,896]{1,0:T(8,128)(2,1)S(1)}, u32[]{:S(2)}, u32[]{:S(2)}) %collective-permute-start.17) | collective-permute-done | bytes 114720 | tf_op jit(solution)/shard_map/ppermute | solution.py:356
  67.2 1.7 %order_rows.1 = bf16[4,64,1792]{2,1,0:T(8,128)(2,1)} custom-call(s32[1]{0:T(128)} %bitcast.ids_ref, bf16[4,64,256]{2,1,0:T(8,128)(2,1)S(1)} %place_rows.1.after_ref.pick_ref, bf16[64,896]{1,0:T(8,128)(2,1)S(1)} %add_convert_fusion.6.rest_0_, bf16[64,896]{1,0:T(8,128)(2,1)S(1)} %collective-permute-done.11.rest_1_, ...), custom_call_target="tpu_custom_call" | custom-call | flops 2000000000 | bytes 6000000 | tf_op jit(solution)/shard_map/order_rows/pallas_call | solution.py:434
  (41 shorter events, 0.3 us)
Async XLA Ops:
  0.0 1.8 %copy-start.2 = (bf16[4,16,32,128]{3,2,1,0:T(8,128)(2,1)S(1)}, bf16[4,16,32,128]{3,2,1,0:T(8,128)(2,1)}, u32[]{:S(2)}) copy-start(bf16[4,16,32,128]{3,2,1,0:T(8,128)(2,1)} %nope_ref.1) | copy-start | bytes 1572868
  0.0 1.9 %copy-start.3 = (bf16[4,16,32,64]{3,2,1,0:T(8,128)(2,1)S(1)}, bf16[4,16,32,64]{3,2,1,0:T(8,128)(2,1)}, u32[]{:S(2)}) copy-start(bf16[4,16,32,64]{3,2,1,0:T(8,128)(2,1)} %rope_ref.1) | copy-start | bytes 786436
  0.0 1.9 %copy-start.4 = (bf16[4,16,576]{2,1,0:T(8,128)(2,1)S(1)}, bf16[4,16,576]{2,1,0:T(8,128)(2,1)}, u32[]{:S(2)}) copy-start(bf16[4,16,576]{2,1,0:T(8,128)(2,1)} %fresh_ref.1) | copy-start | bytes 221188
  0.0 0.7 %copy-start.6 = (s32[64]{0:T(128)S(1)}, s32[64]{0:T(128)}, u32[]{:S(2)}) copy-start(s32[64]{0:T(128)} %decode_ref.7) | copy-start | bytes 772
  0.8 5.5 %slice-start.4 = ((s8[4718592]{0:T(1024)(128)(4,1)}), s8[4194304]{0:T(1024)(128)(4,1)S(1)}, s32[]{:S(2)}) async-start(s8[4718592]{0:T(1024)(128)(4,1)} %bitcast.4), calls=%async_computation.4 | async-start | bytes 8388608
  1.9 4.4 %slice-start.5 = ((s8[4718592]{0:T(1024)(128)(4,1)}), s8[524288]{0:T(1024)(128)(4,1)S(1)}, s32[]{:S(2)}) async-start(s8[4718592]{0:T(1024)(128)(4,1)} %bitcast.4), calls=%async_computation.5 | async-start | bytes 1048576
  1.9 4.4 %copy-start = (bf16[32,128,512]{2,1,0:T(8,128)(2,1)S(1)}, bf16[32,128,512]{2,1,0:T(8,128)(2,1)}, u32[]{:S(2)}) copy-start(bf16[32,128,512]{2,1,0:T(8,128)(2,1)} %rest_3_.3) | copy-start | bytes 12582916
  1.9 4.4 %copy-start.1 = (bf16[32,512,128]{2,1,0:T(8,128)(2,1)S(1)}, bf16[32,512,128]{2,1,0:T(8,128)(2,1)}, u32[]{:S(2)}) copy-start(bf16[32,512,128]{2,1,0:T(8,128)(2,1)} %rest_4_.7) | copy-start | bytes 12582916
  1.9 4.4 %copy-start.5 = (s32[4,16]{1,0:T(4,128)S(1)}, s32[4,16]{1,0:T(4,128)}, u32[]{:S(2)}) copy-start(s32[4,16]{1,0:T(4,128)} %length_ref.3) | copy-start | bytes 772
  1.9 4.4 %copy-start.7 = (s32[64]{0:T(128)S(1)}, s32[64]{0:T(128)}, u32[]{:S(2)}) copy-start(s32[64]{0:T(128)} %decode_ref.7) | copy-start | bytes 772
  3.1 3.2 %collective-permute-start = (bf16[1,848,128]{2,1,0:T(8,128)(2,1)S(1)}, bf16[1,848,128]{2,1,0:T(8,128)(2,1)S(1)}, u32[]{:S(2)}, u32[]{:S(2)}) collective-permute-start(bf16[1,848,128]{2,1,0:T(8,128)(2,1)S(1)} %get-tuple-element.22), channel_id=1, source_target_pairs={{0,4},{4,0},{8,12},{12,8},{1,5},{5,1},{9,13},{13,9},{2,6},{6,2},{1... | collective-permute-start | bytes 651272 | tf_op jit(solution)/shard_map/ppermute | solution.py:356
  3.6 13.7 %collective-permute-start.3 = (bf16[1,848,128]{2,1,0:T(8,128)(2,1)S(1)}, bf16[1,848,128]{2,1,0:T(8,128)(2,1)S(1)}, u32[]{:S(2)}, u32[]{:S(2)}) collective-permute-start(bf16[1,848,128]{2,1,0:T(8,128)(2,1)S(1)} %get-tuple-element.23), channel_id=1, source_target_pairs={{0,8},{4,12},{8,0},{12,4},{1,9},{5,13},{9,1},{13,5},{2,10},{6,14},... | collective-permute-start | bytes 651272 | tf_op jit(solution)/shard_map/ppermute | solution.py:356
  6.2 11.1 %collective-permute-start.4 = (bf16[1,848,128]{2,1,0:T(8,128)(2,1)S(1)}, bf16[1,848,128]{2,1,0:T(8,128)(2,1)S(1)}, u32[]{:S(2)}, u32[]{:S(2)}) collective-permute-start(bf16[1,848,128]{2,1,0:T(8,128)(2,1)S(1)} %get-tuple-element.24), channel_id=1, source_target_pairs={{0,12},{4,8},{8,4},{12,0},{1,13},{5,9},{9,5},{13,1},{2,14},{6,10},... | collective-permute-start | bytes 651272 | tf_op jit(solution)/shard_map/ppermute | solution.py:356
  6.3 22.3 %slice-start = ((s8[14680064]{0:T(1024)(128)(4,1)}), s8[4194304]{0:T(1024)(128)(4,1)S(1)}, s32[]{:S(2)}) async-start(s8[14680064]{0:T(1024)(128)(4,1)} %bitcast.2), calls=%async_computation | async-start | bytes 8388608
  6.3 22.3 %slice-start.1 = ((s8[14680064]{0:T(1024)(128)(4,1)}), s8[4194304]{0:T(1024)(128)(4,1)S(1)}, s32[]{:S(2)}) async-start(s8[14680064]{0:T(1024)(128)(4,1)} %bitcast.2), calls=%async_computation.1 | async-start | bytes 8388608
  13.5 15.1 %slice-start.2 = ((s8[14680064]{0:T(1024)(128)(4,1)}), s8[4194304]{0:T(1024)(128)(4,1)S(1)}, s32[]{:S(2)}) async-start(s8[14680064]{0:T(1024)(128)(4,1)} %bitcast.2), calls=%async_computation.2 | async-start | bytes 8388608
  13.5 15.1 %slice-start.3 = ((s8[14680064]{0:T(1024)(128)(4,1)}), s8[2097152]{0:T(1024)(128)(4,1)S(1)}, s32[]{:S(2)}) async-start(s8[14680064]{0:T(1024)(128)(4,1)} %bitcast.2), calls=%async_computation.3 | async-start | bytes 4194304
  13.5 13.5 %collective-permute-start.2 = (bf16[32,4096]{1,0:T(8,128)(2,1)S(1)}, bf16[32,4096]{1,0:T(8,128)(2,1)S(1)}, u32[]{:S(2)}, u32[]{:S(2)}) collective-permute-start(bf16[32,4096]{1,0:T(8,128)(2,1)S(1)} %attend.2.rest_0_), channel_id=1, source_target_pairs={{0,8},{4,12},{8,0},{12,4},{1,9},{5,13},{9,1},{13,5},{2,10},{6,14},... | collective-permute-start | bytes 786440 | tf_op jit(solution)/shard_map/ppermute | solution.py:356
  17.3 10.3 %collective-permute-start.1 = (bf16[32,4096]{1,0:T(8,128)(2,1)S(1)}, bf16[32,4096]{1,0:T(8,128)(2,1)S(1)}, u32[]{:S(2)}, u32[]{:S(2)}) collective-permute-start(bf16[32,4096]{1,0:T(8,128)(2,1)S(1)} %attend.2.rest_0_), channel_id=1, source_target_pairs={{0,4},{4,0},{8,12},{12,8},{1,5},{5,1},{9,13},{13,9},{2,6},{6,2},{1... | collective-permute-start | bytes 786440 | tf_op jit(solution)/shard_map/ppermute | solution.py:356
  27.0 1.6 %collective-permute-start.5 = (bf16[32,4096]{1,0:T(8,128)(2,1)S(1)}, bf16[32,4096]{1,0:T(8,128)(2,1)S(1)}, u32[]{:S(2)}, u32[]{:S(2)}) collective-permute-start(bf16[32,4096]{1,0:T(8,128)(2,1)S(1)} %collective-permute-done.2.rest_2_), channel_id=1, source_target_pairs={{0,4},{4,0},{8,12},{12,8},{1,5},{5,1},{9,13},{13,9},{2,6},{6,2},{1... | collective-permute-start | bytes 786440 | tf_op jit(solution)/shard_map/ppermute | solution.py:356
  27.1 8.7 %collective-permute-start.9 = (bf16[32,4096]{1,0:T(8,128)(2,1)S(1)}, bf16[32,4096]{1,0:T(8,128)(2,1)S(1)}, u32[]{:S(2)}, u32[]{:S(2)}) collective-permute-start(bf16[32,4096]{1,0:T(8,128)(2,1)S(1)} %attend.3.rest_0_), channel_id=1, source_target_pairs={{0,8},{4,12},{8,0},{12,4},{1,9},{5,13},{9,1},{13,5},{2,10},{6,14},... | collective-permute-start | bytes 786440 | tf_op jit(solution)/shard_map/ppermute | solution.py:356
  27.2 14.3 %collective-permute-start.8 = (bf16[32,4096]{1,0:T(8,128)(2,1)S(1)}, bf16[32,4096]{1,0:T(8,128)(2,1)S(1)}, u32[]{:S(2)}, u32[]{:S(2)}) collective-permute-start(bf16[32,4096]{1,0:T(8,128)(2,1)S(1)} %attend.3.rest_0_), channel_id=1, source_target_pairs={{0,4},{4,0},{8,12},{12,8},{1,5},{5,1},{9,13},{13,9},{2,6},{6,2},{1... | collective-permute-start | bytes 786440 | tf_op jit(solution)/shard_map/ppermute | solution.py:356
  30.0 5.8 %collective-permute-start.12 = (bf16[64,896]{1,0:T(8,128)(2,1)S(1)}, bf16[64,896]{1,0:T(8,128)(2,1)S(1)}, u32[]{:S(2)}, u32[]{:S(2)}) collective-permute-start(bf16[64,896]{1,0:T(8,128)(2,1)S(1)} %get-tuple-element.32), channel_id=1, source_target_pairs={{0,1},{1,0},{2,3},{3,2},{4,5},{5,4},{6,7},{7,6},{8,9},{9,8},{10,11... | collective-permute-start | bytes 344072 | tf_op jit(solution)/shard_map/ppermute | solution.py:356
  33.1 6.8 %collective-permute-start.6 = (bf16[64,896]{1,0:T(8,128)(2,1)S(1)}, bf16[64,896]{1,0:T(8,128)(2,1)S(1)}, u32[]{:S(2)}, u32[]{:S(2)}) collective-permute-start(bf16[64,896]{1,0:T(8,128)(2,1)S(1)} %get-tuple-element.27), channel_id=1, source_target_pairs={{0,1},{1,0},{2,3},{3,2},{4,5},{5,4},{6,7},{7,6},{8,9},{9,8},{10,11... | collective-permute-start | bytes 344072 | tf_op jit(solution)/shard_map/ppermute | solution.py:356
  35.8 5.6 %collective-permute-start.10 = (bf16[32,4096]{1,0:T(8,128)(2,1)S(1)}, bf16[32,4096]{1,0:T(8,128)(2,1)S(1)}, u32[]{:S(2)}, u32[]{:S(2)}) collective-permute-start(bf16[32,4096]{1,0:T(8,128)(2,1)S(1)} %collective-permute-done.9.rest_2_), channel_id=1, source_target_pairs={{0,4},{4,0},{8,12},{12,8},{1,5},{5,1},{9,13},{13,9},{2,6},{6,2},{1... | collective-permute-start | bytes 786440 | tf_op jit(solution)/shard_map/ppermute | solution.py:356
  35.9 10.7 %collective-permute-start.13 = (bf16[64,896]{1,0:T(8,128)(2,1)S(1)}, bf16[64,896]{1,0:T(8,128)(2,1)S(1)}, u32[]{:S(2)}, u32[]{:S(2)}) collective-permute-start(bf16[64,896]{1,0:T(8,128)(2,1)S(1)} %add_convert_fusion.5), channel_id=1, source_target_pairs={{0,3},{1,2},{2,1},{3,0},{4,7},{5,6},{6,5},{7,4},{8,11},{9,10},{10,... | collective-permute-start | bytes 344072 | tf_op jit(solution)/shard_map/ppermute | solution.py:356
  39.8 8.9 %collective-permute-start.7 = (bf16[64,896]{1,0:T(8,128)(2,1)S(1)}, bf16[64,896]{1,0:T(8,128)(2,1)S(1)}, u32[]{:S(2)}, u32[]{:S(2)}) collective-permute-start(bf16[64,896]{1,0:T(8,128)(2,1)S(1)} %add_convert_fusion.7), channel_id=1, source_target_pairs={{0,3},{1,2},{2,1},{3,0},{4,7},{5,6},{6,5},{7,4},{8,11},{9,10},{10,... | collective-permute-start | bytes 344072 | tf_op jit(solution)/shard_map/ppermute | solution.py:356
  43.0 7.5 %collective-permute-start.18 = (bf16[64,896]{1,0:T(8,128)(2,1)S(1)}, bf16[64,896]{1,0:T(8,128)(2,1)S(1)}, u32[]{:S(2)}, u32[]{:S(2)}) collective-permute-start(bf16[64,896]{1,0:T(8,128)(2,1)S(1)} %get-tuple-element.36), channel_id=1, source_target_pairs={{0,1},{1,0},{2,3},{3,2},{4,5},{5,4},{6,7},{7,6},{8,9},{9,8},{10,11... | collective-permute-start | bytes 344072 | tf_op jit(solution)/shard_map/ppermute | solution.py:356
  44.5 8.6 %collective-permute-start.15 = (bf16[64,896]{1,0:T(8,128)(2,1)S(1)}, bf16[64,896]{1,0:T(8,128)(2,1)S(1)}, u32[]{:S(2)}, u32[]{:S(2)}) collective-permute-start(bf16[64,896]{1,0:T(8,128)(2,1)S(1)} %get-tuple-element.35), channel_id=1, source_target_pairs={{0,1},{1,0},{2,3},{3,2},{4,5},{5,4},{6,7},{7,6},{8,9},{9,8},{10,11... | collective-permute-start | bytes 344072 | tf_op jit(solution)/shard_map/ppermute | solution.py:356
  46.6 16.7 %collective-permute-start.14 = (bf16[64,896]{1,0:T(8,128)(2,1)S(1)}, bf16[64,896]{1,0:T(8,128)(2,1)S(1)}, u32[]{:S(2)}, u32[]{:S(2)}) collective-permute-start(bf16[64,896]{1,0:T(8,128)(2,1)S(1)} %add_convert_fusion.4.rest_2_), channel_id=1, source_target_pairs={{0,1},{1,0},{2,3},{3,2},{4,5},{5,4},{6,7},{7,6},{8,9},{9,8},{10,11... | collective-permute-start | bytes 344072 | tf_op jit(solution)/shard_map/ppermute | solution.py:356
  48.8 14.5 %collective-permute-start.11 = (bf16[64,896]{1,0:T(8,128)(2,1)S(1)}, bf16[64,896]{1,0:T(8,128)(2,1)S(1)}, u32[]{:S(2)}, u32[]{:S(2)}) collective-permute-start(bf16[64,896]{1,0:T(8,128)(2,1)S(1)} %add_convert_fusion.6.rest_0_), channel_id=1, source_target_pairs={{0,1},{1,0},{2,3},{3,2},{4,5},{5,4},{6,7},{7,6},{8,9},{9,8},{10,11... | collective-permute-start | bytes 344072 | tf_op jit(solution)/shard_map/ppermute | solution.py:356
  50.6 9.3 %collective-permute-start.19 = (bf16[64,896]{1,0:T(8,128)(2,1)S(1)}, bf16[64,896]{1,0:T(8,128)(2,1)S(1)}, u32[]{:S(2)}, u32[]{:S(2)}) collective-permute-start(bf16[64,896]{1,0:T(8,128)(2,1)S(1)} %add_convert_fusion.1), channel_id=1, source_target_pairs={{0,3},{1,2},{2,1},{3,0},{4,7},{5,6},{6,5},{7,4},{8,11},{9,10},{10,... | collective-permute-start | bytes 344072 | tf_op jit(solution)/shard_map/ppermute | solution.py:356
  53.1 8.5 %collective-permute-start.16 = (bf16[64,896]{1,0:T(8,128)(2,1)S(1)}, bf16[64,896]{1,0:T(8,128)(2,1)S(1)}, u32[]{:S(2)}, u32[]{:S(2)}) collective-permute-start(bf16[64,896]{1,0:T(8,128)(2,1)S(1)} %add_convert_fusion.3), channel_id=1, source_target_pairs={{0,3},{1,2},{2,1},{3,0},{4,7},{5,6},{6,5},{7,4},{8,11},{9,10},{10,... | collective-permute-start | bytes 344072 | tf_op jit(solution)/shard_map/ppermute | solution.py:356
  59.9 6.1 %collective-permute-start.20 = (bf16[64,896]{1,0:T(8,128)(2,1)S(1)}, bf16[64,896]{1,0:T(8,128)(2,1)S(1)}, u32[]{:S(2)}, u32[]{:S(2)}) collective-permute-start(bf16[64,896]{1,0:T(8,128)(2,1)S(1)} %add_convert_fusion.rest_6_), channel_id=1, source_target_pairs={{0,1},{1,0},{2,3},{3,2},{4,5},{5,4},{6,7},{7,6},{8,9},{9,8},{10,11... | collective-permute-start | bytes 344072 | tf_op jit(solution)/shard_map/ppermute | solution.py:356
  61.7 5.6 %collective-permute-start.17 = (bf16[64,896]{1,0:T(8,128)(2,1)S(1)}, bf16[64,896]{1,0:T(8,128)(2,1)S(1)}, u32[]{:S(2)}, u32[]{:S(2)}) collective-permute-start(bf16[64,896]{1,0:T(8,128)(2,1)S(1)} %add_convert_fusion.2.rest_4_), channel_id=1, source_target_pairs={{0,1},{1,0},{2,3},{3,2},{4,5},{5,4},{6,7},{7,6},{8,9},{9,8},{10,11... | collective-permute-start | bytes 344072 | tf_op jit(solution)/shard_map/ppermute | solution.py:356

commit v9 on v8

--- a/solution.py
+++ b/solution.py
@@ -96,7 +96,7 @@
     (
         cache, key_up, value_up, out_ref,
         slot_offset, slot_length, owner_count, pair_slot, pair_start,
-        queries, fresh, acc, run_max, run_sum, latent,
+        queries, fresh, acc, run_max, run_sum, latent, even_scores, odd_scores,
     ) = rest[recv_count:]
     owners = [(ref, e) for ref in recv_refs for e in range(ref.shape[0])]
     here = len(owners)
@@ -180,28 +180,32 @@
     for slot in range(slots):
         acc[slot] = jnp.dot(fresh_weights[slot], fresh[:, 0:LATENT], preferred_element_type=jnp.float32)
 
-    unroll = 4
-
-    def some_pairs(i, carry):
-        for u in range(unroll):
-            p = i * unroll + u
-            slot = pair_slot[jnp.minimum(p, count - 1)]
-            start = pair_start[jnp.minimum(p, count - 1)]
+    def make_scores(buffer, g):
+        for u in range(2):
+            p = jnp.minimum(g * 2 + u, count - 1)
+            q = queries[pl.ds(pl.multiple_of(pair_slot[p] * rows, 16), rows), :]
+            read = pl.multiple_of(jnp.minimum(pair_start[p], tokens - BLOCK), LANES)
+            buffer[u] = jnp.dot(q, cache[:, pl.ds(read, BLOCK)], preferred_element_type=jnp.float32)
+
+    token = lax.broadcasted_iota(jnp.int32, (1, BLOCK), 1)
+
+    def take_scores(buffer, g):
+        for u in range(2):
+            p = jnp.minimum(g * 2 + u, count - 1)
+            slot = pair_slot[p]
+            start = pair_start[p]
             read = jnp.minimum(start, tokens - BLOCK)
             low = jnp.maximum(slot_offset[slot], start) - read
             high = jnp.minimum(slot_offset[slot] + slot_length[slot], start + BLOCK) - read
-            high = jnp.where(p < count, high, low)
-            q = queries[pl.ds(pl.multiple_of(slot * rows, 16), rows), :]
-            keys = cache[:, pl.ds(pl.multiple_of(read, LANES), BLOCK)]
-            scores = jnp.dot(q, keys, preferred_element_type=jnp.float32) * factor
-            token = lax.broadcasted_iota(jnp.int32, scores.shape, 1)
-            scores = jnp.where((token >= low) & (token < high), scores, NEG)
+            high = jnp.where(g * 2 + u < count, high, low)
+            bias = jnp.where((token >= low) & (token < high), 0.0, NEG)
+            scores = buffer[u] * factor + bias
             top = jnp.max(scores, axis=1, keepdims=True)
             weights = jnp.exp2(scores - top)
             part_sum = jnp.broadcast_to(jnp.sum(weights, axis=1, keepdims=True), (rows, LANES))
             part = lax.dot_general(
                 weights.astype(jnp.bfloat16),
-                keys[0:LATENT],
+                cache[0:LATENT, pl.ds(pl.multiple_of(read, LANES), BLOCK)],
                 (((1,), (1,)), ((), ())),
                 preferred_element_type=jnp.float32,
             )
@@ -215,9 +219,17 @@
             for c in range(LATENT // LANES):
                 cols = slice(c * LANES, (c + 1) * LANES)
                 acc[slot, :, cols] = acc[slot, :, cols] * keep + part[:, cols] * add
+
+    make_scores(even_scores, 0)
+
+    def four_pairs(i, carry):
+        make_scores(odd_scores, 2 * i + 1)
+        take_scores(even_scores, 2 * i)
+        make_scores(even_scores, 2 * i + 2)
+        take_scores(odd_scores, 2 * i + 1)
         return carry
 
-    lax.fori_loop(0, (count + unroll - 1) // unroll, some_pairs, jnp.int32(0))
+    lax.fori_loop(0, (count + 3) // 4, four_pairs, jnp.int32(0))
 
     for slot in range(slots):
         inverse = 1.0 / run_sum[slot]
@@ -424,6 +436,8 @@
                 pltpu.VMEM((slots, rows, LANES), jnp.float32),
                 pltpu.VMEM((slots, rows, LANES), jnp.float32),
                 pltpu.VMEM((slots * rows, LATENT), jnp.bfloat16),
+                pltpu.VMEM((2, rows, BLOCK), jnp.float32),
+                pltpu.VMEM((2, rows, BLOCK), jnp.float32),
             ],
             compiler_params=limit(14),
             cost_estimate=cost(8),
@@ -494,12 +508,12 @@
     third_in = swap(third)
     fourth = project(far, 1)
     fourth_in = swap(fourth)
-    first_cross = after(first_cross, fourth[0])
-    second_cross = after(second_cross, fourth[0])
     third_pair = add(third[0], third_in)
     third_cross = flip(third_pair, "head", 3)
     fourth_pair = add(fourth[0], fourth_in)
     fourth_cross = flip(fourth_pair, "head", 3)
+    first_cross = after(first_cross, third_pair, fourth_pair)
+    second_cross = after(second_cross, third_pair, fourth_pair)
     first_sum = add(first_pair, first_cross)
     first_other = flip(first_sum, "head", 1)
     second_sum = add(second_pair, second_cross)

time: 68.5 us -> 68.1 us (level); the launches traced: 69 us -> 67.6 us
  Pallas kernels: 26.5 us -> 23.9 us
  starting transfers between devices: 26.8 us -> 29.4 us
  waiting for transfers between devices: 14.3 us -> 12.9 us
    pallas_call x2, Pallas kernels: 16.8 us -> 14.2 us  [attend(): pl.pallas_call(functools.partial(attend_kernel, sizes, scale, relative, b...]
    ppermute x21, starting transfers between devices: 26.8 us -> 29.4 us  [flip(): return lax.ppermute(x, axis, [(i, i ^ distance) for i in range(size)])]
    ppermute x21, waiting for transfers between devices: 14.3 us -> 12.9 us  [flip(): return lax.ppermute(x, axis, [(i, i ^ distance) for i in range(size)])]
  transfers between devices with their start and end apart: 21 -> 21, of which waited for: 6 -> 8; matrix products, arithmetic and copies ran while one was open for 0% -> 0% of each run, Pallas kernels for 33% -> 29%
where the time goes in v9:
time: 68.1 us; the launch traced here: 67.6 us
  starting transfers between devices  29.4 us (43%)
  Pallas kernels  23.9 us (35%)
  waiting for transfers between devices  12.9 us (19%)
  local copies, waits for them, and re-layouts  0.82 us (1%)
    ppermute x21, starting transfers between devices, flip(): return lax.ppermute(x, axis, [(i, i ^ distance) for i in range(size)])  29.4 us
    pallas_call x2, Pallas kernels, attend(): pl.pallas_call(functools.partial(attend_kernel, sizes, scale, relative, b...  14.2 us
    ppermute x21, waiting for transfers between devices, flip(): return lax.ppermute(x, axis, [(i, i ^ distance) for i in range(size)])  12.9 us
    pallas_call x4, Pallas kernels, project(): pl.pallas_call(functools.partial(project_kernel, piece * cols), out_shape...  5.7 us
    pallas_call x1, Pallas kernels, order(): pl.pallas_call(kernel, out_shape=jax.ShapeDtypeStruct((steps, sources * r...  1.75 us
  transfers between devices with their start and end apart: 21, of which 8 were waited for; matrix products, arithmetic and copies ran while one was open for 0% of the time, Pallas kernels for 29%

profile of v9, /device:TPU:0, one launch (start us, length us, event | category | flops | bytes accessed | tf_op | source)
XLA Modules:
  0.0 67.6 jit_solution(2076201841819545460)
XLA Ops:
  0.0 0.7 %copy-done.6 = s32[64]{0:T(128)S(1)} copy-done((s32[64]{0:T(128)S(1)}, s32[64]{0:T(128)}, u32[]{:S(2)}) %copy-start.6) | copy-done | bytes 280
  0.8 1.1 %place_rows.1.after_ref.pick_ref = bf16[4,64,256]{2,1,0:T(8,128)(2,1)S(1)} custom-call(s32[1]{0:T(128)} %bitcast.ids_ref, s32[64]{0:T(128)S(1)} %copy-done.6), custom_call_target="tpu_custom_call" | custom-call | flops 2000000000 | bytes 6000000 | tf_op jit(solution)/shard_map/place_rows/pallas_call | solution.py:392
  1.9 0.0 slice-start.5
  1.9 0.0 copy-start
  1.9 0.0 copy-start.1
  1.9 0.0 copy-start.5
  1.9 0.0 copy-start.7
  1.9 1.1 %pack_queries.1 = (bf16[1,848,128]{2,1,0:T(8,128)(2,1)S(1)}, bf16[1,848,128]{2,1,0:T(8,128)(2,1)S(1)}, bf16[1,848,128]{2,1,0:T(8,128)(2,1)S(1)}, bf16[1,848,128]{2,1,0:T(8,128)(2,1)S(1)}) custom-call(s32[1]{0:T(128)} %bitcast.ids_ref, s32[64]{0:T(128)S(1)} %copy-done.6, bf16[4,16,32,128]{3,2,1,0:T(8,128)(2,1)S(1)} %copy-done.2, ...), custom_call_target="tpu_custom_call" | custom-call | flops 6000000000 | bytes 18000000 | tf_op jit(solution)/shard_map/pack_queries/pallas_call | solution.py:404
  3.1 0.5 collective-permute-start
  3.6 2.6 %collective-permute-start.3 = (bf16[1,848,128]{2,1,0:T(8,128)(2,1)S(1)}, bf16[1,848,128]{2,1,0:T(8,128)(2,1)S(1)}, u32[]{:S(2)}, u32[]{:S(2)}) collective-permute-start(bf16[1,848,128]{2,1,0:T(8,128)(2,1)S(1)} %get-tuple-element.23), channel_id=1, source_target_pairs={{0,8},{4,12},{8,0},{12,4},{1,9},{5,13},{9,1},{13,5},{2,10},{6,14},... | collective-permute-start | bytes 651272 | tf_op jit(solution)/shard_map/ppermute | solution.py:368
  6.2 0.1 collective-permute-start.4
  6.3 0.0 collective-permute-done.rest_1_
  6.3 0.0 slice-start
  6.3 0.0 slice-start.1
  6.4 7.1 %attend.2.rest_0_ = bf16[32,4096]{1,0:T(8,128)(2,1)S(1)} custom-call(s32[1]{0:T(128)} %bitcast.ids_ref, s32[64]{0:T(128)S(1)} %copy-done.7, s32[4,16]{1,0:T(4,128)S(1)} %copy-done.5, bf16[1,848,128]{2,1,0:T(8,128)(2,1)S(1)} %get-tuple-element.21.rest_0_, bf16[1,848,128]{2,1,0:T(8,128)(2,1)S(1)} %collective-permute-done.rest_1_, ...), custom_call_target="tpu_custom_call" | custom-call | flops 8000000000 | bytes 24000000 | tf_op jit(solution)/shard_map/attend/pallas_call | solution.py:422
  13.4 0.0 slice-start.2
  13.5 2.6 %collective-permute-start.2 = (bf16[32,4096]{1,0:T(8,128)(2,1)S(1)}, bf16[32,4096]{1,0:T(8,128)(2,1)S(1)}, u32[]{:S(2)}, u32[]{:S(2)}) collective-permute-start(bf16[32,4096]{1,0:T(8,128)(2,1)S(1)} %attend.2.rest_0_), channel_id=1, source_target_pairs={{0,8},{4,12},{8,0},{12,4},{1,9},{5,13},{9,1},{13,5},{2,10},{6,14},... | collective-permute-start | bytes 786440 | tf_op jit(solution)/shard_map/ppermute | solution.py:368
  16.1 0.5 collective-permute-done.4.rest_1_
  16.5 7.2 %attend.3.rest_0_ = bf16[32,4096]{1,0:T(8,128)(2,1)S(1)} custom-call(s32[1]{0:T(128)} %bitcast.ids_ref, s32[64]{0:T(128)S(1)} %copy-done.7, s32[4,16]{1,0:T(4,128)S(1)} %copy-done.5, bf16[1,848,128]{2,1,0:T(8,128)(2,1)S(1)} %collective-permute-done.3.rest_0_, bf16[1,848,128]{2,1,0:T(8,128)(2,1)S(1)} %collective-permute-done.4.rest_1_, ...), custom_call_target="tpu_custom_call" | custom-call | flops 8000000000 | bytes 24000000 | tf_op jit(solution)/shard_map/attend/pallas_call | solution.py:422
  23.7 0.2 collective-permute-start.5
  23.9 1.8 %collective-permute-start.9 = (bf16[32,4096]{1,0:T(8,128)(2,1)S(1)}, bf16[32,4096]{1,0:T(8,128)(2,1)S(1)}, u32[]{:S(2)}, u32[]{:S(2)}) collective-permute-start(bf16[32,4096]{1,0:T(8,128)(2,1)S(1)} %attend.3.rest_0_), channel_id=1, source_target_pairs={{0,8},{4,12},{8,0},{12,4},{1,9},{5,13},{9,1},{13,5},{2,10},{6,14},... | collective-permute-start | bytes 786440 | tf_op jit(solution)/shard_map/ppermute | solution.py:368
  25.7 1.4 %project_out.7 = (bf16[64,896]{1,0:T(8,128)(2,1)S(1)}, bf16[64,896]{1,0:T(8,128)(2,1)S(1)}) custom-call(s32[1]{0:T(128)} %bitcast.ids_ref, bf16[32,4096]{1,0:T(8,128)(2,1)S(1)} %attend.2.rest_0_, bf16[32,4096]{1,0:T(8,128)(2,1)S(1)} %collective-permute-done.1.rest_1_, bf16[32,4096]{1,0:T(8,128)(2,1)S(1)} %collective-permute-done.2.rest_2_, ...), custom_call_target="tpu_custom_call" | custom-call | flops 2000000000 | bytes 6000000 | tf_op jit(solution)/shard_map/project_out/pallas_call | solution.py:474
  27.1 1.6 %collective-permute-start.14 = (bf16[64,896]{1,0:T(8,128)(2,1)S(1)}, bf16[64,896]{1,0:T(8,128)(2,1)S(1)}, u32[]{:S(2)}, u32[]{:S(2)}) collective-permute-start(bf16[64,896]{1,0:T(8,128)(2,1)S(1)} %get-tuple-element.35), channel_id=1, source_target_pairs={{0,1},{1,0},{2,3},{3,2},{4,5},{5,4},{6,7},{7,6},{8,9},{9,8},{10,11... | collective-permute-start | bytes 344072 | tf_op jit(solution)/shard_map/ppermute | solution.py:368
  28.7 1.4 %project_out.4 = (bf16[64,896]{1,0:T(8,128)(2,1)S(1)}, bf16[64,896]{1,0:T(8,128)(2,1)S(1)}) custom-call(s32[1]{0:T(128)} %bitcast.ids_ref, bf16[32,4096]{1,0:T(8,128)(2,1)S(1)} %attend.2.rest_0_, bf16[32,4096]{1,0:T(8,128)(2,1)S(1)} %collective-permute-done.1.rest_1_, bf16[32,4096]{1,0:T(8,128)(2,1)S(1)} %collective-permute-done.2.rest_2_, ...), custom_call_target="tpu_custom_call" | custom-call | flops 2000000000 | bytes 6000000 | tf_op jit(solution)/shard_map/project_out/pallas_call | solution.py:474
  30.1 0.5 collective-permute-start.6
  30.6 1.9 %collective-permute-done.9.rest_2_ = bf16[32,4096]{1,0:T(8,128)(2,1)S(1)} collective-permute-done((bf16[32,4096]{1,0:T(8,128)(2,1)S(1)}, bf16[32,4096]{1,0:T(8,128)(2,1)S(1)}, u32[]{:S(2)}, u32[]{:S(2)}) %collective-permute-start.9) | collective-permute-done | bytes 262176 | tf_op jit(solution)/shard_map/ppermute | solution.py:368
  32.5 0.0 collective-permute-start.10
  32.5 0.2 collective-permute-done.14
  32.8 4.1 %collective-permute-start.15 = (bf16[64,896]{1,0:T(8,128)(2,1)S(1)}, bf16[64,896]{1,0:T(8,128)(2,1)S(1)}, u32[]{:S(2)}, u32[]{:S(2)}) collective-permute-start(bf16[64,896]{1,0:T(8,128)(2,1)S(1)} %add_convert_fusion.3), channel_id=1, source_target_pairs={{0,3},{1,2},{2,1},{3,0},{4,7},{5,6},{6,5},{7,4},{8,11},{9,10},{10,... | collective-permute-start | bytes 344072 | tf_op jit(solution)/shard_map/ppermute | solution.py:368
  36.8 0.0 collective-permute-done.6
  36.8 2.0 %collective-permute-start.7 = (bf16[64,896]{1,0:T(8,128)(2,1)S(1)}, bf16[64,896]{1,0:T(8,128)(2,1)S(1)}, u32[]{:S(2)}, u32[]{:S(2)}) collective-permute-start(bf16[64,896]{1,0:T(8,128)(2,1)S(1)} %add_convert_fusion.7), channel_id=1, source_target_pairs={{0,3},{1,2},{2,1},{3,0},{4,7},{5,6},{6,5},{7,4},{8,11},{9,10},{10,... | collective-permute-start | bytes 344072 | tf_op jit(solution)/shard_map/ppermute | solution.py:368
  38.9 0.0 collective-permute-done.8.rest_1_
  38.9 1.6 %project_out.6 = (bf16[64,896]{1,0:T(8,128)(2,1)S(1)}, bf16[64,896]{1,0:T(8,128)(2,1)S(1)}) custom-call(s32[1]{0:T(128)} %bitcast.ids_ref, bf16[32,4096]{1,0:T(8,128)(2,1)S(1)} %attend.3.rest_0_, bf16[32,4096]{1,0:T(8,128)(2,1)S(1)} %collective-permute-done.8.rest_1_, bf16[32,4096]{1,0:T(8,128)(2,1)S(1)} %collective-permute-done.9.rest_2_, ...), custom_call_target="tpu_custom_call" | custom-call | flops 2000000000 | bytes 6000000 | tf_op jit(solution)/shard_map/project_out/pallas_call | solution.py:474
  40.4 0.1 collective-permute-start.12
  40.5 1.4 %project_out.5 = (bf16[64,896]{1,0:T(8,128)(2,1)S(1)}, bf16[64,896]{1,0:T(8,128)(2,1)S(1)}) custom-call(s32[1]{0:T(128)} %bitcast.ids_ref, bf16[32,4096]{1,0:T(8,128)(2,1)S(1)} %attend.3.rest_0_, bf16[32,4096]{1,0:T(8,128)(2,1)S(1)} %collective-permute-done.8.rest_1_, bf16[32,4096]{1,0:T(8,128)(2,1)S(1)} %collective-permute-done.9.rest_2_, ...), custom_call_target="tpu_custom_call" | custom-call | flops 2000000000 | bytes 6000000 | tf_op jit(solution)/shard_map/project_out/pallas_call | solution.py:474
  41.9 2.1 %collective-permute-start.11 = (bf16[64,896]{1,0:T(8,128)(2,1)S(1)}, bf16[64,896]{1,0:T(8,128)(2,1)S(1)}, u32[]{:S(2)}, u32[]{:S(2)}) collective-permute-start(bf16[64,896]{1,0:T(8,128)(2,1)S(1)} %get-tuple-element.30), channel_id=1, source_target_pairs={{0,1},{1,0},{2,3},{3,2},{4,5},{5,4},{6,7},{7,6},{8,9},{9,8},{10,11... | collective-permute-start | bytes 344072 | tf_op jit(solution)/shard_map/ppermute | solution.py:368
  44.0 2.8 %collective-permute-done.12 = bf16[64,896]{1,0:T(8,128)(2,1)S(1)} collective-permute-done((bf16[64,896]{1,0:T(8,128)(2,1)S(1)}, bf16[64,896]{1,0:T(8,128)(2,1)S(1)}, u32[]{:S(2)}, u32[]{:S(2)}) %collective-permute-start.12) | collective-permute-done | bytes 114720 | tf_op jit(solution)/shard_map/ppermute | solution.py:368
  46.8 2.1 %collective-permute-start.19 = (bf16[64,896]{1,0:T(8,128)(2,1)S(1)}, bf16[64,896]{1,0:T(8,128)(2,1)S(1)}, u32[]{:S(2)}, u32[]{:S(2)}) collective-permute-start(bf16[64,896]{1,0:T(8,128)(2,1)S(1)} %add_convert_fusion.5), channel_id=1, source_target_pairs={{0,3},{1,2},{2,1},{3,0},{4,7},{5,6},{6,5},{7,4},{8,11},{9,10},{10,... | collective-permute-start | bytes 344072 | tf_op jit(solution)/shard_map/ppermute | solution.py:368
  49.0 2.2 %collective-permute-start.17 = (bf16[64,896]{1,0:T(8,128)(2,1)S(1)}, bf16[64,896]{1,0:T(8,128)(2,1)S(1)}, u32[]{:S(2)}, u32[]{:S(2)}) collective-permute-start(bf16[64,896]{1,0:T(8,128)(2,1)S(1)} %add_convert_fusion.6), channel_id=1, source_target_pairs={{0,3},{1,2},{2,1},{3,0},{4,7},{5,6},{6,5},{7,4},{8,11},{9,10},{10,... | collective-permute-start | bytes 344072 | tf_op jit(solution)/shard_map/ppermute | solution.py:368
  51.2 0.1 collective-permute-start.16
  51.3 2.1 %collective-permute-start.13 = (bf16[64,896]{1,0:T(8,128)(2,1)S(1)}, bf16[64,896]{1,0:T(8,128)(2,1)S(1)}, u32[]{:S(2)}, u32[]{:S(2)}) collective-permute-start(bf16[64,896]{1,0:T(8,128)(2,1)S(1)} %add_convert_fusion.4.rest_0_), channel_id=1, source_target_pairs={{0,1},{1,0},{2,3},{3,2},{4,5},{5,4},{6,7},{7,6},{8,9},{9,8},{10,11... | collective-permute-start | bytes 344072 | tf_op jit(solution)/shard_map/ppermute | solution.py:368
  53.4 0.9 %collective-permute-done.19 = bf16[64,896]{1,0:T(8,128)(2,1)S(1)} collective-permute-done((bf16[64,896]{1,0:T(8,128)(2,1)S(1)}, bf16[64,896]{1,0:T(8,128)(2,1)S(1)}, u32[]{:S(2)}, u32[]{:S(2)}) %collective-permute-start.19) | collective-permute-done | bytes 114720 | tf_op jit(solution)/shard_map/ppermute | solution.py:368
  54.3 3.6 %collective-permute-start.20 = (bf16[64,896]{1,0:T(8,128)(2,1)S(1)}, bf16[64,896]{1,0:T(8,128)(2,1)S(1)}, u32[]{:S(2)}, u32[]{:S(2)}) collective-permute-start(bf16[64,896]{1,0:T(8,128)(2,1)S(1)} %add_convert_fusion.rest_6_), channel_id=1, source_target_pairs={{0,1},{1,0},{2,3},{3,2},{4,5},{5,4},{6,7},{7,6},{8,9},{9,8},{10,11... | collective-permute-start | bytes 344072 | tf_op jit(solution)/shard_map/ppermute | solution.py:368
  57.9 1.2 %collective-permute-start.18 = (bf16[64,896]{1,0:T(8,128)(2,1)S(1)}, bf16[64,896]{1,0:T(8,128)(2,1)S(1)}, u32[]{:S(2)}, u32[]{:S(2)}) collective-permute-start(bf16[64,896]{1,0:T(8,128)(2,1)S(1)} %add_convert_fusion.1.rest_4_), channel_id=1, source_target_pairs={{0,1},{1,0},{2,3},{3,2},{4,5},{5,4},{6,7},{7,6},{8,9},{9,8},{10,11... | collective-permute-start | bytes 344072 | tf_op jit(solution)/shard_map/ppermute | solution.py:368
  59.1 1.9 %collective-permute-done.13.rest_1_ = bf16[64,896]{1,0:T(8,128)(2,1)S(1)} collective-permute-done((bf16[64,896]{1,0:T(8,128)(2,1)S(1)}, bf16[64,896]{1,0:T(8,128)(2,1)S(1)}, u32[]{:S(2)}, u32[]{:S(2)}) %collective-permute-start.13) | collective-permute-done | bytes 114720 | tf_op jit(solution)/shard_map/ppermute | solution.py:368
  61.0 2.5 %collective-permute-done.20.rest_7_ = bf16[64,896]{1,0:T(8,128)(2,1)S(1)} collective-permute-done((bf16[64,896]{1,0:T(8,128)(2,1)S(1)}, bf16[64,896]{1,0:T(8,128)(2,1)S(1)}, u32[]{:S(2)}, u32[]{:S(2)}) %collective-permute-start.20) | collective-permute-done | bytes 114720 | tf_op jit(solution)/shard_map/ppermute | solution.py:368
  63.5 2.4 %collective-permute-done.18.rest_5_ = bf16[64,896]{1,0:T(8,128)(2,1)S(1)} collective-permute-done((bf16[64,896]{1,0:T(8,128)(2,1)S(1)}, bf16[64,896]{1,0:T(8,128)(2,1)S(1)}, u32[]{:S(2)}, u32[]{:S(2)}) %collective-permute-start.18) | collective-permute-done | bytes 114720 | tf_op jit(solution)/shard_map/ppermute | solution.py:368
  65.8 1.7 %order_rows.1 = bf16[4,64,1792]{2,1,0:T(8,128)(2,1)} custom-call(s32[1]{0:T(128)} %bitcast.ids_ref, bf16[4,64,256]{2,1,0:T(8,128)(2,1)S(1)} %place_rows.1.after_ref.pick_ref, bf16[64,896]{1,0:T(8,128)(2,1)S(1)} %add_convert_fusion.4.rest_0_, bf16[64,896]{1,0:T(8,128)(2,1)S(1)} %collective-permute-done.13.rest_1_, ...), custom_call_target="tpu_custom_call" | custom-call | flops 2000000000 | bytes 6000000 | tf_op jit(solution)/shard_map/order_rows/pallas_call | solution.py:448
  (41 shorter events, 0.3 us)
Async XLA Ops:
  0.0 1.8 %copy-start.2 = (bf16[4,16,32,128]{3,2,1,0:T(8,128)(2,1)S(1)}, bf16[4,16,32,128]{3,2,1,0:T(8,128)(2,1)}, u32[]{:S(2)}) copy-start(bf16[4,16,32,128]{3,2,1,0:T(8,128)(2,1)} %nope_ref.1) | copy-start | bytes 1572868
  0.0 1.9 %copy-start.3 = (bf16[4,16,32,64]{3,2,1,0:T(8,128)(2,1)S(1)}, bf16[4,16,32,64]{3,2,1,0:T(8,128)(2,1)}, u32[]{:S(2)}) copy-start(bf16[4,16,32,64]{3,2,1,0:T(8,128)(2,1)} %rope_ref.1) | copy-start | bytes 786436
  0.0 1.9 %copy-start.4 = (bf16[4,16,576]{2,1,0:T(8,128)(2,1)S(1)}, bf16[4,16,576]{2,1,0:T(8,128)(2,1)}, u32[]{:S(2)}) copy-start(bf16[4,16,576]{2,1,0:T(8,128)(2,1)} %fresh_ref.1) | copy-start | bytes 221188
  0.0 0.7 %copy-start.6 = (s32[64]{0:T(128)S(1)}, s32[64]{0:T(128)}, u32[]{:S(2)}) copy-start(s32[64]{0:T(128)} %decode_ref.7) | copy-start | bytes 772
  0.8 5.5 %slice-start.4 = ((s8[4718592]{0:T(1024)(128)(4,1)}), s8[4194304]{0:T(1024)(128)(4,1)S(1)}, s32[]{:S(2)}) async-start(s8[4718592]{0:T(1024)(128)(4,1)} %bitcast.4), calls=%async_computation.4 | async-start | bytes 8388608
  1.9 4.4 %slice-start.5 = ((s8[4718592]{0:T(1024)(128)(4,1)}), s8[524288]{0:T(1024)(128)(4,1)S(1)}, s32[]{:S(2)}) async-start(s8[4718592]{0:T(1024)(128)(4,1)} %bitcast.4), calls=%async_computation.5 | async-start | bytes 1048576
  1.9 4.4 %copy-start = (bf16[32,128,512]{2,1,0:T(8,128)(2,1)S(1)}, bf16[32,128,512]{2,1,0:T(8,128)(2,1)}, u32[]{:S(2)}) copy-start(bf16[32,128,512]{2,1,0:T(8,128)(2,1)} %rest_3_.3) | copy-start | bytes 12582916
  1.9 4.4 %copy-start.1 = (bf16[32,512,128]{2,1,0:T(8,128)(2,1)S(1)}, bf16[32,512,128]{2,1,0:T(8,128)(2,1)}, u32[]{:S(2)}) copy-start(bf16[32,512,128]{2,1,0:T(8,128)(2,1)} %rest_4_.7) | copy-start | bytes 12582916
  1.9 4.4 %copy-start.5 = (s32[4,16]{1,0:T(4,128)S(1)}, s32[4,16]{1,0:T(4,128)}, u32[]{:S(2)}) copy-start(s32[4,16]{1,0:T(4,128)} %length_ref.3) | copy-start | bytes 772
  1.9 4.4 %copy-start.7 = (s32[64]{0:T(128)S(1)}, s32[64]{0:T(128)}, u32[]{:S(2)}) copy-start(s32[64]{0:T(128)} %decode_ref.7) | copy-start | bytes 772
  3.1 3.2 %collective-permute-start = (bf16[1,848,128]{2,1,0:T(8,128)(2,1)S(1)}, bf16[1,848,128]{2,1,0:T(8,128)(2,1)S(1)}, u32[]{:S(2)}, u32[]{:S(2)}) collective-permute-start(bf16[1,848,128]{2,1,0:T(8,128)(2,1)S(1)} %get-tuple-element.22), channel_id=1, source_target_pairs={{0,4},{4,0},{8,12},{12,8},{1,5},{5,1},{9,13},{13,9},{2,6},{6,2},{1... | collective-permute-start | bytes 651272 | tf_op jit(solution)/shard_map/ppermute | solution.py:368
  3.6 12.4 %collective-permute-start.3 = (bf16[1,848,128]{2,1,0:T(8,128)(2,1)S(1)}, bf16[1,848,128]{2,1,0:T(8,128)(2,1)S(1)}, u32[]{:S(2)}, u32[]{:S(2)}) collective-permute-start(bf16[1,848,128]{2,1,0:T(8,128)(2,1)S(1)} %get-tuple-element.23), channel_id=1, source_target_pairs={{0,8},{4,12},{8,0},{12,4},{1,9},{5,13},{9,1},{13,5},{2,10},{6,14},... | collective-permute-start | bytes 651272 | tf_op jit(solution)/shard_map/ppermute | solution.py:368
  6.2 10.3 %collective-permute-start.4 = (bf16[1,848,128]{2,1,0:T(8,128)(2,1)S(1)}, bf16[1,848,128]{2,1,0:T(8,128)(2,1)S(1)}, u32[]{:S(2)}, u32[]{:S(2)}) collective-permute-start(bf16[1,848,128]{2,1,0:T(8,128)(2,1)S(1)} %get-tuple-element.24), channel_id=1, source_target_pairs={{0,12},{4,8},{8,4},{12,0},{1,13},{5,9},{9,5},{13,1},{2,14},{6,10},... | collective-permute-start | bytes 651272 | tf_op jit(solution)/shard_map/ppermute | solution.py:368
  6.3 19.3 %slice-start = ((s8[14680064]{0:T(1024)(128)(4,1)}), s8[4194304]{0:T(1024)(128)(4,1)S(1)}, s32[]{:S(2)}) async-start(s8[14680064]{0:T(1024)(128)(4,1)} %bitcast.2), calls=%async_computation | async-start | bytes 8388608
  6.3 19.3 %slice-start.1 = ((s8[14680064]{0:T(1024)(128)(4,1)}), s8[4194304]{0:T(1024)(128)(4,1)S(1)}, s32[]{:S(2)}) async-start(s8[14680064]{0:T(1024)(128)(4,1)} %bitcast.2), calls=%async_computation.1 | async-start | bytes 8388608
  13.4 12.2 %slice-start.2 = ((s8[14680064]{0:T(1024)(128)(4,1)}), s8[4194304]{0:T(1024)(128)(4,1)S(1)}, s32[]{:S(2)}) async-start(s8[14680064]{0:T(1024)(128)(4,1)} %bitcast.2), calls=%async_computation.2 | async-start | bytes 8388608
  13.5 12.2 %slice-start.3 = ((s8[14680064]{0:T(1024)(128)(4,1)}), s8[2097152]{0:T(1024)(128)(4,1)S(1)}, s32[]{:S(2)}) async-start(s8[14680064]{0:T(1024)(128)(4,1)} %bitcast.2), calls=%async_computation.3 | async-start | bytes 4194304
  13.5 10.2 %collective-permute-start.2 = (bf16[32,4096]{1,0:T(8,128)(2,1)S(1)}, bf16[32,4096]{1,0:T(8,128)(2,1)S(1)}, u32[]{:S(2)}, u32[]{:S(2)}) collective-permute-start(bf16[32,4096]{1,0:T(8,128)(2,1)S(1)} %attend.2.rest_0_), channel_id=1, source_target_pairs={{0,8},{4,12},{8,0},{12,4},{1,9},{5,13},{9,1},{13,5},{2,10},{6,14},... | collective-permute-start | bytes 786440 | tf_op jit(solution)/shard_map/ppermute | solution.py:368
  16.0 9.6 %collective-permute-start.1 = (bf16[32,4096]{1,0:T(8,128)(2,1)S(1)}, bf16[32,4096]{1,0:T(8,128)(2,1)S(1)}, u32[]{:S(2)}, u32[]{:S(2)}) collective-permute-start(bf16[32,4096]{1,0:T(8,128)(2,1)S(1)} %attend.2.rest_0_), channel_id=1, source_target_pairs={{0,4},{4,0},{8,12},{12,8},{1,5},{5,1},{9,13},{13,9},{2,6},{6,2},{1... | collective-permute-start | bytes 786440 | tf_op jit(solution)/shard_map/ppermute | solution.py:368
  23.7 2.0 %collective-permute-start.5 = (bf16[32,4096]{1,0:T(8,128)(2,1)S(1)}, bf16[32,4096]{1,0:T(8,128)(2,1)S(1)}, u32[]{:S(2)}, u32[]{:S(2)}) collective-permute-start(bf16[32,4096]{1,0:T(8,128)(2,1)S(1)} %collective-permute-done.2.rest_2_), channel_id=1, source_target_pairs={{0,4},{4,0},{8,12},{12,8},{1,5},{5,1},{9,13},{13,9},{2,6},{6,2},{1... | collective-permute-start | bytes 786440 | tf_op jit(solution)/shard_map/ppermute | solution.py:368
  23.9 8.6 %collective-permute-start.9 = (bf16[32,4096]{1,0:T(8,128)(2,1)S(1)}, bf16[32,4096]{1,0:T(8,128)(2,1)S(1)}, u32[]{:S(2)}, u32[]{:S(2)}) collective-permute-start(bf16[32,4096]{1,0:T(8,128)(2,1)S(1)} %attend.3.rest_0_), channel_id=1, source_target_pairs={{0,8},{4,12},{8,0},{12,4},{1,9},{5,13},{9,1},{13,5},{2,10},{6,14},... | collective-permute-start | bytes 786440 | tf_op jit(solution)/shard_map/ppermute | solution.py:368
  25.6 13.2 %collective-permute-start.8 = (bf16[32,4096]{1,0:T(8,128)(2,1)S(1)}, bf16[32,4096]{1,0:T(8,128)(2,1)S(1)}, u32[]{:S(2)}, u32[]{:S(2)}) collective-permute-start(bf16[32,4096]{1,0:T(8,128)(2,1)S(1)} %attend.3.rest_0_), channel_id=1, source_target_pairs={{0,4},{4,0},{8,12},{12,8},{1,5},{5,1},{9,13},{13,9},{2,6},{6,2},{1... | collective-permute-start | bytes 786440 | tf_op jit(solution)/shard_map/ppermute | solution.py:368
  27.1 5.6 %collective-permute-start.14 = (bf16[64,896]{1,0:T(8,128)(2,1)S(1)}, bf16[64,896]{1,0:T(8,128)(2,1)S(1)}, u32[]{:S(2)}, u32[]{:S(2)}) collective-permute-start(bf16[64,896]{1,0:T(8,128)(2,1)S(1)} %get-tuple-element.35), channel_id=1, source_target_pairs={{0,1},{1,0},{2,3},{3,2},{4,5},{5,4},{6,7},{7,6},{8,9},{9,8},{10,11... | collective-permute-start | bytes 344072 | tf_op jit(solution)/shard_map/ppermute | solution.py:368
  30.1 6.7 %collective-permute-start.6 = (bf16[64,896]{1,0:T(8,128)(2,1)S(1)}, bf16[64,896]{1,0:T(8,128)(2,1)S(1)}, u32[]{:S(2)}, u32[]{:S(2)}) collective-permute-start(bf16[64,896]{1,0:T(8,128)(2,1)S(1)} %get-tuple-element.27), channel_id=1, source_target_pairs={{0,1},{1,0},{2,3},{3,2},{4,5},{5,4},{6,7},{7,6},{8,9},{9,8},{10,11... | collective-permute-start | bytes 344072 | tf_op jit(solution)/shard_map/ppermute | solution.py:368
  32.5 6.4 %collective-permute-start.10 = (bf16[32,4096]{1,0:T(8,128)(2,1)S(1)}, bf16[32,4096]{1,0:T(8,128)(2,1)S(1)}, u32[]{:S(2)}, u32[]{:S(2)}) collective-permute-start(bf16[32,4096]{1,0:T(8,128)(2,1)S(1)} %collective-permute-done.9.rest_2_), channel_id=1, source_target_pairs={{0,4},{4,0},{8,12},{12,8},{1,5},{5,1},{9,13},{13,9},{2,6},{6,2},{1... | collective-permute-start | bytes 786440 | tf_op jit(solution)/shard_map/ppermute | solution.py:368
  32.8 18.4 %collective-permute-start.15 = (bf16[64,896]{1,0:T(8,128)(2,1)S(1)}, bf16[64,896]{1,0:T(8,128)(2,1)S(1)}, u32[]{:S(2)}, u32[]{:S(2)}) collective-permute-start(bf16[64,896]{1,0:T(8,128)(2,1)S(1)} %add_convert_fusion.3), channel_id=1, source_target_pairs={{0,3},{1,2},{2,1},{3,0},{4,7},{5,6},{6,5},{7,4},{8,11},{9,10},{10,... | collective-permute-start | bytes 344072 | tf_op jit(solution)/shard_map/ppermute | solution.py:368
  36.8 14.4 %collective-permute-start.7 = (bf16[64,896]{1,0:T(8,128)(2,1)S(1)}, bf16[64,896]{1,0:T(8,128)(2,1)S(1)}, u32[]{:S(2)}, u32[]{:S(2)}) collective-permute-start(bf16[64,896]{1,0:T(8,128)(2,1)S(1)} %add_convert_fusion.7), channel_id=1, source_target_pairs={{0,3},{1,2},{2,1},{3,0},{4,7},{5,6},{6,5},{7,4},{8,11},{9,10},{10,... | collective-permute-start | bytes 344072 | tf_op jit(solution)/shard_map/ppermute | solution.py:368
  40.4 6.3 %collective-permute-start.12 = (bf16[64,896]{1,0:T(8,128)(2,1)S(1)}, bf16[64,896]{1,0:T(8,128)(2,1)S(1)}, u32[]{:S(2)}, u32[]{:S(2)}) collective-permute-start(bf16[64,896]{1,0:T(8,128)(2,1)S(1)} %get-tuple-element.32), channel_id=1, source_target_pairs={{0,1},{1,0},{2,3},{3,2},{4,5},{5,4},{6,7},{7,6},{8,9},{9,8},{10,11... | collective-permute-start | bytes 344072 | tf_op jit(solution)/shard_map/ppermute | solution.py:368
  41.9 7.0 %collective-permute-start.11 = (bf16[64,896]{1,0:T(8,128)(2,1)S(1)}, bf16[64,896]{1,0:T(8,128)(2,1)S(1)}, u32[]{:S(2)}, u32[]{:S(2)}) collective-permute-start(bf16[64,896]{1,0:T(8,128)(2,1)S(1)} %get-tuple-element.30), channel_id=1, source_target_pairs={{0,1},{1,0},{2,3},{3,2},{4,5},{5,4},{6,7},{7,6},{8,9},{9,8},{10,11... | collective-permute-start | bytes 344072 | tf_op jit(solution)/shard_map/ppermute | solution.py:368
  46.8 7.5 %collective-permute-start.19 = (bf16[64,896]{1,0:T(8,128)(2,1)S(1)}, bf16[64,896]{1,0:T(8,128)(2,1)S(1)}, u32[]{:S(2)}, u32[]{:S(2)}) collective-permute-start(bf16[64,896]{1,0:T(8,128)(2,1)S(1)} %add_convert_fusion.5), channel_id=1, source_target_pairs={{0,3},{1,2},{2,1},{3,0},{4,7},{5,6},{6,5},{7,4},{8,11},{9,10},{10,... | collective-permute-start | bytes 344072 | tf_op jit(solution)/shard_map/ppermute | solution.py:368
  49.0 8.9 %collective-permute-start.17 = (bf16[64,896]{1,0:T(8,128)(2,1)S(1)}, bf16[64,896]{1,0:T(8,128)(2,1)S(1)}, u32[]{:S(2)}, u32[]{:S(2)}) collective-permute-start(bf16[64,896]{1,0:T(8,128)(2,1)S(1)} %add_convert_fusion.6), channel_id=1, source_target_pairs={{0,3},{1,2},{2,1},{3,0},{4,7},{5,6},{6,5},{7,4},{8,11},{9,10},{10,... | collective-permute-start | bytes 344072 | tf_op jit(solution)/shard_map/ppermute | solution.py:368
  51.2 7.9 %collective-permute-start.16 = (bf16[64,896]{1,0:T(8,128)(2,1)S(1)}, bf16[64,896]{1,0:T(8,128)(2,1)S(1)}, u32[]{:S(2)}, u32[]{:S(2)}) collective-permute-start(bf16[64,896]{1,0:T(8,128)(2,1)S(1)} %add_convert_fusion.2.rest_2_), channel_id=1, source_target_pairs={{0,1},{1,0},{2,3},{3,2},{4,5},{5,4},{6,7},{7,6},{8,9},{9,8},{10,11... | collective-permute-start | bytes 344072 | tf_op jit(solution)/shard_map/ppermute | solution.py:368
  51.3 9.7 %collective-permute-start.13 = (bf16[64,896]{1,0:T(8,128)(2,1)S(1)}, bf16[64,896]{1,0:T(8,128)(2,1)S(1)}, u32[]{:S(2)}, u32[]{:S(2)}) collective-permute-start(bf16[64,896]{1,0:T(8,128)(2,1)S(1)} %add_convert_fusion.4.rest_0_), channel_id=1, source_target_pairs={{0,1},{1,0},{2,3},{3,2},{4,5},{5,4},{6,7},{7,6},{8,9},{9,8},{10,11... | collective-permute-start | bytes 344072 | tf_op jit(solution)/shard_map/ppermute | solution.py:368
  54.3 9.2 %collective-permute-start.20 = (bf16[64,896]{1,0:T(8,128)(2,1)S(1)}, bf16[64,896]{1,0:T(8,128)(2,1)S(1)}, u32[]{:S(2)}, u32[]{:S(2)}) collective-permute-start(bf16[64,896]{1,0:T(8,128)(2,1)S(1)} %add_convert_fusion.rest_6_), channel_id=1, source_target_pairs={{0,1},{1,0},{2,3},{3,2},{4,5},{5,4},{6,7},{7,6},{8,9},{9,8},{10,11... | collective-permute-start | bytes 344072 | tf_op jit(solution)/shard_map/ppermute | solution.py:368
  57.9 7.9 %collective-permute-start.18 = (bf16[64,896]{1,0:T(8,128)(2,1)S(1)}, bf16[64,896]{1,0:T(8,128)(2,1)S(1)}, u32[]{:S(2)}, u32[]{:S(2)}) collective-permute-start(bf16[64,896]{1,0:T(8,128)(2,1)S(1)} %add_convert_fusion.1.rest_4_), channel_id=1, source_target_pairs={{0,1},{1,0},{2,3},{3,2},{4,5},{5,4},{6,7},{7,6},{8,9},{9,8},{10,11... | collective-permute-start | bytes 344072 | tf_op jit(solution)/shard_map/ppermute | solution.py:368

commit v10 on v9

--- a/solution.py
+++ b/solution.py
@@ -502,22 +502,25 @@
     far = [far_rows, flip(far_rows, "seq", 1), far_across, flip(far_across, "seq", 1)]
     first_pair = add(first[0], first_in)
     first_cross = flip(first_pair, "head", 3)
-    second_pair = add(second[0], second_in)
-    second_cross = flip(second_pair, "head", 3)
     third = project(far, 0)
     third_in = swap(third)
     fourth = project(far, 1)
     fourth_in = swap(fourth)
+    second_in = after(second_in, third[0])
+    second_pair = add(second[0], second_in)
+    second_cross = flip(second_pair, "head", 3)
+    first_cross = after(first_cross, fourth[0])
+    first_sum = add(first_pair, first_cross)
+    first_other = flip(first_sum, "head", 1)
+    third_in = after(third_in, second_pair)
     third_pair = add(third[0], third_in)
     third_cross = flip(third_pair, "head", 3)
+    second_cross = after(second_cross, third_pair)
+    second_sum = add(second_pair, second_cross)
+    second_other = flip(second_sum, "head", 1)
+    fourth_in = after(fourth_in, second_sum)
     fourth_pair = add(fourth[0], fourth_in)
     fourth_cross = flip(fourth_pair, "head", 3)
-    first_cross = after(first_cross, third_pair, fourth_pair)
-    second_cross = after(second_cross, third_pair, fourth_pair)
-    first_sum = add(first_pair, first_cross)
-    first_other = flip(first_sum, "head", 1)
-    second_sum = add(second_pair, second_cross)
-    second_other = flip(second_sum, "head", 1)
     third_sum = add(third_pair, third_cross)
     third_other = flip(third_sum, "head", 1)
     fourth_sum = add(fourth_pair, fourth_cross)

time: 68.1 us -> 68.5 us (level)
  waiting for transfers between devices: 12.9 us -> 21.4 us
  starting transfers between devices: 29.4 us -> 22.6 us
  Pallas kernels: 23.9 us -> 22.9 us
    ppermute x21, waiting for transfers between devices: 12.9 us -> 21.4 us  [flip(): return lax.ppermute(x, axis, [(i, i ^ distance) for i in range(size)])]
    ppermute x21, starting transfers between devices: 29.4 us -> 22.6 us  [flip(): return lax.ppermute(x, axis, [(i, i ^ distance) for i in range(size)])]
    pallas_call x2, Pallas kernels: 14.2 us -> 13.3 us  [attend(): pl.pallas_call(functools.partial(attend_kernel, sizes, scale, relative, b...]
  transfers between devices with their start and end apart: 21 -> 21, of which waited for: 8 -> 8; matrix products, arithmetic and copies ran while one was open for 0% -> 0% of each run, Pallas kernels for 29% -> 28%
where the time goes in v10:
time: 68.5 us; the launch traced here: 68.4 us
  Pallas kernels  22.9 us (33%)
  starting transfers between devices  22.6 us (33%)
  waiting for transfers between devices  21.4 us (31%)
  local copies, waits for them, and re-layouts  0.82 us (1%)
    ppermute x21, starting transfers between devices, flip(): return lax.ppermute(x, axis, [(i, i ^ distance) for i in range(size)])  22.6 us
    ppermute x21, waiting for transfers between devices, flip(): return lax.ppermute(x, axis, [(i, i ^ distance) for i in range(size)])  21.4 us
    pallas_call x2, Pallas kernels, attend(): pl.pallas_call(functools.partial(attend_kernel, sizes, scale, relative, b...  13.3 us
    pallas_call x4, Pallas kernels, project(): pl.pallas_call(functools.partial(project_kernel, piece * cols), out_shape...  5.68 us
    pallas_call x1, Pallas kernels, order(): pl.pallas_call(kernel, out_shape=jax.ShapeDtypeStruct((steps, sources * r...  1.75 us
  transfers between devices with their start and end apart: 21, of which 8 were waited for; matrix products, arithmetic and copies ran while one was open for 0% of the time, Pallas kernels for 28%

profile of v10, /device:TPU:0, one launch (start us, length us, event | category | flops | bytes accessed | tf_op | source)
XLA Modules:
  0.0 68.4 jit_solution(4830782615600139595)
XLA Ops:
  0.0 0.7 %copy-done.6 = s32[64]{0:T(128)S(1)} copy-done((s32[64]{0:T(128)S(1)}, s32[64]{0:T(128)}, u32[]{:S(2)}) %copy-start.6) | copy-done | bytes 280
  0.8 1.1 %place_rows.1.after_ref.pick_ref = bf16[4,64,256]{2,1,0:T(8,128)(2,1)S(1)} custom-call(s32[1]{0:T(128)} %bitcast.ids_ref, s32[64]{0:T(128)S(1)} %copy-done.6), custom_call_target="tpu_custom_call" | custom-call | flops 2000000000 | bytes 6000000 | tf_op jit(solution)/shard_map/place_rows/pallas_call | solution.py:392
  1.9 0.0 slice-start.5
  1.9 0.0 copy-start
  1.9 0.0 copy-start.1
  1.9 0.0 copy-start.5
  1.9 0.0 copy-start.7
  1.9 1.1 %pack_queries.1 = (bf16[1,848,128]{2,1,0:T(8,128)(2,1)S(1)}, bf16[1,848,128]{2,1,0:T(8,128)(2,1)S(1)}, bf16[1,848,128]{2,1,0:T(8,128)(2,1)S(1)}, bf16[1,848,128]{2,1,0:T(8,128)(2,1)S(1)}) custom-call(s32[1]{0:T(128)} %bitcast.ids_ref, s32[64]{0:T(128)S(1)} %copy-done.6, bf16[4,16,32,128]{3,2,1,0:T(8,128)(2,1)S(1)} %copy-done.2, ...), custom_call_target="tpu_custom_call" | custom-call | flops 6000000000 | bytes 18000000 | tf_op jit(solution)/shard_map/pack_queries/pallas_call | solution.py:404
  3.1 0.5 collective-permute-start
  3.6 2.6 %collective-permute-start.3 = (bf16[1,848,128]{2,1,0:T(8,128)(2,1)S(1)}, bf16[1,848,128]{2,1,0:T(8,128)(2,1)S(1)}, u32[]{:S(2)}, u32[]{:S(2)}) collective-permute-start(bf16[1,848,128]{2,1,0:T(8,128)(2,1)S(1)} %get-tuple-element.26), channel_id=1, source_target_pairs={{0,8},{4,12},{8,0},{12,4},{1,9},{5,13},{9,1},{13,5},{2,10},{6,14},... | collective-permute-start | bytes 651272 | tf_op jit(solution)/shard_map/ppermute | solution.py:368
  6.2 0.1 collective-permute-start.4
  6.3 0.0 collective-permute-done.rest_1_
  6.3 0.0 slice-start
  6.3 0.0 slice-start.1
  6.4 6.2 %attend.2.rest_0_ = bf16[32,4096]{1,0:T(8,128)(2,1)S(1)} custom-call(s32[1]{0:T(128)} %bitcast.ids_ref, s32[64]{0:T(128)S(1)} %copy-done.7, s32[4,16]{1,0:T(4,128)S(1)} %copy-done.5, bf16[1,848,128]{2,1,0:T(8,128)(2,1)S(1)} %get-tuple-element.24.rest_0_, bf16[1,848,128]{2,1,0:T(8,128)(2,1)S(1)} %collective-permute-done.rest_1_, ...), custom_call_target="tpu_custom_call" | custom-call | flops 8000000000 | bytes 24000000 | tf_op jit(solution)/shard_map/attend/pallas_call | solution.py:422
  12.6 0.0 slice-start.2
  12.6 0.0 slice-start.3
  12.6 3.4 %collective-permute-start.2 = (bf16[32,4096]{1,0:T(8,128)(2,1)S(1)}, bf16[32,4096]{1,0:T(8,128)(2,1)S(1)}, u32[]{:S(2)}, u32[]{:S(2)}) collective-permute-start(bf16[32,4096]{1,0:T(8,128)(2,1)S(1)} %attend.2.rest_0_), channel_id=1, source_target_pairs={{0,8},{4,12},{8,0},{12,4},{1,9},{5,13},{9,1},{13,5},{2,10},{6,14},... | collective-permute-start | bytes 786440 | tf_op jit(solution)/shard_map/ppermute | solution.py:368
  16.0 0.0 collective-permute-done.3.rest_0_
  16.0 0.5 collective-permute-done.4.rest_1_
  16.5 7.1 %attend.3.rest_0_ = bf16[32,4096]{1,0:T(8,128)(2,1)S(1)} custom-call(s32[1]{0:T(128)} %bitcast.ids_ref, s32[64]{0:T(128)S(1)} %copy-done.7, s32[4,16]{1,0:T(4,128)S(1)} %copy-done.5, bf16[1,848,128]{2,1,0:T(8,128)(2,1)S(1)} %collective-permute-done.3.rest_0_, bf16[1,848,128]{2,1,0:T(8,128)(2,1)S(1)} %collective-permute-done.4.rest_1_, ...), custom_call_target="tpu_custom_call" | custom-call | flops 8000000000 | bytes 24000000 | tf_op jit(solution)/shard_map/attend/pallas_call | solution.py:422
  23.6 0.0 collective-permute-done.2.rest_2_
  23.6 0.5 collective-permute-start.5
  24.1 1.9 %collective-permute-start.9 = (bf16[32,4096]{1,0:T(8,128)(2,1)S(1)}, bf16[32,4096]{1,0:T(8,128)(2,1)S(1)}, u32[]{:S(2)}, u32[]{:S(2)}) collective-permute-start(bf16[32,4096]{1,0:T(8,128)(2,1)S(1)} %attend.3.rest_0_), channel_id=1, source_target_pairs={{0,8},{4,12},{8,0},{12,4},{1,9},{5,13},{9,1},{13,5},{2,10},{6,14},... | collective-permute-start | bytes 786440 | tf_op jit(solution)/shard_map/ppermute | solution.py:368
  26.1 1.4 %project_out.4 = (bf16[64,896]{1,0:T(8,128)(2,1)S(1)}, bf16[64,896]{1,0:T(8,128)(2,1)S(1)}) custom-call(s32[1]{0:T(128)} %bitcast.ids_ref, bf16[32,4096]{1,0:T(8,128)(2,1)S(1)} %attend.2.rest_0_, bf16[32,4096]{1,0:T(8,128)(2,1)S(1)} %collective-permute-done.1.rest_1_, bf16[32,4096]{1,0:T(8,128)(2,1)S(1)} %collective-permute-done.2.rest_2_, ...), custom_call_target="tpu_custom_call" | custom-call | flops 2000000000 | bytes 6000000 | tf_op jit(solution)/shard_map/project_out/pallas_call | solution.py:474
  27.5 1.6 %collective-permute-start.6 = (bf16[64,896]{1,0:T(8,128)(2,1)S(1)}, bf16[64,896]{1,0:T(8,128)(2,1)S(1)}, u32[]{:S(2)}, u32[]{:S(2)}) collective-permute-start(bf16[64,896]{1,0:T(8,128)(2,1)S(1)} %get-tuple-element.30), channel_id=1, source_target_pairs={{0,1},{1,0},{2,3},{3,2},{4,5},{5,4},{6,7},{7,6},{8,9},{9,8},{10,11... | collective-permute-start | bytes 344072 | tf_op jit(solution)/shard_map/ppermute | solution.py:368
  29.1 3.5 %collective-permute-done.9.rest_2_ = bf16[32,4096]{1,0:T(8,128)(2,1)S(1)} collective-permute-done((bf16[32,4096]{1,0:T(8,128)(2,1)S(1)}, bf16[32,4096]{1,0:T(8,128)(2,1)S(1)}, u32[]{:S(2)}, u32[]{:S(2)}) %collective-permute-start.9) | collective-permute-done | bytes 262176 | tf_op jit(solution)/shard_map/ppermute | solution.py:368
  32.6 1.4 %project_out.6 = (bf16[64,896]{1,0:T(8,128)(2,1)S(1)}, bf16[64,896]{1,0:T(8,128)(2,1)S(1)}) custom-call(s32[1]{0:T(128)} %bitcast.ids_ref, bf16[32,4096]{1,0:T(8,128)(2,1)S(1)} %attend.2.rest_0_, bf16[32,4096]{1,0:T(8,128)(2,1)S(1)} %collective-permute-done.1.rest_1_, bf16[32,4096]{1,0:T(8,128)(2,1)S(1)} %collective-permute-done.2.rest_2_, ...), custom_call_target="tpu_custom_call" | custom-call | flops 2000000000 | bytes 6000000 | tf_op jit(solution)/shard_map/project_out/pallas_call | solution.py:474
  34.0 1.6 %collective-permute-start.12 = (bf16[64,896]{1,0:T(8,128)(2,1)S(1)}, bf16[64,896]{1,0:T(8,128)(2,1)S(1)}, u32[]{:S(2)}, u32[]{:S(2)}) collective-permute-start(bf16[64,896]{1,0:T(8,128)(2,1)S(1)} %get-tuple-element.35), channel_id=1, source_target_pairs={{0,1},{1,0},{2,3},{3,2},{4,5},{5,4},{6,7},{7,6},{8,9},{9,8},{10,11... | collective-permute-start | bytes 344072 | tf_op jit(solution)/shard_map/ppermute | solution.py:368
  35.6 2.5 %collective-permute-start.7 = (bf16[64,896]{1,0:T(8,128)(2,1)S(1)}, bf16[64,896]{1,0:T(8,128)(2,1)S(1)}, u32[]{:S(2)}, u32[]{:S(2)}) collective-permute-start(bf16[64,896]{1,0:T(8,128)(2,1)S(1)} %add_convert_fusion.7), channel_id=1, source_target_pairs={{0,3},{1,2},{2,1},{3,0},{4,7},{5,6},{6,5},{7,4},{8,11},{9,10},{10,... | collective-permute-start | bytes 344072 | tf_op jit(solution)/shard_map/ppermute | solution.py:368
  38.2 1.5 %project_out.7 = (bf16[64,896]{1,0:T(8,128)(2,1)S(1)}, bf16[64,896]{1,0:T(8,128)(2,1)S(1)}) custom-call(s32[1]{0:T(128)} %bitcast.ids_ref, bf16[32,4096]{1,0:T(8,128)(2,1)S(1)} %attend.3.rest_0_, bf16[32,4096]{1,0:T(8,128)(2,1)S(1)} %collective-permute-done.8.rest_1_, bf16[32,4096]{1,0:T(8,128)(2,1)S(1)} %collective-permute-done.9.rest_2_, ...), custom_call_target="tpu_custom_call" | custom-call | flops 2000000000 | bytes 6000000 | tf_op jit(solution)/shard_map/project_out/pallas_call | solution.py:474
  39.7 0.8 %collective-permute-start.14 = (bf16[64,896]{1,0:T(8,128)(2,1)S(1)}, bf16[64,896]{1,0:T(8,128)(2,1)S(1)}, u32[]{:S(2)}, u32[]{:S(2)}) collective-permute-start(bf16[64,896]{1,0:T(8,128)(2,1)S(1)} %get-tuple-element.38), channel_id=1, source_target_pairs={{0,1},{1,0},{2,3},{3,2},{4,5},{5,4},{6,7},{7,6},{8,9},{9,8},{10,11... | collective-permute-start | bytes 344072 | tf_op jit(solution)/shard_map/ppermute | solution.py:368
  40.5 1.4 %project_out.5 = (bf16[64,896]{1,0:T(8,128)(2,1)S(1)}, bf16[64,896]{1,0:T(8,128)(2,1)S(1)}) custom-call(s32[1]{0:T(128)} %bitcast.ids_ref, bf16[32,4096]{1,0:T(8,128)(2,1)S(1)} %attend.3.rest_0_, bf16[32,4096]{1,0:T(8,128)(2,1)S(1)} %collective-permute-done.8.rest_1_, bf16[32,4096]{1,0:T(8,128)(2,1)S(1)} %collective-permute-done.9.rest_2_, ...), custom_call_target="tpu_custom_call" | custom-call | flops 2000000000 | bytes 6000000 | tf_op jit(solution)/shard_map/project_out/pallas_call | solution.py:474
  41.9 1.4 %collective-permute-start.18 = (bf16[64,896]{1,0:T(8,128)(2,1)S(1)}, bf16[64,896]{1,0:T(8,128)(2,1)S(1)}, u32[]{:S(2)}, u32[]{:S(2)}) collective-permute-start(bf16[64,896]{1,0:T(8,128)(2,1)S(1)} %get-tuple-element.41), channel_id=1, source_target_pairs={{0,1},{1,0},{2,3},{3,2},{4,5},{5,4},{6,7},{7,6},{8,9},{9,8},{10,11... | collective-permute-start | bytes 344072 | tf_op jit(solution)/shard_map/ppermute | solution.py:368
  43.3 2.1 %collective-permute-start.13 = (bf16[64,896]{1,0:T(8,128)(2,1)S(1)}, bf16[64,896]{1,0:T(8,128)(2,1)S(1)}, u32[]{:S(2)}, u32[]{:S(2)}) collective-permute-start(bf16[64,896]{1,0:T(8,128)(2,1)S(1)} %add_convert_fusion.5), channel_id=1, source_target_pairs={{0,3},{1,2},{2,1},{3,0},{4,7},{5,6},{6,5},{7,4},{8,11},{9,10},{10,... | collective-permute-start | bytes 344072 | tf_op jit(solution)/shard_map/ppermute | solution.py:368
  45.4 0.1 collective-permute-start.11
  45.5 1.2 %collective-permute-done.14 = bf16[64,896]{1,0:T(8,128)(2,1)S(1)} collective-permute-done((bf16[64,896]{1,0:T(8,128)(2,1)S(1)}, bf16[64,896]{1,0:T(8,128)(2,1)S(1)}, u32[]{:S(2)}, u32[]{:S(2)}) %collective-permute-start.14) | collective-permute-done | bytes 114720 | tf_op jit(solution)/shard_map/ppermute | solution.py:368
  46.7 1.5 %collective-permute-start.16 = (bf16[64,896]{1,0:T(8,128)(2,1)S(1)}, bf16[64,896]{1,0:T(8,128)(2,1)S(1)}, u32[]{:S(2)}, u32[]{:S(2)}) collective-permute-start(bf16[64,896]{1,0:T(8,128)(2,1)S(1)} %add_convert_fusion.4), channel_id=1, source_target_pairs={{0,3},{1,2},{2,1},{3,0},{4,7},{5,6},{6,5},{7,4},{8,11},{9,10},{10,... | collective-permute-start | bytes 344072 | tf_op jit(solution)/shard_map/ppermute | solution.py:368
  48.2 3.7 %collective-permute-done.13 = bf16[64,896]{1,0:T(8,128)(2,1)S(1)} collective-permute-done((bf16[64,896]{1,0:T(8,128)(2,1)S(1)}, bf16[64,896]{1,0:T(8,128)(2,1)S(1)}, u32[]{:S(2)}, u32[]{:S(2)}) %collective-permute-start.13) | collective-permute-done | bytes 114720 | tf_op jit(solution)/shard_map/ppermute | solution.py:368
  51.9 0.1 collective-permute-start.15
  52.1 1.8 %collective-permute-start.19 = (bf16[64,896]{1,0:T(8,128)(2,1)S(1)}, bf16[64,896]{1,0:T(8,128)(2,1)S(1)}, u32[]{:S(2)}, u32[]{:S(2)}) collective-permute-start(bf16[64,896]{1,0:T(8,128)(2,1)S(1)} %add_convert_fusion.1), channel_id=1, source_target_pairs={{0,3},{1,2},{2,1},{3,0},{4,7},{5,6},{6,5},{7,4},{8,11},{9,10},{10,... | collective-permute-start | bytes 344072 | tf_op jit(solution)/shard_map/ppermute | solution.py:368
  53.8 3.0 %collective-permute-done.16 = bf16[64,896]{1,0:T(8,128)(2,1)S(1)} collective-permute-done((bf16[64,896]{1,0:T(8,128)(2,1)S(1)}, bf16[64,896]{1,0:T(8,128)(2,1)S(1)}, u32[]{:S(2)}, u32[]{:S(2)}) %collective-permute-start.16) | collective-permute-done | bytes 114720 | tf_op jit(solution)/shard_map/ppermute | solution.py:368
  56.9 0.1 collective-permute-start.17
  56.9 4.8 %collective-permute-done.19 = bf16[64,896]{1,0:T(8,128)(2,1)S(1)} collective-permute-done((bf16[64,896]{1,0:T(8,128)(2,1)S(1)}, bf16[64,896]{1,0:T(8,128)(2,1)S(1)}, u32[]{:S(2)}, u32[]{:S(2)}) %collective-permute-start.19) | collective-permute-done | bytes 114720 | tf_op jit(solution)/shard_map/ppermute | solution.py:368
  61.8 0.1 collective-permute-start.20
  61.9 2.0 %collective-permute-done.17.rest_5_ = bf16[64,896]{1,0:T(8,128)(2,1)S(1)} collective-permute-done((bf16[64,896]{1,0:T(8,128)(2,1)S(1)}, bf16[64,896]{1,0:T(8,128)(2,1)S(1)}, u32[]{:S(2)}, u32[]{:S(2)}) %collective-permute-start.17) | collective-permute-done | bytes 114720 | tf_op jit(solution)/shard_map/ppermute | solution.py:368
  63.8 2.8 %collective-permute-done.20.rest_7_ = bf16[64,896]{1,0:T(8,128)(2,1)S(1)} collective-permute-done((bf16[64,896]{1,0:T(8,128)(2,1)S(1)}, bf16[64,896]{1,0:T(8,128)(2,1)S(1)}, u32[]{:S(2)}, u32[]{:S(2)}) %collective-permute-start.20) | collective-permute-done | bytes 114720 | tf_op jit(solution)/shard_map/ppermute | solution.py:368
  66.6 1.7 %order_rows.1 = bf16[4,64,1792]{2,1,0:T(8,128)(2,1)} custom-call(s32[1]{0:T(128)} %bitcast.ids_ref, bf16[4,64,256]{2,1,0:T(8,128)(2,1)S(1)} %place_rows.1.after_ref.pick_ref, bf16[64,896]{1,0:T(8,128)(2,1)S(1)} %add_convert_fusion.6.rest_0_, bf16[64,896]{1,0:T(8,128)(2,1)S(1)} %collective-permute-done.11.rest_1_, ...), custom_call_target="tpu_custom_call" | custom-call | flops 2000000000 | bytes 6000000 | tf_op jit(solution)/shard_map/order_rows/pallas_call | solution.py:448
  (41 shorter events, 0.3 us)
Async XLA Ops:
  0.0 1.8 %copy-start.4 = (bf16[4,16,576]{2,1,0:T(8,128)(2,1)S(1)}, bf16[4,16,576]{2,1,0:T(8,128)(2,1)}, u32[]{:S(2)}) copy-start(bf16[4,16,576]{2,1,0:T(8,128)(2,1)} %fresh_ref.1) | copy-start | bytes 221188
  0.0 1.9 %copy-start.3 = (bf16[4,16,32,64]{3,2,1,0:T(8,128)(2,1)S(1)}, bf16[4,16,32,64]{3,2,1,0:T(8,128)(2,1)}, u32[]{:S(2)}) copy-start(bf16[4,16,32,64]{3,2,1,0:T(8,128)(2,1)} %rope_ref.1) | copy-start | bytes 786436
  0.0 1.9 %copy-start.2 = (bf16[4,16,32,128]{3,2,1,0:T(8,128)(2,1)S(1)}, bf16[4,16,32,128]{3,2,1,0:T(8,128)(2,1)}, u32[]{:S(2)}) copy-start(bf16[4,16,32,128]{3,2,1,0:T(8,128)(2,1)} %nope_ref.1) | copy-start | bytes 1572868
  0.0 0.7 %copy-start.6 = (s32[64]{0:T(128)S(1)}, s32[64]{0:T(128)}, u32[]{:S(2)}) copy-start(s32[64]{0:T(128)} %decode_ref.7) | copy-start | bytes 772
  0.8 5.5 %slice-start.4 = ((s8[4718592]{0:T(1024)(128)(4,1)}), s8[4194304]{0:T(1024)(128)(4,1)S(1)}, s32[]{:S(2)}) async-start(s8[4718592]{0:T(1024)(128)(4,1)} %bitcast.4), calls=%async_computation.4 | async-start | bytes 8388608
  1.9 4.4 %slice-start.5 = ((s8[4718592]{0:T(1024)(128)(4,1)}), s8[524288]{0:T(1024)(128)(4,1)S(1)}, s32[]{:S(2)}) async-start(s8[4718592]{0:T(1024)(128)(4,1)} %bitcast.4), calls=%async_computation.5 | async-start | bytes 1048576
  1.9 4.4 %copy-start = (bf16[32,128,512]{2,1,0:T(8,128)(2,1)S(1)}, bf16[32,128,512]{2,1,0:T(8,128)(2,1)}, u32[]{:S(2)}) copy-start(bf16[32,128,512]{2,1,0:T(8,128)(2,1)} %rest_3_.3) | copy-start | bytes 12582916
  1.9 4.4 %copy-start.1 = (bf16[32,512,128]{2,1,0:T(8,128)(2,1)S(1)}, bf16[32,512,128]{2,1,0:T(8,128)(2,1)}, u32[]{:S(2)}) copy-start(bf16[32,512,128]{2,1,0:T(8,128)(2,1)} %rest_4_.7) | copy-start | bytes 12582916
  1.9 4.4 %copy-start.5 = (s32[4,16]{1,0:T(4,128)S(1)}, s32[4,16]{1,0:T(4,128)}, u32[]{:S(2)}) copy-start(s32[4,16]{1,0:T(4,128)} %length_ref.3) | copy-start | bytes 772
  1.9 4.4 %copy-start.7 = (s32[64]{0:T(128)S(1)}, s32[64]{0:T(128)}, u32[]{:S(2)}) copy-start(s32[64]{0:T(128)} %decode_ref.7) | copy-start | bytes 772
  3.1 3.2 %collective-permute-start = (bf16[1,848,128]{2,1,0:T(8,128)(2,1)S(1)}, bf16[1,848,128]{2,1,0:T(8,128)(2,1)S(1)}, u32[]{:S(2)}, u32[]{:S(2)}) collective-permute-start(bf16[1,848,128]{2,1,0:T(8,128)(2,1)S(1)} %get-tuple-element.25), channel_id=1, source_target_pairs={{0,4},{4,0},{8,12},{12,8},{1,5},{5,1},{9,13},{13,9},{2,6},{6,2},{1... | collective-permute-start | bytes 651272 | tf_op jit(solution)/shard_map/ppermute | solution.py:368
  3.6 12.4 %collective-permute-start.3 = (bf16[1,848,128]{2,1,0:T(8,128)(2,1)S(1)}, bf16[1,848,128]{2,1,0:T(8,128)(2,1)S(1)}, u32[]{:S(2)}, u32[]{:S(2)}) collective-permute-start(bf16[1,848,128]{2,1,0:T(8,128)(2,1)S(1)} %get-tuple-element.26), channel_id=1, source_target_pairs={{0,8},{4,12},{8,0},{12,4},{1,9},{5,13},{9,1},{13,5},{2,10},{6,14},... | collective-permute-start | bytes 651272 | tf_op jit(solution)/shard_map/ppermute | solution.py:368
  6.2 10.3 %collective-permute-start.4 = (bf16[1,848,128]{2,1,0:T(8,128)(2,1)S(1)}, bf16[1,848,128]{2,1,0:T(8,128)(2,1)S(1)}, u32[]{:S(2)}, u32[]{:S(2)}) collective-permute-start(bf16[1,848,128]{2,1,0:T(8,128)(2,1)S(1)} %get-tuple-element.27), channel_id=1, source_target_pairs={{0,12},{4,8},{8,4},{12,0},{1,13},{5,9},{9,5},{13,1},{2,14},{6,10},... | collective-permute-start | bytes 651272 | tf_op jit(solution)/shard_map/ppermute | solution.py:368
  6.3 19.7 %slice-start = ((s8[14680064]{0:T(1024)(128)(4,1)}), s8[4194304]{0:T(1024)(128)(4,1)S(1)}, s32[]{:S(2)}) async-start(s8[14680064]{0:T(1024)(128)(4,1)} %bitcast.2), calls=%async_computation | async-start | bytes 8388608
  6.3 19.7 %slice-start.1 = ((s8[14680064]{0:T(1024)(128)(4,1)}), s8[4194304]{0:T(1024)(128)(4,1)S(1)}, s32[]{:S(2)}) async-start(s8[14680064]{0:T(1024)(128)(4,1)} %bitcast.2), calls=%async_computation.1 | async-start | bytes 8388608
  12.6 13.5 %slice-start.2 = ((s8[14680064]{0:T(1024)(128)(4,1)}), s8[4194304]{0:T(1024)(128)(4,1)S(1)}, s32[]{:S(2)}) async-start(s8[14680064]{0:T(1024)(128)(4,1)} %bitcast.2), calls=%async_computation.2 | async-start | bytes 8388608
  12.6 13.5 %slice-start.3 = ((s8[14680064]{0:T(1024)(128)(4,1)}), s8[2097152]{0:T(1024)(128)(4,1)S(1)}, s32[]{:S(2)}) async-start(s8[14680064]{0:T(1024)(128)(4,1)} %bitcast.2), calls=%async_computation.3 | async-start | bytes 4194304
  12.6 11.0 %collective-permute-start.2 = (bf16[32,4096]{1,0:T(8,128)(2,1)S(1)}, bf16[32,4096]{1,0:T(8,128)(2,1)S(1)}, u32[]{:S(2)}, u32[]{:S(2)}) collective-permute-start(bf16[32,4096]{1,0:T(8,128)(2,1)S(1)} %attend.2.rest_0_), channel_id=1, source_target_pairs={{0,8},{4,12},{8,0},{12,4},{1,9},{5,13},{9,1},{13,5},{2,10},{6,14},... | collective-permute-start | bytes 786440 | tf_op jit(solution)/shard_map/ppermute | solution.py:368
  16.0 10.0 %collective-permute-start.1 = (bf16[32,4096]{1,0:T(8,128)(2,1)S(1)}, bf16[32,4096]{1,0:T(8,128)(2,1)S(1)}, u32[]{:S(2)}, u32[]{:S(2)}) collective-permute-start(bf16[32,4096]{1,0:T(8,128)(2,1)S(1)} %attend.2.rest_0_), channel_id=1, source_target_pairs={{0,4},{4,0},{8,12},{12,8},{1,5},{5,1},{9,13},{13,9},{2,6},{6,2},{1... | collective-permute-start | bytes 786440 | tf_op jit(solution)/shard_map/ppermute | solution.py:368
  23.6 2.4 %collective-permute-start.5 = (bf16[32,4096]{1,0:T(8,128)(2,1)S(1)}, bf16[32,4096]{1,0:T(8,128)(2,1)S(1)}, u32[]{:S(2)}, u32[]{:S(2)}) collective-permute-start(bf16[32,4096]{1,0:T(8,128)(2,1)S(1)} %collective-permute-done.2.rest_2_), channel_id=1, source_target_pairs={{0,4},{4,0},{8,12},{12,8},{1,5},{5,1},{9,13},{13,9},{2,6},{6,2},{1... | collective-permute-start | bytes 786440 | tf_op jit(solution)/shard_map/ppermute | solution.py:368
  24.1 8.5 %collective-permute-start.9 = (bf16[32,4096]{1,0:T(8,128)(2,1)S(1)}, bf16[32,4096]{1,0:T(8,128)(2,1)S(1)}, u32[]{:S(2)}, u32[]{:S(2)}) collective-permute-start(bf16[32,4096]{1,0:T(8,128)(2,1)S(1)} %attend.3.rest_0_), channel_id=1, source_target_pairs={{0,8},{4,12},{8,0},{12,4},{1,9},{5,13},{9,1},{13,5},{2,10},{6,14},... | collective-permute-start | bytes 786440 | tf_op jit(solution)/shard_map/ppermute | solution.py:368
  26.0 12.1 %collective-permute-start.8 = (bf16[32,4096]{1,0:T(8,128)(2,1)S(1)}, bf16[32,4096]{1,0:T(8,128)(2,1)S(1)}, u32[]{:S(2)}, u32[]{:S(2)}) collective-permute-start(bf16[32,4096]{1,0:T(8,128)(2,1)S(1)} %attend.3.rest_0_), channel_id=1, source_target_pairs={{0,4},{4,0},{8,12},{12,8},{1,5},{5,1},{9,13},{13,9},{2,6},{6,2},{1... | collective-permute-start | bytes 786440 | tf_op jit(solution)/shard_map/ppermute | solution.py:368
  27.5 8.1 %collective-permute-start.6 = (bf16[64,896]{1,0:T(8,128)(2,1)S(1)}, bf16[64,896]{1,0:T(8,128)(2,1)S(1)}, u32[]{:S(2)}, u32[]{:S(2)}) collective-permute-start(bf16[64,896]{1,0:T(8,128)(2,1)S(1)} %get-tuple-element.30), channel_id=1, source_target_pairs={{0,1},{1,0},{2,3},{3,2},{4,5},{5,4},{6,7},{7,6},{8,9},{9,8},{10,11... | collective-permute-start | bytes 344072 | tf_op jit(solution)/shard_map/ppermute | solution.py:368
  32.6 5.6 %collective-permute-start.10 = (bf16[32,4096]{1,0:T(8,128)(2,1)S(1)}, bf16[32,4096]{1,0:T(8,128)(2,1)S(1)}, u32[]{:S(2)}, u32[]{:S(2)}) collective-permute-start(bf16[32,4096]{1,0:T(8,128)(2,1)S(1)} %collective-permute-done.9.rest_2_), channel_id=1, source_target_pairs={{0,4},{4,0},{8,12},{12,8},{1,5},{5,1},{9,13},{13,9},{2,6},{6,2},{1... | collective-permute-start | bytes 786440 | tf_op jit(solution)/shard_map/ppermute | solution.py:368
  34.0 9.3 %collective-permute-start.12 = (bf16[64,896]{1,0:T(8,128)(2,1)S(1)}, bf16[64,896]{1,0:T(8,128)(2,1)S(1)}, u32[]{:S(2)}, u32[]{:S(2)}) collective-permute-start(bf16[64,896]{1,0:T(8,128)(2,1)S(1)} %get-tuple-element.35), channel_id=1, source_target_pairs={{0,1},{1,0},{2,3},{3,2},{4,5},{5,4},{6,7},{7,6},{8,9},{9,8},{10,11... | collective-permute-start | bytes 344072 | tf_op jit(solution)/shard_map/ppermute | solution.py:368
  35.6 9.8 %collective-permute-start.7 = (bf16[64,896]{1,0:T(8,128)(2,1)S(1)}, bf16[64,896]{1,0:T(8,128)(2,1)S(1)}, u32[]{:S(2)}, u32[]{:S(2)}) collective-permute-start(bf16[64,896]{1,0:T(8,128)(2,1)S(1)} %add_convert_fusion.7), channel_id=1, source_target_pairs={{0,3},{1,2},{2,1},{3,0},{4,7},{5,6},{6,5},{7,4},{8,11},{9,10},{10,... | collective-permute-start | bytes 344072 | tf_op jit(solution)/shard_map/ppermute | solution.py:368
  39.7 7.0 %collective-permute-start.14 = (bf16[64,896]{1,0:T(8,128)(2,1)S(1)}, bf16[64,896]{1,0:T(8,128)(2,1)S(1)}, u32[]{:S(2)}, u32[]{:S(2)}) collective-permute-start(bf16[64,896]{1,0:T(8,128)(2,1)S(1)} %get-tuple-element.38), channel_id=1, source_target_pairs={{0,1},{1,0},{2,3},{3,2},{4,5},{5,4},{6,7},{7,6},{8,9},{9,8},{10,11... | collective-permute-start | bytes 344072 | tf_op jit(solution)/shard_map/ppermute | solution.py:368
  41.9 10.2 %collective-permute-start.18 = (bf16[64,896]{1,0:T(8,128)(2,1)S(1)}, bf16[64,896]{1,0:T(8,128)(2,1)S(1)}, u32[]{:S(2)}, u32[]{:S(2)}) collective-permute-start(bf16[64,896]{1,0:T(8,128)(2,1)S(1)} %get-tuple-element.41), channel_id=1, source_target_pairs={{0,1},{1,0},{2,3},{3,2},{4,5},{5,4},{6,7},{7,6},{8,9},{9,8},{10,11... | collective-permute-start | bytes 344072 | tf_op jit(solution)/shard_map/ppermute | solution.py:368
  43.3 8.6 %collective-permute-start.13 = (bf16[64,896]{1,0:T(8,128)(2,1)S(1)}, bf16[64,896]{1,0:T(8,128)(2,1)S(1)}, u32[]{:S(2)}, u32[]{:S(2)}) collective-permute-start(bf16[64,896]{1,0:T(8,128)(2,1)S(1)} %add_convert_fusion.5), channel_id=1, source_target_pairs={{0,3},{1,2},{2,1},{3,0},{4,7},{5,6},{6,5},{7,4},{8,11},{9,10},{10,... | collective-permute-start | bytes 344072 | tf_op jit(solution)/shard_map/ppermute | solution.py:368
  45.4 16.4 %collective-permute-start.11 = (bf16[64,896]{1,0:T(8,128)(2,1)S(1)}, bf16[64,896]{1,0:T(8,128)(2,1)S(1)}, u32[]{:S(2)}, u32[]{:S(2)}) collective-permute-start(bf16[64,896]{1,0:T(8,128)(2,1)S(1)} %add_convert_fusion.6.rest_0_), channel_id=1, source_target_pairs={{0,1},{1,0},{2,3},{3,2},{4,5},{5,4},{6,7},{7,6},{8,9},{9,8},{10,11... | collective-permute-start | bytes 344072 | tf_op jit(solution)/shard_map/ppermute | solution.py:368
  46.7 10.1 %collective-permute-start.16 = (bf16[64,896]{1,0:T(8,128)(2,1)S(1)}, bf16[64,896]{1,0:T(8,128)(2,1)S(1)}, u32[]{:S(2)}, u32[]{:S(2)}) collective-permute-start(bf16[64,896]{1,0:T(8,128)(2,1)S(1)} %add_convert_fusion.4), channel_id=1, source_target_pairs={{0,3},{1,2},{2,1},{3,0},{4,7},{5,6},{6,5},{7,4},{8,11},{9,10},{10,... | collective-permute-start | bytes 344072 | tf_op jit(solution)/shard_map/ppermute | solution.py:368
  51.9 9.9 %collective-permute-start.15 = (bf16[64,896]{1,0:T(8,128)(2,1)S(1)}, bf16[64,896]{1,0:T(8,128)(2,1)S(1)}, u32[]{:S(2)}, u32[]{:S(2)}) collective-permute-start(bf16[64,896]{1,0:T(8,128)(2,1)S(1)} %add_convert_fusion.3.rest_2_), channel_id=1, source_target_pairs={{0,1},{1,0},{2,3},{3,2},{4,5},{5,4},{6,7},{7,6},{8,9},{9,8},{10,11... | collective-permute-start | bytes 344072 | tf_op jit(solution)/shard_map/ppermute | solution.py:368
  52.1 9.7 %collective-permute-start.19 = (bf16[64,896]{1,0:T(8,128)(2,1)S(1)}, bf16[64,896]{1,0:T(8,128)(2,1)S(1)}, u32[]{:S(2)}, u32[]{:S(2)}) collective-permute-start(bf16[64,896]{1,0:T(8,128)(2,1)S(1)} %add_convert_fusion.1), channel_id=1, source_target_pairs={{0,3},{1,2},{2,1},{3,0},{4,7},{5,6},{6,5},{7,4},{8,11},{9,10},{10,... | collective-permute-start | bytes 344072 | tf_op jit(solution)/shard_map/ppermute | solution.py:368
  56.9 7.0 %collective-permute-start.17 = (bf16[64,896]{1,0:T(8,128)(2,1)S(1)}, bf16[64,896]{1,0:T(8,128)(2,1)S(1)}, u32[]{:S(2)}, u32[]{:S(2)}) collective-permute-start(bf16[64,896]{1,0:T(8,128)(2,1)S(1)} %add_convert_fusion.2.rest_4_), channel_id=1, source_target_pairs={{0,1},{1,0},{2,3},{3,2},{4,5},{5,4},{6,7},{7,6},{8,9},{9,8},{10,11... | collective-permute-start | bytes 344072 | tf_op jit(solution)/shard_map/ppermute | solution.py:368
  61.8 4.9 %collective-permute-start.20 = (bf16[64,896]{1,0:T(8,128)(2,1)S(1)}, bf16[64,896]{1,0:T(8,128)(2,1)S(1)}, u32[]{:S(2)}, u32[]{:S(2)}) collective-permute-start(bf16[64,896]{1,0:T(8,128)(2,1)S(1)} %add_convert_fusion.rest_6_), channel_id=1, source_target_pairs={{0,1},{1,0},{2,3},{3,2},{4,5},{5,4},{6,7},{7,6},{8,9},{9,8},{10,11... | collective-permute-start | bytes 344072 | tf_op jit(solution)/shard_map/ppermute | solution.py:368

commit v11 on v9

--- a/solution.py
+++ b/solution.py
@@ -295,25 +295,24 @@
     return (z == 1) | (z == 2)
 
 
-def order_kernel(halves, ids_ref, pick_ref, *rest):
+def order_kernel(layout, ids_ref, pick_ref, *rest):
     pieces, out_ref, x = rest[:-2], rest[-2], rest[-1]
     upper = keeps_upper(ids_ref)
-    rows = x.shape[0] // (2 * halves)
-    each = len(pieces) // (2 * halves)
-    cols = x.shape[1] // each
 
     def assemble(first, second):
-        for h in range(halves):
-            for c in range(each):
-                at = slice(c * cols, (c + 1) * cols)
-                i = 2 * (h * each + c)
-                x[2 * h * rows : (2 * h + 1) * rows, at] = pieces[i + first][...]
-                x[(2 * h + 1) * rows : (2 * h + 2) * rows, at] = pieces[i + second][...]
+        for i, (row, col) in enumerate(layout):
+            rows, cols = pieces[2 * i].shape
+            x[row : row + rows, col : col + cols] = pieces[2 * i + first][...]
+            x[row + rows : row + 2 * rows, col : col + cols] = pieces[2 * i + second][...]
 
     pl.when(upper)(lambda: assemble(1, 0))
     pl.when(jnp.logical_not(upper))(lambda: assemble(0, 1))
-    for t in range(pick_ref.shape[0]):
-        out_ref[t] = jnp.dot(pick_ref[t], x[...], preferred_element_type=jnp.float32).astype(jnp.bfloat16)
+    steps, rows, _ = pick_ref.shape
+    pick = jnp.concatenate([pick_ref[t] for t in range(steps)], axis=0)
+    for c in range(0, x.shape[1], BLOCK):
+        tile = jnp.dot(pick, x[:, c : c + BLOCK], preferred_element_type=jnp.float32).astype(jnp.bfloat16)
+        for t in range(steps):
+            out_ref[t, :, c : c + BLOCK] = tile[t * rows : (t + 1) * rows]
 
 
 def order_whole_kernel(pick_ref, x_ref, out_ref):
@@ -322,23 +321,16 @@
 
 
 def project_kernel(first_col, ids_ref, *rest):
-    parts, weight, keep, send, x = rest[:4], rest[4], rest[5], rest[6], rest[7]
-    rows = parts[0].shape[0]
+    parts, (weight, keep, send) = rest[:-3], rest[-3:]
+    half = keep.shape[0]
     upper = keeps_upper(ids_ref)
-
-    def assemble(order):
-        for place, q in enumerate(order):
-            x[place * rows : (place + 1) * rows, :] = parts[q][...]
-
-    pl.when(upper)(lambda: assemble((2, 3, 0, 1)))
-    pl.when(jnp.logical_not(upper))(lambda: assemble((0, 1, 2, 3)))
     cols = keep.shape[1]
+    x = jnp.concatenate([part[...] for part in parts], axis=0)
     for c in range(0, cols, BLOCK):
         n = min(BLOCK, cols - c)
-        tile = jnp.dot(x[...], weight[:, first_col + c : first_col + c + n], preferred_element_type=jnp.float32)
-        tile = tile.astype(jnp.bfloat16)
-        keep[:, c : c + n] = tile[: 2 * rows]
-        send[:, c : c + n] = tile[2 * rows :]
+        tile = jnp.dot(x, weight[:, first_col + c : first_col + c + n], preferred_element_type=jnp.float32)
+        keep[:, c : c + n] = jnp.where(upper, tile[half:], tile[:half]).astype(jnp.bfloat16)
+        send[:, c : c + n] = jnp.where(upper, tile[:half], tile[half:]).astype(jnp.bfloat16)
 
 
 def smem():
@@ -466,17 +458,13 @@
         whole = lax.all_gather(summed, "head", axis=0, tiled=True)
         return order(order_whole_kernel, [vmem()] * 2, [], [pick, whole])
 
-    pieces = 2
-
-    def project(parts, piece):
-        part_rows = parts[0].shape[0]
-        cols = columns // pieces
+    def project(parts, first_col, cols):
+        rows_here = len(parts) * parts[0].shape[0]
         return pl.pallas_call(
-            functools.partial(project_kernel, piece * cols),
-            out_shape=[jax.ShapeDtypeStruct((2 * part_rows, cols), jnp.bfloat16)] * 2,
-            in_specs=[smem()] + [vmem()] * 5,
+            functools.partial(project_kernel, first_col),
+            out_shape=[jax.ShapeDtypeStruct((rows_here // 2, cols), jnp.bfloat16)] * 2,
+            in_specs=[smem()] + [vmem()] * (len(parts) + 1),
             out_specs=[vmem()] * 2,
-            scratch_shapes=[pltpu.VMEM((4 * part_rows, out_proj.shape[0]), jnp.bfloat16)],
             compiler_params=limit(10),
             cost_estimate=cost(2),
             name="project_out",
@@ -489,42 +477,38 @@
     near_across, far_rows = lax.optimization_barrier((near_across, far_rows))
     near = [near_rows, flip(near_rows, "seq", 1), near_across, flip(near_across, "seq", 1)]
     far_across = flip(far_rows, "seq", 2)
+
     def after(value, *others):
         return lax.optimization_barrier((value,) + others)[0]
 
     def swap(piece):
         return flip(piece[1], "head", 1)
 
-    first = project(near, 0)
-    first_in = swap(first)
-    second = project(near, 1)
-    second_in = swap(second)
     far = [far_rows, flip(far_rows, "seq", 1), far_across, flip(far_across, "seq", 1)]
-    first_pair = add(first[0], first_in)
-    first_cross = flip(first_pair, "head", 3)
-    second_pair = add(second[0], second_in)
-    second_cross = flip(second_pair, "head", 3)
-    third = project(far, 0)
-    third_in = swap(third)
-    fourth = project(far, 1)
-    fourth_in = swap(fourth)
-    third_pair = add(third[0], third_in)
-    third_cross = flip(third_pair, "head", 3)
-    fourth_pair = add(fourth[0], fourth_in)
-    fourth_cross = flip(fourth_pair, "head", 3)
-    first_cross = after(first_cross, third_pair, fourth_pair)
-    second_cross = after(second_cross, third_pair, fourth_pair)
-    first_sum = add(first_pair, first_cross)
-    first_other = flip(first_sum, "head", 1)
-    second_sum = add(second_pair, second_cross)
-    second_other = flip(second_sum, "head", 1)
-    third_sum = add(third_pair, third_cross)
-    third_other = flip(third_sum, "head", 1)
-    fourth_sum = add(fourth_pair, fourth_cross)
-    fourth_other = flip(fourth_sum, "head", 1)
-    arrays = [first_sum, first_other, second_sum, second_other, third_sum, third_other, fourth_sum, fourth_other]
-    scratch = [pltpu.VMEM((steps * sources * requests, columns), jnp.bfloat16)]
-    kernel = functools.partial(order_kernel, 2)
+    half = steps * sources * requests // 2
+
+    def cut(parts, first_row, shares):
+        groups = columns // LANES
+        edges = [LANES * (groups * sum(shares[:i]) // sum(shares)) for i in range(len(shares) + 1)]
+        return [(parts, first_row, at, end - at) for at, end in zip(edges, edges[1:])]
+
+    near_pieces, far_pieces = cut(near, 0, (5, 9)), cut(far, half, (6, 5, 3))
+    made = []
+    for parts, first_row, first_col, cols in near_pieces + far_pieces:
+        keep, send = project(parts, first_col, cols)
+        made.append((first_row, first_col, keep, swap((keep, send))))
+    pairs = [add(keep, incoming) for _, _, keep, incoming in made]
+    crossed = [flip(pair, "head", 3) for pair in pairs]
+    last_made = made[-1][2]
+    arrays = []
+    for i, (pair, cross) in enumerate(zip(pairs, crossed)):
+        if i < len(near_pieces):
+            cross = after(cross, last_made)
+        total = add(pair, cross)
+        arrays += [total, flip(total, "head", 1)]
+    layout = tuple((row, col) for row, col, _, _ in made)
+    scratch = [pltpu.VMEM((2 * half, columns), jnp.bfloat16)]
+    kernel = functools.partial(order_kernel, layout)
     return order(kernel, [smem()] + [vmem()] * (1 + len(arrays)), scratch, [ids, pick] + arrays)
 
 

time: 68.1 us -> 67.1 us (0.985)
  starting transfers between devices: 29.4 us -> 31.4 us
  waiting for transfers between devices: 12.9 us -> 11.5 us
  Pallas kernels: 23.9 us -> 22.5 us
    ppermute x21 -> x24, starting transfers between devices: 29.4 us -> 31.4 us  [flip(): return lax.ppermute(x, axis, [(i, i ^ distance) for i in range(size)])]
    ppermute x21 -> x24, waiting for transfers between devices: 12.9 us -> 11.5 us  [flip(): return lax.ppermute(x, axis, [(i, i ^ distance) for i in range(size)])]
    pallas_call x2, Pallas kernels: 14.2 us -> 13.5 us  [attend(): pl.pallas_call(functools.partial(attend_kernel, sizes, scale, relative, b...]
    pallas_call x4 -> x5, Pallas kernels: 5.7 us -> 5.29 us  [project(): pl.pallas_call(functools.partial(project_kernel, first_col), out_shape=[j...]
  transfers between devices with their start and end apart: 21 -> 24, of which waited for: 8 -> 5; matrix products, arithmetic and copies ran while one was open for 0% -> 0% of each run, Pallas kernels for 29% -> 28%
where the time goes in v11:
time: 67.1 us; the launch traced here: 66.8 us
  starting transfers between devices  31.4 us (47%)
  Pallas kernels  22.5 us (34%)
  waiting for transfers between devices  11.5 us (17%)
  local copies, waits for them, and re-layouts  0.82 us (1%)
    ppermute x24, starting transfers between devices, flip(): return lax.ppermute(x, axis, [(i, i ^ distance) for i in range(size)])  31.4 us
    pallas_call x2, Pallas kernels, attend(): pl.pallas_call(functools.partial(attend_kernel, sizes, scale, relative, b...  13.5 us
    ppermute x24, waiting for transfers between devices, flip(): return lax.ppermute(x, axis, [(i, i ^ distance) for i in range(size)])  11.5 us
    pallas_call x5, Pallas kernels, project(): pl.pallas_call(functools.partial(project_kernel, first_col), out_shape=[j...  5.29 us
    pallas_call x1, Pallas kernels, order(): pl.pallas_call(kernel, out_shape=jax.ShapeDtypeStruct((steps, sources * r...  1.43 us
  transfers between devices with their start and end apart: 24, of which 5 were waited for; matrix products, arithmetic and copies ran while one was open for 0% of the time, Pallas kernels for 28%

profile of v11, /device:TPU:0, one launch (start us, length us, event | category | flops | bytes accessed | tf_op | source)
XLA Modules:
  0.0 66.8 jit_solution(129725081704779840)
XLA Ops:
  0.0 0.7 %copy-done.6 = s32[64]{0:T(128)S(1)} copy-done((s32[64]{0:T(128)S(1)}, s32[64]{0:T(128)}, u32[]{:S(2)}) %copy-start.6) | copy-done | bytes 280
  0.8 1.1 %place_rows.1.after_ref.pick_ref = bf16[4,64,256]{2,1,0:T(8,128)(2,1)S(1)} custom-call(s32[1]{0:T(128)} %bitcast.ids_ref, s32[64]{0:T(128)S(1)} %copy-done.6), custom_call_target="tpu_custom_call" | custom-call | flops 2000000000 | bytes 6000000 | tf_op jit(solution)/shard_map/place_rows/pallas_call | solution.py:384
  1.9 0.0 slice-start.5
  1.9 0.0 copy-start
  1.9 0.0 copy-start.1
  1.9 0.0 copy-start.5
  1.9 0.0 copy-start.7
  1.9 1.1 %pack_queries.1 = (bf16[1,848,128]{2,1,0:T(8,128)(2,1)S(1)}, bf16[1,848,128]{2,1,0:T(8,128)(2,1)S(1)}, bf16[1,848,128]{2,1,0:T(8,128)(2,1)S(1)}, bf16[1,848,128]{2,1,0:T(8,128)(2,1)S(1)}) custom-call(s32[1]{0:T(128)} %bitcast.ids_ref, s32[64]{0:T(128)S(1)} %copy-done.6, bf16[4,16,32,128]{3,2,1,0:T(8,128)(2,1)S(1)} %copy-done.2, ...), custom_call_target="tpu_custom_call" | custom-call | flops 6000000000 | bytes 18000000 | tf_op jit(solution)/shard_map/pack_queries/pallas_call | solution.py:396
  3.1 0.5 collective-permute-start
  3.6 2.6 %collective-permute-start.3 = (bf16[1,848,128]{2,1,0:T(8,128)(2,1)S(1)}, bf16[1,848,128]{2,1,0:T(8,128)(2,1)S(1)}, u32[]{:S(2)}, u32[]{:S(2)}) collective-permute-start(bf16[1,848,128]{2,1,0:T(8,128)(2,1)S(1)} %get-tuple-element.25), channel_id=1, source_target_pairs={{0,8},{4,12},{8,0},{12,4},{1,9},{5,13},{9,1},{13,5},{2,10},{6,14},... | collective-permute-start | bytes 651272 | tf_op jit(solution)/shard_map/ppermute | solution.py:360
  6.2 0.1 collective-permute-start.4
  6.3 0.0 collective-permute-done.rest_1_
  6.3 0.0 slice-start
  6.3 0.0 slice-start.1
  6.4 6.2 %attend.2.rest_0_ = bf16[32,4096]{1,0:T(8,128)(2,1)S(1)} custom-call(s32[1]{0:T(128)} %bitcast.ids_ref, s32[64]{0:T(128)S(1)} %copy-done.7, s32[4,16]{1,0:T(4,128)S(1)} %copy-done.5, bf16[1,848,128]{2,1,0:T(8,128)(2,1)S(1)} %get-tuple-element.23.rest_0_, bf16[1,848,128]{2,1,0:T(8,128)(2,1)S(1)} %collective-permute-done.rest_1_, ...), custom_call_target="tpu_custom_call" | custom-call | flops 8000000000 | bytes 24000000 | tf_op jit(solution)/shard_map/attend/pallas_call | solution.py:414
  12.6 0.0 slice-start.2
  12.6 0.0 slice-start.3
  12.6 3.4 %collective-permute-start.2 = (bf16[32,4096]{1,0:T(8,128)(2,1)S(1)}, bf16[32,4096]{1,0:T(8,128)(2,1)S(1)}, u32[]{:S(2)}, u32[]{:S(2)}) collective-permute-start(bf16[32,4096]{1,0:T(8,128)(2,1)S(1)} %attend.2.rest_0_), channel_id=1, source_target_pairs={{0,8},{4,12},{8,0},{12,4},{1,9},{5,13},{9,1},{13,5},{2,10},{6,14},... | collective-permute-start | bytes 786440 | tf_op jit(solution)/shard_map/ppermute | solution.py:360
  16.0 0.5 collective-permute-done.4.rest_1_
  16.5 7.3 %attend.3.rest_0_ = bf16[32,4096]{1,0:T(8,128)(2,1)S(1)} custom-call(s32[1]{0:T(128)} %bitcast.ids_ref, s32[64]{0:T(128)S(1)} %copy-done.7, s32[4,16]{1,0:T(4,128)S(1)} %copy-done.5, bf16[1,848,128]{2,1,0:T(8,128)(2,1)S(1)} %collective-permute-done.3.rest_0_, bf16[1,848,128]{2,1,0:T(8,128)(2,1)S(1)} %collective-permute-done.4.rest_1_, ...), custom_call_target="tpu_custom_call" | custom-call | flops 8000000000 | bytes 24000000 | tf_op jit(solution)/shard_map/attend/pallas_call | solution.py:414
  23.9 0.1 collective-permute-start.5
  24.0 1.8 %collective-permute-start.9 = (bf16[32,4096]{1,0:T(8,128)(2,1)S(1)}, bf16[32,4096]{1,0:T(8,128)(2,1)S(1)}, u32[]{:S(2)}, u32[]{:S(2)}) collective-permute-start(bf16[32,4096]{1,0:T(8,128)(2,1)S(1)} %attend.3.rest_0_), channel_id=1, source_target_pairs={{0,8},{4,12},{8,0},{12,4},{1,9},{5,13},{9,1},{13,5},{2,10},{6,14},... | collective-permute-start | bytes 786440 | tf_op jit(solution)/shard_map/ppermute | solution.py:360
  25.8 0.0 collective-permute-done.5.rest_3_
  25.8 1.0 %project_out.5 = (bf16[64,640]{1,0:T(8,128)(2,1)S(1)}, bf16[64,640]{1,0:T(8,128)(2,1)S(1)}) custom-call(s32[1]{0:T(128)} %bitcast.ids_ref, bf16[32,4096]{1,0:T(8,128)(2,1)S(1)} %attend.2.rest_0_, bf16[32,4096]{1,0:T(8,128)(2,1)S(1)} %collective-permute-done.1.rest_1_, bf16[32,4096]{1,0:T(8,128)(2,1)S(1)} %collective-permute-done.2.rest_2_, ...), custom_call_target="tpu_custom_call" | custom-call | flops 2000000000 | bytes 6000000 | tf_op jit(solution)/shard_map/project_out/pallas_call | solution.py:463
  26.9 1.6 %collective-permute-start.6 = (bf16[64,640]{1,0:T(8,128)(2,1)S(1)}, bf16[64,640]{1,0:T(8,128)(2,1)S(1)}, u32[]{:S(2)}, u32[]{:S(2)}) collective-permute-start(bf16[64,640]{1,0:T(8,128)(2,1)S(1)} %get-tuple-element.29), channel_id=1, source_target_pairs={{0,1},{1,0},{2,3},{3,2},{4,5},{5,4},{6,7},{7,6},{8,9},{9,8},{10,11... | collective-permute-start | bytes 245768 | tf_op jit(solution)/shard_map/ppermute | solution.py:360
  28.5 1.5 %project_out.7 = (bf16[64,1152]{1,0:T(8,128)(2,1)S(1)}, bf16[64,1152]{1,0:T(8,128)(2,1)S(1)}) custom-call(s32[1]{0:T(128)} %bitcast.ids_ref, bf16[32,4096]{1,0:T(8,128)(2,1)S(1)} %attend.2.rest_0_, bf16[32,4096]{1,0:T(8,128)(2,1)S(1)} %collective-permute-done.1.rest_1_, bf16[32,4096]{1,0:T(8,128)(2,1)S(1)} %collective-permute-done.2.rest_2_, ...), custom_call_target="tpu_custom_call" | custom-call | flops 2000000000 | bytes 6000000 | tf_op jit(solution)/shard_map/project_out/pallas_call | solution.py:463
  30.0 0.5 collective-permute-start.12
  30.6 2.1 %collective-permute-done.9.rest_2_ = bf16[32,4096]{1,0:T(8,128)(2,1)S(1)} collective-permute-done((bf16[32,4096]{1,0:T(8,128)(2,1)S(1)}, bf16[32,4096]{1,0:T(8,128)(2,1)S(1)}, u32[]{:S(2)}, u32[]{:S(2)}) %collective-permute-start.9) | collective-permute-done | bytes 262176 | tf_op jit(solution)/shard_map/ppermute | solution.py:360
  32.7 3.8 %collective-permute-start.7 = (bf16[64,640]{1,0:T(8,128)(2,1)S(1)}, bf16[64,640]{1,0:T(8,128)(2,1)S(1)}, u32[]{:S(2)}, u32[]{:S(2)}) collective-permute-start(bf16[64,640]{1,0:T(8,128)(2,1)S(1)} %add_convert_fusion.7), channel_id=1, source_target_pairs={{0,3},{1,2},{2,1},{3,0},{4,7},{5,6},{6,5},{7,4},{8,11},{9,10},{10,... | collective-permute-start | bytes 245768 | tf_op jit(solution)/shard_map/ppermute | solution.py:360
  36.5 2.2 %collective-permute-start.13 = (bf16[64,1152]{1,0:T(8,128)(2,1)S(1)}, bf16[64,1152]{1,0:T(8,128)(2,1)S(1)}, u32[]{:S(2)}, u32[]{:S(2)}) collective-permute-start(bf16[64,1152]{1,0:T(8,128)(2,1)S(1)} %add_convert_fusion.1), channel_id=1, source_target_pairs={{0,3},{1,2},{2,1},{3,0},{4,7},{5,6},{6,5},{7,4},{8,11},{9,10},{10,... | collective-permute-start | bytes 442376 | tf_op jit(solution)/shard_map/ppermute | solution.py:360
  38.7 0.7 %project_out.6 = (bf16[64,384]{1,0:T(8,128)(2,1)S(1)}, bf16[64,384]{1,0:T(8,128)(2,1)S(1)}) custom-call(s32[1]{0:T(128)} %bitcast.ids_ref, bf16[32,4096]{1,0:T(8,128)(2,1)S(1)} %attend.3.rest_0_, bf16[32,4096]{1,0:T(8,128)(2,1)S(1)} %collective-permute-done.8.rest_1_, bf16[32,4096]{1,0:T(8,128)(2,1)S(1)} %collective-permute-done.9.rest_2_, ...), custom_call_target="tpu_custom_call" | custom-call | flops 2000000000 | bytes 6000000 | tf_op jit(solution)/shard_map/project_out/pallas_call | solution.py:463
  39.4 1.0 %collective-permute-start.21 = (bf16[64,384]{1,0:T(8,128)(2,1)S(1)}, bf16[64,384]{1,0:T(8,128)(2,1)S(1)}, u32[]{:S(2)}, u32[]{:S(2)}) collective-permute-start(bf16[64,384]{1,0:T(8,128)(2,1)S(1)} %get-tuple-element.40), channel_id=1, source_target_pairs={{0,1},{1,0},{2,3},{3,2},{4,5},{5,4},{6,7},{7,6},{8,9},{9,8},{10,11... | collective-permute-start | bytes 147464 | tf_op jit(solution)/shard_map/ppermute | solution.py:360
  40.3 1.0 %project_out.9 = (bf16[64,640]{1,0:T(8,128)(2,1)S(1)}, bf16[64,640]{1,0:T(8,128)(2,1)S(1)}) custom-call(s32[1]{0:T(128)} %bitcast.ids_ref, bf16[32,4096]{1,0:T(8,128)(2,1)S(1)} %attend.3.rest_0_, bf16[32,4096]{1,0:T(8,128)(2,1)S(1)} %collective-permute-done.8.rest_1_, bf16[32,4096]{1,0:T(8,128)(2,1)S(1)} %collective-permute-done.9.rest_2_, ...), custom_call_target="tpu_custom_call" | custom-call | flops 2000000000 | bytes 6000000 | tf_op jit(solution)/shard_map/project_out/pallas_call | solution.py:463
  41.3 1.2 %collective-permute-start.18 = (bf16[64,640]{1,0:T(8,128)(2,1)S(1)}, bf16[64,640]{1,0:T(8,128)(2,1)S(1)}, u32[]{:S(2)}, u32[]{:S(2)}) collective-permute-start(bf16[64,640]{1,0:T(8,128)(2,1)S(1)} %get-tuple-element.39), channel_id=1, source_target_pairs={{0,1},{1,0},{2,3},{3,2},{4,5},{5,4},{6,7},{7,6},{8,9},{9,8},{10,11... | collective-permute-start | bytes 245768 | tf_op jit(solution)/shard_map/ppermute | solution.py:360
  42.5 1.0 %project_out.8 = (bf16[64,768]{1,0:T(8,128)(2,1)S(1)}, bf16[64,768]{1,0:T(8,128)(2,1)S(1)}) custom-call(s32[1]{0:T(128)} %bitcast.ids_ref, bf16[32,4096]{1,0:T(8,128)(2,1)S(1)} %attend.3.rest_0_, bf16[32,4096]{1,0:T(8,128)(2,1)S(1)} %collective-permute-done.8.rest_1_, bf16[32,4096]{1,0:T(8,128)(2,1)S(1)} %collective-permute-done.9.rest_2_, ...), custom_call_target="tpu_custom_call" | custom-call | flops 2000000000 | bytes 6000000 | tf_op jit(solution)/shard_map/project_out/pallas_call | solution.py:463
  43.6 1.0 %collective-permute-start.15 = (bf16[64,768]{1,0:T(8,128)(2,1)S(1)}, bf16[64,768]{1,0:T(8,128)(2,1)S(1)}, u32[]{:S(2)}, u32[]{:S(2)}) collective-permute-start(bf16[64,768]{1,0:T(8,128)(2,1)S(1)} %get-tuple-element.37), channel_id=1, source_target_pairs={{0,1},{1,0},{2,3},{3,2},{4,5},{5,4},{6,7},{7,6},{8,9},{9,8},{10,11... | collective-permute-start | bytes 294920 | tf_op jit(solution)/shard_map/ppermute | solution.py:360
  44.6 1.2 %collective-permute-start.11 = (bf16[64,640]{1,0:T(8,128)(2,1)S(1)}, bf16[64,640]{1,0:T(8,128)(2,1)S(1)}, u32[]{:S(2)}, u32[]{:S(2)}) collective-permute-start(bf16[64,640]{1,0:T(8,128)(2,1)S(1)} %add_convert_fusion.6.rest_0_), channel_id=1, source_target_pairs={{0,1},{1,0},{2,3},{3,2},{4,5},{5,4},{6,7},{7,6},{8,9},{9,8},{10,11... | collective-permute-start | bytes 245768 | tf_op jit(solution)/shard_map/ppermute | solution.py:360
  45.8 1.7 %collective-permute-start.14 = (bf16[64,1152]{1,0:T(8,128)(2,1)S(1)}, bf16[64,1152]{1,0:T(8,128)(2,1)S(1)}, u32[]{:S(2)}, u32[]{:S(2)}) collective-permute-start(bf16[64,1152]{1,0:T(8,128)(2,1)S(1)} %add_convert_fusion.rest_2_), channel_id=1, source_target_pairs={{0,1},{1,0},{2,3},{3,2},{4,5},{5,4},{6,7},{7,6},{8,9},{9,8},{10,11... | collective-permute-start | bytes 442376 | tf_op jit(solution)/shard_map/ppermute | solution.py:360
  47.5 2.7 %collective-permute-start.22 = (bf16[64,384]{1,0:T(8,128)(2,1)S(1)}, bf16[64,384]{1,0:T(8,128)(2,1)S(1)}, u32[]{:S(2)}, u32[]{:S(2)}) collective-permute-start(bf16[64,384]{1,0:T(8,128)(2,1)S(1)} %add_convert_fusion.9), channel_id=1, source_target_pairs={{0,3},{1,2},{2,1},{3,0},{4,7},{5,6},{6,5},{7,4},{8,11},{9,10},{10,... | collective-permute-start | bytes 147464 | tf_op jit(solution)/shard_map/ppermute | solution.py:360
  50.2 1.3 %collective-permute-start.19 = (bf16[64,640]{1,0:T(8,128)(2,1)S(1)}, bf16[64,640]{1,0:T(8,128)(2,1)S(1)}, u32[]{:S(2)}, u32[]{:S(2)}) collective-permute-start(bf16[64,640]{1,0:T(8,128)(2,1)S(1)} %add_convert_fusion.5), channel_id=1, source_target_pairs={{0,3},{1,2},{2,1},{3,0},{4,7},{5,6},{6,5},{7,4},{8,11},{9,10},{10,... | collective-permute-start | bytes 245768 | tf_op jit(solution)/shard_map/ppermute | solution.py:360
  51.5 2.7 %collective-permute-start.16 = (bf16[64,768]{1,0:T(8,128)(2,1)S(1)}, bf16[64,768]{1,0:T(8,128)(2,1)S(1)}, u32[]{:S(2)}, u32[]{:S(2)}) collective-permute-start(bf16[64,768]{1,0:T(8,128)(2,1)S(1)} %add_convert_fusion.3), channel_id=1, source_target_pairs={{0,3},{1,2},{2,1},{3,0},{4,7},{5,6},{6,5},{7,4},{8,11},{9,10},{10,... | collective-permute-start | bytes 294920 | tf_op jit(solution)/shard_map/ppermute | solution.py:360
  54.2 3.5 %collective-permute-done.19 = bf16[64,640]{1,0:T(8,128)(2,1)S(1)} collective-permute-done((bf16[64,640]{1,0:T(8,128)(2,1)S(1)}, bf16[64,640]{1,0:T(8,128)(2,1)S(1)}, u32[]{:S(2)}, u32[]{:S(2)}) %collective-permute-start.19) | collective-permute-done | bytes 81952 | tf_op jit(solution)/shard_map/ppermute | solution.py:360
  57.7 0.1 collective-permute-start.20
  57.8 1.4 %collective-permute-done.16 = bf16[64,768]{1,0:T(8,128)(2,1)S(1)} collective-permute-done((bf16[64,768]{1,0:T(8,128)(2,1)S(1)}, bf16[64,768]{1,0:T(8,128)(2,1)S(1)}, u32[]{:S(2)}, u32[]{:S(2)}) %collective-permute-start.16) | collective-permute-done | bytes 98336 | tf_op jit(solution)/shard_map/ppermute | solution.py:360
  59.3 1.7 %collective-permute-start.17 = (bf16[64,768]{1,0:T(8,128)(2,1)S(1)}, bf16[64,768]{1,0:T(8,128)(2,1)S(1)}, u32[]{:S(2)}, u32[]{:S(2)}) collective-permute-start(bf16[64,768]{1,0:T(8,128)(2,1)S(1)} %add_convert_fusion.2.rest_4_), channel_id=1, source_target_pairs={{0,1},{1,0},{2,3},{3,2},{4,5},{5,4},{6,7},{7,6},{8,9},{9,8},{10,11... | collective-permute-start | bytes 294920 | tf_op jit(solution)/shard_map/ppermute | solution.py:360
  61.0 0.5 collective-permute-start.23
  61.5 3.9 %collective-permute-done.23.rest_9_ = bf16[64,384]{1,0:T(8,128)(2,1)S(1)} collective-permute-done((bf16[64,384]{1,0:T(8,128)(2,1)S(1)}, bf16[64,384]{1,0:T(8,128)(2,1)S(1)}, u32[]{:S(2)}, u32[]{:S(2)}) %collective-permute-start.23) | collective-permute-done | bytes 49184 | tf_op jit(solution)/shard_map/ppermute | solution.py:360
  65.4 1.4 %order_rows.1 = bf16[4,64,1792]{2,1,0:T(8,128)(2,1)} custom-call(s32[1]{0:T(128)} %bitcast.ids_ref, bf16[4,64,256]{2,1,0:T(8,128)(2,1)S(1)} %place_rows.1.after_ref.pick_ref, bf16[64,640]{1,0:T(8,128)(2,1)S(1)} %add_convert_fusion.6.rest_0_, bf16[64,640]{1,0:T(8,128)(2,1)S(1)} %collective-permute-done.11.rest_1_, ...), custom_call_target="tpu_custom_call" | custom-call | flops 2000000000 | bytes 6000000 | tf_op jit(solution)/shard_map/order_rows/pallas_call | solution.py:440
  (50 shorter events, 0.3 us)
Async XLA Ops:
  0.0 1.8 %copy-start.2 = (bf16[4,16,32,128]{3,2,1,0:T(8,128)(2,1)S(1)}, bf16[4,16,32,128]{3,2,1,0:T(8,128)(2,1)}, u32[]{:S(2)}) copy-start(bf16[4,16,32,128]{3,2,1,0:T(8,128)(2,1)} %nope_ref.1) | copy-start | bytes 1572868
  0.0 1.9 %copy-start.3 = (bf16[4,16,32,64]{3,2,1,0:T(8,128)(2,1)S(1)}, bf16[4,16,32,64]{3,2,1,0:T(8,128)(2,1)}, u32[]{:S(2)}) copy-start(bf16[4,16,32,64]{3,2,1,0:T(8,128)(2,1)} %rope_ref.1) | copy-start | bytes 786436
  0.0 1.9 %copy-start.4 = (bf16[4,16,576]{2,1,0:T(8,128)(2,1)S(1)}, bf16[4,16,576]{2,1,0:T(8,128)(2,1)}, u32[]{:S(2)}) copy-start(bf16[4,16,576]{2,1,0:T(8,128)(2,1)} %fresh_ref.1) | copy-start | bytes 221188
  0.0 0.7 %copy-start.6 = (s32[64]{0:T(128)S(1)}, s32[64]{0:T(128)}, u32[]{:S(2)}) copy-start(s32[64]{0:T(128)} %decode_ref.7) | copy-start | bytes 772
  0.8 5.5 %slice-start.4 = ((s8[4718592]{0:T(1024)(128)(4,1)}), s8[4194304]{0:T(1024)(128)(4,1)S(1)}, s32[]{:S(2)}) async-start(s8[4718592]{0:T(1024)(128)(4,1)} %bitcast.4), calls=%async_computation.4 | async-start | bytes 8388608
  1.9 4.4 %slice-start.5 = ((s8[4718592]{0:T(1024)(128)(4,1)}), s8[524288]{0:T(1024)(128)(4,1)S(1)}, s32[]{:S(2)}) async-start(s8[4718592]{0:T(1024)(128)(4,1)} %bitcast.4), calls=%async_computation.5 | async-start | bytes 1048576
  1.9 4.4 %copy-start = (bf16[32,128,512]{2,1,0:T(8,128)(2,1)S(1)}, bf16[32,128,512]{2,1,0:T(8,128)(2,1)}, u32[]{:S(2)}) copy-start(bf16[32,128,512]{2,1,0:T(8,128)(2,1)} %rest_3_.3) | copy-start | bytes 12582916
  1.9 4.4 %copy-start.1 = (bf16[32,512,128]{2,1,0:T(8,128)(2,1)S(1)}, bf16[32,512,128]{2,1,0:T(8,128)(2,1)}, u32[]{:S(2)}) copy-start(bf16[32,512,128]{2,1,0:T(8,128)(2,1)} %rest_4_.8) | copy-start | bytes 12582916
  1.9 4.4 %copy-start.5 = (s32[4,16]{1,0:T(4,128)S(1)}, s32[4,16]{1,0:T(4,128)}, u32[]{:S(2)}) copy-start(s32[4,16]{1,0:T(4,128)} %length_ref.3) | copy-start | bytes 772
  1.9 4.4 %copy-start.7 = (s32[64]{0:T(128)S(1)}, s32[64]{0:T(128)}, u32[]{:S(2)}) copy-start(s32[64]{0:T(128)} %decode_ref.7) | copy-start | bytes 772
  3.1 3.2 %collective-permute-start = (bf16[1,848,128]{2,1,0:T(8,128)(2,1)S(1)}, bf16[1,848,128]{2,1,0:T(8,128)(2,1)S(1)}, u32[]{:S(2)}, u32[]{:S(2)}) collective-permute-start(bf16[1,848,128]{2,1,0:T(8,128)(2,1)S(1)} %get-tuple-element.24), channel_id=1, source_target_pairs={{0,4},{4,0},{8,12},{12,8},{1,5},{5,1},{9,13},{13,9},{2,6},{6,2},{1... | collective-permute-start | bytes 651272 | tf_op jit(solution)/shard_map/ppermute | solution.py:360
  3.6 12.4 %collective-permute-start.3 = (bf16[1,848,128]{2,1,0:T(8,128)(2,1)S(1)}, bf16[1,848,128]{2,1,0:T(8,128)(2,1)S(1)}, u32[]{:S(2)}, u32[]{:S(2)}) collective-permute-start(bf16[1,848,128]{2,1,0:T(8,128)(2,1)S(1)} %get-tuple-element.25), channel_id=1, source_target_pairs={{0,8},{4,12},{8,0},{12,4},{1,9},{5,13},{9,1},{13,5},{2,10},{6,14},... | collective-permute-start | bytes 651272 | tf_op jit(solution)/shard_map/ppermute | solution.py:360
  6.2 10.3 %collective-permute-start.4 = (bf16[1,848,128]{2,1,0:T(8,128)(2,1)S(1)}, bf16[1,848,128]{2,1,0:T(8,128)(2,1)S(1)}, u32[]{:S(2)}, u32[]{:S(2)}) collective-permute-start(bf16[1,848,128]{2,1,0:T(8,128)(2,1)S(1)} %get-tuple-element.26), channel_id=1, source_target_pairs={{0,12},{4,8},{8,4},{12,0},{1,13},{5,9},{9,5},{13,1},{2,14},{6,10},... | collective-permute-start | bytes 651272 | tf_op jit(solution)/shard_map/ppermute | solution.py:360
  6.3 19.5 %slice-start = ((s8[14680064]{0:T(1024)(128)(4,1)}), s8[4194304]{0:T(1024)(128)(4,1)S(1)}, s32[]{:S(2)}) async-start(s8[14680064]{0:T(1024)(128)(4,1)} %bitcast.2), calls=%async_computation | async-start | bytes 8388608
  6.3 19.5 %slice-start.1 = ((s8[14680064]{0:T(1024)(128)(4,1)}), s8[4194304]{0:T(1024)(128)(4,1)S(1)}, s32[]{:S(2)}) async-start(s8[14680064]{0:T(1024)(128)(4,1)} %bitcast.2), calls=%async_computation.1 | async-start | bytes 8388608
  12.6 13.2 %slice-start.2 = ((s8[14680064]{0:T(1024)(128)(4,1)}), s8[4194304]{0:T(1024)(128)(4,1)S(1)}, s32[]{:S(2)}) async-start(s8[14680064]{0:T(1024)(128)(4,1)} %bitcast.2), calls=%async_computation.2 | async-start | bytes 8388608
  12.6 13.2 %slice-start.3 = ((s8[14680064]{0:T(1024)(128)(4,1)}), s8[2097152]{0:T(1024)(128)(4,1)S(1)}, s32[]{:S(2)}) async-start(s8[14680064]{0:T(1024)(128)(4,1)} %bitcast.2), calls=%async_computation.3 | async-start | bytes 4194304
  12.6 11.3 %collective-permute-start.2 = (bf16[32,4096]{1,0:T(8,128)(2,1)S(1)}, bf16[32,4096]{1,0:T(8,128)(2,1)S(1)}, u32[]{:S(2)}, u32[]{:S(2)}) collective-permute-start(bf16[32,4096]{1,0:T(8,128)(2,1)S(1)} %attend.2.rest_0_), channel_id=1, source_target_pairs={{0,8},{4,12},{8,0},{12,4},{1,9},{5,13},{9,1},{13,5},{2,10},{6,14},... | collective-permute-start | bytes 786440 | tf_op jit(solution)/shard_map/ppermute | solution.py:360
  16.0 9.8 %collective-permute-start.1 = (bf16[32,4096]{1,0:T(8,128)(2,1)S(1)}, bf16[32,4096]{1,0:T(8,128)(2,1)S(1)}, u32[]{:S(2)}, u32[]{:S(2)}) collective-permute-start(bf16[32,4096]{1,0:T(8,128)(2,1)S(1)} %attend.2.rest_0_), channel_id=1, source_target_pairs={{0,4},{4,0},{8,12},{12,8},{1,5},{5,1},{9,13},{13,9},{2,6},{6,2},{1... | collective-permute-start | bytes 786440 | tf_op jit(solution)/shard_map/ppermute | solution.py:360
  23.9 1.9 %collective-permute-start.5 = (bf16[32,4096]{1,0:T(8,128)(2,1)S(1)}, bf16[32,4096]{1,0:T(8,128)(2,1)S(1)}, u32[]{:S(2)}, u32[]{:S(2)}) collective-permute-start(bf16[32,4096]{1,0:T(8,128)(2,1)S(1)} %collective-permute-done.2.rest_2_), channel_id=1, source_target_pairs={{0,4},{4,0},{8,12},{12,8},{1,5},{5,1},{9,13},{13,9},{2,6},{6,2},{1... | collective-permute-start | bytes 786440 | tf_op jit(solution)/shard_map/ppermute | solution.py:360
  24.0 8.7 %collective-permute-start.9 = (bf16[32,4096]{1,0:T(8,128)(2,1)S(1)}, bf16[32,4096]{1,0:T(8,128)(2,1)S(1)}, u32[]{:S(2)}, u32[]{:S(2)}) collective-permute-start(bf16[32,4096]{1,0:T(8,128)(2,1)S(1)} %attend.3.rest_0_), channel_id=1, source_target_pairs={{0,8},{4,12},{8,0},{12,4},{1,9},{5,13},{9,1},{13,5},{2,10},{6,14},... | collective-permute-start | bytes 786440 | tf_op jit(solution)/shard_map/ppermute | solution.py:360
  25.8 12.9 %collective-permute-start.8 = (bf16[32,4096]{1,0:T(8,128)(2,1)S(1)}, bf16[32,4096]{1,0:T(8,128)(2,1)S(1)}, u32[]{:S(2)}, u32[]{:S(2)}) collective-permute-start(bf16[32,4096]{1,0:T(8,128)(2,1)S(1)} %attend.3.rest_0_), channel_id=1, source_target_pairs={{0,4},{4,0},{8,12},{12,8},{1,5},{5,1},{9,13},{13,9},{2,6},{6,2},{1... | collective-permute-start | bytes 786440 | tf_op jit(solution)/shard_map/ppermute | solution.py:360
  26.9 5.8 %collective-permute-start.6 = (bf16[64,640]{1,0:T(8,128)(2,1)S(1)}, bf16[64,640]{1,0:T(8,128)(2,1)S(1)}, u32[]{:S(2)}, u32[]{:S(2)}) collective-permute-start(bf16[64,640]{1,0:T(8,128)(2,1)S(1)} %get-tuple-element.29), channel_id=1, source_target_pairs={{0,1},{1,0},{2,3},{3,2},{4,5},{5,4},{6,7},{7,6},{8,9},{9,8},{10,11... | collective-permute-start | bytes 245768 | tf_op jit(solution)/shard_map/ppermute | solution.py:360
  30.0 6.4 %collective-permute-start.12 = (bf16[64,1152]{1,0:T(8,128)(2,1)S(1)}, bf16[64,1152]{1,0:T(8,128)(2,1)S(1)}, u32[]{:S(2)}, u32[]{:S(2)}) collective-permute-start(bf16[64,1152]{1,0:T(8,128)(2,1)S(1)} %get-tuple-element.34), channel_id=1, source_target_pairs={{0,1},{1,0},{2,3},{3,2},{4,5},{5,4},{6,7},{7,6},{8,9},{9,8},{10,11... | collective-permute-start | bytes 442376 | tf_op jit(solution)/shard_map/ppermute | solution.py:360
  32.7 6.0 %collective-permute-start.10 = (bf16[32,4096]{1,0:T(8,128)(2,1)S(1)}, bf16[32,4096]{1,0:T(8,128)(2,1)S(1)}, u32[]{:S(2)}, u32[]{:S(2)}) collective-permute-start(bf16[32,4096]{1,0:T(8,128)(2,1)S(1)} %collective-permute-done.9.rest_2_), channel_id=1, source_target_pairs={{0,4},{4,0},{8,12},{12,8},{1,5},{5,1},{9,13},{13,9},{2,6},{6,2},{1... | collective-permute-start | bytes 786440 | tf_op jit(solution)/shard_map/ppermute | solution.py:360
  32.7 11.8 %collective-permute-start.7 = (bf16[64,640]{1,0:T(8,128)(2,1)S(1)}, bf16[64,640]{1,0:T(8,128)(2,1)S(1)}, u32[]{:S(2)}, u32[]{:S(2)}) collective-permute-start(bf16[64,640]{1,0:T(8,128)(2,1)S(1)} %add_convert_fusion.7), channel_id=1, source_target_pairs={{0,3},{1,2},{2,1},{3,0},{4,7},{5,6},{6,5},{7,4},{8,11},{9,10},{10,... | collective-permute-start | bytes 245768 | tf_op jit(solution)/shard_map/ppermute | solution.py:360
  36.5 9.3 %collective-permute-start.13 = (bf16[64,1152]{1,0:T(8,128)(2,1)S(1)}, bf16[64,1152]{1,0:T(8,128)(2,1)S(1)}, u32[]{:S(2)}, u32[]{:S(2)}) collective-permute-start(bf16[64,1152]{1,0:T(8,128)(2,1)S(1)} %add_convert_fusion.1), channel_id=1, source_target_pairs={{0,3},{1,2},{2,1},{3,0},{4,7},{5,6},{6,5},{7,4},{8,11},{9,10},{10,... | collective-permute-start | bytes 442376 | tf_op jit(solution)/shard_map/ppermute | solution.py:360
  39.4 8.1 %collective-permute-start.21 = (bf16[64,384]{1,0:T(8,128)(2,1)S(1)}, bf16[64,384]{1,0:T(8,128)(2,1)S(1)}, u32[]{:S(2)}, u32[]{:S(2)}) collective-permute-start(bf16[64,384]{1,0:T(8,128)(2,1)S(1)} %get-tuple-element.40), channel_id=1, source_target_pairs={{0,1},{1,0},{2,3},{3,2},{4,5},{5,4},{6,7},{7,6},{8,9},{9,8},{10,11... | collective-permute-start | bytes 147464 | tf_op jit(solution)/shard_map/ppermute | solution.py:360
  41.3 8.9 %collective-permute-start.18 = (bf16[64,640]{1,0:T(8,128)(2,1)S(1)}, bf16[64,640]{1,0:T(8,128)(2,1)S(1)}, u32[]{:S(2)}, u32[]{:S(2)}) collective-permute-start(bf16[64,640]{1,0:T(8,128)(2,1)S(1)} %get-tuple-element.39), channel_id=1, source_target_pairs={{0,1},{1,0},{2,3},{3,2},{4,5},{5,4},{6,7},{7,6},{8,9},{9,8},{10,11... | collective-permute-start | bytes 245768 | tf_op jit(solution)/shard_map/ppermute | solution.py:360
  43.6 7.9 %collective-permute-start.15 = (bf16[64,768]{1,0:T(8,128)(2,1)S(1)}, bf16[64,768]{1,0:T(8,128)(2,1)S(1)}, u32[]{:S(2)}, u32[]{:S(2)}) collective-permute-start(bf16[64,768]{1,0:T(8,128)(2,1)S(1)} %get-tuple-element.37), channel_id=1, source_target_pairs={{0,1},{1,0},{2,3},{3,2},{4,5},{5,4},{6,7},{7,6},{8,9},{9,8},{10,11... | collective-permute-start | bytes 294920 | tf_op jit(solution)/shard_map/ppermute | solution.py:360
  44.6 16.9 %collective-permute-start.11 = (bf16[64,640]{1,0:T(8,128)(2,1)S(1)}, bf16[64,640]{1,0:T(8,128)(2,1)S(1)}, u32[]{:S(2)}, u32[]{:S(2)}) collective-permute-start(bf16[64,640]{1,0:T(8,128)(2,1)S(1)} %add_convert_fusion.6.rest_0_), channel_id=1, source_target_pairs={{0,1},{1,0},{2,3},{3,2},{4,5},{5,4},{6,7},{7,6},{8,9},{9,8},{10,11... | collective-permute-start | bytes 245768 | tf_op jit(solution)/shard_map/ppermute | solution.py:360
  45.8 19.6 %collective-permute-start.14 = (bf16[64,1152]{1,0:T(8,128)(2,1)S(1)}, bf16[64,1152]{1,0:T(8,128)(2,1)S(1)}, u32[]{:S(2)}, u32[]{:S(2)}) collective-permute-start(bf16[64,1152]{1,0:T(8,128)(2,1)S(1)} %add_convert_fusion.rest_2_), channel_id=1, source_target_pairs={{0,1},{1,0},{2,3},{3,2},{4,5},{5,4},{6,7},{7,6},{8,9},{9,8},{10,11... | collective-permute-start | bytes 442376 | tf_op jit(solution)/shard_map/ppermute | solution.py:360
  47.5 13.5 %collective-permute-start.22 = (bf16[64,384]{1,0:T(8,128)(2,1)S(1)}, bf16[64,384]{1,0:T(8,128)(2,1)S(1)}, u32[]{:S(2)}, u32[]{:S(2)}) collective-permute-start(bf16[64,384]{1,0:T(8,128)(2,1)S(1)} %add_convert_fusion.9), channel_id=1, source_target_pairs={{0,3},{1,2},{2,1},{3,0},{4,7},{5,6},{6,5},{7,4},{8,11},{9,10},{10,... | collective-permute-start | bytes 147464 | tf_op jit(solution)/shard_map/ppermute | solution.py:360
  50.2 7.5 %collective-permute-start.19 = (bf16[64,640]{1,0:T(8,128)(2,1)S(1)}, bf16[64,640]{1,0:T(8,128)(2,1)S(1)}, u32[]{:S(2)}, u32[]{:S(2)}) collective-permute-start(bf16[64,640]{1,0:T(8,128)(2,1)S(1)} %add_convert_fusion.5), channel_id=1, source_target_pairs={{0,3},{1,2},{2,1},{3,0},{4,7},{5,6},{6,5},{7,4},{8,11},{9,10},{10,... | collective-permute-start | bytes 245768 | tf_op jit(solution)/shard_map/ppermute | solution.py:360
  51.5 7.7 %collective-permute-start.16 = (bf16[64,768]{1,0:T(8,128)(2,1)S(1)}, bf16[64,768]{1,0:T(8,128)(2,1)S(1)}, u32[]{:S(2)}, u32[]{:S(2)}) collective-permute-start(bf16[64,768]{1,0:T(8,128)(2,1)S(1)} %add_convert_fusion.3), channel_id=1, source_target_pairs={{0,3},{1,2},{2,1},{3,0},{4,7},{5,6},{6,5},{7,4},{8,11},{9,10},{10,... | collective-permute-start | bytes 294920 | tf_op jit(solution)/shard_map/ppermute | solution.py:360
  57.7 7.7 %collective-permute-start.20 = (bf16[64,640]{1,0:T(8,128)(2,1)S(1)}, bf16[64,640]{1,0:T(8,128)(2,1)S(1)}, u32[]{:S(2)}, u32[]{:S(2)}) collective-permute-start(bf16[64,640]{1,0:T(8,128)(2,1)S(1)} %add_convert_fusion.4.rest_6_), channel_id=1, source_target_pairs={{0,1},{1,0},{2,3},{3,2},{4,5},{5,4},{6,7},{7,6},{8,9},{9,8},{10,11... | collective-permute-start | bytes 245768 | tf_op jit(solution)/shard_map/ppermute | solution.py:360
  59.3 6.1 %collective-permute-start.17 = (bf16[64,768]{1,0:T(8,128)(2,1)S(1)}, bf16[64,768]{1,0:T(8,128)(2,1)S(1)}, u32[]{:S(2)}, u32[]{:S(2)}) collective-permute-start(bf16[64,768]{1,0:T(8,128)(2,1)S(1)} %add_convert_fusion.2.rest_4_), channel_id=1, source_target_pairs={{0,1},{1,0},{2,3},{3,2},{4,5},{5,4},{6,7},{7,6},{8,9},{9,8},{10,11... | collective-permute-start | bytes 294920 | tf_op jit(solution)/shard_map/ppermute | solution.py:360
  61.0 4.4 %collective-permute-start.23 = (bf16[64,384]{1,0:T(8,128)(2,1)S(1)}, bf16[64,384]{1,0:T(8,128)(2,1)S(1)}, u32[]{:S(2)}, u32[]{:S(2)}) collective-permute-start(bf16[64,384]{1,0:T(8,128)(2,1)S(1)} %add_convert_fusion.8.rest_8_), channel_id=1, source_target_pairs={{0,1},{1,0},{2,3},{3,2},{4,5},{5,4},{6,7},{7,6},{8,9},{9,8},{10,11... | collective-permute-start | bytes 147464 | tf_op jit(solution)/shard_map/ppermute | solution.py:360

commit v12 on v11

--- a/solution.py
+++ b/solution.py
@@ -291,8 +291,7 @@
 
 
 def keeps_upper(ids_ref):
-    z = ids_ref[0] // PLACES
-    return (z == 1) | (z == 2)
+    return (ids_ref[0] // PLACES) % 2 == 1
 
 
 def order_kernel(layout, ids_ref, pick_ref, *rest):
@@ -484,25 +483,29 @@
     def swap(piece):
         return flip(piece[1], "head", 1)
 
-    far = [far_rows, flip(far_rows, "seq", 1), far_across, flip(far_across, "seq", 1)]
     half = steps * sources * requests // 2
 
     def cut(parts, first_row, shares):
         groups = columns // LANES
         edges = [LANES * (groups * sum(shares[:i]) // sum(shares)) for i in range(len(shares) + 1)]
-        return [(parts, first_row, at, end - at) for at, end in zip(edges, edges[1:])]
-
-    near_pieces, far_pieces = cut(near, 0, (5, 9)), cut(far, half, (6, 5, 3))
-    made = []
-    for parts, first_row, first_col, cols in near_pieces + far_pieces:
-        keep, send = project(parts, first_col, cols)
-        made.append((first_row, first_col, keep, swap((keep, send))))
-    pairs = [add(keep, incoming) for _, _, keep, incoming in made]
-    crossed = [flip(pair, "head", 3) for pair in pairs]
+        made = []
+        for at, end in zip(edges, edges[1:]):
+            keep, send = project(parts, at, end - at)
+            made.append((first_row, at, keep, swap((keep, send))))
+        return made
+
+    near_made = cut(near, 0, (5, 9))
+    pairs = [add(near_made[0][2], near_made[0][3])]
+    relayed = far_across
+    far = [far_rows, flip(far_rows, "seq", 1), far_across, flip(relayed, "seq", 1)]
+    far_made = cut(far, half, (6, 5, 3))
+    made = near_made + far_made
+    pairs += [add(keep, incoming) for _, _, keep, incoming in made[1:]]
+    crossed = [flip(pair, "head", 2) for pair in pairs]
     last_made = made[-1][2]
     arrays = []
     for i, (pair, cross) in enumerate(zip(pairs, crossed)):
-        if i < len(near_pieces):
+        if i < len(near_made):
             cross = after(cross, last_made)
         total = add(pair, cross)
         arrays += [total, flip(total, "head", 1)]

time: 67.1 us -> 70.4 us (1.049)
  waiting for transfers between devices: 11.5 us -> 16.8 us
  starting transfers between devices: 31.4 us -> 29.6 us
    ppermute x24, waiting for transfers between devices: 11.5 us -> 16.8 us  [flip(): return lax.ppermute(x, axis, [(i, i ^ distance) for i in range(size)])]
    ppermute x24, starting transfers between devices: 31.4 us -> 29.6 us  [flip(): return lax.ppermute(x, axis, [(i, i ^ distance) for i in range(size)])]
  transfers between devices with their start and end apart: 24 -> 24, of which waited for: 5 -> 7; matrix products, arithmetic and copies ran while one was open for 0% -> 0% of each run, Pallas kernels for 28% -> 27%
where the time goes in v12:
time: 70.4 us; the launch traced here: 70.3 us
  starting transfers between devices  29.6 us (42%)
  Pallas kernels  22.5 us (32%)
  waiting for transfers between devices  16.8 us (24%)
  local copies, waits for them, and re-layouts  0.82 us (1%)
    ppermute x24, starting transfers between devices, flip(): return lax.ppermute(x, axis, [(i, i ^ distance) for i in range(size)])  29.6 us
    ppermute x24, waiting for transfers between devices, flip(): return lax.ppermute(x, axis, [(i, i ^ distance) for i in range(size)])  16.8 us
    pallas_call x2, Pallas kernels, attend(): pl.pallas_call(functools.partial(attend_kernel, sizes, scale, relative, b...  13.5 us
    pallas_call x5, Pallas kernels, project(): pl.pallas_call(functools.partial(project_kernel, first_col), out_shape=[j...  5.29 us
    pallas_call x1, Pallas kernels, order(): pl.pallas_call(kernel, out_shape=jax.ShapeDtypeStruct((steps, sources * r...  1.43 us
  transfers between devices with their start and end apart: 24, of which 7 were waited for; matrix products, arithmetic and copies ran while one was open for 0% of the time, Pallas kernels for 27%

profile of v12, /device:TPU:0, one launch (start us, length us, event | category | flops | bytes accessed | tf_op | source)
XLA Modules:
  0.0 70.3 jit_solution(13330601552098745722)
XLA Ops:
  0.0 0.7 %copy-done.6 = s32[64]{0:T(128)S(1)} copy-done((s32[64]{0:T(128)S(1)}, s32[64]{0:T(128)}, u32[]{:S(2)}) %copy-start.6) | copy-done | bytes 280
  0.8 1.1 %place_rows.1.after_ref.pick_ref = bf16[4,64,256]{2,1,0:T(8,128)(2,1)S(1)} custom-call(s32[1]{0:T(128)} %bitcast.ids_ref, s32[64]{0:T(128)S(1)} %copy-done.6), custom_call_target="tpu_custom_call" | custom-call | flops 2000000000 | bytes 6000000 | tf_op jit(solution)/shard_map/place_rows/pallas_call | solution.py:383
  1.9 0.0 slice-start.5
  1.9 0.0 copy-start
  1.9 0.0 copy-start.1
  1.9 0.0 copy-start.5
  1.9 0.0 copy-start.7
  1.9 1.1 %pack_queries.1 = (bf16[1,848,128]{2,1,0:T(8,128)(2,1)S(1)}, bf16[1,848,128]{2,1,0:T(8,128)(2,1)S(1)}, bf16[1,848,128]{2,1,0:T(8,128)(2,1)S(1)}, bf16[1,848,128]{2,1,0:T(8,128)(2,1)S(1)}) custom-call(s32[1]{0:T(128)} %bitcast.ids_ref, s32[64]{0:T(128)S(1)} %copy-done.6, bf16[4,16,32,128]{3,2,1,0:T(8,128)(2,1)S(1)} %copy-done.2, ...), custom_call_target="tpu_custom_call" | custom-call | flops 6000000000 | bytes 18000000 | tf_op jit(solution)/shard_map/pack_queries/pallas_call | solution.py:395
  3.1 0.5 collective-permute-start
  3.6 2.6 %collective-permute-start.3 = (bf16[1,848,128]{2,1,0:T(8,128)(2,1)S(1)}, bf16[1,848,128]{2,1,0:T(8,128)(2,1)S(1)}, u32[]{:S(2)}, u32[]{:S(2)}) collective-permute-start(bf16[1,848,128]{2,1,0:T(8,128)(2,1)S(1)} %get-tuple-element.25), channel_id=1, source_target_pairs={{0,8},{4,12},{8,0},{12,4},{1,9},{5,13},{9,1},{13,5},{2,10},{6,14},... | collective-permute-start | bytes 651272 | tf_op jit(solution)/shard_map/ppermute | solution.py:359
  6.2 0.1 collective-permute-start.4
  6.3 0.0 slice-start
  6.4 6.2 %attend.2.rest_0_ = bf16[32,4096]{1,0:T(8,128)(2,1)S(1)} custom-call(s32[1]{0:T(128)} %bitcast.ids_ref, s32[64]{0:T(128)S(1)} %copy-done.7, s32[4,16]{1,0:T(4,128)S(1)} %copy-done.5, bf16[1,848,128]{2,1,0:T(8,128)(2,1)S(1)} %get-tuple-element.23.rest_0_, bf16[1,848,128]{2,1,0:T(8,128)(2,1)S(1)} %collective-permute-done.rest_1_, ...), custom_call_target="tpu_custom_call" | custom-call | flops 8000000000 | bytes 24000000 | tf_op jit(solution)/shard_map/attend/pallas_call | solution.py:413
  12.6 0.0 slice-start.2
  12.6 2.5 %collective-permute-start.2 = (bf16[32,4096]{1,0:T(8,128)(2,1)S(1)}, bf16[32,4096]{1,0:T(8,128)(2,1)S(1)}, u32[]{:S(2)}, u32[]{:S(2)}) collective-permute-start(bf16[32,4096]{1,0:T(8,128)(2,1)S(1)} %attend.2.rest_0_), channel_id=1, source_target_pairs={{0,8},{4,12},{8,0},{12,4},{1,9},{5,13},{9,1},{13,5},{2,10},{6,14},... | collective-permute-start | bytes 786440 | tf_op jit(solution)/shard_map/ppermute | solution.py:359
  15.1 0.4 collective-permute-start.1
  15.5 1.0 %collective-permute-done.4.rest_1_ = bf16[1,848,128]{2,1,0:T(8,128)(2,1)S(1)} collective-permute-done((bf16[1,848,128]{2,1,0:T(8,128)(2,1)S(1)}, bf16[1,848,128]{2,1,0:T(8,128)(2,1)S(1)}, u32[]{:S(2)}, u32[]{:S(2)}) %collective-permute-start.4) | collective-permute-done | bytes 217120 | tf_op jit(solution)/shard_map/ppermute | solution.py:359
  16.5 7.3 %attend.3.rest_0_ = bf16[32,4096]{1,0:T(8,128)(2,1)S(1)} custom-call(s32[1]{0:T(128)} %bitcast.ids_ref, s32[64]{0:T(128)S(1)} %copy-done.7, s32[4,16]{1,0:T(4,128)S(1)} %copy-done.5, bf16[1,848,128]{2,1,0:T(8,128)(2,1)S(1)} %collective-permute-done.3.rest_0_, bf16[1,848,128]{2,1,0:T(8,128)(2,1)S(1)} %collective-permute-done.4.rest_1_, ...), custom_call_target="tpu_custom_call" | custom-call | flops 8000000000 | bytes 24000000 | tf_op jit(solution)/shard_map/attend/pallas_call | solution.py:413
  23.8 0.1 collective-permute-start.5
  23.9 1.9 %collective-permute-start.9 = (bf16[32,4096]{1,0:T(8,128)(2,1)S(1)}, bf16[32,4096]{1,0:T(8,128)(2,1)S(1)}, u32[]{:S(2)}, u32[]{:S(2)}) collective-permute-start(bf16[32,4096]{1,0:T(8,128)(2,1)S(1)} %attend.3.rest_0_), channel_id=1, source_target_pairs={{0,8},{4,12},{8,0},{12,4},{1,9},{5,13},{9,1},{13,5},{2,10},{6,14},... | collective-permute-start | bytes 786440 | tf_op jit(solution)/shard_map/ppermute | solution.py:359
  25.9 1.0 %project_out.5 = (bf16[64,640]{1,0:T(8,128)(2,1)S(1)}, bf16[64,640]{1,0:T(8,128)(2,1)S(1)}) custom-call(s32[1]{0:T(128)} %bitcast.ids_ref, bf16[32,4096]{1,0:T(8,128)(2,1)S(1)} %attend.2.rest_0_, bf16[32,4096]{1,0:T(8,128)(2,1)S(1)} %collective-permute-done.1.rest_1_, bf16[32,4096]{1,0:T(8,128)(2,1)S(1)} %collective-permute-done.2.rest_2_, ...), custom_call_target="tpu_custom_call" | custom-call | flops 2000000000 | bytes 6000000 | tf_op jit(solution)/shard_map/project_out/pallas_call | solution.py:462
  26.9 1.6 %collective-permute-start.6 = (bf16[64,640]{1,0:T(8,128)(2,1)S(1)}, bf16[64,640]{1,0:T(8,128)(2,1)S(1)}, u32[]{:S(2)}, u32[]{:S(2)}) collective-permute-start(bf16[64,640]{1,0:T(8,128)(2,1)S(1)} %get-tuple-element.29), channel_id=1, source_target_pairs={{0,1},{1,0},{2,3},{3,2},{4,5},{5,4},{6,7},{7,6},{8,9},{9,8},{10,11... | collective-permute-start | bytes 245768 | tf_op jit(solution)/shard_map/ppermute | solution.py:359
  28.5 1.5 %project_out.7 = (bf16[64,1152]{1,0:T(8,128)(2,1)S(1)}, bf16[64,1152]{1,0:T(8,128)(2,1)S(1)}) custom-call(s32[1]{0:T(128)} %bitcast.ids_ref, bf16[32,4096]{1,0:T(8,128)(2,1)S(1)} %attend.2.rest_0_, bf16[32,4096]{1,0:T(8,128)(2,1)S(1)} %collective-permute-done.1.rest_1_, bf16[32,4096]{1,0:T(8,128)(2,1)S(1)} %collective-permute-done.2.rest_2_, ...), custom_call_target="tpu_custom_call" | custom-call | flops 2000000000 | bytes 6000000 | tf_op jit(solution)/shard_map/project_out/pallas_call | solution.py:462
  30.1 0.5 collective-permute-start.12
  30.6 2.1 %collective-permute-done.9.rest_2_ = bf16[32,4096]{1,0:T(8,128)(2,1)S(1)} collective-permute-done((bf16[32,4096]{1,0:T(8,128)(2,1)S(1)}, bf16[32,4096]{1,0:T(8,128)(2,1)S(1)}, u32[]{:S(2)}, u32[]{:S(2)}) %collective-permute-start.9) | collective-permute-done | bytes 262176 | tf_op jit(solution)/shard_map/ppermute | solution.py:359
  32.7 2.7 %collective-permute-start.7 = (bf16[64,640]{1,0:T(8,128)(2,1)S(1)}, bf16[64,640]{1,0:T(8,128)(2,1)S(1)}, u32[]{:S(2)}, u32[]{:S(2)}) collective-permute-start(bf16[64,640]{1,0:T(8,128)(2,1)S(1)} %add_convert_fusion.7), channel_id=1, source_target_pairs={{0,2},{1,3},{2,0},{3,1},{4,6},{5,7},{6,4},{7,5},{8,10},{9,11},{10,... | collective-permute-start | bytes 245768 | tf_op jit(solution)/shard_map/ppermute | solution.py:359
  35.4 0.7 %collective-permute-done.12 = bf16[64,1152]{1,0:T(8,128)(2,1)S(1)} collective-permute-done((bf16[64,1152]{1,0:T(8,128)(2,1)S(1)}, bf16[64,1152]{1,0:T(8,128)(2,1)S(1)}, u32[]{:S(2)}, u32[]{:S(2)}) %collective-permute-start.12) | collective-permute-done | bytes 147488 | tf_op jit(solution)/shard_map/ppermute | solution.py:359
  36.1 2.9 %collective-permute-start.13 = (bf16[64,1152]{1,0:T(8,128)(2,1)S(1)}, bf16[64,1152]{1,0:T(8,128)(2,1)S(1)}, u32[]{:S(2)}, u32[]{:S(2)}) collective-permute-start(bf16[64,1152]{1,0:T(8,128)(2,1)S(1)} %add_convert_fusion.1), channel_id=1, source_target_pairs={{0,2},{1,3},{2,0},{3,1},{4,6},{5,7},{6,4},{7,5},{8,10},{9,11},{10,... | collective-permute-start | bytes 442376 | tf_op jit(solution)/shard_map/ppermute | solution.py:359
  39.1 0.7 %project_out.6 = (bf16[64,384]{1,0:T(8,128)(2,1)S(1)}, bf16[64,384]{1,0:T(8,128)(2,1)S(1)}) custom-call(s32[1]{0:T(128)} %bitcast.ids_ref, bf16[32,4096]{1,0:T(8,128)(2,1)S(1)} %attend.3.rest_0_, bf16[32,4096]{1,0:T(8,128)(2,1)S(1)} %collective-permute-done.8.rest_1_, bf16[32,4096]{1,0:T(8,128)(2,1)S(1)} %collective-permute-done.9.rest_2_, ...), custom_call_target="tpu_custom_call" | custom-call | flops 2000000000 | bytes 6000000 | tf_op jit(solution)/shard_map/project_out/pallas_call | solution.py:462
  39.8 0.2 collective-permute-start.21
  40.0 1.0 %project_out.9 = (bf16[64,640]{1,0:T(8,128)(2,1)S(1)}, bf16[64,640]{1,0:T(8,128)(2,1)S(1)}) custom-call(s32[1]{0:T(128)} %bitcast.ids_ref, bf16[32,4096]{1,0:T(8,128)(2,1)S(1)} %attend.3.rest_0_, bf16[32,4096]{1,0:T(8,128)(2,1)S(1)} %collective-permute-done.8.rest_1_, bf16[32,4096]{1,0:T(8,128)(2,1)S(1)} %collective-permute-done.9.rest_2_, ...), custom_call_target="tpu_custom_call" | custom-call | flops 2000000000 | bytes 6000000 | tf_op jit(solution)/shard_map/project_out/pallas_call | solution.py:462
  41.0 1.9 %collective-permute-start.18 = (bf16[64,640]{1,0:T(8,128)(2,1)S(1)}, bf16[64,640]{1,0:T(8,128)(2,1)S(1)}, u32[]{:S(2)}, u32[]{:S(2)}) collective-permute-start(bf16[64,640]{1,0:T(8,128)(2,1)S(1)} %get-tuple-element.39), channel_id=1, source_target_pairs={{0,1},{1,0},{2,3},{3,2},{4,5},{5,4},{6,7},{7,6},{8,9},{9,8},{10,11... | collective-permute-start | bytes 245768 | tf_op jit(solution)/shard_map/ppermute | solution.py:359
  43.0 1.0 %project_out.8 = (bf16[64,768]{1,0:T(8,128)(2,1)S(1)}, bf16[64,768]{1,0:T(8,128)(2,1)S(1)}) custom-call(s32[1]{0:T(128)} %bitcast.ids_ref, bf16[32,4096]{1,0:T(8,128)(2,1)S(1)} %attend.3.rest_0_, bf16[32,4096]{1,0:T(8,128)(2,1)S(1)} %collective-permute-done.8.rest_1_, bf16[32,4096]{1,0:T(8,128)(2,1)S(1)} %collective-permute-done.9.rest_2_, ...), custom_call_target="tpu_custom_call" | custom-call | flops 2000000000 | bytes 6000000 | tf_op jit(solution)/shard_map/project_out/pallas_call | solution.py:462
  44.0 0.2 collective-permute-start.15
  44.3 1.9 %collective-permute-start.11 = (bf16[64,640]{1,0:T(8,128)(2,1)S(1)}, bf16[64,640]{1,0:T(8,128)(2,1)S(1)}, u32[]{:S(2)}, u32[]{:S(2)}) collective-permute-start(bf16[64,640]{1,0:T(8,128)(2,1)S(1)} %add_convert_fusion.6.rest_0_), channel_id=1, source_target_pairs={{0,1},{1,0},{2,3},{3,2},{4,5},{5,4},{6,7},{7,6},{8,9},{9,8},{10,11... | collective-permute-start | bytes 245768 | tf_op jit(solution)/shard_map/ppermute | solution.py:359
  46.2 0.5 collective-permute-done.13
  46.7 0.7 %collective-permute-start.14 = (bf16[64,1152]{1,0:T(8,128)(2,1)S(1)}, bf16[64,1152]{1,0:T(8,128)(2,1)S(1)}, u32[]{:S(2)}, u32[]{:S(2)}) collective-permute-start(bf16[64,1152]{1,0:T(8,128)(2,1)S(1)} %add_convert_fusion.rest_2_), channel_id=1, source_target_pairs={{0,1},{1,0},{2,3},{3,2},{4,5},{5,4},{6,7},{7,6},{8,9},{9,8},{10,11... | collective-permute-start | bytes 442376 | tf_op jit(solution)/shard_map/ppermute | solution.py:359
  47.5 3.5 %collective-permute-start.22 = (bf16[64,384]{1,0:T(8,128)(2,1)S(1)}, bf16[64,384]{1,0:T(8,128)(2,1)S(1)}, u32[]{:S(2)}, u32[]{:S(2)}) collective-permute-start(bf16[64,384]{1,0:T(8,128)(2,1)S(1)} %add_convert_fusion.9), channel_id=1, source_target_pairs={{0,2},{1,3},{2,0},{3,1},{4,6},{5,7},{6,4},{7,5},{8,10},{9,11},{10,... | collective-permute-start | bytes 147464 | tf_op jit(solution)/shard_map/ppermute | solution.py:359
  51.0 0.1 collective-permute-start.19
  51.1 0.0 collective-permute-done.15
  51.2 2.9 %collective-permute-start.16 = (bf16[64,768]{1,0:T(8,128)(2,1)S(1)}, bf16[64,768]{1,0:T(8,128)(2,1)S(1)}, u32[]{:S(2)}, u32[]{:S(2)}) collective-permute-start(bf16[64,768]{1,0:T(8,128)(2,1)S(1)} %add_convert_fusion.3), channel_id=1, source_target_pairs={{0,2},{1,3},{2,0},{3,1},{4,6},{5,7},{6,4},{7,5},{8,10},{9,11},{10,... | collective-permute-start | bytes 294920 | tf_op jit(solution)/shard_map/ppermute | solution.py:359
  54.1 7.1 %collective-permute-done.19 = bf16[64,640]{1,0:T(8,128)(2,1)S(1)} collective-permute-done((bf16[64,640]{1,0:T(8,128)(2,1)S(1)}, bf16[64,640]{1,0:T(8,128)(2,1)S(1)}, u32[]{:S(2)}, u32[]{:S(2)}) %collective-permute-start.19) | collective-permute-done | bytes 81952 | tf_op jit(solution)/shard_map/ppermute | solution.py:359
  61.2 0.1 collective-permute-start.20
  61.3 1.4 %collective-permute-done.16 = bf16[64,768]{1,0:T(8,128)(2,1)S(1)} collective-permute-done((bf16[64,768]{1,0:T(8,128)(2,1)S(1)}, bf16[64,768]{1,0:T(8,128)(2,1)S(1)}, u32[]{:S(2)}, u32[]{:S(2)}) %collective-permute-start.16) | collective-permute-done | bytes 98336 | tf_op jit(solution)/shard_map/ppermute | solution.py:359
  62.7 0.7 %collective-permute-start.17 = (bf16[64,768]{1,0:T(8,128)(2,1)S(1)}, bf16[64,768]{1,0:T(8,128)(2,1)S(1)}, u32[]{:S(2)}, u32[]{:S(2)}) collective-permute-start(bf16[64,768]{1,0:T(8,128)(2,1)S(1)} %add_convert_fusion.2.rest_4_), channel_id=1, source_target_pairs={{0,1},{1,0},{2,3},{3,2},{4,5},{5,4},{6,7},{7,6},{8,9},{9,8},{10,11... | collective-permute-start | bytes 294920 | tf_op jit(solution)/shard_map/ppermute | solution.py:359
  63.4 1.4 %collective-permute-start.23 = (bf16[64,384]{1,0:T(8,128)(2,1)S(1)}, bf16[64,384]{1,0:T(8,128)(2,1)S(1)}, u32[]{:S(2)}, u32[]{:S(2)}) collective-permute-start(bf16[64,384]{1,0:T(8,128)(2,1)S(1)} %add_convert_fusion.8.rest_8_), channel_id=1, source_target_pairs={{0,1},{1,0},{2,3},{3,2},{4,5},{5,4},{6,7},{7,6},{8,9},{9,8},{10,11... | collective-permute-start | bytes 147464 | tf_op jit(solution)/shard_map/ppermute | solution.py:359
  64.9 4.0 %collective-permute-done.23.rest_9_ = bf16[64,384]{1,0:T(8,128)(2,1)S(1)} collective-permute-done((bf16[64,384]{1,0:T(8,128)(2,1)S(1)}, bf16[64,384]{1,0:T(8,128)(2,1)S(1)}, u32[]{:S(2)}, u32[]{:S(2)}) %collective-permute-start.23) | collective-permute-done | bytes 49184 | tf_op jit(solution)/shard_map/ppermute | solution.py:359
  68.8 1.4 %order_rows.1 = bf16[4,64,1792]{2,1,0:T(8,128)(2,1)} custom-call(s32[1]{0:T(128)} %bitcast.ids_ref, bf16[4,64,256]{2,1,0:T(8,128)(2,1)S(1)} %place_rows.1.after_ref.pick_ref, bf16[64,640]{1,0:T(8,128)(2,1)S(1)} %add_convert_fusion.6.rest_0_, bf16[64,640]{1,0:T(8,128)(2,1)S(1)} %collective-permute-done.11.rest_1_, ...), custom_call_target="tpu_custom_call" | custom-call | flops 2000000000 | bytes 6000000 | tf_op jit(solution)/shard_map/order_rows/pallas_call | solution.py:439
  (50 shorter events, 0.3 us)
Async XLA Ops:
  0.0 1.8 %copy-start.2 = (bf16[4,16,32,128]{3,2,1,0:T(8,128)(2,1)S(1)}, bf16[4,16,32,128]{3,2,1,0:T(8,128)(2,1)}, u32[]{:S(2)}) copy-start(bf16[4,16,32,128]{3,2,1,0:T(8,128)(2,1)} %nope_ref.1) | copy-start | bytes 1572868
  0.0 1.9 %copy-start.3 = (bf16[4,16,32,64]{3,2,1,0:T(8,128)(2,1)S(1)}, bf16[4,16,32,64]{3,2,1,0:T(8,128)(2,1)}, u32[]{:S(2)}) copy-start(bf16[4,16,32,64]{3,2,1,0:T(8,128)(2,1)} %rope_ref.1) | copy-start | bytes 786436
  0.0 1.9 %copy-start.4 = (bf16[4,16,576]{2,1,0:T(8,128)(2,1)S(1)}, bf16[4,16,576]{2,1,0:T(8,128)(2,1)}, u32[]{:S(2)}) copy-start(bf16[4,16,576]{2,1,0:T(8,128)(2,1)} %fresh_ref.1) | copy-start | bytes 221188
  0.0 0.7 %copy-start.6 = (s32[64]{0:T(128)S(1)}, s32[64]{0:T(128)}, u32[]{:S(2)}) copy-start(s32[64]{0:T(128)} %decode_ref.7) | copy-start | bytes 772
  0.8 5.5 %slice-start.4 = ((s8[4718592]{0:T(1024)(128)(4,1)}), s8[4194304]{0:T(1024)(128)(4,1)S(1)}, s32[]{:S(2)}) async-start(s8[4718592]{0:T(1024)(128)(4,1)} %bitcast.4), calls=%async_computation.4 | async-start | bytes 8388608
  1.9 4.4 %slice-start.5 = ((s8[4718592]{0:T(1024)(128)(4,1)}), s8[524288]{0:T(1024)(128)(4,1)S(1)}, s32[]{:S(2)}) async-start(s8[4718592]{0:T(1024)(128)(4,1)} %bitcast.4), calls=%async_computation.5 | async-start | bytes 1048576
  1.9 4.4 %copy-start = (bf16[32,128,512]{2,1,0:T(8,128)(2,1)S(1)}, bf16[32,128,512]{2,1,0:T(8,128)(2,1)}, u32[]{:S(2)}) copy-start(bf16[32,128,512]{2,1,0:T(8,128)(2,1)} %rest_3_.3) | copy-start | bytes 12582916
  1.9 4.4 %copy-start.1 = (bf16[32,512,128]{2,1,0:T(8,128)(2,1)S(1)}, bf16[32,512,128]{2,1,0:T(8,128)(2,1)}, u32[]{:S(2)}) copy-start(bf16[32,512,128]{2,1,0:T(8,128)(2,1)} %rest_4_.8) | copy-start | bytes 12582916
  1.9 4.4 %copy-start.5 = (s32[4,16]{1,0:T(4,128)S(1)}, s32[4,16]{1,0:T(4,128)}, u32[]{:S(2)}) copy-start(s32[4,16]{1,0:T(4,128)} %length_ref.3) | copy-start | bytes 772
  1.9 4.4 %copy-start.7 = (s32[64]{0:T(128)S(1)}, s32[64]{0:T(128)}, u32[]{:S(2)}) copy-start(s32[64]{0:T(128)} %decode_ref.7) | copy-start | bytes 772
  3.1 3.2 %collective-permute-start = (bf16[1,848,128]{2,1,0:T(8,128)(2,1)S(1)}, bf16[1,848,128]{2,1,0:T(8,128)(2,1)S(1)}, u32[]{:S(2)}, u32[]{:S(2)}) collective-permute-start(bf16[1,848,128]{2,1,0:T(8,128)(2,1)S(1)} %get-tuple-element.24), channel_id=1, source_target_pairs={{0,4},{4,0},{8,12},{12,8},{1,5},{5,1},{9,13},{13,9},{2,6},{6,2},{1... | collective-permute-start | bytes 651272 | tf_op jit(solution)/shard_map/ppermute | solution.py:359
  3.6 11.9 %collective-permute-start.3 = (bf16[1,848,128]{2,1,0:T(8,128)(2,1)S(1)}, bf16[1,848,128]{2,1,0:T(8,128)(2,1)S(1)}, u32[]{:S(2)}, u32[]{:S(2)}) collective-permute-start(bf16[1,848,128]{2,1,0:T(8,128)(2,1)S(1)} %get-tuple-element.25), channel_id=1, source_target_pairs={{0,8},{4,12},{8,0},{12,4},{1,9},{5,13},{9,1},{13,5},{2,10},{6,14},... | collective-permute-start | bytes 651272 | tf_op jit(solution)/shard_map/ppermute | solution.py:359
  6.2 10.3 %collective-permute-start.4 = (bf16[1,848,128]{2,1,0:T(8,128)(2,1)S(1)}, bf16[1,848,128]{2,1,0:T(8,128)(2,1)S(1)}, u32[]{:S(2)}, u32[]{:S(2)}) collective-permute-start(bf16[1,848,128]{2,1,0:T(8,128)(2,1)S(1)} %get-tuple-element.26), channel_id=1, source_target_pairs={{0,12},{4,8},{8,4},{12,0},{1,13},{5,9},{9,5},{13,1},{2,14},{6,10},... | collective-permute-start | bytes 651272 | tf_op jit(solution)/shard_map/ppermute | solution.py:359
  6.3 19.5 %slice-start = ((s8[14680064]{0:T(1024)(128)(4,1)}), s8[4194304]{0:T(1024)(128)(4,1)S(1)}, s32[]{:S(2)}) async-start(s8[14680064]{0:T(1024)(128)(4,1)} %bitcast.2), calls=%async_computation | async-start | bytes 8388608
  6.3 19.5 %slice-start.1 = ((s8[14680064]{0:T(1024)(128)(4,1)}), s8[4194304]{0:T(1024)(128)(4,1)S(1)}, s32[]{:S(2)}) async-start(s8[14680064]{0:T(1024)(128)(4,1)} %bitcast.2), calls=%async_computation.1 | async-start | bytes 8388608
  12.6 13.2 %slice-start.2 = ((s8[14680064]{0:T(1024)(128)(4,1)}), s8[4194304]{0:T(1024)(128)(4,1)S(1)}, s32[]{:S(2)}) async-start(s8[14680064]{0:T(1024)(128)(4,1)} %bitcast.2), calls=%async_computation.2 | async-start | bytes 8388608
  12.6 13.2 %slice-start.3 = ((s8[14680064]{0:T(1024)(128)(4,1)}), s8[2097152]{0:T(1024)(128)(4,1)S(1)}, s32[]{:S(2)}) async-start(s8[14680064]{0:T(1024)(128)(4,1)} %bitcast.2), calls=%async_computation.3 | async-start | bytes 4194304
  12.6 11.2 %collective-permute-start.2 = (bf16[32,4096]{1,0:T(8,128)(2,1)S(1)}, bf16[32,4096]{1,0:T(8,128)(2,1)S(1)}, u32[]{:S(2)}, u32[]{:S(2)}) collective-permute-start(bf16[32,4096]{1,0:T(8,128)(2,1)S(1)} %attend.2.rest_0_), channel_id=1, source_target_pairs={{0,8},{4,12},{8,0},{12,4},{1,9},{5,13},{9,1},{13,5},{2,10},{6,14},... | collective-permute-start | bytes 786440 | tf_op jit(solution)/shard_map/ppermute | solution.py:359
  15.1 10.7 %collective-permute-start.1 = (bf16[32,4096]{1,0:T(8,128)(2,1)S(1)}, bf16[32,4096]{1,0:T(8,128)(2,1)S(1)}, u32[]{:S(2)}, u32[]{:S(2)}) collective-permute-start(bf16[32,4096]{1,0:T(8,128)(2,1)S(1)} %attend.2.rest_0_), channel_id=1, source_target_pairs={{0,4},{4,0},{8,12},{12,8},{1,5},{5,1},{9,13},{13,9},{2,6},{6,2},{1... | collective-permute-start | bytes 786440 | tf_op jit(solution)/shard_map/ppermute | solution.py:359
  23.8 2.0 %collective-permute-start.5 = (bf16[32,4096]{1,0:T(8,128)(2,1)S(1)}, bf16[32,4096]{1,0:T(8,128)(2,1)S(1)}, u32[]{:S(2)}, u32[]{:S(2)}) collective-permute-start(bf16[32,4096]{1,0:T(8,128)(2,1)S(1)} %collective-permute-done.2.rest_2_), channel_id=1, source_target_pairs={{0,4},{4,0},{8,12},{12,8},{1,5},{5,1},{9,13},{13,9},{2,6},{6,2},{1... | collective-permute-start | bytes 786440 | tf_op jit(solution)/shard_map/ppermute | solution.py:359
  23.9 8.7 %collective-permute-start.9 = (bf16[32,4096]{1,0:T(8,128)(2,1)S(1)}, bf16[32,4096]{1,0:T(8,128)(2,1)S(1)}, u32[]{:S(2)}, u32[]{:S(2)}) collective-permute-start(bf16[32,4096]{1,0:T(8,128)(2,1)S(1)} %attend.3.rest_0_), channel_id=1, source_target_pairs={{0,8},{4,12},{8,0},{12,4},{1,9},{5,13},{9,1},{13,5},{2,10},{6,14},... | collective-permute-start | bytes 786440 | tf_op jit(solution)/shard_map/ppermute | solution.py:359
  25.8 13.3 %collective-permute-start.8 = (bf16[32,4096]{1,0:T(8,128)(2,1)S(1)}, bf16[32,4096]{1,0:T(8,128)(2,1)S(1)}, u32[]{:S(2)}, u32[]{:S(2)}) collective-permute-start(bf16[32,4096]{1,0:T(8,128)(2,1)S(1)} %attend.3.rest_0_), channel_id=1, source_target_pairs={{0,4},{4,0},{8,12},{12,8},{1,5},{5,1},{9,13},{13,9},{2,6},{6,2},{1... | collective-permute-start | bytes 786440 | tf_op jit(solution)/shard_map/ppermute | solution.py:359
  26.9 5.8 %collective-permute-start.6 = (bf16[64,640]{1,0:T(8,128)(2,1)S(1)}, bf16[64,640]{1,0:T(8,128)(2,1)S(1)}, u32[]{:S(2)}, u32[]{:S(2)}) collective-permute-start(bf16[64,640]{1,0:T(8,128)(2,1)S(1)} %get-tuple-element.29), channel_id=1, source_target_pairs={{0,1},{1,0},{2,3},{3,2},{4,5},{5,4},{6,7},{7,6},{8,9},{9,8},{10,11... | collective-permute-start | bytes 245768 | tf_op jit(solution)/shard_map/ppermute | solution.py:359
  30.1 6.0 %collective-permute-start.12 = (bf16[64,1152]{1,0:T(8,128)(2,1)S(1)}, bf16[64,1152]{1,0:T(8,128)(2,1)S(1)}, u32[]{:S(2)}, u32[]{:S(2)}) collective-permute-start(bf16[64,1152]{1,0:T(8,128)(2,1)S(1)} %get-tuple-element.34), channel_id=1, source_target_pairs={{0,1},{1,0},{2,3},{3,2},{4,5},{5,4},{6,7},{7,6},{8,9},{9,8},{10,11... | collective-permute-start | bytes 442376 | tf_op jit(solution)/shard_map/ppermute | solution.py:359
  32.6 6.4 %collective-permute-start.10 = (bf16[32,4096]{1,0:T(8,128)(2,1)S(1)}, bf16[32,4096]{1,0:T(8,128)(2,1)S(1)}, u32[]{:S(2)}, u32[]{:S(2)}) collective-permute-start(bf16[32,4096]{1,0:T(8,128)(2,1)S(1)} %collective-permute-done.9.rest_2_), channel_id=1, source_target_pairs={{0,4},{4,0},{8,12},{12,8},{1,5},{5,1},{9,13},{13,9},{2,6},{6,2},{1... | collective-permute-start | bytes 786440 | tf_op jit(solution)/shard_map/ppermute | solution.py:359
  32.7 11.6 %collective-permute-start.7 = (bf16[64,640]{1,0:T(8,128)(2,1)S(1)}, bf16[64,640]{1,0:T(8,128)(2,1)S(1)}, u32[]{:S(2)}, u32[]{:S(2)}) collective-permute-start(bf16[64,640]{1,0:T(8,128)(2,1)S(1)} %add_convert_fusion.7), channel_id=1, source_target_pairs={{0,2},{1,3},{2,0},{3,1},{4,6},{5,7},{6,4},{7,5},{8,10},{9,11},{10,... | collective-permute-start | bytes 245768 | tf_op jit(solution)/shard_map/ppermute | solution.py:359
  36.1 10.5 %collective-permute-start.13 = (bf16[64,1152]{1,0:T(8,128)(2,1)S(1)}, bf16[64,1152]{1,0:T(8,128)(2,1)S(1)}, u32[]{:S(2)}, u32[]{:S(2)}) collective-permute-start(bf16[64,1152]{1,0:T(8,128)(2,1)S(1)} %add_convert_fusion.1), channel_id=1, source_target_pairs={{0,2},{1,3},{2,0},{3,1},{4,6},{5,7},{6,4},{7,5},{8,10},{9,11},{10,... | collective-permute-start | bytes 442376 | tf_op jit(solution)/shard_map/ppermute | solution.py:359
  39.8 7.7 %collective-permute-start.21 = (bf16[64,384]{1,0:T(8,128)(2,1)S(1)}, bf16[64,384]{1,0:T(8,128)(2,1)S(1)}, u32[]{:S(2)}, u32[]{:S(2)}) collective-permute-start(bf16[64,384]{1,0:T(8,128)(2,1)S(1)} %get-tuple-element.40), channel_id=1, source_target_pairs={{0,1},{1,0},{2,3},{3,2},{4,5},{5,4},{6,7},{7,6},{8,9},{9,8},{10,11... | collective-permute-start | bytes 147464 | tf_op jit(solution)/shard_map/ppermute | solution.py:359
  41.0 9.9 %collective-permute-start.18 = (bf16[64,640]{1,0:T(8,128)(2,1)S(1)}, bf16[64,640]{1,0:T(8,128)(2,1)S(1)}, u32[]{:S(2)}, u32[]{:S(2)}) collective-permute-start(bf16[64,640]{1,0:T(8,128)(2,1)S(1)} %get-tuple-element.39), channel_id=1, source_target_pairs={{0,1},{1,0},{2,3},{3,2},{4,5},{5,4},{6,7},{7,6},{8,9},{9,8},{10,11... | collective-permute-start | bytes 245768 | tf_op jit(solution)/shard_map/ppermute | solution.py:359
  44.0 7.1 %collective-permute-start.15 = (bf16[64,768]{1,0:T(8,128)(2,1)S(1)}, bf16[64,768]{1,0:T(8,128)(2,1)S(1)}, u32[]{:S(2)}, u32[]{:S(2)}) collective-permute-start(bf16[64,768]{1,0:T(8,128)(2,1)S(1)} %get-tuple-element.37), channel_id=1, source_target_pairs={{0,1},{1,0},{2,3},{3,2},{4,5},{5,4},{6,7},{7,6},{8,9},{9,8},{10,11... | collective-permute-start | bytes 294920 | tf_op jit(solution)/shard_map/ppermute | solution.py:359
  44.3 20.6 %collective-permute-start.11 = (bf16[64,640]{1,0:T(8,128)(2,1)S(1)}, bf16[64,640]{1,0:T(8,128)(2,1)S(1)}, u32[]{:S(2)}, u32[]{:S(2)}) collective-permute-start(bf16[64,640]{1,0:T(8,128)(2,1)S(1)} %add_convert_fusion.6.rest_0_), channel_id=1, source_target_pairs={{0,1},{1,0},{2,3},{3,2},{4,5},{5,4},{6,7},{7,6},{8,9},{9,8},{10,11... | collective-permute-start | bytes 245768 | tf_op jit(solution)/shard_map/ppermute | solution.py:359
  46.7 22.1 %collective-permute-start.14 = (bf16[64,1152]{1,0:T(8,128)(2,1)S(1)}, bf16[64,1152]{1,0:T(8,128)(2,1)S(1)}, u32[]{:S(2)}, u32[]{:S(2)}) collective-permute-start(bf16[64,1152]{1,0:T(8,128)(2,1)S(1)} %add_convert_fusion.rest_2_), channel_id=1, source_target_pairs={{0,1},{1,0},{2,3},{3,2},{4,5},{5,4},{6,7},{7,6},{8,9},{9,8},{10,11... | collective-permute-start | bytes 442376 | tf_op jit(solution)/shard_map/ppermute | solution.py:359
  47.5 15.9 %collective-permute-start.22 = (bf16[64,384]{1,0:T(8,128)(2,1)S(1)}, bf16[64,384]{1,0:T(8,128)(2,1)S(1)}, u32[]{:S(2)}, u32[]{:S(2)}) collective-permute-start(bf16[64,384]{1,0:T(8,128)(2,1)S(1)} %add_convert_fusion.9), channel_id=1, source_target_pairs={{0,2},{1,3},{2,0},{3,1},{4,6},{5,7},{6,4},{7,5},{8,10},{9,11},{10,... | collective-permute-start | bytes 147464 | tf_op jit(solution)/shard_map/ppermute | solution.py:359
  51.0 10.2 %collective-permute-start.19 = (bf16[64,640]{1,0:T(8,128)(2,1)S(1)}, bf16[64,640]{1,0:T(8,128)(2,1)S(1)}, u32[]{:S(2)}, u32[]{:S(2)}) collective-permute-start(bf16[64,640]{1,0:T(8,128)(2,1)S(1)} %add_convert_fusion.5), channel_id=1, source_target_pairs={{0,2},{1,3},{2,0},{3,1},{4,6},{5,7},{6,4},{7,5},{8,10},{9,11},{10,... | collective-permute-start | bytes 245768 | tf_op jit(solution)/shard_map/ppermute | solution.py:359
  51.2 11.5 %collective-permute-start.16 = (bf16[64,768]{1,0:T(8,128)(2,1)S(1)}, bf16[64,768]{1,0:T(8,128)(2,1)S(1)}, u32[]{:S(2)}, u32[]{:S(2)}) collective-permute-start(bf16[64,768]{1,0:T(8,128)(2,1)S(1)} %add_convert_fusion.3), channel_id=1, source_target_pairs={{0,2},{1,3},{2,0},{3,1},{4,6},{5,7},{6,4},{7,5},{8,10},{9,11},{10,... | collective-permute-start | bytes 294920 | tf_op jit(solution)/shard_map/ppermute | solution.py:359
  61.2 7.6 %collective-permute-start.20 = (bf16[64,640]{1,0:T(8,128)(2,1)S(1)}, bf16[64,640]{1,0:T(8,128)(2,1)S(1)}, u32[]{:S(2)}, u32[]{:S(2)}) collective-permute-start(bf16[64,640]{1,0:T(8,128)(2,1)S(1)} %add_convert_fusion.4.rest_6_), channel_id=1, source_target_pairs={{0,1},{1,0},{2,3},{3,2},{4,5},{5,4},{6,7},{7,6},{8,9},{9,8},{10,11... | collective-permute-start | bytes 245768 | tf_op jit(solution)/shard_map/ppermute | solution.py:359
  62.7 6.2 %collective-permute-start.17 = (bf16[64,768]{1,0:T(8,128)(2,1)S(1)}, bf16[64,768]{1,0:T(8,128)(2,1)S(1)}, u32[]{:S(2)}, u32[]{:S(2)}) collective-permute-start(bf16[64,768]{1,0:T(8,128)(2,1)S(1)} %add_convert_fusion.2.rest_4_), channel_id=1, source_target_pairs={{0,1},{1,0},{2,3},{3,2},{4,5},{5,4},{6,7},{7,6},{8,9},{9,8},{10,11... | collective-permute-start | bytes 294920 | tf_op jit(solution)/shard_map/ppermute | solution.py:359
  63.4 5.4 %collective-permute-start.23 = (bf16[64,384]{1,0:T(8,128)(2,1)S(1)}, bf16[64,384]{1,0:T(8,128)(2,1)S(1)}, u32[]{:S(2)}, u32[]{:S(2)}) collective-permute-start(bf16[64,384]{1,0:T(8,128)(2,1)S(1)} %add_convert_fusion.8.rest_8_), channel_id=1, source_target_pairs={{0,1},{1,0},{2,3},{3,2},{4,5},{5,4},{6,7},{7,6},{8,9},{9,8},{10,11... | collective-permute-start | bytes 147464 | tf_op jit(solution)/shard_map/ppermute | solution.py:359

commit v13 on v12

--- a/solution.py
+++ b/solution.py
@@ -229,7 +229,17 @@
         take_scores(odd_scores, 2 * i + 1)
         return carry
 
-    lax.fori_loop(0, (count + 3) // 4, four_pairs, jnp.int32(0))
+    fours = count >> 2
+    lax.fori_loop(0, fours, four_pairs, jnp.int32(0))
+
+    @pl.when(count > 4 * fours)
+    def _():
+        take_scores(even_scores, 2 * fours)
+
+    @pl.when(count > 4 * fours + 2)
+    def _():
+        make_scores(odd_scores, 2 * fours + 1)
+        take_scores(odd_scores, 2 * fours + 1)
 
     for slot in range(slots):
         inverse = 1.0 / run_sum[slot]
@@ -291,7 +301,8 @@
 
 
 def keeps_upper(ids_ref):
-    return (ids_ref[0] // PLACES) % 2 == 1
+    z = ids_ref[0] // PLACES
+    return (z == 1) | (z == 2)
 
 
 def order_kernel(layout, ids_ref, pick_ref, *rest):
@@ -496,17 +507,17 @@
 
     near_made = cut(near, 0, (5, 9))
     pairs = [add(near_made[0][2], near_made[0][3])]
-    relayed = far_across
-    far = [far_rows, flip(far_rows, "seq", 1), far_across, flip(relayed, "seq", 1)]
+    far = [far_rows, flip(far_rows, "seq", 1), far_across, flip(far_across, "seq", 1)]
     far_made = cut(far, half, (6, 5, 3))
     made = near_made + far_made
-    pairs += [add(keep, incoming) for _, _, keep, incoming in made[1:]]
-    crossed = [flip(pair, "head", 2) for pair in pairs]
+    for i, (_, _, keep, incoming) in enumerate(made[1:], 1):
+        pairs.append(add(keep, incoming))
+    crossed = [flip(pair, "head", 3) for pair in pairs]
     last_made = made[-1][2]
     arrays = []
     for i, (pair, cross) in enumerate(zip(pairs, crossed)):
         if i < len(near_made):
-            cross = after(cross, last_made)
+            cross = after(cross, *(pairs[len(near_made)],))
         total = add(pair, cross)
         arrays += [total, flip(total, "head", 1)]
     layout = tuple((row, col) for row, col, _, _ in made)

time: 70.4 us -> 67.4 us (0.957)
  waiting for transfers between devices: 16.8 us -> 11.2 us
  starting transfers between devices: 29.6 us -> 31.8 us
    ppermute x24, waiting for transfers between devices: 16.8 us -> 11.2 us  [flip(): return lax.ppermute(x, axis, [(i, i ^ distance) for i in range(size)])]
    ppermute x24, starting transfers between devices: 29.6 us -> 31.8 us  [flip(): return lax.ppermute(x, axis, [(i, i ^ distance) for i in range(size)])]
  transfers between devices with their start and end apart: 24 -> 24, of which waited for: 7 -> 5; matrix products, arithmetic and copies ran while one was open for 0% -> 0% of each run, Pallas kernels for 27% -> 29%
where the time goes in v13:
time: 67.4 us
  starting transfers between devices  31.8 us (47%)
  Pallas kernels  23 us (34%)
  waiting for transfers between devices  11.2 us (17%)
  local copies, waits for them, and re-layouts  0.82 us (1%)
    ppermute x24, starting transfers between devices, flip(): return lax.ppermute(x, axis, [(i, i ^ distance) for i in range(size)])  31.8 us
    pallas_call x2, Pallas kernels, attend(): pl.pallas_call(functools.partial(attend_kernel, sizes, scale, relative, b...  14.1 us
    ppermute x24, waiting for transfers between devices, flip(): return lax.ppermute(x, axis, [(i, i ^ distance) for i in range(size)])  11.2 us
    pallas_call x5, Pallas kernels, project(): pl.pallas_call(functools.partial(project_kernel, first_col), out_shape=[j...  5.29 us
    pallas_call x1, Pallas kernels, order(): pl.pallas_call(kernel, out_shape=jax.ShapeDtypeStruct((steps, sources * r...  1.42 us
  transfers between devices with their start and end apart: 24, of which 5 were waited for; matrix products, arithmetic and copies ran while one was open for 0% of the time, Pallas kernels for 29%

profile of v13, /device:TPU:0, one launch (start us, length us, event | category | flops | bytes accessed | tf_op | source)
XLA Modules:
  0.0 67.4 jit_solution(3530468688376030304)
XLA Ops:
  0.0 0.7 %copy-done.6 = s32[64]{0:T(128)S(1)} copy-done((s32[64]{0:T(128)S(1)}, s32[64]{0:T(128)}, u32[]{:S(2)}) %copy-start.6) | copy-done | bytes 280
  0.8 1.1 %place_rows.1.after_ref.pick_ref = bf16[4,64,256]{2,1,0:T(8,128)(2,1)S(1)} custom-call(s32[1]{0:T(128)} %bitcast.ids_ref, s32[64]{0:T(128)S(1)} %copy-done.6), custom_call_target="tpu_custom_call" | custom-call | flops 2000000000 | bytes 6000000 | tf_op jit(solution)/shard_map/place_rows/pallas_call | solution.py:394
  1.9 0.0 slice-start.5
  1.9 0.0 copy-start
  1.9 0.0 copy-start.1
  1.9 0.0 copy-start.5
  1.9 0.0 copy-start.7
  1.9 1.1 %pack_queries.1 = (bf16[1,848,128]{2,1,0:T(8,128)(2,1)S(1)}, bf16[1,848,128]{2,1,0:T(8,128)(2,1)S(1)}, bf16[1,848,128]{2,1,0:T(8,128)(2,1)S(1)}, bf16[1,848,128]{2,1,0:T(8,128)(2,1)S(1)}) custom-call(s32[1]{0:T(128)} %bitcast.ids_ref, s32[64]{0:T(128)S(1)} %copy-done.6, bf16[4,16,32,128]{3,2,1,0:T(8,128)(2,1)S(1)} %copy-done.2, ...), custom_call_target="tpu_custom_call" | custom-call | flops 6000000000 | bytes 18000000 | tf_op jit(solution)/shard_map/pack_queries/pallas_call | solution.py:406
  3.1 0.5 collective-permute-start
  3.6 2.6 %collective-permute-start.3 = (bf16[1,848,128]{2,1,0:T(8,128)(2,1)S(1)}, bf16[1,848,128]{2,1,0:T(8,128)(2,1)S(1)}, u32[]{:S(2)}, u32[]{:S(2)}) collective-permute-start(bf16[1,848,128]{2,1,0:T(8,128)(2,1)S(1)} %get-tuple-element.25), channel_id=1, source_target_pairs={{0,8},{4,12},{8,0},{12,4},{1,9},{5,13},{9,1},{13,5},{2,10},{6,14},... | collective-permute-start | bytes 651272 | tf_op jit(solution)/shard_map/ppermute | solution.py:370
  6.2 0.1 collective-permute-start.4
  6.3 0.0 collective-permute-done.rest_1_
  6.3 0.0 slice-start
  6.3 0.0 slice-start.1
  6.4 6.6 %attend.2.rest_0_ = bf16[32,4096]{1,0:T(8,128)(2,1)S(1)} custom-call(s32[1]{0:T(128)} %bitcast.ids_ref, s32[64]{0:T(128)S(1)} %copy-done.7, s32[4,16]{1,0:T(4,128)S(1)} %copy-done.5, bf16[1,848,128]{2,1,0:T(8,128)(2,1)S(1)} %get-tuple-element.23.rest_0_, bf16[1,848,128]{2,1,0:T(8,128)(2,1)S(1)} %collective-permute-done.rest_1_, ...), custom_call_target="tpu_custom_call" | custom-call | flops 8000000000 | bytes 24000000 | tf_op jit(solution)/shard_map/attend/pallas_call | solution.py:424
  13.0 0.0 slice-start.2
  13.0 0.0 slice-start.3
  13.0 2.5 %collective-permute-start.2 = (bf16[32,4096]{1,0:T(8,128)(2,1)S(1)}, bf16[32,4096]{1,0:T(8,128)(2,1)S(1)}, u32[]{:S(2)}, u32[]{:S(2)}) collective-permute-start(bf16[32,4096]{1,0:T(8,128)(2,1)S(1)} %attend.2.rest_0_), channel_id=1, source_target_pairs={{0,8},{4,12},{8,0},{12,4},{1,9},{5,13},{9,1},{13,5},{2,10},{6,14},... | collective-permute-start | bytes 786440 | tf_op jit(solution)/shard_map/ppermute | solution.py:370
  15.5 0.0 collective-permute-start.1
  15.5 1.0 %collective-permute-done.4.rest_1_ = bf16[1,848,128]{2,1,0:T(8,128)(2,1)S(1)} collective-permute-done((bf16[1,848,128]{2,1,0:T(8,128)(2,1)S(1)}, bf16[1,848,128]{2,1,0:T(8,128)(2,1)S(1)}, u32[]{:S(2)}, u32[]{:S(2)}) %collective-permute-start.4) | collective-permute-done | bytes 217120 | tf_op jit(solution)/shard_map/ppermute | solution.py:370
  16.5 7.4 %attend.3.rest_0_ = bf16[32,4096]{1,0:T(8,128)(2,1)S(1)} custom-call(s32[1]{0:T(128)} %bitcast.ids_ref, s32[64]{0:T(128)S(1)} %copy-done.7, s32[4,16]{1,0:T(4,128)S(1)} %copy-done.5, bf16[1,848,128]{2,1,0:T(8,128)(2,1)S(1)} %collective-permute-done.3.rest_0_, bf16[1,848,128]{2,1,0:T(8,128)(2,1)S(1)} %collective-permute-done.4.rest_1_, ...), custom_call_target="tpu_custom_call" | custom-call | flops 8000000000 | bytes 24000000 | tf_op jit(solution)/shard_map/attend/pallas_call | solution.py:424
  24.0 0.1 collective-permute-start.5
  24.0 1.6 %collective-permute-start.9 = (bf16[32,4096]{1,0:T(8,128)(2,1)S(1)}, bf16[32,4096]{1,0:T(8,128)(2,1)S(1)}, u32[]{:S(2)}, u32[]{:S(2)}) collective-permute-start(bf16[32,4096]{1,0:T(8,128)(2,1)S(1)} %attend.3.rest_0_), channel_id=1, source_target_pairs={{0,8},{4,12},{8,0},{12,4},{1,9},{5,13},{9,1},{13,5},{2,10},{6,14},... | collective-permute-start | bytes 786440 | tf_op jit(solution)/shard_map/ppermute | solution.py:370
  25.7 1.0 %project_out.5 = (bf16[64,640]{1,0:T(8,128)(2,1)S(1)}, bf16[64,640]{1,0:T(8,128)(2,1)S(1)}) custom-call(s32[1]{0:T(128)} %bitcast.ids_ref, bf16[32,4096]{1,0:T(8,128)(2,1)S(1)} %attend.2.rest_0_, bf16[32,4096]{1,0:T(8,128)(2,1)S(1)} %collective-permute-done.1.rest_1_, bf16[32,4096]{1,0:T(8,128)(2,1)S(1)} %collective-permute-done.2.rest_2_, ...), custom_call_target="tpu_custom_call" | custom-call | flops 2000000000 | bytes 6000000 | tf_op jit(solution)/shard_map/project_out/pallas_call | solution.py:473
  26.7 1.6 %collective-permute-start.6 = (bf16[64,640]{1,0:T(8,128)(2,1)S(1)}, bf16[64,640]{1,0:T(8,128)(2,1)S(1)}, u32[]{:S(2)}, u32[]{:S(2)}) collective-permute-start(bf16[64,640]{1,0:T(8,128)(2,1)S(1)} %get-tuple-element.29), channel_id=1, source_target_pairs={{0,1},{1,0},{2,3},{3,2},{4,5},{5,4},{6,7},{7,6},{8,9},{9,8},{10,11... | collective-permute-start | bytes 245768 | tf_op jit(solution)/shard_map/ppermute | solution.py:370
  28.4 1.5 %project_out.7 = (bf16[64,1152]{1,0:T(8,128)(2,1)S(1)}, bf16[64,1152]{1,0:T(8,128)(2,1)S(1)}) custom-call(s32[1]{0:T(128)} %bitcast.ids_ref, bf16[32,4096]{1,0:T(8,128)(2,1)S(1)} %attend.2.rest_0_, bf16[32,4096]{1,0:T(8,128)(2,1)S(1)} %collective-permute-done.1.rest_1_, bf16[32,4096]{1,0:T(8,128)(2,1)S(1)} %collective-permute-done.2.rest_2_, ...), custom_call_target="tpu_custom_call" | custom-call | flops 2000000000 | bytes 6000000 | tf_op jit(solution)/shard_map/project_out/pallas_call | solution.py:473
  29.9 0.5 collective-permute-start.13
  30.5 2.3 %collective-permute-done.9.rest_2_ = bf16[32,4096]{1,0:T(8,128)(2,1)S(1)} collective-permute-done((bf16[32,4096]{1,0:T(8,128)(2,1)S(1)}, bf16[32,4096]{1,0:T(8,128)(2,1)S(1)}, u32[]{:S(2)}, u32[]{:S(2)}) %collective-permute-start.9) | collective-permute-done | bytes 262176 | tf_op jit(solution)/shard_map/ppermute | solution.py:370
  32.8 3.7 %collective-permute-start.7 = (bf16[64,640]{1,0:T(8,128)(2,1)S(1)}, bf16[64,640]{1,0:T(8,128)(2,1)S(1)}, u32[]{:S(2)}, u32[]{:S(2)}) collective-permute-start(bf16[64,640]{1,0:T(8,128)(2,1)S(1)} %add_convert_fusion.7), channel_id=1, source_target_pairs={{0,3},{1,2},{2,1},{3,0},{4,7},{5,6},{6,5},{7,4},{8,11},{9,10},{10,... | collective-permute-start | bytes 245768 | tf_op jit(solution)/shard_map/ppermute | solution.py:370
  36.6 2.0 %collective-permute-start.14 = (bf16[64,1152]{1,0:T(8,128)(2,1)S(1)}, bf16[64,1152]{1,0:T(8,128)(2,1)S(1)}, u32[]{:S(2)}, u32[]{:S(2)}) collective-permute-start(bf16[64,1152]{1,0:T(8,128)(2,1)S(1)} %add_convert_fusion.1), channel_id=1, source_target_pairs={{0,3},{1,2},{2,1},{3,0},{4,7},{5,6},{6,5},{7,4},{8,11},{9,10},{10,... | collective-permute-start | bytes 442376 | tf_op jit(solution)/shard_map/ppermute | solution.py:370
  38.6 0.7 %project_out.9 = (bf16[64,384]{1,0:T(8,128)(2,1)S(1)}, bf16[64,384]{1,0:T(8,128)(2,1)S(1)}) custom-call(s32[1]{0:T(128)} %bitcast.ids_ref, bf16[32,4096]{1,0:T(8,128)(2,1)S(1)} %attend.3.rest_0_, bf16[32,4096]{1,0:T(8,128)(2,1)S(1)} %collective-permute-done.8.rest_1_, bf16[32,4096]{1,0:T(8,128)(2,1)S(1)} %collective-permute-done.9.rest_2_, ...), custom_call_target="tpu_custom_call" | custom-call | flops 2000000000 | bytes 6000000 | tf_op jit(solution)/shard_map/project_out/pallas_call | solution.py:473
  39.3 0.8 %collective-permute-start.21 = (bf16[64,384]{1,0:T(8,128)(2,1)S(1)}, bf16[64,384]{1,0:T(8,128)(2,1)S(1)}, u32[]{:S(2)}, u32[]{:S(2)}) collective-permute-start(bf16[64,384]{1,0:T(8,128)(2,1)S(1)} %get-tuple-element.40), channel_id=1, source_target_pairs={{0,1},{1,0},{2,3},{3,2},{4,5},{5,4},{6,7},{7,6},{8,9},{9,8},{10,11... | collective-permute-start | bytes 147464 | tf_op jit(solution)/shard_map/ppermute | solution.py:370
  40.1 1.0 %project_out.8 = (bf16[64,640]{1,0:T(8,128)(2,1)S(1)}, bf16[64,640]{1,0:T(8,128)(2,1)S(1)}) custom-call(s32[1]{0:T(128)} %bitcast.ids_ref, bf16[32,4096]{1,0:T(8,128)(2,1)S(1)} %attend.3.rest_0_, bf16[32,4096]{1,0:T(8,128)(2,1)S(1)} %collective-permute-done.8.rest_1_, bf16[32,4096]{1,0:T(8,128)(2,1)S(1)} %collective-permute-done.9.rest_2_, ...), custom_call_target="tpu_custom_call" | custom-call | flops 2000000000 | bytes 6000000 | tf_op jit(solution)/shard_map/project_out/pallas_call | solution.py:473
  41.1 1.3 %collective-permute-start.18 = (bf16[64,640]{1,0:T(8,128)(2,1)S(1)}, bf16[64,640]{1,0:T(8,128)(2,1)S(1)}, u32[]{:S(2)}, u32[]{:S(2)}) collective-permute-start(bf16[64,640]{1,0:T(8,128)(2,1)S(1)} %get-tuple-element.38), channel_id=1, source_target_pairs={{0,1},{1,0},{2,3},{3,2},{4,5},{5,4},{6,7},{7,6},{8,9},{9,8},{10,11... | collective-permute-start | bytes 245768 | tf_op jit(solution)/shard_map/ppermute | solution.py:370
  42.4 1.0 %project_out.6 = (bf16[64,768]{1,0:T(8,128)(2,1)S(1)}, bf16[64,768]{1,0:T(8,128)(2,1)S(1)}) custom-call(s32[1]{0:T(128)} %bitcast.ids_ref, bf16[32,4096]{1,0:T(8,128)(2,1)S(1)} %attend.3.rest_0_, bf16[32,4096]{1,0:T(8,128)(2,1)S(1)} %collective-permute-done.8.rest_1_, bf16[32,4096]{1,0:T(8,128)(2,1)S(1)} %collective-permute-done.9.rest_2_, ...), custom_call_target="tpu_custom_call" | custom-call | flops 2000000000 | bytes 6000000 | tf_op jit(solution)/shard_map/project_out/pallas_call | solution.py:473
  43.5 0.8 %collective-permute-start.11 = (bf16[64,768]{1,0:T(8,128)(2,1)S(1)}, bf16[64,768]{1,0:T(8,128)(2,1)S(1)}, u32[]{:S(2)}, u32[]{:S(2)}) collective-permute-start(bf16[64,768]{1,0:T(8,128)(2,1)S(1)} %get-tuple-element.32), channel_id=1, source_target_pairs={{0,1},{1,0},{2,3},{3,2},{4,5},{5,4},{6,7},{7,6},{8,9},{9,8},{10,11... | collective-permute-start | bytes 294920 | tf_op jit(solution)/shard_map/ppermute | solution.py:370
  44.3 1.3 %collective-permute-done.21 = bf16[64,384]{1,0:T(8,128)(2,1)S(1)} collective-permute-done((bf16[64,384]{1,0:T(8,128)(2,1)S(1)}, bf16[64,384]{1,0:T(8,128)(2,1)S(1)}, u32[]{:S(2)}, u32[]{:S(2)}) %collective-permute-start.21) | collective-permute-done | bytes 49184 | tf_op jit(solution)/shard_map/ppermute | solution.py:370
  45.6 2.0 %collective-permute-start.22 = (bf16[64,384]{1,0:T(8,128)(2,1)S(1)}, bf16[64,384]{1,0:T(8,128)(2,1)S(1)}, u32[]{:S(2)}, u32[]{:S(2)}) collective-permute-start(bf16[64,384]{1,0:T(8,128)(2,1)S(1)} %add_convert_fusion.9), channel_id=1, source_target_pairs={{0,3},{1,2},{2,1},{3,0},{4,7},{5,6},{6,5},{7,4},{8,11},{9,10},{10,... | collective-permute-start | bytes 147464 | tf_op jit(solution)/shard_map/ppermute | solution.py:370
  47.7 1.9 %collective-permute-start.19 = (bf16[64,640]{1,0:T(8,128)(2,1)S(1)}, bf16[64,640]{1,0:T(8,128)(2,1)S(1)}, u32[]{:S(2)}, u32[]{:S(2)}) collective-permute-start(bf16[64,640]{1,0:T(8,128)(2,1)S(1)} %add_convert_fusion.5), channel_id=1, source_target_pairs={{0,3},{1,2},{2,1},{3,0},{4,7},{5,6},{6,5},{7,4},{8,11},{9,10},{10,... | collective-permute-start | bytes 245768 | tf_op jit(solution)/shard_map/ppermute | solution.py:370
  49.6 2.0 %collective-permute-start.16 = (bf16[64,768]{1,0:T(8,128)(2,1)S(1)}, bf16[64,768]{1,0:T(8,128)(2,1)S(1)}, u32[]{:S(2)}, u32[]{:S(2)}) collective-permute-start(bf16[64,768]{1,0:T(8,128)(2,1)S(1)} %add_convert_fusion.3), channel_id=1, source_target_pairs={{0,3},{1,2},{2,1},{3,0},{4,7},{5,6},{6,5},{7,4},{8,11},{9,10},{10,... | collective-permute-start | bytes 294920 | tf_op jit(solution)/shard_map/ppermute | solution.py:370
  51.7 0.1 collective-permute-start.15
  51.8 2.1 %collective-permute-start.12 = (bf16[64,640]{1,0:T(8,128)(2,1)S(1)}, bf16[64,640]{1,0:T(8,128)(2,1)S(1)}, u32[]{:S(2)}, u32[]{:S(2)}) collective-permute-start(bf16[64,640]{1,0:T(8,128)(2,1)S(1)} %add_convert_fusion.6.rest_0_), channel_id=1, source_target_pairs={{0,1},{1,0},{2,3},{3,2},{4,5},{5,4},{6,7},{7,6},{8,9},{9,8},{10,11... | collective-permute-start | bytes 245768 | tf_op jit(solution)/shard_map/ppermute | solution.py:370
  53.9 0.7 %collective-permute-done.19 = bf16[64,640]{1,0:T(8,128)(2,1)S(1)} collective-permute-done((bf16[64,640]{1,0:T(8,128)(2,1)S(1)}, bf16[64,640]{1,0:T(8,128)(2,1)S(1)}, u32[]{:S(2)}, u32[]{:S(2)}) %collective-permute-start.19) | collective-permute-done | bytes 81952 | tf_op jit(solution)/shard_map/ppermute | solution.py:370
  54.7 3.3 %collective-permute-start.20 = (bf16[64,640]{1,0:T(8,128)(2,1)S(1)}, bf16[64,640]{1,0:T(8,128)(2,1)S(1)}, u32[]{:S(2)}, u32[]{:S(2)}) collective-permute-start(bf16[64,640]{1,0:T(8,128)(2,1)S(1)} %add_convert_fusion.4.rest_6_), channel_id=1, source_target_pairs={{0,1},{1,0},{2,3},{3,2},{4,5},{5,4},{6,7},{7,6},{8,9},{9,8},{10,11... | collective-permute-start | bytes 245768 | tf_op jit(solution)/shard_map/ppermute | solution.py:370
  58.0 1.0 %collective-permute-start.17 = (bf16[64,768]{1,0:T(8,128)(2,1)S(1)}, bf16[64,768]{1,0:T(8,128)(2,1)S(1)}, u32[]{:S(2)}, u32[]{:S(2)}) collective-permute-start(bf16[64,768]{1,0:T(8,128)(2,1)S(1)} %add_convert_fusion.2.rest_4_), channel_id=1, source_target_pairs={{0,1},{1,0},{2,3},{3,2},{4,5},{5,4},{6,7},{7,6},{8,9},{9,8},{10,11... | collective-permute-start | bytes 294920 | tf_op jit(solution)/shard_map/ppermute | solution.py:370
  59.0 1.1 %collective-permute-start.23 = (bf16[64,384]{1,0:T(8,128)(2,1)S(1)}, bf16[64,384]{1,0:T(8,128)(2,1)S(1)}, u32[]{:S(2)}, u32[]{:S(2)}) collective-permute-start(bf16[64,384]{1,0:T(8,128)(2,1)S(1)} %add_convert_fusion.8.rest_8_), channel_id=1, source_target_pairs={{0,1},{1,0},{2,3},{3,2},{4,5},{5,4},{6,7},{7,6},{8,9},{9,8},{10,11... | collective-permute-start | bytes 147464 | tf_op jit(solution)/shard_map/ppermute | solution.py:370
  60.1 5.8 %collective-permute-done.23.rest_9_ = bf16[64,384]{1,0:T(8,128)(2,1)S(1)} collective-permute-done((bf16[64,384]{1,0:T(8,128)(2,1)S(1)}, bf16[64,384]{1,0:T(8,128)(2,1)S(1)}, u32[]{:S(2)}, u32[]{:S(2)}) %collective-permute-start.23) | collective-permute-done | bytes 49184 | tf_op jit(solution)/shard_map/ppermute | solution.py:370
  66.0 1.4 %order_rows.1 = bf16[4,64,1792]{2,1,0:T(8,128)(2,1)} custom-call(s32[1]{0:T(128)} %bitcast.ids_ref, bf16[4,64,256]{2,1,0:T(8,128)(2,1)S(1)} %place_rows.1.after_ref.pick_ref, bf16[64,640]{1,0:T(8,128)(2,1)S(1)} %add_convert_fusion.6.rest_0_, bf16[64,640]{1,0:T(8,128)(2,1)S(1)} %collective-permute-done.12.rest_1_, ...), custom_call_target="tpu_custom_call" | custom-call | flops 2000000000 | bytes 6000000 | tf_op jit(solution)/shard_map/order_rows/pallas_call | solution.py:450
  (50 shorter events, 0.3 us)
Async XLA Ops:
  0.0 1.8 %copy-start.2 = (bf16[4,16,32,128]{3,2,1,0:T(8,128)(2,1)S(1)}, bf16[4,16,32,128]{3,2,1,0:T(8,128)(2,1)}, u32[]{:S(2)}) copy-start(bf16[4,16,32,128]{3,2,1,0:T(8,128)(2,1)} %nope_ref.1) | copy-start | bytes 1572868
  0.0 1.9 %copy-start.3 = (bf16[4,16,32,64]{3,2,1,0:T(8,128)(2,1)S(1)}, bf16[4,16,32,64]{3,2,1,0:T(8,128)(2,1)}, u32[]{:S(2)}) copy-start(bf16[4,16,32,64]{3,2,1,0:T(8,128)(2,1)} %rope_ref.1) | copy-start | bytes 786436
  0.0 1.9 %copy-start.4 = (bf16[4,16,576]{2,1,0:T(8,128)(2,1)S(1)}, bf16[4,16,576]{2,1,0:T(8,128)(2,1)}, u32[]{:S(2)}) copy-start(bf16[4,16,576]{2,1,0:T(8,128)(2,1)} %fresh_ref.1) | copy-start | bytes 221188
  0.0 0.7 %copy-start.6 = (s32[64]{0:T(128)S(1)}, s32[64]{0:T(128)}, u32[]{:S(2)}) copy-start(s32[64]{0:T(128)} %decode_ref.7) | copy-start | bytes 772
  0.8 5.5 %slice-start.4 = ((s8[4718592]{0:T(1024)(128)(4,1)}), s8[4194304]{0:T(1024)(128)(4,1)S(1)}, s32[]{:S(2)}) async-start(s8[4718592]{0:T(1024)(128)(4,1)} %bitcast.4), calls=%async_computation.4 | async-start | bytes 8388608
  1.9 4.4 %slice-start.5 = ((s8[4718592]{0:T(1024)(128)(4,1)}), s8[524288]{0:T(1024)(128)(4,1)S(1)}, s32[]{:S(2)}) async-start(s8[4718592]{0:T(1024)(128)(4,1)} %bitcast.4), calls=%async_computation.5 | async-start | bytes 1048576
  1.9 4.4 %copy-start = (bf16[32,128,512]{2,1,0:T(8,128)(2,1)S(1)}, bf16[32,128,512]{2,1,0:T(8,128)(2,1)}, u32[]{:S(2)}) copy-start(bf16[32,128,512]{2,1,0:T(8,128)(2,1)} %rest_3_.3) | copy-start | bytes 12582916
  1.9 4.4 %copy-start.1 = (bf16[32,512,128]{2,1,0:T(8,128)(2,1)S(1)}, bf16[32,512,128]{2,1,0:T(8,128)(2,1)}, u32[]{:S(2)}) copy-start(bf16[32,512,128]{2,1,0:T(8,128)(2,1)} %rest_4_.8) | copy-start | bytes 12582916
  1.9 4.4 %copy-start.5 = (s32[4,16]{1,0:T(4,128)S(1)}, s32[4,16]{1,0:T(4,128)}, u32[]{:S(2)}) copy-start(s32[4,16]{1,0:T(4,128)} %length_ref.3) | copy-start | bytes 772
  1.9 4.4 %copy-start.7 = (s32[64]{0:T(128)S(1)}, s32[64]{0:T(128)}, u32[]{:S(2)}) copy-start(s32[64]{0:T(128)} %decode_ref.7) | copy-start | bytes 772
  3.1 3.2 %collective-permute-start = (bf16[1,848,128]{2,1,0:T(8,128)(2,1)S(1)}, bf16[1,848,128]{2,1,0:T(8,128)(2,1)S(1)}, u32[]{:S(2)}, u32[]{:S(2)}) collective-permute-start(bf16[1,848,128]{2,1,0:T(8,128)(2,1)S(1)} %get-tuple-element.24), channel_id=1, source_target_pairs={{0,4},{4,0},{8,12},{12,8},{1,5},{5,1},{9,13},{13,9},{2,6},{6,2},{1... | collective-permute-start | bytes 651272 | tf_op jit(solution)/shard_map/ppermute | solution.py:370
  3.6 11.9 %collective-permute-start.3 = (bf16[1,848,128]{2,1,0:T(8,128)(2,1)S(1)}, bf16[1,848,128]{2,1,0:T(8,128)(2,1)S(1)}, u32[]{:S(2)}, u32[]{:S(2)}) collective-permute-start(bf16[1,848,128]{2,1,0:T(8,128)(2,1)S(1)} %get-tuple-element.25), channel_id=1, source_target_pairs={{0,8},{4,12},{8,0},{12,4},{1,9},{5,13},{9,1},{13,5},{2,10},{6,14},... | collective-permute-start | bytes 651272 | tf_op jit(solution)/shard_map/ppermute | solution.py:370
  6.2 10.3 %collective-permute-start.4 = (bf16[1,848,128]{2,1,0:T(8,128)(2,1)S(1)}, bf16[1,848,128]{2,1,0:T(8,128)(2,1)S(1)}, u32[]{:S(2)}, u32[]{:S(2)}) collective-permute-start(bf16[1,848,128]{2,1,0:T(8,128)(2,1)S(1)} %get-tuple-element.26), channel_id=1, source_target_pairs={{0,12},{4,8},{8,4},{12,0},{1,13},{5,9},{9,5},{13,1},{2,14},{6,10},... | collective-permute-start | bytes 651272 | tf_op jit(solution)/shard_map/ppermute | solution.py:370
  6.3 19.4 %slice-start = ((s8[14680064]{0:T(1024)(128)(4,1)}), s8[4194304]{0:T(1024)(128)(4,1)S(1)}, s32[]{:S(2)}) async-start(s8[14680064]{0:T(1024)(128)(4,1)} %bitcast.2), calls=%async_computation | async-start | bytes 8388608
  6.3 19.4 %slice-start.1 = ((s8[14680064]{0:T(1024)(128)(4,1)}), s8[4194304]{0:T(1024)(128)(4,1)S(1)}, s32[]{:S(2)}) async-start(s8[14680064]{0:T(1024)(128)(4,1)} %bitcast.2), calls=%async_computation.1 | async-start | bytes 8388608
  13.0 12.7 %slice-start.2 = ((s8[14680064]{0:T(1024)(128)(4,1)}), s8[4194304]{0:T(1024)(128)(4,1)S(1)}, s32[]{:S(2)}) async-start(s8[14680064]{0:T(1024)(128)(4,1)} %bitcast.2), calls=%async_computation.2 | async-start | bytes 8388608
  13.0 12.7 %slice-start.3 = ((s8[14680064]{0:T(1024)(128)(4,1)}), s8[2097152]{0:T(1024)(128)(4,1)S(1)}, s32[]{:S(2)}) async-start(s8[14680064]{0:T(1024)(128)(4,1)} %bitcast.2), calls=%async_computation.3 | async-start | bytes 4194304
  13.0 10.9 %collective-permute-start.2 = (bf16[32,4096]{1,0:T(8,128)(2,1)S(1)}, bf16[32,4096]{1,0:T(8,128)(2,1)S(1)}, u32[]{:S(2)}, u32[]{:S(2)}) collective-permute-start(bf16[32,4096]{1,0:T(8,128)(2,1)S(1)} %attend.2.rest_0_), channel_id=1, source_target_pairs={{0,8},{4,12},{8,0},{12,4},{1,9},{5,13},{9,1},{13,5},{2,10},{6,14},... | collective-permute-start | bytes 786440 | tf_op jit(solution)/shard_map/ppermute | solution.py:370
  15.5 10.1 %collective-permute-start.1 = (bf16[32,4096]{1,0:T(8,128)(2,1)S(1)}, bf16[32,4096]{1,0:T(8,128)(2,1)S(1)}, u32[]{:S(2)}, u32[]{:S(2)}) collective-permute-start(bf16[32,4096]{1,0:T(8,128)(2,1)S(1)} %attend.2.rest_0_), channel_id=1, source_target_pairs={{0,4},{4,0},{8,12},{12,8},{1,5},{5,1},{9,13},{13,9},{2,6},{6,2},{1... | collective-permute-start | bytes 786440 | tf_op jit(solution)/shard_map/ppermute | solution.py:370
  24.0 1.7 %collective-permute-start.5 = (bf16[32,4096]{1,0:T(8,128)(2,1)S(1)}, bf16[32,4096]{1,0:T(8,128)(2,1)S(1)}, u32[]{:S(2)}, u32[]{:S(2)}) collective-permute-start(bf16[32,4096]{1,0:T(8,128)(2,1)S(1)} %collective-permute-done.2.rest_2_), channel_id=1, source_target_pairs={{0,4},{4,0},{8,12},{12,8},{1,5},{5,1},{9,13},{13,9},{2,6},{6,2},{1... | collective-permute-start | bytes 786440 | tf_op jit(solution)/shard_map/ppermute | solution.py:370
  24.0 8.7 %collective-permute-start.9 = (bf16[32,4096]{1,0:T(8,128)(2,1)S(1)}, bf16[32,4096]{1,0:T(8,128)(2,1)S(1)}, u32[]{:S(2)}, u32[]{:S(2)}) collective-permute-start(bf16[32,4096]{1,0:T(8,128)(2,1)S(1)} %attend.3.rest_0_), channel_id=1, source_target_pairs={{0,8},{4,12},{8,0},{12,4},{1,9},{5,13},{9,1},{13,5},{2,10},{6,14},... | collective-permute-start | bytes 786440 | tf_op jit(solution)/shard_map/ppermute | solution.py:370
  25.7 12.9 %collective-permute-start.8 = (bf16[32,4096]{1,0:T(8,128)(2,1)S(1)}, bf16[32,4096]{1,0:T(8,128)(2,1)S(1)}, u32[]{:S(2)}, u32[]{:S(2)}) collective-permute-start(bf16[32,4096]{1,0:T(8,128)(2,1)S(1)} %attend.3.rest_0_), channel_id=1, source_target_pairs={{0,4},{4,0},{8,12},{12,8},{1,5},{5,1},{9,13},{13,9},{2,6},{6,2},{1... | collective-permute-start | bytes 786440 | tf_op jit(solution)/shard_map/ppermute | solution.py:370
  26.7 6.0 %collective-permute-start.6 = (bf16[64,640]{1,0:T(8,128)(2,1)S(1)}, bf16[64,640]{1,0:T(8,128)(2,1)S(1)}, u32[]{:S(2)}, u32[]{:S(2)}) collective-permute-start(bf16[64,640]{1,0:T(8,128)(2,1)S(1)} %get-tuple-element.29), channel_id=1, source_target_pairs={{0,1},{1,0},{2,3},{3,2},{4,5},{5,4},{6,7},{7,6},{8,9},{9,8},{10,11... | collective-permute-start | bytes 245768 | tf_op jit(solution)/shard_map/ppermute | solution.py:370
  29.9 6.6 %collective-permute-start.13 = (bf16[64,1152]{1,0:T(8,128)(2,1)S(1)}, bf16[64,1152]{1,0:T(8,128)(2,1)S(1)}, u32[]{:S(2)}, u32[]{:S(2)}) collective-permute-start(bf16[64,1152]{1,0:T(8,128)(2,1)S(1)} %get-tuple-element.35), channel_id=1, source_target_pairs={{0,1},{1,0},{2,3},{3,2},{4,5},{5,4},{6,7},{7,6},{8,9},{9,8},{10,11... | collective-permute-start | bytes 442376 | tf_op jit(solution)/shard_map/ppermute | solution.py:370
  32.8 5.8 %collective-permute-start.10 = (bf16[32,4096]{1,0:T(8,128)(2,1)S(1)}, bf16[32,4096]{1,0:T(8,128)(2,1)S(1)}, u32[]{:S(2)}, u32[]{:S(2)}) collective-permute-start(bf16[32,4096]{1,0:T(8,128)(2,1)S(1)} %collective-permute-done.9.rest_2_), channel_id=1, source_target_pairs={{0,4},{4,0},{8,12},{12,8},{1,5},{5,1},{9,13},{13,9},{2,6},{6,2},{1... | collective-permute-start | bytes 786440 | tf_op jit(solution)/shard_map/ppermute | solution.py:370
  32.8 19.0 %collective-permute-start.7 = (bf16[64,640]{1,0:T(8,128)(2,1)S(1)}, bf16[64,640]{1,0:T(8,128)(2,1)S(1)}, u32[]{:S(2)}, u32[]{:S(2)}) collective-permute-start(bf16[64,640]{1,0:T(8,128)(2,1)S(1)} %add_convert_fusion.7), channel_id=1, source_target_pairs={{0,3},{1,2},{2,1},{3,0},{4,7},{5,6},{6,5},{7,4},{8,11},{9,10},{10,... | collective-permute-start | bytes 245768 | tf_op jit(solution)/shard_map/ppermute | solution.py:370
  36.6 15.1 %collective-permute-start.14 = (bf16[64,1152]{1,0:T(8,128)(2,1)S(1)}, bf16[64,1152]{1,0:T(8,128)(2,1)S(1)}, u32[]{:S(2)}, u32[]{:S(2)}) collective-permute-start(bf16[64,1152]{1,0:T(8,128)(2,1)S(1)} %add_convert_fusion.1), channel_id=1, source_target_pairs={{0,3},{1,2},{2,1},{3,0},{4,7},{5,6},{6,5},{7,4},{8,11},{9,10},{10,... | collective-permute-start | bytes 442376 | tf_op jit(solution)/shard_map/ppermute | solution.py:370
  39.3 6.3 %collective-permute-start.21 = (bf16[64,384]{1,0:T(8,128)(2,1)S(1)}, bf16[64,384]{1,0:T(8,128)(2,1)S(1)}, u32[]{:S(2)}, u32[]{:S(2)}) collective-permute-start(bf16[64,384]{1,0:T(8,128)(2,1)S(1)} %get-tuple-element.40), channel_id=1, source_target_pairs={{0,1},{1,0},{2,3},{3,2},{4,5},{5,4},{6,7},{7,6},{8,9},{9,8},{10,11... | collective-permute-start | bytes 147464 | tf_op jit(solution)/shard_map/ppermute | solution.py:370
  41.1 6.6 %collective-permute-start.18 = (bf16[64,640]{1,0:T(8,128)(2,1)S(1)}, bf16[64,640]{1,0:T(8,128)(2,1)S(1)}, u32[]{:S(2)}, u32[]{:S(2)}) collective-permute-start(bf16[64,640]{1,0:T(8,128)(2,1)S(1)} %get-tuple-element.38), channel_id=1, source_target_pairs={{0,1},{1,0},{2,3},{3,2},{4,5},{5,4},{6,7},{7,6},{8,9},{9,8},{10,11... | collective-permute-start | bytes 245768 | tf_op jit(solution)/shard_map/ppermute | solution.py:370
  43.5 6.1 %collective-permute-start.11 = (bf16[64,768]{1,0:T(8,128)(2,1)S(1)}, bf16[64,768]{1,0:T(8,128)(2,1)S(1)}, u32[]{:S(2)}, u32[]{:S(2)}) collective-permute-start(bf16[64,768]{1,0:T(8,128)(2,1)S(1)} %get-tuple-element.32), channel_id=1, source_target_pairs={{0,1},{1,0},{2,3},{3,2},{4,5},{5,4},{6,7},{7,6},{8,9},{9,8},{10,11... | collective-permute-start | bytes 294920 | tf_op jit(solution)/shard_map/ppermute | solution.py:370
  45.6 13.4 %collective-permute-start.22 = (bf16[64,384]{1,0:T(8,128)(2,1)S(1)}, bf16[64,384]{1,0:T(8,128)(2,1)S(1)}, u32[]{:S(2)}, u32[]{:S(2)}) collective-permute-start(bf16[64,384]{1,0:T(8,128)(2,1)S(1)} %add_convert_fusion.9), channel_id=1, source_target_pairs={{0,3},{1,2},{2,1},{3,0},{4,7},{5,6},{6,5},{7,4},{8,11},{9,10},{10,... | collective-permute-start | bytes 147464 | tf_op jit(solution)/shard_map/ppermute | solution.py:370
  47.7 6.9 %collective-permute-start.19 = (bf16[64,640]{1,0:T(8,128)(2,1)S(1)}, bf16[64,640]{1,0:T(8,128)(2,1)S(1)}, u32[]{:S(2)}, u32[]{:S(2)}) collective-permute-start(bf16[64,640]{1,0:T(8,128)(2,1)S(1)} %add_convert_fusion.5), channel_id=1, source_target_pairs={{0,3},{1,2},{2,1},{3,0},{4,7},{5,6},{6,5},{7,4},{8,11},{9,10},{10,... | collective-permute-start | bytes 245768 | tf_op jit(solution)/shard_map/ppermute | solution.py:370
  49.6 8.3 %collective-permute-start.16 = (bf16[64,768]{1,0:T(8,128)(2,1)S(1)}, bf16[64,768]{1,0:T(8,128)(2,1)S(1)}, u32[]{:S(2)}, u32[]{:S(2)}) collective-permute-start(bf16[64,768]{1,0:T(8,128)(2,1)S(1)} %add_convert_fusion.3), channel_id=1, source_target_pairs={{0,3},{1,2},{2,1},{3,0},{4,7},{5,6},{6,5},{7,4},{8,11},{9,10},{10,... | collective-permute-start | bytes 294920 | tf_op jit(solution)/shard_map/ppermute | solution.py:370
  51.7 14.3 %collective-permute-start.15 = (bf16[64,1152]{1,0:T(8,128)(2,1)S(1)}, bf16[64,1152]{1,0:T(8,128)(2,1)S(1)}, u32[]{:S(2)}, u32[]{:S(2)}) collective-permute-start(bf16[64,1152]{1,0:T(8,128)(2,1)S(1)} %add_convert_fusion.rest_2_), channel_id=1, source_target_pairs={{0,1},{1,0},{2,3},{3,2},{4,5},{5,4},{6,7},{7,6},{8,9},{9,8},{10,11... | collective-permute-start | bytes 442376 | tf_op jit(solution)/shard_map/ppermute | solution.py:370
  51.8 14.1 %collective-permute-start.12 = (bf16[64,640]{1,0:T(8,128)(2,1)S(1)}, bf16[64,640]{1,0:T(8,128)(2,1)S(1)}, u32[]{:S(2)}, u32[]{:S(2)}) collective-permute-start(bf16[64,640]{1,0:T(8,128)(2,1)S(1)} %add_convert_fusion.6.rest_0_), channel_id=1, source_target_pairs={{0,1},{1,0},{2,3},{3,2},{4,5},{5,4},{6,7},{7,6},{8,9},{9,8},{10,11... | collective-permute-start | bytes 245768 | tf_op jit(solution)/shard_map/ppermute | solution.py:370
  54.7 11.3 %collective-permute-start.20 = (bf16[64,640]{1,0:T(8,128)(2,1)S(1)}, bf16[64,640]{1,0:T(8,128)(2,1)S(1)}, u32[]{:S(2)}, u32[]{:S(2)}) collective-permute-start(bf16[64,640]{1,0:T(8,128)(2,1)S(1)} %add_convert_fusion.4.rest_6_), channel_id=1, source_target_pairs={{0,1},{1,0},{2,3},{3,2},{4,5},{5,4},{6,7},{7,6},{8,9},{9,8},{10,11... | collective-permute-start | bytes 245768 | tf_op jit(solution)/shard_map/ppermute | solution.py:370
  58.0 8.0 %collective-permute-start.17 = (bf16[64,768]{1,0:T(8,128)(2,1)S(1)}, bf16[64,768]{1,0:T(8,128)(2,1)S(1)}, u32[]{:S(2)}, u32[]{:S(2)}) collective-permute-start(bf16[64,768]{1,0:T(8,128)(2,1)S(1)} %add_convert_fusion.2.rest_4_), channel_id=1, source_target_pairs={{0,1},{1,0},{2,3},{3,2},{4,5},{5,4},{6,7},{7,6},{8,9},{9,8},{10,11... | collective-permute-start | bytes 294920 | tf_op jit(solution)/shard_map/ppermute | solution.py:370
  59.0 7.0 %collective-permute-start.23 = (bf16[64,384]{1,0:T(8,128)(2,1)S(1)}, bf16[64,384]{1,0:T(8,128)(2,1)S(1)}, u32[]{:S(2)}, u32[]{:S(2)}) collective-permute-start(bf16[64,384]{1,0:T(8,128)(2,1)S(1)} %add_convert_fusion.8.rest_8_), channel_id=1, source_target_pairs={{0,1},{1,0},{2,3},{3,2},{4,5},{5,4},{6,7},{7,6},{8,9},{9,8},{10,11... | collective-permute-start | bytes 147464 | tf_op jit(solution)/shard_map/ppermute | solution.py:370

commit v14 on v13

--- a/solution.py
+++ b/solution.py
@@ -90,14 +90,22 @@
                 out_refs[0][k, first : first + fresh_rows, :] = piece
 
 
-def attend_kernel(sizes, scale, relative, base, recv_count, ids_ref, decode_ref, length_ref, *rest):
+def attend_kernel(sizes, scale, relative, base, recv_count, ids_any, decode_any, length_any, *rest):
     sources, per_pair, steps, heads, requests, fresh_rows = sizes
     recv_refs = rest[:recv_count]
     (
         cache, key_up, value_up, out_ref,
         slot_offset, slot_length, owner_count, pair_slot, pair_start,
         queries, fresh, acc, run_max, run_sum, latent, even_scores, odd_scores,
+        ids_ref, decode_ref, length_ref, sems,
     ) = rest[recv_count:]
+    tables = [
+        pltpu.make_async_copy(ids_any, ids_ref, sems.at[0]),
+        pltpu.make_async_copy(decode_any, decode_ref, sems.at[1]),
+        pltpu.make_async_copy(length_any, length_ref, sems.at[2]),
+    ]
+    for table in tables:
+        table.start()
     owners = [(ref, e) for ref in recv_refs for e in range(ref.shape[0])]
     here = len(owners)
     slots = here * per_pair
@@ -127,7 +135,8 @@
 
     inner_head = lax.broadcasted_iota(jnp.int32, (slots * 16, LANES), 0) // steps % group
     own_head = [jnp.where(inner_head == u, 1.0, 0.0).astype(jnp.bfloat16) for u in range(group)]
-    for i in range(heads // group):
+
+    def absorb(i):
         tall = jnp.concatenate(
             [ref[at, j * rows + i * 16 : j * rows + (i + 1) * 16, :] for ref, at in owners for j in range(per_pair)],
             axis=0,
@@ -137,6 +146,12 @@
         res = jnp.dot(left, right, preferred_element_type=jnp.float32).astype(jnp.bfloat16)
         for slot in range(slots):
             queries[slot * rows + i * 16 : slot * rows + (i + 1) * 16, 0:LATENT] = res[slot * 16 : (slot + 1) * 16]
+
+    groups = heads // group
+    for i in range(groups // 4):
+        absorb(i)
+    for table in tables:
+        table.wait()
 
     me = ids_ref[0] & (PLACES - 1)
     for o in range(sources):
@@ -160,6 +175,9 @@
             pair_slot[count] = jnp.int32(slot)
             pair_start[count] = start + k * BLOCK
             count = count + jnp.where(start + k * BLOCK < end, 1, 0).astype(jnp.int32)
+
+    for i in range(groups // 4, groups):
+        absorb(i)
 
     fresh_scores = (
         lax.dot_general(queries[...], fresh[...], (((1,), (1,)), ((), ())), preferred_element_type=jnp.float32) * factor
@@ -413,7 +431,7 @@
             pltpu.VMEM((2 * per_pair, rows, LANES), jnp.float32),
         ],
         compiler_params=limit(8),
-        cost_estimate=cost(6),
+        cost_estimate=cost(2),
         name="pack_queries",
     )(ids, decode_rows, q_nope, q_rope, new_latent, pick)
 
@@ -424,7 +442,7 @@
         return pl.pallas_call(
             functools.partial(attend_kernel, sizes, scale, relative, base, len(received)),
             out_shape=jax.ShapeDtypeStruct((slots * steps, heads * value_up.shape[2]), jnp.bfloat16),
-            in_specs=[smem(), smem(), smem()] + [vmem()] * (len(received) + 3),
+            in_specs=[anywhere()] * 3 + [vmem()] * (len(received) + 3),
             out_specs=vmem(),
             scratch_shapes=[
                 pltpu.SMEM((slots + 1,), jnp.int32),
@@ -440,6 +458,10 @@
                 pltpu.VMEM((slots * rows, LATENT), jnp.bfloat16),
                 pltpu.VMEM((2, rows, BLOCK), jnp.float32),
                 pltpu.VMEM((2, rows, BLOCK), jnp.float32),
+                pltpu.SMEM(ids.shape, jnp.int32),
+                pltpu.SMEM(decode_rows.shape, jnp.int32),
+                pltpu.SMEM(lengths.shape, jnp.int32),
+                pltpu.SemaphoreType.DMA((3,)),
             ],
             compiler_params=limit(14),
             cost_estimate=cost(8),

time: 67.4 us -> 67.8 us (level)
  starting transfers between devices: 31.8 us -> 30.8 us
  waiting for transfers between devices: 11.2 us -> 12.2 us
    ppermute x24, starting transfers between devices: 31.8 us -> 30.8 us  [flip(): return lax.ppermute(x, axis, [(i, i ^ distance) for i in range(size)])]
    ppermute x24, waiting for transfers between devices: 11.2 us -> 12.2 us  [flip(): return lax.ppermute(x, axis, [(i, i ^ distance) for i in range(size)])]
  transfers between devices with their start and end apart: 24 -> 24, of which waited for: 5 -> 7; matrix products, arithmetic and copies ran while one was open for 0% -> 0% of each run, Pallas kernels for 29% -> 29%
where the time goes in v14:
time: 67.8 us; the launch traced here: 67.5 us
  starting transfers between devices  30.8 us (45%)
  Pallas kernels  23.2 us (34%)
  waiting for transfers between devices  12.2 us (18%)
  local copies, waits for them, and re-layouts  0.81 us (1%)
    ppermute x24, starting transfers between devices, flip(): return lax.ppermute(x, axis, [(i, i ^ distance) for i in range(size)])  30.8 us
    pallas_call x2, Pallas kernels, attend(): pl.pallas_call(functools.partial(attend_kernel, sizes, scale, relative, b...  14.2 us
    ppermute x24, waiting for transfers between devices, flip(): return lax.ppermute(x, axis, [(i, i ^ distance) for i in range(size)])  12.2 us
    pallas_call x5, Pallas kernels, project(): pl.pallas_call(functools.partial(project_kernel, first_col), out_shape=[j...  5.29 us
    pallas_call x1, Pallas kernels, order(): pl.pallas_call(kernel, out_shape=jax.ShapeDtypeStruct((steps, sources * r...  1.42 us
  transfers between devices with their start and end apart: 24, of which 7 were waited for; matrix products, arithmetic and copies ran while one was open for 0% of the time, Pallas kernels for 29%

profile of v14, /device:TPU:0, one launch (start us, length us, event | category | flops | bytes accessed | tf_op | source)
XLA Modules:
  0.0 67.5 jit_solution(16426568121197729003)
XLA Ops:
  0.0 0.7 %copy-done.7 = s32[64]{0:T(128)S(1)} copy-done((s32[64]{0:T(128)S(1)}, s32[64]{0:T(128)}, u32[]{:S(2)}) %copy-start.7) | copy-done | bytes 280
  0.8 1.1 %place_rows.1.after_ref.pick_ref = bf16[4,64,256]{2,1,0:T(8,128)(2,1)S(1)} custom-call(s32[1]{0:T(128)} %bitcast.ids_ref.ids_any, s32[64]{0:T(128)S(1)} %copy-done.7), custom_call_target="tpu_custom_call" | custom-call | flops 2000000000 | bytes 6000000 | tf_op jit(solution)/shard_map/place_rows/pallas_call | solution.py:412
  1.9 0.0 copy-start
  1.9 0.0 copy-start.6
  1.9 0.0 copy-start.8
  1.9 1.1 %pack_queries.1 = (bf16[1,848,128]{2,1,0:T(8,128)(2,1)S(1)}, bf16[1,848,128]{2,1,0:T(8,128)(2,1)S(1)}, bf16[1,848,128]{2,1,0:T(8,128)(2,1)S(1)}, bf16[1,848,128]{2,1,0:T(8,128)(2,1)S(1)}) custom-call(s32[1]{0:T(128)} %bitcast.ids_ref.ids_any, s32[64]{0:T(128)S(1)} %copy-done.7, bf16[4,16,32,128]{3,2,1,0:T(8,128)(2,1)S(1)} %copy-done.3, ...), custom_call_target="tpu_custom_call" | custom-call | flops 2000000000 | bytes 6000000 | tf_op jit(solution)/shard_map/pack_queries/pallas_call | solution.py:424
  3.1 0.5 collective-permute-start
  3.6 2.6 %collective-permute-start.3 = (bf16[1,848,128]{2,1,0:T(8,128)(2,1)S(1)}, bf16[1,848,128]{2,1,0:T(8,128)(2,1)S(1)}, u32[]{:S(2)}, u32[]{:S(2)}) collective-permute-start(bf16[1,848,128]{2,1,0:T(8,128)(2,1)S(1)} %get-tuple-element.25), channel_id=1, source_target_pairs={{0,8},{4,12},{8,0},{12,4},{1,9},{5,13},{9,1},{13,5},{2,10},{6,14},... | collective-permute-start | bytes 651272 | tf_op jit(solution)/shard_map/ppermute | solution.py:388
  6.2 0.1 collective-permute-start.4
  6.2 0.0 collective-permute-done.rest_1_
  6.3 0.0 slice-start
  6.3 0.0 slice-start.1
  6.3 6.7 %attend.2.rest_0_ = bf16[32,4096]{1,0:T(8,128)(2,1)S(1)} custom-call(s32[1]{0:T(128)} %bitcast.ids_ref.ids_any, s32[64]{0:T(128)S(1)} %copy-done.8, s32[4,16]{1,0:T(4,128)S(1)} %copy-done.6, bf16[1,848,128]{2,1,0:T(8,128)(2,1)S(1)} %get-tuple-element.23.rest_0_, bf16[1,848,128]{2,1,0:T(8,128)(2,1)S(1)} %collective-permute-done.rest_1_, ...), custom_call_target="tpu_custom_call" | custom-call | flops 8000000000 | bytes 24000000 | tf_op jit(solution)/shard_map/attend/pallas_call | solution.py:442
  13.0 0.0 slice-start.2
  13.1 0.0 slice-start.3
  13.1 3.1 %collective-permute-start.2 = (bf16[32,4096]{1,0:T(8,128)(2,1)S(1)}, bf16[32,4096]{1,0:T(8,128)(2,1)S(1)}, u32[]{:S(2)}, u32[]{:S(2)}) collective-permute-start(bf16[32,4096]{1,0:T(8,128)(2,1)S(1)} %attend.2.rest_0_), channel_id=1, source_target_pairs={{0,8},{4,12},{8,0},{12,4},{1,9},{5,13},{9,1},{13,5},{2,10},{6,14},... | collective-permute-start | bytes 786440 | tf_op jit(solution)/shard_map/ppermute | solution.py:388
  16.2 0.3 collective-permute-done.4.rest_1_
  16.5 7.5 %attend.3.rest_0_ = bf16[32,4096]{1,0:T(8,128)(2,1)S(1)} custom-call(s32[1]{0:T(128)} %bitcast.ids_ref.ids_any, s32[64]{0:T(128)S(1)} %copy-done.8, s32[4,16]{1,0:T(4,128)S(1)} %copy-done.6, bf16[1,848,128]{2,1,0:T(8,128)(2,1)S(1)} %collective-permute-done.3.rest_0_, bf16[1,848,128]{2,1,0:T(8,128)(2,1)S(1)} %collective-permute-done.4.rest_1_, ...), custom_call_target="tpu_custom_call" | custom-call | flops 8000000000 | bytes 24000000 | tf_op jit(solution)/shard_map/attend/pallas_call | solution.py:442
  24.1 0.3 collective-permute-start.5
  24.3 0.8 %collective-permute-start.9 = (bf16[32,4096]{1,0:T(8,128)(2,1)S(1)}, bf16[32,4096]{1,0:T(8,128)(2,1)S(1)}, u32[]{:S(2)}, u32[]{:S(2)}) collective-permute-start(bf16[32,4096]{1,0:T(8,128)(2,1)S(1)} %attend.3.rest_0_), channel_id=1, source_target_pairs={{0,8},{4,12},{8,0},{12,4},{1,9},{5,13},{9,1},{13,5},{2,10},{6,14},... | collective-permute-start | bytes 786440 | tf_op jit(solution)/shard_map/ppermute | solution.py:388
  25.1 0.2 collective-permute-start.8
  25.3 0.3 collective-permute-done.5.rest_3_
  25.7 1.0 %project_out.5 = (bf16[64,640]{1,0:T(8,128)(2,1)S(1)}, bf16[64,640]{1,0:T(8,128)(2,1)S(1)}) custom-call(s32[1]{0:T(128)} %bitcast.ids_ref.ids_any, bf16[32,4096]{1,0:T(8,128)(2,1)S(1)} %attend.2.rest_0_, bf16[32,4096]{1,0:T(8,128)(2,1)S(1)} %collective-permute-done.1.rest_1_, bf16[32,4096]{1,0:T(8,128)(2,1)S(1)} %collective-permute-done.2.rest_2_, ...), custom_call_target="tpu_custom_call" | custom-call | flops 2000000000 | bytes 6000000 | tf_op jit(solution)/shard_map/project_out/pallas_call | solution.py:495
  26.7 1.7 %collective-permute-start.6 = (bf16[64,640]{1,0:T(8,128)(2,1)S(1)}, bf16[64,640]{1,0:T(8,128)(2,1)S(1)}, u32[]{:S(2)}, u32[]{:S(2)}) collective-permute-start(bf16[64,640]{1,0:T(8,128)(2,1)S(1)} %get-tuple-element.29), channel_id=1, source_target_pairs={{0,1},{1,0},{2,3},{3,2},{4,5},{5,4},{6,7},{7,6},{8,9},{9,8},{10,11... | collective-permute-start | bytes 245768 | tf_op jit(solution)/shard_map/ppermute | solution.py:388
  28.4 1.5 %project_out.7 = (bf16[64,1152]{1,0:T(8,128)(2,1)S(1)}, bf16[64,1152]{1,0:T(8,128)(2,1)S(1)}) custom-call(s32[1]{0:T(128)} %bitcast.ids_ref.ids_any, bf16[32,4096]{1,0:T(8,128)(2,1)S(1)} %attend.2.rest_0_, bf16[32,4096]{1,0:T(8,128)(2,1)S(1)} %collective-permute-done.1.rest_1_, bf16[32,4096]{1,0:T(8,128)(2,1)S(1)} %collective-permute-done.2.rest_2_, ...), custom_call_target="tpu_custom_call" | custom-call | flops 2000000000 | bytes 6000000 | tf_op jit(solution)/shard_map/project_out/pallas_call | solution.py:495
  29.9 0.5 collective-permute-start.13
  30.4 2.4 %collective-permute-done.9.rest_2_ = bf16[32,4096]{1,0:T(8,128)(2,1)S(1)} collective-permute-done((bf16[32,4096]{1,0:T(8,128)(2,1)S(1)}, bf16[32,4096]{1,0:T(8,128)(2,1)S(1)}, u32[]{:S(2)}, u32[]{:S(2)}) %collective-permute-start.9) | collective-permute-done | bytes 262176 | tf_op jit(solution)/shard_map/ppermute | solution.py:388
  32.9 3.7 %collective-permute-start.7 = (bf16[64,640]{1,0:T(8,128)(2,1)S(1)}, bf16[64,640]{1,0:T(8,128)(2,1)S(1)}, u32[]{:S(2)}, u32[]{:S(2)}) collective-permute-start(bf16[64,640]{1,0:T(8,128)(2,1)S(1)} %add_convert_fusion.7), channel_id=1, source_target_pairs={{0,3},{1,2},{2,1},{3,0},{4,7},{5,6},{6,5},{7,4},{8,11},{9,10},{10,... | collective-permute-start | bytes 245768 | tf_op jit(solution)/shard_map/ppermute | solution.py:388
  36.6 1.7 %collective-permute-start.14 = (bf16[64,1152]{1,0:T(8,128)(2,1)S(1)}, bf16[64,1152]{1,0:T(8,128)(2,1)S(1)}, u32[]{:S(2)}, u32[]{:S(2)}) collective-permute-start(bf16[64,1152]{1,0:T(8,128)(2,1)S(1)} %add_convert_fusion.1), channel_id=1, source_target_pairs={{0,3},{1,2},{2,1},{3,0},{4,7},{5,6},{6,5},{7,4},{8,11},{9,10},{10,... | collective-permute-start | bytes 442376 | tf_op jit(solution)/shard_map/ppermute | solution.py:388
  38.3 0.7 %project_out.9 = (bf16[64,384]{1,0:T(8,128)(2,1)S(1)}, bf16[64,384]{1,0:T(8,128)(2,1)S(1)}) custom-call(s32[1]{0:T(128)} %bitcast.ids_ref.ids_any, bf16[32,4096]{1,0:T(8,128)(2,1)S(1)} %attend.3.rest_0_, bf16[32,4096]{1,0:T(8,128)(2,1)S(1)} %collective-permute-done.8.rest_1_, bf16[32,4096]{1,0:T(8,128)(2,1)S(1)} %collective-permute-done.9.rest_2_, ...), custom_call_target="tpu_custom_call" | custom-call | flops 2000000000 | bytes 6000000 | tf_op jit(solution)/shard_map/project_out/pallas_call | solution.py:495
  39.0 0.7 %collective-permute-start.21 = (bf16[64,384]{1,0:T(8,128)(2,1)S(1)}, bf16[64,384]{1,0:T(8,128)(2,1)S(1)}, u32[]{:S(2)}, u32[]{:S(2)}) collective-permute-start(bf16[64,384]{1,0:T(8,128)(2,1)S(1)} %get-tuple-element.40), channel_id=1, source_target_pairs={{0,1},{1,0},{2,3},{3,2},{4,5},{5,4},{6,7},{7,6},{8,9},{9,8},{10,11... | collective-permute-start | bytes 147464 | tf_op jit(solution)/shard_map/ppermute | solution.py:388
  39.8 1.0 %project_out.8 = (bf16[64,640]{1,0:T(8,128)(2,1)S(1)}, bf16[64,640]{1,0:T(8,128)(2,1)S(1)}) custom-call(s32[1]{0:T(128)} %bitcast.ids_ref.ids_any, bf16[32,4096]{1,0:T(8,128)(2,1)S(1)} %attend.3.rest_0_, bf16[32,4096]{1,0:T(8,128)(2,1)S(1)} %collective-permute-done.8.rest_1_, bf16[32,4096]{1,0:T(8,128)(2,1)S(1)} %collective-permute-done.9.rest_2_, ...), custom_call_target="tpu_custom_call" | custom-call | flops 2000000000 | bytes 6000000 | tf_op jit(solution)/shard_map/project_out/pallas_call | solution.py:495
  40.8 1.4 %collective-permute-start.18 = (bf16[64,640]{1,0:T(8,128)(2,1)S(1)}, bf16[64,640]{1,0:T(8,128)(2,1)S(1)}, u32[]{:S(2)}, u32[]{:S(2)}) collective-permute-start(bf16[64,640]{1,0:T(8,128)(2,1)S(1)} %get-tuple-element.38), channel_id=1, source_target_pairs={{0,1},{1,0},{2,3},{3,2},{4,5},{5,4},{6,7},{7,6},{8,9},{9,8},{10,11... | collective-permute-start | bytes 245768 | tf_op jit(solution)/shard_map/ppermute | solution.py:388
  42.2 1.0 %project_out.6 = (bf16[64,768]{1,0:T(8,128)(2,1)S(1)}, bf16[64,768]{1,0:T(8,128)(2,1)S(1)}) custom-call(s32[1]{0:T(128)} %bitcast.ids_ref.ids_any, bf16[32,4096]{1,0:T(8,128)(2,1)S(1)} %attend.3.rest_0_, bf16[32,4096]{1,0:T(8,128)(2,1)S(1)} %collective-permute-done.8.rest_1_, bf16[32,4096]{1,0:T(8,128)(2,1)S(1)} %collective-permute-done.9.rest_2_, ...), custom_call_target="tpu_custom_call" | custom-call | flops 2000000000 | bytes 6000000 | tf_op jit(solution)/shard_map/project_out/pallas_call | solution.py:495
  43.2 0.7 %collective-permute-start.11 = (bf16[64,768]{1,0:T(8,128)(2,1)S(1)}, bf16[64,768]{1,0:T(8,128)(2,1)S(1)}, u32[]{:S(2)}, u32[]{:S(2)}) collective-permute-start(bf16[64,768]{1,0:T(8,128)(2,1)S(1)} %get-tuple-element.32), channel_id=1, source_target_pairs={{0,1},{1,0},{2,3},{3,2},{4,5},{5,4},{6,7},{7,6},{8,9},{9,8},{10,11... | collective-permute-start | bytes 294920 | tf_op jit(solution)/shard_map/ppermute | solution.py:388
  44.0 1.7 %collective-permute-done.21 = bf16[64,384]{1,0:T(8,128)(2,1)S(1)} collective-permute-done((bf16[64,384]{1,0:T(8,128)(2,1)S(1)}, bf16[64,384]{1,0:T(8,128)(2,1)S(1)}, u32[]{:S(2)}, u32[]{:S(2)}) %collective-permute-start.21) | collective-permute-done | bytes 49184 | tf_op jit(solution)/shard_map/ppermute | solution.py:388
  45.7 2.0 %collective-permute-start.22 = (bf16[64,384]{1,0:T(8,128)(2,1)S(1)}, bf16[64,384]{1,0:T(8,128)(2,1)S(1)}, u32[]{:S(2)}, u32[]{:S(2)}) collective-permute-start(bf16[64,384]{1,0:T(8,128)(2,1)S(1)} %add_convert_fusion.9), channel_id=1, source_target_pairs={{0,3},{1,2},{2,1},{3,0},{4,7},{5,6},{6,5},{7,4},{8,11},{9,10},{10,... | collective-permute-start | bytes 147464 | tf_op jit(solution)/shard_map/ppermute | solution.py:388
  47.8 1.9 %collective-permute-start.19 = (bf16[64,640]{1,0:T(8,128)(2,1)S(1)}, bf16[64,640]{1,0:T(8,128)(2,1)S(1)}, u32[]{:S(2)}, u32[]{:S(2)}) collective-permute-start(bf16[64,640]{1,0:T(8,128)(2,1)S(1)} %add_convert_fusion.5), channel_id=1, source_target_pairs={{0,3},{1,2},{2,1},{3,0},{4,7},{5,6},{6,5},{7,4},{8,11},{9,10},{10,... | collective-permute-start | bytes 245768 | tf_op jit(solution)/shard_map/ppermute | solution.py:388
  49.7 2.0 %collective-permute-start.16 = (bf16[64,768]{1,0:T(8,128)(2,1)S(1)}, bf16[64,768]{1,0:T(8,128)(2,1)S(1)}, u32[]{:S(2)}, u32[]{:S(2)}) collective-permute-start(bf16[64,768]{1,0:T(8,128)(2,1)S(1)} %add_convert_fusion.3), channel_id=1, source_target_pairs={{0,3},{1,2},{2,1},{3,0},{4,7},{5,6},{6,5},{7,4},{8,11},{9,10},{10,... | collective-permute-start | bytes 294920 | tf_op jit(solution)/shard_map/ppermute | solution.py:388
  51.8 0.1 collective-permute-start.15
  51.9 2.1 %collective-permute-start.12 = (bf16[64,640]{1,0:T(8,128)(2,1)S(1)}, bf16[64,640]{1,0:T(8,128)(2,1)S(1)}, u32[]{:S(2)}, u32[]{:S(2)}) collective-permute-start(bf16[64,640]{1,0:T(8,128)(2,1)S(1)} %add_convert_fusion.6.rest_0_), channel_id=1, source_target_pairs={{0,1},{1,0},{2,3},{3,2},{4,5},{5,4},{6,7},{7,6},{8,9},{9,8},{10,11... | collective-permute-start | bytes 245768 | tf_op jit(solution)/shard_map/ppermute | solution.py:388
  54.0 0.7 %collective-permute-done.19 = bf16[64,640]{1,0:T(8,128)(2,1)S(1)} collective-permute-done((bf16[64,640]{1,0:T(8,128)(2,1)S(1)}, bf16[64,640]{1,0:T(8,128)(2,1)S(1)}, u32[]{:S(2)}, u32[]{:S(2)}) %collective-permute-start.19) | collective-permute-done | bytes 81952 | tf_op jit(solution)/shard_map/ppermute | solution.py:388
  54.7 2.5 %collective-permute-start.20 = (bf16[64,640]{1,0:T(8,128)(2,1)S(1)}, bf16[64,640]{1,0:T(8,128)(2,1)S(1)}, u32[]{:S(2)}, u32[]{:S(2)}) collective-permute-start(bf16[64,640]{1,0:T(8,128)(2,1)S(1)} %add_convert_fusion.4.rest_6_), channel_id=1, source_target_pairs={{0,1},{1,0},{2,3},{3,2},{4,5},{5,4},{6,7},{7,6},{8,9},{9,8},{10,11... | collective-permute-start | bytes 245768 | tf_op jit(solution)/shard_map/ppermute | solution.py:388
  57.2 0.1 collective-permute-done.16
  57.3 1.7 %collective-permute-start.17 = (bf16[64,768]{1,0:T(8,128)(2,1)S(1)}, bf16[64,768]{1,0:T(8,128)(2,1)S(1)}, u32[]{:S(2)}, u32[]{:S(2)}) collective-permute-start(bf16[64,768]{1,0:T(8,128)(2,1)S(1)} %add_convert_fusion.2.rest_4_), channel_id=1, source_target_pairs={{0,1},{1,0},{2,3},{3,2},{4,5},{5,4},{6,7},{7,6},{8,9},{9,8},{10,11... | collective-permute-start | bytes 294920 | tf_op jit(solution)/shard_map/ppermute | solution.py:388
  59.1 0.5 collective-permute-start.23
  59.5 6.5 %collective-permute-done.23.rest_9_ = bf16[64,384]{1,0:T(8,128)(2,1)S(1)} collective-permute-done((bf16[64,384]{1,0:T(8,128)(2,1)S(1)}, bf16[64,384]{1,0:T(8,128)(2,1)S(1)}, u32[]{:S(2)}, u32[]{:S(2)}) %collective-permute-start.23) | collective-permute-done | bytes 49184 | tf_op jit(solution)/shard_map/ppermute | solution.py:388
  66.1 1.4 %order_rows.1 = bf16[4,64,1792]{2,1,0:T(8,128)(2,1)} custom-call(s32[1]{0:T(128)} %bitcast.ids_ref.ids_any, bf16[4,64,256]{2,1,0:T(8,128)(2,1)S(1)} %place_rows.1.after_ref.pick_ref, bf16[64,640]{1,0:T(8,128)(2,1)S(1)} %add_convert_fusion.6.rest_0_, bf16[64,640]{1,0:T(8,128)(2,1)S(1)} %collective-permute-done.12.rest_1_, ...), custom_call_target="tpu_custom_call" | custom-call | flops 2000000000 | bytes 6000000 | tf_op jit(solution)/shard_map/order_rows/pallas_call | solution.py:472
  (47 shorter events, 0.3 us)
Async XLA Ops:
  0.0 1.9 %copy-start.3 = (bf16[4,16,32,128]{3,2,1,0:T(8,128)(2,1)S(1)}, bf16[4,16,32,128]{3,2,1,0:T(8,128)(2,1)}, u32[]{:S(2)}) copy-start(bf16[4,16,32,128]{3,2,1,0:T(8,128)(2,1)} %nope_ref.1) | copy-start | bytes 1572868
  0.0 1.9 %copy-start.4 = (bf16[4,16,32,64]{3,2,1,0:T(8,128)(2,1)S(1)}, bf16[4,16,32,64]{3,2,1,0:T(8,128)(2,1)}, u32[]{:S(2)}) copy-start(bf16[4,16,32,64]{3,2,1,0:T(8,128)(2,1)} %rope_ref.1) | copy-start | bytes 786436
  0.0 1.9 %copy-start.5 = (bf16[4,16,576]{2,1,0:T(8,128)(2,1)S(1)}, bf16[4,16,576]{2,1,0:T(8,128)(2,1)}, u32[]{:S(2)}) copy-start(bf16[4,16,576]{2,1,0:T(8,128)(2,1)} %fresh_ref.1) | copy-start | bytes 221188
  0.0 0.7 %copy-start.7 = (s32[64]{0:T(128)S(1)}, s32[64]{0:T(128)}, u32[]{:S(2)}) copy-start(s32[64]{0:T(128)} %decode_any.3) | copy-start | bytes 772
  0.8 5.5 %copy-start.1 = (bf16[32,128,512]{2,1,0:T(8,128)(2,1)S(1)}, bf16[32,128,512]{2,1,0:T(8,128)(2,1)}, u32[]{:S(2)}) copy-start(bf16[32,128,512]{2,1,0:T(8,128)(2,1)} %rest_3_.3) | copy-start | bytes 12582916
  0.8 5.5 %copy-start.2 = (bf16[32,512,128]{2,1,0:T(8,128)(2,1)S(1)}, bf16[32,512,128]{2,1,0:T(8,128)(2,1)}, u32[]{:S(2)}) copy-start(bf16[32,512,128]{2,1,0:T(8,128)(2,1)} %rest_4_.8) | copy-start | bytes 12582916
  1.9 4.4 %copy-start = (bf16[4096,576]{0,1:T(8,128)(2,1)S(1)}, bf16[4096,576]{0,1:T(8,128)(2,1)}, u32[]{:S(2)}) copy-start(bf16[4096,576]{0,1:T(8,128)(2,1)} %param.9) | copy-start | bytes 14155780
  1.9 4.4 %copy-start.6 = (s32[4,16]{1,0:T(4,128)S(1)}, s32[4,16]{1,0:T(4,128)}, u32[]{:S(2)}) copy-start(s32[4,16]{1,0:T(4,128)} %length_any.3) | copy-start | bytes 772
  1.9 4.4 %copy-start.8 = (s32[64]{0:T(128)S(1)}, s32[64]{0:T(128)}, u32[]{:S(2)}) copy-start(s32[64]{0:T(128)} %decode_any.3) | copy-start | bytes 772
  3.1 3.2 %collective-permute-start = (bf16[1,848,128]{2,1,0:T(8,128)(2,1)S(1)}, bf16[1,848,128]{2,1,0:T(8,128)(2,1)S(1)}, u32[]{:S(2)}, u32[]{:S(2)}) collective-permute-start(bf16[1,848,128]{2,1,0:T(8,128)(2,1)S(1)} %get-tuple-element.24), channel_id=1, source_target_pairs={{0,4},{4,0},{8,12},{12,8},{1,5},{5,1},{9,13},{13,9},{2,6},{6,2},{1... | collective-permute-start | bytes 651272 | tf_op jit(solution)/shard_map/ppermute | solution.py:388
  3.6 12.6 %collective-permute-start.3 = (bf16[1,848,128]{2,1,0:T(8,128)(2,1)S(1)}, bf16[1,848,128]{2,1,0:T(8,128)(2,1)S(1)}, u32[]{:S(2)}, u32[]{:S(2)}) collective-permute-start(bf16[1,848,128]{2,1,0:T(8,128)(2,1)S(1)} %get-tuple-element.25), channel_id=1, source_target_pairs={{0,8},{4,12},{8,0},{12,4},{1,9},{5,13},{9,1},{13,5},{2,10},{6,14},... | collective-permute-start | bytes 651272 | tf_op jit(solution)/shard_map/ppermute | solution.py:388
  6.2 10.3 %collective-permute-start.4 = (bf16[1,848,128]{2,1,0:T(8,128)(2,1)S(1)}, bf16[1,848,128]{2,1,0:T(8,128)(2,1)S(1)}, u32[]{:S(2)}, u32[]{:S(2)}) collective-permute-start(bf16[1,848,128]{2,1,0:T(8,128)(2,1)S(1)} %get-tuple-element.26), channel_id=1, source_target_pairs={{0,12},{4,8},{8,4},{12,0},{1,13},{5,9},{9,5},{13,1},{2,14},{6,10},... | collective-permute-start | bytes 651272 | tf_op jit(solution)/shard_map/ppermute | solution.py:388
  6.3 19.4 %slice-start = ((s8[14680064]{0:T(1024)(128)(4,1)}), s8[4194304]{0:T(1024)(128)(4,1)S(1)}, s32[]{:S(2)}) async-start(s8[14680064]{0:T(1024)(128)(4,1)} %bitcast.2), calls=%async_computation | async-start | bytes 8388608
  6.3 19.4 %slice-start.1 = ((s8[14680064]{0:T(1024)(128)(4,1)}), s8[4194304]{0:T(1024)(128)(4,1)S(1)}, s32[]{:S(2)}) async-start(s8[14680064]{0:T(1024)(128)(4,1)} %bitcast.2), calls=%async_computation.1 | async-start | bytes 8388608
  13.0 12.6 %slice-start.2 = ((s8[14680064]{0:T(1024)(128)(4,1)}), s8[4194304]{0:T(1024)(128)(4,1)S(1)}, s32[]{:S(2)}) async-start(s8[14680064]{0:T(1024)(128)(4,1)} %bitcast.2), calls=%async_computation.2 | async-start | bytes 8388608
  13.1 12.6 %slice-start.3 = ((s8[14680064]{0:T(1024)(128)(4,1)}), s8[2097152]{0:T(1024)(128)(4,1)S(1)}, s32[]{:S(2)}) async-start(s8[14680064]{0:T(1024)(128)(4,1)} %bitcast.2), calls=%async_computation.3 | async-start | bytes 4194304
  13.1 11.0 %collective-permute-start.2 = (bf16[32,4096]{1,0:T(8,128)(2,1)S(1)}, bf16[32,4096]{1,0:T(8,128)(2,1)S(1)}, u32[]{:S(2)}, u32[]{:S(2)}) collective-permute-start(bf16[32,4096]{1,0:T(8,128)(2,1)S(1)} %attend.2.rest_0_), channel_id=1, source_target_pairs={{0,8},{4,12},{8,0},{12,4},{1,9},{5,13},{9,1},{13,5},{2,10},{6,14},... | collective-permute-start | bytes 786440 | tf_op jit(solution)/shard_map/ppermute | solution.py:388
  16.2 9.1 %collective-permute-start.1 = (bf16[32,4096]{1,0:T(8,128)(2,1)S(1)}, bf16[32,4096]{1,0:T(8,128)(2,1)S(1)}, u32[]{:S(2)}, u32[]{:S(2)}) collective-permute-start(bf16[32,4096]{1,0:T(8,128)(2,1)S(1)} %attend.2.rest_0_), channel_id=1, source_target_pairs={{0,4},{4,0},{8,12},{12,8},{1,5},{5,1},{9,13},{13,9},{2,6},{6,2},{1... | collective-permute-start | bytes 786440 | tf_op jit(solution)/shard_map/ppermute | solution.py:388
  24.1 1.6 %collective-permute-start.5 = (bf16[32,4096]{1,0:T(8,128)(2,1)S(1)}, bf16[32,4096]{1,0:T(8,128)(2,1)S(1)}, u32[]{:S(2)}, u32[]{:S(2)}) collective-permute-start(bf16[32,4096]{1,0:T(8,128)(2,1)S(1)} %collective-permute-done.2.rest_2_), channel_id=1, source_target_pairs={{0,4},{4,0},{8,12},{12,8},{1,5},{5,1},{9,13},{13,9},{2,6},{6,2},{1... | collective-permute-start | bytes 786440 | tf_op jit(solution)/shard_map/ppermute | solution.py:388
  24.3 8.5 %collective-permute-start.9 = (bf16[32,4096]{1,0:T(8,128)(2,1)S(1)}, bf16[32,4096]{1,0:T(8,128)(2,1)S(1)}, u32[]{:S(2)}, u32[]{:S(2)}) collective-permute-start(bf16[32,4096]{1,0:T(8,128)(2,1)S(1)} %attend.3.rest_0_), channel_id=1, source_target_pairs={{0,8},{4,12},{8,0},{12,4},{1,9},{5,13},{9,1},{13,5},{2,10},{6,14},... | collective-permute-start | bytes 786440 | tf_op jit(solution)/shard_map/ppermute | solution.py:388
  25.1 13.2 %collective-permute-start.8 = (bf16[32,4096]{1,0:T(8,128)(2,1)S(1)}, bf16[32,4096]{1,0:T(8,128)(2,1)S(1)}, u32[]{:S(2)}, u32[]{:S(2)}) collective-permute-start(bf16[32,4096]{1,0:T(8,128)(2,1)S(1)} %attend.3.rest_0_), channel_id=1, source_target_pairs={{0,4},{4,0},{8,12},{12,8},{1,5},{5,1},{9,13},{13,9},{2,6},{6,2},{1... | collective-permute-start | bytes 786440 | tf_op jit(solution)/shard_map/ppermute | solution.py:388
  26.7 6.2 %collective-permute-start.6 = (bf16[64,640]{1,0:T(8,128)(2,1)S(1)}, bf16[64,640]{1,0:T(8,128)(2,1)S(1)}, u32[]{:S(2)}, u32[]{:S(2)}) collective-permute-start(bf16[64,640]{1,0:T(8,128)(2,1)S(1)} %get-tuple-element.29), channel_id=1, source_target_pairs={{0,1},{1,0},{2,3},{3,2},{4,5},{5,4},{6,7},{7,6},{8,9},{9,8},{10,11... | collective-permute-start | bytes 245768 | tf_op jit(solution)/shard_map/ppermute | solution.py:388
  29.9 6.7 %collective-permute-start.13 = (bf16[64,1152]{1,0:T(8,128)(2,1)S(1)}, bf16[64,1152]{1,0:T(8,128)(2,1)S(1)}, u32[]{:S(2)}, u32[]{:S(2)}) collective-permute-start(bf16[64,1152]{1,0:T(8,128)(2,1)S(1)} %get-tuple-element.35), channel_id=1, source_target_pairs={{0,1},{1,0},{2,3},{3,2},{4,5},{5,4},{6,7},{7,6},{8,9},{9,8},{10,11... | collective-permute-start | bytes 442376 | tf_op jit(solution)/shard_map/ppermute | solution.py:388
  32.8 5.5 %collective-permute-start.10 = (bf16[32,4096]{1,0:T(8,128)(2,1)S(1)}, bf16[32,4096]{1,0:T(8,128)(2,1)S(1)}, u32[]{:S(2)}, u32[]{:S(2)}) collective-permute-start(bf16[32,4096]{1,0:T(8,128)(2,1)S(1)} %collective-permute-done.9.rest_2_), channel_id=1, source_target_pairs={{0,4},{4,0},{8,12},{12,8},{1,5},{5,1},{9,13},{13,9},{2,6},{6,2},{1... | collective-permute-start | bytes 786440 | tf_op jit(solution)/shard_map/ppermute | solution.py:388
  32.9 19.0 %collective-permute-start.7 = (bf16[64,640]{1,0:T(8,128)(2,1)S(1)}, bf16[64,640]{1,0:T(8,128)(2,1)S(1)}, u32[]{:S(2)}, u32[]{:S(2)}) collective-permute-start(bf16[64,640]{1,0:T(8,128)(2,1)S(1)} %add_convert_fusion.7), channel_id=1, source_target_pairs={{0,3},{1,2},{2,1},{3,0},{4,7},{5,6},{6,5},{7,4},{8,11},{9,10},{10,... | collective-permute-start | bytes 245768 | tf_op jit(solution)/shard_map/ppermute | solution.py:388
  36.6 15.1 %collective-permute-start.14 = (bf16[64,1152]{1,0:T(8,128)(2,1)S(1)}, bf16[64,1152]{1,0:T(8,128)(2,1)S(1)}, u32[]{:S(2)}, u32[]{:S(2)}) collective-permute-start(bf16[64,1152]{1,0:T(8,128)(2,1)S(1)} %add_convert_fusion.1), channel_id=1, source_target_pairs={{0,3},{1,2},{2,1},{3,0},{4,7},{5,6},{6,5},{7,4},{8,11},{9,10},{10,... | collective-permute-start | bytes 442376 | tf_op jit(solution)/shard_map/ppermute | solution.py:388
  39.0 6.6 %collective-permute-start.21 = (bf16[64,384]{1,0:T(8,128)(2,1)S(1)}, bf16[64,384]{1,0:T(8,128)(2,1)S(1)}, u32[]{:S(2)}, u32[]{:S(2)}) collective-permute-start(bf16[64,384]{1,0:T(8,128)(2,1)S(1)} %get-tuple-element.40), channel_id=1, source_target_pairs={{0,1},{1,0},{2,3},{3,2},{4,5},{5,4},{6,7},{7,6},{8,9},{9,8},{10,11... | collective-permute-start | bytes 147464 | tf_op jit(solution)/shard_map/ppermute | solution.py:388
  40.8 6.9 %collective-permute-start.18 = (bf16[64,640]{1,0:T(8,128)(2,1)S(1)}, bf16[64,640]{1,0:T(8,128)(2,1)S(1)}, u32[]{:S(2)}, u32[]{:S(2)}) collective-permute-start(bf16[64,640]{1,0:T(8,128)(2,1)S(1)} %get-tuple-element.38), channel_id=1, source_target_pairs={{0,1},{1,0},{2,3},{3,2},{4,5},{5,4},{6,7},{7,6},{8,9},{9,8},{10,11... | collective-permute-start | bytes 245768 | tf_op jit(solution)/shard_map/ppermute | solution.py:388
  43.2 6.4 %collective-permute-start.11 = (bf16[64,768]{1,0:T(8,128)(2,1)S(1)}, bf16[64,768]{1,0:T(8,128)(2,1)S(1)}, u32[]{:S(2)}, u32[]{:S(2)}) collective-permute-start(bf16[64,768]{1,0:T(8,128)(2,1)S(1)} %get-tuple-element.32), channel_id=1, source_target_pairs={{0,1},{1,0},{2,3},{3,2},{4,5},{5,4},{6,7},{7,6},{8,9},{9,8},{10,11... | collective-permute-start | bytes 294920 | tf_op jit(solution)/shard_map/ppermute | solution.py:388
  45.7 13.3 %collective-permute-start.22 = (bf16[64,384]{1,0:T(8,128)(2,1)S(1)}, bf16[64,384]{1,0:T(8,128)(2,1)S(1)}, u32[]{:S(2)}, u32[]{:S(2)}) collective-permute-start(bf16[64,384]{1,0:T(8,128)(2,1)S(1)} %add_convert_fusion.9), channel_id=1, source_target_pairs={{0,3},{1,2},{2,1},{3,0},{4,7},{5,6},{6,5},{7,4},{8,11},{9,10},{10,... | collective-permute-start | bytes 147464 | tf_op jit(solution)/shard_map/ppermute | solution.py:388
  47.8 6.9 %collective-permute-start.19 = (bf16[64,640]{1,0:T(8,128)(2,1)S(1)}, bf16[64,640]{1,0:T(8,128)(2,1)S(1)}, u32[]{:S(2)}, u32[]{:S(2)}) collective-permute-start(bf16[64,640]{1,0:T(8,128)(2,1)S(1)} %add_convert_fusion.5), channel_id=1, source_target_pairs={{0,3},{1,2},{2,1},{3,0},{4,7},{5,6},{6,5},{7,4},{8,11},{9,10},{10,... | collective-permute-start | bytes 245768 | tf_op jit(solution)/shard_map/ppermute | solution.py:388
  49.7 7.6 %collective-permute-start.16 = (bf16[64,768]{1,0:T(8,128)(2,1)S(1)}, bf16[64,768]{1,0:T(8,128)(2,1)S(1)}, u32[]{:S(2)}, u32[]{:S(2)}) collective-permute-start(bf16[64,768]{1,0:T(8,128)(2,1)S(1)} %add_convert_fusion.3), channel_id=1, source_target_pairs={{0,3},{1,2},{2,1},{3,0},{4,7},{5,6},{6,5},{7,4},{8,11},{9,10},{10,... | collective-permute-start | bytes 294920 | tf_op jit(solution)/shard_map/ppermute | solution.py:388
  51.8 14.3 %collective-permute-start.15 = (bf16[64,1152]{1,0:T(8,128)(2,1)S(1)}, bf16[64,1152]{1,0:T(8,128)(2,1)S(1)}, u32[]{:S(2)}, u32[]{:S(2)}) collective-permute-start(bf16[64,1152]{1,0:T(8,128)(2,1)S(1)} %add_convert_fusion.rest_2_), channel_id=1, source_target_pairs={{0,1},{1,0},{2,3},{3,2},{4,5},{5,4},{6,7},{7,6},{8,9},{9,8},{10,11... | collective-permute-start | bytes 442376 | tf_op jit(solution)/shard_map/ppermute | solution.py:388
  51.9 14.1 %collective-permute-start.12 = (bf16[64,640]{1,0:T(8,128)(2,1)S(1)}, bf16[64,640]{1,0:T(8,128)(2,1)S(1)}, u32[]{:S(2)}, u32[]{:S(2)}) collective-permute-start(bf16[64,640]{1,0:T(8,128)(2,1)S(1)} %add_convert_fusion.6.rest_0_), channel_id=1, source_target_pairs={{0,1},{1,0},{2,3},{3,2},{4,5},{5,4},{6,7},{7,6},{8,9},{9,8},{10,11... | collective-permute-start | bytes 245768 | tf_op jit(solution)/shard_map/ppermute | solution.py:388
  54.7 11.3 %collective-permute-start.20 = (bf16[64,640]{1,0:T(8,128)(2,1)S(1)}, bf16[64,640]{1,0:T(8,128)(2,1)S(1)}, u32[]{:S(2)}, u32[]{:S(2)}) collective-permute-start(bf16[64,640]{1,0:T(8,128)(2,1)S(1)} %add_convert_fusion.4.rest_6_), channel_id=1, source_target_pairs={{0,1},{1,0},{2,3},{3,2},{4,5},{5,4},{6,7},{7,6},{8,9},{9,8},{10,11... | collective-permute-start | bytes 245768 | tf_op jit(solution)/shard_map/ppermute | solution.py:388
  57.3 8.7 %collective-permute-start.17 = (bf16[64,768]{1,0:T(8,128)(2,1)S(1)}, bf16[64,768]{1,0:T(8,128)(2,1)S(1)}, u32[]{:S(2)}, u32[]{:S(2)}) collective-permute-start(bf16[64,768]{1,0:T(8,128)(2,1)S(1)} %add_convert_fusion.2.rest_4_), channel_id=1, source_target_pairs={{0,1},{1,0},{2,3},{3,2},{4,5},{5,4},{6,7},{7,6},{8,9},{9,8},{10,11... | collective-permute-start | bytes 294920 | tf_op jit(solution)/shard_map/ppermute | solution.py:388
  59.1 7.0 %collective-permute-start.23 = (bf16[64,384]{1,0:T(8,128)(2,1)S(1)}, bf16[64,384]{1,0:T(8,128)(2,1)S(1)}, u32[]{:S(2)}, u32[]{:S(2)}) collective-permute-start(bf16[64,384]{1,0:T(8,128)(2,1)S(1)} %add_convert_fusion.8.rest_8_), channel_id=1, source_target_pairs={{0,1},{1,0},{2,3},{3,2},{4,5},{5,4},{6,7},{7,6},{8,9},{9,8},{10,11... | collective-permute-start | bytes 147464 | tf_op jit(solution)/shard_map/ppermute | solution.py:388

commit v15 on v14

--- a/solution.py
+++ b/solution.py
@@ -527,12 +527,14 @@
             made.append((first_row, at, keep, swap((keep, send))))
         return made
 
-    near_made = cut(near, 0, (5, 9))
+    near_made = cut(near, 0, (1, 1))
     pairs = [add(near_made[0][2], near_made[0][3])]
-    far = [far_rows, flip(far_rows, "seq", 1), far_across, flip(far_across, "seq", 1)]
-    far_made = cut(far, half, (6, 5, 3))
+    relayed = after(far_across, near_made[1][2])
+    far = [far_rows, flip(far_rows, "seq", 1), far_across, flip(relayed, "seq", 1)]
+    far_made = cut(far, half, (1, 1))
     made = near_made + far_made
     for i, (_, _, keep, incoming) in enumerate(made[1:], 1):
+        if i == 1: incoming = after(incoming, made[2][2])
         pairs.append(add(keep, incoming))
     crossed = [flip(pair, "head", 3) for pair in pairs]
     last_made = made[-1][2]

time: 67.8 us -> 68.3 us (level)
  waiting for transfers between devices: 12.2 us -> 15.5 us
  starting transfers between devices: 30.8 us -> 28.2 us
    ppermute x24 -> x21, waiting for transfers between devices: 12.2 us -> 15.5 us  [flip(): return lax.ppermute(x, axis, [(i, i ^ distance) for i in range(size)])]
    ppermute x24 -> x21, starting transfers between devices: 30.8 us -> 28.2 us  [flip(): return lax.ppermute(x, axis, [(i, i ^ distance) for i in range(size)])]
    pallas_call x5 -> x4, Pallas kernels: 5.29 us -> 5.11 us  [project(): pl.pallas_call(functools.partial(project_kernel, first_col), out_shape=[j...]
  transfers between devices with their start and end apart: 24 -> 21, of which waited for: 7 -> 7; matrix products, arithmetic and copies ran while one was open for 0% -> 0% of each run, Pallas kernels for 29% -> 28%
where the time goes in v15:
time: 68.3 us; the launch traced here: 67.7 us
  starting transfers between devices  28.2 us (41%)
  Pallas kernels  22.6 us (33%)
  waiting for transfers between devices  15.5 us (23%)
  local copies, waits for them, and re-layouts  0.81 us (1%)
    ppermute x21, starting transfers between devices, flip(): return lax.ppermute(x, axis, [(i, i ^ distance) for i in range(size)])  28.2 us
    ppermute x21, waiting for transfers between devices, flip(): return lax.ppermute(x, axis, [(i, i ^ distance) for i in range(size)])  15.5 us
    pallas_call x2, Pallas kernels, attend(): pl.pallas_call(functools.partial(attend_kernel, sizes, scale, relative, b...  13.9 us
    pallas_call x4, Pallas kernels, project(): pl.pallas_call(functools.partial(project_kernel, first_col), out_shape=[j...  5.11 us
    pallas_call x1, Pallas kernels, order(): pl.pallas_call(kernel, out_shape=jax.ShapeDtypeStruct((steps, sources * r...  1.41 us
  transfers between devices with their start and end apart: 21, of which 7 were waited for; matrix products, arithmetic and copies ran while one was open for 0% of the time, Pallas kernels for 28%

profile of v15, /device:TPU:0, one launch (start us, length us, event | category | flops | bytes accessed | tf_op | source)
XLA Modules:
  0.0 67.7 jit_solution(17703675261964495499)
XLA Ops:
  0.0 0.7 %copy-done.7 = s32[64]{0:T(128)S(1)} copy-done((s32[64]{0:T(128)S(1)}, s32[64]{0:T(128)}, u32[]{:S(2)}) %copy-start.7) | copy-done | bytes 280
  0.8 1.1 %place_rows.1.after_ref.pick_ref = bf16[4,64,256]{2,1,0:T(8,128)(2,1)S(1)} custom-call(s32[1]{0:T(128)} %bitcast.ids_ref.ids_any, s32[64]{0:T(128)S(1)} %copy-done.7), custom_call_target="tpu_custom_call" | custom-call | flops 2000000000 | bytes 6000000 | tf_op jit(solution)/shard_map/place_rows/pallas_call | solution.py:412
  1.9 0.0 copy-start
  1.9 0.0 copy-start.6
  1.9 0.0 copy-start.8
  1.9 1.1 %pack_queries.1 = (bf16[1,848,128]{2,1,0:T(8,128)(2,1)S(1)}, bf16[1,848,128]{2,1,0:T(8,128)(2,1)S(1)}, bf16[1,848,128]{2,1,0:T(8,128)(2,1)S(1)}, bf16[1,848,128]{2,1,0:T(8,128)(2,1)S(1)}) custom-call(s32[1]{0:T(128)} %bitcast.ids_ref.ids_any, s32[64]{0:T(128)S(1)} %copy-done.7, bf16[4,16,32,128]{3,2,1,0:T(8,128)(2,1)S(1)} %copy-done.3, ...), custom_call_target="tpu_custom_call" | custom-call | flops 2000000000 | bytes 6000000 | tf_op jit(solution)/shard_map/pack_queries/pallas_call | solution.py:424
  3.1 0.5 collective-permute-start
  3.6 2.6 %collective-permute-start.3 = (bf16[1,848,128]{2,1,0:T(8,128)(2,1)S(1)}, bf16[1,848,128]{2,1,0:T(8,128)(2,1)S(1)}, u32[]{:S(2)}, u32[]{:S(2)}) collective-permute-start(bf16[1,848,128]{2,1,0:T(8,128)(2,1)S(1)} %get-tuple-element.25), channel_id=1, source_target_pairs={{0,8},{4,12},{8,0},{12,4},{1,9},{5,13},{9,1},{13,5},{2,10},{6,14},... | collective-permute-start | bytes 651272 | tf_op jit(solution)/shard_map/ppermute | solution.py:388
  6.2 0.1 collective-permute-start.4
  6.3 0.0 slice-start
  6.3 0.0 slice-start.1
  6.3 7.3 %attend.2.rest_0_ = bf16[32,4096]{1,0:T(8,128)(2,1)S(1)} custom-call(s32[1]{0:T(128)} %bitcast.ids_ref.ids_any, s32[64]{0:T(128)S(1)} %copy-done.8, s32[4,16]{1,0:T(4,128)S(1)} %copy-done.6, bf16[1,848,128]{2,1,0:T(8,128)(2,1)S(1)} %get-tuple-element.23.rest_0_, bf16[1,848,128]{2,1,0:T(8,128)(2,1)S(1)} %collective-permute-done.rest_1_, ...), custom_call_target="tpu_custom_call" | custom-call | flops 8000000000 | bytes 24000000 | tf_op jit(solution)/shard_map/attend/pallas_call | solution.py:442
  13.7 0.0 slice-start.2
  13.7 0.1 collective-permute-start.1
  13.8 2.6 %collective-permute-start.2 = (bf16[32,4096]{1,0:T(8,128)(2,1)S(1)}, bf16[32,4096]{1,0:T(8,128)(2,1)S(1)}, u32[]{:S(2)}, u32[]{:S(2)}) collective-permute-start(bf16[32,4096]{1,0:T(8,128)(2,1)S(1)} %attend.2.rest_0_), channel_id=1, source_target_pairs={{0,8},{4,12},{8,0},{12,4},{1,9},{5,13},{9,1},{13,5},{2,10},{6,14},... | collective-permute-start | bytes 786440 | tf_op jit(solution)/shard_map/ppermute | solution.py:388
  16.4 0.1 collective-permute-done.4.rest_1_
  16.5 6.5 %attend.3.rest_0_ = bf16[32,4096]{1,0:T(8,128)(2,1)S(1)} custom-call(s32[1]{0:T(128)} %bitcast.ids_ref.ids_any, s32[64]{0:T(128)S(1)} %copy-done.8, s32[4,16]{1,0:T(4,128)S(1)} %copy-done.6, bf16[1,848,128]{2,1,0:T(8,128)(2,1)S(1)} %collective-permute-done.3.rest_0_, bf16[1,848,128]{2,1,0:T(8,128)(2,1)S(1)} %collective-permute-done.4.rest_1_, ...), custom_call_target="tpu_custom_call" | custom-call | flops 8000000000 | bytes 24000000 | tf_op jit(solution)/shard_map/attend/pallas_call | solution.py:442
  23.1 0.6 collective-permute-start.5
  23.6 0.1 collective-permute-start.8
  23.7 2.5 %collective-permute-start.9 = (bf16[32,4096]{1,0:T(8,128)(2,1)S(1)}, bf16[32,4096]{1,0:T(8,128)(2,1)S(1)}, u32[]{:S(2)}, u32[]{:S(2)}) collective-permute-start(bf16[32,4096]{1,0:T(8,128)(2,1)S(1)} %attend.3.rest_0_), channel_id=1, source_target_pairs={{0,8},{4,12},{8,0},{12,4},{1,9},{5,13},{9,1},{13,5},{2,10},{6,14},... | collective-permute-start | bytes 786440 | tf_op jit(solution)/shard_map/ppermute | solution.py:388
  26.2 0.0 collective-permute-done.1.rest_1_
  26.2 0.0 collective-permute-done.5.rest_3_
  26.2 1.3 %project_out.4 = (bf16[64,896]{1,0:T(8,128)(2,1)S(1)}, bf16[64,896]{1,0:T(8,128)(2,1)S(1)}) custom-call(s32[1]{0:T(128)} %bitcast.ids_ref.ids_any, bf16[32,4096]{1,0:T(8,128)(2,1)S(1)} %attend.2.rest_0_, bf16[32,4096]{1,0:T(8,128)(2,1)S(1)} %collective-permute-done.1.rest_1_, bf16[32,4096]{1,0:T(8,128)(2,1)S(1)} %collective-permute-done.2.rest_2_, ...), custom_call_target="tpu_custom_call" | custom-call | flops 2000000000 | bytes 6000000 | tf_op jit(solution)/shard_map/project_out/pallas_call | solution.py:495
  27.5 1.7 %collective-permute-start.6 = (bf16[64,896]{1,0:T(8,128)(2,1)S(1)}, bf16[64,896]{1,0:T(8,128)(2,1)S(1)}, u32[]{:S(2)}, u32[]{:S(2)}) collective-permute-start(bf16[64,896]{1,0:T(8,128)(2,1)S(1)} %get-tuple-element.29), channel_id=1, source_target_pairs={{0,1},{1,0},{2,3},{3,2},{4,5},{5,4},{6,7},{7,6},{8,9},{9,8},{10,11... | collective-permute-start | bytes 344072 | tf_op jit(solution)/shard_map/ppermute | solution.py:388
  29.1 1.3 %project_out.5 = (bf16[64,896]{1,0:T(8,128)(2,1)S(1)}, bf16[64,896]{1,0:T(8,128)(2,1)S(1)}) custom-call(s32[1]{0:T(128)} %bitcast.ids_ref.ids_any, bf16[32,4096]{1,0:T(8,128)(2,1)S(1)} %attend.2.rest_0_, bf16[32,4096]{1,0:T(8,128)(2,1)S(1)} %collective-permute-done.1.rest_1_, bf16[32,4096]{1,0:T(8,128)(2,1)S(1)} %collective-permute-done.2.rest_2_, ...), custom_call_target="tpu_custom_call" | custom-call | flops 2000000000 | bytes 6000000 | tf_op jit(solution)/shard_map/project_out/pallas_call | solution.py:495
  30.4 2.3 %collective-permute-done.9.rest_2_ = bf16[32,4096]{1,0:T(8,128)(2,1)S(1)} collective-permute-done((bf16[32,4096]{1,0:T(8,128)(2,1)S(1)}, bf16[32,4096]{1,0:T(8,128)(2,1)S(1)}, u32[]{:S(2)}, u32[]{:S(2)}) %collective-permute-start.9) | collective-permute-done | bytes 262176 | tf_op jit(solution)/shard_map/ppermute | solution.py:388
  32.7 0.0 collective-permute-start.10
  32.7 1.6 %collective-permute-start.13 = (bf16[64,896]{1,0:T(8,128)(2,1)S(1)}, bf16[64,896]{1,0:T(8,128)(2,1)S(1)}, u32[]{:S(2)}, u32[]{:S(2)}) collective-permute-start(bf16[64,896]{1,0:T(8,128)(2,1)S(1)} %get-tuple-element.36), channel_id=1, source_target_pairs={{0,1},{1,0},{2,3},{3,2},{4,5},{5,4},{6,7},{7,6},{8,9},{9,8},{10,11... | collective-permute-start | bytes 344072 | tf_op jit(solution)/shard_map/ppermute | solution.py:388
  34.3 0.0 collective-permute-done.6
  34.3 2.5 %collective-permute-start.7 = (bf16[64,896]{1,0:T(8,128)(2,1)S(1)}, bf16[64,896]{1,0:T(8,128)(2,1)S(1)}, u32[]{:S(2)}, u32[]{:S(2)}) collective-permute-start(bf16[64,896]{1,0:T(8,128)(2,1)S(1)} %add_convert_fusion.7), channel_id=1, source_target_pairs={{0,3},{1,2},{2,1},{3,0},{4,7},{5,6},{6,5},{7,4},{8,11},{9,10},{10,... | collective-permute-start | bytes 344072 | tf_op jit(solution)/shard_map/ppermute | solution.py:388
  36.9 1.3 %project_out.6 = (bf16[64,896]{1,0:T(8,128)(2,1)S(1)}, bf16[64,896]{1,0:T(8,128)(2,1)S(1)}) custom-call(s32[1]{0:T(128)} %bitcast.ids_ref.ids_any, bf16[32,4096]{1,0:T(8,128)(2,1)S(1)} %attend.3.rest_0_, bf16[32,4096]{1,0:T(8,128)(2,1)S(1)} %collective-permute-done.8.rest_1_, bf16[32,4096]{1,0:T(8,128)(2,1)S(1)} %collective-permute-done.9.rest_2_, ...), custom_call_target="tpu_custom_call" | custom-call | flops 2000000000 | bytes 6000000 | tf_op jit(solution)/shard_map/project_out/pallas_call | solution.py:495
  38.2 0.7 %collective-permute-start.11 = (bf16[64,896]{1,0:T(8,128)(2,1)S(1)}, bf16[64,896]{1,0:T(8,128)(2,1)S(1)}, u32[]{:S(2)}, u32[]{:S(2)}) collective-permute-start(bf16[64,896]{1,0:T(8,128)(2,1)S(1)} %get-tuple-element.34), channel_id=1, source_target_pairs={{0,1},{1,0},{2,3},{3,2},{4,5},{5,4},{6,7},{7,6},{8,9},{9,8},{10,11... | collective-permute-start | bytes 344072 | tf_op jit(solution)/shard_map/ppermute | solution.py:388
  38.9 5.2 %collective-permute-start.14 = (bf16[64,896]{1,0:T(8,128)(2,1)S(1)}, bf16[64,896]{1,0:T(8,128)(2,1)S(1)}, u32[]{:S(2)}, u32[]{:S(2)}) collective-permute-start(bf16[64,896]{1,0:T(8,128)(2,1)S(1)} %add_convert_fusion.4), channel_id=1, source_target_pairs={{0,3},{1,2},{2,1},{3,0},{4,7},{5,6},{6,5},{7,4},{8,11},{9,10},{10,... | collective-permute-start | bytes 344072 | tf_op jit(solution)/shard_map/ppermute | solution.py:388
  44.1 1.3 %project_out.7 = (bf16[64,896]{1,0:T(8,128)(2,1)S(1)}, bf16[64,896]{1,0:T(8,128)(2,1)S(1)}) custom-call(s32[1]{0:T(128)} %bitcast.ids_ref.ids_any, bf16[32,4096]{1,0:T(8,128)(2,1)S(1)} %attend.3.rest_0_, bf16[32,4096]{1,0:T(8,128)(2,1)S(1)} %collective-permute-done.8.rest_1_, bf16[32,4096]{1,0:T(8,128)(2,1)S(1)} %collective-permute-done.9.rest_2_, ...), custom_call_target="tpu_custom_call" | custom-call | flops 2000000000 | bytes 6000000 | tf_op jit(solution)/shard_map/project_out/pallas_call | solution.py:495
  45.4 0.1 collective-permute-start.18
  45.4 0.8 %collective-permute-done.11 = bf16[64,896]{1,0:T(8,128)(2,1)S(1)} collective-permute-done((bf16[64,896]{1,0:T(8,128)(2,1)S(1)}, bf16[64,896]{1,0:T(8,128)(2,1)S(1)}, u32[]{:S(2)}, u32[]{:S(2)}) %collective-permute-start.11) | collective-permute-done | bytes 114720 | tf_op jit(solution)/shard_map/ppermute | solution.py:388
  46.3 1.9 %collective-permute-start.16 = (bf16[64,896]{1,0:T(8,128)(2,1)S(1)}, bf16[64,896]{1,0:T(8,128)(2,1)S(1)}, u32[]{:S(2)}, u32[]{:S(2)}) collective-permute-start(bf16[64,896]{1,0:T(8,128)(2,1)S(1)} %add_convert_fusion.6), channel_id=1, source_target_pairs={{0,3},{1,2},{2,1},{3,0},{4,7},{5,6},{6,5},{7,4},{8,11},{9,10},{10,... | collective-permute-start | bytes 344072 | tf_op jit(solution)/shard_map/ppermute | solution.py:388
  48.2 0.1 collective-permute-start.12
  48.3 2.1 %collective-permute-start.15 = (bf16[64,896]{1,0:T(8,128)(2,1)S(1)}, bf16[64,896]{1,0:T(8,128)(2,1)S(1)}, u32[]{:S(2)}, u32[]{:S(2)}) collective-permute-start(bf16[64,896]{1,0:T(8,128)(2,1)S(1)} %add_convert_fusion.3.rest_2_), channel_id=1, source_target_pairs={{0,1},{1,0},{2,3},{3,2},{4,5},{5,4},{6,7},{7,6},{8,9},{9,8},{10,11... | collective-permute-start | bytes 344072 | tf_op jit(solution)/shard_map/ppermute | solution.py:388
  50.4 0.0 collective-permute-done.18
  50.4 2.1 %collective-permute-start.19 = (bf16[64,896]{1,0:T(8,128)(2,1)S(1)}, bf16[64,896]{1,0:T(8,128)(2,1)S(1)}, u32[]{:S(2)}, u32[]{:S(2)}) collective-permute-start(bf16[64,896]{1,0:T(8,128)(2,1)S(1)} %add_convert_fusion.1), channel_id=1, source_target_pairs={{0,3},{1,2},{2,1},{3,0},{4,7},{5,6},{6,5},{7,4},{8,11},{9,10},{10,... | collective-permute-start | bytes 344072 | tf_op jit(solution)/shard_map/ppermute | solution.py:388
  52.5 1.7 %collective-permute-done.16 = bf16[64,896]{1,0:T(8,128)(2,1)S(1)} collective-permute-done((bf16[64,896]{1,0:T(8,128)(2,1)S(1)}, bf16[64,896]{1,0:T(8,128)(2,1)S(1)}, u32[]{:S(2)}, u32[]{:S(2)}) %collective-permute-start.16) | collective-permute-done | bytes 114720 | tf_op jit(solution)/shard_map/ppermute | solution.py:388
  54.3 1.4 %collective-permute-start.17 = (bf16[64,896]{1,0:T(8,128)(2,1)S(1)}, bf16[64,896]{1,0:T(8,128)(2,1)S(1)}, u32[]{:S(2)}, u32[]{:S(2)}) collective-permute-start(bf16[64,896]{1,0:T(8,128)(2,1)S(1)} %add_convert_fusion.2.rest_4_), channel_id=1, source_target_pairs={{0,1},{1,0},{2,3},{3,2},{4,5},{5,4},{6,7},{7,6},{8,9},{9,8},{10,11... | collective-permute-start | bytes 344072 | tf_op jit(solution)/shard_map/ppermute | solution.py:388
  55.6 5.8 %collective-permute-done.19 = bf16[64,896]{1,0:T(8,128)(2,1)S(1)} collective-permute-done((bf16[64,896]{1,0:T(8,128)(2,1)S(1)}, bf16[64,896]{1,0:T(8,128)(2,1)S(1)}, u32[]{:S(2)}, u32[]{:S(2)}) %collective-permute-start.19) | collective-permute-done | bytes 114720 | tf_op jit(solution)/shard_map/ppermute | solution.py:388
  61.4 0.1 collective-permute-start.20
  61.5 1.3 %collective-permute-done.17.rest_5_ = bf16[64,896]{1,0:T(8,128)(2,1)S(1)} collective-permute-done((bf16[64,896]{1,0:T(8,128)(2,1)S(1)}, bf16[64,896]{1,0:T(8,128)(2,1)S(1)}, u32[]{:S(2)}, u32[]{:S(2)}) %collective-permute-start.17) | collective-permute-done | bytes 114720 | tf_op jit(solution)/shard_map/ppermute | solution.py:388
  62.8 3.4 %collective-permute-done.20.rest_7_ = bf16[64,896]{1,0:T(8,128)(2,1)S(1)} collective-permute-done((bf16[64,896]{1,0:T(8,128)(2,1)S(1)}, bf16[64,896]{1,0:T(8,128)(2,1)S(1)}, u32[]{:S(2)}, u32[]{:S(2)}) %collective-permute-start.20) | collective-permute-done | bytes 114720 | tf_op jit(solution)/shard_map/ppermute | solution.py:388
  66.3 1.4 %order_rows.1 = bf16[4,64,1792]{2,1,0:T(8,128)(2,1)} custom-call(s32[1]{0:T(128)} %bitcast.ids_ref.ids_any, bf16[4,64,256]{2,1,0:T(8,128)(2,1)S(1)} %place_rows.1.after_ref.pick_ref, bf16[64,896]{1,0:T(8,128)(2,1)S(1)} %add_convert_fusion.5.rest_0_, bf16[64,896]{1,0:T(8,128)(2,1)S(1)} %collective-permute-done.12.rest_1_, ...), custom_call_target="tpu_custom_call" | custom-call | flops 2000000000 | bytes 6000000 | tf_op jit(solution)/shard_map/order_rows/pallas_call | solution.py:472
  (38 shorter events, 0.3 us)
Async XLA Ops:
  0.0 1.9 %copy-start.3 = (bf16[4,16,32,128]{3,2,1,0:T(8,128)(2,1)S(1)}, bf16[4,16,32,128]{3,2,1,0:T(8,128)(2,1)}, u32[]{:S(2)}) copy-start(bf16[4,16,32,128]{3,2,1,0:T(8,128)(2,1)} %nope_ref.1) | copy-start | bytes 1572868
  0.0 1.9 %copy-start.4 = (bf16[4,16,32,64]{3,2,1,0:T(8,128)(2,1)S(1)}, bf16[4,16,32,64]{3,2,1,0:T(8,128)(2,1)}, u32[]{:S(2)}) copy-start(bf16[4,16,32,64]{3,2,1,0:T(8,128)(2,1)} %rope_ref.1) | copy-start | bytes 786436
  0.0 1.9 %copy-start.5 = (bf16[4,16,576]{2,1,0:T(8,128)(2,1)S(1)}, bf16[4,16,576]{2,1,0:T(8,128)(2,1)}, u32[]{:S(2)}) copy-start(bf16[4,16,576]{2,1,0:T(8,128)(2,1)} %fresh_ref.1) | copy-start | bytes 221188
  0.0 0.7 %copy-start.7 = (s32[64]{0:T(128)S(1)}, s32[64]{0:T(128)}, u32[]{:S(2)}) copy-start(s32[64]{0:T(128)} %decode_any.3) | copy-start | bytes 772
  0.8 5.5 %copy-start.1 = (bf16[32,128,512]{2,1,0:T(8,128)(2,1)S(1)}, bf16[32,128,512]{2,1,0:T(8,128)(2,1)}, u32[]{:S(2)}) copy-start(bf16[32,128,512]{2,1,0:T(8,128)(2,1)} %rest_3_.3) | copy-start | bytes 12582916
  0.8 5.5 %copy-start.2 = (bf16[32,512,128]{2,1,0:T(8,128)(2,1)S(1)}, bf16[32,512,128]{2,1,0:T(8,128)(2,1)}, u32[]{:S(2)}) copy-start(bf16[32,512,128]{2,1,0:T(8,128)(2,1)} %rest_4_.7) | copy-start | bytes 12582916
  1.9 4.4 %copy-start = (bf16[4096,576]{0,1:T(8,128)(2,1)S(1)}, bf16[4096,576]{0,1:T(8,128)(2,1)}, u32[]{:S(2)}) copy-start(bf16[4096,576]{0,1:T(8,128)(2,1)} %param.9) | copy-start | bytes 14155780
  1.9 4.4 %copy-start.6 = (s32[4,16]{1,0:T(4,128)S(1)}, s32[4,16]{1,0:T(4,128)}, u32[]{:S(2)}) copy-start(s32[4,16]{1,0:T(4,128)} %length_any.3) | copy-start | bytes 772
  1.9 4.4 %copy-start.8 = (s32[64]{0:T(128)S(1)}, s32[64]{0:T(128)}, u32[]{:S(2)}) copy-start(s32[64]{0:T(128)} %decode_any.3) | copy-start | bytes 772
  3.1 3.2 %collective-permute-start = (bf16[1,848,128]{2,1,0:T(8,128)(2,1)S(1)}, bf16[1,848,128]{2,1,0:T(8,128)(2,1)S(1)}, u32[]{:S(2)}, u32[]{:S(2)}) collective-permute-start(bf16[1,848,128]{2,1,0:T(8,128)(2,1)S(1)} %get-tuple-element.24), channel_id=1, source_target_pairs={{0,4},{4,0},{8,12},{12,8},{1,5},{5,1},{9,13},{13,9},{2,6},{6,2},{1... | collective-permute-start | bytes 651272 | tf_op jit(solution)/shard_map/ppermute | solution.py:388
  3.6 12.8 %collective-permute-start.3 = (bf16[1,848,128]{2,1,0:T(8,128)(2,1)S(1)}, bf16[1,848,128]{2,1,0:T(8,128)(2,1)S(1)}, u32[]{:S(2)}, u32[]{:S(2)}) collective-permute-start(bf16[1,848,128]{2,1,0:T(8,128)(2,1)S(1)} %get-tuple-element.25), channel_id=1, source_target_pairs={{0,8},{4,12},{8,0},{12,4},{1,9},{5,13},{9,1},{13,5},{2,10},{6,14},... | collective-permute-start | bytes 651272 | tf_op jit(solution)/shard_map/ppermute | solution.py:388
  6.2 10.3 %collective-permute-start.4 = (bf16[1,848,128]{2,1,0:T(8,128)(2,1)S(1)}, bf16[1,848,128]{2,1,0:T(8,128)(2,1)S(1)}, u32[]{:S(2)}, u32[]{:S(2)}) collective-permute-start(bf16[1,848,128]{2,1,0:T(8,128)(2,1)S(1)} %get-tuple-element.26), channel_id=1, source_target_pairs={{0,12},{4,8},{8,4},{12,0},{1,13},{5,9},{9,5},{13,1},{2,14},{6,10},... | collective-permute-start | bytes 651272 | tf_op jit(solution)/shard_map/ppermute | solution.py:388
  6.3 19.9 %slice-start = ((s8[14680064]{0:T(1024)(128)(4,1)}), s8[4194304]{0:T(1024)(128)(4,1)S(1)}, s32[]{:S(2)}) async-start(s8[14680064]{0:T(1024)(128)(4,1)} %bitcast.2), calls=%async_computation | async-start | bytes 8388608
  6.3 19.9 %slice-start.1 = ((s8[14680064]{0:T(1024)(128)(4,1)}), s8[4194304]{0:T(1024)(128)(4,1)S(1)}, s32[]{:S(2)}) async-start(s8[14680064]{0:T(1024)(128)(4,1)} %bitcast.2), calls=%async_computation.1 | async-start | bytes 8388608
  13.7 12.5 %slice-start.2 = ((s8[14680064]{0:T(1024)(128)(4,1)}), s8[4194304]{0:T(1024)(128)(4,1)S(1)}, s32[]{:S(2)}) async-start(s8[14680064]{0:T(1024)(128)(4,1)} %bitcast.2), calls=%async_computation.2 | async-start | bytes 8388608
  13.7 12.5 %slice-start.3 = ((s8[14680064]{0:T(1024)(128)(4,1)}), s8[2097152]{0:T(1024)(128)(4,1)S(1)}, s32[]{:S(2)}) async-start(s8[14680064]{0:T(1024)(128)(4,1)} %bitcast.2), calls=%async_computation.3 | async-start | bytes 4194304
  13.7 12.5 %collective-permute-start.1 = (bf16[32,4096]{1,0:T(8,128)(2,1)S(1)}, bf16[32,4096]{1,0:T(8,128)(2,1)S(1)}, u32[]{:S(2)}, u32[]{:S(2)}) collective-permute-start(bf16[32,4096]{1,0:T(8,128)(2,1)S(1)} %attend.2.rest_0_), channel_id=1, source_target_pairs={{0,4},{4,0},{8,12},{12,8},{1,5},{5,1},{9,13},{13,9},{2,6},{6,2},{1... | collective-permute-start | bytes 786440 | tf_op jit(solution)/shard_map/ppermute | solution.py:388
  13.8 9.3 %collective-permute-start.2 = (bf16[32,4096]{1,0:T(8,128)(2,1)S(1)}, bf16[32,4096]{1,0:T(8,128)(2,1)S(1)}, u32[]{:S(2)}, u32[]{:S(2)}) collective-permute-start(bf16[32,4096]{1,0:T(8,128)(2,1)S(1)} %attend.2.rest_0_), channel_id=1, source_target_pairs={{0,8},{4,12},{8,0},{12,4},{1,9},{5,13},{9,1},{13,5},{2,10},{6,14},... | collective-permute-start | bytes 786440 | tf_op jit(solution)/shard_map/ppermute | solution.py:388
  23.1 3.1 %collective-permute-start.5 = (bf16[32,4096]{1,0:T(8,128)(2,1)S(1)}, bf16[32,4096]{1,0:T(8,128)(2,1)S(1)}, u32[]{:S(2)}, u32[]{:S(2)}) collective-permute-start(bf16[32,4096]{1,0:T(8,128)(2,1)S(1)} %collective-permute-done.2.rest_2_), channel_id=1, source_target_pairs={{0,4},{4,0},{8,12},{12,8},{1,5},{5,1},{9,13},{13,9},{2,6},{6,2},{1... | collective-permute-start | bytes 786440 | tf_op jit(solution)/shard_map/ppermute | solution.py:388
  23.6 13.3 %collective-permute-start.8 = (bf16[32,4096]{1,0:T(8,128)(2,1)S(1)}, bf16[32,4096]{1,0:T(8,128)(2,1)S(1)}, u32[]{:S(2)}, u32[]{:S(2)}) collective-permute-start(bf16[32,4096]{1,0:T(8,128)(2,1)S(1)} %attend.3.rest_0_), channel_id=1, source_target_pairs={{0,4},{4,0},{8,12},{12,8},{1,5},{5,1},{9,13},{13,9},{2,6},{6,2},{1... | collective-permute-start | bytes 786440 | tf_op jit(solution)/shard_map/ppermute | solution.py:388
  23.7 9.0 %collective-permute-start.9 = (bf16[32,4096]{1,0:T(8,128)(2,1)S(1)}, bf16[32,4096]{1,0:T(8,128)(2,1)S(1)}, u32[]{:S(2)}, u32[]{:S(2)}) collective-permute-start(bf16[32,4096]{1,0:T(8,128)(2,1)S(1)} %attend.3.rest_0_), channel_id=1, source_target_pairs={{0,8},{4,12},{8,0},{12,4},{1,9},{5,13},{9,1},{13,5},{2,10},{6,14},... | collective-permute-start | bytes 786440 | tf_op jit(solution)/shard_map/ppermute | solution.py:388
  27.5 6.8 %collective-permute-start.6 = (bf16[64,896]{1,0:T(8,128)(2,1)S(1)}, bf16[64,896]{1,0:T(8,128)(2,1)S(1)}, u32[]{:S(2)}, u32[]{:S(2)}) collective-permute-start(bf16[64,896]{1,0:T(8,128)(2,1)S(1)} %get-tuple-element.29), channel_id=1, source_target_pairs={{0,1},{1,0},{2,3},{3,2},{4,5},{5,4},{6,7},{7,6},{8,9},{9,8},{10,11... | collective-permute-start | bytes 344072 | tf_op jit(solution)/shard_map/ppermute | solution.py:388
  32.7 4.2 %collective-permute-start.10 = (bf16[32,4096]{1,0:T(8,128)(2,1)S(1)}, bf16[32,4096]{1,0:T(8,128)(2,1)S(1)}, u32[]{:S(2)}, u32[]{:S(2)}) collective-permute-start(bf16[32,4096]{1,0:T(8,128)(2,1)S(1)} %collective-permute-done.9.rest_2_), channel_id=1, source_target_pairs={{0,4},{4,0},{8,12},{12,8},{1,5},{5,1},{9,13},{13,9},{2,6},{6,2},{1... | collective-permute-start | bytes 786440 | tf_op jit(solution)/shard_map/ppermute | solution.py:388
  32.7 6.2 %collective-permute-start.13 = (bf16[64,896]{1,0:T(8,128)(2,1)S(1)}, bf16[64,896]{1,0:T(8,128)(2,1)S(1)}, u32[]{:S(2)}, u32[]{:S(2)}) collective-permute-start(bf16[64,896]{1,0:T(8,128)(2,1)S(1)} %get-tuple-element.36), channel_id=1, source_target_pairs={{0,1},{1,0},{2,3},{3,2},{4,5},{5,4},{6,7},{7,6},{8,9},{9,8},{10,11... | collective-permute-start | bytes 344072 | tf_op jit(solution)/shard_map/ppermute | solution.py:388
  34.3 13.8 %collective-permute-start.7 = (bf16[64,896]{1,0:T(8,128)(2,1)S(1)}, bf16[64,896]{1,0:T(8,128)(2,1)S(1)}, u32[]{:S(2)}, u32[]{:S(2)}) collective-permute-start(bf16[64,896]{1,0:T(8,128)(2,1)S(1)} %add_convert_fusion.7), channel_id=1, source_target_pairs={{0,3},{1,2},{2,1},{3,0},{4,7},{5,6},{6,5},{7,4},{8,11},{9,10},{10,... | collective-permute-start | bytes 344072 | tf_op jit(solution)/shard_map/ppermute | solution.py:388
  38.2 8.1 %collective-permute-start.11 = (bf16[64,896]{1,0:T(8,128)(2,1)S(1)}, bf16[64,896]{1,0:T(8,128)(2,1)S(1)}, u32[]{:S(2)}, u32[]{:S(2)}) collective-permute-start(bf16[64,896]{1,0:T(8,128)(2,1)S(1)} %get-tuple-element.34), channel_id=1, source_target_pairs={{0,1},{1,0},{2,3},{3,2},{4,5},{5,4},{6,7},{7,6},{8,9},{9,8},{10,11... | collective-permute-start | bytes 344072 | tf_op jit(solution)/shard_map/ppermute | solution.py:388
  38.9 9.3 %collective-permute-start.14 = (bf16[64,896]{1,0:T(8,128)(2,1)S(1)}, bf16[64,896]{1,0:T(8,128)(2,1)S(1)}, u32[]{:S(2)}, u32[]{:S(2)}) collective-permute-start(bf16[64,896]{1,0:T(8,128)(2,1)S(1)} %add_convert_fusion.4), channel_id=1, source_target_pairs={{0,3},{1,2},{2,1},{3,0},{4,7},{5,6},{6,5},{7,4},{8,11},{9,10},{10,... | collective-permute-start | bytes 344072 | tf_op jit(solution)/shard_map/ppermute | solution.py:388
  45.4 5.0 %collective-permute-start.18 = (bf16[64,896]{1,0:T(8,128)(2,1)S(1)}, bf16[64,896]{1,0:T(8,128)(2,1)S(1)}, u32[]{:S(2)}, u32[]{:S(2)}) collective-permute-start(bf16[64,896]{1,0:T(8,128)(2,1)S(1)} %get-tuple-element.40), channel_id=1, source_target_pairs={{0,1},{1,0},{2,3},{3,2},{4,5},{5,4},{6,7},{7,6},{8,9},{9,8},{10,11... | collective-permute-start | bytes 344072 | tf_op jit(solution)/shard_map/ppermute | solution.py:388
  46.3 8.0 %collective-permute-start.16 = (bf16[64,896]{1,0:T(8,128)(2,1)S(1)}, bf16[64,896]{1,0:T(8,128)(2,1)S(1)}, u32[]{:S(2)}, u32[]{:S(2)}) collective-permute-start(bf16[64,896]{1,0:T(8,128)(2,1)S(1)} %add_convert_fusion.6), channel_id=1, source_target_pairs={{0,3},{1,2},{2,1},{3,0},{4,7},{5,6},{6,5},{7,4},{8,11},{9,10},{10,... | collective-permute-start | bytes 344072 | tf_op jit(solution)/shard_map/ppermute | solution.py:388
  48.2 13.3 %collective-permute-start.12 = (bf16[64,896]{1,0:T(8,128)(2,1)S(1)}, bf16[64,896]{1,0:T(8,128)(2,1)S(1)}, u32[]{:S(2)}, u32[]{:S(2)}) collective-permute-start(bf16[64,896]{1,0:T(8,128)(2,1)S(1)} %add_convert_fusion.5.rest_0_), channel_id=1, source_target_pairs={{0,1},{1,0},{2,3},{3,2},{4,5},{5,4},{6,7},{7,6},{8,9},{9,8},{10,11... | collective-permute-start | bytes 344072 | tf_op jit(solution)/shard_map/ppermute | solution.py:388
  48.3 13.2 %collective-permute-start.15 = (bf16[64,896]{1,0:T(8,128)(2,1)S(1)}, bf16[64,896]{1,0:T(8,128)(2,1)S(1)}, u32[]{:S(2)}, u32[]{:S(2)}) collective-permute-start(bf16[64,896]{1,0:T(8,128)(2,1)S(1)} %add_convert_fusion.3.rest_2_), channel_id=1, source_target_pairs={{0,1},{1,0},{2,3},{3,2},{4,5},{5,4},{6,7},{7,6},{8,9},{9,8},{10,11... | collective-permute-start | bytes 344072 | tf_op jit(solution)/shard_map/ppermute | solution.py:388
  50.4 11.0 %collective-permute-start.19 = (bf16[64,896]{1,0:T(8,128)(2,1)S(1)}, bf16[64,896]{1,0:T(8,128)(2,1)S(1)}, u32[]{:S(2)}, u32[]{:S(2)}) collective-permute-start(bf16[64,896]{1,0:T(8,128)(2,1)S(1)} %add_convert_fusion.1), channel_id=1, source_target_pairs={{0,3},{1,2},{2,1},{3,0},{4,7},{5,6},{6,5},{7,4},{8,11},{9,10},{10,... | collective-permute-start | bytes 344072 | tf_op jit(solution)/shard_map/ppermute | solution.py:388
  54.3 8.6 %collective-permute-start.17 = (bf16[64,896]{1,0:T(8,128)(2,1)S(1)}, bf16[64,896]{1,0:T(8,128)(2,1)S(1)}, u32[]{:S(2)}, u32[]{:S(2)}) collective-permute-start(bf16[64,896]{1,0:T(8,128)(2,1)S(1)} %add_convert_fusion.2.rest_4_), channel_id=1, source_target_pairs={{0,1},{1,0},{2,3},{3,2},{4,5},{5,4},{6,7},{7,6},{8,9},{9,8},{10,11... | collective-permute-start | bytes 344072 | tf_op jit(solution)/shard_map/ppermute | solution.py:388
  61.4 4.9 %collective-permute-start.20 = (bf16[64,896]{1,0:T(8,128)(2,1)S(1)}, bf16[64,896]{1,0:T(8,128)(2,1)S(1)}, u32[]{:S(2)}, u32[]{:S(2)}) collective-permute-start(bf16[64,896]{1,0:T(8,128)(2,1)S(1)} %add_convert_fusion.rest_6_), channel_id=1, source_target_pairs={{0,1},{1,0},{2,3},{3,2},{4,5},{5,4},{6,7},{7,6},{8,9},{9,8},{10,11... | collective-permute-start | bytes 344072 | tf_op jit(solution)/shard_map/ppermute | solution.py:388

commit v16 on v14

--- a/solution.py
+++ b/solution.py
@@ -27,6 +27,10 @@
         return carry
 
     lax.fori_loop(0, sources, one_source, jnp.int32(0))
+
+
+def mark_kernel(ids_ref, out_ref):
+    out_ref[...] = jnp.full(out_ref.shape, ids_ref[0], jnp.int32)
 
 
 def pack_kernel(sizes, relative, ids_ref, decode_ref, nope_ref, rope_ref, fresh_ref, after_ref, *rest):
@@ -420,6 +424,16 @@
         name="place_rows",
     )(ids, decode_rows)
 
+    mark = pl.pallas_call(
+        mark_kernel,
+        out_shape=jax.ShapeDtypeStruct((8, LANES), jnp.int32),
+        in_specs=[smem()],
+        out_specs=vmem(),
+        compiler_params=limit(4),
+        cost_estimate=cost(2),
+        name="mark_start",
+    )(ids)
+
     outs, each = (sources, 1) if relative else (1, sources)
     packed = pl.pallas_call(
         functools.partial(pack_kernel, sizes, relative),
@@ -433,7 +447,7 @@
         compiler_params=limit(8),
         cost_estimate=cost(2),
         name="pack_queries",
-    )(ids, decode_rows, q_nope, q_rope, new_latent, pick)
+    )(ids, decode_rows, q_nope, q_rope, new_latent, mark)
 
     def attend(received, base):
         here = sum(part.shape[0] for part in received)
@@ -539,7 +553,7 @@
     arrays = []
     for i, (pair, cross) in enumerate(zip(pairs, crossed)):
         if i < len(near_made):
-            cross = after(cross, *(pairs[len(near_made)],))
+            cross = after(cross, *(last_made,))
         total = add(pair, cross)
         arrays += [total, flip(total, "head", 1)]
     layout = tuple((row, col) for row, col, _, _ in made)

time: 67.8 us -> 68 us (level)
  starting transfers between devices: 30.8 us -> 32.1 us
    ppermute x24, starting transfers between devices: 30.8 us -> 32.1 us  [flip(): return lax.ppermute(x, axis, [(i, i ^ distance) for i in range(size)])]
  transfers between devices with their start and end apart: 24 -> 24, of which waited for: 7 -> 4; matrix products, arithmetic and copies ran while one was open for 0% -> 0% of each run, Pallas kernels for 29% -> 29%
where the time goes in v16:
time: 68 us; the launch traced here: 68.4 us
  starting transfers between devices  32.1 us (47%)
  Pallas kernels  22.6 us (33%)
  waiting for transfers between devices  11.9 us (18%)
  local copies, waits for them, and re-layouts  1.23 us (2%)
    ppermute x24, starting transfers between devices, flip(): return lax.ppermute(x, axis, [(i, i ^ distance) for i in range(size)])  32.1 us
    pallas_call x2, Pallas kernels, attend(): pl.pallas_call(functools.partial(attend_kernel, sizes, scale, relative, b...  13.7 us
    ppermute x24, waiting for transfers between devices, flip(): return lax.ppermute(x, axis, [(i, i ^ distance) for i in range(size)])  11.9 us
    pallas_call x5, Pallas kernels, project(): pl.pallas_call(functools.partial(project_kernel, first_col), out_shape=[j...  5.29 us
    pallas_call x1, Pallas kernels, order(): pl.pallas_call(kernel, out_shape=jax.ShapeDtypeStruct((steps, sources * r...  1.41 us
  transfers between devices with their start and end apart: 24, of which 4 were waited for; matrix products, arithmetic and copies ran while one was open for 0% of the time, Pallas kernels for 29%

profile of v16, /device:TPU:0, one launch (start us, length us, event | category | flops | bytes accessed | tf_op | source)
XLA Modules:
  0.0 68.4 jit_solution(11620782777339126202)
XLA Ops:
  0.0 0.6 copy-done.7
  0.7 0.4 copy-done.3
  1.1 0.2 copy-done.4
  1.2 1.1 %pack_queries.1 = (bf16[1,848,128]{2,1,0:T(8,128)(2,1)S(1)}, bf16[1,848,128]{2,1,0:T(8,128)(2,1)S(1)}, bf16[1,848,128]{2,1,0:T(8,128)(2,1)S(1)}, bf16[1,848,128]{2,1,0:T(8,128)(2,1)S(1)}) custom-call(s32[1]{0:T(128)} %bitcast.ids_ref.ids_any, s32[64]{0:T(128)S(1)} %copy-done.7, bf16[4,16,32,128]{3,2,1,0:T(8,128)(2,1)S(1)} %copy-done.3, ...), custom_call_target="tpu_custom_call" | custom-call | flops 2000000000 | bytes 6000000 | tf_op jit(solution)/shard_map/pack_queries/pallas_call | solution.py:438
  2.4 0.5 collective-permute-start
  2.9 2.6 %collective-permute-start.3 = (bf16[1,848,128]{2,1,0:T(8,128)(2,1)S(1)}, bf16[1,848,128]{2,1,0:T(8,128)(2,1)S(1)}, u32[]{:S(2)}, u32[]{:S(2)}) collective-permute-start(bf16[1,848,128]{2,1,0:T(8,128)(2,1)S(1)} %get-tuple-element.25), channel_id=1, source_target_pairs={{0,8},{4,12},{8,0},{12,4},{1,9},{5,13},{9,1},{13,5},{2,10},{6,14},... | collective-permute-start | bytes 651272 | tf_op jit(solution)/shard_map/ppermute | solution.py:392
  5.5 0.1 collective-permute-start.4
  5.5 0.0 collective-permute-done.rest_1_
  5.6 0.0 slice-start
  5.6 0.0 slice-start.1
  5.6 6.7 %attend.2.rest_0_ = bf16[32,4096]{1,0:T(8,128)(2,1)S(1)} custom-call(s32[1]{0:T(128)} %bitcast.ids_ref.ids_any, s32[64]{0:T(128)S(1)} %copy-done.7, s32[4,16]{1,0:T(4,128)S(1)} %copy-done.6, bf16[1,848,128]{2,1,0:T(8,128)(2,1)S(1)} %get-tuple-element.23.rest_0_, bf16[1,848,128]{2,1,0:T(8,128)(2,1)S(1)} %collective-permute-done.rest_1_, ...), custom_call_target="tpu_custom_call" | custom-call | flops 8000000000 | bytes 24000000 | tf_op jit(solution)/shard_map/attend/pallas_call | solution.py:456
  12.3 0.0 slice-start.2
  12.4 3.4 %collective-permute-start.2 = (bf16[32,4096]{1,0:T(8,128)(2,1)S(1)}, bf16[32,4096]{1,0:T(8,128)(2,1)S(1)}, u32[]{:S(2)}, u32[]{:S(2)}) collective-permute-start(bf16[32,4096]{1,0:T(8,128)(2,1)S(1)} %attend.2.rest_0_), channel_id=1, source_target_pairs={{0,8},{4,12},{8,0},{12,4},{1,9},{5,13},{9,1},{13,5},{2,10},{6,14},... | collective-permute-start | bytes 786440 | tf_op jit(solution)/shard_map/ppermute | solution.py:392
  15.8 0.0 collective-permute-done.4.rest_1_
  15.8 6.9 %attend.3.rest_0_ = bf16[32,4096]{1,0:T(8,128)(2,1)S(1)} custom-call(s32[1]{0:T(128)} %bitcast.ids_ref.ids_any, s32[64]{0:T(128)S(1)} %copy-done.7, s32[4,16]{1,0:T(4,128)S(1)} %copy-done.6, bf16[1,848,128]{2,1,0:T(8,128)(2,1)S(1)} %collective-permute-done.3.rest_0_, bf16[1,848,128]{2,1,0:T(8,128)(2,1)S(1)} %collective-permute-done.4.rest_1_, ...), custom_call_target="tpu_custom_call" | custom-call | flops 8000000000 | bytes 24000000 | tf_op jit(solution)/shard_map/attend/pallas_call | solution.py:456
  22.7 0.0 collective-permute-done.2.rest_2_
  22.7 0.1 collective-permute-start.5
  22.9 2.8 %collective-permute-start.9 = (bf16[32,4096]{1,0:T(8,128)(2,1)S(1)}, bf16[32,4096]{1,0:T(8,128)(2,1)S(1)}, u32[]{:S(2)}, u32[]{:S(2)}) collective-permute-start(bf16[32,4096]{1,0:T(8,128)(2,1)S(1)} %attend.3.rest_0_), channel_id=1, source_target_pairs={{0,8},{4,12},{8,0},{12,4},{1,9},{5,13},{9,1},{13,5},{2,10},{6,14},... | collective-permute-start | bytes 786440 | tf_op jit(solution)/shard_map/ppermute | solution.py:392
  25.7 0.0 collective-permute-start.8
  25.7 0.0 collective-permute-done.1.rest_1_
  25.7 0.0 collective-permute-done.5.rest_3_
  25.7 1.0 %project_out.5 = (bf16[64,640]{1,0:T(8,128)(2,1)S(1)}, bf16[64,640]{1,0:T(8,128)(2,1)S(1)}) custom-call(s32[1]{0:T(128)} %bitcast.ids_ref.ids_any, bf16[32,4096]{1,0:T(8,128)(2,1)S(1)} %attend.2.rest_0_, bf16[32,4096]{1,0:T(8,128)(2,1)S(1)} %collective-permute-done.1.rest_1_, bf16[32,4096]{1,0:T(8,128)(2,1)S(1)} %collective-permute-done.2.rest_2_, ...), custom_call_target="tpu_custom_call" | custom-call | flops 2000000000 | bytes 6000000 | tf_op jit(solution)/shard_map/project_out/pallas_call | solution.py:509
  26.7 1.6 %collective-permute-start.6 = (bf16[64,640]{1,0:T(8,128)(2,1)S(1)}, bf16[64,640]{1,0:T(8,128)(2,1)S(1)}, u32[]{:S(2)}, u32[]{:S(2)}) collective-permute-start(bf16[64,640]{1,0:T(8,128)(2,1)S(1)} %get-tuple-element.29), channel_id=1, source_target_pairs={{0,1},{1,0},{2,3},{3,2},{4,5},{5,4},{6,7},{7,6},{8,9},{9,8},{10,11... | collective-permute-start | bytes 245768 | tf_op jit(solution)/shard_map/ppermute | solution.py:392
  28.4 1.5 %project_out.7 = (bf16[64,1152]{1,0:T(8,128)(2,1)S(1)}, bf16[64,1152]{1,0:T(8,128)(2,1)S(1)}) custom-call(s32[1]{0:T(128)} %bitcast.ids_ref.ids_any, bf16[32,4096]{1,0:T(8,128)(2,1)S(1)} %attend.2.rest_0_, bf16[32,4096]{1,0:T(8,128)(2,1)S(1)} %collective-permute-done.1.rest_1_, bf16[32,4096]{1,0:T(8,128)(2,1)S(1)} %collective-permute-done.2.rest_2_, ...), custom_call_target="tpu_custom_call" | custom-call | flops 2000000000 | bytes 6000000 | tf_op jit(solution)/shard_map/project_out/pallas_call | solution.py:509
  29.9 0.5 collective-permute-start.12
  30.5 1.8 %collective-permute-done.9.rest_2_ = bf16[32,4096]{1,0:T(8,128)(2,1)S(1)} collective-permute-done((bf16[32,4096]{1,0:T(8,128)(2,1)S(1)}, bf16[32,4096]{1,0:T(8,128)(2,1)S(1)}, u32[]{:S(2)}, u32[]{:S(2)}) %collective-permute-start.9) | collective-permute-done | bytes 262176 | tf_op jit(solution)/shard_map/ppermute | solution.py:392
  32.3 3.7 %collective-permute-start.7 = (bf16[64,640]{1,0:T(8,128)(2,1)S(1)}, bf16[64,640]{1,0:T(8,128)(2,1)S(1)}, u32[]{:S(2)}, u32[]{:S(2)}) collective-permute-start(bf16[64,640]{1,0:T(8,128)(2,1)S(1)} %add_convert_fusion.7), channel_id=1, source_target_pairs={{0,3},{1,2},{2,1},{3,0},{4,7},{5,6},{6,5},{7,4},{8,11},{9,10},{10,... | collective-permute-start | bytes 245768 | tf_op jit(solution)/shard_map/ppermute | solution.py:392
  35.9 0.0 collective-permute-done.12
  36.0 2.5 %collective-permute-start.13 = (bf16[64,1152]{1,0:T(8,128)(2,1)S(1)}, bf16[64,1152]{1,0:T(8,128)(2,1)S(1)}, u32[]{:S(2)}, u32[]{:S(2)}) collective-permute-start(bf16[64,1152]{1,0:T(8,128)(2,1)S(1)} %add_convert_fusion.1), channel_id=1, source_target_pairs={{0,3},{1,2},{2,1},{3,0},{4,7},{5,6},{6,5},{7,4},{8,11},{9,10},{10,... | collective-permute-start | bytes 442376 | tf_op jit(solution)/shard_map/ppermute | solution.py:392
  38.5 0.7 %project_out.6 = (bf16[64,384]{1,0:T(8,128)(2,1)S(1)}, bf16[64,384]{1,0:T(8,128)(2,1)S(1)}) custom-call(s32[1]{0:T(128)} %bitcast.ids_ref.ids_any, bf16[32,4096]{1,0:T(8,128)(2,1)S(1)} %attend.3.rest_0_, bf16[32,4096]{1,0:T(8,128)(2,1)S(1)} %collective-permute-done.8.rest_1_, bf16[32,4096]{1,0:T(8,128)(2,1)S(1)} %collective-permute-done.9.rest_2_, ...), custom_call_target="tpu_custom_call" | custom-call | flops 2000000000 | bytes 6000000 | tf_op jit(solution)/shard_map/project_out/pallas_call | solution.py:509
  39.3 1.5 %collective-permute-start.21 = (bf16[64,384]{1,0:T(8,128)(2,1)S(1)}, bf16[64,384]{1,0:T(8,128)(2,1)S(1)}, u32[]{:S(2)}, u32[]{:S(2)}) collective-permute-start(bf16[64,384]{1,0:T(8,128)(2,1)S(1)} %get-tuple-element.40), channel_id=1, source_target_pairs={{0,1},{1,0},{2,3},{3,2},{4,5},{5,4},{6,7},{7,6},{8,9},{9,8},{10,11... | collective-permute-start | bytes 147464 | tf_op jit(solution)/shard_map/ppermute | solution.py:392
  40.7 1.0 %project_out.9 = (bf16[64,640]{1,0:T(8,128)(2,1)S(1)}, bf16[64,640]{1,0:T(8,128)(2,1)S(1)}) custom-call(s32[1]{0:T(128)} %bitcast.ids_ref.ids_any, bf16[32,4096]{1,0:T(8,128)(2,1)S(1)} %attend.3.rest_0_, bf16[32,4096]{1,0:T(8,128)(2,1)S(1)} %collective-permute-done.8.rest_1_, bf16[32,4096]{1,0:T(8,128)(2,1)S(1)} %collective-permute-done.9.rest_2_, ...), custom_call_target="tpu_custom_call" | custom-call | flops 2000000000 | bytes 6000000 | tf_op jit(solution)/shard_map/project_out/pallas_call | solution.py:509
  41.7 0.7 %collective-permute-start.18 = (bf16[64,640]{1,0:T(8,128)(2,1)S(1)}, bf16[64,640]{1,0:T(8,128)(2,1)S(1)}, u32[]{:S(2)}, u32[]{:S(2)}) collective-permute-start(bf16[64,640]{1,0:T(8,128)(2,1)S(1)} %get-tuple-element.39), channel_id=1, source_target_pairs={{0,1},{1,0},{2,3},{3,2},{4,5},{5,4},{6,7},{7,6},{8,9},{9,8},{10,11... | collective-permute-start | bytes 245768 | tf_op jit(solution)/shard_map/ppermute | solution.py:392
  42.4 1.0 %project_out.8 = (bf16[64,768]{1,0:T(8,128)(2,1)S(1)}, bf16[64,768]{1,0:T(8,128)(2,1)S(1)}) custom-call(s32[1]{0:T(128)} %bitcast.ids_ref.ids_any, bf16[32,4096]{1,0:T(8,128)(2,1)S(1)} %attend.3.rest_0_, bf16[32,4096]{1,0:T(8,128)(2,1)S(1)} %collective-permute-done.8.rest_1_, bf16[32,4096]{1,0:T(8,128)(2,1)S(1)} %collective-permute-done.9.rest_2_, ...), custom_call_target="tpu_custom_call" | custom-call | flops 2000000000 | bytes 6000000 | tf_op jit(solution)/shard_map/project_out/pallas_call | solution.py:509
  43.5 1.4 %collective-permute-start.15 = (bf16[64,768]{1,0:T(8,128)(2,1)S(1)}, bf16[64,768]{1,0:T(8,128)(2,1)S(1)}, u32[]{:S(2)}, u32[]{:S(2)}) collective-permute-start(bf16[64,768]{1,0:T(8,128)(2,1)S(1)} %get-tuple-element.37), channel_id=1, source_target_pairs={{0,1},{1,0},{2,3},{3,2},{4,5},{5,4},{6,7},{7,6},{8,9},{9,8},{10,11... | collective-permute-start | bytes 294920 | tf_op jit(solution)/shard_map/ppermute | solution.py:392
  44.9 0.7 %collective-permute-start.11 = (bf16[64,640]{1,0:T(8,128)(2,1)S(1)}, bf16[64,640]{1,0:T(8,128)(2,1)S(1)}, u32[]{:S(2)}, u32[]{:S(2)}) collective-permute-start(bf16[64,640]{1,0:T(8,128)(2,1)S(1)} %add_convert_fusion.6.rest_0_), channel_id=1, source_target_pairs={{0,1},{1,0},{2,3},{3,2},{4,5},{5,4},{6,7},{7,6},{8,9},{9,8},{10,11... | collective-permute-start | bytes 245768 | tf_op jit(solution)/shard_map/ppermute | solution.py:392
  45.7 1.4 %collective-permute-start.14 = (bf16[64,1152]{1,0:T(8,128)(2,1)S(1)}, bf16[64,1152]{1,0:T(8,128)(2,1)S(1)}, u32[]{:S(2)}, u32[]{:S(2)}) collective-permute-start(bf16[64,1152]{1,0:T(8,128)(2,1)S(1)} %add_convert_fusion.rest_2_), channel_id=1, source_target_pairs={{0,1},{1,0},{2,3},{3,2},{4,5},{5,4},{6,7},{7,6},{8,9},{9,8},{10,11... | collective-permute-start | bytes 442376 | tf_op jit(solution)/shard_map/ppermute | solution.py:392
  47.2 2.5 %collective-permute-start.22 = (bf16[64,384]{1,0:T(8,128)(2,1)S(1)}, bf16[64,384]{1,0:T(8,128)(2,1)S(1)}, u32[]{:S(2)}, u32[]{:S(2)}) collective-permute-start(bf16[64,384]{1,0:T(8,128)(2,1)S(1)} %add_convert_fusion.9), channel_id=1, source_target_pairs={{0,3},{1,2},{2,1},{3,0},{4,7},{5,6},{6,5},{7,4},{8,11},{9,10},{10,... | collective-permute-start | bytes 147464 | tf_op jit(solution)/shard_map/ppermute | solution.py:392
  49.7 1.5 %collective-permute-start.19 = (bf16[64,640]{1,0:T(8,128)(2,1)S(1)}, bf16[64,640]{1,0:T(8,128)(2,1)S(1)}, u32[]{:S(2)}, u32[]{:S(2)}) collective-permute-start(bf16[64,640]{1,0:T(8,128)(2,1)S(1)} %add_convert_fusion.5), channel_id=1, source_target_pairs={{0,3},{1,2},{2,1},{3,0},{4,7},{5,6},{6,5},{7,4},{8,11},{9,10},{10,... | collective-permute-start | bytes 245768 | tf_op jit(solution)/shard_map/ppermute | solution.py:392
  51.2 4.2 %collective-permute-done.22 = bf16[64,384]{1,0:T(8,128)(2,1)S(1)} collective-permute-done((bf16[64,384]{1,0:T(8,128)(2,1)S(1)}, bf16[64,384]{1,0:T(8,128)(2,1)S(1)}, u32[]{:S(2)}, u32[]{:S(2)}) %collective-permute-start.22) | collective-permute-done | bytes 49184 | tf_op jit(solution)/shard_map/ppermute | solution.py:392
  55.4 0.1 collective-permute-start.23
  55.5 2.3 %collective-permute-start.16 = (bf16[64,768]{1,0:T(8,128)(2,1)S(1)}, bf16[64,768]{1,0:T(8,128)(2,1)S(1)}, u32[]{:S(2)}, u32[]{:S(2)}) collective-permute-start(bf16[64,768]{1,0:T(8,128)(2,1)S(1)} %add_convert_fusion.3), channel_id=1, source_target_pairs={{0,3},{1,2},{2,1},{3,0},{4,7},{5,6},{6,5},{7,4},{8,11},{9,10},{10,... | collective-permute-start | bytes 294920 | tf_op jit(solution)/shard_map/ppermute | solution.py:392
  57.8 1.2 %collective-permute-start.20 = (bf16[64,640]{1,0:T(8,128)(2,1)S(1)}, bf16[64,640]{1,0:T(8,128)(2,1)S(1)}, u32[]{:S(2)}, u32[]{:S(2)}) collective-permute-start(bf16[64,640]{1,0:T(8,128)(2,1)S(1)} %add_convert_fusion.4.rest_6_), channel_id=1, source_target_pairs={{0,1},{1,0},{2,3},{3,2},{4,5},{5,4},{6,7},{7,6},{8,9},{9,8},{10,11... | collective-permute-start | bytes 245768 | tf_op jit(solution)/shard_map/ppermute | solution.py:392
  59.0 3.3 %collective-permute-done.16 = bf16[64,768]{1,0:T(8,128)(2,1)S(1)} collective-permute-done((bf16[64,768]{1,0:T(8,128)(2,1)S(1)}, bf16[64,768]{1,0:T(8,128)(2,1)S(1)}, u32[]{:S(2)}, u32[]{:S(2)}) %collective-permute-start.16) | collective-permute-done | bytes 98336 | tf_op jit(solution)/shard_map/ppermute | solution.py:392
  62.3 1.0 %collective-permute-start.17 = (bf16[64,768]{1,0:T(8,128)(2,1)S(1)}, bf16[64,768]{1,0:T(8,128)(2,1)S(1)}, u32[]{:S(2)}, u32[]{:S(2)}) collective-permute-start(bf16[64,768]{1,0:T(8,128)(2,1)S(1)} %add_convert_fusion.2.rest_4_), channel_id=1, source_target_pairs={{0,1},{1,0},{2,3},{3,2},{4,5},{5,4},{6,7},{7,6},{8,9},{9,8},{10,11... | collective-permute-start | bytes 294920 | tf_op jit(solution)/shard_map/ppermute | solution.py:392
  63.3 1.1 %place_rows.1.pick_ref = bf16[4,64,256]{2,1,0:T(8,128)(2,1)S(1)} custom-call(s32[1]{0:T(128)} %bitcast.ids_ref.ids_any, s32[64]{0:T(128)S(1)} %copy-done.7), custom_call_target="tpu_custom_call" | custom-call | flops 2000000000 | bytes 6000000 | tf_op jit(solution)/shard_map/place_rows/pallas_call | solution.py:416
  64.5 2.5 %collective-permute-done.17.rest_5_ = bf16[64,768]{1,0:T(8,128)(2,1)S(1)} collective-permute-done((bf16[64,768]{1,0:T(8,128)(2,1)S(1)}, bf16[64,768]{1,0:T(8,128)(2,1)S(1)}, u32[]{:S(2)}, u32[]{:S(2)}) %collective-permute-start.17) | collective-permute-done | bytes 98336 | tf_op jit(solution)/shard_map/ppermute | solution.py:392
  67.0 1.4 %order_rows.1 = bf16[4,64,1792]{2,1,0:T(8,128)(2,1)} custom-call(s32[1]{0:T(128)} %bitcast.ids_ref.ids_any, bf16[4,64,256]{2,1,0:T(8,128)(2,1)S(1)} %place_rows.1.pick_ref, bf16[64,640]{1,0:T(8,128)(2,1)S(1)} %add_convert_fusion.6.rest_0_, bf16[64,640]{1,0:T(8,128)(2,1)S(1)} %collective-permute-done.11.rest_1_, ...), custom_call_target="tpu_custom_call" | custom-call | flops 2000000000 | bytes 6000000 | tf_op jit(solution)/shard_map/order_rows/pallas_call | solution.py:486
  (46 shorter events, 0.3 us)
Async XLA Ops:
  0.0 0.7 copy-start.7
  0.0 1.1 %copy-start.3 = (bf16[4,16,32,128]{3,2,1,0:T(8,128)(2,1)S(1)}, bf16[4,16,32,128]{3,2,1,0:T(8,128)(2,1)}, u32[]{:S(2)}) copy-start(bf16[4,16,32,128]{3,2,1,0:T(8,128)(2,1)} %nope_ref.1) | copy-start | bytes 1572868
  0.0 1.2 %copy-start.4 = (bf16[4,16,32,64]{3,2,1,0:T(8,128)(2,1)S(1)}, bf16[4,16,32,64]{3,2,1,0:T(8,128)(2,1)}, u32[]{:S(2)}) copy-start(bf16[4,16,32,64]{3,2,1,0:T(8,128)(2,1)} %rope_ref.1) | copy-start | bytes 786436
  0.0 1.2 %copy-start.5 = (bf16[4,16,576]{2,1,0:T(8,128)(2,1)S(1)}, bf16[4,16,576]{2,1,0:T(8,128)(2,1)}, u32[]{:S(2)}) copy-start(bf16[4,16,576]{2,1,0:T(8,128)(2,1)} %fresh_ref.1) | copy-start | bytes 221188
  0.0 5.5 %copy-start.1 = (bf16[32,128,512]{2,1,0:T(8,128)(2,1)S(1)}, bf16[32,128,512]{2,1,0:T(8,128)(2,1)}, u32[]{:S(2)}) copy-start(bf16[32,128,512]{2,1,0:T(8,128)(2,1)} %rest_3_.3) | copy-start | bytes 12582916
  0.0 5.5 %copy-start.2 = (bf16[32,512,128]{2,1,0:T(8,128)(2,1)S(1)}, bf16[32,512,128]{2,1,0:T(8,128)(2,1)}, u32[]{:S(2)}) copy-start(bf16[32,512,128]{2,1,0:T(8,128)(2,1)} %rest_4_.8) | copy-start | bytes 12582916
  1.2 4.3 %copy-start = (bf16[4096,576]{0,1:T(8,128)(2,1)S(1)}, bf16[4096,576]{0,1:T(8,128)(2,1)}, u32[]{:S(2)}) copy-start(bf16[4096,576]{0,1:T(8,128)(2,1)} %param.9) | copy-start | bytes 14155780
  1.2 4.3 %copy-start.6 = (s32[4,16]{1,0:T(4,128)S(1)}, s32[4,16]{1,0:T(4,128)}, u32[]{:S(2)}) copy-start(s32[4,16]{1,0:T(4,128)} %length_any.3) | copy-start | bytes 772
  2.4 3.2 %collective-permute-start = (bf16[1,848,128]{2,1,0:T(8,128)(2,1)S(1)}, bf16[1,848,128]{2,1,0:T(8,128)(2,1)S(1)}, u32[]{:S(2)}, u32[]{:S(2)}) collective-permute-start(bf16[1,848,128]{2,1,0:T(8,128)(2,1)S(1)} %get-tuple-element.24), channel_id=1, source_target_pairs={{0,4},{4,0},{8,12},{12,8},{1,5},{5,1},{9,13},{13,9},{2,6},{6,2},{1... | collective-permute-start | bytes 651272 | tf_op jit(solution)/shard_map/ppermute | solution.py:392
  2.9 12.9 %collective-permute-start.3 = (bf16[1,848,128]{2,1,0:T(8,128)(2,1)S(1)}, bf16[1,848,128]{2,1,0:T(8,128)(2,1)S(1)}, u32[]{:S(2)}, u32[]{:S(2)}) collective-permute-start(bf16[1,848,128]{2,1,0:T(8,128)(2,1)S(1)} %get-tuple-element.25), channel_id=1, source_target_pairs={{0,8},{4,12},{8,0},{12,4},{1,9},{5,13},{9,1},{13,5},{2,10},{6,14},... | collective-permute-start | bytes 651272 | tf_op jit(solution)/shard_map/ppermute | solution.py:392
  5.5 10.3 %collective-permute-start.4 = (bf16[1,848,128]{2,1,0:T(8,128)(2,1)S(1)}, bf16[1,848,128]{2,1,0:T(8,128)(2,1)S(1)}, u32[]{:S(2)}, u32[]{:S(2)}) collective-permute-start(bf16[1,848,128]{2,1,0:T(8,128)(2,1)S(1)} %get-tuple-element.26), channel_id=1, source_target_pairs={{0,12},{4,8},{8,4},{12,0},{1,13},{5,9},{9,5},{13,1},{2,14},{6,10},... | collective-permute-start | bytes 651272 | tf_op jit(solution)/shard_map/ppermute | solution.py:392
  5.6 20.1 %slice-start = ((s8[14680064]{0:T(1024)(128)(4,1)}), s8[4194304]{0:T(1024)(128)(4,1)S(1)}, s32[]{:S(2)}) async-start(s8[14680064]{0:T(1024)(128)(4,1)} %bitcast.2), calls=%async_computation | async-start | bytes 8388608
  5.6 20.1 %slice-start.1 = ((s8[14680064]{0:T(1024)(128)(4,1)}), s8[4194304]{0:T(1024)(128)(4,1)S(1)}, s32[]{:S(2)}) async-start(s8[14680064]{0:T(1024)(128)(4,1)} %bitcast.2), calls=%async_computation.1 | async-start | bytes 8388608
  12.3 13.4 %slice-start.2 = ((s8[14680064]{0:T(1024)(128)(4,1)}), s8[4194304]{0:T(1024)(128)(4,1)S(1)}, s32[]{:S(2)}) async-start(s8[14680064]{0:T(1024)(128)(4,1)} %bitcast.2), calls=%async_computation.2 | async-start | bytes 8388608
  12.4 13.4 %slice-start.3 = ((s8[14680064]{0:T(1024)(128)(4,1)}), s8[2097152]{0:T(1024)(128)(4,1)S(1)}, s32[]{:S(2)}) async-start(s8[14680064]{0:T(1024)(128)(4,1)} %bitcast.2), calls=%async_computation.3 | async-start | bytes 4194304
  12.4 10.4 %collective-permute-start.2 = (bf16[32,4096]{1,0:T(8,128)(2,1)S(1)}, bf16[32,4096]{1,0:T(8,128)(2,1)S(1)}, u32[]{:S(2)}, u32[]{:S(2)}) collective-permute-start(bf16[32,4096]{1,0:T(8,128)(2,1)S(1)} %attend.2.rest_0_), channel_id=1, source_target_pairs={{0,8},{4,12},{8,0},{12,4},{1,9},{5,13},{9,1},{13,5},{2,10},{6,14},... | collective-permute-start | bytes 786440 | tf_op jit(solution)/shard_map/ppermute | solution.py:392
  15.7 9.9 %collective-permute-start.1 = (bf16[32,4096]{1,0:T(8,128)(2,1)S(1)}, bf16[32,4096]{1,0:T(8,128)(2,1)S(1)}, u32[]{:S(2)}, u32[]{:S(2)}) collective-permute-start(bf16[32,4096]{1,0:T(8,128)(2,1)S(1)} %attend.2.rest_0_), channel_id=1, source_target_pairs={{0,4},{4,0},{8,12},{12,8},{1,5},{5,1},{9,13},{13,9},{2,6},{6,2},{1... | collective-permute-start | bytes 786440 | tf_op jit(solution)/shard_map/ppermute | solution.py:392
  22.7 2.9 %collective-permute-start.5 = (bf16[32,4096]{1,0:T(8,128)(2,1)S(1)}, bf16[32,4096]{1,0:T(8,128)(2,1)S(1)}, u32[]{:S(2)}, u32[]{:S(2)}) collective-permute-start(bf16[32,4096]{1,0:T(8,128)(2,1)S(1)} %collective-permute-done.2.rest_2_), channel_id=1, source_target_pairs={{0,4},{4,0},{8,12},{12,8},{1,5},{5,1},{9,13},{13,9},{2,6},{6,2},{1... | collective-permute-start | bytes 786440 | tf_op jit(solution)/shard_map/ppermute | solution.py:392
  22.9 9.3 %collective-permute-start.9 = (bf16[32,4096]{1,0:T(8,128)(2,1)S(1)}, bf16[32,4096]{1,0:T(8,128)(2,1)S(1)}, u32[]{:S(2)}, u32[]{:S(2)}) collective-permute-start(bf16[32,4096]{1,0:T(8,128)(2,1)S(1)} %attend.3.rest_0_), channel_id=1, source_target_pairs={{0,8},{4,12},{8,0},{12,4},{1,9},{5,13},{9,1},{13,5},{2,10},{6,14},... | collective-permute-start | bytes 786440 | tf_op jit(solution)/shard_map/ppermute | solution.py:392
  25.7 12.9 %collective-permute-start.8 = (bf16[32,4096]{1,0:T(8,128)(2,1)S(1)}, bf16[32,4096]{1,0:T(8,128)(2,1)S(1)}, u32[]{:S(2)}, u32[]{:S(2)}) collective-permute-start(bf16[32,4096]{1,0:T(8,128)(2,1)S(1)} %attend.3.rest_0_), channel_id=1, source_target_pairs={{0,4},{4,0},{8,12},{12,8},{1,5},{5,1},{9,13},{13,9},{2,6},{6,2},{1... | collective-permute-start | bytes 786440 | tf_op jit(solution)/shard_map/ppermute | solution.py:392
  26.7 5.5 %collective-permute-start.6 = (bf16[64,640]{1,0:T(8,128)(2,1)S(1)}, bf16[64,640]{1,0:T(8,128)(2,1)S(1)}, u32[]{:S(2)}, u32[]{:S(2)}) collective-permute-start(bf16[64,640]{1,0:T(8,128)(2,1)S(1)} %get-tuple-element.29), channel_id=1, source_target_pairs={{0,1},{1,0},{2,3},{3,2},{4,5},{5,4},{6,7},{7,6},{8,9},{9,8},{10,11... | collective-permute-start | bytes 245768 | tf_op jit(solution)/shard_map/ppermute | solution.py:392
  29.9 6.0 %collective-permute-start.12 = (bf16[64,1152]{1,0:T(8,128)(2,1)S(1)}, bf16[64,1152]{1,0:T(8,128)(2,1)S(1)}, u32[]{:S(2)}, u32[]{:S(2)}) collective-permute-start(bf16[64,1152]{1,0:T(8,128)(2,1)S(1)} %get-tuple-element.34), channel_id=1, source_target_pairs={{0,1},{1,0},{2,3},{3,2},{4,5},{5,4},{6,7},{7,6},{8,9},{9,8},{10,11... | collective-permute-start | bytes 442376 | tf_op jit(solution)/shard_map/ppermute | solution.py:392
  32.2 6.3 %collective-permute-start.10 = (bf16[32,4096]{1,0:T(8,128)(2,1)S(1)}, bf16[32,4096]{1,0:T(8,128)(2,1)S(1)}, u32[]{:S(2)}, u32[]{:S(2)}) collective-permute-start(bf16[32,4096]{1,0:T(8,128)(2,1)S(1)} %collective-permute-done.9.rest_2_), channel_id=1, source_target_pairs={{0,4},{4,0},{8,12},{12,8},{1,5},{5,1},{9,13},{13,9},{2,6},{6,2},{1... | collective-permute-start | bytes 786440 | tf_op jit(solution)/shard_map/ppermute | solution.py:392
  32.3 12.7 %collective-permute-start.7 = (bf16[64,640]{1,0:T(8,128)(2,1)S(1)}, bf16[64,640]{1,0:T(8,128)(2,1)S(1)}, u32[]{:S(2)}, u32[]{:S(2)}) collective-permute-start(bf16[64,640]{1,0:T(8,128)(2,1)S(1)} %add_convert_fusion.7), channel_id=1, source_target_pairs={{0,3},{1,2},{2,1},{3,0},{4,7},{5,6},{6,5},{7,4},{8,11},{9,10},{10,... | collective-permute-start | bytes 245768 | tf_op jit(solution)/shard_map/ppermute | solution.py:392
  36.0 9.7 %collective-permute-start.13 = (bf16[64,1152]{1,0:T(8,128)(2,1)S(1)}, bf16[64,1152]{1,0:T(8,128)(2,1)S(1)}, u32[]{:S(2)}, u32[]{:S(2)}) collective-permute-start(bf16[64,1152]{1,0:T(8,128)(2,1)S(1)} %add_convert_fusion.1), channel_id=1, source_target_pairs={{0,3},{1,2},{2,1},{3,0},{4,7},{5,6},{6,5},{7,4},{8,11},{9,10},{10,... | collective-permute-start | bytes 442376 | tf_op jit(solution)/shard_map/ppermute | solution.py:392
  39.3 7.9 %collective-permute-start.21 = (bf16[64,384]{1,0:T(8,128)(2,1)S(1)}, bf16[64,384]{1,0:T(8,128)(2,1)S(1)}, u32[]{:S(2)}, u32[]{:S(2)}) collective-permute-start(bf16[64,384]{1,0:T(8,128)(2,1)S(1)} %get-tuple-element.40), channel_id=1, source_target_pairs={{0,1},{1,0},{2,3},{3,2},{4,5},{5,4},{6,7},{7,6},{8,9},{9,8},{10,11... | collective-permute-start | bytes 147464 | tf_op jit(solution)/shard_map/ppermute | solution.py:392
  41.7 7.9 %collective-permute-start.18 = (bf16[64,640]{1,0:T(8,128)(2,1)S(1)}, bf16[64,640]{1,0:T(8,128)(2,1)S(1)}, u32[]{:S(2)}, u32[]{:S(2)}) collective-permute-start(bf16[64,640]{1,0:T(8,128)(2,1)S(1)} %get-tuple-element.39), channel_id=1, source_target_pairs={{0,1},{1,0},{2,3},{3,2},{4,5},{5,4},{6,7},{7,6},{8,9},{9,8},{10,11... | collective-permute-start | bytes 245768 | tf_op jit(solution)/shard_map/ppermute | solution.py:392
  43.5 12.0 %collective-permute-start.15 = (bf16[64,768]{1,0:T(8,128)(2,1)S(1)}, bf16[64,768]{1,0:T(8,128)(2,1)S(1)}, u32[]{:S(2)}, u32[]{:S(2)}) collective-permute-start(bf16[64,768]{1,0:T(8,128)(2,1)S(1)} %get-tuple-element.37), channel_id=1, source_target_pairs={{0,1},{1,0},{2,3},{3,2},{4,5},{5,4},{6,7},{7,6},{8,9},{9,8},{10,11... | collective-permute-start | bytes 294920 | tf_op jit(solution)/shard_map/ppermute | solution.py:392
  44.9 19.5 %collective-permute-start.11 = (bf16[64,640]{1,0:T(8,128)(2,1)S(1)}, bf16[64,640]{1,0:T(8,128)(2,1)S(1)}, u32[]{:S(2)}, u32[]{:S(2)}) collective-permute-start(bf16[64,640]{1,0:T(8,128)(2,1)S(1)} %add_convert_fusion.6.rest_0_), channel_id=1, source_target_pairs={{0,1},{1,0},{2,3},{3,2},{4,5},{5,4},{6,7},{7,6},{8,9},{9,8},{10,11... | collective-permute-start | bytes 245768 | tf_op jit(solution)/shard_map/ppermute | solution.py:392
  45.7 18.7 %collective-permute-start.14 = (bf16[64,1152]{1,0:T(8,128)(2,1)S(1)}, bf16[64,1152]{1,0:T(8,128)(2,1)S(1)}, u32[]{:S(2)}, u32[]{:S(2)}) collective-permute-start(bf16[64,1152]{1,0:T(8,128)(2,1)S(1)} %add_convert_fusion.rest_2_), channel_id=1, source_target_pairs={{0,1},{1,0},{2,3},{3,2},{4,5},{5,4},{6,7},{7,6},{8,9},{9,8},{10,11... | collective-permute-start | bytes 442376 | tf_op jit(solution)/shard_map/ppermute | solution.py:392
  47.2 8.2 %collective-permute-start.22 = (bf16[64,384]{1,0:T(8,128)(2,1)S(1)}, bf16[64,384]{1,0:T(8,128)(2,1)S(1)}, u32[]{:S(2)}, u32[]{:S(2)}) collective-permute-start(bf16[64,384]{1,0:T(8,128)(2,1)S(1)} %add_convert_fusion.9), channel_id=1, source_target_pairs={{0,3},{1,2},{2,1},{3,0},{4,7},{5,6},{6,5},{7,4},{8,11},{9,10},{10,... | collective-permute-start | bytes 147464 | tf_op jit(solution)/shard_map/ppermute | solution.py:392
  49.7 8.1 %collective-permute-start.19 = (bf16[64,640]{1,0:T(8,128)(2,1)S(1)}, bf16[64,640]{1,0:T(8,128)(2,1)S(1)}, u32[]{:S(2)}, u32[]{:S(2)}) collective-permute-start(bf16[64,640]{1,0:T(8,128)(2,1)S(1)} %add_convert_fusion.5), channel_id=1, source_target_pairs={{0,3},{1,2},{2,1},{3,0},{4,7},{5,6},{6,5},{7,4},{8,11},{9,10},{10,... | collective-permute-start | bytes 245768 | tf_op jit(solution)/shard_map/ppermute | solution.py:392
  55.4 9.1 %collective-permute-start.23 = (bf16[64,384]{1,0:T(8,128)(2,1)S(1)}, bf16[64,384]{1,0:T(8,128)(2,1)S(1)}, u32[]{:S(2)}, u32[]{:S(2)}) collective-permute-start(bf16[64,384]{1,0:T(8,128)(2,1)S(1)} %add_convert_fusion.8.rest_8_), channel_id=1, source_target_pairs={{0,1},{1,0},{2,3},{3,2},{4,5},{5,4},{6,7},{7,6},{8,9},{9,8},{10,11... | collective-permute-start | bytes 147464 | tf_op jit(solution)/shard_map/ppermute | solution.py:392
  55.5 6.8 %collective-permute-start.16 = (bf16[64,768]{1,0:T(8,128)(2,1)S(1)}, bf16[64,768]{1,0:T(8,128)(2,1)S(1)}, u32[]{:S(2)}, u32[]{:S(2)}) collective-permute-start(bf16[64,768]{1,0:T(8,128)(2,1)S(1)} %add_convert_fusion.3), channel_id=1, source_target_pairs={{0,3},{1,2},{2,1},{3,0},{4,7},{5,6},{6,5},{7,4},{8,11},{9,10},{10,... | collective-permute-start | bytes 294920 | tf_op jit(solution)/shard_map/ppermute | solution.py:392
  57.8 6.6 %collective-permute-start.20 = (bf16[64,640]{1,0:T(8,128)(2,1)S(1)}, bf16[64,640]{1,0:T(8,128)(2,1)S(1)}, u32[]{:S(2)}, u32[]{:S(2)}) collective-permute-start(bf16[64,640]{1,0:T(8,128)(2,1)S(1)} %add_convert_fusion.4.rest_6_), channel_id=1, source_target_pairs={{0,1},{1,0},{2,3},{3,2},{4,5},{5,4},{6,7},{7,6},{8,9},{9,8},{10,11... | collective-permute-start | bytes 245768 | tf_op jit(solution)/shard_map/ppermute | solution.py:392
  62.3 4.7 %collective-permute-start.17 = (bf16[64,768]{1,0:T(8,128)(2,1)S(1)}, bf16[64,768]{1,0:T(8,128)(2,1)S(1)}, u32[]{:S(2)}, u32[]{:S(2)}) collective-permute-start(bf16[64,768]{1,0:T(8,128)(2,1)S(1)} %add_convert_fusion.2.rest_4_), channel_id=1, source_target_pairs={{0,1},{1,0},{2,3},{3,2},{4,5},{5,4},{6,7},{7,6},{8,9},{9,8},{10,11... | collective-permute-start | bytes 294920 | tf_op jit(solution)/shard_map/ppermute | solution.py:392

commit v17 on v16

--- a/solution.py
+++ b/solution.py
@@ -420,7 +420,7 @@
         out_specs=vmem(),
         scratch_shapes=[pltpu.SMEM((sources,), jnp.int32), pltpu.SMEM((sources * requests,), jnp.int32)],
         compiler_params=limit(12),
-        cost_estimate=cost(2),
+        cost_estimate=cost(0.1),
         name="place_rows",
     )(ids, decode_rows)
 

time: 68 us -> 66.3 us (0.975)
  waiting for transfers between devices: 11.9 us -> 10.2 us
    ppermute x24, waiting for transfers between devices: 11.9 us -> 10.2 us  [flip(): return lax.ppermute(x, axis, [(i, i ^ distance) for i in range(size)])]
    ppermute x24, starting transfers between devices: 32.1 us -> 31.5 us  [flip(): return lax.ppermute(x, axis, [(i, i ^ distance) for i in range(size)])]
  transfers between devices with their start and end apart: 24 -> 24, of which waited for: 4 -> 6; matrix products, arithmetic and copies ran while one was open for 0% -> 0% of each run, Pallas kernels for 29% -> 30%
where the time goes in v17:
time: 66.3 us; the launch traced here: 66 us
  starting transfers between devices  31.5 us (48%)
  Pallas kernels  22.6 us (34%)
  waiting for transfers between devices  10.2 us (15%)
  local copies, waits for them, and re-layouts  1.23 us (2%)
    ppermute x24, starting transfers between devices, flip(): return lax.ppermute(x, axis, [(i, i ^ distance) for i in range(size)])  31.5 us
    pallas_call x2, Pallas kernels, attend(): pl.pallas_call(functools.partial(attend_kernel, sizes, scale, relative, b...  13.6 us
    ppermute x24, waiting for transfers between devices, flip(): return lax.ppermute(x, axis, [(i, i ^ distance) for i in range(size)])  10.2 us
    pallas_call x5, Pallas kernels, project(): pl.pallas_call(functools.partial(project_kernel, first_col), out_shape=[j...  5.29 us
    pallas_call x1, Pallas kernels, order(): pl.pallas_call(kernel, out_shape=jax.ShapeDtypeStruct((steps, sources * r...  1.42 us
  transfers between devices with their start and end apart: 24, of which 6 were waited for; matrix products, arithmetic and copies ran while one was open for 0% of the time, Pallas kernels for 30%

profile of v17, /device:TPU:0, one launch (start us, length us, event | category | flops | bytes accessed | tf_op | source)
XLA Modules:
  0.0 66.0 jit_solution(13844313714217812825)
XLA Ops:
  0.0 0.6 copy-done.7
  0.7 0.4 copy-done.3
  1.1 0.2 copy-done.4
  1.2 1.1 %pack_queries.1 = (bf16[1,848,128]{2,1,0:T(8,128)(2,1)S(1)}, bf16[1,848,128]{2,1,0:T(8,128)(2,1)S(1)}, bf16[1,848,128]{2,1,0:T(8,128)(2,1)S(1)}, bf16[1,848,128]{2,1,0:T(8,128)(2,1)S(1)}) custom-call(s32[1]{0:T(128)} %bitcast.ids_ref.ids_any, s32[64]{0:T(128)S(1)} %copy-done.7, bf16[4,16,32,128]{3,2,1,0:T(8,128)(2,1)S(1)} %copy-done.3, ...), custom_call_target="tpu_custom_call" | custom-call | flops 2000000000 | bytes 6000000 | tf_op jit(solution)/shard_map/pack_queries/pallas_call | solution.py:438
  2.4 0.5 collective-permute-start
  2.9 2.6 %collective-permute-start.3 = (bf16[1,848,128]{2,1,0:T(8,128)(2,1)S(1)}, bf16[1,848,128]{2,1,0:T(8,128)(2,1)S(1)}, u32[]{:S(2)}, u32[]{:S(2)}) collective-permute-start(bf16[1,848,128]{2,1,0:T(8,128)(2,1)S(1)} %get-tuple-element.25), channel_id=1, source_target_pairs={{0,8},{4,12},{8,0},{12,4},{1,9},{5,13},{9,1},{13,5},{2,10},{6,14},... | collective-permute-start | bytes 651272 | tf_op jit(solution)/shard_map/ppermute | solution.py:392
  5.5 0.1 collective-permute-start.4
  5.6 0.0 slice-start
  5.6 0.0 slice-start.1
  5.6 6.7 %attend.2.rest_0_ = bf16[32,4096]{1,0:T(8,128)(2,1)S(1)} custom-call(s32[1]{0:T(128)} %bitcast.ids_ref.ids_any, s32[64]{0:T(128)S(1)} %copy-done.7, s32[4,16]{1,0:T(4,128)S(1)} %copy-done.6, bf16[1,848,128]{2,1,0:T(8,128)(2,1)S(1)} %get-tuple-element.23.rest_0_, bf16[1,848,128]{2,1,0:T(8,128)(2,1)S(1)} %collective-permute-done.rest_1_, ...), custom_call_target="tpu_custom_call" | custom-call | flops 8000000000 | bytes 24000000 | tf_op jit(solution)/shard_map/attend/pallas_call | solution.py:456
  12.3 0.0 slice-start.2
  12.3 2.8 %collective-permute-start.2 = (bf16[32,4096]{1,0:T(8,128)(2,1)S(1)}, bf16[32,4096]{1,0:T(8,128)(2,1)S(1)}, u32[]{:S(2)}, u32[]{:S(2)}) collective-permute-start(bf16[32,4096]{1,0:T(8,128)(2,1)S(1)} %attend.2.rest_0_), channel_id=1, source_target_pairs={{0,8},{4,12},{8,0},{12,4},{1,9},{5,13},{9,1},{13,5},{2,10},{6,14},... | collective-permute-start | bytes 786440 | tf_op jit(solution)/shard_map/ppermute | solution.py:392
  15.2 0.0 collective-permute-start.1
  15.2 0.0 collective-permute-done.3.rest_0_
  15.2 0.6 collective-permute-done.4.rest_1_
  15.8 6.9 %attend.3.rest_0_ = bf16[32,4096]{1,0:T(8,128)(2,1)S(1)} custom-call(s32[1]{0:T(128)} %bitcast.ids_ref.ids_any, s32[64]{0:T(128)S(1)} %copy-done.7, s32[4,16]{1,0:T(4,128)S(1)} %copy-done.6, bf16[1,848,128]{2,1,0:T(8,128)(2,1)S(1)} %collective-permute-done.3.rest_0_, bf16[1,848,128]{2,1,0:T(8,128)(2,1)S(1)} %collective-permute-done.4.rest_1_, ...), custom_call_target="tpu_custom_call" | custom-call | flops 8000000000 | bytes 24000000 | tf_op jit(solution)/shard_map/attend/pallas_call | solution.py:456
  22.7 0.0 collective-permute-done.2.rest_2_
  22.7 0.3 collective-permute-start.5
  23.0 2.4 %collective-permute-start.9 = (bf16[32,4096]{1,0:T(8,128)(2,1)S(1)}, bf16[32,4096]{1,0:T(8,128)(2,1)S(1)}, u32[]{:S(2)}, u32[]{:S(2)}) collective-permute-start(bf16[32,4096]{1,0:T(8,128)(2,1)S(1)} %attend.3.rest_0_), channel_id=1, source_target_pairs={{0,8},{4,12},{8,0},{12,4},{1,9},{5,13},{9,1},{13,5},{2,10},{6,14},... | collective-permute-start | bytes 786440 | tf_op jit(solution)/shard_map/ppermute | solution.py:392
  25.5 1.0 %project_out.5 = (bf16[64,640]{1,0:T(8,128)(2,1)S(1)}, bf16[64,640]{1,0:T(8,128)(2,1)S(1)}) custom-call(s32[1]{0:T(128)} %bitcast.ids_ref.ids_any, bf16[32,4096]{1,0:T(8,128)(2,1)S(1)} %attend.2.rest_0_, bf16[32,4096]{1,0:T(8,128)(2,1)S(1)} %collective-permute-done.1.rest_1_, bf16[32,4096]{1,0:T(8,128)(2,1)S(1)} %collective-permute-done.2.rest_2_, ...), custom_call_target="tpu_custom_call" | custom-call | flops 2000000000 | bytes 6000000 | tf_op jit(solution)/shard_map/project_out/pallas_call | solution.py:509
  26.5 1.6 %collective-permute-start.6 = (bf16[64,640]{1,0:T(8,128)(2,1)S(1)}, bf16[64,640]{1,0:T(8,128)(2,1)S(1)}, u32[]{:S(2)}, u32[]{:S(2)}) collective-permute-start(bf16[64,640]{1,0:T(8,128)(2,1)S(1)} %get-tuple-element.29), channel_id=1, source_target_pairs={{0,1},{1,0},{2,3},{3,2},{4,5},{5,4},{6,7},{7,6},{8,9},{9,8},{10,11... | collective-permute-start | bytes 245768 | tf_op jit(solution)/shard_map/ppermute | solution.py:392
  28.1 1.5 %project_out.7 = (bf16[64,1152]{1,0:T(8,128)(2,1)S(1)}, bf16[64,1152]{1,0:T(8,128)(2,1)S(1)}) custom-call(s32[1]{0:T(128)} %bitcast.ids_ref.ids_any, bf16[32,4096]{1,0:T(8,128)(2,1)S(1)} %attend.2.rest_0_, bf16[32,4096]{1,0:T(8,128)(2,1)S(1)} %collective-permute-done.1.rest_1_, bf16[32,4096]{1,0:T(8,128)(2,1)S(1)} %collective-permute-done.2.rest_2_, ...), custom_call_target="tpu_custom_call" | custom-call | flops 2000000000 | bytes 6000000 | tf_op jit(solution)/shard_map/project_out/pallas_call | solution.py:509
  29.7 0.5 collective-permute-start.12
  30.2 1.8 %collective-permute-done.9.rest_2_ = bf16[32,4096]{1,0:T(8,128)(2,1)S(1)} collective-permute-done((bf16[32,4096]{1,0:T(8,128)(2,1)S(1)}, bf16[32,4096]{1,0:T(8,128)(2,1)S(1)}, u32[]{:S(2)}, u32[]{:S(2)}) %collective-permute-start.9) | collective-permute-done | bytes 262176 | tf_op jit(solution)/shard_map/ppermute | solution.py:392
  32.0 0.0 collective-permute-start.10
  32.0 0.0 collective-permute-done.6
  32.0 3.7 %collective-permute-start.7 = (bf16[64,640]{1,0:T(8,128)(2,1)S(1)}, bf16[64,640]{1,0:T(8,128)(2,1)S(1)}, u32[]{:S(2)}, u32[]{:S(2)}) collective-permute-start(bf16[64,640]{1,0:T(8,128)(2,1)S(1)} %add_convert_fusion.7), channel_id=1, source_target_pairs={{0,3},{1,2},{2,1},{3,0},{4,7},{5,6},{6,5},{7,4},{8,11},{9,10},{10,... | collective-permute-start | bytes 245768 | tf_op jit(solution)/shard_map/ppermute | solution.py:392
  35.7 0.1 collective-permute-done.12
  35.8 2.5 %collective-permute-start.13 = (bf16[64,1152]{1,0:T(8,128)(2,1)S(1)}, bf16[64,1152]{1,0:T(8,128)(2,1)S(1)}, u32[]{:S(2)}, u32[]{:S(2)}) collective-permute-start(bf16[64,1152]{1,0:T(8,128)(2,1)S(1)} %add_convert_fusion.1), channel_id=1, source_target_pairs={{0,3},{1,2},{2,1},{3,0},{4,7},{5,6},{6,5},{7,4},{8,11},{9,10},{10,... | collective-permute-start | bytes 442376 | tf_op jit(solution)/shard_map/ppermute | solution.py:392
  38.3 0.7 %project_out.6 = (bf16[64,384]{1,0:T(8,128)(2,1)S(1)}, bf16[64,384]{1,0:T(8,128)(2,1)S(1)}) custom-call(s32[1]{0:T(128)} %bitcast.ids_ref.ids_any, bf16[32,4096]{1,0:T(8,128)(2,1)S(1)} %attend.3.rest_0_, bf16[32,4096]{1,0:T(8,128)(2,1)S(1)} %collective-permute-done.8.rest_1_, bf16[32,4096]{1,0:T(8,128)(2,1)S(1)} %collective-permute-done.9.rest_2_, ...), custom_call_target="tpu_custom_call" | custom-call | flops 2000000000 | bytes 6000000 | tf_op jit(solution)/shard_map/project_out/pallas_call | solution.py:509
  39.0 1.4 %collective-permute-start.21 = (bf16[64,384]{1,0:T(8,128)(2,1)S(1)}, bf16[64,384]{1,0:T(8,128)(2,1)S(1)}, u32[]{:S(2)}, u32[]{:S(2)}) collective-permute-start(bf16[64,384]{1,0:T(8,128)(2,1)S(1)} %get-tuple-element.40), channel_id=1, source_target_pairs={{0,1},{1,0},{2,3},{3,2},{4,5},{5,4},{6,7},{7,6},{8,9},{9,8},{10,11... | collective-permute-start | bytes 147464 | tf_op jit(solution)/shard_map/ppermute | solution.py:392
  40.5 1.0 %project_out.9 = (bf16[64,640]{1,0:T(8,128)(2,1)S(1)}, bf16[64,640]{1,0:T(8,128)(2,1)S(1)}) custom-call(s32[1]{0:T(128)} %bitcast.ids_ref.ids_any, bf16[32,4096]{1,0:T(8,128)(2,1)S(1)} %attend.3.rest_0_, bf16[32,4096]{1,0:T(8,128)(2,1)S(1)} %collective-permute-done.8.rest_1_, bf16[32,4096]{1,0:T(8,128)(2,1)S(1)} %collective-permute-done.9.rest_2_, ...), custom_call_target="tpu_custom_call" | custom-call | flops 2000000000 | bytes 6000000 | tf_op jit(solution)/shard_map/project_out/pallas_call | solution.py:509
  41.5 0.7 %collective-permute-start.18 = (bf16[64,640]{1,0:T(8,128)(2,1)S(1)}, bf16[64,640]{1,0:T(8,128)(2,1)S(1)}, u32[]{:S(2)}, u32[]{:S(2)}) collective-permute-start(bf16[64,640]{1,0:T(8,128)(2,1)S(1)} %get-tuple-element.39), channel_id=1, source_target_pairs={{0,1},{1,0},{2,3},{3,2},{4,5},{5,4},{6,7},{7,6},{8,9},{9,8},{10,11... | collective-permute-start | bytes 245768 | tf_op jit(solution)/shard_map/ppermute | solution.py:392
  42.2 1.0 %project_out.8 = (bf16[64,768]{1,0:T(8,128)(2,1)S(1)}, bf16[64,768]{1,0:T(8,128)(2,1)S(1)}) custom-call(s32[1]{0:T(128)} %bitcast.ids_ref.ids_any, bf16[32,4096]{1,0:T(8,128)(2,1)S(1)} %attend.3.rest_0_, bf16[32,4096]{1,0:T(8,128)(2,1)S(1)} %collective-permute-done.8.rest_1_, bf16[32,4096]{1,0:T(8,128)(2,1)S(1)} %collective-permute-done.9.rest_2_, ...), custom_call_target="tpu_custom_call" | custom-call | flops 2000000000 | bytes 6000000 | tf_op jit(solution)/shard_map/project_out/pallas_call | solution.py:509
  43.2 1.4 %collective-permute-start.15 = (bf16[64,768]{1,0:T(8,128)(2,1)S(1)}, bf16[64,768]{1,0:T(8,128)(2,1)S(1)}, u32[]{:S(2)}, u32[]{:S(2)}) collective-permute-start(bf16[64,768]{1,0:T(8,128)(2,1)S(1)} %get-tuple-element.37), channel_id=1, source_target_pairs={{0,1},{1,0},{2,3},{3,2},{4,5},{5,4},{6,7},{7,6},{8,9},{9,8},{10,11... | collective-permute-start | bytes 294920 | tf_op jit(solution)/shard_map/ppermute | solution.py:392
  44.7 0.7 %collective-permute-start.11 = (bf16[64,640]{1,0:T(8,128)(2,1)S(1)}, bf16[64,640]{1,0:T(8,128)(2,1)S(1)}, u32[]{:S(2)}, u32[]{:S(2)}) collective-permute-start(bf16[64,640]{1,0:T(8,128)(2,1)S(1)} %add_convert_fusion.6.rest_0_), channel_id=1, source_target_pairs={{0,1},{1,0},{2,3},{3,2},{4,5},{5,4},{6,7},{7,6},{8,9},{9,8},{10,11... | collective-permute-start | bytes 245768 | tf_op jit(solution)/shard_map/ppermute | solution.py:392
  45.5 1.4 %collective-permute-start.14 = (bf16[64,1152]{1,0:T(8,128)(2,1)S(1)}, bf16[64,1152]{1,0:T(8,128)(2,1)S(1)}, u32[]{:S(2)}, u32[]{:S(2)}) collective-permute-start(bf16[64,1152]{1,0:T(8,128)(2,1)S(1)} %add_convert_fusion.rest_2_), channel_id=1, source_target_pairs={{0,1},{1,0},{2,3},{3,2},{4,5},{5,4},{6,7},{7,6},{8,9},{9,8},{10,11... | collective-permute-start | bytes 442376 | tf_op jit(solution)/shard_map/ppermute | solution.py:392
  46.9 2.5 %collective-permute-start.22 = (bf16[64,384]{1,0:T(8,128)(2,1)S(1)}, bf16[64,384]{1,0:T(8,128)(2,1)S(1)}, u32[]{:S(2)}, u32[]{:S(2)}) collective-permute-start(bf16[64,384]{1,0:T(8,128)(2,1)S(1)} %add_convert_fusion.9), channel_id=1, source_target_pairs={{0,3},{1,2},{2,1},{3,0},{4,7},{5,6},{6,5},{7,4},{8,11},{9,10},{10,... | collective-permute-start | bytes 147464 | tf_op jit(solution)/shard_map/ppermute | solution.py:392
  49.4 1.5 %collective-permute-start.19 = (bf16[64,640]{1,0:T(8,128)(2,1)S(1)}, bf16[64,640]{1,0:T(8,128)(2,1)S(1)}, u32[]{:S(2)}, u32[]{:S(2)}) collective-permute-start(bf16[64,640]{1,0:T(8,128)(2,1)S(1)} %add_convert_fusion.5), channel_id=1, source_target_pairs={{0,3},{1,2},{2,1},{3,0},{4,7},{5,6},{6,5},{7,4},{8,11},{9,10},{10,... | collective-permute-start | bytes 245768 | tf_op jit(solution)/shard_map/ppermute | solution.py:392
  50.9 2.5 %collective-permute-start.16 = (bf16[64,768]{1,0:T(8,128)(2,1)S(1)}, bf16[64,768]{1,0:T(8,128)(2,1)S(1)}, u32[]{:S(2)}, u32[]{:S(2)}) collective-permute-start(bf16[64,768]{1,0:T(8,128)(2,1)S(1)} %add_convert_fusion.3), channel_id=1, source_target_pairs={{0,3},{1,2},{2,1},{3,0},{4,7},{5,6},{6,5},{7,4},{8,11},{9,10},{10,... | collective-permute-start | bytes 294920 | tf_op jit(solution)/shard_map/ppermute | solution.py:392
  53.4 3.5 %collective-permute-done.19 = bf16[64,640]{1,0:T(8,128)(2,1)S(1)} collective-permute-done((bf16[64,640]{1,0:T(8,128)(2,1)S(1)}, bf16[64,640]{1,0:T(8,128)(2,1)S(1)}, u32[]{:S(2)}, u32[]{:S(2)}) %collective-permute-start.19) | collective-permute-done | bytes 81952 | tf_op jit(solution)/shard_map/ppermute | solution.py:392
  56.9 0.1 collective-permute-start.20
  57.0 1.9 %collective-permute-done.16 = bf16[64,768]{1,0:T(8,128)(2,1)S(1)} collective-permute-done((bf16[64,768]{1,0:T(8,128)(2,1)S(1)}, bf16[64,768]{1,0:T(8,128)(2,1)S(1)}, u32[]{:S(2)}, u32[]{:S(2)}) %collective-permute-start.16) | collective-permute-done | bytes 98336 | tf_op jit(solution)/shard_map/ppermute | solution.py:392
  59.0 1.4 %collective-permute-start.17 = (bf16[64,768]{1,0:T(8,128)(2,1)S(1)}, bf16[64,768]{1,0:T(8,128)(2,1)S(1)}, u32[]{:S(2)}, u32[]{:S(2)}) collective-permute-start(bf16[64,768]{1,0:T(8,128)(2,1)S(1)} %add_convert_fusion.2.rest_4_), channel_id=1, source_target_pairs={{0,1},{1,0},{2,3},{3,2},{4,5},{5,4},{6,7},{7,6},{8,9},{9,8},{10,11... | collective-permute-start | bytes 294920 | tf_op jit(solution)/shard_map/ppermute | solution.py:392
  60.4 0.8 %collective-permute-start.23 = (bf16[64,384]{1,0:T(8,128)(2,1)S(1)}, bf16[64,384]{1,0:T(8,128)(2,1)S(1)}, u32[]{:S(2)}, u32[]{:S(2)}) collective-permute-start(bf16[64,384]{1,0:T(8,128)(2,1)S(1)} %add_convert_fusion.8.rest_8_), channel_id=1, source_target_pairs={{0,1},{1,0},{2,3},{3,2},{4,5},{5,4},{6,7},{7,6},{8,9},{9,8},{10,11... | collective-permute-start | bytes 147464 | tf_op jit(solution)/shard_map/ppermute | solution.py:392
  61.2 1.1 %place_rows.1.pick_ref = bf16[4,64,256]{2,1,0:T(8,128)(2,1)S(1)} custom-call(s32[1]{0:T(128)} %bitcast.ids_ref.ids_any, s32[64]{0:T(128)S(1)} %copy-done.7), custom_call_target="tpu_custom_call" | custom-call | flops 100000000 | bytes 300000 | tf_op jit(solution)/shard_map/place_rows/pallas_call | solution.py:416
  62.3 2.3 %collective-permute-done.23.rest_9_ = bf16[64,384]{1,0:T(8,128)(2,1)S(1)} collective-permute-done((bf16[64,384]{1,0:T(8,128)(2,1)S(1)}, bf16[64,384]{1,0:T(8,128)(2,1)S(1)}, u32[]{:S(2)}, u32[]{:S(2)}) %collective-permute-start.23) | collective-permute-done | bytes 49184 | tf_op jit(solution)/shard_map/ppermute | solution.py:392
  64.6 1.4 %order_rows.1 = bf16[4,64,1792]{2,1,0:T(8,128)(2,1)} custom-call(s32[1]{0:T(128)} %bitcast.ids_ref.ids_any, bf16[4,64,256]{2,1,0:T(8,128)(2,1)S(1)} %place_rows.1.pick_ref, bf16[64,640]{1,0:T(8,128)(2,1)S(1)} %add_convert_fusion.6.rest_0_, bf16[64,640]{1,0:T(8,128)(2,1)S(1)} %collective-permute-done.11.rest_1_, ...), custom_call_target="tpu_custom_call" | custom-call | flops 2000000000 | bytes 6000000 | tf_op jit(solution)/shard_map/order_rows/pallas_call | solution.py:486
  (46 shorter events, 0.3 us)
Async XLA Ops:
  0.0 0.7 copy-start.7
  0.0 1.1 %copy-start.3 = (bf16[4,16,32,128]{3,2,1,0:T(8,128)(2,1)S(1)}, bf16[4,16,32,128]{3,2,1,0:T(8,128)(2,1)}, u32[]{:S(2)}) copy-start(bf16[4,16,32,128]{3,2,1,0:T(8,128)(2,1)} %nope_ref.1) | copy-start | bytes 1572868
  0.0 1.2 %copy-start.4 = (bf16[4,16,32,64]{3,2,1,0:T(8,128)(2,1)S(1)}, bf16[4,16,32,64]{3,2,1,0:T(8,128)(2,1)}, u32[]{:S(2)}) copy-start(bf16[4,16,32,64]{3,2,1,0:T(8,128)(2,1)} %rope_ref.1) | copy-start | bytes 786436
  0.0 1.2 %copy-start.5 = (bf16[4,16,576]{2,1,0:T(8,128)(2,1)S(1)}, bf16[4,16,576]{2,1,0:T(8,128)(2,1)}, u32[]{:S(2)}) copy-start(bf16[4,16,576]{2,1,0:T(8,128)(2,1)} %fresh_ref.1) | copy-start | bytes 221188
  0.0 5.5 %copy-start.1 = (bf16[32,128,512]{2,1,0:T(8,128)(2,1)S(1)}, bf16[32,128,512]{2,1,0:T(8,128)(2,1)}, u32[]{:S(2)}) copy-start(bf16[32,128,512]{2,1,0:T(8,128)(2,1)} %rest_3_.3) | copy-start | bytes 12582916
  0.0 5.5 %copy-start.2 = (bf16[32,512,128]{2,1,0:T(8,128)(2,1)S(1)}, bf16[32,512,128]{2,1,0:T(8,128)(2,1)}, u32[]{:S(2)}) copy-start(bf16[32,512,128]{2,1,0:T(8,128)(2,1)} %rest_4_.8) | copy-start | bytes 12582916
  1.2 4.3 %copy-start = (bf16[4096,576]{0,1:T(8,128)(2,1)S(1)}, bf16[4096,576]{0,1:T(8,128)(2,1)}, u32[]{:S(2)}) copy-start(bf16[4096,576]{0,1:T(8,128)(2,1)} %param.9) | copy-start | bytes 14155780
  1.2 4.3 %copy-start.6 = (s32[4,16]{1,0:T(4,128)S(1)}, s32[4,16]{1,0:T(4,128)}, u32[]{:S(2)}) copy-start(s32[4,16]{1,0:T(4,128)} %length_any.3) | copy-start | bytes 772
  2.4 3.2 %collective-permute-start = (bf16[1,848,128]{2,1,0:T(8,128)(2,1)S(1)}, bf16[1,848,128]{2,1,0:T(8,128)(2,1)S(1)}, u32[]{:S(2)}, u32[]{:S(2)}) collective-permute-start(bf16[1,848,128]{2,1,0:T(8,128)(2,1)S(1)} %get-tuple-element.24), channel_id=1, source_target_pairs={{0,4},{4,0},{8,12},{12,8},{1,5},{5,1},{9,13},{13,9},{2,6},{6,2},{1... | collective-permute-start | bytes 651272 | tf_op jit(solution)/shard_map/ppermute | solution.py:392
  2.9 12.3 %collective-permute-start.3 = (bf16[1,848,128]{2,1,0:T(8,128)(2,1)S(1)}, bf16[1,848,128]{2,1,0:T(8,128)(2,1)S(1)}, u32[]{:S(2)}, u32[]{:S(2)}) collective-permute-start(bf16[1,848,128]{2,1,0:T(8,128)(2,1)S(1)} %get-tuple-element.25), channel_id=1, source_target_pairs={{0,8},{4,12},{8,0},{12,4},{1,9},{5,13},{9,1},{13,5},{2,10},{6,14},... | collective-permute-start | bytes 651272 | tf_op jit(solution)/shard_map/ppermute | solution.py:392
  5.5 10.3 %collective-permute-start.4 = (bf16[1,848,128]{2,1,0:T(8,128)(2,1)S(1)}, bf16[1,848,128]{2,1,0:T(8,128)(2,1)S(1)}, u32[]{:S(2)}, u32[]{:S(2)}) collective-permute-start(bf16[1,848,128]{2,1,0:T(8,128)(2,1)S(1)} %get-tuple-element.26), channel_id=1, source_target_pairs={{0,12},{4,8},{8,4},{12,0},{1,13},{5,9},{9,5},{13,1},{2,14},{6,10},... | collective-permute-start | bytes 651272 | tf_op jit(solution)/shard_map/ppermute | solution.py:392
  5.6 19.8 %slice-start = ((s8[14680064]{0:T(1024)(128)(4,1)}), s8[4194304]{0:T(1024)(128)(4,1)S(1)}, s32[]{:S(2)}) async-start(s8[14680064]{0:T(1024)(128)(4,1)} %bitcast.2), calls=%async_computation | async-start | bytes 8388608
  5.6 19.8 %slice-start.1 = ((s8[14680064]{0:T(1024)(128)(4,1)}), s8[4194304]{0:T(1024)(128)(4,1)S(1)}, s32[]{:S(2)}) async-start(s8[14680064]{0:T(1024)(128)(4,1)} %bitcast.2), calls=%async_computation.1 | async-start | bytes 8388608
  12.3 13.1 %slice-start.2 = ((s8[14680064]{0:T(1024)(128)(4,1)}), s8[4194304]{0:T(1024)(128)(4,1)S(1)}, s32[]{:S(2)}) async-start(s8[14680064]{0:T(1024)(128)(4,1)} %bitcast.2), calls=%async_computation.2 | async-start | bytes 8388608
  12.3 13.1 %slice-start.3 = ((s8[14680064]{0:T(1024)(128)(4,1)}), s8[2097152]{0:T(1024)(128)(4,1)S(1)}, s32[]{:S(2)}) async-start(s8[14680064]{0:T(1024)(128)(4,1)} %bitcast.2), calls=%async_computation.3 | async-start | bytes 4194304
  12.3 10.4 %collective-permute-start.2 = (bf16[32,4096]{1,0:T(8,128)(2,1)S(1)}, bf16[32,4096]{1,0:T(8,128)(2,1)S(1)}, u32[]{:S(2)}, u32[]{:S(2)}) collective-permute-start(bf16[32,4096]{1,0:T(8,128)(2,1)S(1)} %attend.2.rest_0_), channel_id=1, source_target_pairs={{0,8},{4,12},{8,0},{12,4},{1,9},{5,13},{9,1},{13,5},{2,10},{6,14},... | collective-permute-start | bytes 786440 | tf_op jit(solution)/shard_map/ppermute | solution.py:392
  15.2 10.2 %collective-permute-start.1 = (bf16[32,4096]{1,0:T(8,128)(2,1)S(1)}, bf16[32,4096]{1,0:T(8,128)(2,1)S(1)}, u32[]{:S(2)}, u32[]{:S(2)}) collective-permute-start(bf16[32,4096]{1,0:T(8,128)(2,1)S(1)} %attend.2.rest_0_), channel_id=1, source_target_pairs={{0,4},{4,0},{8,12},{12,8},{1,5},{5,1},{9,13},{13,9},{2,6},{6,2},{1... | collective-permute-start | bytes 786440 | tf_op jit(solution)/shard_map/ppermute | solution.py:392
  22.7 2.7 %collective-permute-start.5 = (bf16[32,4096]{1,0:T(8,128)(2,1)S(1)}, bf16[32,4096]{1,0:T(8,128)(2,1)S(1)}, u32[]{:S(2)}, u32[]{:S(2)}) collective-permute-start(bf16[32,4096]{1,0:T(8,128)(2,1)S(1)} %collective-permute-done.2.rest_2_), channel_id=1, source_target_pairs={{0,4},{4,0},{8,12},{12,8},{1,5},{5,1},{9,13},{13,9},{2,6},{6,2},{1... | collective-permute-start | bytes 786440 | tf_op jit(solution)/shard_map/ppermute | solution.py:392
  23.0 8.9 %collective-permute-start.9 = (bf16[32,4096]{1,0:T(8,128)(2,1)S(1)}, bf16[32,4096]{1,0:T(8,128)(2,1)S(1)}, u32[]{:S(2)}, u32[]{:S(2)}) collective-permute-start(bf16[32,4096]{1,0:T(8,128)(2,1)S(1)} %attend.3.rest_0_), channel_id=1, source_target_pairs={{0,8},{4,12},{8,0},{12,4},{1,9},{5,13},{9,1},{13,5},{2,10},{6,14},... | collective-permute-start | bytes 786440 | tf_op jit(solution)/shard_map/ppermute | solution.py:392
  25.4 12.9 %collective-permute-start.8 = (bf16[32,4096]{1,0:T(8,128)(2,1)S(1)}, bf16[32,4096]{1,0:T(8,128)(2,1)S(1)}, u32[]{:S(2)}, u32[]{:S(2)}) collective-permute-start(bf16[32,4096]{1,0:T(8,128)(2,1)S(1)} %attend.3.rest_0_), channel_id=1, source_target_pairs={{0,4},{4,0},{8,12},{12,8},{1,5},{5,1},{9,13},{13,9},{2,6},{6,2},{1... | collective-permute-start | bytes 786440 | tf_op jit(solution)/shard_map/ppermute | solution.py:392
  26.5 5.5 %collective-permute-start.6 = (bf16[64,640]{1,0:T(8,128)(2,1)S(1)}, bf16[64,640]{1,0:T(8,128)(2,1)S(1)}, u32[]{:S(2)}, u32[]{:S(2)}) collective-permute-start(bf16[64,640]{1,0:T(8,128)(2,1)S(1)} %get-tuple-element.29), channel_id=1, source_target_pairs={{0,1},{1,0},{2,3},{3,2},{4,5},{5,4},{6,7},{7,6},{8,9},{9,8},{10,11... | collective-permute-start | bytes 245768 | tf_op jit(solution)/shard_map/ppermute | solution.py:392
  29.7 6.0 %collective-permute-start.12 = (bf16[64,1152]{1,0:T(8,128)(2,1)S(1)}, bf16[64,1152]{1,0:T(8,128)(2,1)S(1)}, u32[]{:S(2)}, u32[]{:S(2)}) collective-permute-start(bf16[64,1152]{1,0:T(8,128)(2,1)S(1)} %get-tuple-element.34), channel_id=1, source_target_pairs={{0,1},{1,0},{2,3},{3,2},{4,5},{5,4},{6,7},{7,6},{8,9},{9,8},{10,11... | collective-permute-start | bytes 442376 | tf_op jit(solution)/shard_map/ppermute | solution.py:392
  32.0 6.3 %collective-permute-start.10 = (bf16[32,4096]{1,0:T(8,128)(2,1)S(1)}, bf16[32,4096]{1,0:T(8,128)(2,1)S(1)}, u32[]{:S(2)}, u32[]{:S(2)}) collective-permute-start(bf16[32,4096]{1,0:T(8,128)(2,1)S(1)} %collective-permute-done.9.rest_2_), channel_id=1, source_target_pairs={{0,4},{4,0},{8,12},{12,8},{1,5},{5,1},{9,13},{13,9},{2,6},{6,2},{1... | collective-permute-start | bytes 786440 | tf_op jit(solution)/shard_map/ppermute | solution.py:392
  32.0 12.7 %collective-permute-start.7 = (bf16[64,640]{1,0:T(8,128)(2,1)S(1)}, bf16[64,640]{1,0:T(8,128)(2,1)S(1)}, u32[]{:S(2)}, u32[]{:S(2)}) collective-permute-start(bf16[64,640]{1,0:T(8,128)(2,1)S(1)} %add_convert_fusion.7), channel_id=1, source_target_pairs={{0,3},{1,2},{2,1},{3,0},{4,7},{5,6},{6,5},{7,4},{8,11},{9,10},{10,... | collective-permute-start | bytes 245768 | tf_op jit(solution)/shard_map/ppermute | solution.py:392
  35.8 9.7 %collective-permute-start.13 = (bf16[64,1152]{1,0:T(8,128)(2,1)S(1)}, bf16[64,1152]{1,0:T(8,128)(2,1)S(1)}, u32[]{:S(2)}, u32[]{:S(2)}) collective-permute-start(bf16[64,1152]{1,0:T(8,128)(2,1)S(1)} %add_convert_fusion.1), channel_id=1, source_target_pairs={{0,3},{1,2},{2,1},{3,0},{4,7},{5,6},{6,5},{7,4},{8,11},{9,10},{10,... | collective-permute-start | bytes 442376 | tf_op jit(solution)/shard_map/ppermute | solution.py:392
  39.0 7.9 %collective-permute-start.21 = (bf16[64,384]{1,0:T(8,128)(2,1)S(1)}, bf16[64,384]{1,0:T(8,128)(2,1)S(1)}, u32[]{:S(2)}, u32[]{:S(2)}) collective-permute-start(bf16[64,384]{1,0:T(8,128)(2,1)S(1)} %get-tuple-element.40), channel_id=1, source_target_pairs={{0,1},{1,0},{2,3},{3,2},{4,5},{5,4},{6,7},{7,6},{8,9},{9,8},{10,11... | collective-permute-start | bytes 147464 | tf_op jit(solution)/shard_map/ppermute | solution.py:392
  41.5 7.9 %collective-permute-start.18 = (bf16[64,640]{1,0:T(8,128)(2,1)S(1)}, bf16[64,640]{1,0:T(8,128)(2,1)S(1)}, u32[]{:S(2)}, u32[]{:S(2)}) collective-permute-start(bf16[64,640]{1,0:T(8,128)(2,1)S(1)} %get-tuple-element.39), channel_id=1, source_target_pairs={{0,1},{1,0},{2,3},{3,2},{4,5},{5,4},{6,7},{7,6},{8,9},{9,8},{10,11... | collective-permute-start | bytes 245768 | tf_op jit(solution)/shard_map/ppermute | solution.py:392
  43.2 7.7 %collective-permute-start.15 = (bf16[64,768]{1,0:T(8,128)(2,1)S(1)}, bf16[64,768]{1,0:T(8,128)(2,1)S(1)}, u32[]{:S(2)}, u32[]{:S(2)}) collective-permute-start(bf16[64,768]{1,0:T(8,128)(2,1)S(1)} %get-tuple-element.37), channel_id=1, source_target_pairs={{0,1},{1,0},{2,3},{3,2},{4,5},{5,4},{6,7},{7,6},{8,9},{9,8},{10,11... | collective-permute-start | bytes 294920 | tf_op jit(solution)/shard_map/ppermute | solution.py:392
  44.7 17.6 %collective-permute-start.11 = (bf16[64,640]{1,0:T(8,128)(2,1)S(1)}, bf16[64,640]{1,0:T(8,128)(2,1)S(1)}, u32[]{:S(2)}, u32[]{:S(2)}) collective-permute-start(bf16[64,640]{1,0:T(8,128)(2,1)S(1)} %add_convert_fusion.6.rest_0_), channel_id=1, source_target_pairs={{0,1},{1,0},{2,3},{3,2},{4,5},{5,4},{6,7},{7,6},{8,9},{9,8},{10,11... | collective-permute-start | bytes 245768 | tf_op jit(solution)/shard_map/ppermute | solution.py:392
  45.5 19.1 %collective-permute-start.14 = (bf16[64,1152]{1,0:T(8,128)(2,1)S(1)}, bf16[64,1152]{1,0:T(8,128)(2,1)S(1)}, u32[]{:S(2)}, u32[]{:S(2)}) collective-permute-start(bf16[64,1152]{1,0:T(8,128)(2,1)S(1)} %add_convert_fusion.rest_2_), channel_id=1, source_target_pairs={{0,1},{1,0},{2,3},{3,2},{4,5},{5,4},{6,7},{7,6},{8,9},{9,8},{10,11... | collective-permute-start | bytes 442376 | tf_op jit(solution)/shard_map/ppermute | solution.py:392
  46.9 13.4 %collective-permute-start.22 = (bf16[64,384]{1,0:T(8,128)(2,1)S(1)}, bf16[64,384]{1,0:T(8,128)(2,1)S(1)}, u32[]{:S(2)}, u32[]{:S(2)}) collective-permute-start(bf16[64,384]{1,0:T(8,128)(2,1)S(1)} %add_convert_fusion.9), channel_id=1, source_target_pairs={{0,3},{1,2},{2,1},{3,0},{4,7},{5,6},{6,5},{7,4},{8,11},{9,10},{10,... | collective-permute-start | bytes 147464 | tf_op jit(solution)/shard_map/ppermute | solution.py:392
  49.4 7.5 %collective-permute-start.19 = (bf16[64,640]{1,0:T(8,128)(2,1)S(1)}, bf16[64,640]{1,0:T(8,128)(2,1)S(1)}, u32[]{:S(2)}, u32[]{:S(2)}) collective-permute-start(bf16[64,640]{1,0:T(8,128)(2,1)S(1)} %add_convert_fusion.5), channel_id=1, source_target_pairs={{0,3},{1,2},{2,1},{3,0},{4,7},{5,6},{6,5},{7,4},{8,11},{9,10},{10,... | collective-permute-start | bytes 245768 | tf_op jit(solution)/shard_map/ppermute | solution.py:392
  50.9 8.0 %collective-permute-start.16 = (bf16[64,768]{1,0:T(8,128)(2,1)S(1)}, bf16[64,768]{1,0:T(8,128)(2,1)S(1)}, u32[]{:S(2)}, u32[]{:S(2)}) collective-permute-start(bf16[64,768]{1,0:T(8,128)(2,1)S(1)} %add_convert_fusion.3), channel_id=1, source_target_pairs={{0,3},{1,2},{2,1},{3,0},{4,7},{5,6},{6,5},{7,4},{8,11},{9,10},{10,... | collective-permute-start | bytes 294920 | tf_op jit(solution)/shard_map/ppermute | solution.py:392
  56.9 7.7 %collective-permute-start.20 = (bf16[64,640]{1,0:T(8,128)(2,1)S(1)}, bf16[64,640]{1,0:T(8,128)(2,1)S(1)}, u32[]{:S(2)}, u32[]{:S(2)}) collective-permute-start(bf16[64,640]{1,0:T(8,128)(2,1)S(1)} %add_convert_fusion.4.rest_6_), channel_id=1, source_target_pairs={{0,1},{1,0},{2,3},{3,2},{4,5},{5,4},{6,7},{7,6},{8,9},{9,8},{10,11... | collective-permute-start | bytes 245768 | tf_op jit(solution)/shard_map/ppermute | solution.py:392
  59.0 5.6 %collective-permute-start.17 = (bf16[64,768]{1,0:T(8,128)(2,1)S(1)}, bf16[64,768]{1,0:T(8,128)(2,1)S(1)}, u32[]{:S(2)}, u32[]{:S(2)}) collective-permute-start(bf16[64,768]{1,0:T(8,128)(2,1)S(1)} %add_convert_fusion.2.rest_4_), channel_id=1, source_target_pairs={{0,1},{1,0},{2,3},{3,2},{4,5},{5,4},{6,7},{7,6},{8,9},{9,8},{10,11... | collective-permute-start | bytes 294920 | tf_op jit(solution)/shard_map/ppermute | solution.py:392
  60.4 4.2 %collective-permute-start.23 = (bf16[64,384]{1,0:T(8,128)(2,1)S(1)}, bf16[64,384]{1,0:T(8,128)(2,1)S(1)}, u32[]{:S(2)}, u32[]{:S(2)}) collective-permute-start(bf16[64,384]{1,0:T(8,128)(2,1)S(1)} %add_convert_fusion.8.rest_8_), channel_id=1, source_target_pairs={{0,1},{1,0},{2,3},{3,2},{4,5},{5,4},{6,7},{7,6},{8,9},{9,8},{10,11... | collective-permute-start | bytes 147464 | tf_op jit(solution)/shard_map/ppermute | solution.py:392

commit v18 on v17

--- a/solution.py
+++ b/solution.py
@@ -543,7 +543,8 @@
 
     near_made = cut(near, 0, (5, 9))
     pairs = [add(near_made[0][2], near_made[0][3])]
-    far = [far_rows, flip(far_rows, "seq", 1), far_across, flip(far_across, "seq", 1)]
+    relayed = after(far_across, pairs[0])
+    far = [far_rows, flip(far_rows, "seq", 1), far_across, flip(relayed, "seq", 1)]
     far_made = cut(far, half, (6, 5, 3))
     made = near_made + far_made
     for i, (_, _, keep, incoming) in enumerate(made[1:], 1):
@@ -553,7 +554,7 @@
     arrays = []
     for i, (pair, cross) in enumerate(zip(pairs, crossed)):
         if i < len(near_made):
-            cross = after(cross, *(last_made,))
+            cross = after(cross, *(pairs[len(near_made)],))
         total = add(pair, cross)
         arrays += [total, flip(total, "head", 1)]
     layout = tuple((row, col) for row, col, _, _ in made)

time: 66.3 us -> 66.7 us (level)
  transfers between devices with their start and end apart: 24 -> 24, of which waited for: 6 -> 7; matrix products, arithmetic and copies ran while one was open for 0% -> 0% of each run, Pallas kernels for 30% -> 31%
where the time goes in v18:
time: 66.7 us; the launch traced here: 66.8 us
  starting transfers between devices  31.9 us (48%)
  Pallas kernels  23.2 us (35%)
  waiting for transfers between devices  9.82 us (15%)
  local copies, waits for them, and re-layouts  1.27 us (2%)
    ppermute x24, starting transfers between devices, flip(): return lax.ppermute(x, axis, [(i, i ^ distance) for i in range(size)])  31.9 us
    pallas_call x2, Pallas kernels, attend(): pl.pallas_call(functools.partial(attend_kernel, sizes, scale, relative, b...  14.3 us
    ppermute x24, waiting for transfers between devices, flip(): return lax.ppermute(x, axis, [(i, i ^ distance) for i in range(size)])  9.82 us
    pallas_call x5, Pallas kernels, project(): pl.pallas_call(functools.partial(project_kernel, first_col), out_shape=[j...  5.3 us
    pallas_call x1, Pallas kernels, order(): pl.pallas_call(kernel, out_shape=jax.ShapeDtypeStruct((steps, sources * r...  1.42 us
  transfers between devices with their start and end apart: 24, of which 7 were waited for; matrix products, arithmetic and copies ran while one was open for 0% of the time, Pallas kernels for 31%

profile of v18, /device:TPU:0, one launch (start us, length us, event | category | flops | bytes accessed | tf_op | source)
XLA Modules:
  0.0 66.8 jit_solution(9915797556770621966)
XLA Ops:
  0.0 0.6 copy-done.7
  0.7 0.2 copy-done.5
  0.9 0.2 copy-done.4
  1.1 0.2 copy-done.3
  1.3 1.1 %pack_queries.1 = (bf16[1,848,128]{2,1,0:T(8,128)(2,1)S(1)}, bf16[1,848,128]{2,1,0:T(8,128)(2,1)S(1)}, bf16[1,848,128]{2,1,0:T(8,128)(2,1)S(1)}, bf16[1,848,128]{2,1,0:T(8,128)(2,1)S(1)}) custom-call(s32[1]{0:T(128)} %bitcast.ids_ref.ids_any, s32[64]{0:T(128)S(1)} %copy-done.7, bf16[4,16,32,128]{3,2,1,0:T(8,128)(2,1)S(1)} %copy-done.3, ...), custom_call_target="tpu_custom_call" | custom-call | flops 2000000000 | bytes 6000000 | tf_op jit(solution)/shard_map/pack_queries/pallas_call | solution.py:438
  2.4 0.5 collective-permute-start
  2.9 2.6 %collective-permute-start.3 = (bf16[1,848,128]{2,1,0:T(8,128)(2,1)S(1)}, bf16[1,848,128]{2,1,0:T(8,128)(2,1)S(1)}, u32[]{:S(2)}, u32[]{:S(2)}) collective-permute-start(bf16[1,848,128]{2,1,0:T(8,128)(2,1)S(1)} %get-tuple-element.26), channel_id=1, source_target_pairs={{0,8},{4,12},{8,0},{12,4},{1,9},{5,13},{9,1},{13,5},{2,10},{6,14},... | collective-permute-start | bytes 651272 | tf_op jit(solution)/shard_map/ppermute | solution.py:392
  5.5 0.1 collective-permute-start.4
  5.6 0.0 slice-start
  5.6 0.0 slice-start.1
  5.6 7.4 %attend.2.rest_0_ = bf16[32,4096]{1,0:T(8,128)(2,1)S(1)} custom-call(s32[1]{0:T(128)} %bitcast.ids_ref.ids_any, s32[64]{0:T(128)S(1)} %copy-done.7, s32[4,16]{1,0:T(4,128)S(1)} %copy-done.6, bf16[1,848,128]{2,1,0:T(8,128)(2,1)S(1)} %get-tuple-element.24.rest_0_, bf16[1,848,128]{2,1,0:T(8,128)(2,1)S(1)} %collective-permute-done.rest_1_, ...), custom_call_target="tpu_custom_call" | custom-call | flops 8000000000 | bytes 24000000 | tf_op jit(solution)/shard_map/attend/pallas_call | solution.py:456
  13.0 0.0 slice-start.2
  13.0 2.2 %collective-permute-start.2 = (bf16[32,4096]{1,0:T(8,128)(2,1)S(1)}, bf16[32,4096]{1,0:T(8,128)(2,1)S(1)}, u32[]{:S(2)}, u32[]{:S(2)}) collective-permute-start(bf16[32,4096]{1,0:T(8,128)(2,1)S(1)} %attend.2.rest_0_), channel_id=1, source_target_pairs={{0,8},{4,12},{8,0},{12,4},{1,9},{5,13},{9,1},{13,5},{2,10},{6,14},... | collective-permute-start | bytes 786440 | tf_op jit(solution)/shard_map/ppermute | solution.py:392
  15.2 0.0 collective-permute-start.1
  15.2 0.0 collective-permute-done.3.rest_0_
  15.2 0.6 collective-permute-done.4.rest_1_
  15.8 6.9 %attend.3.rest_0_ = bf16[32,4096]{1,0:T(8,128)(2,1)S(1)} custom-call(s32[1]{0:T(128)} %bitcast.ids_ref.ids_any, s32[64]{0:T(128)S(1)} %copy-done.7, s32[4,16]{1,0:T(4,128)S(1)} %copy-done.6, bf16[1,848,128]{2,1,0:T(8,128)(2,1)S(1)} %collective-permute-done.3.rest_0_, bf16[1,848,128]{2,1,0:T(8,128)(2,1)S(1)} %collective-permute-done.4.rest_1_, ...), custom_call_target="tpu_custom_call" | custom-call | flops 8000000000 | bytes 24000000 | tf_op jit(solution)/shard_map/attend/pallas_call | solution.py:456
  22.8 0.0 collective-permute-done.2.rest_2_
  22.8 0.3 collective-permute-start.5
  23.1 2.4 %collective-permute-start.9 = (bf16[32,4096]{1,0:T(8,128)(2,1)S(1)}, bf16[32,4096]{1,0:T(8,128)(2,1)S(1)}, u32[]{:S(2)}, u32[]{:S(2)}) collective-permute-start(bf16[32,4096]{1,0:T(8,128)(2,1)S(1)} %attend.3.rest_0_), channel_id=1, source_target_pairs={{0,8},{4,12},{8,0},{12,4},{1,9},{5,13},{9,1},{13,5},{2,10},{6,14},... | collective-permute-start | bytes 786440 | tf_op jit(solution)/shard_map/ppermute | solution.py:392
  25.5 1.0 %project_out.5 = (bf16[64,640]{1,0:T(8,128)(2,1)S(1)}, bf16[64,640]{1,0:T(8,128)(2,1)S(1)}) custom-call(s32[1]{0:T(128)} %bitcast.ids_ref.ids_any, bf16[32,4096]{1,0:T(8,128)(2,1)S(1)} %attend.2.rest_0_, bf16[32,4096]{1,0:T(8,128)(2,1)S(1)} %collective-permute-done.1.rest_1_, bf16[32,4096]{1,0:T(8,128)(2,1)S(1)} %collective-permute-done.2.rest_2_, ...), custom_call_target="tpu_custom_call" | custom-call | flops 2000000000 | bytes 6000000 | tf_op jit(solution)/shard_map/project_out/pallas_call | solution.py:509
  26.5 1.6 %collective-permute-start.6 = (bf16[64,640]{1,0:T(8,128)(2,1)S(1)}, bf16[64,640]{1,0:T(8,128)(2,1)S(1)}, u32[]{:S(2)}, u32[]{:S(2)}) collective-permute-start(bf16[64,640]{1,0:T(8,128)(2,1)S(1)} %get-tuple-element.30), channel_id=1, source_target_pairs={{0,1},{1,0},{2,3},{3,2},{4,5},{5,4},{6,7},{7,6},{8,9},{9,8},{10,11... | collective-permute-start | bytes 245768 | tf_op jit(solution)/shard_map/ppermute | solution.py:392
  28.1 1.6 %project_out.7 = (bf16[64,1152]{1,0:T(8,128)(2,1)S(1)}, bf16[64,1152]{1,0:T(8,128)(2,1)S(1)}) custom-call(s32[1]{0:T(128)} %bitcast.ids_ref.ids_any, bf16[32,4096]{1,0:T(8,128)(2,1)S(1)} %attend.2.rest_0_, bf16[32,4096]{1,0:T(8,128)(2,1)S(1)} %collective-permute-done.1.rest_1_, bf16[32,4096]{1,0:T(8,128)(2,1)S(1)} %collective-permute-done.2.rest_2_, ...), custom_call_target="tpu_custom_call" | custom-call | flops 2000000000 | bytes 6000000 | tf_op jit(solution)/shard_map/project_out/pallas_call | solution.py:509
  29.7 0.5 collective-permute-start.13
  30.2 1.2 %collective-permute-done.6 = bf16[64,640]{1,0:T(8,128)(2,1)S(1)} collective-permute-done((bf16[64,640]{1,0:T(8,128)(2,1)S(1)}, bf16[64,640]{1,0:T(8,128)(2,1)S(1)}, u32[]{:S(2)}, u32[]{:S(2)}) %collective-permute-start.6) | collective-permute-done | bytes 81952 | tf_op jit(solution)/shard_map/ppermute | solution.py:392
  31.4 3.7 %collective-permute-start.7 = (bf16[64,640]{1,0:T(8,128)(2,1)S(1)}, bf16[64,640]{1,0:T(8,128)(2,1)S(1)}, u32[]{:S(2)}, u32[]{:S(2)}) collective-permute-start(bf16[64,640]{1,0:T(8,128)(2,1)S(1)} %add_convert_fusion.7), channel_id=1, source_target_pairs={{0,3},{1,2},{2,1},{3,0},{4,7},{5,6},{6,5},{7,4},{8,11},{9,10},{10,... | collective-permute-start | bytes 245768 | tf_op jit(solution)/shard_map/ppermute | solution.py:392
  35.1 0.6 collective-permute-done.13
  35.8 2.6 %collective-permute-start.14 = (bf16[64,1152]{1,0:T(8,128)(2,1)S(1)}, bf16[64,1152]{1,0:T(8,128)(2,1)S(1)}, u32[]{:S(2)}, u32[]{:S(2)}) collective-permute-start(bf16[64,1152]{1,0:T(8,128)(2,1)S(1)} %add_convert_fusion.1), channel_id=1, source_target_pairs={{0,3},{1,2},{2,1},{3,0},{4,7},{5,6},{6,5},{7,4},{8,11},{9,10},{10,... | collective-permute-start | bytes 442376 | tf_op jit(solution)/shard_map/ppermute | solution.py:392
  38.3 0.7 %project_out.9 = (bf16[64,384]{1,0:T(8,128)(2,1)S(1)}, bf16[64,384]{1,0:T(8,128)(2,1)S(1)}) custom-call(s32[1]{0:T(128)} %bitcast.ids_ref.ids_any, bf16[32,4096]{1,0:T(8,128)(2,1)S(1)} %attend.3.rest_0_, bf16[32,4096]{1,0:T(8,128)(2,1)S(1)} %collective-permute-done.8.rest_1_, bf16[32,4096]{1,0:T(8,128)(2,1)S(1)} %collective-permute-done.9.rest_2_, ...), custom_call_target="tpu_custom_call" | custom-call | flops 2000000000 | bytes 6000000 | tf_op jit(solution)/shard_map/project_out/pallas_call | solution.py:509
  39.0 1.5 %collective-permute-start.21 = (bf16[64,384]{1,0:T(8,128)(2,1)S(1)}, bf16[64,384]{1,0:T(8,128)(2,1)S(1)}, u32[]{:S(2)}, u32[]{:S(2)}) collective-permute-start(bf16[64,384]{1,0:T(8,128)(2,1)S(1)} %get-tuple-element.42), channel_id=1, source_target_pairs={{0,1},{1,0},{2,3},{3,2},{4,5},{5,4},{6,7},{7,6},{8,9},{9,8},{10,11... | collective-permute-start | bytes 147464 | tf_op jit(solution)/shard_map/ppermute | solution.py:392
  40.5 1.0 %project_out.8 = (bf16[64,640]{1,0:T(8,128)(2,1)S(1)}, bf16[64,640]{1,0:T(8,128)(2,1)S(1)}) custom-call(s32[1]{0:T(128)} %bitcast.ids_ref.ids_any, bf16[32,4096]{1,0:T(8,128)(2,1)S(1)} %attend.3.rest_0_, bf16[32,4096]{1,0:T(8,128)(2,1)S(1)} %collective-permute-done.8.rest_1_, bf16[32,4096]{1,0:T(8,128)(2,1)S(1)} %collective-permute-done.9.rest_2_, ...), custom_call_target="tpu_custom_call" | custom-call | flops 2000000000 | bytes 6000000 | tf_op jit(solution)/shard_map/project_out/pallas_call | solution.py:509
  41.5 0.7 %collective-permute-start.18 = (bf16[64,640]{1,0:T(8,128)(2,1)S(1)}, bf16[64,640]{1,0:T(8,128)(2,1)S(1)}, u32[]{:S(2)}, u32[]{:S(2)}) collective-permute-start(bf16[64,640]{1,0:T(8,128)(2,1)S(1)} %get-tuple-element.40), channel_id=1, source_target_pairs={{0,1},{1,0},{2,3},{3,2},{4,5},{5,4},{6,7},{7,6},{8,9},{9,8},{10,11... | collective-permute-start | bytes 245768 | tf_op jit(solution)/shard_map/ppermute | solution.py:392
  42.2 1.0 %project_out.6 = (bf16[64,768]{1,0:T(8,128)(2,1)S(1)}, bf16[64,768]{1,0:T(8,128)(2,1)S(1)}) custom-call(s32[1]{0:T(128)} %bitcast.ids_ref.ids_any, bf16[32,4096]{1,0:T(8,128)(2,1)S(1)} %attend.3.rest_0_, bf16[32,4096]{1,0:T(8,128)(2,1)S(1)} %collective-permute-done.8.rest_1_, bf16[32,4096]{1,0:T(8,128)(2,1)S(1)} %collective-permute-done.9.rest_2_, ...), custom_call_target="tpu_custom_call" | custom-call | flops 2000000000 | bytes 6000000 | tf_op jit(solution)/shard_map/project_out/pallas_call | solution.py:509
  43.3 1.5 %collective-permute-start.11 = (bf16[64,768]{1,0:T(8,128)(2,1)S(1)}, bf16[64,768]{1,0:T(8,128)(2,1)S(1)}, u32[]{:S(2)}, u32[]{:S(2)}) collective-permute-start(bf16[64,768]{1,0:T(8,128)(2,1)S(1)} %get-tuple-element.34), channel_id=1, source_target_pairs={{0,1},{1,0},{2,3},{3,2},{4,5},{5,4},{6,7},{7,6},{8,9},{9,8},{10,11... | collective-permute-start | bytes 294920 | tf_op jit(solution)/shard_map/ppermute | solution.py:392
  44.7 1.9 %collective-permute-start.22 = (bf16[64,384]{1,0:T(8,128)(2,1)S(1)}, bf16[64,384]{1,0:T(8,128)(2,1)S(1)}, u32[]{:S(2)}, u32[]{:S(2)}) collective-permute-start(bf16[64,384]{1,0:T(8,128)(2,1)S(1)} %add_convert_fusion.9), channel_id=1, source_target_pairs={{0,3},{1,2},{2,1},{3,0},{4,7},{5,6},{6,5},{7,4},{8,11},{9,10},{10,... | collective-permute-start | bytes 147464 | tf_op jit(solution)/shard_map/ppermute | solution.py:392
  46.6 0.4 collective-permute-done.18
  47.0 1.7 %collective-permute-start.19 = (bf16[64,640]{1,0:T(8,128)(2,1)S(1)}, bf16[64,640]{1,0:T(8,128)(2,1)S(1)}, u32[]{:S(2)}, u32[]{:S(2)}) collective-permute-start(bf16[64,640]{1,0:T(8,128)(2,1)S(1)} %add_convert_fusion.5), channel_id=1, source_target_pairs={{0,3},{1,2},{2,1},{3,0},{4,7},{5,6},{6,5},{7,4},{8,11},{9,10},{10,... | collective-permute-start | bytes 245768 | tf_op jit(solution)/shard_map/ppermute | solution.py:392
  48.8 2.2 %collective-permute-start.16 = (bf16[64,768]{1,0:T(8,128)(2,1)S(1)}, bf16[64,768]{1,0:T(8,128)(2,1)S(1)}, u32[]{:S(2)}, u32[]{:S(2)}) collective-permute-start(bf16[64,768]{1,0:T(8,128)(2,1)S(1)} %add_convert_fusion.3), channel_id=1, source_target_pairs={{0,3},{1,2},{2,1},{3,0},{4,7},{5,6},{6,5},{7,4},{8,11},{9,10},{10,... | collective-permute-start | bytes 294920 | tf_op jit(solution)/shard_map/ppermute | solution.py:392
  51.1 0.1 collective-permute-start.12
  51.1 2.0 %collective-permute-start.15 = (bf16[64,1152]{1,0:T(8,128)(2,1)S(1)}, bf16[64,1152]{1,0:T(8,128)(2,1)S(1)}, u32[]{:S(2)}, u32[]{:S(2)}) collective-permute-start(bf16[64,1152]{1,0:T(8,128)(2,1)S(1)} %add_convert_fusion.rest_2_), channel_id=1, source_target_pairs={{0,1},{1,0},{2,3},{3,2},{4,5},{5,4},{6,7},{7,6},{8,9},{9,8},{10,11... | collective-permute-start | bytes 442376 | tf_op jit(solution)/shard_map/ppermute | solution.py:392
  53.2 1.1 %collective-permute-done.19 = bf16[64,640]{1,0:T(8,128)(2,1)S(1)} collective-permute-done((bf16[64,640]{1,0:T(8,128)(2,1)S(1)}, bf16[64,640]{1,0:T(8,128)(2,1)S(1)}, u32[]{:S(2)}, u32[]{:S(2)}) %collective-permute-start.19) | collective-permute-done | bytes 81952 | tf_op jit(solution)/shard_map/ppermute | solution.py:392
  54.3 1.9 %collective-permute-start.20 = (bf16[64,640]{1,0:T(8,128)(2,1)S(1)}, bf16[64,640]{1,0:T(8,128)(2,1)S(1)}, u32[]{:S(2)}, u32[]{:S(2)}) collective-permute-start(bf16[64,640]{1,0:T(8,128)(2,1)S(1)} %add_convert_fusion.4.rest_6_), channel_id=1, source_target_pairs={{0,1},{1,0},{2,3},{3,2},{4,5},{5,4},{6,7},{7,6},{8,9},{9,8},{10,11... | collective-permute-start | bytes 245768 | tf_op jit(solution)/shard_map/ppermute | solution.py:392
  56.2 0.2 collective-permute-done.16
  56.4 1.3 %collective-permute-start.17 = (bf16[64,768]{1,0:T(8,128)(2,1)S(1)}, bf16[64,768]{1,0:T(8,128)(2,1)S(1)}, u32[]{:S(2)}, u32[]{:S(2)}) collective-permute-start(bf16[64,768]{1,0:T(8,128)(2,1)S(1)} %add_convert_fusion.2.rest_4_), channel_id=1, source_target_pairs={{0,1},{1,0},{2,3},{3,2},{4,5},{5,4},{6,7},{7,6},{8,9},{9,8},{10,11... | collective-permute-start | bytes 294920 | tf_op jit(solution)/shard_map/ppermute | solution.py:392
  57.7 0.9 %collective-permute-start.23 = (bf16[64,384]{1,0:T(8,128)(2,1)S(1)}, bf16[64,384]{1,0:T(8,128)(2,1)S(1)}, u32[]{:S(2)}, u32[]{:S(2)}) collective-permute-start(bf16[64,384]{1,0:T(8,128)(2,1)S(1)} %add_convert_fusion.8.rest_8_), channel_id=1, source_target_pairs={{0,1},{1,0},{2,3},{3,2},{4,5},{5,4},{6,7},{7,6},{8,9},{9,8},{10,11... | collective-permute-start | bytes 147464 | tf_op jit(solution)/shard_map/ppermute | solution.py:392
  58.6 1.1 %place_rows.1.pick_ref = bf16[4,64,256]{2,1,0:T(8,128)(2,1)S(1)} custom-call(s32[1]{0:T(128)} %bitcast.ids_ref.ids_any, s32[64]{0:T(128)S(1)} %copy-done.7), custom_call_target="tpu_custom_call" | custom-call | flops 100000000 | bytes 300000 | tf_op jit(solution)/shard_map/place_rows/pallas_call | solution.py:416
  59.7 5.7 %collective-permute-done.23.rest_9_ = bf16[64,384]{1,0:T(8,128)(2,1)S(1)} collective-permute-done((bf16[64,384]{1,0:T(8,128)(2,1)S(1)}, bf16[64,384]{1,0:T(8,128)(2,1)S(1)}, u32[]{:S(2)}, u32[]{:S(2)}) %collective-permute-start.23) | collective-permute-done | bytes 49184 | tf_op jit(solution)/shard_map/ppermute | solution.py:392
  65.4 1.4 %order_rows.1 = bf16[4,64,1792]{2,1,0:T(8,128)(2,1)} custom-call(s32[1]{0:T(128)} %bitcast.ids_ref.ids_any, bf16[4,64,256]{2,1,0:T(8,128)(2,1)S(1)} %place_rows.1.pick_ref, bf16[64,640]{1,0:T(8,128)(2,1)S(1)} %add_convert_fusion.6.rest_0_, bf16[64,640]{1,0:T(8,128)(2,1)S(1)} %collective-permute-done.12.rest_1_, ...), custom_call_target="tpu_custom_call" | custom-call | flops 2000000000 | bytes 6000000 | tf_op jit(solution)/shard_map/order_rows/pallas_call | solution.py:486
  (46 shorter events, 0.3 us)
Async XLA Ops:
  0.0 0.7 copy-start.7
  0.0 0.9 %copy-start.5 = (bf16[4,16,576]{2,1,0:T(8,128)(2,1)S(1)}, bf16[4,16,576]{2,1,0:T(8,128)(2,1)}, u32[]{:S(2)}) copy-start(bf16[4,16,576]{2,1,0:T(8,128)(2,1)} %fresh_ref.1) | copy-start | bytes 221188
  0.0 1.1 %copy-start.4 = (bf16[4,16,32,64]{3,2,1,0:T(8,128)(2,1)S(1)}, bf16[4,16,32,64]{3,2,1,0:T(8,128)(2,1)}, u32[]{:S(2)}) copy-start(bf16[4,16,32,64]{3,2,1,0:T(8,128)(2,1)} %rope_ref.1) | copy-start | bytes 786436
  0.0 1.3 %copy-start.3 = (bf16[4,16,32,128]{3,2,1,0:T(8,128)(2,1)S(1)}, bf16[4,16,32,128]{3,2,1,0:T(8,128)(2,1)}, u32[]{:S(2)}) copy-start(bf16[4,16,32,128]{3,2,1,0:T(8,128)(2,1)} %nope_ref.1) | copy-start | bytes 1572868
  0.0 5.6 %copy-start.1 = (bf16[32,128,512]{2,1,0:T(8,128)(2,1)S(1)}, bf16[32,128,512]{2,1,0:T(8,128)(2,1)}, u32[]{:S(2)}) copy-start(bf16[32,128,512]{2,1,0:T(8,128)(2,1)} %rest_3_.3) | copy-start | bytes 12582916
  0.0 5.6 %copy-start.2 = (bf16[32,512,128]{2,1,0:T(8,128)(2,1)S(1)}, bf16[32,512,128]{2,1,0:T(8,128)(2,1)}, u32[]{:S(2)}) copy-start(bf16[32,512,128]{2,1,0:T(8,128)(2,1)} %rest_4_.8) | copy-start | bytes 12582916
  1.3 4.3 %copy-start = (bf16[4096,576]{0,1:T(8,128)(2,1)S(1)}, bf16[4096,576]{0,1:T(8,128)(2,1)}, u32[]{:S(2)}) copy-start(bf16[4096,576]{0,1:T(8,128)(2,1)} %param.9) | copy-start | bytes 14155780
  1.3 4.3 %copy-start.6 = (s32[4,16]{1,0:T(4,128)S(1)}, s32[4,16]{1,0:T(4,128)}, u32[]{:S(2)}) copy-start(s32[4,16]{1,0:T(4,128)} %length_any.3) | copy-start | bytes 772
  2.4 3.2 %collective-permute-start = (bf16[1,848,128]{2,1,0:T(8,128)(2,1)S(1)}, bf16[1,848,128]{2,1,0:T(8,128)(2,1)S(1)}, u32[]{:S(2)}, u32[]{:S(2)}) collective-permute-start(bf16[1,848,128]{2,1,0:T(8,128)(2,1)S(1)} %get-tuple-element.25), channel_id=1, source_target_pairs={{0,4},{4,0},{8,12},{12,8},{1,5},{5,1},{9,13},{13,9},{2,6},{6,2},{1... | collective-permute-start | bytes 651272 | tf_op jit(solution)/shard_map/ppermute | solution.py:392
  2.9 12.3 %collective-permute-start.3 = (bf16[1,848,128]{2,1,0:T(8,128)(2,1)S(1)}, bf16[1,848,128]{2,1,0:T(8,128)(2,1)S(1)}, u32[]{:S(2)}, u32[]{:S(2)}) collective-permute-start(bf16[1,848,128]{2,1,0:T(8,128)(2,1)S(1)} %get-tuple-element.26), channel_id=1, source_target_pairs={{0,8},{4,12},{8,0},{12,4},{1,9},{5,13},{9,1},{13,5},{2,10},{6,14},... | collective-permute-start | bytes 651272 | tf_op jit(solution)/shard_map/ppermute | solution.py:392
  5.5 10.3 %collective-permute-start.4 = (bf16[1,848,128]{2,1,0:T(8,128)(2,1)S(1)}, bf16[1,848,128]{2,1,0:T(8,128)(2,1)S(1)}, u32[]{:S(2)}, u32[]{:S(2)}) collective-permute-start(bf16[1,848,128]{2,1,0:T(8,128)(2,1)S(1)} %get-tuple-element.27), channel_id=1, source_target_pairs={{0,12},{4,8},{8,4},{12,0},{1,13},{5,9},{9,5},{13,1},{2,14},{6,10},... | collective-permute-start | bytes 651272 | tf_op jit(solution)/shard_map/ppermute | solution.py:392
  5.6 19.8 %slice-start = ((s8[14680064]{0:T(1024)(128)(4,1)}), s8[4194304]{0:T(1024)(128)(4,1)S(1)}, s32[]{:S(2)}) async-start(s8[14680064]{0:T(1024)(128)(4,1)} %bitcast.2), calls=%async_computation | async-start | bytes 8388608
  5.6 19.8 %slice-start.1 = ((s8[14680064]{0:T(1024)(128)(4,1)}), s8[4194304]{0:T(1024)(128)(4,1)S(1)}, s32[]{:S(2)}) async-start(s8[14680064]{0:T(1024)(128)(4,1)} %bitcast.2), calls=%async_computation.1 | async-start | bytes 8388608
  13.0 12.5 %slice-start.2 = ((s8[14680064]{0:T(1024)(128)(4,1)}), s8[4194304]{0:T(1024)(128)(4,1)S(1)}, s32[]{:S(2)}) async-start(s8[14680064]{0:T(1024)(128)(4,1)} %bitcast.2), calls=%async_computation.2 | async-start | bytes 8388608
  13.0 12.5 %slice-start.3 = ((s8[14680064]{0:T(1024)(128)(4,1)}), s8[2097152]{0:T(1024)(128)(4,1)S(1)}, s32[]{:S(2)}) async-start(s8[14680064]{0:T(1024)(128)(4,1)} %bitcast.2), calls=%async_computation.3 | async-start | bytes 4194304
  13.0 9.7 %collective-permute-start.2 = (bf16[32,4096]{1,0:T(8,128)(2,1)S(1)}, bf16[32,4096]{1,0:T(8,128)(2,1)S(1)}, u32[]{:S(2)}, u32[]{:S(2)}) collective-permute-start(bf16[32,4096]{1,0:T(8,128)(2,1)S(1)} %attend.2.rest_0_), channel_id=1, source_target_pairs={{0,8},{4,12},{8,0},{12,4},{1,9},{5,13},{9,1},{13,5},{2,10},{6,14},... | collective-permute-start | bytes 786440 | tf_op jit(solution)/shard_map/ppermute | solution.py:392
  15.2 10.2 %collective-permute-start.1 = (bf16[32,4096]{1,0:T(8,128)(2,1)S(1)}, bf16[32,4096]{1,0:T(8,128)(2,1)S(1)}, u32[]{:S(2)}, u32[]{:S(2)}) collective-permute-start(bf16[32,4096]{1,0:T(8,128)(2,1)S(1)} %attend.2.rest_0_), channel_id=1, source_target_pairs={{0,4},{4,0},{8,12},{12,8},{1,5},{5,1},{9,13},{13,9},{2,6},{6,2},{1... | collective-permute-start | bytes 786440 | tf_op jit(solution)/shard_map/ppermute | solution.py:392
  22.8 2.7 %collective-permute-start.5 = (bf16[32,4096]{1,0:T(8,128)(2,1)S(1)}, bf16[32,4096]{1,0:T(8,128)(2,1)S(1)}, u32[]{:S(2)}, u32[]{:S(2)}) collective-permute-start(bf16[32,4096]{1,0:T(8,128)(2,1)S(1)} %collective-permute-done.2.rest_2_), channel_id=1, source_target_pairs={{0,4},{4,0},{8,12},{12,8},{1,5},{5,1},{9,13},{13,9},{2,6},{6,2},{1... | collective-permute-start | bytes 786440 | tf_op jit(solution)/shard_map/ppermute | solution.py:392
  23.1 12.0 %collective-permute-start.9 = (bf16[32,4096]{1,0:T(8,128)(2,1)S(1)}, bf16[32,4096]{1,0:T(8,128)(2,1)S(1)}, u32[]{:S(2)}, u32[]{:S(2)}) collective-permute-start(bf16[32,4096]{1,0:T(8,128)(2,1)S(1)} %attend.3.rest_0_), channel_id=1, source_target_pairs={{0,8},{4,12},{8,0},{12,4},{1,9},{5,13},{9,1},{13,5},{2,10},{6,14},... | collective-permute-start | bytes 786440 | tf_op jit(solution)/shard_map/ppermute | solution.py:392
  25.4 12.9 %collective-permute-start.8 = (bf16[32,4096]{1,0:T(8,128)(2,1)S(1)}, bf16[32,4096]{1,0:T(8,128)(2,1)S(1)}, u32[]{:S(2)}, u32[]{:S(2)}) collective-permute-start(bf16[32,4096]{1,0:T(8,128)(2,1)S(1)} %attend.3.rest_0_), channel_id=1, source_target_pairs={{0,4},{4,0},{8,12},{12,8},{1,5},{5,1},{9,13},{13,9},{2,6},{6,2},{1... | collective-permute-start | bytes 786440 | tf_op jit(solution)/shard_map/ppermute | solution.py:392
  26.5 4.9 %collective-permute-start.6 = (bf16[64,640]{1,0:T(8,128)(2,1)S(1)}, bf16[64,640]{1,0:T(8,128)(2,1)S(1)}, u32[]{:S(2)}, u32[]{:S(2)}) collective-permute-start(bf16[64,640]{1,0:T(8,128)(2,1)S(1)} %get-tuple-element.30), channel_id=1, source_target_pairs={{0,1},{1,0},{2,3},{3,2},{4,5},{5,4},{6,7},{7,6},{8,9},{9,8},{10,11... | collective-permute-start | bytes 245768 | tf_op jit(solution)/shard_map/ppermute | solution.py:392
  29.7 6.0 %collective-permute-start.13 = (bf16[64,1152]{1,0:T(8,128)(2,1)S(1)}, bf16[64,1152]{1,0:T(8,128)(2,1)S(1)}, u32[]{:S(2)}, u32[]{:S(2)}) collective-permute-start(bf16[64,1152]{1,0:T(8,128)(2,1)S(1)} %get-tuple-element.37), channel_id=1, source_target_pairs={{0,1},{1,0},{2,3},{3,2},{4,5},{5,4},{6,7},{7,6},{8,9},{9,8},{10,11... | collective-permute-start | bytes 442376 | tf_op jit(solution)/shard_map/ppermute | solution.py:392
  31.4 19.6 %collective-permute-start.7 = (bf16[64,640]{1,0:T(8,128)(2,1)S(1)}, bf16[64,640]{1,0:T(8,128)(2,1)S(1)}, u32[]{:S(2)}, u32[]{:S(2)}) collective-permute-start(bf16[64,640]{1,0:T(8,128)(2,1)S(1)} %add_convert_fusion.7), channel_id=1, source_target_pairs={{0,3},{1,2},{2,1},{3,0},{4,7},{5,6},{6,5},{7,4},{8,11},{9,10},{10,... | collective-permute-start | bytes 245768 | tf_op jit(solution)/shard_map/ppermute | solution.py:392
  35.1 3.2 %collective-permute-start.10 = (bf16[32,4096]{1,0:T(8,128)(2,1)S(1)}, bf16[32,4096]{1,0:T(8,128)(2,1)S(1)}, u32[]{:S(2)}, u32[]{:S(2)}) collective-permute-start(bf16[32,4096]{1,0:T(8,128)(2,1)S(1)} %collective-permute-done.9.rest_2_), channel_id=1, source_target_pairs={{0,4},{4,0},{8,12},{12,8},{1,5},{5,1},{9,13},{13,9},{2,6},{6,2},{1... | collective-permute-start | bytes 786440 | tf_op jit(solution)/shard_map/ppermute | solution.py:392
  35.8 15.2 %collective-permute-start.14 = (bf16[64,1152]{1,0:T(8,128)(2,1)S(1)}, bf16[64,1152]{1,0:T(8,128)(2,1)S(1)}, u32[]{:S(2)}, u32[]{:S(2)}) collective-permute-start(bf16[64,1152]{1,0:T(8,128)(2,1)S(1)} %add_convert_fusion.1), channel_id=1, source_target_pairs={{0,3},{1,2},{2,1},{3,0},{4,7},{5,6},{6,5},{7,4},{8,11},{9,10},{10,... | collective-permute-start | bytes 442376 | tf_op jit(solution)/shard_map/ppermute | solution.py:392
  39.0 5.7 %collective-permute-start.21 = (bf16[64,384]{1,0:T(8,128)(2,1)S(1)}, bf16[64,384]{1,0:T(8,128)(2,1)S(1)}, u32[]{:S(2)}, u32[]{:S(2)}) collective-permute-start(bf16[64,384]{1,0:T(8,128)(2,1)S(1)} %get-tuple-element.42), channel_id=1, source_target_pairs={{0,1},{1,0},{2,3},{3,2},{4,5},{5,4},{6,7},{7,6},{8,9},{9,8},{10,11... | collective-permute-start | bytes 147464 | tf_op jit(solution)/shard_map/ppermute | solution.py:392
  41.5 5.5 %collective-permute-start.18 = (bf16[64,640]{1,0:T(8,128)(2,1)S(1)}, bf16[64,640]{1,0:T(8,128)(2,1)S(1)}, u32[]{:S(2)}, u32[]{:S(2)}) collective-permute-start(bf16[64,640]{1,0:T(8,128)(2,1)S(1)} %get-tuple-element.40), channel_id=1, source_target_pairs={{0,1},{1,0},{2,3},{3,2},{4,5},{5,4},{6,7},{7,6},{8,9},{9,8},{10,11... | collective-permute-start | bytes 245768 | tf_op jit(solution)/shard_map/ppermute | solution.py:392
  43.3 5.5 %collective-permute-start.11 = (bf16[64,768]{1,0:T(8,128)(2,1)S(1)}, bf16[64,768]{1,0:T(8,128)(2,1)S(1)}, u32[]{:S(2)}, u32[]{:S(2)}) collective-permute-start(bf16[64,768]{1,0:T(8,128)(2,1)S(1)} %get-tuple-element.34), channel_id=1, source_target_pairs={{0,1},{1,0},{2,3},{3,2},{4,5},{5,4},{6,7},{7,6},{8,9},{9,8},{10,11... | collective-permute-start | bytes 294920 | tf_op jit(solution)/shard_map/ppermute | solution.py:392
  44.7 12.9 %collective-permute-start.22 = (bf16[64,384]{1,0:T(8,128)(2,1)S(1)}, bf16[64,384]{1,0:T(8,128)(2,1)S(1)}, u32[]{:S(2)}, u32[]{:S(2)}) collective-permute-start(bf16[64,384]{1,0:T(8,128)(2,1)S(1)} %add_convert_fusion.9), channel_id=1, source_target_pairs={{0,3},{1,2},{2,1},{3,0},{4,7},{5,6},{6,5},{7,4},{8,11},{9,10},{10,... | collective-permute-start | bytes 147464 | tf_op jit(solution)/shard_map/ppermute | solution.py:392
  47.0 7.3 %collective-permute-start.19 = (bf16[64,640]{1,0:T(8,128)(2,1)S(1)}, bf16[64,640]{1,0:T(8,128)(2,1)S(1)}, u32[]{:S(2)}, u32[]{:S(2)}) collective-permute-start(bf16[64,640]{1,0:T(8,128)(2,1)S(1)} %add_convert_fusion.5), channel_id=1, source_target_pairs={{0,3},{1,2},{2,1},{3,0},{4,7},{5,6},{6,5},{7,4},{8,11},{9,10},{10,... | collective-permute-start | bytes 245768 | tf_op jit(solution)/shard_map/ppermute | solution.py:392
  48.8 7.6 %collective-permute-start.16 = (bf16[64,768]{1,0:T(8,128)(2,1)S(1)}, bf16[64,768]{1,0:T(8,128)(2,1)S(1)}, u32[]{:S(2)}, u32[]{:S(2)}) collective-permute-start(bf16[64,768]{1,0:T(8,128)(2,1)S(1)} %add_convert_fusion.3), channel_id=1, source_target_pairs={{0,3},{1,2},{2,1},{3,0},{4,7},{5,6},{6,5},{7,4},{8,11},{9,10},{10,... | collective-permute-start | bytes 294920 | tf_op jit(solution)/shard_map/ppermute | solution.py:392
  51.1 14.3 %collective-permute-start.12 = (bf16[64,640]{1,0:T(8,128)(2,1)S(1)}, bf16[64,640]{1,0:T(8,128)(2,1)S(1)}, u32[]{:S(2)}, u32[]{:S(2)}) collective-permute-start(bf16[64,640]{1,0:T(8,128)(2,1)S(1)} %add_convert_fusion.6.rest_0_), channel_id=1, source_target_pairs={{0,1},{1,0},{2,3},{3,2},{4,5},{5,4},{6,7},{7,6},{8,9},{9,8},{10,11... | collective-permute-start | bytes 245768 | tf_op jit(solution)/shard_map/ppermute | solution.py:392
  51.1 14.2 %collective-permute-start.15 = (bf16[64,1152]{1,0:T(8,128)(2,1)S(1)}, bf16[64,1152]{1,0:T(8,128)(2,1)S(1)}, u32[]{:S(2)}, u32[]{:S(2)}) collective-permute-start(bf16[64,1152]{1,0:T(8,128)(2,1)S(1)} %add_convert_fusion.rest_2_), channel_id=1, source_target_pairs={{0,1},{1,0},{2,3},{3,2},{4,5},{5,4},{6,7},{7,6},{8,9},{9,8},{10,11... | collective-permute-start | bytes 442376 | tf_op jit(solution)/shard_map/ppermute | solution.py:392
  54.3 11.0 %collective-permute-start.20 = (bf16[64,640]{1,0:T(8,128)(2,1)S(1)}, bf16[64,640]{1,0:T(8,128)(2,1)S(1)}, u32[]{:S(2)}, u32[]{:S(2)}) collective-permute-start(bf16[64,640]{1,0:T(8,128)(2,1)S(1)} %add_convert_fusion.4.rest_6_), channel_id=1, source_target_pairs={{0,1},{1,0},{2,3},{3,2},{4,5},{5,4},{6,7},{7,6},{8,9},{9,8},{10,11... | collective-permute-start | bytes 245768 | tf_op jit(solution)/shard_map/ppermute | solution.py:392
  56.4 9.0 %collective-permute-start.17 = (bf16[64,768]{1,0:T(8,128)(2,1)S(1)}, bf16[64,768]{1,0:T(8,128)(2,1)S(1)}, u32[]{:S(2)}, u32[]{:S(2)}) collective-permute-start(bf16[64,768]{1,0:T(8,128)(2,1)S(1)} %add_convert_fusion.2.rest_4_), channel_id=1, source_target_pairs={{0,1},{1,0},{2,3},{3,2},{4,5},{5,4},{6,7},{7,6},{8,9},{9,8},{10,11... | collective-permute-start | bytes 294920 | tf_op jit(solution)/shard_map/ppermute | solution.py:392
  57.7 7.7 %collective-permute-start.23 = (bf16[64,384]{1,0:T(8,128)(2,1)S(1)}, bf16[64,384]{1,0:T(8,128)(2,1)S(1)}, u32[]{:S(2)}, u32[]{:S(2)}) collective-permute-start(bf16[64,384]{1,0:T(8,128)(2,1)S(1)} %add_convert_fusion.8.rest_8_), channel_id=1, source_target_pairs={{0,1},{1,0},{2,3},{3,2},{4,5},{5,4},{6,7},{7,6},{8,9},{9,8},{10,11... | collective-permute-start | bytes 147464 | tf_op jit(solution)/shard_map/ppermute | solution.py:392

commit v19 on v17

--- a/solution.py
+++ b/solution.py
@@ -541,10 +541,10 @@
             made.append((first_row, at, keep, swap((keep, send))))
         return made
 
-    near_made = cut(near, 0, (5, 9))
+    near_made = cut(near, 0, (1, 1))
     pairs = [add(near_made[0][2], near_made[0][3])]
     far = [far_rows, flip(far_rows, "seq", 1), far_across, flip(far_across, "seq", 1)]
-    far_made = cut(far, half, (6, 5, 3))
+    far_made = cut(far, half, (1, 1))
     made = near_made + far_made
     for i, (_, _, keep, incoming) in enumerate(made[1:], 1):
         pairs.append(add(keep, incoming))

time: 66.3 us -> 64.8 us (0.977)
  starting transfers between devices: 31.5 us -> 27.2 us
  waiting for transfers between devices: 10.2 us -> 12.5 us
    ppermute x24 -> x21, starting transfers between devices: 31.5 us -> 27.2 us  [flip(): return lax.ppermute(x, axis, [(i, i ^ distance) for i in range(size)])]
    ppermute x24 -> x21, waiting for transfers between devices: 10.2 us -> 12.5 us  [flip(): return lax.ppermute(x, axis, [(i, i ^ distance) for i in range(size)])]
    pallas_call x5 -> x4, Pallas kernels: 5.29 us -> 5.12 us  [project(): pl.pallas_call(functools.partial(project_kernel, first_col), out_shape=[j...]
  transfers between devices with their start and end apart: 24 -> 21, of which waited for: 6 -> 6; matrix products, arithmetic and copies ran while one was open for 0% -> 0% of each run, Pallas kernels for 30% -> 32%
where the time goes in v19:
time: 64.8 us; the launch traced here: 64.3 us
  starting transfers between devices  27.2 us (42%)
  Pallas kernels  23 us (35%)
  waiting for transfers between devices  12.5 us (19%)
  local copies, waits for them, and re-layouts  1.23 us (2%)
    ppermute x21, starting transfers between devices, flip(): return lax.ppermute(x, axis, [(i, i ^ distance) for i in range(size)])  27.2 us
    pallas_call x2, Pallas kernels, attend(): pl.pallas_call(functools.partial(attend_kernel, sizes, scale, relative, b...  14.3 us
    ppermute x21, waiting for transfers between devices, flip(): return lax.ppermute(x, axis, [(i, i ^ distance) for i in range(size)])  12.5 us
    pallas_call x4, Pallas kernels, project(): pl.pallas_call(functools.partial(project_kernel, first_col), out_shape=[j...  5.12 us
    pallas_call x1, Pallas kernels, order(): pl.pallas_call(kernel, out_shape=jax.ShapeDtypeStruct((steps, sources * r...  1.4 us
  transfers between devices with their start and end apart: 21, of which 6 were waited for; matrix products, arithmetic and copies ran while one was open for 0% of the time, Pallas kernels for 32%

profile of v19, /device:TPU:0, one launch (start us, length us, event | category | flops | bytes accessed | tf_op | source)
XLA Modules:
  0.0 64.3 jit_solution(10048680301101866189)
XLA Ops:
  0.0 0.6 copy-done.7
  0.7 0.4 copy-done.3
  1.1 0.2 copy-done.4
  1.2 1.1 %pack_queries.1 = (bf16[1,848,128]{2,1,0:T(8,128)(2,1)S(1)}, bf16[1,848,128]{2,1,0:T(8,128)(2,1)S(1)}, bf16[1,848,128]{2,1,0:T(8,128)(2,1)S(1)}, bf16[1,848,128]{2,1,0:T(8,128)(2,1)S(1)}) custom-call(s32[1]{0:T(128)} %bitcast.ids_ref.ids_any, s32[64]{0:T(128)S(1)} %copy-done.7, bf16[4,16,32,128]{3,2,1,0:T(8,128)(2,1)S(1)} %copy-done.3, ...), custom_call_target="tpu_custom_call" | custom-call | flops 2000000000 | bytes 6000000 | tf_op jit(solution)/shard_map/pack_queries/pallas_call | solution.py:438
  2.4 0.5 collective-permute-start
  2.9 2.6 %collective-permute-start.3 = (bf16[1,848,128]{2,1,0:T(8,128)(2,1)S(1)}, bf16[1,848,128]{2,1,0:T(8,128)(2,1)S(1)}, u32[]{:S(2)}, u32[]{:S(2)}) collective-permute-start(bf16[1,848,128]{2,1,0:T(8,128)(2,1)S(1)} %get-tuple-element.23), channel_id=1, source_target_pairs={{0,8},{4,12},{8,0},{12,4},{1,9},{5,13},{9,1},{13,5},{2,10},{6,14},... | collective-permute-start | bytes 651272 | tf_op jit(solution)/shard_map/ppermute | solution.py:392
  5.5 0.1 collective-permute-start.4
  5.5 0.0 collective-permute-done.rest_1_
  5.6 0.0 slice-start
  5.6 0.0 slice-start.1
  5.6 7.3 %attend.2.rest_0_ = bf16[32,4096]{1,0:T(8,128)(2,1)S(1)} custom-call(s32[1]{0:T(128)} %bitcast.ids_ref.ids_any, s32[64]{0:T(128)S(1)} %copy-done.7, s32[4,16]{1,0:T(4,128)S(1)} %copy-done.6, bf16[1,848,128]{2,1,0:T(8,128)(2,1)S(1)} %get-tuple-element.21.rest_0_, bf16[1,848,128]{2,1,0:T(8,128)(2,1)S(1)} %collective-permute-done.rest_1_, ...), custom_call_target="tpu_custom_call" | custom-call | flops 8000000000 | bytes 24000000 | tf_op jit(solution)/shard_map/attend/pallas_call | solution.py:456
  12.9 0.0 slice-start.2
  13.0 0.0 slice-start.3
  13.0 2.8 %collective-permute-start.2 = (bf16[32,4096]{1,0:T(8,128)(2,1)S(1)}, bf16[32,4096]{1,0:T(8,128)(2,1)S(1)}, u32[]{:S(2)}, u32[]{:S(2)}) collective-permute-start(bf16[32,4096]{1,0:T(8,128)(2,1)S(1)} %attend.2.rest_0_), channel_id=1, source_target_pairs={{0,8},{4,12},{8,0},{12,4},{1,9},{5,13},{9,1},{13,5},{2,10},{6,14},... | collective-permute-start | bytes 786440 | tf_op jit(solution)/shard_map/ppermute | solution.py:392
  15.8 0.0 collective-permute-start.1
  15.8 0.0 collective-permute-done.3.rest_0_
  15.8 0.0 collective-permute-done.4.rest_1_
  15.8 6.9 %attend.3.rest_0_ = bf16[32,4096]{1,0:T(8,128)(2,1)S(1)} custom-call(s32[1]{0:T(128)} %bitcast.ids_ref.ids_any, s32[64]{0:T(128)S(1)} %copy-done.7, s32[4,16]{1,0:T(4,128)S(1)} %copy-done.6, bf16[1,848,128]{2,1,0:T(8,128)(2,1)S(1)} %collective-permute-done.3.rest_0_, bf16[1,848,128]{2,1,0:T(8,128)(2,1)S(1)} %collective-permute-done.4.rest_1_, ...), custom_call_target="tpu_custom_call" | custom-call | flops 8000000000 | bytes 24000000 | tf_op jit(solution)/shard_map/attend/pallas_call | solution.py:456
  22.7 0.0 collective-permute-done.2.rest_2_
  22.7 0.5 collective-permute-start.5
  23.3 1.0 %collective-permute-start.9 = (bf16[32,4096]{1,0:T(8,128)(2,1)S(1)}, bf16[32,4096]{1,0:T(8,128)(2,1)S(1)}, u32[]{:S(2)}, u32[]{:S(2)}) collective-permute-start(bf16[32,4096]{1,0:T(8,128)(2,1)S(1)} %attend.3.rest_0_), channel_id=1, source_target_pairs={{0,8},{4,12},{8,0},{12,4},{1,9},{5,13},{9,1},{13,5},{2,10},{6,14},... | collective-permute-start | bytes 786440 | tf_op jit(solution)/shard_map/ppermute | solution.py:392
  24.3 0.0 collective-permute-start.8
  24.3 0.2 collective-permute-done.5.rest_3_
  24.5 1.3 %project_out.6 = (bf16[64,896]{1,0:T(8,128)(2,1)S(1)}, bf16[64,896]{1,0:T(8,128)(2,1)S(1)}) custom-call(s32[1]{0:T(128)} %bitcast.ids_ref.ids_any, bf16[32,4096]{1,0:T(8,128)(2,1)S(1)} %attend.2.rest_0_, bf16[32,4096]{1,0:T(8,128)(2,1)S(1)} %collective-permute-done.1.rest_1_, bf16[32,4096]{1,0:T(8,128)(2,1)S(1)} %collective-permute-done.2.rest_2_, ...), custom_call_target="tpu_custom_call" | custom-call | flops 2000000000 | bytes 6000000 | tf_op jit(solution)/shard_map/project_out/pallas_call | solution.py:509
  25.7 1.7 %collective-permute-start.12 = (bf16[64,896]{1,0:T(8,128)(2,1)S(1)}, bf16[64,896]{1,0:T(8,128)(2,1)S(1)}, u32[]{:S(2)}, u32[]{:S(2)}) collective-permute-start(bf16[64,896]{1,0:T(8,128)(2,1)S(1)} %get-tuple-element.32), channel_id=1, source_target_pairs={{0,1},{1,0},{2,3},{3,2},{4,5},{5,4},{6,7},{7,6},{8,9},{9,8},{10,11... | collective-permute-start | bytes 344072 | tf_op jit(solution)/shard_map/ppermute | solution.py:392
  27.4 1.3 %project_out.4 = (bf16[64,896]{1,0:T(8,128)(2,1)S(1)}, bf16[64,896]{1,0:T(8,128)(2,1)S(1)}) custom-call(s32[1]{0:T(128)} %bitcast.ids_ref.ids_any, bf16[32,4096]{1,0:T(8,128)(2,1)S(1)} %attend.2.rest_0_, bf16[32,4096]{1,0:T(8,128)(2,1)S(1)} %collective-permute-done.1.rest_1_, bf16[32,4096]{1,0:T(8,128)(2,1)S(1)} %collective-permute-done.2.rest_2_, ...), custom_call_target="tpu_custom_call" | custom-call | flops 2000000000 | bytes 6000000 | tf_op jit(solution)/shard_map/project_out/pallas_call | solution.py:509
  28.7 0.5 collective-permute-start.6
  29.2 2.4 %collective-permute-done.9.rest_2_ = bf16[32,4096]{1,0:T(8,128)(2,1)S(1)} collective-permute-done((bf16[32,4096]{1,0:T(8,128)(2,1)S(1)}, bf16[32,4096]{1,0:T(8,128)(2,1)S(1)}, u32[]{:S(2)}, u32[]{:S(2)}) %collective-permute-start.9) | collective-permute-done | bytes 262176 | tf_op jit(solution)/shard_map/ppermute | solution.py:392
  31.6 3.9 %collective-permute-start.13 = (bf16[64,896]{1,0:T(8,128)(2,1)S(1)}, bf16[64,896]{1,0:T(8,128)(2,1)S(1)}, u32[]{:S(2)}, u32[]{:S(2)}) collective-permute-start(bf16[64,896]{1,0:T(8,128)(2,1)S(1)} %add_convert_fusion.5), channel_id=1, source_target_pairs={{0,3},{1,2},{2,1},{3,0},{4,7},{5,6},{6,5},{7,4},{8,11},{9,10},{10,... | collective-permute-start | bytes 344072 | tf_op jit(solution)/shard_map/ppermute | solution.py:392
  35.5 1.9 %collective-permute-start.7 = (bf16[64,896]{1,0:T(8,128)(2,1)S(1)}, bf16[64,896]{1,0:T(8,128)(2,1)S(1)}, u32[]{:S(2)}, u32[]{:S(2)}) collective-permute-start(bf16[64,896]{1,0:T(8,128)(2,1)S(1)} %add_convert_fusion.7), channel_id=1, source_target_pairs={{0,3},{1,2},{2,1},{3,0},{4,7},{5,6},{6,5},{7,4},{8,11},{9,10},{10,... | collective-permute-start | bytes 344072 | tf_op jit(solution)/shard_map/ppermute | solution.py:392
  37.4 0.0 collective-permute-done.8.rest_1_
  37.4 0.0 collective-permute-done.10.rest_3_
  37.4 1.3 %project_out.5 = (bf16[64,896]{1,0:T(8,128)(2,1)S(1)}, bf16[64,896]{1,0:T(8,128)(2,1)S(1)}) custom-call(s32[1]{0:T(128)} %bitcast.ids_ref.ids_any, bf16[32,4096]{1,0:T(8,128)(2,1)S(1)} %attend.3.rest_0_, bf16[32,4096]{1,0:T(8,128)(2,1)S(1)} %collective-permute-done.8.rest_1_, bf16[32,4096]{1,0:T(8,128)(2,1)S(1)} %collective-permute-done.9.rest_2_, ...), custom_call_target="tpu_custom_call" | custom-call | flops 2000000000 | bytes 6000000 | tf_op jit(solution)/shard_map/project_out/pallas_call | solution.py:509
  38.7 0.1 collective-permute-start.18
  38.8 1.3 %project_out.7 = (bf16[64,896]{1,0:T(8,128)(2,1)S(1)}, bf16[64,896]{1,0:T(8,128)(2,1)S(1)}) custom-call(s32[1]{0:T(128)} %bitcast.ids_ref.ids_any, bf16[32,4096]{1,0:T(8,128)(2,1)S(1)} %attend.3.rest_0_, bf16[32,4096]{1,0:T(8,128)(2,1)S(1)} %collective-permute-done.8.rest_1_, bf16[32,4096]{1,0:T(8,128)(2,1)S(1)} %collective-permute-done.9.rest_2_, ...), custom_call_target="tpu_custom_call" | custom-call | flops 2000000000 | bytes 6000000 | tf_op jit(solution)/shard_map/project_out/pallas_call | solution.py:509
  40.0 2.1 %collective-permute-start.15 = (bf16[64,896]{1,0:T(8,128)(2,1)S(1)}, bf16[64,896]{1,0:T(8,128)(2,1)S(1)}, u32[]{:S(2)}, u32[]{:S(2)}) collective-permute-start(bf16[64,896]{1,0:T(8,128)(2,1)S(1)} %get-tuple-element.35), channel_id=1, source_target_pairs={{0,1},{1,0},{2,3},{3,2},{4,5},{5,4},{6,7},{7,6},{8,9},{9,8},{10,11... | collective-permute-start | bytes 344072 | tf_op jit(solution)/shard_map/ppermute | solution.py:392
  42.2 2.3 %collective-permute-start.14 = (bf16[64,896]{1,0:T(8,128)(2,1)S(1)}, bf16[64,896]{1,0:T(8,128)(2,1)S(1)}, u32[]{:S(2)}, u32[]{:S(2)}) collective-permute-start(bf16[64,896]{1,0:T(8,128)(2,1)S(1)} %add_convert_fusion.4.rest_2_), channel_id=1, source_target_pairs={{0,1},{1,0},{2,3},{3,2},{4,5},{5,4},{6,7},{7,6},{8,9},{9,8},{10,11... | collective-permute-start | bytes 344072 | tf_op jit(solution)/shard_map/ppermute | solution.py:392
  44.5 1.8 %collective-permute-start.11 = (bf16[64,896]{1,0:T(8,128)(2,1)S(1)}, bf16[64,896]{1,0:T(8,128)(2,1)S(1)}, u32[]{:S(2)}, u32[]{:S(2)}) collective-permute-start(bf16[64,896]{1,0:T(8,128)(2,1)S(1)} %add_convert_fusion.6.rest_0_), channel_id=1, source_target_pairs={{0,1},{1,0},{2,3},{3,2},{4,5},{5,4},{6,7},{7,6},{8,9},{9,8},{10,11... | collective-permute-start | bytes 344072 | tf_op jit(solution)/shard_map/ppermute | solution.py:392
  46.3 2.5 %collective-permute-start.19 = (bf16[64,896]{1,0:T(8,128)(2,1)S(1)}, bf16[64,896]{1,0:T(8,128)(2,1)S(1)}, u32[]{:S(2)}, u32[]{:S(2)}) collective-permute-start(bf16[64,896]{1,0:T(8,128)(2,1)S(1)} %add_convert_fusion.1), channel_id=1, source_target_pairs={{0,3},{1,2},{2,1},{3,0},{4,7},{5,6},{6,5},{7,4},{8,11},{9,10},{10,... | collective-permute-start | bytes 344072 | tf_op jit(solution)/shard_map/ppermute | solution.py:392
  48.9 1.4 %collective-permute-start.16 = (bf16[64,896]{1,0:T(8,128)(2,1)S(1)}, bf16[64,896]{1,0:T(8,128)(2,1)S(1)}, u32[]{:S(2)}, u32[]{:S(2)}) collective-permute-start(bf16[64,896]{1,0:T(8,128)(2,1)S(1)} %add_convert_fusion.3), channel_id=1, source_target_pairs={{0,3},{1,2},{2,1},{3,0},{4,7},{5,6},{6,5},{7,4},{8,11},{9,10},{10,... | collective-permute-start | bytes 344072 | tf_op jit(solution)/shard_map/ppermute | solution.py:392
  50.3 5.4 %collective-permute-done.19 = bf16[64,896]{1,0:T(8,128)(2,1)S(1)} collective-permute-done((bf16[64,896]{1,0:T(8,128)(2,1)S(1)}, bf16[64,896]{1,0:T(8,128)(2,1)S(1)}, u32[]{:S(2)}, u32[]{:S(2)}) %collective-permute-start.19) | collective-permute-done | bytes 114720 | tf_op jit(solution)/shard_map/ppermute | solution.py:392
  55.8 0.1 collective-permute-start.20
  55.8 1.6 %collective-permute-done.16 = bf16[64,896]{1,0:T(8,128)(2,1)S(1)} collective-permute-done((bf16[64,896]{1,0:T(8,128)(2,1)S(1)}, bf16[64,896]{1,0:T(8,128)(2,1)S(1)}, u32[]{:S(2)}, u32[]{:S(2)}) %collective-permute-start.16) | collective-permute-done | bytes 114720 | tf_op jit(solution)/shard_map/ppermute | solution.py:392
  57.4 1.5 %collective-permute-start.17 = (bf16[64,896]{1,0:T(8,128)(2,1)S(1)}, bf16[64,896]{1,0:T(8,128)(2,1)S(1)}, u32[]{:S(2)}, u32[]{:S(2)}) collective-permute-start(bf16[64,896]{1,0:T(8,128)(2,1)S(1)} %add_convert_fusion.2.rest_4_), channel_id=1, source_target_pairs={{0,1},{1,0},{2,3},{3,2},{4,5},{5,4},{6,7},{7,6},{8,9},{9,8},{10,11... | collective-permute-start | bytes 344072 | tf_op jit(solution)/shard_map/ppermute | solution.py:392
  58.9 1.1 %place_rows.1.pick_ref = bf16[4,64,256]{2,1,0:T(8,128)(2,1)S(1)} custom-call(s32[1]{0:T(128)} %bitcast.ids_ref.ids_any, s32[64]{0:T(128)S(1)} %copy-done.7), custom_call_target="tpu_custom_call" | custom-call | flops 100000000 | bytes 300000 | tf_op jit(solution)/shard_map/place_rows/pallas_call | solution.py:416
  60.1 1.6 %collective-permute-done.20.rest_7_ = bf16[64,896]{1,0:T(8,128)(2,1)S(1)} collective-permute-done((bf16[64,896]{1,0:T(8,128)(2,1)S(1)}, bf16[64,896]{1,0:T(8,128)(2,1)S(1)}, u32[]{:S(2)}, u32[]{:S(2)}) %collective-permute-start.20) | collective-permute-done | bytes 114720 | tf_op jit(solution)/shard_map/ppermute | solution.py:392
  61.7 1.2 %collective-permute-done.17.rest_5_ = bf16[64,896]{1,0:T(8,128)(2,1)S(1)} collective-permute-done((bf16[64,896]{1,0:T(8,128)(2,1)S(1)}, bf16[64,896]{1,0:T(8,128)(2,1)S(1)}, u32[]{:S(2)}, u32[]{:S(2)}) %collective-permute-start.17) | collective-permute-done | bytes 114720 | tf_op jit(solution)/shard_map/ppermute | solution.py:392
  62.9 1.4 %order_rows.1 = bf16[4,64,1792]{2,1,0:T(8,128)(2,1)} custom-call(s32[1]{0:T(128)} %bitcast.ids_ref.ids_any, bf16[4,64,256]{2,1,0:T(8,128)(2,1)S(1)} %place_rows.1.pick_ref, bf16[64,896]{1,0:T(8,128)(2,1)S(1)} %add_convert_fusion.6.rest_0_, bf16[64,896]{1,0:T(8,128)(2,1)S(1)} %collective-permute-done.11.rest_1_, ...), custom_call_target="tpu_custom_call" | custom-call | flops 2000000000 | bytes 6000000 | tf_op jit(solution)/shard_map/order_rows/pallas_call | solution.py:486
  (37 shorter events, 0.3 us)
Async XLA Ops:
  0.0 0.7 %copy-start.7 = (s32[64]{0:T(128)S(1)}, s32[64]{0:T(128)}, u32[]{:S(2)}) copy-start(s32[64]{0:T(128)} %decode_any.3) | copy-start | bytes 772
  0.0 1.1 %copy-start.3 = (bf16[4,16,32,128]{3,2,1,0:T(8,128)(2,1)S(1)}, bf16[4,16,32,128]{3,2,1,0:T(8,128)(2,1)}, u32[]{:S(2)}) copy-start(bf16[4,16,32,128]{3,2,1,0:T(8,128)(2,1)} %nope_ref.1) | copy-start | bytes 1572868
  0.0 1.2 %copy-start.4 = (bf16[4,16,32,64]{3,2,1,0:T(8,128)(2,1)S(1)}, bf16[4,16,32,64]{3,2,1,0:T(8,128)(2,1)}, u32[]{:S(2)}) copy-start(bf16[4,16,32,64]{3,2,1,0:T(8,128)(2,1)} %rope_ref.1) | copy-start | bytes 786436
  0.0 1.2 %copy-start.5 = (bf16[4,16,576]{2,1,0:T(8,128)(2,1)S(1)}, bf16[4,16,576]{2,1,0:T(8,128)(2,1)}, u32[]{:S(2)}) copy-start(bf16[4,16,576]{2,1,0:T(8,128)(2,1)} %fresh_ref.1) | copy-start | bytes 221188
  0.0 5.5 %copy-start.1 = (bf16[32,128,512]{2,1,0:T(8,128)(2,1)S(1)}, bf16[32,128,512]{2,1,0:T(8,128)(2,1)}, u32[]{:S(2)}) copy-start(bf16[32,128,512]{2,1,0:T(8,128)(2,1)} %rest_3_.3) | copy-start | bytes 12582916
  0.0 5.5 %copy-start.2 = (bf16[32,512,128]{2,1,0:T(8,128)(2,1)S(1)}, bf16[32,512,128]{2,1,0:T(8,128)(2,1)}, u32[]{:S(2)}) copy-start(bf16[32,512,128]{2,1,0:T(8,128)(2,1)} %rest_4_.7) | copy-start | bytes 12582916
  1.2 4.3 %copy-start = (bf16[4096,576]{0,1:T(8,128)(2,1)S(1)}, bf16[4096,576]{0,1:T(8,128)(2,1)}, u32[]{:S(2)}) copy-start(bf16[4096,576]{0,1:T(8,128)(2,1)} %param.9) | copy-start | bytes 14155780
  1.2 4.3 %copy-start.6 = (s32[4,16]{1,0:T(4,128)S(1)}, s32[4,16]{1,0:T(4,128)}, u32[]{:S(2)}) copy-start(s32[4,16]{1,0:T(4,128)} %length_any.3) | copy-start | bytes 772
  2.4 3.2 %collective-permute-start = (bf16[1,848,128]{2,1,0:T(8,128)(2,1)S(1)}, bf16[1,848,128]{2,1,0:T(8,128)(2,1)S(1)}, u32[]{:S(2)}, u32[]{:S(2)}) collective-permute-start(bf16[1,848,128]{2,1,0:T(8,128)(2,1)S(1)} %get-tuple-element.22), channel_id=1, source_target_pairs={{0,4},{4,0},{8,12},{12,8},{1,5},{5,1},{9,13},{13,9},{2,6},{6,2},{1... | collective-permute-start | bytes 651272 | tf_op jit(solution)/shard_map/ppermute | solution.py:392
  2.9 12.9 %collective-permute-start.3 = (bf16[1,848,128]{2,1,0:T(8,128)(2,1)S(1)}, bf16[1,848,128]{2,1,0:T(8,128)(2,1)S(1)}, u32[]{:S(2)}, u32[]{:S(2)}) collective-permute-start(bf16[1,848,128]{2,1,0:T(8,128)(2,1)S(1)} %get-tuple-element.23), channel_id=1, source_target_pairs={{0,8},{4,12},{8,0},{12,4},{1,9},{5,13},{9,1},{13,5},{2,10},{6,14},... | collective-permute-start | bytes 651272 | tf_op jit(solution)/shard_map/ppermute | solution.py:392
  5.5 10.3 %collective-permute-start.4 = (bf16[1,848,128]{2,1,0:T(8,128)(2,1)S(1)}, bf16[1,848,128]{2,1,0:T(8,128)(2,1)S(1)}, u32[]{:S(2)}, u32[]{:S(2)}) collective-permute-start(bf16[1,848,128]{2,1,0:T(8,128)(2,1)S(1)} %get-tuple-element.24), channel_id=1, source_target_pairs={{0,12},{4,8},{8,4},{12,0},{1,13},{5,9},{9,5},{13,1},{2,14},{6,10},... | collective-permute-start | bytes 651272 | tf_op jit(solution)/shard_map/ppermute | solution.py:392
  5.6 18.9 %slice-start = ((s8[14680064]{0:T(1024)(128)(4,1)}), s8[4194304]{0:T(1024)(128)(4,1)S(1)}, s32[]{:S(2)}) async-start(s8[14680064]{0:T(1024)(128)(4,1)} %bitcast.2), calls=%async_computation | async-start | bytes 8388608
  5.6 18.8 %slice-start.1 = ((s8[14680064]{0:T(1024)(128)(4,1)}), s8[4194304]{0:T(1024)(128)(4,1)S(1)}, s32[]{:S(2)}) async-start(s8[14680064]{0:T(1024)(128)(4,1)} %bitcast.2), calls=%async_computation.1 | async-start | bytes 8388608
  12.9 11.5 %slice-start.2 = ((s8[14680064]{0:T(1024)(128)(4,1)}), s8[4194304]{0:T(1024)(128)(4,1)S(1)}, s32[]{:S(2)}) async-start(s8[14680064]{0:T(1024)(128)(4,1)} %bitcast.2), calls=%async_computation.2 | async-start | bytes 8388608
  13.0 11.5 %slice-start.3 = ((s8[14680064]{0:T(1024)(128)(4,1)}), s8[2097152]{0:T(1024)(128)(4,1)S(1)}, s32[]{:S(2)}) async-start(s8[14680064]{0:T(1024)(128)(4,1)} %bitcast.2), calls=%async_computation.3 | async-start | bytes 4194304
  13.0 9.8 %collective-permute-start.2 = (bf16[32,4096]{1,0:T(8,128)(2,1)S(1)}, bf16[32,4096]{1,0:T(8,128)(2,1)S(1)}, u32[]{:S(2)}, u32[]{:S(2)}) collective-permute-start(bf16[32,4096]{1,0:T(8,128)(2,1)S(1)} %attend.2.rest_0_), channel_id=1, source_target_pairs={{0,8},{4,12},{8,0},{12,4},{1,9},{5,13},{9,1},{13,5},{2,10},{6,14},... | collective-permute-start | bytes 786440 | tf_op jit(solution)/shard_map/ppermute | solution.py:392
  15.8 8.5 %collective-permute-start.1 = (bf16[32,4096]{1,0:T(8,128)(2,1)S(1)}, bf16[32,4096]{1,0:T(8,128)(2,1)S(1)}, u32[]{:S(2)}, u32[]{:S(2)}) collective-permute-start(bf16[32,4096]{1,0:T(8,128)(2,1)S(1)} %attend.2.rest_0_), channel_id=1, source_target_pairs={{0,4},{4,0},{8,12},{12,8},{1,5},{5,1},{9,13},{13,9},{2,6},{6,2},{1... | collective-permute-start | bytes 786440 | tf_op jit(solution)/shard_map/ppermute | solution.py:392
  22.7 1.7 %collective-permute-start.5 = (bf16[32,4096]{1,0:T(8,128)(2,1)S(1)}, bf16[32,4096]{1,0:T(8,128)(2,1)S(1)}, u32[]{:S(2)}, u32[]{:S(2)}) collective-permute-start(bf16[32,4096]{1,0:T(8,128)(2,1)S(1)} %collective-permute-done.2.rest_2_), channel_id=1, source_target_pairs={{0,4},{4,0},{8,12},{12,8},{1,5},{5,1},{9,13},{13,9},{2,6},{6,2},{1... | collective-permute-start | bytes 786440 | tf_op jit(solution)/shard_map/ppermute | solution.py:392
  23.3 8.3 %collective-permute-start.9 = (bf16[32,4096]{1,0:T(8,128)(2,1)S(1)}, bf16[32,4096]{1,0:T(8,128)(2,1)S(1)}, u32[]{:S(2)}, u32[]{:S(2)}) collective-permute-start(bf16[32,4096]{1,0:T(8,128)(2,1)S(1)} %attend.3.rest_0_), channel_id=1, source_target_pairs={{0,8},{4,12},{8,0},{12,4},{1,9},{5,13},{9,1},{13,5},{2,10},{6,14},... | collective-permute-start | bytes 786440 | tf_op jit(solution)/shard_map/ppermute | solution.py:392
  24.3 13.1 %collective-permute-start.8 = (bf16[32,4096]{1,0:T(8,128)(2,1)S(1)}, bf16[32,4096]{1,0:T(8,128)(2,1)S(1)}, u32[]{:S(2)}, u32[]{:S(2)}) collective-permute-start(bf16[32,4096]{1,0:T(8,128)(2,1)S(1)} %attend.3.rest_0_), channel_id=1, source_target_pairs={{0,4},{4,0},{8,12},{12,8},{1,5},{5,1},{9,13},{13,9},{2,6},{6,2},{1... | collective-permute-start | bytes 786440 | tf_op jit(solution)/shard_map/ppermute | solution.py:392
  25.7 5.8 %collective-permute-start.12 = (bf16[64,896]{1,0:T(8,128)(2,1)S(1)}, bf16[64,896]{1,0:T(8,128)(2,1)S(1)}, u32[]{:S(2)}, u32[]{:S(2)}) collective-permute-start(bf16[64,896]{1,0:T(8,128)(2,1)S(1)} %get-tuple-element.32), channel_id=1, source_target_pairs={{0,1},{1,0},{2,3},{3,2},{4,5},{5,4},{6,7},{7,6},{8,9},{9,8},{10,11... | collective-permute-start | bytes 344072 | tf_op jit(solution)/shard_map/ppermute | solution.py:392
  28.7 6.8 %collective-permute-start.6 = (bf16[64,896]{1,0:T(8,128)(2,1)S(1)}, bf16[64,896]{1,0:T(8,128)(2,1)S(1)}, u32[]{:S(2)}, u32[]{:S(2)}) collective-permute-start(bf16[64,896]{1,0:T(8,128)(2,1)S(1)} %get-tuple-element.27), channel_id=1, source_target_pairs={{0,1},{1,0},{2,3},{3,2},{4,5},{5,4},{6,7},{7,6},{8,9},{9,8},{10,11... | collective-permute-start | bytes 344072 | tf_op jit(solution)/shard_map/ppermute | solution.py:392
  31.6 5.8 %collective-permute-start.10 = (bf16[32,4096]{1,0:T(8,128)(2,1)S(1)}, bf16[32,4096]{1,0:T(8,128)(2,1)S(1)}, u32[]{:S(2)}, u32[]{:S(2)}) collective-permute-start(bf16[32,4096]{1,0:T(8,128)(2,1)S(1)} %collective-permute-done.9.rest_2_), channel_id=1, source_target_pairs={{0,4},{4,0},{8,12},{12,8},{1,5},{5,1},{9,13},{13,9},{2,6},{6,2},{1... | collective-permute-start | bytes 786440 | tf_op jit(solution)/shard_map/ppermute | solution.py:392
  31.6 10.5 %collective-permute-start.13 = (bf16[64,896]{1,0:T(8,128)(2,1)S(1)}, bf16[64,896]{1,0:T(8,128)(2,1)S(1)}, u32[]{:S(2)}, u32[]{:S(2)}) collective-permute-start(bf16[64,896]{1,0:T(8,128)(2,1)S(1)} %add_convert_fusion.5), channel_id=1, source_target_pairs={{0,3},{1,2},{2,1},{3,0},{4,7},{5,6},{6,5},{7,4},{8,11},{9,10},{10,... | collective-permute-start | bytes 344072 | tf_op jit(solution)/shard_map/ppermute | solution.py:392
  35.5 8.9 %collective-permute-start.7 = (bf16[64,896]{1,0:T(8,128)(2,1)S(1)}, bf16[64,896]{1,0:T(8,128)(2,1)S(1)}, u32[]{:S(2)}, u32[]{:S(2)}) collective-permute-start(bf16[64,896]{1,0:T(8,128)(2,1)S(1)} %add_convert_fusion.7), channel_id=1, source_target_pairs={{0,3},{1,2},{2,1},{3,0},{4,7},{5,6},{6,5},{7,4},{8,11},{9,10},{10,... | collective-permute-start | bytes 344072 | tf_op jit(solution)/shard_map/ppermute | solution.py:392
  38.7 7.6 %collective-permute-start.18 = (bf16[64,896]{1,0:T(8,128)(2,1)S(1)}, bf16[64,896]{1,0:T(8,128)(2,1)S(1)}, u32[]{:S(2)}, u32[]{:S(2)}) collective-permute-start(bf16[64,896]{1,0:T(8,128)(2,1)S(1)} %get-tuple-element.36), channel_id=1, source_target_pairs={{0,1},{1,0},{2,3},{3,2},{4,5},{5,4},{6,7},{7,6},{8,9},{9,8},{10,11... | collective-permute-start | bytes 344072 | tf_op jit(solution)/shard_map/ppermute | solution.py:392
  40.0 8.8 %collective-permute-start.15 = (bf16[64,896]{1,0:T(8,128)(2,1)S(1)}, bf16[64,896]{1,0:T(8,128)(2,1)S(1)}, u32[]{:S(2)}, u32[]{:S(2)}) collective-permute-start(bf16[64,896]{1,0:T(8,128)(2,1)S(1)} %get-tuple-element.35), channel_id=1, source_target_pairs={{0,1},{1,0},{2,3},{3,2},{4,5},{5,4},{6,7},{7,6},{8,9},{9,8},{10,11... | collective-permute-start | bytes 344072 | tf_op jit(solution)/shard_map/ppermute | solution.py:392
  42.2 17.9 %collective-permute-start.14 = (bf16[64,896]{1,0:T(8,128)(2,1)S(1)}, bf16[64,896]{1,0:T(8,128)(2,1)S(1)}, u32[]{:S(2)}, u32[]{:S(2)}) collective-permute-start(bf16[64,896]{1,0:T(8,128)(2,1)S(1)} %add_convert_fusion.4.rest_2_), channel_id=1, source_target_pairs={{0,1},{1,0},{2,3},{3,2},{4,5},{5,4},{6,7},{7,6},{8,9},{9,8},{10,11... | collective-permute-start | bytes 344072 | tf_op jit(solution)/shard_map/ppermute | solution.py:392
  44.5 15.6 %collective-permute-start.11 = (bf16[64,896]{1,0:T(8,128)(2,1)S(1)}, bf16[64,896]{1,0:T(8,128)(2,1)S(1)}, u32[]{:S(2)}, u32[]{:S(2)}) collective-permute-start(bf16[64,896]{1,0:T(8,128)(2,1)S(1)} %add_convert_fusion.6.rest_0_), channel_id=1, source_target_pairs={{0,1},{1,0},{2,3},{3,2},{4,5},{5,4},{6,7},{7,6},{8,9},{9,8},{10,11... | collective-permute-start | bytes 344072 | tf_op jit(solution)/shard_map/ppermute | solution.py:392
  46.3 9.4 %collective-permute-start.19 = (bf16[64,896]{1,0:T(8,128)(2,1)S(1)}, bf16[64,896]{1,0:T(8,128)(2,1)S(1)}, u32[]{:S(2)}, u32[]{:S(2)}) collective-permute-start(bf16[64,896]{1,0:T(8,128)(2,1)S(1)} %add_convert_fusion.1), channel_id=1, source_target_pairs={{0,3},{1,2},{2,1},{3,0},{4,7},{5,6},{6,5},{7,4},{8,11},{9,10},{10,... | collective-permute-start | bytes 344072 | tf_op jit(solution)/shard_map/ppermute | solution.py:392
  48.9 8.5 %collective-permute-start.16 = (bf16[64,896]{1,0:T(8,128)(2,1)S(1)}, bf16[64,896]{1,0:T(8,128)(2,1)S(1)}, u32[]{:S(2)}, u32[]{:S(2)}) collective-permute-start(bf16[64,896]{1,0:T(8,128)(2,1)S(1)} %add_convert_fusion.3), channel_id=1, source_target_pairs={{0,3},{1,2},{2,1},{3,0},{4,7},{5,6},{6,5},{7,4},{8,11},{9,10},{10,... | collective-permute-start | bytes 344072 | tf_op jit(solution)/shard_map/ppermute | solution.py:392
  55.8 5.9 %collective-permute-start.20 = (bf16[64,896]{1,0:T(8,128)(2,1)S(1)}, bf16[64,896]{1,0:T(8,128)(2,1)S(1)}, u32[]{:S(2)}, u32[]{:S(2)}) collective-permute-start(bf16[64,896]{1,0:T(8,128)(2,1)S(1)} %add_convert_fusion.rest_6_), channel_id=1, source_target_pairs={{0,1},{1,0},{2,3},{3,2},{4,5},{5,4},{6,7},{7,6},{8,9},{9,8},{10,11... | collective-permute-start | bytes 344072 | tf_op jit(solution)/shard_map/ppermute | solution.py:392
  57.4 5.5 %collective-permute-start.17 = (bf16[64,896]{1,0:T(8,128)(2,1)S(1)}, bf16[64,896]{1,0:T(8,128)(2,1)S(1)}, u32[]{:S(2)}, u32[]{:S(2)}) collective-permute-start(bf16[64,896]{1,0:T(8,128)(2,1)S(1)} %add_convert_fusion.2.rest_4_), channel_id=1, source_target_pairs={{0,1},{1,0},{2,3},{3,2},{4,5},{5,4},{6,7},{7,6},{8,9},{9,8},{10,11... | collective-permute-start | bytes 344072 | tf_op jit(solution)/shard_map/ppermute | solution.py:392

commit v20 on v19

--- a/solution.py
+++ b/solution.py
@@ -550,13 +550,14 @@
         pairs.append(add(keep, incoming))
     crossed = [flip(pair, "head", 3) for pair in pairs]
     last_made = made[-1][2]
-    arrays = []
-    for i, (pair, cross) in enumerate(zip(pairs, crossed)):
-        if i < len(near_made):
-            cross = after(cross, *(last_made,))
+    near_total = jnp.concatenate(
+        [add(pair, after(cross, last_made)) for pair, cross in zip(pairs[: len(near_made)], crossed)], axis=1
+    )
+    arrays = [near_total, flip(near_total, "head", 1)]
+    for pair, cross in list(zip(pairs, crossed))[len(near_made) :]:
         total = add(pair, cross)
         arrays += [total, flip(total, "head", 1)]
-    layout = tuple((row, col) for row, col, _, _ in made)
+    layout = ((0, 0),) + tuple((row, col) for row, col, _, _ in far_made)
     scratch = [pltpu.VMEM((2 * half, columns), jnp.bfloat16)]
     kernel = functools.partial(order_kernel, layout)
     return order(kernel, [smem()] + [vmem()] * (1 + len(arrays)), scratch, [ids, pick] + arrays)

time: 64.8 us -> 67.2 us (1.037)
  waiting for transfers between devices: 12.5 us -> 17.6 us
  starting transfers between devices: 27.2 us -> 24.9 us
    ppermute x21 -> x20, waiting for transfers between devices: 12.5 us -> 17.6 us  [flip(): return lax.ppermute(x, axis, [(i, i ^ distance) for i in range(size)])]
    ppermute x21 -> x20, starting transfers between devices: 27.2 us -> 24.9 us  [flip(): return lax.ppermute(x, axis, [(i, i ^ distance) for i in range(size)])]
  transfers between devices with their start and end apart: 21 -> 20, of which waited for: 6 -> 7; matrix products, arithmetic and copies ran while one was open for 0% -> 0% of each run, Pallas kernels for 32% -> 30%
where the time goes in v20:
time: 67.2 us; the launch traced here: 67.3 us
  starting transfers between devices  24.9 us (37%)
  Pallas kernels  23 us (34%)
  waiting for transfers between devices  17.6 us (26%)
  local copies, waits for them, and re-layouts  1.23 us (2%)
    ppermute x20, starting transfers between devices, flip(): return lax.ppermute(x, axis, [(i, i ^ distance) for i in range(size)])  24.9 us
    ppermute x20, waiting for transfers between devices, flip(): return lax.ppermute(x, axis, [(i, i ^ distance) for i in range(size)])  17.6 us
    pallas_call x2, Pallas kernels, attend(): pl.pallas_call(functools.partial(attend_kernel, sizes, scale, relative, b...  14.2 us
    pallas_call x4, Pallas kernels, project(): pl.pallas_call(functools.partial(project_kernel, first_col), out_shape=[j...  5.12 us
    pallas_call x1, Pallas kernels, order(): pl.pallas_call(kernel, out_shape=jax.ShapeDtypeStruct((steps, sources * r...  1.4 us
  transfers between devices with their start and end apart: 20, of which 7 were waited for; matrix products, arithmetic and copies ran while one was open for 0% of the time, Pallas kernels for 30%

profile of v20, /device:TPU:0, one launch (start us, length us, event | category | flops | bytes accessed | tf_op | source)
XLA Modules:
  0.0 67.3 jit_solution(18045941529318802306)
XLA Ops:
  0.0 0.6 copy-done.7
  0.7 0.4 copy-done.3
  1.1 0.2 copy-done.4
  1.2 1.1 %pack_queries.1 = (bf16[1,848,128]{2,1,0:T(8,128)(2,1)S(1)}, bf16[1,848,128]{2,1,0:T(8,128)(2,1)S(1)}, bf16[1,848,128]{2,1,0:T(8,128)(2,1)S(1)}, bf16[1,848,128]{2,1,0:T(8,128)(2,1)S(1)}) custom-call(s32[1]{0:T(128)} %bitcast.ids_ref.ids_any, s32[64]{0:T(128)S(1)} %copy-done.7, bf16[4,16,32,128]{3,2,1,0:T(8,128)(2,1)S(1)} %copy-done.3, ...), custom_call_target="tpu_custom_call" | custom-call | flops 2000000000 | bytes 6000000 | tf_op jit(solution)/shard_map/pack_queries/pallas_call | solution.py:438
  2.4 0.5 collective-permute-start
  2.9 2.6 %collective-permute-start.3 = (bf16[1,848,128]{2,1,0:T(8,128)(2,1)S(1)}, bf16[1,848,128]{2,1,0:T(8,128)(2,1)S(1)}, u32[]{:S(2)}, u32[]{:S(2)}) collective-permute-start(bf16[1,848,128]{2,1,0:T(8,128)(2,1)S(1)} %get-tuple-element.23), channel_id=1, source_target_pairs={{0,8},{4,12},{8,0},{12,4},{1,9},{5,13},{9,1},{13,5},{2,10},{6,14},... | collective-permute-start | bytes 651272 | tf_op jit(solution)/shard_map/ppermute | solution.py:392
  5.5 0.1 collective-permute-start.4
  5.5 0.0 collective-permute-done.rest_1_
  5.6 0.0 slice-start
  5.6 0.0 slice-start.1
  5.6 7.7 %attend.2.rest_0_ = bf16[32,4096]{1,0:T(8,128)(2,1)S(1)} custom-call(s32[1]{0:T(128)} %bitcast.ids_ref.ids_any, s32[64]{0:T(128)S(1)} %copy-done.7, s32[4,16]{1,0:T(4,128)S(1)} %copy-done.6, bf16[1,848,128]{2,1,0:T(8,128)(2,1)S(1)} %get-tuple-element.21.rest_0_, bf16[1,848,128]{2,1,0:T(8,128)(2,1)S(1)} %collective-permute-done.rest_1_, ...), custom_call_target="tpu_custom_call" | custom-call | flops 8000000000 | bytes 24000000 | tf_op jit(solution)/shard_map/attend/pallas_call | solution.py:456
  13.3 0.0 slice-start.2
  13.3 0.0 slice-start.3
  13.3 1.9 %collective-permute-start.2 = (bf16[32,4096]{1,0:T(8,128)(2,1)S(1)}, bf16[32,4096]{1,0:T(8,128)(2,1)S(1)}, u32[]{:S(2)}, u32[]{:S(2)}) collective-permute-start(bf16[32,4096]{1,0:T(8,128)(2,1)S(1)} %attend.2.rest_0_), channel_id=1, source_target_pairs={{0,8},{4,12},{8,0},{12,4},{1,9},{5,13},{9,1},{13,5},{2,10},{6,14},... | collective-permute-start | bytes 786440 | tf_op jit(solution)/shard_map/ppermute | solution.py:392
  15.2 0.0 collective-permute-start.1
  15.2 0.0 collective-permute-done.3.rest_0_
  15.2 0.6 collective-permute-done.4.rest_1_
  15.8 6.6 %attend.3.rest_0_ = bf16[32,4096]{1,0:T(8,128)(2,1)S(1)} custom-call(s32[1]{0:T(128)} %bitcast.ids_ref.ids_any, s32[64]{0:T(128)S(1)} %copy-done.7, s32[4,16]{1,0:T(4,128)S(1)} %copy-done.6, bf16[1,848,128]{2,1,0:T(8,128)(2,1)S(1)} %collective-permute-done.3.rest_0_, bf16[1,848,128]{2,1,0:T(8,128)(2,1)S(1)} %collective-permute-done.4.rest_1_, ...), custom_call_target="tpu_custom_call" | custom-call | flops 8000000000 | bytes 24000000 | tf_op jit(solution)/shard_map/attend/pallas_call | solution.py:456
  22.4 0.0 collective-permute-done.2.rest_2_
  22.4 1.2 %collective-permute-start.5 = (bf16[32,4096]{1,0:T(8,128)(2,1)S(1)}, bf16[32,4096]{1,0:T(8,128)(2,1)S(1)}, u32[]{:S(2)}, u32[]{:S(2)}) collective-permute-start(bf16[32,4096]{1,0:T(8,128)(2,1)S(1)} %collective-permute-done.2.rest_2_), channel_id=1, source_target_pairs={{0,4},{4,0},{8,12},{12,8},{1,5},{5,1},{9,13},{13,9},{2,6},{6,2},{1... | collective-permute-start | bytes 786440 | tf_op jit(solution)/shard_map/ppermute | solution.py:392
  23.6 1.2 %collective-permute-start.9 = (bf16[32,4096]{1,0:T(8,128)(2,1)S(1)}, bf16[32,4096]{1,0:T(8,128)(2,1)S(1)}, u32[]{:S(2)}, u32[]{:S(2)}) collective-permute-start(bf16[32,4096]{1,0:T(8,128)(2,1)S(1)} %attend.3.rest_0_), channel_id=1, source_target_pairs={{0,8},{4,12},{8,0},{12,4},{1,9},{5,13},{9,1},{13,5},{2,10},{6,14},... | collective-permute-start | bytes 786440 | tf_op jit(solution)/shard_map/ppermute | solution.py:392
  24.8 0.0 collective-permute-done.5.rest_3_
  24.8 1.3 %project_out.4 = (bf16[64,896]{1,0:T(8,128)(2,1)S(1)}, bf16[64,896]{1,0:T(8,128)(2,1)S(1)}) custom-call(s32[1]{0:T(128)} %bitcast.ids_ref.ids_any, bf16[32,4096]{1,0:T(8,128)(2,1)S(1)} %attend.2.rest_0_, bf16[32,4096]{1,0:T(8,128)(2,1)S(1)} %collective-permute-done.1.rest_1_, bf16[32,4096]{1,0:T(8,128)(2,1)S(1)} %collective-permute-done.2.rest_2_, ...), custom_call_target="tpu_custom_call" | custom-call | flops 2000000000 | bytes 6000000 | tf_op jit(solution)/shard_map/project_out/pallas_call | solution.py:509
  26.1 2.1 %collective-permute-start.6 = (bf16[64,896]{1,0:T(8,128)(2,1)S(1)}, bf16[64,896]{1,0:T(8,128)(2,1)S(1)}, u32[]{:S(2)}, u32[]{:S(2)}) collective-permute-start(bf16[64,896]{1,0:T(8,128)(2,1)S(1)} %get-tuple-element.27), channel_id=1, source_target_pairs={{0,1},{1,0},{2,3},{3,2},{4,5},{5,4},{6,7},{7,6},{8,9},{9,8},{10,11... | collective-permute-start | bytes 344072 | tf_op jit(solution)/shard_map/ppermute | solution.py:392
  28.2 1.3 %project_out.6 = (bf16[64,896]{1,0:T(8,128)(2,1)S(1)}, bf16[64,896]{1,0:T(8,128)(2,1)S(1)}) custom-call(s32[1]{0:T(128)} %bitcast.ids_ref.ids_any, bf16[32,4096]{1,0:T(8,128)(2,1)S(1)} %attend.2.rest_0_, bf16[32,4096]{1,0:T(8,128)(2,1)S(1)} %collective-permute-done.1.rest_1_, bf16[32,4096]{1,0:T(8,128)(2,1)S(1)} %collective-permute-done.2.rest_2_, ...), custom_call_target="tpu_custom_call" | custom-call | flops 2000000000 | bytes 6000000 | tf_op jit(solution)/shard_map/project_out/pallas_call | solution.py:509
  29.5 0.1 collective-permute-start.11
  29.6 2.3 %collective-permute-done.9.rest_2_ = bf16[32,4096]{1,0:T(8,128)(2,1)S(1)} collective-permute-done((bf16[32,4096]{1,0:T(8,128)(2,1)S(1)}, bf16[32,4096]{1,0:T(8,128)(2,1)S(1)}, u32[]{:S(2)}, u32[]{:S(2)}) %collective-permute-start.9) | collective-permute-done | bytes 262176 | tf_op jit(solution)/shard_map/ppermute | solution.py:392
  31.9 0.0 collective-permute-done.6
  31.9 4.4 %collective-permute-start.7 = (bf16[64,896]{1,0:T(8,128)(2,1)S(1)}, bf16[64,896]{1,0:T(8,128)(2,1)S(1)}, u32[]{:S(2)}, u32[]{:S(2)}) collective-permute-start(bf16[64,896]{1,0:T(8,128)(2,1)S(1)} %add_convert_fusion.7), channel_id=1, source_target_pairs={{0,3},{1,2},{2,1},{3,0},{4,7},{5,6},{6,5},{7,4},{8,11},{9,10},{10,... | collective-permute-start | bytes 344072 | tf_op jit(solution)/shard_map/ppermute | solution.py:392
  36.3 0.0 collective-permute-done.11
  36.4 1.9 %collective-permute-start.12 = (bf16[64,896]{1,0:T(8,128)(2,1)S(1)}, bf16[64,896]{1,0:T(8,128)(2,1)S(1)}, u32[]{:S(2)}, u32[]{:S(2)}) collective-permute-start(bf16[64,896]{1,0:T(8,128)(2,1)S(1)} %add_convert_fusion.5), channel_id=1, source_target_pairs={{0,3},{1,2},{2,1},{3,0},{4,7},{5,6},{6,5},{7,4},{8,11},{9,10},{10,... | collective-permute-start | bytes 344072 | tf_op jit(solution)/shard_map/ppermute | solution.py:392
  38.2 1.3 %project_out.5 = (bf16[64,896]{1,0:T(8,128)(2,1)S(1)}, bf16[64,896]{1,0:T(8,128)(2,1)S(1)}) custom-call(s32[1]{0:T(128)} %bitcast.ids_ref.ids_any, bf16[32,4096]{1,0:T(8,128)(2,1)S(1)} %attend.3.rest_0_, bf16[32,4096]{1,0:T(8,128)(2,1)S(1)} %collective-permute-done.8.rest_1_, bf16[32,4096]{1,0:T(8,128)(2,1)S(1)} %collective-permute-done.9.rest_2_, ...), custom_call_target="tpu_custom_call" | custom-call | flops 2000000000 | bytes 6000000 | tf_op jit(solution)/shard_map/project_out/pallas_call | solution.py:509
  39.5 0.1 collective-permute-start.17
  39.6 1.3 %project_out.7 = (bf16[64,896]{1,0:T(8,128)(2,1)S(1)}, bf16[64,896]{1,0:T(8,128)(2,1)S(1)}) custom-call(s32[1]{0:T(128)} %bitcast.ids_ref.ids_any, bf16[32,4096]{1,0:T(8,128)(2,1)S(1)} %attend.3.rest_0_, bf16[32,4096]{1,0:T(8,128)(2,1)S(1)} %collective-permute-done.8.rest_1_, bf16[32,4096]{1,0:T(8,128)(2,1)S(1)} %collective-permute-done.9.rest_2_, ...), custom_call_target="tpu_custom_call" | custom-call | flops 2000000000 | bytes 6000000 | tf_op jit(solution)/shard_map/project_out/pallas_call | solution.py:509
  40.9 2.1 %collective-permute-start.14 = (bf16[64,896]{1,0:T(8,128)(2,1)S(1)}, bf16[64,896]{1,0:T(8,128)(2,1)S(1)}, u32[]{:S(2)}, u32[]{:S(2)}) collective-permute-start(bf16[64,896]{1,0:T(8,128)(2,1)S(1)} %get-tuple-element.35), channel_id=1, source_target_pairs={{0,1},{1,0},{2,3},{3,2},{4,5},{5,4},{6,7},{7,6},{8,9},{9,8},{10,11... | collective-permute-start | bytes 344072 | tf_op jit(solution)/shard_map/ppermute | solution.py:392
  43.0 1.3 %collective-permute-done.12 = bf16[64,896]{1,0:T(8,128)(2,1)S(1)} collective-permute-done((bf16[64,896]{1,0:T(8,128)(2,1)S(1)}, bf16[64,896]{1,0:T(8,128)(2,1)S(1)}, u32[]{:S(2)}, u32[]{:S(2)}) %collective-permute-start.12) | collective-permute-done | bytes 114720 | tf_op jit(solution)/shard_map/ppermute | solution.py:392
  44.3 2.8 %collective-permute-start.13 = (bf16[64,1792]{1,0:T(8,128)(2,1)S(1)}, bf16[64,1792]{1,0:T(8,128)(2,1)S(1)}, u32[]{:S(2)}, u32[]{:S(2)}) collective-permute-start(bf16[64,1792]{1,0:T(8,128)(2,1)S(1)} %pad_maximum_fusion.rest_0_), channel_id=1, source_target_pairs={{0,1},{1,0},{2,3},{3,2},{4,5},{5,4},{6,7},{7,6},{8,9},{9,8},{10,11... | collective-permute-start | bytes 688136 | tf_op jit(solution)/shard_map/ppermute | solution.py:392
  47.1 0.0 collective-permute-done.17
  47.2 2.5 %collective-permute-start.18 = (bf16[64,896]{1,0:T(8,128)(2,1)S(1)}, bf16[64,896]{1,0:T(8,128)(2,1)S(1)}, u32[]{:S(2)}, u32[]{:S(2)}) collective-permute-start(bf16[64,896]{1,0:T(8,128)(2,1)S(1)} %add_convert_fusion.1), channel_id=1, source_target_pairs={{0,3},{1,2},{2,1},{3,0},{4,7},{5,6},{6,5},{7,4},{8,11},{9,10},{10,... | collective-permute-start | bytes 344072 | tf_op jit(solution)/shard_map/ppermute | solution.py:392
  49.7 1.4 %collective-permute-start.15 = (bf16[64,896]{1,0:T(8,128)(2,1)S(1)}, bf16[64,896]{1,0:T(8,128)(2,1)S(1)}, u32[]{:S(2)}, u32[]{:S(2)}) collective-permute-start(bf16[64,896]{1,0:T(8,128)(2,1)S(1)} %add_convert_fusion.3), channel_id=1, source_target_pairs={{0,3},{1,2},{2,1},{3,0},{4,7},{5,6},{6,5},{7,4},{8,11},{9,10},{10,... | collective-permute-start | bytes 344072 | tf_op jit(solution)/shard_map/ppermute | solution.py:392
  51.2 7.4 %collective-permute-done.18 = bf16[64,896]{1,0:T(8,128)(2,1)S(1)} collective-permute-done((bf16[64,896]{1,0:T(8,128)(2,1)S(1)}, bf16[64,896]{1,0:T(8,128)(2,1)S(1)}, u32[]{:S(2)}, u32[]{:S(2)}) %collective-permute-start.18) | collective-permute-done | bytes 114720 | tf_op jit(solution)/shard_map/ppermute | solution.py:392
  58.6 0.1 collective-permute-start.19
  58.7 2.3 %collective-permute-done.15 = bf16[64,896]{1,0:T(8,128)(2,1)S(1)} collective-permute-done((bf16[64,896]{1,0:T(8,128)(2,1)S(1)}, bf16[64,896]{1,0:T(8,128)(2,1)S(1)}, u32[]{:S(2)}, u32[]{:S(2)}) %collective-permute-start.15) | collective-permute-done | bytes 114720 | tf_op jit(solution)/shard_map/ppermute | solution.py:392
  61.0 0.1 collective-permute-start.16
  61.1 1.1 %place_rows.1.pick_ref = bf16[4,64,256]{2,1,0:T(8,128)(2,1)S(1)} custom-call(s32[1]{0:T(128)} %bitcast.ids_ref.ids_any, s32[64]{0:T(128)S(1)} %copy-done.7), custom_call_target="tpu_custom_call" | custom-call | flops 100000000 | bytes 300000 | tf_op jit(solution)/shard_map/place_rows/pallas_call | solution.py:416
  62.2 1.5 %collective-permute-done.19.rest_5_ = bf16[64,896]{1,0:T(8,128)(2,1)S(1)} collective-permute-done((bf16[64,896]{1,0:T(8,128)(2,1)S(1)}, bf16[64,896]{1,0:T(8,128)(2,1)S(1)}, u32[]{:S(2)}, u32[]{:S(2)}) %collective-permute-start.19) | collective-permute-done | bytes 114720 | tf_op jit(solution)/shard_map/ppermute | solution.py:392
  63.7 2.2 %collective-permute-done.16.rest_3_ = bf16[64,896]{1,0:T(8,128)(2,1)S(1)} collective-permute-done((bf16[64,896]{1,0:T(8,128)(2,1)S(1)}, bf16[64,896]{1,0:T(8,128)(2,1)S(1)}, u32[]{:S(2)}, u32[]{:S(2)}) %collective-permute-start.16) | collective-permute-done | bytes 114720 | tf_op jit(solution)/shard_map/ppermute | solution.py:392
  65.9 1.4 %order_rows.1 = bf16[4,64,1792]{2,1,0:T(8,128)(2,1)} custom-call(s32[1]{0:T(128)} %bitcast.ids_ref.ids_any, bf16[4,64,256]{2,1,0:T(8,128)(2,1)S(1)} %place_rows.1.pick_ref, bf16[64,1792]{1,0:T(8,128)(2,1)S(1)} %pad_maximum_fusion.rest_0_, bf16[64,1792]{1,0:T(8,128)(2,1)S(1)} %collective-permute-done.13.rest_1_, ...), custom_call_target="tpu_custom_call" | custom-call | flops 2000000000 | bytes 6000000 | tf_op jit(solution)/shard_map/order_rows/pallas_call | solution.py:486
  (36 shorter events, 0.3 us)
Async XLA Ops:
  0.0 0.7 copy-start.7
  0.0 1.1 %copy-start.3 = (bf16[4,16,32,128]{3,2,1,0:T(8,128)(2,1)S(1)}, bf16[4,16,32,128]{3,2,1,0:T(8,128)(2,1)}, u32[]{:S(2)}) copy-start(bf16[4,16,32,128]{3,2,1,0:T(8,128)(2,1)} %nope_ref.1) | copy-start | bytes 1572868
  0.0 1.2 %copy-start.4 = (bf16[4,16,32,64]{3,2,1,0:T(8,128)(2,1)S(1)}, bf16[4,16,32,64]{3,2,1,0:T(8,128)(2,1)}, u32[]{:S(2)}) copy-start(bf16[4,16,32,64]{3,2,1,0:T(8,128)(2,1)} %rope_ref.1) | copy-start | bytes 786436
  0.0 1.2 %copy-start.5 = (bf16[4,16,576]{2,1,0:T(8,128)(2,1)S(1)}, bf16[4,16,576]{2,1,0:T(8,128)(2,1)}, u32[]{:S(2)}) copy-start(bf16[4,16,576]{2,1,0:T(8,128)(2,1)} %fresh_ref.1) | copy-start | bytes 221188
  0.0 5.5 %copy-start.1 = (bf16[32,128,512]{2,1,0:T(8,128)(2,1)S(1)}, bf16[32,128,512]{2,1,0:T(8,128)(2,1)}, u32[]{:S(2)}) copy-start(bf16[32,128,512]{2,1,0:T(8,128)(2,1)} %rest_3_.3) | copy-start | bytes 12582916
  0.0 5.5 %copy-start.2 = (bf16[32,512,128]{2,1,0:T(8,128)(2,1)S(1)}, bf16[32,512,128]{2,1,0:T(8,128)(2,1)}, u32[]{:S(2)}) copy-start(bf16[32,512,128]{2,1,0:T(8,128)(2,1)} %rest_4_.7) | copy-start | bytes 12582916
  1.2 4.3 %copy-start = (bf16[4096,576]{0,1:T(8,128)(2,1)S(1)}, bf16[4096,576]{0,1:T(8,128)(2,1)}, u32[]{:S(2)}) copy-start(bf16[4096,576]{0,1:T(8,128)(2,1)} %param.9) | copy-start | bytes 14155780
  1.2 4.3 %copy-start.6 = (s32[4,16]{1,0:T(4,128)S(1)}, s32[4,16]{1,0:T(4,128)}, u32[]{:S(2)}) copy-start(s32[4,16]{1,0:T(4,128)} %length_any.3) | copy-start | bytes 772
  2.4 3.2 %collective-permute-start = (bf16[1,848,128]{2,1,0:T(8,128)(2,1)S(1)}, bf16[1,848,128]{2,1,0:T(8,128)(2,1)S(1)}, u32[]{:S(2)}, u32[]{:S(2)}) collective-permute-start(bf16[1,848,128]{2,1,0:T(8,128)(2,1)S(1)} %get-tuple-element.22), channel_id=1, source_target_pairs={{0,4},{4,0},{8,12},{12,8},{1,5},{5,1},{9,13},{13,9},{2,6},{6,2},{1... | collective-permute-start | bytes 651272 | tf_op jit(solution)/shard_map/ppermute | solution.py:392
  2.9 12.3 %collective-permute-start.3 = (bf16[1,848,128]{2,1,0:T(8,128)(2,1)S(1)}, bf16[1,848,128]{2,1,0:T(8,128)(2,1)S(1)}, u32[]{:S(2)}, u32[]{:S(2)}) collective-permute-start(bf16[1,848,128]{2,1,0:T(8,128)(2,1)S(1)} %get-tuple-element.23), channel_id=1, source_target_pairs={{0,8},{4,12},{8,0},{12,4},{1,9},{5,13},{9,1},{13,5},{2,10},{6,14},... | collective-permute-start | bytes 651272 | tf_op jit(solution)/shard_map/ppermute | solution.py:392
  5.5 10.3 %collective-permute-start.4 = (bf16[1,848,128]{2,1,0:T(8,128)(2,1)S(1)}, bf16[1,848,128]{2,1,0:T(8,128)(2,1)S(1)}, u32[]{:S(2)}, u32[]{:S(2)}) collective-permute-start(bf16[1,848,128]{2,1,0:T(8,128)(2,1)S(1)} %get-tuple-element.24), channel_id=1, source_target_pairs={{0,12},{4,8},{8,4},{12,0},{1,13},{5,9},{9,5},{13,1},{2,14},{6,10},... | collective-permute-start | bytes 651272 | tf_op jit(solution)/shard_map/ppermute | solution.py:392
  5.6 19.2 %slice-start = ((s8[14680064]{0:T(1024)(128)(4,1)}), s8[4194304]{0:T(1024)(128)(4,1)S(1)}, s32[]{:S(2)}) async-start(s8[14680064]{0:T(1024)(128)(4,1)} %bitcast.2), calls=%async_computation | async-start | bytes 8388608
  5.6 19.2 %slice-start.1 = ((s8[14680064]{0:T(1024)(128)(4,1)}), s8[4194304]{0:T(1024)(128)(4,1)S(1)}, s32[]{:S(2)}) async-start(s8[14680064]{0:T(1024)(128)(4,1)} %bitcast.2), calls=%async_computation.1 | async-start | bytes 8388608
  13.3 11.5 %slice-start.2 = ((s8[14680064]{0:T(1024)(128)(4,1)}), s8[4194304]{0:T(1024)(128)(4,1)S(1)}, s32[]{:S(2)}) async-start(s8[14680064]{0:T(1024)(128)(4,1)} %bitcast.2), calls=%async_computation.2 | async-start | bytes 8388608
  13.3 11.5 %slice-start.3 = ((s8[14680064]{0:T(1024)(128)(4,1)}), s8[2097152]{0:T(1024)(128)(4,1)S(1)}, s32[]{:S(2)}) async-start(s8[14680064]{0:T(1024)(128)(4,1)} %bitcast.2), calls=%async_computation.3 | async-start | bytes 4194304
  13.3 9.1 %collective-permute-start.2 = (bf16[32,4096]{1,0:T(8,128)(2,1)S(1)}, bf16[32,4096]{1,0:T(8,128)(2,1)S(1)}, u32[]{:S(2)}, u32[]{:S(2)}) collective-permute-start(bf16[32,4096]{1,0:T(8,128)(2,1)S(1)} %attend.2.rest_0_), channel_id=1, source_target_pairs={{0,8},{4,12},{8,0},{12,4},{1,9},{5,13},{9,1},{13,5},{2,10},{6,14},... | collective-permute-start | bytes 786440 | tf_op jit(solution)/shard_map/ppermute | solution.py:392
  15.2 9.6 %collective-permute-start.1 = (bf16[32,4096]{1,0:T(8,128)(2,1)S(1)}, bf16[32,4096]{1,0:T(8,128)(2,1)S(1)}, u32[]{:S(2)}, u32[]{:S(2)}) collective-permute-start(bf16[32,4096]{1,0:T(8,128)(2,1)S(1)} %attend.2.rest_0_), channel_id=1, source_target_pairs={{0,4},{4,0},{8,12},{12,8},{1,5},{5,1},{9,13},{13,9},{2,6},{6,2},{1... | collective-permute-start | bytes 786440 | tf_op jit(solution)/shard_map/ppermute | solution.py:392
  22.4 2.4 %collective-permute-start.5 = (bf16[32,4096]{1,0:T(8,128)(2,1)S(1)}, bf16[32,4096]{1,0:T(8,128)(2,1)S(1)}, u32[]{:S(2)}, u32[]{:S(2)}) collective-permute-start(bf16[32,4096]{1,0:T(8,128)(2,1)S(1)} %collective-permute-done.2.rest_2_), channel_id=1, source_target_pairs={{0,4},{4,0},{8,12},{12,8},{1,5},{5,1},{9,13},{13,9},{2,6},{6,2},{1... | collective-permute-start | bytes 786440 | tf_op jit(solution)/shard_map/ppermute | solution.py:392
  23.6 8.3 %collective-permute-start.9 = (bf16[32,4096]{1,0:T(8,128)(2,1)S(1)}, bf16[32,4096]{1,0:T(8,128)(2,1)S(1)}, u32[]{:S(2)}, u32[]{:S(2)}) collective-permute-start(bf16[32,4096]{1,0:T(8,128)(2,1)S(1)} %attend.3.rest_0_), channel_id=1, source_target_pairs={{0,8},{4,12},{8,0},{12,4},{1,9},{5,13},{9,1},{13,5},{2,10},{6,14},... | collective-permute-start | bytes 786440 | tf_op jit(solution)/shard_map/ppermute | solution.py:392
  24.8 13.5 %collective-permute-start.8 = (bf16[32,4096]{1,0:T(8,128)(2,1)S(1)}, bf16[32,4096]{1,0:T(8,128)(2,1)S(1)}, u32[]{:S(2)}, u32[]{:S(2)}) collective-permute-start(bf16[32,4096]{1,0:T(8,128)(2,1)S(1)} %attend.3.rest_0_), channel_id=1, source_target_pairs={{0,4},{4,0},{8,12},{12,8},{1,5},{5,1},{9,13},{13,9},{2,6},{6,2},{1... | collective-permute-start | bytes 786440 | tf_op jit(solution)/shard_map/ppermute | solution.py:392
  26.1 5.8 %collective-permute-start.6 = (bf16[64,896]{1,0:T(8,128)(2,1)S(1)}, bf16[64,896]{1,0:T(8,128)(2,1)S(1)}, u32[]{:S(2)}, u32[]{:S(2)}) collective-permute-start(bf16[64,896]{1,0:T(8,128)(2,1)S(1)} %get-tuple-element.27), channel_id=1, source_target_pairs={{0,1},{1,0},{2,3},{3,2},{4,5},{5,4},{6,7},{7,6},{8,9},{9,8},{10,11... | collective-permute-start | bytes 344072 | tf_op jit(solution)/shard_map/ppermute | solution.py:392
  29.5 6.8 %collective-permute-start.11 = (bf16[64,896]{1,0:T(8,128)(2,1)S(1)}, bf16[64,896]{1,0:T(8,128)(2,1)S(1)}, u32[]{:S(2)}, u32[]{:S(2)}) collective-permute-start(bf16[64,896]{1,0:T(8,128)(2,1)S(1)} %get-tuple-element.32), channel_id=1, source_target_pairs={{0,1},{1,0},{2,3},{3,2},{4,5},{5,4},{6,7},{7,6},{8,9},{9,8},{10,11... | collective-permute-start | bytes 344072 | tf_op jit(solution)/shard_map/ppermute | solution.py:392
  31.9 6.3 %collective-permute-start.10 = (bf16[32,4096]{1,0:T(8,128)(2,1)S(1)}, bf16[32,4096]{1,0:T(8,128)(2,1)S(1)}, u32[]{:S(2)}, u32[]{:S(2)}) collective-permute-start(bf16[32,4096]{1,0:T(8,128)(2,1)S(1)} %collective-permute-done.9.rest_2_), channel_id=1, source_target_pairs={{0,4},{4,0},{8,12},{12,8},{1,5},{5,1},{9,13},{13,9},{2,6},{6,2},{1... | collective-permute-start | bytes 786440 | tf_op jit(solution)/shard_map/ppermute | solution.py:392
  31.9 11.0 %collective-permute-start.7 = (bf16[64,896]{1,0:T(8,128)(2,1)S(1)}, bf16[64,896]{1,0:T(8,128)(2,1)S(1)}, u32[]{:S(2)}, u32[]{:S(2)}) collective-permute-start(bf16[64,896]{1,0:T(8,128)(2,1)S(1)} %add_convert_fusion.7), channel_id=1, source_target_pairs={{0,3},{1,2},{2,1},{3,0},{4,7},{5,6},{6,5},{7,4},{8,11},{9,10},{10,... | collective-permute-start | bytes 344072 | tf_op jit(solution)/shard_map/ppermute | solution.py:392
  36.4 7.9 %collective-permute-start.12 = (bf16[64,896]{1,0:T(8,128)(2,1)S(1)}, bf16[64,896]{1,0:T(8,128)(2,1)S(1)}, u32[]{:S(2)}, u32[]{:S(2)}) collective-permute-start(bf16[64,896]{1,0:T(8,128)(2,1)S(1)} %add_convert_fusion.5), channel_id=1, source_target_pairs={{0,3},{1,2},{2,1},{3,0},{4,7},{5,6},{6,5},{7,4},{8,11},{9,10},{10,... | collective-permute-start | bytes 344072 | tf_op jit(solution)/shard_map/ppermute | solution.py:392
  39.5 7.6 %collective-permute-start.17 = (bf16[64,896]{1,0:T(8,128)(2,1)S(1)}, bf16[64,896]{1,0:T(8,128)(2,1)S(1)}, u32[]{:S(2)}, u32[]{:S(2)}) collective-permute-start(bf16[64,896]{1,0:T(8,128)(2,1)S(1)} %get-tuple-element.36), channel_id=1, source_target_pairs={{0,1},{1,0},{2,3},{3,2},{4,5},{5,4},{6,7},{7,6},{8,9},{9,8},{10,11... | collective-permute-start | bytes 344072 | tf_op jit(solution)/shard_map/ppermute | solution.py:392
  40.9 8.8 %collective-permute-start.14 = (bf16[64,896]{1,0:T(8,128)(2,1)S(1)}, bf16[64,896]{1,0:T(8,128)(2,1)S(1)}, u32[]{:S(2)}, u32[]{:S(2)}) collective-permute-start(bf16[64,896]{1,0:T(8,128)(2,1)S(1)} %get-tuple-element.35), channel_id=1, source_target_pairs={{0,1},{1,0},{2,3},{3,2},{4,5},{5,4},{6,7},{7,6},{8,9},{9,8},{10,11... | collective-permute-start | bytes 344072 | tf_op jit(solution)/shard_map/ppermute | solution.py:392
  44.3 17.9 %collective-permute-start.13 = (bf16[64,1792]{1,0:T(8,128)(2,1)S(1)}, bf16[64,1792]{1,0:T(8,128)(2,1)S(1)}, u32[]{:S(2)}, u32[]{:S(2)}) collective-permute-start(bf16[64,1792]{1,0:T(8,128)(2,1)S(1)} %pad_maximum_fusion.rest_0_), channel_id=1, source_target_pairs={{0,1},{1,0},{2,3},{3,2},{4,5},{5,4},{6,7},{7,6},{8,9},{9,8},{10,11... | collective-permute-start | bytes 688136 | tf_op jit(solution)/shard_map/ppermute | solution.py:392
  47.2 11.4 %collective-permute-start.18 = (bf16[64,896]{1,0:T(8,128)(2,1)S(1)}, bf16[64,896]{1,0:T(8,128)(2,1)S(1)}, u32[]{:S(2)}, u32[]{:S(2)}) collective-permute-start(bf16[64,896]{1,0:T(8,128)(2,1)S(1)} %add_convert_fusion.1), channel_id=1, source_target_pairs={{0,3},{1,2},{2,1},{3,0},{4,7},{5,6},{6,5},{7,4},{8,11},{9,10},{10,... | collective-permute-start | bytes 344072 | tf_op jit(solution)/shard_map/ppermute | solution.py:392
  49.7 11.3 %collective-permute-start.15 = (bf16[64,896]{1,0:T(8,128)(2,1)S(1)}, bf16[64,896]{1,0:T(8,128)(2,1)S(1)}, u32[]{:S(2)}, u32[]{:S(2)}) collective-permute-start(bf16[64,896]{1,0:T(8,128)(2,1)S(1)} %add_convert_fusion.3), channel_id=1, source_target_pairs={{0,3},{1,2},{2,1},{3,0},{4,7},{5,6},{6,5},{7,4},{8,11},{9,10},{10,... | collective-permute-start | bytes 344072 | tf_op jit(solution)/shard_map/ppermute | solution.py:392
  58.6 5.1 %collective-permute-start.19 = (bf16[64,896]{1,0:T(8,128)(2,1)S(1)}, bf16[64,896]{1,0:T(8,128)(2,1)S(1)}, u32[]{:S(2)}, u32[]{:S(2)}) collective-permute-start(bf16[64,896]{1,0:T(8,128)(2,1)S(1)} %add_convert_fusion.rest_4_), channel_id=1, source_target_pairs={{0,1},{1,0},{2,3},{3,2},{4,5},{5,4},{6,7},{7,6},{8,9},{9,8},{10,11... | collective-permute-start | bytes 344072 | tf_op jit(solution)/shard_map/ppermute | solution.py:392
  61.0 4.9 %collective-permute-start.16 = (bf16[64,896]{1,0:T(8,128)(2,1)S(1)}, bf16[64,896]{1,0:T(8,128)(2,1)S(1)}, u32[]{:S(2)}, u32[]{:S(2)}) collective-permute-start(bf16[64,896]{1,0:T(8,128)(2,1)S(1)} %add_convert_fusion.2.rest_2_), channel_id=1, source_target_pairs={{0,1},{1,0},{2,3},{3,2},{4,5},{5,4},{6,7},{7,6},{8,9},{9,8},{10,11... | collective-permute-start | bytes 344072 | tf_op jit(solution)/shard_map/ppermute | solution.py:392

commit v21 on v19

--- a/solution.py
+++ b/solution.py
@@ -543,17 +543,19 @@
 
     near_made = cut(near, 0, (1, 1))
     pairs = [add(near_made[0][2], near_made[0][3])]
-    far = [far_rows, flip(far_rows, "seq", 1), far_across, flip(far_across, "seq", 1)]
+    relayed = after(far_across, near_made[1][2])
+    far = [far_rows, flip(far_rows, "seq", 1), far_across, flip(relayed, "seq", 1)]
     far_made = cut(far, half, (1, 1))
     made = near_made + far_made
     for i, (_, _, keep, incoming) in enumerate(made[1:], 1):
+        if i == 1: incoming = after(incoming, made[2][2])
         pairs.append(add(keep, incoming))
     crossed = [flip(pair, "head", 3) for pair in pairs]
     last_made = made[-1][2]
     arrays = []
     for i, (pair, cross) in enumerate(zip(pairs, crossed)):
         if i < len(near_made):
-            cross = after(cross, *(last_made,))
+            cross = after(cross, *(pairs[len(near_made)],))
         total = add(pair, cross)
         arrays += [total, flip(total, "head", 1)]
     layout = tuple((row, col) for row, col, _, _ in made)

time: 64.8 us -> 67.5 us (1.042)
  waiting for transfers between devices: 12.5 us -> 16.3 us
  starting transfers between devices: 27.2 us -> 26.5 us
    ppermute x21, waiting for transfers between devices: 12.5 us -> 16.3 us  [flip(): return lax.ppermute(x, axis, [(i, i ^ distance) for i in range(size)])]
    ppermute x21, starting transfers between devices: 27.2 us -> 26.5 us  [flip(): return lax.ppermute(x, axis, [(i, i ^ distance) for i in range(size)])]
  transfers between devices with their start and end apart: 21 -> 21, of which waited for: 6 -> 8; matrix products, arithmetic and copies ran while one was open for 0% -> 0% of each run, Pallas kernels for 32% -> 30%
where the time goes in v21:
time: 67.5 us; the launch traced here: 67.2 us
  starting transfers between devices  26.5 us (39%)
  Pallas kernels  22.7 us (34%)
  waiting for transfers between devices  16.3 us (24%)
  local copies, waits for them, and re-layouts  1.23 us (2%)
    ppermute x21, starting transfers between devices, flip(): return lax.ppermute(x, axis, [(i, i ^ distance) for i in range(size)])  26.5 us
    ppermute x21, waiting for transfers between devices, flip(): return lax.ppermute(x, axis, [(i, i ^ distance) for i in range(size)])  16.3 us
    pallas_call x2, Pallas kernels, attend(): pl.pallas_call(functools.partial(attend_kernel, sizes, scale, relative, b...  13.9 us
    pallas_call x4, Pallas kernels, project(): pl.pallas_call(functools.partial(project_kernel, first_col), out_shape=[j...  5.12 us
    pallas_call x1, Pallas kernels, order(): pl.pallas_call(kernel, out_shape=jax.ShapeDtypeStruct((steps, sources * r...  1.41 us
  transfers between devices with their start and end apart: 21, of which 8 were waited for; matrix products, arithmetic and copies ran while one was open for 0% of the time, Pallas kernels for 30%

profile of v21, /device:TPU:0, one launch (start us, length us, event | category | flops | bytes accessed | tf_op | source)
XLA Modules:
  0.0 67.2 jit_solution(3656280095252181359)
XLA Ops:
  0.0 0.6 copy-done.7
  0.7 0.4 copy-done.3
  1.1 0.2 copy-done.4
  1.2 1.1 %pack_queries.1 = (bf16[1,848,128]{2,1,0:T(8,128)(2,1)S(1)}, bf16[1,848,128]{2,1,0:T(8,128)(2,1)S(1)}, bf16[1,848,128]{2,1,0:T(8,128)(2,1)S(1)}, bf16[1,848,128]{2,1,0:T(8,128)(2,1)S(1)}) custom-call(s32[1]{0:T(128)} %bitcast.ids_ref.ids_any, s32[64]{0:T(128)S(1)} %copy-done.7, bf16[4,16,32,128]{3,2,1,0:T(8,128)(2,1)S(1)} %copy-done.3, ...), custom_call_target="tpu_custom_call" | custom-call | flops 2000000000 | bytes 6000000 | tf_op jit(solution)/shard_map/pack_queries/pallas_call | solution.py:438
  2.4 0.5 collective-permute-start
  2.9 2.6 %collective-permute-start.3 = (bf16[1,848,128]{2,1,0:T(8,128)(2,1)S(1)}, bf16[1,848,128]{2,1,0:T(8,128)(2,1)S(1)}, u32[]{:S(2)}, u32[]{:S(2)}) collective-permute-start(bf16[1,848,128]{2,1,0:T(8,128)(2,1)S(1)} %get-tuple-element.25), channel_id=1, source_target_pairs={{0,8},{4,12},{8,0},{12,4},{1,9},{5,13},{9,1},{13,5},{2,10},{6,14},... | collective-permute-start | bytes 651272 | tf_op jit(solution)/shard_map/ppermute | solution.py:392
  5.5 0.1 collective-permute-start.4
  5.5 0.0 collective-permute-done.rest_1_
  5.6 0.0 slice-start
  5.6 0.0 slice-start.1
  5.6 6.4 %attend.2.rest_0_ = bf16[32,4096]{1,0:T(8,128)(2,1)S(1)} custom-call(s32[1]{0:T(128)} %bitcast.ids_ref.ids_any, s32[64]{0:T(128)S(1)} %copy-done.7, s32[4,16]{1,0:T(4,128)S(1)} %copy-done.6, bf16[1,848,128]{2,1,0:T(8,128)(2,1)S(1)} %get-tuple-element.23.rest_0_, bf16[1,848,128]{2,1,0:T(8,128)(2,1)S(1)} %collective-permute-done.rest_1_, ...), custom_call_target="tpu_custom_call" | custom-call | flops 8000000000 | bytes 24000000 | tf_op jit(solution)/shard_map/attend/pallas_call | solution.py:456
  12.0 0.0 slice-start.2
  12.0 1.2 %collective-permute-start.1 = (bf16[32,4096]{1,0:T(8,128)(2,1)S(1)}, bf16[32,4096]{1,0:T(8,128)(2,1)S(1)}, u32[]{:S(2)}, u32[]{:S(2)}) collective-permute-start(bf16[32,4096]{1,0:T(8,128)(2,1)S(1)} %attend.2.rest_0_), channel_id=1, source_target_pairs={{0,4},{4,0},{8,12},{12,8},{1,5},{5,1},{9,13},{13,9},{2,6},{6,2},{1... | collective-permute-start | bytes 786440 | tf_op jit(solution)/shard_map/ppermute | solution.py:392
  13.2 2.0 %collective-permute-start.2 = (bf16[32,4096]{1,0:T(8,128)(2,1)S(1)}, bf16[32,4096]{1,0:T(8,128)(2,1)S(1)}, u32[]{:S(2)}, u32[]{:S(2)}) collective-permute-start(bf16[32,4096]{1,0:T(8,128)(2,1)S(1)} %attend.2.rest_0_), channel_id=1, source_target_pairs={{0,8},{4,12},{8,0},{12,4},{1,9},{5,13},{9,1},{13,5},{2,10},{6,14},... | collective-permute-start | bytes 786440 | tf_op jit(solution)/shard_map/ppermute | solution.py:392
  15.3 0.5 collective-permute-done.4.rest_1_
  15.8 7.5 %attend.3.rest_0_ = bf16[32,4096]{1,0:T(8,128)(2,1)S(1)} custom-call(s32[1]{0:T(128)} %bitcast.ids_ref.ids_any, s32[64]{0:T(128)S(1)} %copy-done.7, s32[4,16]{1,0:T(4,128)S(1)} %copy-done.6, bf16[1,848,128]{2,1,0:T(8,128)(2,1)S(1)} %collective-permute-done.3.rest_0_, bf16[1,848,128]{2,1,0:T(8,128)(2,1)S(1)} %collective-permute-done.4.rest_1_, ...), custom_call_target="tpu_custom_call" | custom-call | flops 8000000000 | bytes 24000000 | tf_op jit(solution)/shard_map/attend/pallas_call | solution.py:456
  23.3 0.0 collective-permute-done.2.rest_2_
  23.3 0.1 collective-permute-start.5
  23.4 0.5 collective-permute-start.8
  23.9 1.4 %collective-permute-start.9 = (bf16[32,4096]{1,0:T(8,128)(2,1)S(1)}, bf16[32,4096]{1,0:T(8,128)(2,1)S(1)}, u32[]{:S(2)}, u32[]{:S(2)}) collective-permute-start(bf16[32,4096]{1,0:T(8,128)(2,1)S(1)} %attend.3.rest_0_), channel_id=1, source_target_pairs={{0,8},{4,12},{8,0},{12,4},{1,9},{5,13},{9,1},{13,5},{2,10},{6,14},... | collective-permute-start | bytes 786440 | tf_op jit(solution)/shard_map/ppermute | solution.py:392
  25.4 1.3 %project_out.4 = (bf16[64,896]{1,0:T(8,128)(2,1)S(1)}, bf16[64,896]{1,0:T(8,128)(2,1)S(1)}) custom-call(s32[1]{0:T(128)} %bitcast.ids_ref.ids_any, bf16[32,4096]{1,0:T(8,128)(2,1)S(1)} %attend.2.rest_0_, bf16[32,4096]{1,0:T(8,128)(2,1)S(1)} %collective-permute-done.1.rest_1_, bf16[32,4096]{1,0:T(8,128)(2,1)S(1)} %collective-permute-done.2.rest_2_, ...), custom_call_target="tpu_custom_call" | custom-call | flops 2000000000 | bytes 6000000 | tf_op jit(solution)/shard_map/project_out/pallas_call | solution.py:509
  26.6 1.7 %collective-permute-start.6 = (bf16[64,896]{1,0:T(8,128)(2,1)S(1)}, bf16[64,896]{1,0:T(8,128)(2,1)S(1)}, u32[]{:S(2)}, u32[]{:S(2)}) collective-permute-start(bf16[64,896]{1,0:T(8,128)(2,1)S(1)} %get-tuple-element.29), channel_id=1, source_target_pairs={{0,1},{1,0},{2,3},{3,2},{4,5},{5,4},{6,7},{7,6},{8,9},{9,8},{10,11... | collective-permute-start | bytes 344072 | tf_op jit(solution)/shard_map/ppermute | solution.py:392
  28.3 1.3 %project_out.5 = (bf16[64,896]{1,0:T(8,128)(2,1)S(1)}, bf16[64,896]{1,0:T(8,128)(2,1)S(1)}) custom-call(s32[1]{0:T(128)} %bitcast.ids_ref.ids_any, bf16[32,4096]{1,0:T(8,128)(2,1)S(1)} %attend.2.rest_0_, bf16[32,4096]{1,0:T(8,128)(2,1)S(1)} %collective-permute-done.1.rest_1_, bf16[32,4096]{1,0:T(8,128)(2,1)S(1)} %collective-permute-done.2.rest_2_, ...), custom_call_target="tpu_custom_call" | custom-call | flops 2000000000 | bytes 6000000 | tf_op jit(solution)/shard_map/project_out/pallas_call | solution.py:509
  29.6 2.6 %collective-permute-done.9.rest_2_ = bf16[32,4096]{1,0:T(8,128)(2,1)S(1)} collective-permute-done((bf16[32,4096]{1,0:T(8,128)(2,1)S(1)}, bf16[32,4096]{1,0:T(8,128)(2,1)S(1)}, u32[]{:S(2)}, u32[]{:S(2)}) %collective-permute-start.9) | collective-permute-done | bytes 262176 | tf_op jit(solution)/shard_map/ppermute | solution.py:392
  32.2 0.0 collective-permute-start.10
  32.2 1.6 %collective-permute-start.13 = (bf16[64,896]{1,0:T(8,128)(2,1)S(1)}, bf16[64,896]{1,0:T(8,128)(2,1)S(1)}, u32[]{:S(2)}, u32[]{:S(2)}) collective-permute-start(bf16[64,896]{1,0:T(8,128)(2,1)S(1)} %get-tuple-element.36), channel_id=1, source_target_pairs={{0,1},{1,0},{2,3},{3,2},{4,5},{5,4},{6,7},{7,6},{8,9},{9,8},{10,11... | collective-permute-start | bytes 344072 | tf_op jit(solution)/shard_map/ppermute | solution.py:392
  33.9 0.0 collective-permute-done.6
  33.9 2.5 %collective-permute-start.7 = (bf16[64,896]{1,0:T(8,128)(2,1)S(1)}, bf16[64,896]{1,0:T(8,128)(2,1)S(1)}, u32[]{:S(2)}, u32[]{:S(2)}) collective-permute-start(bf16[64,896]{1,0:T(8,128)(2,1)S(1)} %add_convert_fusion.7), channel_id=1, source_target_pairs={{0,3},{1,2},{2,1},{3,0},{4,7},{5,6},{6,5},{7,4},{8,11},{9,10},{10,... | collective-permute-start | bytes 344072 | tf_op jit(solution)/shard_map/ppermute | solution.py:392
  36.4 1.3 %project_out.6 = (bf16[64,896]{1,0:T(8,128)(2,1)S(1)}, bf16[64,896]{1,0:T(8,128)(2,1)S(1)}) custom-call(s32[1]{0:T(128)} %bitcast.ids_ref.ids_any, bf16[32,4096]{1,0:T(8,128)(2,1)S(1)} %attend.3.rest_0_, bf16[32,4096]{1,0:T(8,128)(2,1)S(1)} %collective-permute-done.8.rest_1_, bf16[32,4096]{1,0:T(8,128)(2,1)S(1)} %collective-permute-done.9.rest_2_, ...), custom_call_target="tpu_custom_call" | custom-call | flops 2000000000 | bytes 6000000 | tf_op jit(solution)/shard_map/project_out/pallas_call | solution.py:509
  37.7 0.8 %collective-permute-start.11 = (bf16[64,896]{1,0:T(8,128)(2,1)S(1)}, bf16[64,896]{1,0:T(8,128)(2,1)S(1)}, u32[]{:S(2)}, u32[]{:S(2)}) collective-permute-start(bf16[64,896]{1,0:T(8,128)(2,1)S(1)} %get-tuple-element.34), channel_id=1, source_target_pairs={{0,1},{1,0},{2,3},{3,2},{4,5},{5,4},{6,7},{7,6},{8,9},{9,8},{10,11... | collective-permute-start | bytes 344072 | tf_op jit(solution)/shard_map/ppermute | solution.py:392
  38.5 5.2 %collective-permute-start.14 = (bf16[64,896]{1,0:T(8,128)(2,1)S(1)}, bf16[64,896]{1,0:T(8,128)(2,1)S(1)}, u32[]{:S(2)}, u32[]{:S(2)}) collective-permute-start(bf16[64,896]{1,0:T(8,128)(2,1)S(1)} %add_convert_fusion.4), channel_id=1, source_target_pairs={{0,3},{1,2},{2,1},{3,0},{4,7},{5,6},{6,5},{7,4},{8,11},{9,10},{10,... | collective-permute-start | bytes 344072 | tf_op jit(solution)/shard_map/ppermute | solution.py:392
  43.7 1.3 %project_out.7 = (bf16[64,896]{1,0:T(8,128)(2,1)S(1)}, bf16[64,896]{1,0:T(8,128)(2,1)S(1)}) custom-call(s32[1]{0:T(128)} %bitcast.ids_ref.ids_any, bf16[32,4096]{1,0:T(8,128)(2,1)S(1)} %attend.3.rest_0_, bf16[32,4096]{1,0:T(8,128)(2,1)S(1)} %collective-permute-done.8.rest_1_, bf16[32,4096]{1,0:T(8,128)(2,1)S(1)} %collective-permute-done.9.rest_2_, ...), custom_call_target="tpu_custom_call" | custom-call | flops 2000000000 | bytes 6000000 | tf_op jit(solution)/shard_map/project_out/pallas_call | solution.py:509
  45.0 0.1 collective-permute-start.18
  45.1 0.7 %collective-permute-done.11 = bf16[64,896]{1,0:T(8,128)(2,1)S(1)} collective-permute-done((bf16[64,896]{1,0:T(8,128)(2,1)S(1)}, bf16[64,896]{1,0:T(8,128)(2,1)S(1)}, u32[]{:S(2)}, u32[]{:S(2)}) %collective-permute-start.11) | collective-permute-done | bytes 114720 | tf_op jit(solution)/shard_map/ppermute | solution.py:392
  45.8 1.9 %collective-permute-start.16 = (bf16[64,896]{1,0:T(8,128)(2,1)S(1)}, bf16[64,896]{1,0:T(8,128)(2,1)S(1)}, u32[]{:S(2)}, u32[]{:S(2)}) collective-permute-start(bf16[64,896]{1,0:T(8,128)(2,1)S(1)} %add_convert_fusion.6), channel_id=1, source_target_pairs={{0,3},{1,2},{2,1},{3,0},{4,7},{5,6},{6,5},{7,4},{8,11},{9,10},{10,... | collective-permute-start | bytes 344072 | tf_op jit(solution)/shard_map/ppermute | solution.py:392
  47.8 0.1 collective-permute-start.12
  47.9 2.1 %collective-permute-start.15 = (bf16[64,896]{1,0:T(8,128)(2,1)S(1)}, bf16[64,896]{1,0:T(8,128)(2,1)S(1)}, u32[]{:S(2)}, u32[]{:S(2)}) collective-permute-start(bf16[64,896]{1,0:T(8,128)(2,1)S(1)} %add_convert_fusion.3.rest_2_), channel_id=1, source_target_pairs={{0,1},{1,0},{2,3},{3,2},{4,5},{5,4},{6,7},{7,6},{8,9},{9,8},{10,11... | collective-permute-start | bytes 344072 | tf_op jit(solution)/shard_map/ppermute | solution.py:392
  50.0 1.3 %collective-permute-done.18 = bf16[64,896]{1,0:T(8,128)(2,1)S(1)} collective-permute-done((bf16[64,896]{1,0:T(8,128)(2,1)S(1)}, bf16[64,896]{1,0:T(8,128)(2,1)S(1)}, u32[]{:S(2)}, u32[]{:S(2)}) %collective-permute-start.18) | collective-permute-done | bytes 114720 | tf_op jit(solution)/shard_map/ppermute | solution.py:392
  51.3 0.8 %collective-permute-start.19 = (bf16[64,896]{1,0:T(8,128)(2,1)S(1)}, bf16[64,896]{1,0:T(8,128)(2,1)S(1)}, u32[]{:S(2)}, u32[]{:S(2)}) collective-permute-start(bf16[64,896]{1,0:T(8,128)(2,1)S(1)} %add_convert_fusion.1), channel_id=1, source_target_pairs={{0,3},{1,2},{2,1},{3,0},{4,7},{5,6},{6,5},{7,4},{8,11},{9,10},{10,... | collective-permute-start | bytes 344072 | tf_op jit(solution)/shard_map/ppermute | solution.py:392
  52.1 1.7 %collective-permute-done.16 = bf16[64,896]{1,0:T(8,128)(2,1)S(1)} collective-permute-done((bf16[64,896]{1,0:T(8,128)(2,1)S(1)}, bf16[64,896]{1,0:T(8,128)(2,1)S(1)}, u32[]{:S(2)}, u32[]{:S(2)}) %collective-permute-start.16) | collective-permute-done | bytes 114720 | tf_op jit(solution)/shard_map/ppermute | solution.py:392
  53.8 1.4 %collective-permute-start.17 = (bf16[64,896]{1,0:T(8,128)(2,1)S(1)}, bf16[64,896]{1,0:T(8,128)(2,1)S(1)}, u32[]{:S(2)}, u32[]{:S(2)}) collective-permute-start(bf16[64,896]{1,0:T(8,128)(2,1)S(1)} %add_convert_fusion.2.rest_4_), channel_id=1, source_target_pairs={{0,1},{1,0},{2,3},{3,2},{4,5},{5,4},{6,7},{7,6},{8,9},{9,8},{10,11... | collective-permute-start | bytes 344072 | tf_op jit(solution)/shard_map/ppermute | solution.py:392
  55.2 5.7 %collective-permute-done.19 = bf16[64,896]{1,0:T(8,128)(2,1)S(1)} collective-permute-done((bf16[64,896]{1,0:T(8,128)(2,1)S(1)}, bf16[64,896]{1,0:T(8,128)(2,1)S(1)}, u32[]{:S(2)}, u32[]{:S(2)}) %collective-permute-start.19) | collective-permute-done | bytes 114720 | tf_op jit(solution)/shard_map/ppermute | solution.py:392
  61.0 0.1 collective-permute-start.20
  61.1 1.1 %place_rows.1.pick_ref = bf16[4,64,256]{2,1,0:T(8,128)(2,1)S(1)} custom-call(s32[1]{0:T(128)} %bitcast.ids_ref.ids_any, s32[64]{0:T(128)S(1)} %copy-done.7), custom_call_target="tpu_custom_call" | custom-call | flops 100000000 | bytes 300000 | tf_op jit(solution)/shard_map/place_rows/pallas_call | solution.py:416
  62.1 0.0 collective-permute-done.12.rest_1_
  62.2 0.2 collective-permute-done.17.rest_5_
  62.4 3.4 %collective-permute-done.20.rest_7_ = bf16[64,896]{1,0:T(8,128)(2,1)S(1)} collective-permute-done((bf16[64,896]{1,0:T(8,128)(2,1)S(1)}, bf16[64,896]{1,0:T(8,128)(2,1)S(1)}, u32[]{:S(2)}, u32[]{:S(2)}) %collective-permute-start.20) | collective-permute-done | bytes 114720 | tf_op jit(solution)/shard_map/ppermute | solution.py:392
  65.8 1.4 %order_rows.1 = bf16[4,64,1792]{2,1,0:T(8,128)(2,1)} custom-call(s32[1]{0:T(128)} %bitcast.ids_ref.ids_any, bf16[4,64,256]{2,1,0:T(8,128)(2,1)S(1)} %place_rows.1.pick_ref, bf16[64,896]{1,0:T(8,128)(2,1)S(1)} %add_convert_fusion.5.rest_0_, bf16[64,896]{1,0:T(8,128)(2,1)S(1)} %collective-permute-done.12.rest_1_, ...), custom_call_target="tpu_custom_call" | custom-call | flops 2000000000 | bytes 6000000 | tf_op jit(solution)/shard_map/order_rows/pallas_call | solution.py:486
  (37 shorter events, 0.3 us)
Async XLA Ops:
  0.0 0.7 copy-start.7
  0.0 1.1 %copy-start.3 = (bf16[4,16,32,128]{3,2,1,0:T(8,128)(2,1)S(1)}, bf16[4,16,32,128]{3,2,1,0:T(8,128)(2,1)}, u32[]{:S(2)}) copy-start(bf16[4,16,32,128]{3,2,1,0:T(8,128)(2,1)} %nope_ref.1) | copy-start | bytes 1572868
  0.0 1.2 %copy-start.4 = (bf16[4,16,32,64]{3,2,1,0:T(8,128)(2,1)S(1)}, bf16[4,16,32,64]{3,2,1,0:T(8,128)(2,1)}, u32[]{:S(2)}) copy-start(bf16[4,16,32,64]{3,2,1,0:T(8,128)(2,1)} %rope_ref.1) | copy-start | bytes 786436
  0.0 1.2 %copy-start.5 = (bf16[4,16,576]{2,1,0:T(8,128)(2,1)S(1)}, bf16[4,16,576]{2,1,0:T(8,128)(2,1)}, u32[]{:S(2)}) copy-start(bf16[4,16,576]{2,1,0:T(8,128)(2,1)} %fresh_ref.1) | copy-start | bytes 221188
  0.0 5.5 %copy-start.1 = (bf16[32,128,512]{2,1,0:T(8,128)(2,1)S(1)}, bf16[32,128,512]{2,1,0:T(8,128)(2,1)}, u32[]{:S(2)}) copy-start(bf16[32,128,512]{2,1,0:T(8,128)(2,1)} %rest_3_.3) | copy-start | bytes 12582916
  0.0 5.5 %copy-start.2 = (bf16[32,512,128]{2,1,0:T(8,128)(2,1)S(1)}, bf16[32,512,128]{2,1,0:T(8,128)(2,1)}, u32[]{:S(2)}) copy-start(bf16[32,512,128]{2,1,0:T(8,128)(2,1)} %rest_4_.7) | copy-start | bytes 12582916
  1.2 4.3 %copy-start = (bf16[4096,576]{0,1:T(8,128)(2,1)S(1)}, bf16[4096,576]{0,1:T(8,128)(2,1)}, u32[]{:S(2)}) copy-start(bf16[4096,576]{0,1:T(8,128)(2,1)} %param.9) | copy-start | bytes 14155780
  1.2 4.3 %copy-start.6 = (s32[4,16]{1,0:T(4,128)S(1)}, s32[4,16]{1,0:T(4,128)}, u32[]{:S(2)}) copy-start(s32[4,16]{1,0:T(4,128)} %length_any.3) | copy-start | bytes 772
  2.4 3.2 %collective-permute-start = (bf16[1,848,128]{2,1,0:T(8,128)(2,1)S(1)}, bf16[1,848,128]{2,1,0:T(8,128)(2,1)S(1)}, u32[]{:S(2)}, u32[]{:S(2)}) collective-permute-start(bf16[1,848,128]{2,1,0:T(8,128)(2,1)S(1)} %get-tuple-element.24), channel_id=1, source_target_pairs={{0,4},{4,0},{8,12},{12,8},{1,5},{5,1},{9,13},{13,9},{2,6},{6,2},{1... | collective-permute-start | bytes 651272 | tf_op jit(solution)/shard_map/ppermute | solution.py:392
  2.9 12.4 %collective-permute-start.3 = (bf16[1,848,128]{2,1,0:T(8,128)(2,1)S(1)}, bf16[1,848,128]{2,1,0:T(8,128)(2,1)S(1)}, u32[]{:S(2)}, u32[]{:S(2)}) collective-permute-start(bf16[1,848,128]{2,1,0:T(8,128)(2,1)S(1)} %get-tuple-element.25), channel_id=1, source_target_pairs={{0,8},{4,12},{8,0},{12,4},{1,9},{5,13},{9,1},{13,5},{2,10},{6,14},... | collective-permute-start | bytes 651272 | tf_op jit(solution)/shard_map/ppermute | solution.py:392
  5.5 10.3 %collective-permute-start.4 = (bf16[1,848,128]{2,1,0:T(8,128)(2,1)S(1)}, bf16[1,848,128]{2,1,0:T(8,128)(2,1)S(1)}, u32[]{:S(2)}, u32[]{:S(2)}) collective-permute-start(bf16[1,848,128]{2,1,0:T(8,128)(2,1)S(1)} %get-tuple-element.26), channel_id=1, source_target_pairs={{0,12},{4,8},{8,4},{12,0},{1,13},{5,9},{9,5},{13,1},{2,14},{6,10},... | collective-permute-start | bytes 651272 | tf_op jit(solution)/shard_map/ppermute | solution.py:392
  5.6 19.7 %slice-start = ((s8[14680064]{0:T(1024)(128)(4,1)}), s8[4194304]{0:T(1024)(128)(4,1)S(1)}, s32[]{:S(2)}) async-start(s8[14680064]{0:T(1024)(128)(4,1)} %bitcast.2), calls=%async_computation | async-start | bytes 8388608
  5.6 19.7 %slice-start.1 = ((s8[14680064]{0:T(1024)(128)(4,1)}), s8[4194304]{0:T(1024)(128)(4,1)S(1)}, s32[]{:S(2)}) async-start(s8[14680064]{0:T(1024)(128)(4,1)} %bitcast.2), calls=%async_computation.1 | async-start | bytes 8388608
  12.0 13.3 %slice-start.2 = ((s8[14680064]{0:T(1024)(128)(4,1)}), s8[4194304]{0:T(1024)(128)(4,1)S(1)}, s32[]{:S(2)}) async-start(s8[14680064]{0:T(1024)(128)(4,1)} %bitcast.2), calls=%async_computation.2 | async-start | bytes 8388608
  12.0 13.3 %slice-start.3 = ((s8[14680064]{0:T(1024)(128)(4,1)}), s8[2097152]{0:T(1024)(128)(4,1)S(1)}, s32[]{:S(2)}) async-start(s8[14680064]{0:T(1024)(128)(4,1)} %bitcast.2), calls=%async_computation.3 | async-start | bytes 4194304
  12.0 13.3 %collective-permute-start.1 = (bf16[32,4096]{1,0:T(8,128)(2,1)S(1)}, bf16[32,4096]{1,0:T(8,128)(2,1)S(1)}, u32[]{:S(2)}, u32[]{:S(2)}) collective-permute-start(bf16[32,4096]{1,0:T(8,128)(2,1)S(1)} %attend.2.rest_0_), channel_id=1, source_target_pairs={{0,4},{4,0},{8,12},{12,8},{1,5},{5,1},{9,13},{13,9},{2,6},{6,2},{1... | collective-permute-start | bytes 786440 | tf_op jit(solution)/shard_map/ppermute | solution.py:392
  13.2 10.1 %collective-permute-start.2 = (bf16[32,4096]{1,0:T(8,128)(2,1)S(1)}, bf16[32,4096]{1,0:T(8,128)(2,1)S(1)}, u32[]{:S(2)}, u32[]{:S(2)}) collective-permute-start(bf16[32,4096]{1,0:T(8,128)(2,1)S(1)} %attend.2.rest_0_), channel_id=1, source_target_pairs={{0,8},{4,12},{8,0},{12,4},{1,9},{5,13},{9,1},{13,5},{2,10},{6,14},... | collective-permute-start | bytes 786440 | tf_op jit(solution)/shard_map/ppermute | solution.py:392
  23.3 2.0 %collective-permute-start.5 = (bf16[32,4096]{1,0:T(8,128)(2,1)S(1)}, bf16[32,4096]{1,0:T(8,128)(2,1)S(1)}, u32[]{:S(2)}, u32[]{:S(2)}) collective-permute-start(bf16[32,4096]{1,0:T(8,128)(2,1)S(1)} %collective-permute-done.2.rest_2_), channel_id=1, source_target_pairs={{0,4},{4,0},{8,12},{12,8},{1,5},{5,1},{9,13},{13,9},{2,6},{6,2},{1... | collective-permute-start | bytes 786440 | tf_op jit(solution)/shard_map/ppermute | solution.py:392
  23.4 13.0 %collective-permute-start.8 = (bf16[32,4096]{1,0:T(8,128)(2,1)S(1)}, bf16[32,4096]{1,0:T(8,128)(2,1)S(1)}, u32[]{:S(2)}, u32[]{:S(2)}) collective-permute-start(bf16[32,4096]{1,0:T(8,128)(2,1)S(1)} %attend.3.rest_0_), channel_id=1, source_target_pairs={{0,4},{4,0},{8,12},{12,8},{1,5},{5,1},{9,13},{13,9},{2,6},{6,2},{1... | collective-permute-start | bytes 786440 | tf_op jit(solution)/shard_map/ppermute | solution.py:392
  23.9 8.3 %collective-permute-start.9 = (bf16[32,4096]{1,0:T(8,128)(2,1)S(1)}, bf16[32,4096]{1,0:T(8,128)(2,1)S(1)}, u32[]{:S(2)}, u32[]{:S(2)}) collective-permute-start(bf16[32,4096]{1,0:T(8,128)(2,1)S(1)} %attend.3.rest_0_), channel_id=1, source_target_pairs={{0,8},{4,12},{8,0},{12,4},{1,9},{5,13},{9,1},{13,5},{2,10},{6,14},... | collective-permute-start | bytes 786440 | tf_op jit(solution)/shard_map/ppermute | solution.py:392
  26.6 7.2 %collective-permute-start.6 = (bf16[64,896]{1,0:T(8,128)(2,1)S(1)}, bf16[64,896]{1,0:T(8,128)(2,1)S(1)}, u32[]{:S(2)}, u32[]{:S(2)}) collective-permute-start(bf16[64,896]{1,0:T(8,128)(2,1)S(1)} %get-tuple-element.29), channel_id=1, source_target_pairs={{0,1},{1,0},{2,3},{3,2},{4,5},{5,4},{6,7},{7,6},{8,9},{9,8},{10,11... | collective-permute-start | bytes 344072 | tf_op jit(solution)/shard_map/ppermute | solution.py:392
  32.2 4.2 %collective-permute-start.10 = (bf16[32,4096]{1,0:T(8,128)(2,1)S(1)}, bf16[32,4096]{1,0:T(8,128)(2,1)S(1)}, u32[]{:S(2)}, u32[]{:S(2)}) collective-permute-start(bf16[32,4096]{1,0:T(8,128)(2,1)S(1)} %collective-permute-done.9.rest_2_), channel_id=1, source_target_pairs={{0,4},{4,0},{8,12},{12,8},{1,5},{5,1},{9,13},{13,9},{2,6},{6,2},{1... | collective-permute-start | bytes 786440 | tf_op jit(solution)/shard_map/ppermute | solution.py:392
  32.2 6.3 %collective-permute-start.13 = (bf16[64,896]{1,0:T(8,128)(2,1)S(1)}, bf16[64,896]{1,0:T(8,128)(2,1)S(1)}, u32[]{:S(2)}, u32[]{:S(2)}) collective-permute-start(bf16[64,896]{1,0:T(8,128)(2,1)S(1)} %get-tuple-element.36), channel_id=1, source_target_pairs={{0,1},{1,0},{2,3},{3,2},{4,5},{5,4},{6,7},{7,6},{8,9},{9,8},{10,11... | collective-permute-start | bytes 344072 | tf_op jit(solution)/shard_map/ppermute | solution.py:392
  33.9 13.8 %collective-permute-start.7 = (bf16[64,896]{1,0:T(8,128)(2,1)S(1)}, bf16[64,896]{1,0:T(8,128)(2,1)S(1)}, u32[]{:S(2)}, u32[]{:S(2)}) collective-permute-start(bf16[64,896]{1,0:T(8,128)(2,1)S(1)} %add_convert_fusion.7), channel_id=1, source_target_pairs={{0,3},{1,2},{2,1},{3,0},{4,7},{5,6},{6,5},{7,4},{8,11},{9,10},{10,... | collective-permute-start | bytes 344072 | tf_op jit(solution)/shard_map/ppermute | solution.py:392
  37.7 8.1 %collective-permute-start.11 = (bf16[64,896]{1,0:T(8,128)(2,1)S(1)}, bf16[64,896]{1,0:T(8,128)(2,1)S(1)}, u32[]{:S(2)}, u32[]{:S(2)}) collective-permute-start(bf16[64,896]{1,0:T(8,128)(2,1)S(1)} %get-tuple-element.34), channel_id=1, source_target_pairs={{0,1},{1,0},{2,3},{3,2},{4,5},{5,4},{6,7},{7,6},{8,9},{9,8},{10,11... | collective-permute-start | bytes 344072 | tf_op jit(solution)/shard_map/ppermute | solution.py:392
  38.5 9.3 %collective-permute-start.14 = (bf16[64,896]{1,0:T(8,128)(2,1)S(1)}, bf16[64,896]{1,0:T(8,128)(2,1)S(1)}, u32[]{:S(2)}, u32[]{:S(2)}) collective-permute-start(bf16[64,896]{1,0:T(8,128)(2,1)S(1)} %add_convert_fusion.4), channel_id=1, source_target_pairs={{0,3},{1,2},{2,1},{3,0},{4,7},{5,6},{6,5},{7,4},{8,11},{9,10},{10,... | collective-permute-start | bytes 344072 | tf_op jit(solution)/shard_map/ppermute | solution.py:392
  45.0 6.2 %collective-permute-start.18 = (bf16[64,896]{1,0:T(8,128)(2,1)S(1)}, bf16[64,896]{1,0:T(8,128)(2,1)S(1)}, u32[]{:S(2)}, u32[]{:S(2)}) collective-permute-start(bf16[64,896]{1,0:T(8,128)(2,1)S(1)} %get-tuple-element.40), channel_id=1, source_target_pairs={{0,1},{1,0},{2,3},{3,2},{4,5},{5,4},{6,7},{7,6},{8,9},{9,8},{10,11... | collective-permute-start | bytes 344072 | tf_op jit(solution)/shard_map/ppermute | solution.py:392
  45.8 8.0 %collective-permute-start.16 = (bf16[64,896]{1,0:T(8,128)(2,1)S(1)}, bf16[64,896]{1,0:T(8,128)(2,1)S(1)}, u32[]{:S(2)}, u32[]{:S(2)}) collective-permute-start(bf16[64,896]{1,0:T(8,128)(2,1)S(1)} %add_convert_fusion.6), channel_id=1, source_target_pairs={{0,3},{1,2},{2,1},{3,0},{4,7},{5,6},{6,5},{7,4},{8,11},{9,10},{10,... | collective-permute-start | bytes 344072 | tf_op jit(solution)/shard_map/ppermute | solution.py:392
  47.8 14.4 %collective-permute-start.12 = (bf16[64,896]{1,0:T(8,128)(2,1)S(1)}, bf16[64,896]{1,0:T(8,128)(2,1)S(1)}, u32[]{:S(2)}, u32[]{:S(2)}) collective-permute-start(bf16[64,896]{1,0:T(8,128)(2,1)S(1)} %add_convert_fusion.5.rest_0_), channel_id=1, source_target_pairs={{0,1},{1,0},{2,3},{3,2},{4,5},{5,4},{6,7},{7,6},{8,9},{9,8},{10,11... | collective-permute-start | bytes 344072 | tf_op jit(solution)/shard_map/ppermute | solution.py:392
  47.9 14.3 %collective-permute-start.15 = (bf16[64,896]{1,0:T(8,128)(2,1)S(1)}, bf16[64,896]{1,0:T(8,128)(2,1)S(1)}, u32[]{:S(2)}, u32[]{:S(2)}) collective-permute-start(bf16[64,896]{1,0:T(8,128)(2,1)S(1)} %add_convert_fusion.3.rest_2_), channel_id=1, source_target_pairs={{0,1},{1,0},{2,3},{3,2},{4,5},{5,4},{6,7},{7,6},{8,9},{9,8},{10,11... | collective-permute-start | bytes 344072 | tf_op jit(solution)/shard_map/ppermute | solution.py:392
  51.3 9.7 %collective-permute-start.19 = (bf16[64,896]{1,0:T(8,128)(2,1)S(1)}, bf16[64,896]{1,0:T(8,128)(2,1)S(1)}, u32[]{:S(2)}, u32[]{:S(2)}) collective-permute-start(bf16[64,896]{1,0:T(8,128)(2,1)S(1)} %add_convert_fusion.1), channel_id=1, source_target_pairs={{0,3},{1,2},{2,1},{3,0},{4,7},{5,6},{6,5},{7,4},{8,11},{9,10},{10,... | collective-permute-start | bytes 344072 | tf_op jit(solution)/shard_map/ppermute | solution.py:392
  53.8 8.6 %collective-permute-start.17 = (bf16[64,896]{1,0:T(8,128)(2,1)S(1)}, bf16[64,896]{1,0:T(8,128)(2,1)S(1)}, u32[]{:S(2)}, u32[]{:S(2)}) collective-permute-start(bf16[64,896]{1,0:T(8,128)(2,1)S(1)} %add_convert_fusion.2.rest_4_), channel_id=1, source_target_pairs={{0,1},{1,0},{2,3},{3,2},{4,5},{5,4},{6,7},{7,6},{8,9},{9,8},{10,11... | collective-permute-start | bytes 344072 | tf_op jit(solution)/shard_map/ppermute | solution.py:392
  61.0 4.9 %collective-permute-start.20 = (bf16[64,896]{1,0:T(8,128)(2,1)S(1)}, bf16[64,896]{1,0:T(8,128)(2,1)S(1)}, u32[]{:S(2)}, u32[]{:S(2)}) collective-permute-start(bf16[64,896]{1,0:T(8,128)(2,1)S(1)} %add_convert_fusion.rest_6_), channel_id=1, source_target_pairs={{0,1},{1,0},{2,3},{3,2},{4,5},{5,4},{6,7},{7,6},{8,9},{9,8},{10,11... | collective-permute-start | bytes 344072 | tf_op jit(solution)/shard_map/ppermute | solution.py:392
